TPU v7x, 32 devices: a whole 2x2x4 slice. The times are simulated.
32 devices in a mesh: pipe: 4 (over z), sp: 4 (over y, core), cfg: 2 (over x).
Axes of the slice: x: 2, y: 2, z: 4, core: 2. Of those that a mesh axis runs over, the one named last changes fastest.
Arguments:
- flight: bfloat16 [4, 2, 512, 5120], P('pipe', 'cfg', 'sp'), may hold values from -6 to 6
- modulation: float32 [4, 2, 3, 5120], P('pipe', 'cfg'), may hold values from -4 to 4
- project_in: bfloat16 [4, 3, 5120, 3072], P('pipe', None, None, ('sp', 'cfg')), may hold values from -0.078125 to 0.078125
- project_out: bfloat16 [4, 3072, 5120], P('pipe', ('sp', 'cfg')), may hold values from -0.5 to 0.5
- stale_cache: bfloat16 [4, 2, 1024, 2, 3072], P('pipe', 'cfg', 'sp'), may hold values from -4 to 4
- visible: int32 [4, 4, 6], P('pipe'), may hold values from 0 to 11, all different within a row
Outputs:
- advanced: bfloat16 [4, 2, 512, 5120], P('pipe', 'cfg', 'sp')
Inputs may be any that keep to these rules, and one draw needn't show every extreme that they name: `visible`: 6 different tile numbers for each query tile; number j < 4 is tile j of the segment's own patch, number 4 + j is tile j of its stale context.
All inputs are finite; a program needn't handle non-finite values.
Results may differ from a plain program's by a relative error of at most 0.006.
Values may be sent and summed in bfloat16 or wider, within the bound.
No kernel may reach another device: no remote copies, remote signals or barrier semaphores. Data moves between devices by JAX's collectives and lax.ppermute only.
A program may use at most 128 MiB of HBM per device.

v0:
```python
import jax
import jax.numpy as jnp
from jax import lax
from jax.sharding import PartitionSpec as P

HD = 128
TILE = 128


guidance_scale = 5.0


def from_behind(x, axis, by):
    count = lax.axis_size(axis)
    return lax.ppermute(x, axis, [(i, (i + by) % count) for i in range(count)])


def from_partner(value, axis, bit):
    mask = 2**bit
    pairs = [(source, source ^ mask) for source in range(lax.axis_size(axis))]
    return lax.ppermute(value, axis, pairs)


def layer_norm(values):
    centre = values - jnp.mean(values, axis=-1, keepdims=True)
    spread = jnp.mean(centre * centre, axis=-1, keepdims=True)
    return centre * lax.rsqrt(spread + 1e-06)


def head_norm(values):
    return values * lax.rsqrt(jnp.mean(values * values, axis=-1, keepdims=True) + 1e-06)


def projector(weights, piece_rows):
    product = jnp.einsum("rd,idc->ric", piece_rows, weights, preferred_element_type=jnp.float32)
    row_count = product.shape[0]
    head_count = product.shape[2] // HD
    split_heads = product.reshape(row_count, 3, head_count, HD)
    normed = jnp.concatenate([head_norm(split_heads[:, :2]), split_heads[:, 2:]], axis=1)
    return normed.reshape(row_count, 3, head_count * HD).astype(jnp.bfloat16)


def attend(projected, context, visible):
    batch_count, patch_len, _, width_local = projected.shape
    head_count = width_local // HD
    tiles_query = patch_len // TILE
    tiles_total = tiles_query + context.shape[1] // TILE
    keys_pool = jnp.concatenate([projected[:, :, 1], context[:, :, 0]], axis=1).reshape(
        batch_count, tiles_total, TILE, head_count, HD
    )
    values_pool = jnp.concatenate([projected[:, :, 2], context[:, :, 1]], axis=1).reshape(
        batch_count, tiles_total, TILE, head_count, HD
    )
    key_tiles = jnp.take(keys_pool, visible, axis=1).reshape(
        batch_count, tiles_query, -1, head_count, HD
    )
    value_tiles = jnp.take(values_pool, visible, axis=1).reshape(
        batch_count, tiles_query, -1, head_count, HD
    )
    query_tiles = projected[:, :, 0].reshape(batch_count, tiles_query, TILE, head_count, HD)
    scores = jnp.einsum(
        "bqthd,bqkhd->bqhtk", query_tiles, key_tiles, preferred_element_type=jnp.float32
    ) * HD ** (-0.5)
    exponent = jnp.exp(scores)
    probabilities = (exponent / jnp.sum(exponent, axis=-1, keepdims=True)).astype(jnp.bfloat16)
    attended = jnp.einsum(
        "bqhtk,bqkhd->bqthd", probabilities, value_tiles, preferred_element_type=jnp.float32
    )
    return attended.astype(jnp.bfloat16).reshape(batch_count, patch_len, width_local)


def per_device(flight, modulation, project_in, project_out, stale_cache, visible):
    current = flight[0, 0]
    modulate = modulation[0, 0]
    modulated = (
        layer_norm(current.astype(jnp.float32)) * (1.0 + modulate[1]) + modulate[0]
    ).astype(jnp.bfloat16)
    token_rows = current.shape[0]
    groups = lax.axis_size("sp")
    branches = lax.axis_size("cfg")
    gathered = projector(
        project_in[0], lax.all_gather(modulated, ("sp", "cfg"), axis=0, tiled=True)
    )
    width_local = gathered.shape[-1]
    projected = gathered.reshape(groups, branches, token_rows, 3, width_local).transpose(
        1, 0, 2, 3, 4
    )
    projected = projected.reshape(branches, groups * token_rows, 3, width_local)
    received = lax.all_to_all(
        stale_cache[0, 0], ("sp", "cfg"), split_axis=2, concat_axis=0, tiled=True
    )
    context_rows = stale_cache.shape[2]
    context = received.reshape(groups, branches, context_rows, 2, width_local).transpose(
        1, 0, 2, 3, 4
    )
    context = context.reshape(branches, groups * context_rows, 2, width_local)
    attended = attend(projected, context, visible[0])
    arranged = attended.reshape(branches, groups, token_rows, width_local).transpose(1, 0, 2, 3)
    arranged = arranged.reshape(groups * branches * token_rows, width_local)
    mixed_sum = lax.psum_scatter(
        jnp.dot(arranged, project_out[0], preferred_element_type=jnp.float32),
        ("sp", "cfg"),
        scatter_dimension=0,
        tiled=True,
    )
    layer_out = (current.astype(jnp.float32) + modulate[2] * mixed_sum).astype(jnp.bfloat16)
    arrived = from_behind(layer_out, "pipe", 1)
    partner = from_partner(arrived, "cfg", 0)
    conditional = lax.axis_index("cfg") == 1
    cond_rows = jnp.where(conditional, arrived, partner).astype(jnp.float32)
    uncond_rows = jnp.where(conditional, partner, arrived).astype(jnp.float32)
    guided = (uncond_rows + guidance_scale * (cond_rows - uncond_rows)).astype(jnp.bfloat16)
    result = jnp.where(lax.axis_index("pipe") == 0, guided, arrived)
    return result[None, None]


def solution(mesh):
    placed = (
        P("pipe", "cfg", "sp", None),
        P("pipe", "cfg", None, None),
        P("pipe", None, None, ("sp", "cfg")),
        P("pipe", ("sp", "cfg"), None),
        P("pipe", "cfg", "sp", None, None),
        P("pipe", None, None),
    )
    return jax.shard_map(
        per_device,
        mesh=mesh,
        in_specs=placed,
        out_specs=P("pipe", "cfg", "sp", None),
        check_vma=False,
    )
```

profile of v0, /device:TPU:0, one launch (start us, length us, event | category | flops | bytes accessed | tf_op | source)
XLA Modules:
  0.0 404.0 jit_solution(16330824907245483914)
XLA Ops:
  6.5 0.0 copy-start
  6.5 0.0 all-gather.2.cloned.1.call-start
  6.5 0.9 fusion.24
  7.4 1.6 convert_reduce_fusion
  9.0 1.8 fusion.10
  10.8 0.0 copy-done
  10.9 1.6 fusion.13
  12.5 0.0 all-gather.2.cloned.1.call-update
  12.5 11.3 %copy.49 = bf16[1,1,256,2,3072]{2,3,4,1,0:T(2,128)(2,1)} copy(bf16[1,1,256,2,3072]{4,3,2,1,0:T(2,128)(2,1)} %param.12) | data formatting | bytes 6291456 | tf_op args[4]
  23.8 5.2 %all-to-all-start = ((bf16[256,2,3072]{0,1,2:T(2,128)(2,1)}), bf16[256,2,3072]{0,1,2:T(2,128)(2,1)S(1)}, u32[]{:S(2)}, u32[]{:S(2)}) async-start(bf16[256,2,3072]{0,1,2:T(2,128)(2,1)} %bitcast.93), calls=%async_computation | async-start | bytes 6291456 | tf_op jit(solution)/shard_map/all_to_all | solution.py:89
  29.0 0.0 copy-start.5
  29.0 0.0 reduce-scatter.2.cloned.1.call-start
  29.1 15.6 %copy.47 = bf16[1,3,5120,384]{2,3,1,0:T(8,128)(2,1)} copy(bf16[1,3,5120,384]{3,2,1,0:T(8,128)(2,1)} %param.10) | data formatting | bytes 23592960 | tf_op args[2]
  44.7 0.0 copy-done.5
  44.7 0.1 reshape.99
  44.8 30.1 %all-to-all-done = bf16[256,2,3072]{0,1,2:T(2,128)(2,1)S(1)} async-done(((bf16[256,2,3072]{0,1,2:T(2,128)(2,1)}), bf16[256,2,3072]{0,1,2:T(2,128)(2,1)S(1)}, u32[]{:S(2)}, u32[]{:S(2)}) %all-to-all-start) | async-done | bytes 3145760 | tf_op jit(solution)/shard_map/all_to_all | solution.py:89
  74.8 2.1 copy.50
  77.0 3.4 copy.52
  80.4 2.0 slice_bitcast_fusion
  82.4 22.3 %all-gather.2.cloned.1.call-done = bf16[1024,5120]{1,0:T(8,128)(2,1)} async-done(((bf16[128,5120]{1,0:T(8,128)(2,1)}), bf16[1024,5120]{1,0:T(8,128)(2,1)}) %all-gather.2.cloned.1.call-update) | async-done | bytes 10485776 | tf_op jit(solution)/shard_map/all_gather | solution.py:82
  104.7 17.2 %fusion = f32[1024,3,3,128]{0,3,2,1:T(8,128)S(1)} fusion(bf16[3,3,128,5120]{3,2,1,0:T(8,128)(2,1)} %bitcast.96, bf16[1024,5120]{1,0:T(8,128)(2,1)} %all-gather.2.cloned.1.call-done), kind=kOutput, calls=%fused_computation.2 | convolution fusion | flops 12079595520 | bytes 27000832 | tf_op jit(solution)/shard_map/rd,idc->ric/dot_general | solution.py:35
  121.9 0.4 multiply_reduce_fusion
  122.3 0.1 slice.63
  122.5 0.4 multiply_convert_fusion
  122.9 0.2 pad_maximum_fusion
  123.1 2.9 convert_element_type.39
  126.0 5.8 %copy.48 = bf16[4,2,128,3,384]{4,2,0,3,1:T(8,128)(2,1)S(1)} copy(bf16[4,2,128,3,384]{2,1,0,4,3:T(2,128)(2,1)} %convert_element_type.39) | data formatting | bytes 4718592 | tf_op jit(solution)/shard_map/convert_element_type | solution.py:40
  131.9 0.0 copy-start.2
  131.9 0.0 copy-start.3
  131.9 0.2 fusion.23
  132.1 1.1 copy-done.2
  133.3 0.5 copy-done.3
  133.7 1.7 pad_maximum_fusion.1
  135.5 3.5 reshape.108
  139.0 2.6 copy.54
  141.5 7.0 %reshape.110 = bf16[2,12,128,3,128]{4,3,2,1,0:T(4,128)(2,1)} reshape(bf16[2,1536,384]{2,1,0:T(8,128)(2,1)} %get-tuple-element.19) | data formatting | bytes 4718592 | tf_op jit(solution)/shard_map/reshape | solution.py:48
  148.5 3.9 copy.58
  152.5 3.5 gather_fusion
  156.0 5.1 %gather_fusion.1 = bf16[24,2,128,3,128]{4,2,3,1,0:T(8,128)(2,1)} fusion(bf16[2,12,128,3,128]{4,2,3,1,0:T(8,128)(2,1)} %copy.58, s32[1024]{0:T(1024)S(1)} %pad_clamp_fusion), kind=kCustom, calls=%fused_computation.1.clone | custom fusion | bytes 9437280 | tf_op jit(solution)/shard_map/jit(_take)/gather | solution.py:54
  161.1 6.9 %select_bitcast_fusion = (bf16[2,4,6,128,3,128]{5,3,4,0,2,1:T(8,128)(2,1)S(1)}, bf16[2,4,6,128,3,128]{5,3,4,0,2,1:T(8,128)(2,1)}) fusion(bf16[4,6,2,128,3,128]{5,3,4,2,1,0:T(8,128)(2,1)} %bitcast.89, pred[4,6]{1,0:T(4,128)(4,1)S(1)} %compare_and_fusion, bf16[4,6,2,128,3,128]{5,3,4,2,1,0:T(8,128)(2,1)} %bitcast.88), kind=kLoop, calls=%fused_computation.7 | loop fusion | flops 4718592 | bytes 18874392 | tf_op jit(solution)/shard_map/jit(_take)/select_n | solution.py:54
  168.0 3.1 copy.59
  171.1 1.1 reshape.109
  172.2 0.0 slice-start
  172.2 0.0 slice-start.1
  172.2 0.0 copy-start.4
  172.2 3.5 copy.55
  175.6 0.1 slice-done
  175.8 0.1 slice-done.1
  175.9 0.3 copy-done.4
  176.2 1.7 fusion.2
  177.9 3.8 fusion.17
  181.7 1.5 copy.62
  183.2 12.0 %fusion.4 = f32[1024,5120]{1,0:T(8,128)} fusion(bf16[1024,384]{1,0:T(8,128)(2,1)S(1)} %bitcast.99, bf16[1,384,5120]{2,1,0:T(8,128)(2,1)} %param.11), kind=kOutput, calls=%fused_computation.10 | convolution fusion | flops 4026531840 | bytes 25690112 | tf_op jit(solution)/shard_map/dot_general | solution.py:101
  195.2 0.0 copy-start.1
  195.2 0.0 reduce-scatter.2.cloned.1.call-update
  195.2 136.1 %reduce-scatter.2.cloned.1.call-done = f32[128,5120]{1,0:T(8,128)} async-done(((f32[1024,5120]{1,0:T(8,128)}), f32[128,5120]{1,0:T(8,128)}) %reduce-scatter.2.cloned.1.call-update) | async-done | bytes 2621456 | tf_op jit(solution)/shard_map/reduce_scatter | solution.py:100
  331.3 0.0 copy-done.1
  331.3 2.1 fusion.14
  333.4 1.5 collective-permute-start
  334.9 30.8 %collective-permute-done = bf16[128,5120]{1,0:T(8,128)(2,1)S(1)} collective-permute-done((bf16[128,5120]{1,0:T(8,128)(2,1)S(1)}, bf16[128,5120]{1,0:T(8,128)(2,1)S(1)}, u32[]{:S(2)}, u32[]{:S(2)}) %collective-permute-start) | collective-permute-done | bytes 1310752 | tf_op jit(solution)/shard_map/ppermute | solution.py:15
  365.7 1.3 collective-permute-start.1
  367.1 28.3 %collective-permute-done.1 = bf16[128,5120]{1,0:T(8,128)(2,1)S(1)} collective-permute-done((bf16[128,5120]{1,0:T(8,128)(2,1)S(1)}, bf16[128,5120]{1,0:T(8,128)(2,1)S(1)}, u32[]{:S(2)}, u32[]{:S(2)}) %collective-permute-start.1) | collective-permute-done | bytes 1310752 | tf_op jit(solution)/shard_map/ppermute | solution.py:21
  395.4 1.8 fusion.19
  (7 shorter events, 0.1 us)
Async XLA Ops:
  6.5 4.3 %copy-start = (bf16[1,1,128,5120]{3,2,1,0:T(8,128)(2,1)S(1)}, bf16[1,1,128,5120]{3,2,1,0:T(8,128)(2,1)}, u32[]{:S(2)}) copy-start(bf16[1,1,128,5120]{3,2,1,0:T(8,128)(2,1)} %param.8) | copy-start | bytes 3932164
  6.5 98.1 %all-gather.2.cloned.1.call-start = ((), (), s32[]{:S(2)}) async-start(), calls=%async_computation.2 | async-start | bytes 11796480 | tf_op jit(solution)/shard_map/all_gather | solution.py:82
  23.8 51.0 %all-to-all-start = ((bf16[256,2,3072]{0,1,2:T(2,128)(2,1)}), bf16[256,2,3072]{0,1,2:T(2,128)(2,1)S(1)}, u32[]{:S(2)}, u32[]{:S(2)}) async-start(bf16[256,2,3072]{0,1,2:T(2,128)(2,1)} %bitcast.93), calls=%async_computation | async-start | bytes 6291456 | tf_op jit(solution)/shard_map/all_to_all | solution.py:89
  29.0 15.6 %copy-start.5 = (s32[1,4,6]{2,1,0:T(4,128)S(1)}, s32[1,4,6]{2,1,0:T(4,128)}, u32[]{:S(2)}) copy-start(s32[1,4,6]{2,1,0:T(4,128)} %param.13) | copy-start | bytes 292
  29.0 302.3 %reduce-scatter.2.cloned.1.call-start = ((), (), s32[]{:S(2)}) async-start(), calls=%async_computation.3 | async-start | bytes 23592960 | tf_op jit(solution)/shard_map/reduce_scatter | solution.py:100
  131.9 1.4 copy-start.2
  131.9 1.9 copy-start.3
  172.2 3.6 slice-start
  172.2 3.7 slice-start.1
  172.2 4.1 %copy-start.4 = (bf16[2,4,128,3,128]{4,3,2,1,0:T(4,128)(2,1)S(1)}, bf16[2,4,128,3,128]{4,3,2,1,0:T(4,128)(2,1)}, u32[]{:S(2)}) copy-start(bf16[2,4,128,3,128]{4,3,2,1,0:T(4,128)(2,1)} %reshape.109) | copy-start | bytes 2359300
  195.2 136.1 %copy-start.1 = (bf16[1,1,128,5120]{3,2,1,0:T(8,128)(2,1)S(1)}, bf16[1,1,128,5120]{3,2,1,0:T(8,128)(2,1)}, u32[]{:S(2)}) copy-start(bf16[1,1,128,5120]{3,2,1,0:T(8,128)(2,1)} %param.8) | copy-start | bytes 3932164
  333.4 32.4 %collective-permute-start = (bf16[128,5120]{1,0:T(8,128)(2,1)S(1)}, bf16[128,5120]{1,0:T(8,128)(2,1)S(1)}, u32[]{:S(2)}, u32[]{:S(2)}) collective-permute-start(bf16[128,5120]{1,0:T(8,128)(2,1)S(1)} %fusion.14), channel_id=1, source_target_pairs={{0,8},{8,16},{16,24},{24,0},{1,9},{9,17},{17,25},{25,1},{2,10},{10... | collective-permute-start | bytes 3932168 | tf_op jit(solution)/shard_map/ppermute | solution.py:15
  365.7 29.6 %collective-permute-start.1 = (bf16[128,5120]{1,0:T(8,128)(2,1)S(1)}, bf16[128,5120]{1,0:T(8,128)(2,1)S(1)}, u32[]{:S(2)}, u32[]{:S(2)}) collective-permute-start(bf16[128,5120]{1,0:T(8,128)(2,1)S(1)} %collective-permute-done), channel_id=1, source_target_pairs={{0,1},{1,0},{2,3},{3,2},{4,5},{5,4},{6,7},{7,6},{8,9},{9,8},{10,11... | collective-permute-start | bytes 3932168 | tf_op jit(solution)/shard_map/ppermute | solution.py:21
Sparse Core Ops, SparseCore 0:
  12.6 92.0 all-gather.1
  195.3 135.9 reduce-scatter.1
where the time goes:
time: 405 us; the launch traced here: 404 us
  waiting for transfers between devices  248 us (61%)
  local copies, waits for them, and re-layouts  80.6 us (20%)
  matrix products  34.7 us (9%)
  other arithmetic  19.4 us (5%)
  between operations  13.6 us (3%)
  starting transfers between devices  8.12 us (2%)
    reduce_scatter x1, waiting for transfers between devices, per_device(): lax.psum_scatter(jnp.dot(arranged, project_out[0], preferred_element_type...  136 us
    ppermute x1, waiting for transfers between devices, from_behind(): return lax.ppermute(x, axis, [(i, (i + by) % count) for i in range(count)])  30.8 us
    all_to_all x1, waiting for transfers between devices, per_device(): lax.all_to_all(stale_cache[0, 0], ('sp', 'cfg'), split_axis=2, concat_axi...  30.1 us
    unnamed x18, local copies, waits for them, and re-layouts  29.1 us
    ppermute x1, waiting for transfers between devices, from_partner(): return lax.ppermute(value, axis, pairs)  28.3 us
    all_gather x1, waiting for transfers between devices, per_device(): lax.all_gather(modulated, ('sp', 'cfg'), axis=0, tiled=True)  22.3 us
    dot_general x1, matrix products, projector(): jnp.einsum('rd,idc->ric', piece_rows, weights, preferred_element_type=jnp...  17.2 us
    dot_general x1, matrix products, per_device(): jnp.dot(arranged, project_out[0], preferred_element_type=jnp.float32)  12 us
  transfers between devices with their start and end apart: 5, of which 5 were waited for; matrix products, arithmetic and copies ran while one was open for 9% of the time, Pallas kernels for 0%

commit v1 on v0

v1 whole, which is shorter than its diff:
```python
import functools

import jax
import jax.numpy as jnp
from jax import lax
from jax.experimental import pallas as pl
from jax.experimental.pallas import tpu as pltpu
from jax.sharding import PartitionSpec as P

HD = 128
TILE = 128
MIB = 2**20
COLUMN_CHUNKS = 2

guidance_scale = 5.0


def from_behind(x, axis, by):
    count = lax.axis_size(axis)
    return lax.ppermute(x, axis, [(i, (i + by) % count) for i in range(count)])


def from_partner(value, axis, mask):
    pairs = [(source, source ^ mask) for source in range(lax.axis_size(axis))]
    return lax.ppermute(value, axis, pairs)


def norm_kernel(rows_ref, modulation_ref, out_ref):
    step = 16

    def body(index, carry):
        rows = pl.ds(pl.multiple_of(index * step, step), step)
        values = rows_ref[rows, :].astype(jnp.float32)
        centre = values - jnp.mean(values, axis=-1, keepdims=True)
        spread = jnp.mean(centre * centre, axis=-1, keepdims=True)
        normed = centre * lax.rsqrt(spread + 1e-06)
        out_ref[rows, :] = (
            normed * (1.0 + modulation_ref[1:2, :]) + modulation_ref[0:1, :]
        ).astype(jnp.bfloat16)
        return carry

    lax.fori_loop(0, rows_ref.shape[0] // step, body, 0)


def modulated_norm(rows, modulation):
    return pl.pallas_call(
        norm_kernel,
        out_shape=jax.ShapeDtypeStruct(rows.shape, jnp.bfloat16),
        name="modulated_norm",
        cost_estimate=pl.CostEstimate(
            flops=10 * rows.size, bytes_accessed=4 * rows.size, transcendentals=0
        ),
        compiler_params=pltpu.CompilerParams(vmem_limit_bytes=16 * MIB),
    )(rows, modulation)


def project_kernel(rows_ref, weights_ref, out_ref, total_ref):
    step = pl.program_id(0)
    weights = jnp.concatenate([weights_ref[0], weights_ref[1], weights_ref[2]], axis=1)
    product = jnp.dot(rows_ref[...], weights, preferred_element_type=jnp.float32)

    @pl.when(step == 0)
    def _():
        total_ref[...] = product

    @pl.when(step > 0)
    def _():
        total_ref[...] += product

    @pl.when(step == pl.num_programs(0) - 1)
    def _():
        width = weights_ref.shape[2]
        for head in range(2 * width // HD):
            columns = slice(head * HD, (head + 1) * HD)
            values = total_ref[:, columns]
            scale = lax.rsqrt(jnp.mean(values * values, axis=-1, keepdims=True) + 1e-06)
            out_ref[:, columns] = (values * scale).astype(jnp.bfloat16)
        out_ref[:, 2 * width :] = total_ref[:, 2 * width :].astype(jnp.bfloat16)


def project(rows, weights):
    count, depth = rows.shape
    width = weights.shape[2]
    block = 1024
    return pl.pallas_call(
        project_kernel,
        grid=(depth // block,),
        in_specs=[
            pl.BlockSpec((count, block), lambda k: (0, k)),
            pl.BlockSpec((3, block, width), lambda k: (0, k, 0)),
        ],
        out_specs=pl.BlockSpec((count, 3 * width), lambda k: (0, 0)),
        out_shape=jax.ShapeDtypeStruct((count, 3 * width), jnp.bfloat16),
        scratch_shapes=[pltpu.VMEM((count, 3 * width), jnp.float32)],
        name="project_heads",
        cost_estimate=pl.CostEstimate(
            flops=2 * count * depth * 3 * width,
            bytes_accessed=2 * (rows.size + weights.size),
            transcendentals=0,
        ),
        compiler_params=pltpu.CompilerParams(vmem_limit_bytes=40 * MIB),
    )(rows, weights)


def attend_kernel(
    visible_ref, heads_ref, context_ref, out_ref, queries, pool, query_sem, fresh_sem, stale_sem
):
    fresh_rows = heads_ref.shape[0]
    width = out_ref.shape[1]
    copies = (
        pltpu.make_async_copy(heads_ref.at[:, pl.ds(0, width)], queries, query_sem),
        pltpu.make_async_copy(
            heads_ref.at[:, pl.ds(width, 2 * width)], pool.at[pl.ds(0, fresh_rows)], fresh_sem
        ),
        pltpu.make_async_copy(
            context_ref, pool.at[pl.ds(fresh_rows, context_ref.shape[0])], stale_sem
        ),
    )
    for copy in copies:
        copy.start()
    for copy in copies:
        copy.wait()
    tiles_seen = visible_ref.shape[1]
    tiles_fresh = visible_ref.shape[0]

    def body(index, carry):
        tile, branch = index // 2, index % 2
        rows = pl.ds(pl.multiple_of(index * TILE, TILE), TILE)
        starts = []
        for seen in range(tiles_seen):
            number = visible_ref[tile, seen]
            older = number - tiles_fresh
            fresh = (number * 2 + branch) * TILE
            stale = fresh_rows + ((older // 2) * 2 + branch) * 2 * TILE + (older % 2) * TILE
            starts.append(pl.multiple_of(jnp.where(older < 0, fresh, stale), TILE))
        for head in range(width // HD):
            columns = slice(head * HD, (head + 1) * HD)
            value_columns = slice(width + head * HD, width + (head + 1) * HD)
            keys = jnp.concatenate([pool[pl.ds(s, TILE), columns] for s in starts], axis=0)
            values = jnp.concatenate([pool[pl.ds(s, TILE), value_columns] for s in starts], axis=0)
            scores = lax.dot_general(
                queries[rows, columns],
                keys,
                (((1,), (1,)), ((), ())),
                preferred_element_type=jnp.float32,
            )
            exponent = jnp.exp(scores * HD ** (-0.5))
            total = jnp.sum(exponent, axis=-1, keepdims=True)
            probabilities = (exponent / total).astype(jnp.bfloat16)
            mixed = jnp.dot(probabilities, values, preferred_element_type=jnp.float32)
            out_ref[rows, columns] = mixed.astype(jnp.bfloat16)
        return carry

    lax.fori_loop(0, fresh_rows // TILE, body, 0)


def attend(heads, context, visible):
    count = heads.shape[0]
    width = heads.shape[1] // 3
    return pl.pallas_call(
        attend_kernel,
        in_specs=[
            pl.BlockSpec(memory_space=pltpu.SMEM),
            pl.BlockSpec(memory_space=pl.ANY),
            pl.BlockSpec(memory_space=pl.ANY),
        ],
        out_shape=jax.ShapeDtypeStruct((count, width), jnp.bfloat16),
        scratch_shapes=[
            pltpu.VMEM((count, width), jnp.bfloat16),
            pltpu.VMEM((count + context.shape[0], 2 * width), jnp.bfloat16),
            pltpu.SemaphoreType.DMA,
            pltpu.SemaphoreType.DMA,
            pltpu.SemaphoreType.DMA,
        ],
        name="attend",
        cost_estimate=pl.CostEstimate(
            flops=4 * count * visible.shape[1] * TILE * width,
            bytes_accessed=2 * (heads.size + context.size),
            transcendentals=count * visible.shape[1] * TILE * width // HD,
        ),
        compiler_params=pltpu.CompilerParams(vmem_limit_bytes=32 * MIB),
    )(visible, heads, context)


def pick(values, index, axis):
    return lax.dynamic_index_in_dim(values, index, axis, keepdims=False)


def per_device(flight, modulation, project_in, project_out, stale_cache, visible):
    current = flight[0, 0]
    modulate = modulation[0, 0]
    token_rows, features = current.shape
    devices = lax.axis_size("sp") * lax.axis_size("cfg")
    branch = lax.axis_index("cfg")
    high, low = lax.axis_index("sp") // 2, lax.axis_index("sp") % 2

    modulated = modulated_norm(current, modulate)
    gathered = lax.all_gather(modulated, ("sp", "cfg"), axis=0, tiled=True)

    context_rows = stale_cache.shape[2]
    width = project_in.shape[3]
    packed = stale_cache[0, 0].reshape(context_rows, 2, devices, width)
    packed = packed.transpose(2, 0, 1, 3).reshape(devices, context_rows, 2 * width)
    context = lax.all_to_all(packed, ("sp", "cfg"), split_axis=0, concat_axis=0, tiled=True)
    context = context.reshape(devices * context_rows, 2 * width)

    heads = project(gathered, project_in[0])
    attended = attend(heads, context, visible[0])

    blocks = attended.reshape(2, 2, 2, token_rows, width)
    rows_sent = pick(blocks, 1 - low, 1).reshape(4 * token_rows, width)
    rows_kept = pick(blocks, low, 1).reshape(4 * token_rows, width)
    chunk = features // COLUMN_CHUNKS
    half = chunk // 2
    results = []
    for start in range(0, features, chunk):
        weights = project_out[0, :, start : start + chunk]
        sent = jnp.dot(rows_sent, weights, preferred_element_type=jnp.float32)
        received = from_partner(sent.astype(jnp.bfloat16), "sp", 1)
        kept = jnp.dot(rows_kept, weights, preferred_element_type=jnp.float32)
        kept = (kept + received.astype(jnp.float32)).reshape(2, 2, token_rows, chunk)

        first, second = kept[..., :half], kept[..., half:]
        first_in = from_partner(pick(first, 1 - branch, 1).astype(jnp.bfloat16), "cfg", 1)
        second_in = from_partner(pick(second, 1 - high, 0).astype(jnp.bfloat16), "sp", 2)
        first = pick(first, branch, 1) + first_in.astype(jnp.float32)
        second = pick(second, high, 0) + second_in.astype(jnp.float32)
        first_in = from_partner(pick(first, 1 - high, 0).astype(jnp.bfloat16), "sp", 2)
        second_in = from_partner(pick(second, 1 - branch, 0).astype(jnp.bfloat16), "cfg", 1)
        first = pick(first, high, 0) + first_in.astype(jnp.float32)
        second = pick(second, branch, 0) + second_in.astype(jnp.float32)
        mixed_sum = jnp.concatenate([first, second], axis=1)

        columns = slice(start, start + chunk)
        layer_out = (
            current[:, columns].astype(jnp.float32) + modulate[2, columns] * mixed_sum
        ).astype(jnp.bfloat16)
        arrived = from_behind(layer_out, "pipe", 1)
        partner = from_partner(arrived, "cfg", 1)
        cond_rows = jnp.where(branch == 1, arrived, partner).astype(jnp.float32)
        uncond_rows = jnp.where(branch == 1, partner, arrived).astype(jnp.float32)
        guided = (uncond_rows + guidance_scale * (cond_rows - uncond_rows)).astype(jnp.bfloat16)
        results.append(jnp.where(lax.axis_index("pipe") == 0, guided, arrived))
    return jnp.concatenate(results, axis=1)[None, None]


def solution(mesh):
    placed = (
        P("pipe", "cfg", "sp", None),
        P("pipe", "cfg", None, None),
        P("pipe", None, None, ("sp", "cfg")),
        P("pipe", ("sp", "cfg"), None),
        P("pipe", "cfg", "sp", None, None),
        P("pipe", None, None),
    )
    return jax.shard_map(
        per_device,
        mesh=mesh,
        in_specs=placed,
        out_specs=P("pipe", "cfg", "sp", None),
        check_vma=False,
    )
```

time: 405 us -> 255 us (0.63)
  waiting for transfers between devices: 248 us -> 151 us
  local copies, waits for them, and re-layouts: 80.6 us -> 21.8 us
  Pallas kernels: 0 us -> 33.3 us
  matrix products: 34.7 us -> 11.5 us
  other arithmetic: 19.4 us -> 2.93 us
  starting transfers between devices: 8.12 us -> 20.4 us
    reduce_scatter x1 -> x0, waiting for transfers between devices: 136 us -> none  [per_device(): lax.psum_scatter(jnp.dot(arranged, project_out[0], preferred_element_type...]
    all_gather x1, waiting for transfers between devices: 22.3 us -> 76 us  [per_device(): gathered = lax.all_gather(modulated, ('sp', 'cfg'), axis=0, tiled=True)]
    pallas_call x0 -> x3, Pallas kernels: none -> 33.3 us  [the longest x1 19.7 us: project(): pl.pallas_call(project_kernel, grid=(depth // block,), in_specs=[pl.Block...]
    all_to_all x1, waiting for transfers between devices: 30.1 us -> 0.01 us  [per_device(): lax.all_to_all(packed, ('sp', 'cfg'), split_axis=0, concat_axis=0, tiled=...]
    dot_general x4, matrix products: 34.7 us -> 11.5 us  [the longest x2 6.07 us: per_device(): sent = jnp.dot(rows_sent, weights, preferred_element_type=jnp.float32)]
    ppermute x1 -> x12, waiting for transfers between devices: 28.3 us -> 48.2 us  [from_partner(): return lax.ppermute(value, axis, pairs)]
    unnamed x18 -> x19, local copies, waits for them, and re-layouts: 29.1 us -> 9.26 us
    reshape x4 -> x1, local copies, waits for them, and re-layouts: 17 us -> 3.31 us  [per_device(): packed.transpose(2, 0, 1, 3).reshape(devices, context_rows, 2 * width)]
  transfers between devices with their start and end apart: 5 -> 16, of which waited for: 5 -> 9; matrix products, arithmetic and copies ran while one was open for 9% -> 9% of each run, Pallas kernels for 0% -> 8%
where the time goes in v1:
time: 255 us
  waiting for transfers between devices  151 us (59%)
  Pallas kernels  33.3 us (13%)
  local copies, waits for them, and re-layouts  21.8 us (9%)
  starting transfers between devices  20.4 us (8%)
  between operations  13.6 us (5%)
  matrix products  11.5 us (5%)
  other arithmetic  2.93 us (1%)
    all_gather x1, waiting for transfers between devices, per_device(): gathered = lax.all_gather(modulated, ('sp', 'cfg'), axis=0, tiled=True)  76 us
    ppermute x12, waiting for transfers between devices, from_partner(): return lax.ppermute(value, axis, pairs)  48.2 us
    ppermute x2, waiting for transfers between devices, from_behind(): return lax.ppermute(x, axis, [(i, (i + by) % count) for i in range(count)])  27.1 us
    pallas_call x1, Pallas kernels, project(): pl.pallas_call(project_kernel, grid=(depth // block,), in_specs=[pl.Block...  19.7 us
    ppermute x12, starting transfers between devices, from_partner(): return lax.ppermute(value, axis, pairs)  12.2 us
    pallas_call x1, Pallas kernels, attend(): pl.pallas_call(attend_kernel, in_specs=[pl.BlockSpec(memory_space=pltpu.S...  10.1 us
    unnamed x19, local copies, waits for them, and re-layouts  9.26 us
    dot_general x2, matrix products, per_device(): sent = jnp.dot(rows_sent, weights, preferred_element_type=jnp.float32)  6.07 us
  transfers between devices with their start and end apart: 16, of which 9 were waited for; matrix products, arithmetic and copies ran while one was open for 9% of the time, Pallas kernels for 8%

profile of v1, /device:TPU:0, one launch (start us, length us, event | category | flops | bytes accessed | tf_op | source)
XLA Modules:
  0.0 254.9 jit_solution(1416744969492755306)
XLA Ops:
  6.5 0.8 copy.10
  7.4 0.0 copy-start
  7.4 1.3 copy-done
  8.7 3.5 %modulated_norm.1 = bf16[128,5120]{1,0:T(8,128)(2,1)} custom-call(bf16[128,5120]{1,0:T(8,128)(2,1)S(1)} %bitcast.66, f32[3,5120]{1,0:T(4,128)S(1)} %bitcast.69), custom_call_target="tpu_custom_call" | custom-call | flops 6553600 | bytes 2621440 | tf_op jit(solution)/shard_map/modulated_norm/pallas_call | solution.py:46
  12.2 0.0 all-gather.2.cloned.1.call-update
  12.3 3.3 %reshape_squeeze.3 = bf16[256,2,8,384]{3,2,1,0:T(8,128)(2,1)} reshape(bf16[1,1,256,2,3072]{4,3,2,1,0:T(2,128)(2,1)S(1)} %copy-done.8) | data formatting | bytes 6291456 | tf_op jit(solution)/shard_map/reshape;squeeze | solution.py:202
  15.6 4.3 %copy.7 = bf16[8,256,2,384]{3,2,1,0:T(2,128)(2,1)S(1)} copy(bf16[8,256,2,384]{3,0,2,1:T(8,128)(2,1)} %bitcast.74) | data formatting | bytes 6291456 | tf_op jit(solution)/shard_map/transpose | solution.py:203
  19.9 3.3 %reshape.31 = bf16[8,256,768]{2,1,0:T(8,128)(2,1)} reshape(bf16[8,256,2,384]{3,2,1,0:T(2,128)(2,1)S(1)} %copy.7) | data formatting | bytes 6291456 | tf_op jit(solution)/shard_map/reshape | solution.py:203
  23.2 5.2 %all-to-all-start = ((bf16[8,256,768]{2,1,0:T(8,128)(2,1)}), bf16[8,256,768]{2,1,0:T(8,128)(2,1)S(1)}, u32[]{:S(2)}, u32[]{:S(2)}) async-start(bf16[8,256,768]{2,1,0:T(8,128)(2,1)} %reshape.31), calls=%async_computation | async-start | bytes 6291456 | tf_op jit(solution)/shard_map/all_to_all | solution.py:204
  28.4 76.0 %all-gather.2.cloned.1.call-done.rows_ref = bf16[1024,5120]{1,0:T(8,128)(2,1)} async-done(((bf16[128,5120]{1,0:T(8,128)(2,1)}), bf16[1024,5120]{1,0:T(8,128)(2,1)}) %all-gather.2.cloned.1.call-update) | async-done | bytes 10485776 | tf_op jit(solution)/shard_map/all_gather | solution.py:198
  104.4 4.0 %copy-done.5 = bf16[1024,5120]{1,0:T(8,128)(2,1)S(1)} copy-done((bf16[1024,5120]{1,0:T(8,128)(2,1)S(1)}, bf16[1024,5120]{1,0:T(8,128)(2,1)}, u32[]{:S(2)}) %copy-start.5) | copy-done | bytes 10485784
  108.4 19.7 %project_heads.1.heads_ref = bf16[1024,1152]{1,0:T(8,128)(2,1)S(1)} custom-call(bf16[1024,5120]{1,0:T(8,128)(2,1)S(1)} %copy-done.5, bf16[3,5120,384]{2,1,0:T(8,128)(2,1)} %bitcast.79), custom_call_target="tpu_custom_call" | custom-call | flops 12079595520 | bytes 22282240 | tf_op jit(solution)/shard_map/project_heads/pallas_call | solution.py:85
  128.1 1.4 copy-done.2
  129.6 1.7 copy-done.3
  131.2 10.1 %attend.1 = bf16[1024,384]{1,0:T(8,128)(2,1)S(1)} custom-call(s32[4,6]{1,0:T(4,128)S(1)} %bitcast.71, bf16[1024,1152]{1,0:T(8,128)(2,1)S(1)} %copy-done.3, bf16[2048,768]{1,0:T(8,128)(2,1)S(1)} %bitcast.65), custom_call_target="tpu_custom_call" | custom-call | flops 1207959552 | bytes 5505024 | tf_op jit(solution)/shard_map/attend/pallas_call | solution.py:160
  141.3 0.1 constant_dynamic-slice_fusion.1
  141.4 3.0 %convolution_convert_fusion.1 = bf16[512,2560]{1,0:T(8,128)(2,1)} fusion(bf16[512,384]{1,0:T(8,128)(2,1)S(1)} %bitcast.77, bf16[1,384,5120]{2,1,0:T(8,128)(2,1)S(1)} %copy-done.6), kind=kOutput, calls=%fused_computation.3 | convolution fusion | flops 1007943680 | bytes 4980736 | tf_op jit(solution)/shard_map/dot_general | solution.py:218
  144.5 0.3 collective-permute-start
  144.7 3.0 %convolution_convert_fusion = bf16[512,2560]{1,0:T(8,128)(2,1)} fusion(bf16[512,384]{1,0:T(8,128)(2,1)S(1)} %bitcast.78, bf16[1,384,5120]{2,1,0:T(8,128)(2,1)S(1)} %copy-done.6), kind=kOutput, calls=%fused_computation.2 | convolution fusion | flops 1007943680 | bytes 4980736 | tf_op jit(solution)/shard_map/dot_general | solution.py:218
  147.8 0.3 collective-permute-start.7
  148.0 0.1 slice_reduce_fusion.1
  148.1 1.6 collective-permute-done
  149.7 3.9 %convert_add_fusion.1 = f32[512,2560]{1,0:T(8,128)S(1)} fusion(bf16[512,2560]{1,0:T(8,128)(2,1)} %collective-permute-done, bf16[512,384]{1,0:T(8,128)(2,1)S(1)} %bitcast.75, bf16[1,384,5120]{2,1,0:T(8,128)(2,1)} %param.9), kind=kOutput, calls=%fused_computation.1 | convolution fusion | flops 1009254400 | bytes 10223616 | tf_op jit(solution)/shard_map/dot_general | solution.py:220
  153.6 0.0 copy-start.7
  153.6 0.5 fusion.32
  154.1 0.1 fusion.23
  154.2 0.6 collective-permute-start.3
  154.8 0.1 fusion.22
  154.8 1.6 collective-permute-start.1
  156.4 0.0 collective-permute-done.7
  156.4 1.6 convert_add_fusion
  158.0 0.5 fusion.33
  158.5 0.1 fusion.25
  158.5 1.5 collective-permute-start.10
  160.1 0.1 fusion.24
  160.2 0.6 collective-permute-start.8
  160.8 11.0 %collective-permute-done.3 = bf16[2,128,1280]{2,1,0:T(8,128)(2,1)S(1)} collective-permute-done((bf16[2,128,1280]{2,1,0:T(8,128)(2,1)S(1)}, bf16[2,128,1280]{2,1,0:T(8,128)(2,1)S(1)}, u32[]{:S(2)}, u32[]{:S(2)}) %collective-permute-start.3) | collective-permute-done | bytes 655392 | tf_op jit(solution)/shard_map/ppermute | solution.py:25
  171.8 0.1 bitcast_add_fusion.2
  172.0 1.5 collective-permute-start.4
  173.5 0.1 bitcast_add_fusion.3
  173.7 0.6 collective-permute-start.2
  174.3 11.6 %collective-permute-done.10 = bf16[2,128,1280]{2,1,0:T(8,128)(2,1)S(1)} collective-permute-done((bf16[2,128,1280]{2,1,0:T(8,128)(2,1)S(1)}, bf16[2,128,1280]{2,1,0:T(8,128)(2,1)S(1)}, u32[]{:S(2)}, u32[]{:S(2)}) %collective-permute-start.10) | collective-permute-done | bytes 655392 | tf_op jit(solution)/shard_map/ppermute | solution.py:25
  185.8 0.1 bitcast_add_fusion
  186.0 1.5 collective-permute-start.11
  187.5 0.1 bitcast_add_fusion.1
  187.7 0.6 collective-permute-start.9
  188.3 5.2 %collective-permute-done.4 = bf16[128,1280]{1,0:T(8,128)(2,1)S(1)} collective-permute-done((bf16[128,1280]{1,0:T(8,128)(2,1)S(1)}, bf16[128,1280]{1,0:T(8,128)(2,1)S(1)}, u32[]{:S(2)}, u32[]{:S(2)}) %collective-permute-start.4) | collective-permute-done | bytes 327712 | tf_op jit(solution)/shard_map/ppermute | solution.py:25
  193.6 0.1 bitcast_add_fusion.6
  193.6 0.1 bitcast_add_fusion.7
  193.7 0.0 copy-start.1
  193.7 5.9 %collective-permute-done.11 = bf16[128,1280]{1,0:T(8,128)(2,1)S(1)} collective-permute-done((bf16[128,1280]{1,0:T(8,128)(2,1)S(1)}, bf16[128,1280]{1,0:T(8,128)(2,1)S(1)}, u32[]{:S(2)}, u32[]{:S(2)}) %collective-permute-start.11) | collective-permute-done | bytes 327712 | tf_op jit(solution)/shard_map/ppermute | solution.py:25
  199.6 0.1 bitcast_add_fusion.4
  199.7 0.1 bitcast_add_fusion.5
  199.7 0.3 fusion.19
  200.1 1.6 collective-permute-start.12
  201.6 1.5 collective-permute-start.5
  203.1 16.5 %collective-permute-done.12 = bf16[128,2560]{1,0:T(8,128)(2,1)S(1)} collective-permute-done((bf16[128,2560]{1,0:T(8,128)(2,1)S(1)}, bf16[128,2560]{1,0:T(8,128)(2,1)S(1)}, u32[]{:S(2)}, u32[]{:S(2)}) %collective-permute-start.12) | collective-permute-done | bytes 655392 | tf_op jit(solution)/shard_map/ppermute | solution.py:20
  219.6 1.5 collective-permute-start.13
  221.1 10.6 %collective-permute-done.5 = bf16[128,2560]{1,0:T(8,128)(2,1)S(1)} collective-permute-done((bf16[128,2560]{1,0:T(8,128)(2,1)S(1)}, bf16[128,2560]{1,0:T(8,128)(2,1)S(1)}, u32[]{:S(2)}, u32[]{:S(2)}) %collective-permute-start.5) | collective-permute-done | bytes 655392 | tf_op jit(solution)/shard_map/ppermute | solution.py:20
  231.7 1.5 collective-permute-start.6
  233.2 0.4 fusion.26
  233.6 12.9 %collective-permute-done.6 = bf16[128,2560]{1,0:T(8,128)(2,1)S(1)} collective-permute-done((bf16[128,2560]{1,0:T(8,128)(2,1)S(1)}, bf16[128,2560]{1,0:T(8,128)(2,1)S(1)}, u32[]{:S(2)}, u32[]{:S(2)}) %collective-permute-start.6) | collective-permute-done | bytes 655392 | tf_op jit(solution)/shard_map/ppermute | solution.py:25
  246.5 0.4 fusion.27
  246.9 1.2 maximum_bitcast_fusion
  (22 shorter events, 0.2 us)
Async XLA Ops:
  6.5 97.9 %all-gather.2.cloned.1.call-start = ((), (), s32[]{:S(2)}) async-start(), calls=%async_computation.1 | async-start | bytes 11796480 | tf_op jit(solution)/shard_map/all_gather | solution.py:198
  7.4 1.3 copy-start
  8.7 3.5 %copy-start.8 = (bf16[1,1,256,2,3072]{4,3,2,1,0:T(2,128)(2,1)S(1)}, bf16[1,1,256,2,3072]{4,3,2,1,0:T(2,128)(2,1)}, u32[]{:S(2)}) copy-start(bf16[1,1,256,2,3072]{4,3,2,1,0:T(2,128)(2,1)} %param.10) | copy-start | bytes 9437188
  23.2 106.4 %all-to-all-start = ((bf16[8,256,768]{2,1,0:T(8,128)(2,1)}), bf16[8,256,768]{2,1,0:T(8,128)(2,1)S(1)}, u32[]{:S(2)}, u32[]{:S(2)}) async-start(bf16[8,256,768]{2,1,0:T(8,128)(2,1)} %reshape.31), calls=%async_computation | async-start | bytes 6291456 | tf_op jit(solution)/shard_map/all_to_all | solution.py:204
  104.4 4.0 %copy-start.5 = (bf16[1024,5120]{1,0:T(8,128)(2,1)S(1)}, bf16[1024,5120]{1,0:T(8,128)(2,1)}, u32[]{:S(2)}) copy-start(bf16[1024,5120]{1,0:T(8,128)(2,1)} %all-gather.2.cloned.1.call-done.rows_ref) | copy-start | bytes 31457284
  108.4 21.2 %copy-start.4 = (s32[1,4,6]{2,1,0:T(4,128)S(1)}, s32[1,4,6]{2,1,0:T(4,128)}, u32[]{:S(2)}) copy-start(s32[1,4,6]{2,1,0:T(4,128)} %param.11) | copy-start | bytes 292
  128.1 1.4 copy-start.2
  129.6 1.7 copy-start.3
  131.2 10.2 %copy-start.6 = (bf16[1,384,5120]{2,1,0:T(8,128)(2,1)S(1)}, bf16[1,384,5120]{2,1,0:T(8,128)(2,1)}, u32[]{:S(2)}) copy-start(bf16[1,384,5120]{2,1,0:T(8,128)(2,1)} %param.9) | copy-start | bytes 11796484
  144.5 5.3 %collective-permute-start = (bf16[512,2560]{1,0:T(8,128)(2,1)}, bf16[512,2560]{1,0:T(8,128)(2,1)}, u32[]{:S(2)}, u32[]{:S(2)}) collective-permute-start(bf16[512,2560]{1,0:T(8,128)(2,1)} %convolution_convert_fusion.1), channel_id=1, source_target_pairs={{0,2},{2,0},{4,6},{6,4},{1,3},{3,1},{5,7},{7,5},{8,10},{10,8},{12,... | collective-permute-start | bytes 7864328 | tf_op jit(solution)/shard_map/ppermute | solution.py:25
  147.8 8.6 %collective-permute-start.7 = (bf16[512,2560]{1,0:T(8,128)(2,1)}, bf16[512,2560]{1,0:T(8,128)(2,1)S(1)}, u32[]{:S(2)}, u32[]{:S(2)}) collective-permute-start(bf16[512,2560]{1,0:T(8,128)(2,1)} %convolution_convert_fusion), channel_id=1, source_target_pairs={{0,2},{2,0},{4,6},{6,4},{1,3},{3,1},{5,7},{7,5},{8,10},{10,8},{12,... | collective-permute-start | bytes 7864328 | tf_op jit(solution)/shard_map/ppermute | solution.py:25
  153.6 2.8 %copy-start.7 = (bf16[1,384,5120]{2,1,0:T(8,128)(2,1)S(1)}, bf16[1,384,5120]{2,1,0:T(8,128)(2,1)}, u32[]{:S(2)}) copy-start(bf16[1,384,5120]{2,1,0:T(8,128)(2,1)} %param.9) | copy-start | bytes 11796484
  154.2 17.6 %collective-permute-start.3 = (bf16[2,128,1280]{2,1,0:T(8,128)(2,1)S(1)}, bf16[2,128,1280]{2,1,0:T(8,128)(2,1)S(1)}, u32[]{:S(2)}, u32[]{:S(2)}) collective-permute-start(bf16[2,128,1280]{2,1,0:T(8,128)(2,1)S(1)} %fusion.23), channel_id=1, source_target_pairs={{0,4},{2,6},{4,0},{6,2},{1,5},{3,7},{5,1},{7,3},{8,12},{10,14},{12... | collective-permute-start | bytes 1966088 | tf_op jit(solution)/shard_map/ppermute | solution.py:25
  154.8 18.7 %collective-permute-start.1 = (bf16[2,128,1280]{2,1,0:T(8,128)(2,1)S(1)}, bf16[2,128,1280]{2,1,0:T(8,128)(2,1)S(1)}, u32[]{:S(2)}, u32[]{:S(2)}) collective-permute-start(bf16[2,128,1280]{2,1,0:T(8,128)(2,1)S(1)} %fusion.22), channel_id=1, source_target_pairs={{0,1},{1,0},{2,3},{3,2},{4,5},{5,4},{6,7},{7,6},{8,9},{9,8},{10,11... | collective-permute-start | bytes 1966088 | tf_op jit(solution)/shard_map/ppermute | solution.py:25
  158.5 27.3 %collective-permute-start.10 = (bf16[2,128,1280]{2,1,0:T(8,128)(2,1)S(1)}, bf16[2,128,1280]{2,1,0:T(8,128)(2,1)S(1)}, u32[]{:S(2)}, u32[]{:S(2)}) collective-permute-start(bf16[2,128,1280]{2,1,0:T(8,128)(2,1)S(1)} %fusion.25), channel_id=1, source_target_pairs={{0,4},{2,6},{4,0},{6,2},{1,5},{3,7},{5,1},{7,3},{8,12},{10,14},{12... | collective-permute-start | bytes 1966088 | tf_op jit(solution)/shard_map/ppermute | solution.py:25
  160.2 27.4 %collective-permute-start.8 = (bf16[2,128,1280]{2,1,0:T(8,128)(2,1)S(1)}, bf16[2,128,1280]{2,1,0:T(8,128)(2,1)S(1)}, u32[]{:S(2)}, u32[]{:S(2)}) collective-permute-start(bf16[2,128,1280]{2,1,0:T(8,128)(2,1)S(1)} %fusion.24), channel_id=1, source_target_pairs={{0,1},{1,0},{2,3},{3,2},{4,5},{5,4},{6,7},{7,6},{8,9},{9,8},{10,11... | collective-permute-start | bytes 1966088 | tf_op jit(solution)/shard_map/ppermute | solution.py:25
  172.0 21.6 %collective-permute-start.4 = (bf16[128,1280]{1,0:T(8,128)(2,1)S(1)}, bf16[128,1280]{1,0:T(8,128)(2,1)S(1)}, u32[]{:S(2)}, u32[]{:S(2)}) collective-permute-start(bf16[128,1280]{1,0:T(8,128)(2,1)S(1)} %fusion.29), channel_id=1, source_target_pairs={{0,1},{1,0},{2,3},{3,2},{4,5},{5,4},{6,7},{7,6},{8,9},{9,8},{10,11... | collective-permute-start | bytes 983048 | tf_op jit(solution)/shard_map/ppermute | solution.py:25
  173.7 20.0 %collective-permute-start.2 = (bf16[128,1280]{1,0:T(8,128)(2,1)S(1)}, bf16[128,1280]{1,0:T(8,128)(2,1)S(1)}, u32[]{:S(2)}, u32[]{:S(2)}) collective-permute-start(bf16[128,1280]{1,0:T(8,128)(2,1)S(1)} %fusion.28), channel_id=1, source_target_pairs={{0,4},{2,6},{4,0},{6,2},{1,5},{3,7},{5,1},{7,3},{8,12},{10,14},{12... | collective-permute-start | bytes 983048 | tf_op jit(solution)/shard_map/ppermute | solution.py:25
  186.0 13.6 %collective-permute-start.11 = (bf16[128,1280]{1,0:T(8,128)(2,1)S(1)}, bf16[128,1280]{1,0:T(8,128)(2,1)S(1)}, u32[]{:S(2)}, u32[]{:S(2)}) collective-permute-start(bf16[128,1280]{1,0:T(8,128)(2,1)S(1)} %fusion.31), channel_id=1, source_target_pairs={{0,1},{1,0},{2,3},{3,2},{4,5},{5,4},{6,7},{7,6},{8,9},{9,8},{10,11... | collective-permute-start | bytes 983048 | tf_op jit(solution)/shard_map/ppermute | solution.py:25
  187.7 11.9 %collective-permute-start.9 = (bf16[128,1280]{1,0:T(8,128)(2,1)S(1)}, bf16[128,1280]{1,0:T(8,128)(2,1)S(1)}, u32[]{:S(2)}, u32[]{:S(2)}) collective-permute-start(bf16[128,1280]{1,0:T(8,128)(2,1)S(1)} %fusion.30), channel_id=1, source_target_pairs={{0,4},{2,6},{4,0},{6,2},{1,5},{3,7},{5,1},{7,3},{8,12},{10,14},{12... | collective-permute-start | bytes 983048 | tf_op jit(solution)/shard_map/ppermute | solution.py:25
  193.7 6.0 %copy-start.1 = (bf16[1,1,128,5120]{3,2,1,0:T(8,128)(2,1)S(1)}, bf16[1,1,128,5120]{3,2,1,0:T(8,128)(2,1)}, u32[]{:S(2)}) copy-start(bf16[1,1,128,5120]{3,2,1,0:T(8,128)(2,1)} %param.6) | copy-start | bytes 3932164
  200.1 19.5 %collective-permute-start.12 = (bf16[128,2560]{1,0:T(8,128)(2,1)S(1)}, bf16[128,2560]{1,0:T(8,128)(2,1)S(1)}, u32[]{:S(2)}, u32[]{:S(2)}) collective-permute-start(bf16[128,2560]{1,0:T(8,128)(2,1)S(1)} %get-tuple-element.12), channel_id=1, source_target_pairs={{0,8},{8,16},{16,24},{24,0},{1,9},{9,17},{17,25},{25,1},{2,10},{10... | collective-permute-start | bytes 1966088 | tf_op jit(solution)/shard_map/ppermute | solution.py:20
  201.6 30.1 %collective-permute-start.5 = (bf16[128,2560]{1,0:T(8,128)(2,1)S(1)}, bf16[128,2560]{1,0:T(8,128)(2,1)S(1)}, u32[]{:S(2)}, u32[]{:S(2)}) collective-permute-start(bf16[128,2560]{1,0:T(8,128)(2,1)S(1)} %get-tuple-element.11), channel_id=1, source_target_pairs={{0,8},{8,16},{16,24},{24,0},{1,9},{9,17},{17,25},{25,1},{2,10},{10... | collective-permute-start | bytes 1966088 | tf_op jit(solution)/shard_map/ppermute | solution.py:20
  219.6 13.6 %collective-permute-start.13 = (bf16[128,2560]{1,0:T(8,128)(2,1)S(1)}, bf16[128,2560]{1,0:T(8,128)(2,1)S(1)}, u32[]{:S(2)}, u32[]{:S(2)}) collective-permute-start(bf16[128,2560]{1,0:T(8,128)(2,1)S(1)} %collective-permute-done.12), channel_id=1, source_target_pairs={{0,1},{1,0},{2,3},{3,2},{4,5},{5,4},{6,7},{7,6},{8,9},{9,8},{10,11... | collective-permute-start | bytes 1966088 | tf_op jit(solution)/shard_map/ppermute | solution.py:25
  231.7 14.8 %collective-permute-start.6 = (bf16[128,2560]{1,0:T(8,128)(2,1)S(1)}, bf16[128,2560]{1,0:T(8,128)(2,1)S(1)}, u32[]{:S(2)}, u32[]{:S(2)}) collective-permute-start(bf16[128,2560]{1,0:T(8,128)(2,1)S(1)} %collective-permute-done.5), channel_id=1, source_target_pairs={{0,1},{1,0},{2,3},{3,2},{4,5},{5,4},{6,7},{7,6},{8,9},{9,8},{10,11... | collective-permute-start | bytes 1966088 | tf_op jit(solution)/shard_map/ppermute | solution.py:25
Sparse Core Ops, SparseCore 0:
  12.4 92.0 all-gather.1

commit v2 on v1

--- a/solution.py
+++ b/solution.py
@@ -54,10 +54,31 @@
     )(rows, modulation)
 
 
-def project_kernel(rows_ref, weights_ref, out_ref, total_ref):
-    step = pl.program_id(0)
+def gate_kernel(value_ref, *refs):
+    pass
+
+
+def after(value, earlier):
+    return pl.pallas_call(
+        gate_kernel,
+        in_specs=[pl.BlockSpec(memory_space=pl.ANY)] * (1 + len(earlier)),
+        out_specs=pl.BlockSpec(memory_space=pl.ANY),
+        out_shape=jax.ShapeDtypeStruct(value.shape, value.dtype),
+        input_output_aliases={0: 0},
+        name="after",
+    )(value, *earlier)
+
+
+def project_kernel(*refs):
+    (*whole_refs, near_first, near_second, far_first, far_second, weights_ref, out_ref, total_ref) = refs
+    step, steps = pl.program_id(0), pl.num_programs(0)
     weights = jnp.concatenate([weights_ref[0], weights_ref[1], weights_ref[2]], axis=1)
-    product = jnp.dot(rows_ref[...], weights, preferred_element_type=jnp.float32)
+    early = step < steps // 2
+    blocks = [ref[...] for ref in whole_refs]
+    blocks.insert(3, jnp.where(early, near_first[...], near_second[...]))
+    blocks.append(jnp.where(early, far_first[...], far_second[...]))
+    rows = jnp.concatenate(blocks, axis=0)
+    product = jnp.dot(rows, weights, preferred_element_type=jnp.float32)
 
     @pl.when(step == 0)
     def _():
@@ -67,7 +88,7 @@
     def _():
         total_ref[...] += product
 
-    @pl.when(step == pl.num_programs(0) - 1)
+    @pl.when(step == steps - 1)
     def _():
         width = weights_ref.shape[2]
         for head in range(2 * width // HD):
@@ -78,28 +99,32 @@
         out_ref[:, 2 * width :] = total_ref[:, 2 * width :].astype(jnp.bfloat16)
 
 
-def project(rows, weights):
-    count, depth = rows.shape
+def project(near, far, weights):
+    rows, depth = near[0].shape
     width = weights.shape[2]
-    block = 1024
+    steps = 4
+    block = depth // steps
+    count = 8 * rows
+    whole = pl.BlockSpec((rows, block), lambda k: (0, k))
+    first = pl.BlockSpec((rows, block), lambda k: (0, jnp.minimum(k, steps // 2 - 1)))
+    second = pl.BlockSpec((rows, block), lambda k: (0, jnp.maximum(k - steps // 2, 0)))
     return pl.pallas_call(
         project_kernel,
-        grid=(depth // block,),
-        in_specs=[
-            pl.BlockSpec((count, block), lambda k: (0, k)),
-            pl.BlockSpec((3, block, width), lambda k: (0, k, 0)),
-        ],
+        grid=(steps,),
+        in_specs=[whole] * 6
+        + [first, second] * 2
+        + [pl.BlockSpec((3, block, width), lambda k: (0, k, 0))],
         out_specs=pl.BlockSpec((count, 3 * width), lambda k: (0, 0)),
         out_shape=jax.ShapeDtypeStruct((count, 3 * width), jnp.bfloat16),
         scratch_shapes=[pltpu.VMEM((count, 3 * width), jnp.float32)],
         name="project_heads",
         cost_estimate=pl.CostEstimate(
             flops=2 * count * depth * 3 * width,
-            bytes_accessed=2 * (rows.size + weights.size),
+            bytes_accessed=2 * (count * depth + weights.size),
             transcendentals=0,
         ),
-        compiler_params=pltpu.CompilerParams(vmem_limit_bytes=40 * MIB),
-    )(rows, weights)
+        compiler_params=pltpu.CompilerParams(vmem_limit_bytes=48 * MIB),
+    )(*near[:3], *far[:3], *near[3:], *far[3:], weights)
 
 
 def attend_kernel(
@@ -123,14 +148,19 @@
     tiles_seen = visible_ref.shape[1]
     tiles_fresh = visible_ref.shape[0]
 
+    mine_high, mine_low = lax.axis_index("sp") // 2, lax.axis_index("sp") % 2
+    mine_branch = lax.axis_index("cfg")
+
     def body(index, carry):
-        tile, branch = index // 2, index % 2
+        high, low = mine_high ^ ((index // 2) % 2), mine_low ^ (index // 4)
+        tile, branch = high * 2 + low, mine_branch ^ (index % 2)
         rows = pl.ds(pl.multiple_of(index * TILE, TILE), TILE)
         starts = []
         for seen in range(tiles_seen):
             number = visible_ref[tile, seen]
             older = number - tiles_fresh
-            fresh = (number * 2 + branch) * TILE
+            fresh = (mine_low ^ (number % 2)) * 4 + (mine_high ^ ((number // 2) % 2)) * 2
+            fresh = (fresh + index % 2) * TILE
             stale = fresh_rows + ((older // 2) * 2 + branch) * 2 * TILE + (older % 2) * TILE
             starts.append(pl.multiple_of(jnp.where(older < 0, fresh, stale), TILE))
         for head in range(width // HD):
@@ -182,37 +212,45 @@
     )(visible, heads, context)
 
 
-def pick(values, index, axis):
-    return lax.dynamic_index_in_dim(values, index, axis, keepdims=False)
-
-
 def per_device(flight, modulation, project_in, project_out, stale_cache, visible):
     current = flight[0, 0]
     modulate = modulation[0, 0]
     token_rows, features = current.shape
     devices = lax.axis_size("sp") * lax.axis_size("cfg")
     branch = lax.axis_index("cfg")
-    high, low = lax.axis_index("sp") // 2, lax.axis_index("sp") % 2
-
-    modulated = modulated_norm(current, modulate)
-    gathered = lax.all_gather(modulated, ("sp", "cfg"), axis=0, tiled=True)
+
+    own = modulated_norm(current, modulate)
+    across = from_partner(own, "cfg", 1)
+    along = from_partner(own, "sp", 2)
+    own_core = from_partner(own, "sp", 1)
+    middle = features // 2
+    first = from_partner(across[:, :middle], "sp", 2)
+    second = from_partner(along[:, middle:], "cfg", 1)
+    across_core = from_partner(across, "sp", 1)
+    along_core = from_partner(along, "sp", 1)
+    first_core = from_partner(first, "sp", 1)
+    second_core = from_partner(second, "sp", 1)
 
     context_rows = stale_cache.shape[2]
     width = project_in.shape[3]
     packed = stale_cache[0, 0].reshape(context_rows, 2, devices, width)
     packed = packed.transpose(2, 0, 1, 3).reshape(devices, context_rows, 2 * width)
+    packed = after(packed, (across, along))
     context = lax.all_to_all(packed, ("sp", "cfg"), split_axis=0, concat_axis=0, tiled=True)
     context = context.reshape(devices * context_rows, 2 * width)
 
-    heads = project(gathered, project_in[0])
+    heads = project(
+        (own, across, along, first, second),
+        (own_core, across_core, along_core, first_core, second_core),
+        project_in[0],
+    )
     attended = attend(heads, context, visible[0])
 
-    blocks = attended.reshape(2, 2, 2, token_rows, width)
-    rows_sent = pick(blocks, 1 - low, 1).reshape(4 * token_rows, width)
-    rows_kept = pick(blocks, low, 1).reshape(4 * token_rows, width)
+    rows_kept, rows_sent = attended[: 4 * token_rows], attended[4 * token_rows :]
     chunk = features // COLUMN_CHUNKS
     half = chunk // 2
     results = []
+    current_columns = current
     for start in range(0, features, chunk):
         weights = project_out[0, :, start : start + chunk]
         sent = jnp.dot(rows_sent, weights, preferred_element_type=jnp.float32)
@@ -221,20 +259,21 @@
         kept = (kept + received.astype(jnp.float32)).reshape(2, 2, token_rows, chunk)
 
         first, second = kept[..., :half], kept[..., half:]
-        first_in = from_partner(pick(first, 1 - branch, 1).astype(jnp.bfloat16), "cfg", 1)
-        second_in = from_partner(pick(second, 1 - high, 0).astype(jnp.bfloat16), "sp", 2)
-        first = pick(first, branch, 1) + first_in.astype(jnp.float32)
-        second = pick(second, high, 0) + second_in.astype(jnp.float32)
-        first_in = from_partner(pick(first, 1 - high, 0).astype(jnp.bfloat16), "sp", 2)
-        second_in = from_partner(pick(second, 1 - branch, 0).astype(jnp.bfloat16), "cfg", 1)
-        first = pick(first, high, 0) + first_in.astype(jnp.float32)
-        second = pick(second, branch, 0) + second_in.astype(jnp.float32)
+        first_in = from_partner(first[:, 1].astype(jnp.bfloat16), "cfg", 1)
+        second_in = from_partner(second[1].astype(jnp.bfloat16), "sp", 2)
+        first = first[:, 0] + first_in.astype(jnp.float32)
+        second = second[0] + second_in.astype(jnp.float32)
+        first_in = from_partner(first[1].astype(jnp.bfloat16), "sp", 2)
+        second_in = from_partner(second[1].astype(jnp.bfloat16), "cfg", 1)
+        first = first[0] + first_in.astype(jnp.float32)
+        second = second[0] + second_in.astype(jnp.float32)
         mixed_sum = jnp.concatenate([first, second], axis=1)
 
         columns = slice(start, start + chunk)
         layer_out = (
-            current[:, columns].astype(jnp.float32) + modulate[2, columns] * mixed_sum
+            current_columns[:, columns].astype(jnp.float32) + modulate[2, columns] * mixed_sum
         ).astype(jnp.bfloat16)
+        current_columns, layer_out = lax.optimization_barrier((current_columns, layer_out))
         arrived = from_behind(layer_out, "pipe", 1)
         partner = from_partner(arrived, "cfg", 1)
         cond_rows = jnp.where(branch == 1, arrived, partner).astype(jnp.float32)

time: 255 us -> 225 us (0.88)
  waiting for transfers between devices: 151 us -> 121 us
  between operations: 13.6 us -> 0.27 us
  starting transfers between devices: 20.4 us -> 30.3 us
  local copies, waits for them, and re-layouts: 21.8 us -> 29.8 us
  matrix products: 11.5 us -> 6.16 us
    all_gather x1 -> x0, waiting for transfers between devices: 76 us -> none  [per_device(): gathered = lax.all_gather(modulated, ('sp', 'cfg'), axis=0, tiled=True)]
    ppermute x12 -> x21, waiting for transfers between devices: 48.2 us -> 99.1 us  [from_partner(): return lax.ppermute(value, axis, pairs)]
    ppermute x12 -> x21, starting transfers between devices: 12.2 us -> 23.4 us  [from_partner(): return lax.ppermute(value, axis, pairs)]
    another operation x1 -> x2, local copies, waits for them, and re-layouts: 3.31 us -> 13.9 us  [per_device(): packed = stale_cache[0, 0].reshape(context_rows, 2, devices, width)]
    ppermute x2, waiting for transfers between devices: 27.1 us -> 21.5 us  [from_behind(): return lax.ppermute(x, axis, [(i, (i + by) % count) for i in range(count)])]
    reshape x1, local copies, waits for them, and re-layouts: 3.31 us -> 8.03 us  [per_device(): packed.transpose(2, 0, 1, 3).reshape(devices, context_rows, 2 * width)]
    transpose x1 -> x0, local copies, waits for them, and re-layouts: 4.31 us -> none  [per_device(): packed.transpose(2, 0, 1, 3).reshape(devices, context_rows, 2 * width)]
    unnamed x19 -> x25, local copies, waits for them, and re-layouts: 9.26 us -> 6.09 us
  transfers between devices with their start and end apart: 16 -> 24, of which waited for: 9 -> 17; matrix products, arithmetic and copies ran while one was open for 9% -> 14% of each run, Pallas kernels for 8% -> 9%
where the time goes in v2:
time: 225 us
  waiting for transfers between devices  121 us (54%)
  Pallas kernels  33.9 us (15%)
  starting transfers between devices  30.3 us (13%)
  local copies, waits for them, and re-layouts  29.8 us (13%)
  matrix products  6.16 us (3%)
  other arithmetic  3.68 us (2%)
    ppermute x21, waiting for transfers between devices, from_partner(): return lax.ppermute(value, axis, pairs)  99.1 us
    ppermute x21, starting transfers between devices, from_partner(): return lax.ppermute(value, axis, pairs)  23.4 us
    ppermute x2, waiting for transfers between devices, from_behind(): return lax.ppermute(x, axis, [(i, (i + by) % count) for i in range(count)])  21.5 us
    pallas_call x1, Pallas kernels, project(): pl.pallas_call(project_kernel, grid=(steps,), in_specs=[whole] * 6 + [fir...  21 us
    another operation x2, local copies, waits for them, and re-layouts, per_device(): packed = stale_cache[0, 0].reshape(context_rows, 2, devices, width)  13.9 us
    pallas_call x1, Pallas kernels, attend(): pl.pallas_call(attend_kernel, in_specs=[pl.BlockSpec(memory_space=pltpu.S...  10.5 us
    reshape x1, local copies, waits for them, and re-layouts, per_device(): packed.transpose(2, 0, 1, 3).reshape(devices, context_rows, 2 * width)  8.03 us
    unnamed x25, local copies, waits for them, and re-layouts  6.09 us
  transfers between devices with their start and end apart: 24, of which 17 were waited for; matrix products, arithmetic and copies ran while one was open for 14% of the time, Pallas kernels for 9%

profile of v2, /device:TPU:0, one launch (start us, length us, event | category | flops | bytes accessed | tf_op | source)
XLA Modules:
  0.0 224.8 jit_solution(18329541524914791679)
XLA Ops:
  0.0 0.8 copy.20
  0.9 1.3 copy-done
  2.2 2.5 %modulated_norm.1.refs_0_ = bf16[128,5120]{1,0:T(8,128)(2,1)S(1)} custom-call(bf16[128,5120]{1,0:T(8,128)(2,1)S(1)} %bitcast.77, f32[3,5120]{1,0:T(4,128)S(1)} %bitcast.80), custom_call_target="tpu_custom_call" | custom-call | flops 6553600 | bytes 2621440 | tf_op jit(solution)/shard_map/modulated_norm/pallas_call | solution.py:46
  4.6 3.0 %collective-permute-start.1 = (bf16[128,5120]{1,0:T(8,128)(2,1)S(1)}, bf16[128,5120]{1,0:T(8,128)(2,1)}, u32[]{:S(2)}, u32[]{:S(2)}) collective-permute-start(bf16[128,5120]{1,0:T(8,128)(2,1)S(1)} %modulated_norm.1.refs_0_), channel_id=1, source_target_pairs={{0,4},{2,6},{4,0},{6,2},{1,5},{3,7},{5,1},{7,3},{8,12},{10,14},{12... | collective-permute-start | bytes 3932168 | tf_op jit(solution)/shard_map/ppermute | solution.py:25
  7.7 1.5 collective-permute-start
  9.2 8.0 %reshape_squeeze.3 = bf16[256,2,8,384]{3,2,1,0:T(8,128)(2,1)} reshape(bf16[1,1,256,2,3072]{4,3,2,1,0:T(2,128)(2,1)} %param.10) | data formatting | bytes 6291456 | tf_op jit(solution)/shard_map/reshape;squeeze | solution.py:236
  17.2 5.9 %copy.19 = bf16[256,2,8,384]{3,1,0,2:T(2,128)(2,1)} copy(bf16[256,2,8,384]{3,2,1,0:T(8,128)(2,1)} %reshape_squeeze.3) | data formatting | bytes 6291456 | tf_op jit(solution)/shard_map/reshape;squeeze | solution.py:236
  23.1 8.0 %reshape.20.value_ref = bf16[8,256,768]{2,1,0:T(8,128)(2,1)} reshape(bf16[8,256,2,384]{3,2,1,0:T(2,128)(2,1)} %bitcast.87) | data formatting | bytes 6291456 | tf_op jit(solution)/shard_map/reshape | solution.py:237
  31.1 5.4 %collective-permute-done.1.refs_2_.refs_1_ = bf16[128,5120]{1,0:T(8,128)(2,1)} collective-permute-done((bf16[128,5120]{1,0:T(8,128)(2,1)S(1)}, bf16[128,5120]{1,0:T(8,128)(2,1)}, u32[]{:S(2)}, u32[]{:S(2)}) %collective-permute-start.1) | collective-permute-done | bytes 1310752 | tf_op jit(solution)/shard_map/ppermute | solution.py:25
  36.6 1.4 collective-permute-done.refs_1_.refs_0_
  37.9 1.1 copy-done.2
  39.0 3.6 %all-to-all-start = ((bf16[8,256,768]{2,1,0:T(8,128)(2,1)}), bf16[8,256,768]{2,1,0:T(8,128)(2,1)S(1)}, u32[]{:S(2)}, u32[]{:S(2)}) async-start(bf16[8,256,768]{2,1,0:T(8,128)(2,1)} %after.1), calls=%async_computation | async-start | bytes 6291456 | tf_op jit(solution)/shard_map/all_to_all | solution.py:239
  42.7 0.4 collective-permute-start.2
  43.1 1.3 slice.127
  44.4 1.7 collective-permute-start.6
  46.2 1.6 collective-permute-start.5
  47.7 0.5 collective-permute-start.3
  48.2 45.4 %collective-permute-done.6.refs_7_ = bf16[128,2560]{1,0:T(8,128)(2,1)S(1)} collective-permute-done((bf16[128,2560]{1,0:T(8,128)(2,1)S(1)}, bf16[128,2560]{1,0:T(8,128)(2,1)S(1)}, u32[]{:S(2)}, u32[]{:S(2)}) %collective-permute-start.6) | collective-permute-done | bytes 655392 | tf_op jit(solution)/shard_map/ppermute | solution.py:25
  93.6 0.5 collective-permute-start.7
  94.1 1.6 collective-permute-done.8.refs_9_
  95.7 0.9 collective-permute-done.7.refs_8_
  96.7 1.0 copy-done.11
  97.8 21.0 %project_heads.1.heads_ref = bf16[1024,1152]{1,0:T(8,128)(2,1)} custom-call(bf16[128,5120]{1,0:T(8,128)(2,1)S(1)} %copy-done.6, bf16[128,5120]{1,0:T(8,128)(2,1)S(1)} %copy-done.3, bf16[128,5120]{1,0:T(8,128)(2,1)} %collective-permute-done.1.refs_2_.refs_1_, bf16[128,5120]{1,0:T(8,128)(2,1)} %copy-done.9, bf16[128,5120]{1,0:T(8,128)(2,1)} %copy-done.11, ...), custom_call_target="tpu_custom_call" | custom-call | flops 12079595520 | bytes 22282240 | tf_op jit(solution)/shard_map/project_heads/pallas_call | solution.py:111
  118.8 1.7 copy-done.4
  120.4 10.5 %attend.1 = bf16[1024,384]{1,0:T(8,128)(2,1)S(1)} custom-call(s32[4,6]{1,0:T(4,128)S(1)} %bitcast.82, bf16[1024,1152]{1,0:T(8,128)(2,1)S(1)} %copy-done.4, bf16[2048,768]{1,0:T(8,128)(2,1)S(1)} %bitcast.76), custom_call_target="tpu_custom_call" | custom-call | flops 1207959552 | bytes 5505024 | tf_op jit(solution)/shard_map/attend/pallas_call | solution.py:190
  130.9 1.5 convolution_convert_fusion.1
  132.5 0.2 collective-permute-start.9
  132.7 1.5 convolution_convert_fusion
  134.2 0.4 collective-permute-start.16
  134.7 2.7 %collective-permute-done.9 = bf16[512,2560]{1,0:T(8,128)(2,1)S(1)} collective-permute-done((bf16[512,2560]{1,0:T(8,128)(2,1)S(1)}, bf16[512,2560]{1,0:T(8,128)(2,1)S(1)}, u32[]{:S(2)}, u32[]{:S(2)}) %collective-permute-start.9) | collective-permute-done | bytes 2621472 | tf_op jit(solution)/shard_map/ppermute | solution.py:25
  137.4 1.6 convert_add_fusion.1
  139.0 0.3 convert.20
  139.4 0.6 collective-permute-start.10
  140.0 1.6 collective-permute-start.12
  141.6 1.5 convert_add_fusion
  143.1 0.3 convert.23
  143.4 1.6 collective-permute-start.17
  145.1 0.6 collective-permute-start.19
  145.7 11.3 %collective-permute-done.10 = bf16[2,128,1280]{2,1,0:T(8,128)(2,1)S(1)} collective-permute-done((bf16[2,128,1280]{2,1,0:T(8,128)(2,1)S(1)}, bf16[2,128,1280]{2,1,0:T(8,128)(2,1)S(1)}, u32[]{:S(2)}, u32[]{:S(2)}) %collective-permute-start.10) | collective-permute-done | bytes 655392 | tf_op jit(solution)/shard_map/ppermute | solution.py:25
  157.0 0.7 collective-permute-done.12
  157.7 0.3 fusion.15
  158.0 1.6 collective-permute-start.13
  159.6 1.6 collective-permute-start.11
  161.2 9.9 %collective-permute-done.17 = bf16[2,128,1280]{2,1,0:T(8,128)(2,1)S(1)} collective-permute-done((bf16[2,128,1280]{2,1,0:T(8,128)(2,1)S(1)}, bf16[2,128,1280]{2,1,0:T(8,128)(2,1)S(1)}, u32[]{:S(2)}, u32[]{:S(2)}) %collective-permute-start.17) | collective-permute-done | bytes 655392 | tf_op jit(solution)/shard_map/ppermute | solution.py:25
  171.1 0.7 collective-permute-done.19
  171.7 0.4 fusion.13
  172.1 1.6 collective-permute-start.20
  173.8 1.6 collective-permute-start.18
  175.3 2.8 %collective-permute-done.13 = bf16[128,1280]{1,0:T(8,128)(2,1)S(1)} collective-permute-done((bf16[128,1280]{1,0:T(8,128)(2,1)S(1)}, bf16[128,1280]{1,0:T(8,128)(2,1)S(1)}, u32[]{:S(2)}, u32[]{:S(2)}) %collective-permute-start.13) | collective-permute-done | bytes 327712 | tf_op jit(solution)/shard_map/ppermute | solution.py:25
  178.1 0.6 collective-permute-done.11
  178.8 0.2 fusion.17
  179.0 1.6 collective-permute-start.14
  180.6 3.7 %collective-permute-done.20 = bf16[128,1280]{1,0:T(8,128)(2,1)S(1)} collective-permute-done((bf16[128,1280]{1,0:T(8,128)(2,1)S(1)}, bf16[128,1280]{1,0:T(8,128)(2,1)S(1)}, u32[]{:S(2)}, u32[]{:S(2)}) %collective-permute-start.20) | collective-permute-done | bytes 327712 | tf_op jit(solution)/shard_map/ppermute | solution.py:25
  184.4 0.3 collective-permute-done.18
  184.7 0.2 fusion.19
  184.9 1.6 collective-permute-start.21
  186.5 12.0 %collective-permute-done.14 = bf16[128,2560]{1,0:T(8,128)(2,1)S(1)} collective-permute-done((bf16[128,2560]{1,0:T(8,128)(2,1)S(1)}, bf16[128,2560]{1,0:T(8,128)(2,1)S(1)}, u32[]{:S(2)}, u32[]{:S(2)}) %collective-permute-start.14) | collective-permute-done | bytes 655392 | tf_op jit(solution)/shard_map/ppermute | solution.py:20
  198.5 1.5 collective-permute-start.15
  200.0 9.5 %collective-permute-done.21 = bf16[128,2560]{1,0:T(8,128)(2,1)S(1)} collective-permute-done((bf16[128,2560]{1,0:T(8,128)(2,1)S(1)}, bf16[128,2560]{1,0:T(8,128)(2,1)S(1)}, u32[]{:S(2)}, u32[]{:S(2)}) %collective-permute-start.21) | collective-permute-done | bytes 655392 | tf_op jit(solution)/shard_map/ppermute | solution.py:20
  209.5 1.5 collective-permute-start.22
  211.0 0.4 fusion.21
  211.3 11.9 %collective-permute-done.22 = bf16[128,2560]{1,0:T(8,128)(2,1)S(1)} collective-permute-done((bf16[128,2560]{1,0:T(8,128)(2,1)S(1)}, bf16[128,2560]{1,0:T(8,128)(2,1)S(1)}, u32[]{:S(2)}, u32[]{:S(2)}) %collective-permute-start.22) | collective-permute-done | bytes 655392 | tf_op jit(solution)/shard_map/ppermute | solution.py:25
  223.2 0.4 fusion.20
  223.6 1.2 maximum_bitcast_fusion
  (44 shorter events, 0.8 us)
Async XLA Ops:
  0.9 1.3 copy-start
  4.6 12.5 %copy-start.5 = (bf16[128,5120]{1,0:T(8,128)(2,1)}, bf16[128,5120]{1,0:T(8,128)(2,1)S(1)}, u32[]{:S(2)}) copy-start(bf16[128,5120]{1,0:T(8,128)(2,1)S(1)} %modulated_norm.1.refs_0_) | copy-start | bytes 3932164
  4.6 31.9 %collective-permute-start.1 = (bf16[128,5120]{1,0:T(8,128)(2,1)S(1)}, bf16[128,5120]{1,0:T(8,128)(2,1)}, u32[]{:S(2)}, u32[]{:S(2)}) collective-permute-start(bf16[128,5120]{1,0:T(8,128)(2,1)S(1)} %modulated_norm.1.refs_0_), channel_id=1, source_target_pairs={{0,4},{2,6},{4,0},{6,2},{1,5},{3,7},{5,1},{7,3},{8,12},{10,14},{12... | collective-permute-start | bytes 3932168 | tf_op jit(solution)/shard_map/ppermute | solution.py:25
  7.7 30.2 %collective-permute-start = (bf16[128,5120]{1,0:T(8,128)(2,1)S(1)}, bf16[128,5120]{1,0:T(8,128)(2,1)S(1)}, u32[]{:S(2)}, u32[]{:S(2)}) collective-permute-start(bf16[128,5120]{1,0:T(8,128)(2,1)S(1)} %modulated_norm.1.refs_0_), channel_id=1, source_target_pairs={{0,1},{1,0},{2,3},{3,2},{4,5},{5,4},{6,7},{7,6},{8,9},{9,8},{10,11... | collective-permute-start | bytes 3932168 | tf_op jit(solution)/shard_map/ppermute | solution.py:25
  37.9 1.1 copy-start.2
  39.0 79.8 %all-to-all-start = ((bf16[8,256,768]{2,1,0:T(8,128)(2,1)}), bf16[8,256,768]{2,1,0:T(8,128)(2,1)S(1)}, u32[]{:S(2)}, u32[]{:S(2)}) async-start(bf16[8,256,768]{2,1,0:T(8,128)(2,1)} %after.1), calls=%async_computation | async-start | bytes 6291456 | tf_op jit(solution)/shard_map/all_to_all | solution.py:239
  42.7 3.5 %copy-start.3 = (bf16[128,5120]{1,0:T(8,128)(2,1)S(1)}, bf16[128,5120]{1,0:T(8,128)(2,1)}, u32[]{:S(2)}) copy-start(bf16[128,5120]{1,0:T(8,128)(2,1)} %copy-done.2) | copy-start | bytes 3932164
  42.7 55.1 %copy-start.6 = (bf16[128,5120]{1,0:T(8,128)(2,1)S(1)}, bf16[128,5120]{1,0:T(8,128)(2,1)}, u32[]{:S(2)}) copy-start(bf16[128,5120]{1,0:T(8,128)(2,1)} %copy-done.5) | copy-start | bytes 3932164
  42.7 51.4 %collective-permute-start.2 = (bf16[128,5120]{1,0:T(8,128)(2,1)}, bf16[128,5120]{1,0:T(8,128)(2,1)S(1)}, u32[]{:S(2)}, u32[]{:S(2)}) collective-permute-start(bf16[128,5120]{1,0:T(8,128)(2,1)} %copy-done.5), channel_id=1, source_target_pairs={{0,2},{2,0},{4,6},{6,4},{1,3},{3,1},{5,7},{7,5},{8,10},{10,8},{12,... | collective-permute-start | bytes 3932168 | tf_op jit(solution)/shard_map/ppermute | solution.py:25
  44.4 49.2 %collective-permute-start.6 = (bf16[128,2560]{1,0:T(8,128)(2,1)S(1)}, bf16[128,2560]{1,0:T(8,128)(2,1)S(1)}, u32[]{:S(2)}, u32[]{:S(2)}) collective-permute-start(bf16[128,2560]{1,0:T(8,128)(2,1)S(1)} %slice.127), channel_id=1, source_target_pairs={{0,1},{1,0},{2,3},{3,2},{4,5},{5,4},{6,7},{7,6},{8,9},{9,8},{10,11... | collective-permute-start | bytes 1966088 | tf_op jit(solution)/shard_map/ppermute | solution.py:25
  46.2 47.4 %collective-permute-start.5 = (bf16[128,2560]{1,0:T(8,128)(2,1)S(1)}, bf16[128,2560]{1,0:T(8,128)(2,1)S(1)}, u32[]{:S(2)}, u32[]{:S(2)}) collective-permute-start(bf16[128,2560]{1,0:T(8,128)(2,1)S(1)} %slice.126), channel_id=1, source_target_pairs={{0,4},{2,6},{4,0},{6,2},{1,5},{3,7},{5,1},{7,3},{8,12},{10,14},{12... | collective-permute-start | bytes 1966088 | tf_op jit(solution)/shard_map/ppermute | solution.py:25
  47.7 48.0 %collective-permute-start.4 = (bf16[128,5120]{1,0:T(8,128)(2,1)}, bf16[128,5120]{1,0:T(8,128)(2,1)S(1)}, u32[]{:S(2)}, u32[]{:S(2)}) collective-permute-start(bf16[128,5120]{1,0:T(8,128)(2,1)} %collective-permute-done.1.refs_2_.refs_1_), channel_id=1, source_target_pairs={{0,2},{2,0},{4,6},{6,4},{1,3},{3,1},{5,7},{7,5},{8,10},{10,8},{12,... | collective-permute-start | bytes 3932168 | tf_op jit(solution)/shard_map/ppermute | solution.py:25
  47.7 48.9 %collective-permute-start.3 = (bf16[128,5120]{1,0:T(8,128)(2,1)S(1)}, bf16[128,5120]{1,0:T(8,128)(2,1)S(1)}, u32[]{:S(2)}, u32[]{:S(2)}) collective-permute-start(bf16[128,5120]{1,0:T(8,128)(2,1)S(1)} %copy-done.3), channel_id=1, source_target_pairs={{0,2},{2,0},{4,6},{6,4},{1,3},{3,1},{5,7},{7,5},{8,10},{10,8},{12,... | collective-permute-start | bytes 3932168 | tf_op jit(solution)/shard_map/ppermute | solution.py:25
  93.6 2.1 collective-permute-start.8
  93.6 3.0 %collective-permute-start.7 = (bf16[128,2560]{1,0:T(8,128)(2,1)S(1)}, bf16[128,2560]{1,0:T(8,128)(2,1)S(1)}, u32[]{:S(2)}, u32[]{:S(2)}) collective-permute-start(bf16[128,2560]{1,0:T(8,128)(2,1)S(1)} %collective-permute-done.5.refs_6_), channel_id=1, source_target_pairs={{0,2},{2,0},{4,6},{6,4},{1,3},{3,1},{5,7},{7,5},{8,10},{10,8},{12,... | collective-permute-start | bytes 1966088 | tf_op jit(solution)/shard_map/ppermute | solution.py:25
  94.1 2.5 %copy-start.9 = (bf16[128,5120]{1,0:T(8,128)(2,1)}, bf16[128,5120]{1,0:T(8,128)(2,1)S(1)}, u32[]{:S(2)}) copy-start(bf16[128,5120]{1,0:T(8,128)(2,1)S(1)} %collective-permute-done.2.refs_3_) | copy-start | bytes 3932164
  95.7 1.1 copy-start.10
  96.6 1.2 copy-start.11
  97.8 21.0 %copy-start.7 = (s32[1,4,6]{2,1,0:T(4,128)S(1)}, s32[1,4,6]{2,1,0:T(4,128)}, u32[]{:S(2)}) copy-start(s32[1,4,6]{2,1,0:T(4,128)} %param.11) | copy-start | bytes 292
  118.8 1.7 copy-start.4
  120.4 10.5 %copy-start.8 = (bf16[1,384,5120]{2,1,0:T(8,128)(2,1)S(1)}, bf16[1,384,5120]{2,1,0:T(8,128)(2,1)}, u32[]{:S(2)}) copy-start(bf16[1,384,5120]{2,1,0:T(8,128)(2,1)} %param.9) | copy-start | bytes 11796484
  132.5 5.0 %collective-permute-start.9 = (bf16[512,2560]{1,0:T(8,128)(2,1)S(1)}, bf16[512,2560]{1,0:T(8,128)(2,1)S(1)}, u32[]{:S(2)}, u32[]{:S(2)}) collective-permute-start(bf16[512,2560]{1,0:T(8,128)(2,1)S(1)} %convolution_convert_fusion.1), channel_id=1, source_target_pairs={{0,2},{2,0},{4,6},{6,4},{1,3},{3,1},{5,7},{7,5},{8,10},{10,8},{12,... | collective-permute-start | bytes 7864328 | tf_op jit(solution)/shard_map/ppermute | solution.py:25
  134.2 7.4 %collective-permute-start.16 = (bf16[512,2560]{1,0:T(8,128)(2,1)S(1)}, bf16[512,2560]{1,0:T(8,128)(2,1)S(1)}, u32[]{:S(2)}, u32[]{:S(2)}) collective-permute-start(bf16[512,2560]{1,0:T(8,128)(2,1)S(1)} %convolution_convert_fusion), channel_id=1, source_target_pairs={{0,2},{2,0},{4,6},{6,4},{1,3},{3,1},{5,7},{7,5},{8,10},{10,8},{12,... | collective-permute-start | bytes 7864328 | tf_op jit(solution)/shard_map/ppermute | solution.py:25
  139.4 17.6 %collective-permute-start.10 = (bf16[2,128,1280]{2,1,0:T(8,128)(2,1)S(1)}, bf16[2,128,1280]{2,1,0:T(8,128)(2,1)S(1)}, u32[]{:S(2)}, u32[]{:S(2)}) collective-permute-start(bf16[2,128,1280]{2,1,0:T(8,128)(2,1)S(1)} %slice_bitcast_fusion.11), channel_id=1, source_target_pairs={{0,1},{1,0},{2,3},{3,2},{4,5},{5,4},{6,7},{7,6},{8,9},{9,8},{10,11... | collective-permute-start | bytes 1966088 | tf_op jit(solution)/shard_map/ppermute | solution.py:25
  140.0 17.7 %collective-permute-start.12 = (bf16[2,128,1280]{2,1,0:T(8,128)(2,1)S(1)}, bf16[2,128,1280]{2,1,0:T(8,128)(2,1)S(1)}, u32[]{:S(2)}, u32[]{:S(2)}) collective-permute-start(bf16[2,128,1280]{2,1,0:T(8,128)(2,1)S(1)} %slice_bitcast_fusion.9), channel_id=1, source_target_pairs={{0,4},{2,6},{4,0},{6,2},{1,5},{3,7},{5,1},{7,3},{8,12},{10,14},{12... | collective-permute-start | bytes 1966088 | tf_op jit(solution)/shard_map/ppermute | solution.py:25
  143.4 27.6 %collective-permute-start.17 = (bf16[2,128,1280]{2,1,0:T(8,128)(2,1)S(1)}, bf16[2,128,1280]{2,1,0:T(8,128)(2,1)S(1)}, u32[]{:S(2)}, u32[]{:S(2)}) collective-permute-start(bf16[2,128,1280]{2,1,0:T(8,128)(2,1)S(1)} %slice_bitcast_fusion.7), channel_id=1, source_target_pairs={{0,1},{1,0},{2,3},{3,2},{4,5},{5,4},{6,7},{7,6},{8,9},{9,8},{10,11... | collective-permute-start | bytes 1966088 | tf_op jit(solution)/shard_map/ppermute | solution.py:25
  145.1 26.7 %collective-permute-start.19 = (bf16[2,128,1280]{2,1,0:T(8,128)(2,1)S(1)}, bf16[2,128,1280]{2,1,0:T(8,128)(2,1)S(1)}, u32[]{:S(2)}, u32[]{:S(2)}) collective-permute-start(bf16[2,128,1280]{2,1,0:T(8,128)(2,1)S(1)} %slice_bitcast_fusion.5), channel_id=1, source_target_pairs={{0,4},{2,6},{4,0},{6,2},{1,5},{3,7},{5,1},{7,3},{8,12},{10,14},{12... | collective-permute-start | bytes 1966088 | tf_op jit(solution)/shard_map/ppermute | solution.py:25
  158.0 20.1 %collective-permute-start.13 = (bf16[128,1280]{1,0:T(8,128)(2,1)S(1)}, bf16[128,1280]{1,0:T(8,128)(2,1)S(1)}, u32[]{:S(2)}, u32[]{:S(2)}) collective-permute-start(bf16[128,1280]{1,0:T(8,128)(2,1)S(1)} %fusion.31), channel_id=1, source_target_pairs={{0,1},{1,0},{2,3},{3,2},{4,5},{5,4},{6,7},{7,6},{8,9},{9,8},{10,11... | collective-permute-start | bytes 983048 | tf_op jit(solution)/shard_map/ppermute | solution.py:25
  159.6 19.1 %collective-permute-start.11 = (bf16[128,1280]{1,0:T(8,128)(2,1)S(1)}, bf16[128,1280]{1,0:T(8,128)(2,1)S(1)}, u32[]{:S(2)}, u32[]{:S(2)}) collective-permute-start(bf16[128,1280]{1,0:T(8,128)(2,1)S(1)} %fusion.30), channel_id=1, source_target_pairs={{0,4},{2,6},{4,0},{6,2},{1,5},{3,7},{5,1},{7,3},{8,12},{10,14},{12... | collective-permute-start | bytes 983048 | tf_op jit(solution)/shard_map/ppermute | solution.py:25
  172.1 12.2 %collective-permute-start.20 = (bf16[128,1280]{1,0:T(8,128)(2,1)S(1)}, bf16[128,1280]{1,0:T(8,128)(2,1)S(1)}, u32[]{:S(2)}, u32[]{:S(2)}) collective-permute-start(bf16[128,1280]{1,0:T(8,128)(2,1)S(1)} %fusion.33), channel_id=1, source_target_pairs={{0,1},{1,0},{2,3},{3,2},{4,5},{5,4},{6,7},{7,6},{8,9},{9,8},{10,11... | collective-permute-start | bytes 983048 | tf_op jit(solution)/shard_map/ppermute | solution.py:25
  173.8 5.0 %copy-start.1 = (bf16[1,1,128,5120]{3,2,1,0:T(8,128)(2,1)S(1)}, bf16[1,1,128,5120]{3,2,1,0:T(8,128)(2,1)}, u32[]{:S(2)}) copy-start(bf16[1,1,128,5120]{3,2,1,0:T(8,128)(2,1)} %param.6) | copy-start | bytes 3932164
  173.8 10.9 %collective-permute-start.18 = (bf16[128,1280]{1,0:T(8,128)(2,1)S(1)}, bf16[128,1280]{1,0:T(8,128)(2,1)S(1)}, u32[]{:S(2)}, u32[]{:S(2)}) collective-permute-start(bf16[128,1280]{1,0:T(8,128)(2,1)S(1)} %fusion.32), channel_id=1, source_target_pairs={{0,4},{2,6},{4,0},{6,2},{1,5},{3,7},{5,1},{7,3},{8,12},{10,14},{12... | collective-permute-start | bytes 983048 | tf_op jit(solution)/shard_map/ppermute | solution.py:25
  179.0 19.5 %collective-permute-start.14 = (bf16[128,2560]{1,0:T(8,128)(2,1)S(1)}, bf16[128,2560]{1,0:T(8,128)(2,1)S(1)}, u32[]{:S(2)}, u32[]{:S(2)}) collective-permute-start(bf16[128,2560]{1,0:T(8,128)(2,1)S(1)} %fusion.17), channel_id=1, source_target_pairs={{0,8},{8,16},{16,24},{24,0},{1,9},{9,17},{17,25},{25,1},{2,10},{10... | collective-permute-start | bytes 1966088 | tf_op jit(solution)/shard_map/ppermute | solution.py:20
  184.9 24.6 %collective-permute-start.21 = (bf16[128,2560]{1,0:T(8,128)(2,1)S(1)}, bf16[128,2560]{1,0:T(8,128)(2,1)S(1)}, u32[]{:S(2)}, u32[]{:S(2)}) collective-permute-start(bf16[128,2560]{1,0:T(8,128)(2,1)S(1)} %fusion.19), channel_id=1, source_target_pairs={{0,8},{8,16},{16,24},{24,0},{1,9},{9,17},{17,25},{25,1},{2,10},{10... | collective-permute-start | bytes 1966088 | tf_op jit(solution)/shard_map/ppermute | solution.py:20
  198.5 12.5 %collective-permute-start.15 = (bf16[128,2560]{1,0:T(8,128)(2,1)S(1)}, bf16[128,2560]{1,0:T(8,128)(2,1)S(1)}, u32[]{:S(2)}, u32[]{:S(2)}) collective-permute-start(bf16[128,2560]{1,0:T(8,128)(2,1)S(1)} %collective-permute-done.14), channel_id=1, source_target_pairs={{0,1},{1,0},{2,3},{3,2},{4,5},{5,4},{6,7},{7,6},{8,9},{9,8},{10,11... | collective-permute-start | bytes 1966088 | tf_op jit(solution)/shard_map/ppermute | solution.py:25
  209.5 13.7 %collective-permute-start.22 = (bf16[128,2560]{1,0:T(8,128)(2,1)S(1)}, bf16[128,2560]{1,0:T(8,128)(2,1)S(1)}, u32[]{:S(2)}, u32[]{:S(2)}) collective-permute-start(bf16[128,2560]{1,0:T(8,128)(2,1)S(1)} %collective-permute-done.21), channel_id=1, source_target_pairs={{0,1},{1,0},{2,3},{3,2},{4,5},{5,4},{6,7},{7,6},{8,9},{9,8},{10,11... | collective-permute-start | bytes 1966088 | tf_op jit(solution)/shard_map/ppermute | solution.py:25

commit v3 on v2

--- a/solution.py
+++ b/solution.py
@@ -1,5 +1,3 @@
-import functools
-
 import jax
 import jax.numpy as jnp
 from jax import lax
@@ -10,7 +8,7 @@
 HD = 128
 TILE = 128
 MIB = 2**20
-COLUMN_CHUNKS = 2
+COLUMN_CHUNKS = 4
 
 guidance_scale = 5.0
 
@@ -127,27 +125,10 @@
     )(*near[:3], *far[:3], *near[3:], *far[3:], weights)
 
 
-def attend_kernel(
-    visible_ref, heads_ref, context_ref, out_ref, queries, pool, query_sem, fresh_sem, stale_sem
-):
-    fresh_rows = heads_ref.shape[0]
+def attend_kernel(visible_ref, heads_ref, context_ref, out_ref):
     width = out_ref.shape[1]
-    copies = (
-        pltpu.make_async_copy(heads_ref.at[:, pl.ds(0, width)], queries, query_sem),
-        pltpu.make_async_copy(
-            heads_ref.at[:, pl.ds(width, 2 * width)], pool.at[pl.ds(0, fresh_rows)], fresh_sem
-        ),
-        pltpu.make_async_copy(
-            context_ref, pool.at[pl.ds(fresh_rows, context_ref.shape[0])], stale_sem
-        ),
-    )
-    for copy in copies:
-        copy.start()
-    for copy in copies:
-        copy.wait()
     tiles_seen = visible_ref.shape[1]
     tiles_fresh = visible_ref.shape[0]
-
     mine_high, mine_low = lax.axis_index("sp") // 2, lax.axis_index("sp") % 2
     mine_branch = lax.axis_index("cfg")
 
@@ -155,33 +136,51 @@
         high, low = mine_high ^ ((index // 2) % 2), mine_low ^ (index // 4)
         tile, branch = high * 2 + low, mine_branch ^ (index % 2)
         rows = pl.ds(pl.multiple_of(index * TILE, TILE), TILE)
-        starts = []
+        places = []
         for seen in range(tiles_seen):
             number = visible_ref[tile, seen]
-            older = number - tiles_fresh
+            older = jnp.maximum(number - tiles_fresh, 0)
             fresh = (mine_low ^ (number % 2)) * 4 + (mine_high ^ ((number // 2) % 2)) * 2
             fresh = (fresh + index % 2) * TILE
-            stale = fresh_rows + ((older // 2) * 2 + branch) * 2 * TILE + (older % 2) * TILE
-            starts.append(pl.multiple_of(jnp.where(older < 0, fresh, stale), TILE))
+            stale = ((older // 2) * 2 + branch) * 2 * TILE + (older % 2) * TILE
+            places.append(
+                (
+                    number < tiles_fresh,
+                    pl.ds(pl.multiple_of(fresh, TILE), TILE),
+                    pl.ds(pl.multiple_of(stale, TILE), TILE),
+                )
+            )
+
+        def tiles(kind, head):
+            fresh_columns = slice(kind * width + head * HD, kind * width + (head + 1) * HD)
+            start = (kind - 1) * width + head * HD
+            return jnp.concatenate(
+                [
+                    jnp.where(
+                        is_fresh, heads_ref[fresh, fresh_columns], context_ref[stale, start : start + HD]
+                    )
+                    for is_fresh, fresh, stale in places
+                ],
+                axis=0,
+            )
+
         for head in range(width // HD):
             columns = slice(head * HD, (head + 1) * HD)
-            value_columns = slice(width + head * HD, width + (head + 1) * HD)
-            keys = jnp.concatenate([pool[pl.ds(s, TILE), columns] for s in starts], axis=0)
-            values = jnp.concatenate([pool[pl.ds(s, TILE), value_columns] for s in starts], axis=0)
             scores = lax.dot_general(
-                queries[rows, columns],
-                keys,
+                heads_ref[rows, columns],
+                tiles(1, head),
                 (((1,), (1,)), ((), ())),
                 preferred_element_type=jnp.float32,
             )
             exponent = jnp.exp(scores * HD ** (-0.5))
             total = jnp.sum(exponent, axis=-1, keepdims=True)
-            probabilities = (exponent / total).astype(jnp.bfloat16)
-            mixed = jnp.dot(probabilities, values, preferred_element_type=jnp.float32)
-            out_ref[rows, columns] = mixed.astype(jnp.bfloat16)
+            mixed = jnp.dot(
+                exponent.astype(jnp.bfloat16), tiles(2, head), preferred_element_type=jnp.float32
+            )
+            out_ref[rows, columns] = (mixed / total).astype(jnp.bfloat16)
         return carry
 
-    lax.fori_loop(0, fresh_rows // TILE, body, 0)
+    lax.fori_loop(0, heads_ref.shape[0] // TILE, body, 0)
 
 
 def attend(heads, context, visible):
@@ -191,17 +190,10 @@
         attend_kernel,
         in_specs=[
             pl.BlockSpec(memory_space=pltpu.SMEM),
-            pl.BlockSpec(memory_space=pl.ANY),
-            pl.BlockSpec(memory_space=pl.ANY),
+            pl.BlockSpec(memory_space=pltpu.VMEM),
+            pl.BlockSpec(memory_space=pltpu.VMEM),
         ],
         out_shape=jax.ShapeDtypeStruct((count, width), jnp.bfloat16),
-        scratch_shapes=[
-            pltpu.VMEM((count, width), jnp.bfloat16),
-            pltpu.VMEM((count + context.shape[0], 2 * width), jnp.bfloat16),
-            pltpu.SemaphoreType.DMA,
-            pltpu.SemaphoreType.DMA,
-            pltpu.SemaphoreType.DMA,
-        ],
         name="attend",
         cost_estimate=pl.CostEstimate(
             flops=4 * count * visible.shape[1] * TILE * width,
@@ -217,7 +209,18 @@
     modulate = modulation[0, 0]
     token_rows, features = current.shape
     devices = lax.axis_size("sp") * lax.axis_size("cfg")
-    branch = lax.axis_index("cfg")
+    wide = current.astype(jnp.float32)
+
+    gate = modulate[2]
+    other_gate = from_partner(gate, "cfg", 1)
+    last = lax.axis_index("pipe") == lax.axis_size("pipe") - 1
+    conditional = lax.axis_index("cfg") == 1
+    weight = jnp.where(conditional, guidance_scale, 1.0 - guidance_scale)
+    other_weight = jnp.where(conditional, 1.0 - guidance_scale, guidance_scale)
+    own_sent = jnp.where(last, weight, 0.0)
+    other_sent = jnp.where(last, other_weight, 1.0)
+    own_kept = jnp.where(last, weight, 1.0)
+    other_kept = jnp.where(last, other_weight, 0.0)
 
     own = modulated_norm(current, modulate)
     across = from_partner(own, "cfg", 1)
@@ -235,7 +238,7 @@
     width = project_in.shape[3]
     packed = stale_cache[0, 0].reshape(context_rows, 2, devices, width)
     packed = packed.transpose(2, 0, 1, 3).reshape(devices, context_rows, 2 * width)
-    packed = after(packed, (across, along))
+    packed = after(packed, (first, second))
     context = lax.all_to_all(packed, ("sp", "cfg"), split_axis=0, concat_axis=0, tiled=True)
     context = context.reshape(devices * context_rows, 2 * width)
 
@@ -250,7 +253,7 @@
     chunk = features // COLUMN_CHUNKS
     half = chunk // 2
     results = []
-    current_columns = current
+    previous = None
     for start in range(0, features, chunk):
         weights = project_out[0, :, start : start + chunk]
         sent = jnp.dot(rows_sent, weights, preferred_element_type=jnp.float32)
@@ -258,28 +261,34 @@
         kept = jnp.dot(rows_kept, weights, preferred_element_type=jnp.float32)
         kept = (kept + received.astype(jnp.float32)).reshape(2, 2, token_rows, chunk)
 
-        first, second = kept[..., :half], kept[..., half:]
-        first_in = from_partner(first[:, 1].astype(jnp.bfloat16), "cfg", 1)
-        second_in = from_partner(second[1].astype(jnp.bfloat16), "sp", 2)
-        first = first[:, 0] + first_in.astype(jnp.float32)
-        second = second[0] + second_in.astype(jnp.float32)
+        columns = slice(start, start + half)
+        own, other = kept[:, 0, :, :half] * gate[columns], kept[:, 1, :, :half] * other_gate[columns]
+        mine = jnp.stack([wide[:, columns], jnp.zeros_like(wide[:, columns])])
+        first_out = (own_sent * (own + mine) + other_sent * other).astype(jnp.bfloat16)
+        first = own_kept * (own + mine) + other_kept * other
+        second_out = kept[1, :, :, half:].astype(jnp.bfloat16)
+        second = kept[0, :, :, half:]
+        if previous is not None:
+            first_out = after(first_out, previous)
+            second_out = after(second_out, previous)
+        first_in = from_partner(first_out, "cfg", 1)
+        second_in = from_partner(second_out, "sp", 2)
+        previous = (first_in, second_in)
+
+        first = first + first_in.astype(jnp.float32)
         first_in = from_partner(first[1].astype(jnp.bfloat16), "sp", 2)
-        second_in = from_partner(second[1].astype(jnp.bfloat16), "cfg", 1)
+        columns = slice(start + half, start + chunk)
+        second = second + second_in.astype(jnp.float32)
+        own, other = second[0] * gate[columns], second[1] * other_gate[columns]
+        mine = wide[:, columns]
+        second_out = (own_sent * (own + mine) + other_sent * other).astype(jnp.bfloat16)
+        second_in = from_partner(second_out, "cfg", 1)
+        second = own_kept * (own + mine) + other_kept * other
+
         first = first[0] + first_in.astype(jnp.float32)
-        second = second[0] + second_in.astype(jnp.float32)
-        mixed_sum = jnp.concatenate([first, second], axis=1)
-
-        columns = slice(start, start + chunk)
-        layer_out = (
-            current_columns[:, columns].astype(jnp.float32) + modulate[2, columns] * mixed_sum
-        ).astype(jnp.bfloat16)
-        current_columns, layer_out = lax.optimization_barrier((current_columns, layer_out))
-        arrived = from_behind(layer_out, "pipe", 1)
-        partner = from_partner(arrived, "cfg", 1)
-        cond_rows = jnp.where(branch == 1, arrived, partner).astype(jnp.float32)
-        uncond_rows = jnp.where(branch == 1, partner, arrived).astype(jnp.float32)
-        guided = (uncond_rows + guidance_scale * (cond_rows - uncond_rows)).astype(jnp.bfloat16)
-        results.append(jnp.where(lax.axis_index("pipe") == 0, guided, arrived))
+        second = second + second_in.astype(jnp.float32)
+        summed = jnp.concatenate([first, second], axis=1).astype(jnp.bfloat16)
+        results.append(from_behind(summed, "pipe", 1))
     return jnp.concatenate(results, axis=1)[None, None]
 
 

time: 225 us -> 217 us (0.964)
  waiting for transfers between devices: 121 us -> 63.9 us
  other arithmetic: 3.68 us -> 26 us
  local copies, waits for them, and re-layouts: 29.8 us -> 41.3 us
  starting transfers between devices: 30.3 us -> 40.7 us
  matrix products: 6.16 us -> 13.2 us
  Pallas kernels: 33.9 us -> 30.9 us
    ppermute x21 -> x30, waiting for transfers between devices: 99.1 us -> 51.1 us  [from_partner(): return lax.ppermute(value, axis, pairs)]
    ppermute x2 -> x4, waiting for transfers between devices: 21.5 us -> 7.44 us  [from_behind(): return lax.ppermute(x, axis, [(i, (i + by) % count) for i in range(count)])]
    unnamed x25 -> x75, local copies, waits for them, and re-layouts: 6.09 us -> 14.3 us
    ppermute x21 -> x30, starting transfers between devices: 23.4 us -> 30.4 us  [from_partner(): return lax.ppermute(value, axis, pairs)]
    convert_element_type x2 -> x7, other arithmetic: 0.34 us -> 6.81 us  [the longest x6 3.73 us: per_device(): (own_sent * (own + mine) + other_sent * other).astype(jnp.bfloat16)]
    add x6, other arithmetic: 0.86 us -> 7.17 us  [the longest x4 7.05 us: per_device(): first = first + first_in.astype(jnp.float32)]
    another operation x2 -> x7, other arithmetic: 0.58 us -> 6.05 us
    dot_general x2 -> x4, matrix products: 3.05 us -> 8.44 us  [per_device(): sent = jnp.dot(rows_sent, weights, preferred_element_type=jnp.float32)]
  transfers between devices with their start and end apart: 24 -> 35, of which waited for: 17 -> 16; matrix products, arithmetic and copies ran while one was open for 14% -> 30% of each run, Pallas kernels for 9% -> 13%
where the time goes in v3:
time: 217 us; the launch traced here: 216 us
  waiting for transfers between devices  63.9 us (29%)
  local copies, waits for them, and re-layouts  41.3 us (19%)
  starting transfers between devices  40.7 us (19%)
  Pallas kernels  30.9 us (14%)
  other arithmetic  26 us (12%)
  matrix products  13.2 us (6%)
    ppermute x30, waiting for transfers between devices, from_partner(): return lax.ppermute(value, axis, pairs)  51.1 us
    ppermute x30, starting transfers between devices, from_partner(): return lax.ppermute(value, axis, pairs)  30.4 us
    pallas_call x1, Pallas kernels, project(): pl.pallas_call(project_kernel, grid=(steps,), in_specs=[whole] * 6 + [fir...  21 us
    unnamed x75, local copies, waits for them, and re-layouts  14.3 us
    another operation x2, local copies, waits for them, and re-layouts, per_device(): packed = stale_cache[0, 0].reshape(context_rows, 2, devices, width)  14 us
    dot_general x4, matrix products, per_device(): sent = jnp.dot(rows_sent, weights, preferred_element_type=jnp.float32)  8.44 us
    reshape x1, local copies, waits for them, and re-layouts, per_device(): packed.transpose(2, 0, 1, 3).reshape(devices, context_rows, 2 * width)  8.02 us
    pallas_call x1, Pallas kernels, attend(): pl.pallas_call(attend_kernel, in_specs=[pl.BlockSpec(memory_space=pltpu.S...  7.45 us
  transfers between devices with their start and end apart: 35, of which 16 were waited for; matrix products, arithmetic and copies ran while one was open for 30% of the time, Pallas kernels for 13%

profile of v3, /device:TPU:0, one launch (start us, length us, event | category | flops | bytes accessed | tf_op | source)
XLA Modules:
  0.0 216.5 jit_solution(13453715382276706480)
XLA Ops:
  0.9 1.3 copy-done.2
  2.2 2.5 %modulated_norm.1.refs_0_ = bf16[128,5120]{1,0:T(8,128)(2,1)S(1)} custom-call(bf16[128,5120]{1,0:T(8,128)(2,1)S(1)} %bitcast.257, f32[3,5120]{1,0:T(4,128)S(1)} %bitcast.258), custom_call_target="tpu_custom_call" | custom-call | flops 6553600 | bytes 2621440 | tf_op jit(solution)/shard_map/modulated_norm/pallas_call | solution.py:44
  4.6 3.0 %collective-permute-start = (bf16[128,5120]{1,0:T(8,128)(2,1)S(1)}, bf16[128,5120]{1,0:T(8,128)(2,1)S(1)}, u32[]{:S(2)}, u32[]{:S(2)}) collective-permute-start(bf16[128,5120]{1,0:T(8,128)(2,1)S(1)} %modulated_norm.1.refs_0_), channel_id=1, source_target_pairs={{0,1},{1,0},{2,3},{3,2},{4,5},{5,4},{6,7},{7,6},{8,9},{9,8},{10,11... | collective-permute-start | bytes 3932168 | tf_op jit(solution)/shard_map/ppermute | solution.py:23
  7.7 1.5 collective-permute-start.1
  9.2 27.3 %collective-permute-done.refs_1_ = bf16[128,5120]{1,0:T(8,128)(2,1)S(1)} collective-permute-done((bf16[128,5120]{1,0:T(8,128)(2,1)S(1)}, bf16[128,5120]{1,0:T(8,128)(2,1)S(1)}, u32[]{:S(2)}, u32[]{:S(2)}) %collective-permute-start) | collective-permute-done | bytes 1310752 | tf_op jit(solution)/shard_map/ppermute | solution.py:23
  36.5 1.8 collective-permute-start.5
  38.4 1.0 copy-done.32
  39.4 1.5 collective-permute-start.6
  40.9 8.0 %reshape_squeeze.3 = bf16[256,2,8,384]{3,2,1,0:T(8,128)(2,1)} reshape(bf16[1,1,256,2,3072]{4,3,2,1,0:T(2,128)(2,1)} %param.10) | data formatting | bytes 6291456 | tf_op jit(solution)/shard_map/reshape;squeeze | solution.py:239
  48.9 6.0 %copy.30 = bf16[256,2,8,384]{3,1,0,2:T(2,128)(2,1)} copy(bf16[256,2,8,384]{3,2,1,0:T(8,128)(2,1)} %reshape_squeeze.3) | data formatting | bytes 6291456 | tf_op jit(solution)/shard_map/reshape;squeeze | solution.py:239
  54.8 8.0 %reshape.60.value_ref = bf16[8,256,768]{2,1,0:T(8,128)(2,1)} reshape(bf16[8,256,2,384]{3,2,1,0:T(2,128)(2,1)} %bitcast.274) | data formatting | bytes 6291456 | tf_op jit(solution)/shard_map/reshape | solution.py:240
  64.5 4.0 %all-to-all-start = ((bf16[8,256,768]{2,1,0:T(8,128)(2,1)}), bf16[8,256,768]{2,1,0:T(8,128)(2,1)S(1)}, u32[]{:S(2)}, u32[]{:S(2)}) async-start(bf16[8,256,768]{2,1,0:T(8,128)(2,1)} %after.7), calls=%async_computation | async-start | bytes 6291456 | tf_op jit(solution)/shard_map/all_to_all | solution.py:242
  69.9 3.1 %bitcast_convert_fusion = f32[128,5120]{1,0:T(8,128)} fusion(bf16[1,1,128,5120]{3,2,1,0:T(8,128)(2,1)} %param.6), kind=kLoop, calls=%fused_computation.143 | loop fusion | flops 655360 | bytes 3932160 | tf_op jit(solution)/shard_map/convert_element_type | solution.py:212
  72.9 1.7 collective-permute-start.10
  74.6 2.1 collective-permute-done.7.refs_8_
  76.7 0.9 collective-permute-done.8.refs_9_
  77.7 1.1 copy-done.35
  79.3 21.0 %project_heads.1.heads_ref = bf16[1024,1152]{1,0:T(8,128)(2,1)} custom-call(bf16[128,5120]{1,0:T(8,128)(2,1)S(1)} %copy-done.5, bf16[128,5120]{1,0:T(8,128)(2,1)S(1)} %copy-done.11, bf16[128,5120]{1,0:T(8,128)(2,1)} %copy-done.32, bf16[128,5120]{1,0:T(8,128)(2,1)} %copy-done.34, bf16[128,5120]{1,0:T(8,128)(2,1)} %copy-done.35, bf16[128,5120]{1,0:T(8,128)(2,1)} %copy-done.36, ...), custom_call_target="tpu_custom_call" | custom-call | flops 12079595520 | bytes 22282240 | tf_op jit(solution)/shard_map/project_heads/pallas_call | solution.py:109
  100.3 5.4 %all-to-all-done = bf16[8,256,768]{2,1,0:T(8,128)(2,1)S(1)} async-done(((bf16[8,256,768]{2,1,0:T(8,128)(2,1)}), bf16[8,256,768]{2,1,0:T(8,128)(2,1)S(1)}, u32[]{:S(2)}, u32[]{:S(2)}) %all-to-all-start) | async-done | bytes 3145760 | tf_op jit(solution)/shard_map/all_to_all | solution.py:242
  105.7 1.7 copy-done.3
  107.3 7.5 %attend.1 = bf16[1024,384]{1,0:T(8,128)(2,1)S(1)} custom-call(s32[4,6]{1,0:T(4,128)S(1)} %bitcast.259, bf16[1024,1152]{1,0:T(8,128)(2,1)S(1)} %copy-done.3, bf16[2048,768]{1,0:T(8,128)(2,1)S(1)} %bitcast.256), custom_call_target="tpu_custom_call" | custom-call | flops 1207959552 | bytes 5505024 | tf_op jit(solution)/shard_map/attend/pallas_call | solution.py:189
  115.7 3.2 %convolution_convert_fusion.3 = bf16[512,1280]{1,0:T(8,128)(2,1)} fusion(bf16[1,384,5120]{2,1,0:T(8,128)(2,1)} %param.9, bf16[1024,384]{1,0:T(8,128)(2,1)S(1)} %attend.1), kind=kOutput, calls=%fused_computation.8 | convolution fusion | flops 503971840 | bytes 2686976 | tf_op jit(solution)/shard_map/dot_general | solution.py:259
  118.9 0.9 slice_bitcast_fusion.27
  120.0 2.3 %convolution_convert_fusion.2 = bf16[512,1280]{1,0:T(8,128)(2,1)S(1)} fusion(bf16[1,384,5120]{2,1,0:T(8,128)(2,1)} %param.9, bf16[1024,384]{1,0:T(8,128)(2,1)} %copy-done), kind=kOutput, calls=%fused_computation.7 | convolution fusion | flops 503971840 | bytes 2686976 | tf_op jit(solution)/shard_map/dot_general | solution.py:259
  122.9 2.0 convolution_convert_fusion.1
  126.4 2.2 convolution_add_fusion.3
  128.8 1.1 collective-permute-start.11
  135.7 1.5 copy-done.14
  140.1 1.3 collective-permute-start.17
  141.4 2.0 convert_add_fusion.3
  145.0 1.0 collective-permute-start.12
  146.0 3.6 %collective-permute-done.19.refs_1_ = bf16[2,128,640]{2,1,0:T(8,128)(2,1)} collective-permute-done((bf16[2,128,640]{2,1,0:T(8,128)(2,1)}, bf16[2,128,640]{2,1,0:T(8,128)(2,1)}, u32[]{:S(2)}, u32[]{:S(2)}) %collective-permute-start.19) | collective-permute-done | bytes 327712 | tf_op jit(solution)/shard_map/ppermute | solution.py:23
  149.6 1.5 collective-permute-start.25
  151.1 2.0 convert_add_fusion.2
  153.1 1.4 collective-permute-start.20
  154.5 4.1 %collective-permute-done.25.refs_1_ = bf16[2,128,640]{2,1,0:T(8,128)(2,1)S(1)} collective-permute-done((bf16[2,128,640]{2,1,0:T(8,128)(2,1)}, bf16[2,128,640]{2,1,0:T(8,128)(2,1)S(1)}, u32[]{:S(2)}, u32[]{:S(2)}) %collective-permute-start.25) | collective-permute-done | bytes 327712 | tf_op jit(solution)/shard_map/ppermute | solution.py:23
  159.6 1.3 collective-permute-start.26
  161.6 1.2 collective-permute-start.18
  162.8 2.1 collective-permute-done.26
  164.9 0.9 add_convert_fusion.11
  167.4 1.3 collective-permute-start.23
  168.7 1.7 fusion.51
  170.4 1.8 fusion.47
  172.1 2.5 %collective-permute-done.23.refs_0_ = bf16[2,128,640]{2,1,0:T(8,128)(2,1)S(1)} collective-permute-done((bf16[2,128,640]{2,1,0:T(8,128)(2,1)}, bf16[2,128,640]{2,1,0:T(8,128)(2,1)S(1)}, u32[]{:S(2)}, u32[]{:S(2)}) %collective-permute-start.23) | collective-permute-done | bytes 327712 | tf_op jit(solution)/shard_map/ppermute | solution.py:23
  175.4 1.3 collective-permute-start.31
  176.6 1.6 convert_add_fusion.1
  178.2 1.0 collective-permute-start.24
  179.3 1.7 pad_maximum_fusion.1
  181.0 1.6 collective-permute-start.21
  182.6 1.3 collective-permute-start.14
  185.5 3.0 %collective-permute-done.14 = bf16[128,640]{1,0:T(8,128)(2,1)S(1)} collective-permute-done((bf16[128,640]{1,0:T(8,128)(2,1)}, bf16[128,640]{1,0:T(8,128)(2,1)S(1)}, u32[]{:S(2)}, u32[]{:S(2)}) %collective-permute-start.14) | collective-permute-done | bytes 163872 | tf_op jit(solution)/shard_map/ppermute | solution.py:23
  190.9 1.7 collective-permute-start.29
  192.7 1.0 pad_maximum_fusion.2
  193.7 1.6 collective-permute-start.27
  195.3 1.0 pad_maximum_fusion
  196.3 1.6 collective-permute-start.15
  198.4 1.5 convert_add_fusion
  199.9 1.2 collective-permute-start.30
  201.1 2.4 %collective-permute-done.32 = bf16[128,640]{1,0:T(8,128)(2,1)S(1)} collective-permute-done((bf16[128,640]{1,0:T(8,128)(2,1)}, bf16[128,640]{1,0:T(8,128)(2,1)S(1)}, u32[]{:S(2)}, u32[]{:S(2)}) %collective-permute-start.32) | collective-permute-done | bytes 163872 | tf_op jit(solution)/shard_map/ppermute | solution.py:23
  203.6 1.7 collective-permute-done.30
  205.4 1.5 collective-permute-start.33
  206.9 2.7 %collective-permute-done.15 = bf16[128,1280]{1,0:T(8,128)(2,1)S(1)} collective-permute-done((bf16[128,1280]{1,0:T(8,128)(2,1)S(1)}, bf16[128,1280]{1,0:T(8,128)(2,1)S(1)}, u32[]{:S(2)}, u32[]{:S(2)}) %collective-permute-start.15) | collective-permute-done | bytes 327712 | tf_op jit(solution)/shard_map/ppermute | solution.py:18
  209.6 4.7 %collective-permute-done.33 = bf16[128,1280]{1,0:T(8,128)(2,1)S(1)} collective-permute-done((bf16[128,1280]{1,0:T(8,128)(2,1)S(1)}, bf16[128,1280]{1,0:T(8,128)(2,1)S(1)}, u32[]{:S(2)}, u32[]{:S(2)}) %collective-permute-start.33) | collective-permute-done | bytes 327712 | tf_op jit(solution)/shard_map/ppermute | solution.py:18
  214.3 2.2 maximum_bitcast_fusion
  (141 shorter events, 26.7 us)
Async XLA Ops:
  0.9 1.3 copy-start.2
  4.6 3.0 %copy-start.4 = (bf16[128,5120]{1,0:T(8,128)(2,1)}, bf16[128,5120]{1,0:T(8,128)(2,1)S(1)}, u32[]{:S(2)}) copy-start(bf16[128,5120]{1,0:T(8,128)(2,1)S(1)} %modulated_norm.1.refs_0_) | copy-start | bytes 3932164
  4.6 31.8 %collective-permute-start = (bf16[128,5120]{1,0:T(8,128)(2,1)S(1)}, bf16[128,5120]{1,0:T(8,128)(2,1)S(1)}, u32[]{:S(2)}, u32[]{:S(2)}) collective-permute-start(bf16[128,5120]{1,0:T(8,128)(2,1)S(1)} %modulated_norm.1.refs_0_), channel_id=1, source_target_pairs={{0,1},{1,0},{2,3},{3,2},{4,5},{5,4},{6,7},{7,6},{8,9},{9,8},{10,11... | collective-permute-start | bytes 3932168 | tf_op jit(solution)/shard_map/ppermute | solution.py:23
  7.7 30.7 %collective-permute-start.1 = (bf16[128,5120]{1,0:T(8,128)(2,1)S(1)}, bf16[128,5120]{1,0:T(8,128)(2,1)S(1)}, u32[]{:S(2)}, u32[]{:S(2)}) collective-permute-start(bf16[128,5120]{1,0:T(8,128)(2,1)S(1)} %modulated_norm.1.refs_0_), channel_id=1, source_target_pairs={{0,4},{2,6},{4,0},{6,2},{1,5},{3,7},{5,1},{7,3},{8,12},{10,14},{12... | collective-permute-start | bytes 3932168 | tf_op jit(solution)/shard_map/ppermute | solution.py:23
  36.4 1.9 copy-start.10
  36.5 26.4 %collective-permute-start.5 = (bf16[128,2560]{1,0:T(8,128)(2,1)S(1)}, bf16[128,2560]{1,0:T(8,128)(2,1)S(1)}, u32[]{:S(2)}, u32[]{:S(2)}) collective-permute-start(bf16[128,2560]{1,0:T(8,128)(2,1)S(1)} %slice.285), channel_id=1, source_target_pairs={{0,4},{2,6},{4,0},{6,2},{1,5},{3,7},{5,1},{7,3},{8,12},{10,14},{12... | collective-permute-start | bytes 1966088 | tf_op jit(solution)/shard_map/ppermute | solution.py:23
  39.4 23.5 %collective-permute-start.6 = (bf16[128,2560]{1,0:T(8,128)(2,1)S(1)}, bf16[128,2560]{1,0:T(8,128)(2,1)S(1)}, u32[]{:S(2)}, u32[]{:S(2)}) collective-permute-start(bf16[128,2560]{1,0:T(8,128)(2,1)S(1)} %slice.286), channel_id=1, source_target_pairs={{0,1},{1,0},{2,3},{3,2},{4,5},{5,4},{6,7},{7,6},{8,9},{9,8},{10,11... | collective-permute-start | bytes 1966088 | tf_op jit(solution)/shard_map/ppermute | solution.py:23
  64.5 4.8 %copy-start.33 = (f32[1,1,3,5120]{3,1,2,0:T(1,128)S(1)}, f32[1,1,3,5120]{3,1,2,0:T(1,128)}, u32[]{:S(2)}) copy-start(f32[1,1,3,5120]{3,1,2,0:T(1,128)} %param.7) | copy-start | bytes 184324
  64.5 41.1 %all-to-all-start = ((bf16[8,256,768]{2,1,0:T(8,128)(2,1)}), bf16[8,256,768]{2,1,0:T(8,128)(2,1)S(1)}, u32[]{:S(2)}, u32[]{:S(2)}) async-start(bf16[8,256,768]{2,1,0:T(8,128)(2,1)} %after.7), calls=%async_computation | async-start | bytes 6291456 | tf_op jit(solution)/shard_map/all_to_all | solution.py:242
  68.5 10.7 %copy-start.5 = (bf16[128,5120]{1,0:T(8,128)(2,1)S(1)}, bf16[128,5120]{1,0:T(8,128)(2,1)}, u32[]{:S(2)}) copy-start(bf16[128,5120]{1,0:T(8,128)(2,1)} %copy-done.4) | copy-start | bytes 3932164
  68.5 10.7 %copy-start.7 = (bf16[128,2560]{1,0:T(8,128)(2,1)S(1)}, bf16[128,2560]{1,0:T(8,128)(2,1)}, u32[]{:S(2)}) copy-start(bf16[128,2560]{1,0:T(8,128)(2,1)} %copy-done.6) | copy-start | bytes 1966084
  68.5 10.7 %copy-start.9 = (bf16[128,2560]{1,0:T(8,128)(2,1)S(1)}, bf16[128,2560]{1,0:T(8,128)(2,1)}, u32[]{:S(2)}) copy-start(bf16[128,2560]{1,0:T(8,128)(2,1)} %copy-done.8) | copy-start | bytes 1966084
  68.5 10.7 %copy-start.11 = (bf16[128,5120]{1,0:T(8,128)(2,1)S(1)}, bf16[128,5120]{1,0:T(8,128)(2,1)}, u32[]{:S(2)}) copy-start(bf16[128,5120]{1,0:T(8,128)(2,1)} %copy-done.10) | copy-start | bytes 3932164
  68.6 4.4 %collective-permute-start.2 = (bf16[128,5120]{1,0:T(8,128)(2,1)}, bf16[128,5120]{1,0:T(8,128)(2,1)S(1)}, u32[]{:S(2)}, u32[]{:S(2)}) collective-permute-start(bf16[128,5120]{1,0:T(8,128)(2,1)} %copy-done.4), channel_id=1, source_target_pairs={{0,2},{2,0},{4,6},{6,4},{1,3},{3,1},{5,7},{7,5},{8,10},{10,8},{12,... | collective-permute-start | bytes 3932168 | tf_op jit(solution)/shard_map/ppermute | solution.py:23
  68.8 8.8 %collective-permute-start.3 = (bf16[128,5120]{1,0:T(8,128)(2,1)}, bf16[128,5120]{1,0:T(8,128)(2,1)S(1)}, u32[]{:S(2)}, u32[]{:S(2)}) collective-permute-start(bf16[128,5120]{1,0:T(8,128)(2,1)} %copy-done.10), channel_id=1, source_target_pairs={{0,2},{2,0},{4,6},{6,4},{1,3},{3,1},{5,7},{7,5},{8,10},{10,8},{12,... | collective-permute-start | bytes 3932168 | tf_op jit(solution)/shard_map/ppermute | solution.py:23
  69.1 8.5 %collective-permute-start.4 = (bf16[128,5120]{1,0:T(8,128)(2,1)}, bf16[128,5120]{1,0:T(8,128)(2,1)S(1)}, u32[]{:S(2)}, u32[]{:S(2)}) collective-permute-start(bf16[128,5120]{1,0:T(8,128)(2,1)} %copy-done.32), channel_id=1, source_target_pairs={{0,2},{2,0},{4,6},{6,4},{1,3},{3,1},{5,7},{7,5},{8,10},{10,8},{12,... | collective-permute-start | bytes 3932168 | tf_op jit(solution)/shard_map/ppermute | solution.py:23
  69.3 7.4 %collective-permute-start.7 = (bf16[128,2560]{1,0:T(8,128)(2,1)}, bf16[128,2560]{1,0:T(8,128)(2,1)S(1)}, u32[]{:S(2)}, u32[]{:S(2)}) collective-permute-start(bf16[128,2560]{1,0:T(8,128)(2,1)} %copy-done.6), channel_id=1, source_target_pairs={{0,2},{2,0},{4,6},{6,4},{1,3},{3,1},{5,7},{7,5},{8,10},{10,8},{12,... | collective-permute-start | bytes 1966088 | tf_op jit(solution)/shard_map/ppermute | solution.py:23
  69.6 8.0 %collective-permute-start.8 = (bf16[128,2560]{1,0:T(8,128)(2,1)}, bf16[128,2560]{1,0:T(8,128)(2,1)S(1)}, u32[]{:S(2)}, u32[]{:S(2)}) collective-permute-start(bf16[128,2560]{1,0:T(8,128)(2,1)} %copy-done.8), channel_id=1, source_target_pairs={{0,2},{2,0},{4,6},{6,4},{1,3},{3,1},{5,7},{7,5},{8,10},{10,8},{12,... | collective-permute-start | bytes 1966088 | tf_op jit(solution)/shard_map/ppermute | solution.py:23
  72.9 4.7 %copy-start.34 = (bf16[128,5120]{1,0:T(8,128)(2,1)}, bf16[128,5120]{1,0:T(8,128)(2,1)S(1)}, u32[]{:S(2)}) copy-start(bf16[128,5120]{1,0:T(8,128)(2,1)S(1)} %collective-permute-done.2.refs_3_) | copy-start | bytes 3932164
  72.9 47.0 %collective-permute-start.10 = (f32[5120]{0:T(1024)S(1)}, f32[5120]{0:T(1024)S(1)}, u32[]{:S(2)}, u32[]{:S(2)}) collective-permute-start(f32[5120]{0:T(1024)S(1)} %bitcast.275), channel_id=1, source_target_pairs={{0,1},{1,0},{2,3},{3,2},{4,5},{5,4},{6,7},{7,6},{8,9},{9,8},{10,11... | collective-permute-start | bytes 61448 | tf_op jit(solution)/shard_map/ppermute | solution.py:23
  77.7 1.1 copy-start.35
  77.7 1.6 copy-start.36
  79.3 26.4 %copy-start.12 = (s32[1,4,6]{2,1,0:T(4,128)S(1)}, s32[1,4,6]{2,1,0:T(4,128)}, u32[]{:S(2)}) copy-start(s32[1,4,6]{2,1,0:T(4,128)} %param.11) | copy-start | bytes 292
  105.7 1.7 copy-start.3
  115.7 3.3 %copy-start.13 = (f32[128,5120]{1,0:T(8,128)S(1)}, f32[128,5120]{1,0:T(8,128)}, u32[]{:S(2)}) copy-start(f32[128,5120]{1,0:T(8,128)} %bitcast_convert_fusion) | copy-start | bytes 7864324
  118.9 3.9 %copy-start.1 = (bf16[1024,384]{1,0:T(8,128)(2,1)S(1)}, bf16[1024,384]{1,0:T(8,128)(2,1)}, u32[]{:S(2)}) copy-start(bf16[1024,384]{1,0:T(8,128)(2,1)} %copy-done) | copy-start | bytes 2359300
  118.9 7.5 %collective-permute-start.9 = (bf16[512,1280]{1,0:T(8,128)(2,1)}, bf16[512,1280]{1,0:T(8,128)(2,1)}, u32[]{:S(2)}, u32[]{:S(2)}) collective-permute-start(bf16[512,1280]{1,0:T(8,128)(2,1)} %convolution_convert_fusion.3), channel_id=1, source_target_pairs={{0,2},{2,0},{4,6},{6,4},{1,3},{3,1},{5,7},{7,5},{8,10},{10,8},{12,... | collective-permute-start | bytes 3932168 | tf_op jit(solution)/shard_map/ppermute | solution.py:23
  120.0 5.0 %copy-start.22 = (bf16[1,384,5120]{2,1,0:T(8,128)(2,1)S(1)}, bf16[1,384,5120]{2,1,0:T(8,128)(2,1)}, u32[]{:S(2)}) copy-start(bf16[1,384,5120]{2,1,0:T(8,128)(2,1)} %param.9) | copy-start | bytes 11796484
  122.3 8.3 %collective-permute-start.16 = (bf16[512,1280]{1,0:T(8,128)(2,1)S(1)}, bf16[512,1280]{1,0:T(8,128)(2,1)S(1)}, u32[]{:S(2)}, u32[]{:S(2)}) collective-permute-start(bf16[512,1280]{1,0:T(8,128)(2,1)S(1)} %convolution_convert_fusion.2), channel_id=1, source_target_pairs={{0,2},{2,0},{4,6},{6,4},{1,3},{3,1},{5,7},{7,5},{8,10},{10,8},{12,... | collective-permute-start | bytes 3932168 | tf_op jit(solution)/shard_map/ppermute | solution.py:23
  124.9 7.5 %collective-permute-start.22 = (bf16[512,1280]{1,0:T(8,128)(2,1)S(1)}, bf16[512,1280]{1,0:T(8,128)(2,1)S(1)}, u32[]{:S(2)}, u32[]{:S(2)}) collective-permute-start(bf16[512,1280]{1,0:T(8,128)(2,1)S(1)} %convolution_convert_fusion.1), channel_id=1, source_target_pairs={{0,2},{2,0},{4,6},{6,4},{1,3},{3,1},{5,7},{7,5},{8,10},{10,8},{12,... | collective-permute-start | bytes 3932168 | tf_op jit(solution)/shard_map/ppermute | solution.py:23
  125.8 2.7 %copy-start.24 = (f32[1,128,640]{2,1,0:T(8,128)S(1)}, f32[1,128,640]{2,1,0:T(8,128)}, u32[]{:S(2)}) copy-start(f32[1,128,640]{2,1,0:T(8,128)} %get-tuple-element.25) | copy-start | bytes 983044
  125.8 9.0 %collective-permute-start.28 = (bf16[512,1280]{1,0:T(8,128)(2,1)S(1)}, bf16[512,1280]{1,0:T(8,128)(2,1)S(1)}, u32[]{:S(2)}, u32[]{:S(2)}) collective-permute-start(bf16[512,1280]{1,0:T(8,128)(2,1)S(1)} %convolution_convert_fusion), channel_id=1, source_target_pairs={{0,2},{2,0},{4,6},{6,4},{1,3},{3,1},{5,7},{7,5},{8,10},{10,8},{12,... | collective-permute-start | bytes 3932168 | tf_op jit(solution)/shard_map/ppermute | solution.py:23
  128.6 2.9 %copy-start.19 = (f32[512,1280]{1,0:T(8,128)}, f32[512,1280]{1,0:T(8,128)S(1)}, u32[]{:S(2)}) copy-start(f32[512,1280]{1,0:T(8,128)S(1)} %convolution_add_fusion.3) | copy-start | bytes 7864324
  128.8 10.0 %collective-permute-start.11 = (bf16[2,128,640]{2,1,0:T(8,128)(2,1)S(1)}, bf16[2,128,640]{2,1,0:T(8,128)(2,1)}, u32[]{:S(2)}, u32[]{:S(2)}) collective-permute-start(bf16[2,128,640]{2,1,0:T(8,128)(2,1)S(1)} %add_convert_fusion.3), channel_id=1, source_target_pairs={{0,1},{1,0},{2,3},{3,2},{4,5},{5,4},{6,7},{7,6},{8,9},{9,8},{10,11... | collective-permute-start | bytes 983048 | tf_op jit(solution)/shard_map/ppermute | solution.py:23
  129.8 9.5 %collective-permute-start.13 = (bf16[2,128,640]{2,1,0:T(8,128)(2,1)S(1)}, bf16[2,128,640]{2,1,0:T(8,128)(2,1)}, u32[]{:S(2)}, u32[]{:S(2)}) collective-permute-start(bf16[2,128,640]{2,1,0:T(8,128)(2,1)S(1)} %fusion.32), channel_id=1, source_target_pairs={{0,4},{2,6},{4,0},{6,2},{1,5},{3,7},{5,1},{7,3},{8,12},{10,14},{12... | collective-permute-start | bytes 983048 | tf_op jit(solution)/shard_map/ppermute | solution.py:23
  131.5 6.4 %copy-start.18 = (f32[512,1280]{1,0:T(8,128)}, f32[512,1280]{1,0:T(8,128)S(1)}, u32[]{:S(2)}) copy-start(f32[512,1280]{1,0:T(8,128)S(1)} %convolution_add_fusion.2) | copy-start | bytes 7864324
  133.2 1.6 copy-start.16
  134.8 3.1 %copy-start.23 = (f32[1,128,640]{2,1,0:T(8,128)S(1)}, f32[1,128,640]{2,1,0:T(8,128)}, u32[]{:S(2)}) copy-start(f32[1,128,640]{2,1,0:T(8,128)} %get-tuple-element.26) | copy-start | bytes 983044
  135.7 1.5 copy-start.14
  139.3 10.2 %collective-permute-start.19 = (bf16[2,128,640]{2,1,0:T(8,128)(2,1)}, bf16[2,128,640]{2,1,0:T(8,128)(2,1)}, u32[]{:S(2)}, u32[]{:S(2)}) collective-permute-start(bf16[2,128,640]{2,1,0:T(8,128)(2,1)} %after.9), channel_id=1, source_target_pairs={{0,4},{2,6},{4,0},{6,2},{1,5},{3,7},{5,1},{7,3},{8,12},{10,14},{12... | collective-permute-start | bytes 983048 | tf_op jit(solution)/shard_map/ppermute | solution.py:23
  140.1 9.5 %collective-permute-start.17 = (bf16[2,128,640]{2,1,0:T(8,128)(2,1)}, bf16[2,128,640]{2,1,0:T(8,128)(2,1)}, u32[]{:S(2)}, u32[]{:S(2)}) collective-permute-start(bf16[2,128,640]{2,1,0:T(8,128)(2,1)} %after.8), channel_id=1, source_target_pairs={{0,1},{1,0},{2,3},{3,2},{4,5},{5,4},{6,7},{7,6},{8,9},{9,8},{10,11... | collective-permute-start | bytes 983048 | tf_op jit(solution)/shard_map/ppermute | solution.py:23
  143.4 21.5 %copy-start.20 = (f32[2,128,640]{2,1,0:T(8,128)}, f32[2,128,640]{2,1,0:T(8,128)S(1)}, u32[]{:S(2)}) copy-start(f32[2,128,640]{2,1,0:T(8,128)S(1)} %get-tuple-element.14) | copy-start | bytes 1966084
  145.0 23.7 %collective-permute-start.12 = (bf16[128,640]{1,0:T(8,128)(2,1)}, bf16[128,640]{1,0:T(8,128)(2,1)}, u32[]{:S(2)}, u32[]{:S(2)}) collective-permute-start(bf16[128,640]{1,0:T(8,128)(2,1)} %fusion.60), channel_id=1, source_target_pairs={{0,4},{2,6},{4,0},{6,2},{1,5},{3,7},{5,1},{7,3},{8,12},{10,14},{12... | collective-permute-start | bytes 491528 | tf_op jit(solution)/shard_map/ppermute | solution.py:23
  149.6 9.0 %copy-start.17 = (f32[512,1280]{1,0:T(8,128)S(1)}, f32[512,1280]{1,0:T(8,128)}, u32[]{:S(2)}) copy-start(f32[512,1280]{1,0:T(8,128)} %copy-done.16) | copy-start | bytes 7864324
  149.6 9.0 %collective-permute-start.25 = (bf16[2,128,640]{2,1,0:T(8,128)(2,1)}, bf16[2,128,640]{2,1,0:T(8,128)(2,1)S(1)}, u32[]{:S(2)}, u32[]{:S(2)}) collective-permute-start(bf16[2,128,640]{2,1,0:T(8,128)(2,1)} %after.11), channel_id=1, source_target_pairs={{0,4},{2,6},{4,0},{6,2},{1,5},{3,7},{5,1},{7,3},{8,12},{10,14},{12... | collective-permute-start | bytes 983048 | tf_op jit(solution)/shard_map/ppermute | solution.py:23
  153.0 7.8 %copy-start.31 = (f32[2,128,640]{2,1,0:T(8,128)}, f32[2,128,640]{2,1,0:T(8,128)S(1)}, u32[]{:S(2)}) copy-start(f32[2,128,640]{2,1,0:T(8,128)S(1)} %get-tuple-element.21) | copy-start | bytes 1966084
  153.1 5.5 %collective-permute-start.20 = (bf16[128,640]{1,0:T(8,128)(2,1)S(1)}, bf16[128,640]{1,0:T(8,128)(2,1)S(1)}, u32[]{:S(2)}, u32[]{:S(2)}) collective-permute-start(bf16[128,640]{1,0:T(8,128)(2,1)S(1)} %add_convert_fusion.9), channel_id=1, source_target_pairs={{0,1},{1,0},{2,3},{3,2},{4,5},{5,4},{6,7},{7,6},{8,9},{9,8},{10,11... | collective-permute-start | bytes 491528 | tf_op jit(solution)/shard_map/ppermute | solution.py:23
  158.6 7.2 %copy-start.26 = (bf16[2,128,640]{2,1,0:T(8,128)(2,1)}, bf16[2,128,640]{2,1,0:T(8,128)(2,1)S(1)}, u32[]{:S(2)}) copy-start(bf16[2,128,640]{2,1,0:T(8,128)(2,1)S(1)} %collective-permute-done.25.refs_1_) | copy-start | bytes 983044
  159.6 5.3 %collective-permute-start.26 = (bf16[128,640]{1,0:T(8,128)(2,1)S(1)}, bf16[128,640]{1,0:T(8,128)(2,1)S(1)}, u32[]{:S(2)}, u32[]{:S(2)}) collective-permute-start(bf16[128,640]{1,0:T(8,128)(2,1)S(1)} %get-tuple-element.24), channel_id=1, source_target_pairs={{0,1},{1,0},{2,3},{3,2},{4,5},{5,4},{6,7},{7,6},{8,9},{9,8},{10,11... | collective-permute-start | bytes 491528 | tf_op jit(solution)/shard_map/ppermute | solution.py:23
  161.6 8.8 %collective-permute-start.18 = (bf16[128,640]{1,0:T(8,128)(2,1)}, bf16[128,640]{1,0:T(8,128)(2,1)}, u32[]{:S(2)}, u32[]{:S(2)}) collective-permute-start(bf16[128,640]{1,0:T(8,128)(2,1)} %fusion.61), channel_id=1, source_target_pairs={{0,4},{2,6},{4,0},{6,2},{1,5},{3,7},{5,1},{7,3},{8,12},{10,14},{12... | collective-permute-start | bytes 491528 | tf_op jit(solution)/shard_map/ppermute | solution.py:23
  167.4 9.3 %copy-start.29 = (f32[1,128,640]{2,1,0:T(8,128)S(1)}, f32[1,128,640]{2,1,0:T(8,128)}, u32[]{:S(2)}) copy-start(f32[1,128,640]{2,1,0:T(8,128)} %copy-done.28) | copy-start | bytes 983044
  167.4 7.3 %collective-permute-start.23 = (bf16[2,128,640]{2,1,0:T(8,128)(2,1)}, bf16[2,128,640]{2,1,0:T(8,128)(2,1)S(1)}, u32[]{:S(2)}, u32[]{:S(2)}) collective-permute-start(bf16[2,128,640]{2,1,0:T(8,128)(2,1)} %after.10), channel_id=1, source_target_pairs={{0,1},{1,0},{2,3},{3,2},{4,5},{5,4},{6,7},{7,6},{8,9},{9,8},{10,11... | collective-permute-start | bytes 983048 | tf_op jit(solution)/shard_map/ppermute | solution.py:23
  175.4 10.0 %copy-start.15 = (f32[512,1280]{1,0:T(8,128)S(1)}, f32[512,1280]{1,0:T(8,128)}, u32[]{:S(2)}) copy-start(f32[512,1280]{1,0:T(8,128)} %copy-done.14) | copy-start | bytes 7864324
  175.4 13.1 %copy-start.21 = (f32[2,128,640]{2,1,0:T(8,128)S(1)}, f32[2,128,640]{2,1,0:T(8,128)}, u32[]{:S(2)}) copy-start(f32[2,128,640]{2,1,0:T(8,128)} %copy-done.20) | copy-start | bytes 1966084
  175.4 10.0 %collective-permute-start.31 = (bf16[2,128,640]{2,1,0:T(8,128)(2,1)}, bf16[2,128,640]{2,1,0:T(8,128)(2,1)S(1)}, u32[]{:S(2)}, u32[]{:S(2)}) collective-permute-start(bf16[2,128,640]{2,1,0:T(8,128)(2,1)} %after.13), channel_id=1, source_target_pairs={{0,4},{2,6},{4,0},{6,2},{1,5},{3,7},{5,1},{7,3},{8,12},{10,14},{12... | collective-permute-start | bytes 983048 | tf_op jit(solution)/shard_map/ppermute | solution.py:23
  178.2 6.5 %collective-permute-start.24 = (bf16[128,640]{1,0:T(8,128)(2,1)S(1)}, bf16[128,640]{1,0:T(8,128)(2,1)S(1)}, u32[]{:S(2)}, u32[]{:S(2)}) collective-permute-start(bf16[128,640]{1,0:T(8,128)(2,1)S(1)} %fusion.62), channel_id=1, source_target_pairs={{0,4},{2,6},{4,0},{6,2},{1,5},{3,7},{5,1},{7,3},{8,12},{10,14},{12... | collective-permute-start | bytes 491528 | tf_op jit(solution)/shard_map/ppermute | solution.py:23
  181.0 25.9 %collective-permute-start.21 = (bf16[128,1280]{1,0:T(8,128)(2,1)}, bf16[128,1280]{1,0:T(8,128)(2,1)}, u32[]{:S(2)}, u32[]{:S(2)}) collective-permute-start(bf16[128,1280]{1,0:T(8,128)(2,1)} %pad_maximum_fusion.1), channel_id=1, source_target_pairs={{0,8},{8,16},{16,24},{24,0},{1,9},{9,17},{17,25},{25,1},{2,10},{10... | collective-permute-start | bytes 983048 | tf_op jit(solution)/shard_map/ppermute | solution.py:18
  182.6 5.9 %collective-permute-start.14 = (bf16[128,640]{1,0:T(8,128)(2,1)}, bf16[128,640]{1,0:T(8,128)(2,1)S(1)}, u32[]{:S(2)}, u32[]{:S(2)}) collective-permute-start(bf16[128,640]{1,0:T(8,128)(2,1)} %get-tuple-element.18), channel_id=1, source_target_pairs={{0,1},{1,0},{2,3},{3,2},{4,5},{5,4},{6,7},{7,6},{8,9},{9,8},{10,11... | collective-permute-start | bytes 491528 | tf_op jit(solution)/shard_map/ppermute | solution.py:23
  190.9 7.4 %collective-permute-start.29 = (bf16[2,128,640]{2,1,0:T(8,128)(2,1)}, bf16[2,128,640]{2,1,0:T(8,128)(2,1)S(1)}, u32[]{:S(2)}, u32[]{:S(2)}) collective-permute-start(bf16[2,128,640]{2,1,0:T(8,128)(2,1)} %after.12), channel_id=1, source_target_pairs={{0,1},{1,0},{2,3},{3,2},{4,5},{5,4},{6,7},{7,6},{8,9},{9,8},{10,11... | collective-permute-start | bytes 983048 | tf_op jit(solution)/shard_map/ppermute | solution.py:23
  193.7 13.2 %collective-permute-start.27 = (bf16[128,1280]{1,0:T(8,128)(2,1)S(1)}, bf16[128,1280]{1,0:T(8,128)(2,1)S(1)}, u32[]{:S(2)}, u32[]{:S(2)}) collective-permute-start(bf16[128,1280]{1,0:T(8,128)(2,1)S(1)} %pad_maximum_fusion.2), channel_id=1, source_target_pairs={{0,8},{8,16},{16,24},{24,0},{1,9},{9,17},{17,25},{25,1},{2,10},{10... | collective-permute-start | bytes 983048 | tf_op jit(solution)/shard_map/ppermute | solution.py:18
  196.3 13.3 %collective-permute-start.15 = (bf16[128,1280]{1,0:T(8,128)(2,1)S(1)}, bf16[128,1280]{1,0:T(8,128)(2,1)S(1)}, u32[]{:S(2)}, u32[]{:S(2)}) collective-permute-start(bf16[128,1280]{1,0:T(8,128)(2,1)S(1)} %pad_maximum_fusion), channel_id=1, source_target_pairs={{0,8},{8,16},{16,24},{24,0},{1,9},{9,17},{17,25},{25,1},{2,10},{10... | collective-permute-start | bytes 983048 | tf_op jit(solution)/shard_map/ppermute | solution.py:18
  198.0 5.5 %collective-permute-start.32 = (bf16[128,640]{1,0:T(8,128)(2,1)}, bf16[128,640]{1,0:T(8,128)(2,1)S(1)}, u32[]{:S(2)}, u32[]{:S(2)}) collective-permute-start(bf16[128,640]{1,0:T(8,128)(2,1)} %get-tuple-element.16), channel_id=1, source_target_pairs={{0,1},{1,0},{2,3},{3,2},{4,5},{5,4},{6,7},{7,6},{8,9},{9,8},{10,11... | collective-permute-start | bytes 491528 | tf_op jit(solution)/shard_map/ppermute | solution.py:23
  199.9 5.4 %collective-permute-start.30 = (bf16[128,640]{1,0:T(8,128)(2,1)S(1)}, bf16[128,640]{1,0:T(8,128)(2,1)S(1)}, u32[]{:S(2)}, u32[]{:S(2)}) collective-permute-start(bf16[128,640]{1,0:T(8,128)(2,1)S(1)} %fusion.63), channel_id=1, source_target_pairs={{0,4},{2,6},{4,0},{6,2},{1,5},{3,7},{5,1},{7,3},{8,12},{10,14},{12... | collective-permute-start | bytes 491528 | tf_op jit(solution)/shard_map/ppermute | solution.py:23
  205.4 8.9 %collective-permute-start.33 = (bf16[128,1280]{1,0:T(8,128)(2,1)S(1)}, bf16[128,1280]{1,0:T(8,128)(2,1)S(1)}, u32[]{:S(2)}, u32[]{:S(2)}) collective-permute-start(bf16[128,1280]{1,0:T(8,128)(2,1)S(1)} %pad_maximum_fusion.3), channel_id=1, source_target_pairs={{0,8},{8,16},{16,24},{24,0},{1,9},{9,17},{17,25},{25,1},{2,10},{10... | collective-permute-start | bytes 983048 | tf_op jit(solution)/shard_map/ppermute | solution.py:18
  (8 other events, 6.7 us)

commit v4 on v3

--- a/solution.py
+++ b/solution.py
@@ -1,3 +1,5 @@
+import functools
+
 import jax
 import jax.numpy as jnp
 from jax import lax
@@ -8,9 +10,10 @@
 HD = 128
 TILE = 128
 MIB = 2**20
-COLUMN_CHUNKS = 4
+COLUMN_CHUNKS = 5
 
 guidance_scale = 5.0
+SHORT = pl.CostEstimate(flops=1, bytes_accessed=1, transcendentals=0)
 
 
 def from_behind(x, axis, by):
@@ -64,11 +67,13 @@
         out_shape=jax.ShapeDtypeStruct(value.shape, value.dtype),
         input_output_aliases={0: 0},
         name="after",
+        cost_estimate=SHORT,
     )(value, *earlier)
 
 
 def project_kernel(*refs):
-    (*whole_refs, near_first, near_second, far_first, far_second, weights_ref, out_ref, total_ref) = refs
+    *whole_refs, near_first, near_second, far_first, far_second, weights_ref = refs[:11]
+    out_ref, total_ref = refs[-2:]
     step, steps = pl.program_id(0), pl.num_programs(0)
     weights = jnp.concatenate([weights_ref[0], weights_ref[1], weights_ref[2]], axis=1)
     early = step < steps // 2
@@ -97,7 +102,7 @@
         out_ref[:, 2 * width :] = total_ref[:, 2 * width :].astype(jnp.bfloat16)
 
 
-def project(near, far, weights):
+def project(near, far, weights, earlier):
     rows, depth = near[0].shape
     width = weights.shape[2]
     steps = 4
@@ -111,7 +116,8 @@
         grid=(steps,),
         in_specs=[whole] * 6
         + [first, second] * 2
-        + [pl.BlockSpec((3, block, width), lambda k: (0, k, 0))],
+        + [pl.BlockSpec((3, block, width), lambda k: (0, k, 0))]
+        + [pl.BlockSpec(memory_space=pl.ANY)],
         out_specs=pl.BlockSpec((count, 3 * width), lambda k: (0, 0)),
         out_shape=jax.ShapeDtypeStruct((count, 3 * width), jnp.bfloat16),
         scratch_shapes=[pltpu.VMEM((count, 3 * width), jnp.float32)],
@@ -121,8 +127,8 @@
             bytes_accessed=2 * (count * depth + weights.size),
             transcendentals=0,
         ),
-        compiler_params=pltpu.CompilerParams(vmem_limit_bytes=48 * MIB),
-    )(*near[:3], *far[:3], *near[3:], *far[3:], weights)
+        compiler_params=pltpu.CompilerParams(vmem_limit_bytes=36 * MIB),
+    )(*near[:3], *far[:3], *near[3:], *far[3:], weights, earlier)
 
 
 def attend_kernel(visible_ref, heads_ref, context_ref, out_ref):
@@ -204,40 +210,213 @@
     )(visible, heads, context)
 
 
+def half_kernel(rows_ref, *refs, start):
+    out_ref = refs[-1]
+    out_ref[...] = rows_ref[:, start : start + out_ref.shape[1]]
+
+
+def half_of(rows, start, earlier):
+    return pl.pallas_call(
+        functools.partial(half_kernel, start=start),
+        in_specs=[pl.BlockSpec(memory_space=pltpu.VMEM), pl.BlockSpec(memory_space=pl.ANY)],
+        out_shape=jax.ShapeDtypeStruct((rows.shape[0], rows.shape[1] // 2), rows.dtype),
+        name="half_of",
+        cost_estimate=SHORT,
+        compiler_params=pltpu.CompilerParams(vmem_limit_bytes=8 * MIB),
+    )(rows, earlier)
+
+
+def sent_kernel(attended_ref, weights_ref, *out_refs, chunk):
+    rows = attended_ref[attended_ref.shape[0] // 2 :, :]
+    start = 0
+    for out_ref in out_refs:
+        for index in range(out_ref.shape[0]):
+            out_ref[index] = jnp.dot(
+                rows, weights_ref[:, start : start + chunk], preferred_element_type=jnp.float32
+            ).astype(jnp.bfloat16)
+            start += chunk
+
+
+def sent_products(attended, weights, chunk):
+    rows, count = attended.shape[0] // 2, weights.shape[1] // chunk
+    return pl.pallas_call(
+        functools.partial(sent_kernel, chunk=chunk),
+        out_shape=[
+            jax.ShapeDtypeStruct((pieces, rows, chunk), jnp.bfloat16) for pieces in (1, count - 1)
+        ],
+        in_specs=[pl.BlockSpec(memory_space=pltpu.VMEM)] * 2,
+        name="sent_products",
+        cost_estimate=SHORT,
+        compiler_params=pltpu.CompilerParams(vmem_limit_bytes=20 * MIB),
+    )(attended, weights)
+
+
+def combined(own, other, mine, gates_ref, columns):
+    conditional = lax.axis_index("cfg") == 1
+    last = lax.axis_index("pipe") == lax.axis_size("pipe") - 1
+    weight = jnp.where(conditional, guidance_scale, 1.0 - guidance_scale).astype(jnp.float32)
+    other_weight = jnp.where(conditional, 1.0 - guidance_scale, guidance_scale).astype(jnp.float32)
+    own = own * gates_ref[0:1, columns]
+    other = other * gates_ref[1:2, columns]
+    if mine is not None:
+        own = own + mine
+    guided = weight * own + other_weight * other
+    return jnp.where(last, guided, other), jnp.where(last, guided, own)
+
+
+def begin(index, start, refs, across_out, along_out, first_kept, second_kept):
+    attended_ref, weights_ref, received_ref, rows_ref, gates_ref = refs
+    tokens, half = rows_ref.shape[0], first_kept.shape[2]
+    attended = attended_ref[: 4 * tokens, :]
+    columns = slice(start, start + half)
+    product = jnp.dot(attended, weights_ref[:, columns], preferred_element_type=jnp.float32)
+    product = product + received_ref[index, :, :half].astype(jnp.float32)
+    for tile in range(2):
+        own = product[2 * tile * tokens : (2 * tile + 1) * tokens]
+        other = product[(2 * tile + 1) * tokens : (2 * tile + 2) * tokens]
+        mine = rows_ref[:, columns].astype(jnp.float32) if tile == 0 else None
+        sent, kept = combined(own, other, mine, gates_ref, columns)
+        across_out[tile] = sent.astype(jnp.bfloat16)
+        first_kept[tile] = kept
+    columns = slice(start + half, start + 2 * half)
+    product = jnp.dot(attended, weights_ref[:, columns], preferred_element_type=jnp.float32)
+    product = product + received_ref[index, :, half:].astype(jnp.float32)
+    for branch in range(2):
+        second_kept[branch] = product[branch * tokens : (branch + 1) * tokens]
+        along_out[branch] = product[(branch + 2) * tokens : (branch + 3) * tokens].astype(
+            jnp.bfloat16
+        )
+
+
+def stage_kernel(*refs, parts, start, next_start, piece, fresh, middle, final):
+    named = dict(zip(parts, refs))
+    if fresh:
+        begin(
+            piece,
+            next_start,
+            [named[name] for name in ("attended", "weights", "received", "rows", "gates")],
+            named["across_out"],
+            named["along_out"],
+            named["first_kept_out"],
+            named["second_kept_out"],
+        )
+    if middle:
+        across, along = named["across"], named["along"]
+        first_kept, second_kept = named["first_kept"], named["second_kept"]
+        half = first_kept.shape[2]
+        place = 2 if fresh else 0
+        named["along_out"][place] = (first_kept[1] + across[1].astype(jnp.float32)).astype(
+            jnp.bfloat16
+        )
+        named["first_left_out"][...] = first_kept[0] + across[0].astype(jnp.float32)
+        columns = slice(start + half, start + 2 * half)
+        sent, kept = combined(
+            second_kept[0] + along[0].astype(jnp.float32),
+            second_kept[1] + along[1].astype(jnp.float32),
+            named["rows"][:, columns].astype(jnp.float32),
+            named["gates"],
+            columns,
+        )
+        named["across_out"][place] = sent.astype(jnp.bfloat16)
+        named["second_left_out"][...] = kept
+    if final:
+        across, along = named["across"], named["along"]
+        first_left, second_left = named["first_left"], named["second_left"]
+        half = first_left.shape[1]
+        place = 2 if middle else 0
+        named["done_out"][:, :half] = (
+            first_left[...] + along[place].astype(jnp.float32)
+        ).astype(jnp.bfloat16)
+        named["done_out"][:, half:] = (
+            second_left[...] + across[place].astype(jnp.float32)
+        ).astype(jnp.bfloat16)
+
+
+def stage(operands, earlier, chunk, start, next_start, piece, fresh, middle, final):
+    tokens, half = operands["rows"].shape[0], chunk // 2
+    outs = {}
+    if fresh or middle:
+        pieces = 2 * fresh + middle
+        outs["across_out"] = jax.ShapeDtypeStruct((pieces, tokens, half), jnp.bfloat16)
+        outs["along_out"] = outs["across_out"]
+    if fresh:
+        outs["first_kept_out"] = jax.ShapeDtypeStruct((2, tokens, half), jnp.float32)
+        outs["second_kept_out"] = outs["first_kept_out"]
+    if middle:
+        outs["first_left_out"] = jax.ShapeDtypeStruct((tokens, half), jnp.float32)
+        outs["second_left_out"] = outs["first_left_out"]
+    if final:
+        outs["done_out"] = jax.ShapeDtypeStruct((tokens, chunk), jnp.bfloat16)
+    parts = list(operands) + ["earlier"] * len(earlier) + list(outs)
+    results = pl.pallas_call(
+        functools.partial(
+            stage_kernel,
+            parts=parts,
+            start=start,
+            next_start=next_start,
+            piece=piece,
+            fresh=fresh,
+            middle=middle,
+            final=final,
+        ),
+        in_specs=[pl.BlockSpec(memory_space=pltpu.VMEM)] * len(operands)
+        + [pl.BlockSpec(memory_space=pl.ANY)] * len(earlier),
+        out_shape=list(outs.values()),
+        name="sum_stage",
+        cost_estimate=SHORT,
+        compiler_params=pltpu.CompilerParams(vmem_limit_bytes=24 * MIB),
+    )(*operands.values(), *earlier)
+    return dict(zip(outs, results))
+
+
+def place_kernel(part_ref, *refs, start):
+    out_ref, semaphore = refs[-2:]
+    copy = pltpu.make_async_copy(
+        part_ref, out_ref.at[:, pl.ds(start, part_ref.shape[1])], semaphore
+    )
+    copy.start()
+    copy.wait()
+
+
+def place(part, whole, columns, start, earlier):
+    held = () if whole is None else (whole,)
+    return pl.pallas_call(
+        functools.partial(place_kernel, start=start),
+        in_specs=[pl.BlockSpec(memory_space=pl.ANY)] * (1 + len(held) + len(earlier)),
+        out_specs=pl.BlockSpec(memory_space=pl.ANY),
+        out_shape=jax.ShapeDtypeStruct((part.shape[0], columns), part.dtype),
+        scratch_shapes=[pltpu.SemaphoreType.DMA],
+        input_output_aliases={1: 0} if held else {},
+        name="place",
+        cost_estimate=SHORT,
+    )(part, *held, *earlier)
+
+
 def per_device(flight, modulation, project_in, project_out, stale_cache, visible):
     current = flight[0, 0]
     modulate = modulation[0, 0]
     token_rows, features = current.shape
     devices = lax.axis_size("sp") * lax.axis_size("cfg")
-    wide = current.astype(jnp.float32)
-
-    gate = modulate[2]
-    other_gate = from_partner(gate, "cfg", 1)
-    last = lax.axis_index("pipe") == lax.axis_size("pipe") - 1
-    conditional = lax.axis_index("cfg") == 1
-    weight = jnp.where(conditional, guidance_scale, 1.0 - guidance_scale)
-    other_weight = jnp.where(conditional, 1.0 - guidance_scale, guidance_scale)
-    own_sent = jnp.where(last, weight, 0.0)
-    other_sent = jnp.where(last, other_weight, 1.0)
-    own_kept = jnp.where(last, weight, 1.0)
-    other_kept = jnp.where(last, other_weight, 0.0)
+
+    context_rows = stale_cache.shape[2]
+    width = project_in.shape[3]
+    packed = stale_cache[0, 0].reshape(context_rows, 2, devices, width)
+    packed = packed.transpose(2, 0, 1, 3).reshape(devices, context_rows, 2 * width)
 
     own = modulated_norm(current, modulate)
     across = from_partner(own, "cfg", 1)
     along = from_partner(own, "sp", 2)
     own_core = from_partner(own, "sp", 1)
     middle = features // 2
-    first = from_partner(across[:, :middle], "sp", 2)
-    second = from_partner(along[:, middle:], "cfg", 1)
+    first = from_partner(half_of(across, 0, packed), "sp", 2)
+    second = from_partner(half_of(along, middle, packed), "cfg", 1)
     across_core = from_partner(across, "sp", 1)
     along_core = from_partner(along, "sp", 1)
     first_core = from_partner(first, "sp", 1)
     second_core = from_partner(second, "sp", 1)
-
-    context_rows = stale_cache.shape[2]
-    width = project_in.shape[3]
-    packed = stale_cache[0, 0].reshape(context_rows, 2, devices, width)
-    packed = packed.transpose(2, 0, 1, 3).reshape(devices, context_rows, 2 * width)
+    gate = modulate[2:3]
+    gates = jnp.concatenate([gate, from_partner(gate, "cfg", 1)], axis=0)
+
     packed = after(packed, (first, second))
     context = lax.all_to_all(packed, ("sp", "cfg"), split_axis=0, concat_axis=0, tiled=True)
     context = context.reshape(devices * context_rows, 2 * width)
@@ -246,50 +425,54 @@
         (own, across, along, first, second),
         (own_core, across_core, along_core, first_core, second_core),
         project_in[0],
+        gates,
     )
     attended = attend(heads, context, visible[0])
 
-    rows_kept, rows_sent = attended[: 4 * token_rows], attended[4 * token_rows :]
-    chunk = features // COLUMN_CHUNKS
-    half = chunk // 2
-    results = []
-    previous = None
-    for start in range(0, features, chunk):
-        weights = project_out[0, :, start : start + chunk]
-        sent = jnp.dot(rows_sent, weights, preferred_element_type=jnp.float32)
-        received = from_partner(sent.astype(jnp.bfloat16), "sp", 1)
-        kept = jnp.dot(rows_kept, weights, preferred_element_type=jnp.float32)
-        kept = (kept + received.astype(jnp.float32)).reshape(2, 2, token_rows, chunk)
-
-        columns = slice(start, start + half)
-        own, other = kept[:, 0, :, :half] * gate[columns], kept[:, 1, :, :half] * other_gate[columns]
-        mine = jnp.stack([wide[:, columns], jnp.zeros_like(wide[:, columns])])
-        first_out = (own_sent * (own + mine) + other_sent * other).astype(jnp.bfloat16)
-        first = own_kept * (own + mine) + other_kept * other
-        second_out = kept[1, :, :, half:].astype(jnp.bfloat16)
-        second = kept[0, :, :, half:]
-        if previous is not None:
-            first_out = after(first_out, previous)
-            second_out = after(second_out, previous)
-        first_in = from_partner(first_out, "cfg", 1)
-        second_in = from_partner(second_out, "sp", 2)
-        previous = (first_in, second_in)
-
-        first = first + first_in.astype(jnp.float32)
-        first_in = from_partner(first[1].astype(jnp.bfloat16), "sp", 2)
-        columns = slice(start + half, start + chunk)
-        second = second + second_in.astype(jnp.float32)
-        own, other = second[0] * gate[columns], second[1] * other_gate[columns]
-        mine = wide[:, columns]
-        second_out = (own_sent * (own + mine) + other_sent * other).astype(jnp.bfloat16)
-        second_in = from_partner(second_out, "cfg", 1)
-        second = own_kept * (own + mine) + other_kept * other
-
-        first = first[0] + first_in.astype(jnp.float32)
-        second = second + second_in.astype(jnp.float32)
-        summed = jnp.concatenate([first, second], axis=1).astype(jnp.bfloat16)
-        results.append(from_behind(summed, "pipe", 1))
-    return jnp.concatenate(results, axis=1)[None, None]
+    weights = project_out[0]
+    count = COLUMN_CHUNKS
+    chunk = features // count
+    received = [from_partner(part, "sp", 1) for part in sent_products(attended, weights, chunk)]
+    kept, left, flights, result, arrivals, earlier = {}, {}, {}, [], [], []
+    for index in range(-2, count + 2):
+        fresh, middle, final = index + 2 < count, 0 <= index < count, index >= 2
+        operands = {"rows": current, "gates": gates}
+        if fresh:
+            operands["attended"], operands["weights"] = attended, weights
+            operands["received"] = received[min(index + 2, 1)]
+        if index >= 0:
+            operands["across"], operands["along"] = flights.pop(index)
+        if middle:
+            operands["first_kept"], operands["second_kept"] = kept.pop(index)
+        if final:
+            operands["first_left"], operands["second_left"] = left.pop(index - 2)
+        outs = stage(
+            operands,
+            earlier,
+            chunk,
+            max(index, 0) * chunk,
+            (index + 2) * chunk,
+            max(index + 1, 0),
+            fresh,
+            middle,
+            final,
+        )
+        if "across_out" in outs:
+            flights[index + 2] = (
+                from_partner(outs["across_out"], "cfg", 1),
+                from_partner(outs["along_out"], "sp", 2),
+            )
+        if fresh:
+            kept[index + 2] = (outs["first_kept_out"], outs["second_kept_out"])
+        if middle:
+            left[index] = (outs["first_left_out"], outs["second_left_out"])
+        if final:
+            arrived = from_behind(outs["done_out"], "pipe", 1)
+            whole = result[-1] if result else None
+            result.append(place(arrived, whole, features, (index - 2) * chunk, []))
+            arrivals.append(arrived)
+        earlier = [list(outs.values())[-1]] + (arrivals[-2:-1] if 3 <= index < count else [])
+    return result[-1][None, None]
 
 
 def solution(mesh):

time: 217 us -> 244 us (1.12)
  Pallas kernels: 30.9 us -> 85.3 us
  other arithmetic: 26 us -> 0.04 us
  waiting for transfers between devices: 63.9 us -> 83.3 us
  matrix products: 13.2 us -> 0 us
  local copies, waits for them, and re-layouts: 41.3 us -> 34 us
    pallas_call x0 -> x17, Pallas kernels: none -> 53.5 us  [the longest x5 45.2 us: place(): pl.pallas_call(functools.partial(place_kernel, start=start), in_specs=[pl...]
    ppermute x30 -> x26, waiting for transfers between devices: 51.1 us -> 81.6 us  [from_partner(): return lax.ppermute(value, axis, pairs)]
    dot_general x8 -> x0, matrix products: 13.2 us -> none  [the longest x4 8.44 us: per_device(): sent = jnp.dot(rows_sent, weights, preferred_element_type=jnp.float32)]
    add x6 -> x0, other arithmetic: 7.17 us -> none  [the longest x4 7.05 us: per_device(): first = first + first_in.astype(jnp.float32)]
    convert_element_type x7 -> x0, other arithmetic: 6.81 us -> none  [the longest x6 3.73 us: per_device(): (own_sent * (own + mine) + other_sent * other).astype(jnp.bfloat16)]
    another operation x7 -> x0, other arithmetic: 6.05 us -> none
    ppermute x4 -> x5, waiting for transfers between devices: 7.44 us -> 1.71 us  [from_behind(): return lax.ppermute(x, axis, [(i, (i + by) % count) for i in range(count)])]
    all_to_all x1, waiting for transfers between devices: 5.36 us -> 0.01 us  [per_device(): lax.all_to_all(packed, ('sp', 'cfg'), split_axis=0, concat_axis=0, tiled=...]
  transfers between devices with their start and end apart: 35 -> 32, of which waited for: 16 -> 17; matrix products, arithmetic and copies ran while one was open for 30% -> 9% of each run, Pallas kernels for 13% -> 25%
where the time goes in v4:
time: 244 us; the launch traced here: 243 us
  Pallas kernels  85.3 us (35%)
  waiting for transfers between devices  83.3 us (34%)
  starting transfers between devices  40.4 us (17%)
  local copies, waits for them, and re-layouts  34 us (14%)
    ppermute x26, waiting for transfers between devices, from_partner(): return lax.ppermute(value, axis, pairs)  81.6 us
    pallas_call x5, Pallas kernels, place(): pl.pallas_call(functools.partial(place_kernel, start=start), in_specs=[pl...  45.2 us
    ppermute x26, starting transfers between devices, from_partner(): return lax.ppermute(value, axis, pairs)  27.6 us
    pallas_call x1, Pallas kernels, project(): pl.pallas_call(project_kernel, grid=(steps,), in_specs=[whole] * 6 + [fir...  19.6 us
    another operation x2, local copies, waits for them, and re-layouts, per_device(): packed = stale_cache[0, 0].reshape(context_rows, 2, devices, width)  13.9 us
    unnamed x33, local copies, waits for them, and re-layouts  11.3 us
    pallas_call x1, Pallas kernels, attend(): pl.pallas_call(attend_kernel, in_specs=[pl.BlockSpec(memory_space=pltpu.S...  8.72 us
    reshape x1, local copies, waits for them, and re-layouts, per_device(): packed.transpose(2, 0, 1, 3).reshape(devices, context_rows, 2 * width)  8.05 us
  transfers between devices with their start and end apart: 32, of which 17 were waited for; matrix products, arithmetic and copies ran while one was open for 9% of the time, Pallas kernels for 25%

profile of v4, /device:TPU:0, one launch (start us, length us, event | category | flops | bytes accessed | tf_op | source)
XLA Modules:
  0.0 243.5 jit_solution(12503174425802219091)
XLA Ops:
  0.0 0.8 copy.17
  0.9 1.3 copy-done.1
  2.2 3.5 %modulated_norm.1.refs_0_ = bf16[128,5120]{1,0:T(8,128)(2,1)} custom-call(bf16[128,5120]{1,0:T(8,128)(2,1)S(1)} %bitcast.20, f32[3,5120]{1,0:T(4,128)S(1)} %bitcast.30), custom_call_target="tpu_custom_call" | custom-call | flops 6553600 | bytes 2621440 | tf_op jit(solution)/shard_map/modulated_norm/pallas_call | solution.py:47
  5.7 2.9 %collective-permute-start.1 = (bf16[128,5120]{1,0:T(8,128)(2,1)}, bf16[128,5120]{1,0:T(8,128)(2,1)S(1)}, u32[]{:S(2)}, u32[]{:S(2)}) collective-permute-start(bf16[128,5120]{1,0:T(8,128)(2,1)} %modulated_norm.1.refs_0_), channel_id=1, source_target_pairs={{0,1},{1,0},{2,3},{3,2},{4,5},{5,4},{6,7},{7,6},{8,9},{9,8},{10,11... | collective-permute-start | bytes 3932168 | tf_op jit(solution)/shard_map/ppermute | solution.py:26
  8.6 1.5 collective-permute-start.2
  10.1 8.0 %reshape_squeeze.3 = bf16[256,2,8,384]{3,2,1,0:T(8,128)(2,1)} reshape(bf16[1,1,256,2,3072]{4,3,2,1,0:T(2,128)(2,1)} %param.10) | data formatting | bytes 6291456 | tf_op jit(solution)/shard_map/reshape;squeeze | solution.py:403
  18.2 5.9 %copy.16 = bf16[256,2,8,384]{3,1,0,2:T(2,128)(2,1)} copy(bf16[256,2,8,384]{3,2,1,0:T(8,128)(2,1)} %reshape_squeeze.3) | data formatting | bytes 6291456 | tf_op jit(solution)/shard_map/reshape;squeeze | solution.py:403
  24.1 8.0 %reshape.7.refs_0_.value_ref = bf16[8,256,768]{2,1,0:T(8,128)(2,1)} reshape(bf16[8,256,2,384]{3,2,1,0:T(2,128)(2,1)} %bitcast.32) | data formatting | bytes 6291456 | tf_op jit(solution)/shard_map/reshape | solution.py:404
  32.1 5.5 %collective-permute-done.1.rows_ref.refs_1_ = bf16[128,5120]{1,0:T(8,128)(2,1)S(1)} collective-permute-done((bf16[128,5120]{1,0:T(8,128)(2,1)}, bf16[128,5120]{1,0:T(8,128)(2,1)S(1)}, u32[]{:S(2)}, u32[]{:S(2)}) %collective-permute-start.1) | collective-permute-done | bytes 1310752 | tf_op jit(solution)/shard_map/ppermute | solution.py:26
  37.6 1.9 copy-done.3
  39.5 1.8 collective-permute-start.6
  41.4 1.6 collective-permute-start.7
  43.5 12.0 %collective-permute-done.6.refs_6_.refs_0_ = bf16[128,2560]{1,0:T(8,128)(2,1)S(1)} collective-permute-done((bf16[128,2560]{1,0:T(8,128)(2,1)S(1)}, bf16[128,2560]{1,0:T(8,128)(2,1)S(1)}, u32[]{:S(2)}, u32[]{:S(2)}) %collective-permute-start.6) | collective-permute-done | bytes 655392 | tf_op jit(solution)/shard_map/ppermute | solution.py:26
  55.5 1.4 collective-permute-done.7.refs_7_.refs_1_
  56.9 4.8 %all-to-all-start = ((bf16[8,256,768]{2,1,0:T(8,128)(2,1)}), bf16[8,256,768]{2,1,0:T(8,128)(2,1)}, u32[]{:S(2)}, u32[]{:S(2)}) async-start(bf16[8,256,768]{2,1,0:T(8,128)(2,1)} %after.1), calls=%async_computation | async-start | bytes 6291456 | tf_op jit(solution)/shard_map/all_to_all | solution.py:421
  61.7 0.7 slice_bitcast_fusion
  62.5 1.7 collective-permute-start
  64.2 34.7 %collective-permute-done = f32[1,5120]{1,0:T(1,128)S(1)} collective-permute-done((f32[1,5120]{1,0:T(1,128)S(1)}, f32[1,5120]{1,0:T(1,128)S(1)}, u32[]{:S(2)}, u32[]{:S(2)}) %collective-permute-start) | collective-permute-done | bytes 20512 | tf_op jit(solution)/shard_map/ppermute | solution.py:26
  98.9 2.2 collective-permute-done.9.refs_9_
  101.2 1.3 copy-done.7
  102.5 19.6 %project_heads.1.heads_ref = bf16[1024,1152]{1,0:T(8,128)(2,1)S(1)} custom-call(bf16[128,5120]{1,0:T(8,128)(2,1)} %modulated_norm.1.refs_0_, bf16[128,5120]{1,0:T(8,128)(2,1)S(1)} %collective-permute-done.1.rows_ref.refs_1_, bf16[128,5120]{1,0:T(8,128)(2,1)S(1)} %copy-done.7, bf16[128,5120]{1,0:T(8,128)(2,1)} %collective-permute-done.3.refs_3_, ...), custom_call_target="tpu_custom_call" | custom-call | flops 12079595520 | bytes 22282240 | tf_op jit(solution)/shard_map/project_heads/pallas_call | solution.py:114
  122.0 1.5 copy-done.4
  123.5 1.7 copy-done.5
  125.2 8.7 %attend.1.attended_ref.refs_2_ = bf16[1024,384]{1,0:T(8,128)(2,1)S(1)} custom-call(s32[4,6]{1,0:T(4,128)S(1)} %bitcast.31, bf16[1024,1152]{1,0:T(8,128)(2,1)S(1)} %copy-done.5, bf16[2048,768]{1,0:T(8,128)(2,1)} %bitcast.5.context_ref), custom_call_target="tpu_custom_call" | custom-call | flops 1207959552 | bytes 5505024 | tf_op jit(solution)/shard_map/attend/pallas_call | solution.py:195
  133.9 2.9 %sent_products.1 = (bf16[1,512,1024]{2,1,0:T(8,128)(2,1)S(1)}, bf16[4,512,1024]{2,1,0:T(8,128)(2,1)S(1)}) custom-call(bf16[1024,384]{1,0:T(8,128)(2,1)S(1)} %attend.1.attended_ref.refs_2_, bf16[384,5120]{1,0:T(8,128)(2,1)S(1)} %bitcast.14), custom_call_target="tpu_custom_call" | custom-call | flops 1 | bytes 1 | tf_op jit(solution)/shard_map/sent_products/pallas_call | solution.py:242
  137.4 8.1 %collective-permute-done.11.refs_4_ = bf16[1,512,1024]{2,1,0:T(8,128)(2,1)S(1)} collective-permute-done((bf16[1,512,1024]{2,1,0:T(8,128)(2,1)S(1)}, bf16[1,512,1024]{2,1,0:T(8,128)(2,1)S(1)}, u32[]{:S(2)}, u32[]{:S(2)}) %collective-permute-start.11) | collective-permute-done | bytes 1048608 | tf_op jit(solution)/shard_map/ppermute | solution.py:26
  145.6 0.8 sum_stage.9
  146.8 1.7 collective-permute-start.13
  148.4 0.8 sum_stage.10
  149.2 1.6 collective-permute-start.16
  151.4 4.2 %collective-permute-done.12.refs_5_ = bf16[2,128,512]{2,1,0:T(8,128)(2,1)S(1)} collective-permute-done((bf16[2,128,512]{2,1,0:T(8,128)(2,1)S(1)}, bf16[2,128,512]{2,1,0:T(8,128)(2,1)S(1)}, u32[]{:S(2)}, u32[]{:S(2)}) %collective-permute-start.12) | collective-permute-done | bytes 262176 | tf_op jit(solution)/shard_map/ppermute | solution.py:26
  156.0 1.0 sum_stage.11
  157.0 1.8 collective-permute-start.14
  158.8 1.5 collective-permute-start.15
  160.2 1.0 collective-permute-done.16.refs_5_
  161.6 1.0 sum_stage.12
  162.6 1.8 collective-permute-start.20
  164.4 1.5 collective-permute-start.21
  165.9 3.8 %collective-permute-done.14.refs_5_ = bf16[3,128,512]{2,1,0:T(8,128)(2,1)S(1)} collective-permute-done((bf16[3,128,512]{2,1,0:T(8,128)(2,1)S(1)}, bf16[3,128,512]{2,1,0:T(8,128)(2,1)S(1)}, u32[]{:S(2)}, u32[]{:S(2)}) %collective-permute-start.14) | collective-permute-done | bytes 393248 | tf_op jit(solution)/shard_map/ppermute | solution.py:26
  169.6 1.2 collective-permute-done.15.refs_6_
  170.8 1.1 sum_stage.13
  171.9 1.0 collective-permute-start.18
  172.9 1.5 collective-permute-start.19
  174.3 1.6 collective-permute-start.22
  175.9 2.1 collective-permute-done.20.refs_2_
  178.1 1.2 collective-permute-done.21.refs_3_
  179.5 1.6 collective-permute-start.27
  181.1 0.9 collective-permute-start.25
  182.0 1.7 collective-permute-done.22.refs_9_.part_ref
  183.7 2.8 %collective-permute-done.18.refs_2_ = bf16[3,128,512]{2,1,0:T(8,128)(2,1)S(1)} collective-permute-done((bf16[3,128,512]{2,1,0:T(8,128)(2,1)S(1)}, bf16[3,128,512]{2,1,0:T(8,128)(2,1)S(1)}, u32[]{:S(2)}, u32[]{:S(2)}) %collective-permute-start.18) | collective-permute-done | bytes 393248 | tf_op jit(solution)/shard_map/ppermute | solution.py:26
  186.5 0.7 collective-permute-done.19.refs_3_
  187.4 1.5 collective-permute-start.23
  188.9 1.5 collective-permute-start.24
  190.3 1.6 collective-permute-start.30
  192.6 1.6 collective-permute-start.29
  194.3 1.6 collective-permute-start.28
  195.9 9.0 %place.5.refs_0_ = bf16[128,5120]{1,0:T(8,128)(2,1)} custom-call(bf16[128,1024]{1,0:T(8,128)(2,1)} %copy-done.8), custom_call_target="tpu_custom_call" | custom-call | flops 1 | bytes 1 | tf_op jit(solution)/shard_map/place/pallas_call | solution.py:383
  205.0 9.1 %place.6.refs_0_ = bf16[128,5120]{1,0:T(8,128)(2,1)} custom-call(bf16[128,1024]{1,0:T(8,128)(2,1)} %copy-done.9, bf16[128,5120]{1,0:T(8,128)(2,1)} %place.5.refs_0_), custom_call_target="tpu_custom_call", output_to_operand_aliasing={{}: (1, {})} | custom-call | flops 1 | bytes 1 | tf_op jit(solution)/shard_map/place/pallas_call | solution.py:383
  214.0 0.7 copy-done.13
  214.7 9.0 %place.7.refs_0_ = bf16[128,5120]{1,0:T(8,128)(2,1)} custom-call(bf16[128,1024]{1,0:T(8,128)(2,1)} %copy-done.13, bf16[128,5120]{1,0:T(8,128)(2,1)} %place.6.refs_0_), custom_call_target="tpu_custom_call", output_to_operand_aliasing={{}: (1, {})} | custom-call | flops 1 | bytes 1 | tf_op jit(solution)/shard_map/place/pallas_call | solution.py:383
  223.8 0.7 copy-done.14
  224.5 9.0 %place.8.refs_0_ = bf16[128,5120]{1,0:T(8,128)(2,1)} custom-call(bf16[128,1024]{1,0:T(8,128)(2,1)} %copy-done.14, bf16[128,5120]{1,0:T(8,128)(2,1)} %place.7.refs_0_), custom_call_target="tpu_custom_call", output_to_operand_aliasing={{}: (1, {})} | custom-call | flops 1 | bytes 1 | tf_op jit(solution)/shard_map/place/pallas_call | solution.py:383
  233.6 0.7 copy-done.15
  234.3 9.0 %place.9 = bf16[128,5120]{1,0:T(8,128)(2,1)} custom-call(bf16[128,1024]{1,0:T(8,128)(2,1)} %copy-done.15, bf16[128,5120]{1,0:T(8,128)(2,1)} %place.8.refs_0_), custom_call_target="tpu_custom_call", output_to_operand_aliasing={{}: (1, {})} | custom-call | flops 1 | bytes 1 | tf_op jit(solution)/shard_map/place/pallas_call | solution.py:383
  (59 shorter events, 4.1 us)
Async XLA Ops:
  0.9 1.3 copy-start.1
  5.7 31.9 %collective-permute-start.1 = (bf16[128,5120]{1,0:T(8,128)(2,1)}, bf16[128,5120]{1,0:T(8,128)(2,1)S(1)}, u32[]{:S(2)}, u32[]{:S(2)}) collective-permute-start(bf16[128,5120]{1,0:T(8,128)(2,1)} %modulated_norm.1.refs_0_), channel_id=1, source_target_pairs={{0,1},{1,0},{2,3},{3,2},{4,5},{5,4},{6,7},{7,6},{8,9},{9,8},{10,11... | collective-permute-start | bytes 3932168 | tf_op jit(solution)/shard_map/ppermute | solution.py:26
  8.6 32.8 %collective-permute-start.2 = (bf16[128,5120]{1,0:T(8,128)(2,1)}, bf16[128,5120]{1,0:T(8,128)(2,1)S(1)}, u32[]{:S(2)}, u32[]{:S(2)}) collective-permute-start(bf16[128,5120]{1,0:T(8,128)(2,1)} %modulated_norm.1.refs_0_), channel_id=1, source_target_pairs={{0,4},{2,6},{4,0},{6,2},{1,5},{3,7},{5,1},{7,3},{8,12},{10,14},{12... | collective-permute-start | bytes 3932168 | tf_op jit(solution)/shard_map/ppermute | solution.py:26
  37.6 1.9 copy-start.3
  39.5 16.0 %collective-permute-start.6 = (bf16[128,2560]{1,0:T(8,128)(2,1)S(1)}, bf16[128,2560]{1,0:T(8,128)(2,1)S(1)}, u32[]{:S(2)}, u32[]{:S(2)}) collective-permute-start(bf16[128,2560]{1,0:T(8,128)(2,1)S(1)} %half_of.2), channel_id=1, source_target_pairs={{0,4},{2,6},{4,0},{6,2},{1,5},{3,7},{5,1},{7,3},{8,12},{10,14},{12... | collective-permute-start | bytes 1966088 | tf_op jit(solution)/shard_map/ppermute | solution.py:26
  41.4 2.1 copy-start.6
  41.4 15.5 %collective-permute-start.7 = (bf16[128,2560]{1,0:T(8,128)(2,1)S(1)}, bf16[128,2560]{1,0:T(8,128)(2,1)}, u32[]{:S(2)}, u32[]{:S(2)}) collective-permute-start(bf16[128,2560]{1,0:T(8,128)(2,1)S(1)} %half_of.3), channel_id=1, source_target_pairs={{0,1},{1,0},{2,3},{3,2},{4,5},{5,4},{6,7},{7,6},{8,9},{9,8},{10,11... | collective-permute-start | bytes 1966088 | tf_op jit(solution)/shard_map/ppermute | solution.py:26
  43.0 55.9 %collective-permute-start.3 = (bf16[128,5120]{1,0:T(8,128)(2,1)}, bf16[128,5120]{1,0:T(8,128)(2,1)}, u32[]{:S(2)}, u32[]{:S(2)}) collective-permute-start(bf16[128,5120]{1,0:T(8,128)(2,1)} %modulated_norm.1.refs_0_), channel_id=1, source_target_pairs={{0,2},{2,0},{4,6},{6,4},{1,3},{3,1},{5,7},{7,5},{8,10},{10,8},{12,... | collective-permute-start | bytes 3932168 | tf_op jit(solution)/shard_map/ppermute | solution.py:26
  43.0 58.1 %collective-permute-start.4 = (bf16[128,5120]{1,0:T(8,128)(2,1)S(1)}, bf16[128,5120]{1,0:T(8,128)(2,1)}, u32[]{:S(2)}, u32[]{:S(2)}) collective-permute-start(bf16[128,5120]{1,0:T(8,128)(2,1)S(1)} %collective-permute-done.1.rows_ref.refs_1_), channel_id=1, source_target_pairs={{0,2},{2,0},{4,6},{6,4},{1,3},{3,1},{5,7},{7,5},{8,10},{10,8},{12,... | collective-permute-start | bytes 3932168 | tf_op jit(solution)/shard_map/ppermute | solution.py:26
  43.5 57.6 %collective-permute-start.5 = (bf16[128,5120]{1,0:T(8,128)(2,1)S(1)}, bf16[128,5120]{1,0:T(8,128)(2,1)}, u32[]{:S(2)}, u32[]{:S(2)}) collective-permute-start(bf16[128,5120]{1,0:T(8,128)(2,1)S(1)} %collective-permute-done.2.rows_ref.refs_2_), channel_id=1, source_target_pairs={{0,2},{2,0},{4,6},{6,4},{1,3},{3,1},{5,7},{7,5},{8,10},{10,8},{12,... | collective-permute-start | bytes 3932168 | tf_op jit(solution)/shard_map/ppermute | solution.py:26
  55.5 1.4 copy-start.10
  56.9 7.2 %copy-start.11 = (bf16[128,2560]{1,0:T(8,128)(2,1)S(1)}, bf16[128,2560]{1,0:T(8,128)(2,1)}, u32[]{:S(2)}) copy-start(bf16[128,2560]{1,0:T(8,128)(2,1)} %copy-done.10) | copy-start | bytes 1966084
  56.9 66.6 %all-to-all-start = ((bf16[8,256,768]{2,1,0:T(8,128)(2,1)}), bf16[8,256,768]{2,1,0:T(8,128)(2,1)}, u32[]{:S(2)}, u32[]{:S(2)}) async-start(bf16[8,256,768]{2,1,0:T(8,128)(2,1)} %after.1), calls=%async_computation | async-start | bytes 6291456 | tf_op jit(solution)/shard_map/all_to_all | solution.py:421
  62.5 36.4 %collective-permute-start = (f32[1,5120]{1,0:T(1,128)S(1)}, f32[1,5120]{1,0:T(1,128)S(1)}, u32[]{:S(2)}, u32[]{:S(2)}) collective-permute-start(f32[1,5120]{1,0:T(1,128)S(1)} %slice_bitcast_fusion), channel_id=1, source_target_pairs={{0,1},{1,0},{2,3},{3,2},{4,5},{5,4},{6,7},{7,6},{8,9},{9,8},{10,11... | collective-permute-start | bytes 61448 | tf_op jit(solution)/shard_map/ppermute | solution.py:26
  64.2 34.7 %collective-permute-start.8 = (bf16[128,2560]{1,0:T(8,128)(2,1)S(1)}, bf16[128,2560]{1,0:T(8,128)(2,1)S(1)}, u32[]{:S(2)}, u32[]{:S(2)}) collective-permute-start(bf16[128,2560]{1,0:T(8,128)(2,1)S(1)} %copy-done.11), channel_id=1, source_target_pairs={{0,2},{2,0},{4,6},{6,4},{1,3},{3,1},{5,7},{7,5},{8,10},{10,8},{12,... | collective-permute-start | bytes 1966088 | tf_op jit(solution)/shard_map/ppermute | solution.py:26
  98.8 2.3 collective-permute-start.9
  101.1 1.3 copy-start.7
  102.5 21.0 %copy-start.12 = (s32[1,4,6]{2,1,0:T(4,128)S(1)}, s32[1,4,6]{2,1,0:T(4,128)}, u32[]{:S(2)}) copy-start(s32[1,4,6]{2,1,0:T(4,128)} %param.11) | copy-start | bytes 292
  122.0 1.5 copy-start.4
  123.5 1.7 copy-start.5
  125.2 8.7 %copy-start = (bf16[1,384,5120]{2,1,0:T(8,128)(2,1)S(1)}, bf16[1,384,5120]{2,1,0:T(8,128)(2,1)}, u32[]{:S(2)}) copy-start(bf16[1,384,5120]{2,1,0:T(8,128)(2,1)} %param.9) | copy-start | bytes 11796484
  133.9 11.6 %copy-start.2 = (bf16[1,1,128,5120]{3,2,1,0:T(8,128)(2,1)S(1)}, bf16[1,1,128,5120]{3,2,1,0:T(8,128)(2,1)}, u32[]{:S(2)}) copy-start(bf16[1,1,128,5120]{3,2,1,0:T(8,128)(2,1)} %param.6) | copy-start | bytes 3932164
  136.8 11.6 %collective-permute-start.10 = (bf16[4,512,1024]{2,1,0:T(8,128)(2,1)S(1)}, bf16[4,512,1024]{2,1,0:T(8,128)(2,1)S(1)}, u32[]{:S(2)}, u32[]{:S(2)}) collective-permute-start(bf16[4,512,1024]{2,1,0:T(8,128)(2,1)S(1)} %get-tuple-element.44), channel_id=1, source_target_pairs={{0,2},{2,0},{4,6},{6,4},{1,3},{3,1},{5,7},{7,5},{8,10},{10,8},{12,... | collective-permute-start | bytes 12582920 | tf_op jit(solution)/shard_map/ppermute | solution.py:26
  137.0 8.5 %collective-permute-start.11 = (bf16[1,512,1024]{2,1,0:T(8,128)(2,1)S(1)}, bf16[1,512,1024]{2,1,0:T(8,128)(2,1)S(1)}, u32[]{:S(2)}, u32[]{:S(2)}) collective-permute-start(bf16[1,512,1024]{2,1,0:T(8,128)(2,1)S(1)} %get-tuple-element.45), channel_id=1, source_target_pairs={{0,2},{2,0},{4,6},{6,4},{1,3},{3,1},{5,7},{7,5},{8,10},{10,8},{12,... | collective-permute-start | bytes 3145736 | tf_op jit(solution)/shard_map/ppermute | solution.py:26
  146.4 9.2 %collective-permute-start.12 = (bf16[2,128,512]{2,1,0:T(8,128)(2,1)S(1)}, bf16[2,128,512]{2,1,0:T(8,128)(2,1)S(1)}, u32[]{:S(2)}, u32[]{:S(2)}) collective-permute-start(bf16[2,128,512]{2,1,0:T(8,128)(2,1)S(1)} %get-tuple-element.46), channel_id=1, source_target_pairs={{0,1},{1,0},{2,3},{3,2},{4,5},{5,4},{6,7},{7,6},{8,9},{9,8},{10,11... | collective-permute-start | bytes 786440 | tf_op jit(solution)/shard_map/ppermute | solution.py:26
  146.8 9.2 %collective-permute-start.13 = (bf16[2,128,512]{2,1,0:T(8,128)(2,1)S(1)}, bf16[2,128,512]{2,1,0:T(8,128)(2,1)S(1)}, u32[]{:S(2)}, u32[]{:S(2)}) collective-permute-start(bf16[2,128,512]{2,1,0:T(8,128)(2,1)S(1)} %get-tuple-element.47), channel_id=1, source_target_pairs={{0,4},{2,6},{4,0},{6,2},{1,5},{3,7},{5,1},{7,3},{8,12},{10,14},{12... | collective-permute-start | bytes 786440 | tf_op jit(solution)/shard_map/ppermute | solution.py:26
  149.2 12.0 %collective-permute-start.16 = (bf16[2,128,512]{2,1,0:T(8,128)(2,1)S(1)}, bf16[2,128,512]{2,1,0:T(8,128)(2,1)S(1)}, u32[]{:S(2)}, u32[]{:S(2)}) collective-permute-start(bf16[2,128,512]{2,1,0:T(8,128)(2,1)S(1)} %get-tuple-element.57), channel_id=1, source_target_pairs={{0,1},{1,0},{2,3},{3,2},{4,5},{5,4},{6,7},{7,6},{8,9},{9,8},{10,11... | collective-permute-start | bytes 786440 | tf_op jit(solution)/shard_map/ppermute | solution.py:26
  150.8 10.7 %collective-permute-start.17 = (bf16[2,128,512]{2,1,0:T(8,128)(2,1)S(1)}, bf16[2,128,512]{2,1,0:T(8,128)(2,1)S(1)}, u32[]{:S(2)}, u32[]{:S(2)}) collective-permute-start(bf16[2,128,512]{2,1,0:T(8,128)(2,1)S(1)} %get-tuple-element.58), channel_id=1, source_target_pairs={{0,4},{2,6},{4,0},{6,2},{1,5},{3,7},{5,1},{7,3},{8,12},{10,14},{12... | collective-permute-start | bytes 786440 | tf_op jit(solution)/shard_map/ppermute | solution.py:26
  157.0 12.6 %collective-permute-start.14 = (bf16[3,128,512]{2,1,0:T(8,128)(2,1)S(1)}, bf16[3,128,512]{2,1,0:T(8,128)(2,1)S(1)}, u32[]{:S(2)}, u32[]{:S(2)}) collective-permute-start(bf16[3,128,512]{2,1,0:T(8,128)(2,1)S(1)} %get-tuple-element.51), channel_id=1, source_target_pairs={{0,1},{1,0},{2,3},{3,2},{4,5},{5,4},{6,7},{7,6},{8,9},{9,8},{10,11... | collective-permute-start | bytes 1179656 | tf_op jit(solution)/shard_map/ppermute | solution.py:26
  158.8 12.1 %collective-permute-start.15 = (bf16[3,128,512]{2,1,0:T(8,128)(2,1)S(1)}, bf16[3,128,512]{2,1,0:T(8,128)(2,1)S(1)}, u32[]{:S(2)}, u32[]{:S(2)}) collective-permute-start(bf16[3,128,512]{2,1,0:T(8,128)(2,1)S(1)} %get-tuple-element.52), channel_id=1, source_target_pairs={{0,4},{2,6},{4,0},{6,2},{1,5},{3,7},{5,1},{7,3},{8,12},{10,14},{12... | collective-permute-start | bytes 1179656 | tf_op jit(solution)/shard_map/ppermute | solution.py:26
  162.6 15.5 %collective-permute-start.20 = (bf16[3,128,512]{2,1,0:T(8,128)(2,1)S(1)}, bf16[3,128,512]{2,1,0:T(8,128)(2,1)S(1)}, u32[]{:S(2)}, u32[]{:S(2)}) collective-permute-start(bf16[3,128,512]{2,1,0:T(8,128)(2,1)S(1)} %get-tuple-element.67), channel_id=1, source_target_pairs={{0,1},{1,0},{2,3},{3,2},{4,5},{5,4},{6,7},{7,6},{8,9},{9,8},{10,11... | collective-permute-start | bytes 1179656 | tf_op jit(solution)/shard_map/ppermute | solution.py:26
  164.4 14.9 %collective-permute-start.21 = (bf16[3,128,512]{2,1,0:T(8,128)(2,1)S(1)}, bf16[3,128,512]{2,1,0:T(8,128)(2,1)S(1)}, u32[]{:S(2)}, u32[]{:S(2)}) collective-permute-start(bf16[3,128,512]{2,1,0:T(8,128)(2,1)S(1)} %get-tuple-element.68), channel_id=1, source_target_pairs={{0,4},{2,6},{4,0},{6,2},{1,5},{3,7},{5,1},{7,3},{8,12},{10,14},{12... | collective-permute-start | bytes 1179656 | tf_op jit(solution)/shard_map/ppermute | solution.py:26
  171.9 14.6 %collective-permute-start.18 = (bf16[3,128,512]{2,1,0:T(8,128)(2,1)S(1)}, bf16[3,128,512]{2,1,0:T(8,128)(2,1)S(1)}, u32[]{:S(2)}, u32[]{:S(2)}) collective-permute-start(bf16[3,128,512]{2,1,0:T(8,128)(2,1)S(1)} %get-tuple-element.61), channel_id=1, source_target_pairs={{0,1},{1,0},{2,3},{3,2},{4,5},{5,4},{6,7},{7,6},{8,9},{9,8},{10,11... | collective-permute-start | bytes 1179656 | tf_op jit(solution)/shard_map/ppermute | solution.py:26
  172.9 14.3 %collective-permute-start.19 = (bf16[3,128,512]{2,1,0:T(8,128)(2,1)S(1)}, bf16[3,128,512]{2,1,0:T(8,128)(2,1)S(1)}, u32[]{:S(2)}, u32[]{:S(2)}) collective-permute-start(bf16[3,128,512]{2,1,0:T(8,128)(2,1)S(1)} %get-tuple-element.62), channel_id=1, source_target_pairs={{0,4},{2,6},{4,0},{6,2},{1,5},{3,7},{5,1},{7,3},{8,12},{10,14},{12... | collective-permute-start | bytes 1179656 | tf_op jit(solution)/shard_map/ppermute | solution.py:26
  174.3 9.3 %collective-permute-start.22 = (bf16[128,1024]{1,0:T(8,128)(2,1)S(1)}, bf16[128,1024]{1,0:T(8,128)(2,1)S(1)}, u32[]{:S(2)}, u32[]{:S(2)}) collective-permute-start(bf16[128,1024]{1,0:T(8,128)(2,1)S(1)} %get-tuple-element.72.refs_8_), channel_id=1, source_target_pairs={{0,8},{8,16},{16,24},{24,0},{1,9},{9,17},{17,25},{25,1},{2,10},{10... | collective-permute-start | bytes 786440 | tf_op jit(solution)/shard_map/ppermute | solution.py:21
  179.5 12.5 %collective-permute-start.27 = (bf16[128,1024]{1,0:T(8,128)(2,1)S(1)}, bf16[128,1024]{1,0:T(8,128)(2,1)S(1)}, u32[]{:S(2)}, u32[]{:S(2)}) collective-permute-start(bf16[128,1024]{1,0:T(8,128)(2,1)S(1)} %get-tuple-element.73.refs_8_), channel_id=1, source_target_pairs={{0,8},{8,16},{16,24},{24,0},{1,9},{9,17},{17,25},{25,1},{2,10},{10... | collective-permute-start | bytes 786440 | tf_op jit(solution)/shard_map/ppermute | solution.py:21
  181.1 9.2 %collective-permute-start.25 = (bf16[1,128,512]{2,1,0:T(8,128)(2,1)S(1)}, bf16[1,128,512]{2,1,0:T(8,128)(2,1)S(1)}, u32[]{:S(2)}, u32[]{:S(2)}) collective-permute-start(bf16[1,128,512]{2,1,0:T(8,128)(2,1)S(1)} %get-tuple-element.78), channel_id=1, source_target_pairs={{0,1},{1,0},{2,3},{3,2},{4,5},{5,4},{6,7},{7,6},{8,9},{9,8},{10,11... | collective-permute-start | bytes 393224 | tf_op jit(solution)/shard_map/ppermute | solution.py:26
  183.7 3.7 %copy-start.8 = (bf16[128,1024]{1,0:T(8,128)(2,1)}, bf16[128,1024]{1,0:T(8,128)(2,1)S(1)}, u32[]{:S(2)}) copy-start(bf16[128,1024]{1,0:T(8,128)(2,1)S(1)} %collective-permute-done.22.refs_9_.part_ref) | copy-start | bytes 786436
  183.7 8.2 %collective-permute-start.26 = (bf16[1,128,512]{2,1,0:T(8,128)(2,1)S(1)}, bf16[1,128,512]{2,1,0:T(8,128)(2,1)S(1)}, u32[]{:S(2)}, u32[]{:S(2)}) collective-permute-start(bf16[1,128,512]{2,1,0:T(8,128)(2,1)S(1)} %get-tuple-element.79), channel_id=1, source_target_pairs={{0,4},{2,6},{4,0},{6,2},{1,5},{3,7},{5,1},{7,3},{8,12},{10,14},{12... | collective-permute-start | bytes 393224 | tf_op jit(solution)/shard_map/ppermute | solution.py:26
  187.4 6.8 %collective-permute-start.23 = (bf16[1,128,512]{2,1,0:T(8,128)(2,1)S(1)}, bf16[1,128,512]{2,1,0:T(8,128)(2,1)S(1)}, u32[]{:S(2)}, u32[]{:S(2)}) collective-permute-start(bf16[1,128,512]{2,1,0:T(8,128)(2,1)S(1)} %get-tuple-element.74), channel_id=1, source_target_pairs={{0,1},{1,0},{2,3},{3,2},{4,5},{5,4},{6,7},{7,6},{8,9},{9,8},{10,11... | collective-permute-start | bytes 393224 | tf_op jit(solution)/shard_map/ppermute | solution.py:26
  188.9 5.4 %collective-permute-start.24 = (bf16[1,128,512]{2,1,0:T(8,128)(2,1)S(1)}, bf16[1,128,512]{2,1,0:T(8,128)(2,1)S(1)}, u32[]{:S(2)}, u32[]{:S(2)}) collective-permute-start(bf16[1,128,512]{2,1,0:T(8,128)(2,1)S(1)} %get-tuple-element.75), channel_id=1, source_target_pairs={{0,4},{2,6},{4,0},{6,2},{1,5},{3,7},{5,1},{7,3},{8,12},{10,14},{12... | collective-permute-start | bytes 393224 | tf_op jit(solution)/shard_map/ppermute | solution.py:26
  190.3 23.7 %collective-permute-start.30 = (bf16[128,1024]{1,0:T(8,128)(2,1)S(1)}, bf16[128,1024]{1,0:T(8,128)(2,1)S(1)}, u32[]{:S(2)}, u32[]{:S(2)}) collective-permute-start(bf16[128,1024]{1,0:T(8,128)(2,1)S(1)} %get-tuple-element.82.refs_6_), channel_id=1, source_target_pairs={{0,8},{8,16},{16,24},{24,0},{1,9},{9,17},{17,25},{25,1},{2,10},{10... | collective-permute-start | bytes 786440 | tf_op jit(solution)/shard_map/ppermute | solution.py:21
  191.9 0.7 copy-start.9
  192.6 31.2 %collective-permute-start.29 = (bf16[128,1024]{1,0:T(8,128)(2,1)S(1)}, bf16[128,1024]{1,0:T(8,128)(2,1)S(1)}, u32[]{:S(2)}, u32[]{:S(2)}) collective-permute-start(bf16[128,1024]{1,0:T(8,128)(2,1)S(1)} %sum_stage.16.refs_6_), channel_id=1, source_target_pairs={{0,8},{8,16},{16,24},{24,0},{1,9},{9,17},{17,25},{25,1},{2,10},{10... | collective-permute-start | bytes 786440 | tf_op jit(solution)/shard_map/ppermute | solution.py:21
  194.3 39.3 %collective-permute-start.28 = (bf16[128,1024]{1,0:T(8,128)(2,1)S(1)}, bf16[128,1024]{1,0:T(8,128)(2,1)S(1)}, u32[]{:S(2)}, u32[]{:S(2)}) collective-permute-start(bf16[128,1024]{1,0:T(8,128)(2,1)S(1)} %sum_stage.17), channel_id=1, source_target_pairs={{0,8},{8,16},{16,24},{24,0},{1,9},{9,17},{17,25},{25,1},{2,10},{10... | collective-permute-start | bytes 786440 | tf_op jit(solution)/shard_map/ppermute | solution.py:21
  214.0 0.7 copy-start.13
  223.8 0.7 copy-start.14
  233.6 0.7 copy-start.15

commit v5 on v4

--- a/solution.py
+++ b/solution.py
@@ -71,15 +71,18 @@
     )(value, *earlier)
 
 
-def project_kernel(*refs):
-    *whole_refs, near_first, near_second, far_first, far_second, weights_ref = refs[:11]
-    out_ref, total_ref = refs[-2:]
+def project_kernel(*refs, halves):
+    weights_ref, out_ref, total_ref = refs[sum(halves)], refs[-2], refs[-1]
     step, steps = pl.program_id(0), pl.num_programs(0)
     weights = jnp.concatenate([weights_ref[0], weights_ref[1], weights_ref[2]], axis=1)
     early = step < steps // 2
-    blocks = [ref[...] for ref in whole_refs]
-    blocks.insert(3, jnp.where(early, near_first[...], near_second[...]))
-    blocks.append(jnp.where(early, far_first[...], far_second[...]))
+    blocks, place = [], 0
+    for count in halves:
+        if count == 1:
+            blocks.append(refs[place][...])
+        else:
+            blocks.append(jnp.where(early, refs[place][...], refs[place + 1][...]))
+        place += count
     rows = jnp.concatenate(blocks, axis=0)
     product = jnp.dot(rows, weights, preferred_element_type=jnp.float32)
 
@@ -102,22 +105,22 @@
         out_ref[:, 2 * width :] = total_ref[:, 2 * width :].astype(jnp.bfloat16)
 
 
-def project(near, far, weights, earlier):
-    rows, depth = near[0].shape
-    width = weights.shape[2]
+def project(blocks, weights, earlier):
+    _, depth, width = weights.shape
+    rows = blocks[0][0].shape[0]
     steps = 4
     block = depth // steps
-    count = 8 * rows
+    count = len(blocks) * rows
     whole = pl.BlockSpec((rows, block), lambda k: (0, k))
     first = pl.BlockSpec((rows, block), lambda k: (0, jnp.minimum(k, steps // 2 - 1)))
     second = pl.BlockSpec((rows, block), lambda k: (0, jnp.maximum(k - steps // 2, 0)))
+    specs = [spec for parts in blocks for spec in ([whole] if len(parts) == 1 else [first, second])]
     return pl.pallas_call(
-        project_kernel,
+        functools.partial(project_kernel, halves=[len(parts) for parts in blocks]),
         grid=(steps,),
-        in_specs=[whole] * 6
-        + [first, second] * 2
+        in_specs=specs
         + [pl.BlockSpec((3, block, width), lambda k: (0, k, 0))]
-        + [pl.BlockSpec(memory_space=pl.ANY)],
+        + [pl.BlockSpec(memory_space=pl.ANY)] * len(earlier),
         out_specs=pl.BlockSpec((count, 3 * width), lambda k: (0, 0)),
         out_shape=jax.ShapeDtypeStruct((count, 3 * width), jnp.bfloat16),
         scratch_shapes=[pltpu.VMEM((count, 3 * width), jnp.float32)],
@@ -127,21 +130,24 @@
             bytes_accessed=2 * (count * depth + weights.size),
             transcendentals=0,
         ),
-        compiler_params=pltpu.CompilerParams(vmem_limit_bytes=36 * MIB),
-    )(*near[:3], *far[:3], *near[3:], *far[3:], weights, earlier)
-
-
-def attend_kernel(visible_ref, heads_ref, context_ref, out_ref):
+        compiler_params=pltpu.CompilerParams(vmem_limit_bytes=30 * MIB),
+    )(*[part for parts in blocks for part in parts], weights, *earlier)
+
+
+def attend_kernel(visible_ref, heads_ref, context_ref, *refs, first_block):
+    out_ref = refs[-1]
     width = out_ref.shape[1]
     tiles_seen = visible_ref.shape[1]
     tiles_fresh = visible_ref.shape[0]
     mine_high, mine_low = lax.axis_index("sp") // 2, lax.axis_index("sp") % 2
     mine_branch = lax.axis_index("cfg")
 
-    def body(index, carry):
+    def body(step, carry):
+        index = first_block + step
         high, low = mine_high ^ ((index // 2) % 2), mine_low ^ (index // 4)
         tile, branch = high * 2 + low, mine_branch ^ (index % 2)
         rows = pl.ds(pl.multiple_of(index * TILE, TILE), TILE)
+        out_rows = pl.ds(pl.multiple_of(step * TILE, TILE), TILE)
         places = []
         for seen in range(tiles_seen):
             number = visible_ref[tile, seen]
@@ -183,22 +189,23 @@
             mixed = jnp.dot(
                 exponent.astype(jnp.bfloat16), tiles(2, head), preferred_element_type=jnp.float32
             )
-            out_ref[rows, columns] = (mixed / total).astype(jnp.bfloat16)
+            out_ref[out_rows, columns] = (mixed / total).astype(jnp.bfloat16)
         return carry
 
-    lax.fori_loop(0, heads_ref.shape[0] // TILE, body, 0)
-
-
-def attend(heads, context, visible):
-    count = heads.shape[0]
+    lax.fori_loop(0, out_ref.shape[0] // TILE, body, 0)
+
+
+def attend(heads, context, visible, first_block, earlier):
+    count = heads.shape[0] // 2
     width = heads.shape[1] // 3
     return pl.pallas_call(
-        attend_kernel,
+        functools.partial(attend_kernel, first_block=first_block),
         in_specs=[
             pl.BlockSpec(memory_space=pltpu.SMEM),
             pl.BlockSpec(memory_space=pltpu.VMEM),
             pl.BlockSpec(memory_space=pltpu.VMEM),
-        ],
+        ]
+        + [pl.BlockSpec(memory_space=pl.ANY)] * len(earlier),
         out_shape=jax.ShapeDtypeStruct((count, width), jnp.bfloat16),
         name="attend",
         cost_estimate=pl.CostEstimate(
@@ -207,7 +214,7 @@
             transcendentals=count * visible.shape[1] * TILE * width // HD,
         ),
         compiler_params=pltpu.CompilerParams(vmem_limit_bytes=32 * MIB),
-    )(visible, heads, context)
+    )(visible, heads, context, *earlier)
 
 
 def half_kernel(rows_ref, *refs, start):
@@ -218,37 +225,13 @@
 def half_of(rows, start, earlier):
     return pl.pallas_call(
         functools.partial(half_kernel, start=start),
-        in_specs=[pl.BlockSpec(memory_space=pltpu.VMEM), pl.BlockSpec(memory_space=pl.ANY)],
+        in_specs=[pl.BlockSpec(memory_space=pltpu.VMEM)]
+        + [pl.BlockSpec(memory_space=pl.ANY)] * len(earlier),
         out_shape=jax.ShapeDtypeStruct((rows.shape[0], rows.shape[1] // 2), rows.dtype),
         name="half_of",
         cost_estimate=SHORT,
         compiler_params=pltpu.CompilerParams(vmem_limit_bytes=8 * MIB),
-    )(rows, earlier)
-
-
-def sent_kernel(attended_ref, weights_ref, *out_refs, chunk):
-    rows = attended_ref[attended_ref.shape[0] // 2 :, :]
-    start = 0
-    for out_ref in out_refs:
-        for index in range(out_ref.shape[0]):
-            out_ref[index] = jnp.dot(
-                rows, weights_ref[:, start : start + chunk], preferred_element_type=jnp.float32
-            ).astype(jnp.bfloat16)
-            start += chunk
-
-
-def sent_products(attended, weights, chunk):
-    rows, count = attended.shape[0] // 2, weights.shape[1] // chunk
-    return pl.pallas_call(
-        functools.partial(sent_kernel, chunk=chunk),
-        out_shape=[
-            jax.ShapeDtypeStruct((pieces, rows, chunk), jnp.bfloat16) for pieces in (1, count - 1)
-        ],
-        in_specs=[pl.BlockSpec(memory_space=pltpu.VMEM)] * 2,
-        name="sent_products",
-        cost_estimate=SHORT,
-        compiler_params=pltpu.CompilerParams(vmem_limit_bytes=20 * MIB),
-    )(attended, weights)
+    )(rows, *earlier)
 
 
 def combined(own, other, mine, gates_ref, columns):
@@ -264,13 +247,17 @@
     return jnp.where(last, guided, other), jnp.where(last, guided, own)
 
 
-def begin(index, start, refs, across_out, along_out, first_kept, second_kept):
-    attended_ref, weights_ref, received_ref, rows_ref, gates_ref = refs
+def begin(start, refs, across_out, along_out, first_kept, second_kept):
+    attended_ref, core_attended_ref, weights_ref, core_weights_ref, rows_ref, gates_ref = refs
     tokens, half = rows_ref.shape[0], first_kept.shape[2]
-    attended = attended_ref[: 4 * tokens, :]
+    attended = jnp.concatenate([attended_ref[...], core_attended_ref[...]], axis=1)
+
+    def product_of(columns):
+        weights = jnp.concatenate([weights_ref[:, columns], core_weights_ref[:, columns]], axis=0)
+        return jnp.dot(attended, weights, preferred_element_type=jnp.float32)
+
     columns = slice(start, start + half)
-    product = jnp.dot(attended, weights_ref[:, columns], preferred_element_type=jnp.float32)
-    product = product + received_ref[index, :, :half].astype(jnp.float32)
+    product = product_of(columns)
     for tile in range(2):
         own = product[2 * tile * tokens : (2 * tile + 1) * tokens]
         other = product[(2 * tile + 1) * tokens : (2 * tile + 2) * tokens]
@@ -279,8 +266,7 @@
         across_out[tile] = sent.astype(jnp.bfloat16)
         first_kept[tile] = kept
     columns = slice(start + half, start + 2 * half)
-    product = jnp.dot(attended, weights_ref[:, columns], preferred_element_type=jnp.float32)
-    product = product + received_ref[index, :, half:].astype(jnp.float32)
+    product = product_of(columns)
     for branch in range(2):
         second_kept[branch] = product[branch * tokens : (branch + 1) * tokens]
         along_out[branch] = product[(branch + 2) * tokens : (branch + 3) * tokens].astype(
@@ -288,13 +274,17 @@
         )
 
 
-def stage_kernel(*refs, parts, start, next_start, piece, fresh, middle, final):
+def stage_kernel(*refs, parts, start, next_start, fresh, middle, final):
     named = dict(zip(parts, refs))
     if fresh:
         begin(
-            piece,
             next_start,
-            [named[name] for name in ("attended", "weights", "received", "rows", "gates")],
+            [
+                named[name]
+                for name in (
+                    "attended", "core_attended", "weights", "core_weights", "rows", "gates"
+                )
+            ],
             named["across_out"],
             named["along_out"],
             named["first_kept_out"],
@@ -332,7 +322,7 @@
         ).astype(jnp.bfloat16)
 
 
-def stage(operands, earlier, chunk, start, next_start, piece, fresh, middle, final):
+def stage(operands, earlier, chunk, start, next_start, fresh, middle, final):
     tokens, half = operands["rows"].shape[0], chunk // 2
     outs = {}
     if fresh or middle:
@@ -354,7 +344,6 @@
             parts=parts,
             start=start,
             next_start=next_start,
-            piece=piece,
             fresh=fresh,
             middle=middle,
             final=final,
@@ -369,29 +358,6 @@
     return dict(zip(outs, results))
 
 
-def place_kernel(part_ref, *refs, start):
-    out_ref, semaphore = refs[-2:]
-    copy = pltpu.make_async_copy(
-        part_ref, out_ref.at[:, pl.ds(start, part_ref.shape[1])], semaphore
-    )
-    copy.start()
-    copy.wait()
-
-
-def place(part, whole, columns, start, earlier):
-    held = () if whole is None else (whole,)
-    return pl.pallas_call(
-        functools.partial(place_kernel, start=start),
-        in_specs=[pl.BlockSpec(memory_space=pl.ANY)] * (1 + len(held) + len(earlier)),
-        out_specs=pl.BlockSpec(memory_space=pl.ANY),
-        out_shape=jax.ShapeDtypeStruct((part.shape[0], columns), part.dtype),
-        scratch_shapes=[pltpu.SemaphoreType.DMA],
-        input_output_aliases={1: 0} if held else {},
-        name="place",
-        cost_estimate=SHORT,
-    )(part, *held, *earlier)
-
-
 def per_device(flight, modulation, project_in, project_out, stale_cache, visible):
     current = flight[0, 0]
     modulate = modulation[0, 0]
@@ -408,38 +374,37 @@
     along = from_partner(own, "sp", 2)
     own_core = from_partner(own, "sp", 1)
     middle = features // 2
-    first = from_partner(half_of(across, 0, packed), "sp", 2)
-    second = from_partner(half_of(along, middle, packed), "cfg", 1)
-    across_core = from_partner(across, "sp", 1)
-    along_core = from_partner(along, "sp", 1)
-    first_core = from_partner(first, "sp", 1)
-    second_core = from_partner(second, "sp", 1)
     gate = modulate[2:3]
-    gates = jnp.concatenate([gate, from_partner(gate, "cfg", 1)], axis=0)
-
-    packed = after(packed, (first, second))
+    other_gate = from_partner(gate, "cfg", 1)
+    across, along = after(across, (packed,)), after(along, (packed, other_gate))
+    first = from_partner(half_of(across, 0, ()), "sp", 2)
+    second = from_partner(half_of(along, middle, ()), "cfg", 1)
+    gates = jnp.concatenate([gate, other_gate], axis=0)
+    core_weights = from_partner(project_out[0], "sp", 1)
+    near = [(own,), (across,), (along,), (first, second)]
+    far = [(own_core,)] + [
+        tuple(from_partner(part, "sp", 1) for part in parts) for parts in near[1:]
+    ]
+
+    packed = after(packed, far[2])
     context = lax.all_to_all(packed, ("sp", "cfg"), split_axis=0, concat_axis=0, tiled=True)
     context = context.reshape(devices * context_rows, 2 * width)
 
-    heads = project(
-        (own, across, along, first, second),
-        (own_core, across_core, along_core, first_core, second_core),
-        project_in[0],
-        gates,
-    )
-    attended = attend(heads, context, visible[0])
+    heads = project(near + far, project_in[0], (core_weights,))
+    for_core = attend(heads, context, visible[0], 4, ())
+    core_attended = from_partner(for_core, "sp", 1)
+    attended = attend(heads, context, visible[0], 0, (for_core,))
 
     weights = project_out[0]
     count = COLUMN_CHUNKS
     chunk = features // count
-    received = [from_partner(part, "sp", 1) for part in sent_products(attended, weights, chunk)]
-    kept, left, flights, result, arrivals, earlier = {}, {}, {}, [], [], []
+    kept, left, flights, arrivals, earlier = {}, {}, {}, [], []
     for index in range(-2, count + 2):
         fresh, middle, final = index + 2 < count, 0 <= index < count, index >= 2
         operands = {"rows": current, "gates": gates}
         if fresh:
-            operands["attended"], operands["weights"] = attended, weights
-            operands["received"] = received[min(index + 2, 1)]
+            operands["attended"], operands["core_attended"] = attended, core_attended
+            operands["weights"], operands["core_weights"] = weights, core_weights
         if index >= 0:
             operands["across"], operands["along"] = flights.pop(index)
         if middle:
@@ -452,7 +417,6 @@
             chunk,
             max(index, 0) * chunk,
             (index + 2) * chunk,
-            max(index + 1, 0),
             fresh,
             middle,
             final,
@@ -467,12 +431,9 @@
         if middle:
             left[index] = (outs["first_left_out"], outs["second_left_out"])
         if final:
-            arrived = from_behind(outs["done_out"], "pipe", 1)
-            whole = result[-1] if result else None
-            result.append(place(arrived, whole, features, (index - 2) * chunk, []))
-            arrivals.append(arrived)
+            arrivals.append(from_behind(outs["done_out"], "pipe", 1))
         earlier = [list(outs.values())[-1]] + (arrivals[-2:-1] if 3 <= index < count else [])
-    return result[-1][None, None]
+    return jnp.concatenate(arrivals, axis=1)[None, None]
 
 
 def solution(mesh):

time: 244 us -> 220 us (0.902)
  Pallas kernels: 85.3 us -> 50.3 us
  waiting for transfers between devices: 83.3 us -> 91.2 us
  local copies, waits for them, and re-layouts: 34 us -> 37.8 us
    pallas_call x8 -> x3, Pallas kernels: 76.4 us -> 27.4 us  [the longest x1 19.4 us: project(): pl.pallas_call(functools.partial(project_kernel, halves=[len(parts) for p...]
    pallas_call x9, Pallas kernels: 5.29 us -> 17 us  [stage(): pl.pallas_call(functools.partial(stage_kernel, parts=parts, start=start,...]
    ppermute x5, waiting for transfers between devices: 1.71 us -> 11.8 us  [from_behind(): return lax.ppermute(x, axis, [(i, (i + by) % count) for i in range(count)])]
    unnamed x33 -> x34, local copies, waits for them, and re-layouts: 11.3 us -> 15 us
  transfers between devices with their start and end apart: 32 -> 32, of which waited for: 17 -> 17; matrix products, arithmetic and copies ran while one was open for 9% -> 12% of each run, Pallas kernels for 25% -> 18%
where the time goes in v5:
time: 220 us; the launch traced here: 219 us
  waiting for transfers between devices  91.2 us (41%)
  Pallas kernels  50.3 us (23%)
  starting transfers between devices  39.2 us (18%)
  local copies, waits for them, and re-layouts  37.8 us (17%)
    ppermute x26, waiting for transfers between devices, from_partner(): return lax.ppermute(value, axis, pairs)  79.3 us
    ppermute x26, starting transfers between devices, from_partner(): return lax.ppermute(value, axis, pairs)  27.3 us
    pallas_call x1, Pallas kernels, project(): pl.pallas_call(functools.partial(project_kernel, halves=[len(parts) for p...  19.4 us
    pallas_call x9, Pallas kernels, stage(): pl.pallas_call(functools.partial(stage_kernel, parts=parts, start=start,...  17 us
    unnamed x34, local copies, waits for them, and re-layouts  15 us
    another operation x2, local copies, waits for them, and re-layouts, per_device(): packed = stale_cache[0, 0].reshape(context_rows, 2, devices, width)  14 us
    ppermute x5, waiting for transfers between devices, from_behind(): return lax.ppermute(x, axis, [(i, (i + by) % count) for i in range(count)])  11.8 us
    ppermute x5, starting transfers between devices, from_behind(): return lax.ppermute(x, axis, [(i, (i + by) % count) for i in range(count)])  8.09 us
  transfers between devices with their start and end apart: 32, of which 17 were waited for; matrix products, arithmetic and copies ran while one was open for 12% of the time, Pallas kernels for 18%

profile of v5, /device:TPU:0, one launch (start us, length us, event | category | flops | bytes accessed | tf_op | source)
XLA Modules:
  0.0 218.7 jit_solution(578844302813030325)
XLA Ops:
  0.0 0.8 copy.15
  0.9 1.3 copy-done
  2.2 3.5 %modulated_norm.1.refs_0_ = bf16[128,5120]{1,0:T(8,128)(2,1)} custom-call(bf16[128,5120]{1,0:T(8,128)(2,1)S(1)} %bitcast.14, f32[3,5120]{1,0:T(4,128)S(1)} %bitcast.32), custom_call_target="tpu_custom_call" | custom-call | flops 6553600 | bytes 2621440 | tf_op jit(solution)/shard_map/modulated_norm/pallas_call | solution.py:47
  5.7 3.0 %collective-permute-start.2 = (bf16[128,5120]{1,0:T(8,128)(2,1)}, bf16[128,5120]{1,0:T(8,128)(2,1)S(1)}, u32[]{:S(2)}, u32[]{:S(2)}) collective-permute-start(bf16[128,5120]{1,0:T(8,128)(2,1)} %modulated_norm.1.refs_0_), channel_id=1, source_target_pairs={{0,4},{2,6},{4,0},{6,2},{1,5},{3,7},{5,1},{7,3},{8,12},{10,14},{12... | collective-permute-start | bytes 3932168 | tf_op jit(solution)/shard_map/ppermute | solution.py:26
  8.7 0.7 slice_bitcast_fusion
  9.4 1.5 collective-permute-start
  10.9 8.0 %reshape_squeeze.3 = bf16[256,2,8,384]{3,2,1,0:T(8,128)(2,1)} reshape(bf16[1,1,256,2,3072]{4,3,2,1,0:T(2,128)(2,1)} %param.10) | data formatting | bytes 6291456 | tf_op jit(solution)/shard_map/reshape;squeeze | solution.py:369
  18.8 6.1 %copy.14 = bf16[256,2,8,384]{3,1,0,2:T(2,128)(2,1)} copy(bf16[256,2,8,384]{3,2,1,0:T(8,128)(2,1)} %reshape_squeeze.3) | data formatting | bytes 6291456 | tf_op jit(solution)/shard_map/reshape;squeeze | solution.py:369
  24.9 8.0 %reshape.7.refs_0_ = bf16[8,256,768]{2,1,0:T(8,128)(2,1)} reshape(bf16[8,256,2,384]{3,2,1,0:T(2,128)(2,1)} %bitcast.35) | data formatting | bytes 6291456 | tf_op jit(solution)/shard_map/reshape | solution.py:370
  32.9 4.7 %collective-permute-done.2.value_ref = bf16[128,5120]{1,0:T(8,128)(2,1)S(1)} collective-permute-done((bf16[128,5120]{1,0:T(8,128)(2,1)}, bf16[128,5120]{1,0:T(8,128)(2,1)S(1)}, u32[]{:S(2)}, u32[]{:S(2)}) %collective-permute-start.2) | collective-permute-done | bytes 1310752 | tf_op jit(solution)/shard_map/ppermute | solution.py:26
  37.6 1.1 copy-done.5
  38.7 1.7 collective-permute-start.1
  40.4 3.8 %copy.18.value_ref = bf16[8,256,768]{2,1,0:T(8,128)(2,1)} copy(bf16[8,256,768]{2,1,0:T(8,128)(2,1)} %reshape.7.refs_0_) | data formatting | bytes 6291456
  44.3 1.0 copy-done.8
  45.3 3.8 %all-to-all-start = ((bf16[8,256,768]{2,1,0:T(8,128)(2,1)}), bf16[8,256,768]{2,1,0:T(8,128)(2,1)S(1)}, u32[]{:S(2)}, u32[]{:S(2)}) async-start(bf16[8,256,768]{2,1,0:T(8,128)(2,1)} %after.5), calls=%async_computation | async-start | bytes 6291456 | tf_op jit(solution)/shard_map/all_to_all | solution.py:390
  49.2 1.3 copy-done.6
  50.5 0.9 half_of.3
  51.3 1.7 collective-permute-start.4
  53.1 17.5 %collective-permute-done.1.value_ref = bf16[128,5120]{1,0:T(8,128)(2,1)} collective-permute-done((bf16[128,5120]{1,0:T(8,128)(2,1)}, bf16[128,5120]{1,0:T(8,128)(2,1)}, u32[]{:S(2)}, u32[]{:S(2)}) %collective-permute-start.1) | collective-permute-done | bytes 1310752 | tf_op jit(solution)/shard_map/ppermute | solution.py:26
  70.6 1.5 half_of.2
  72.1 1.8 collective-permute-start.3
  74.0 44.0 %collective-permute-done.4.refs_4_ = bf16[128,2560]{1,0:T(8,128)(2,1)} collective-permute-done((bf16[128,2560]{1,0:T(8,128)(2,1)}, bf16[128,2560]{1,0:T(8,128)(2,1)}, u32[]{:S(2)}, u32[]{:S(2)}) %collective-permute-start.4) | collective-permute-done | bytes 655392 | tf_op jit(solution)/shard_map/ppermute | solution.py:26
  118.0 0.5 collective-permute-start.8
  118.5 2.6 %collective-permute-done.9.refs_9_ = bf16[128,2560]{1,0:T(8,128)(2,1)S(1)} collective-permute-done((bf16[128,2560]{1,0:T(8,128)(2,1)}, bf16[128,2560]{1,0:T(8,128)(2,1)S(1)}, u32[]{:S(2)}, u32[]{:S(2)}) %collective-permute-start.9) | collective-permute-done | bytes 655392 | tf_op jit(solution)/shard_map/ppermute | solution.py:26
  121.2 1.3 copy-done.9
  122.5 19.4 %project_heads.1.heads_ref = bf16[1024,1152]{1,0:T(8,128)(2,1)S(1)} custom-call(bf16[128,5120]{1,0:T(8,128)(2,1)} %modulated_norm.1.refs_0_, bf16[128,5120]{1,0:T(8,128)(2,1)} %after.3.rows_ref.refs_1_, bf16[128,5120]{1,0:T(8,128)(2,1)S(1)} %copy-done.7, bf16[128,2560]{1,0:T(8,128)(2,1)S(1)} %collective-permute-done.3.refs_3_, ...), custom_call_target="tpu_custom_call" | custom-call | flops 12079595520 | bytes 22282240 | tf_op jit(solution)/shard_map/project_heads/pallas_call | solution.py:118
  142.0 1.4 copy-done.3
  143.4 1.7 copy-done.4
  145.1 4.0 %attend.2.refs_0_ = bf16[512,384]{1,0:T(8,128)(2,1)S(1)} custom-call(s32[4,6]{1,0:T(4,128)S(1)} %bitcast.33, bf16[1024,1152]{1,0:T(8,128)(2,1)S(1)} %copy-done.4, bf16[2048,768]{1,0:T(8,128)(2,1)S(1)} %bitcast.30), custom_call_target="tpu_custom_call" | custom-call | flops 603979776 | bytes 5505024 | tf_op jit(solution)/shard_map/attend/pallas_call | solution.py:201
  149.3 4.0 %attend.3.refs_2_ = bf16[512,384]{1,0:T(8,128)(2,1)S(1)} custom-call(s32[4,6]{1,0:T(4,128)S(1)} %bitcast.34, bf16[1024,1152]{1,0:T(8,128)(2,1)S(1)} %copy-done.4, bf16[2048,768]{1,0:T(8,128)(2,1)S(1)} %bitcast.31, bf16[512,384]{1,0:T(8,128)(2,1)S(1)} %attend.2.refs_0_), custom_call_target="tpu_custom_call" | custom-call | flops 603979776 | bytes 5505024 | tf_op jit(solution)/shard_map/attend/pallas_call | solution.py:201
  153.3 3.1 %sum_stage.9 = (bf16[2,128,512]{2,1,0:T(8,128)(2,1)S(1)}, bf16[2,128,512]{2,1,0:T(8,128)(2,1)S(1)}, f32[2,128,512]{2,1,0:T(8,128)S(1)}, f32[2,128,512]{2,1,0:T(8,128)S(1)}) custom-call(bf16[128,5120]{1,0:T(8,128)(2,1)S(1)} %bitcast.15, f32[2,5120]{1,0:T(2,128)S(1)} %pad_maximum_fusion.refs_1_, bf16[512,384]{1,0:T(8,128)(2,1)S(1)} %attend.3.refs_2_, ...), custom_call_target="tpu_custom_call" | custom-call | flops 1 | bytes 1 | tf_op jit(solution)/shard_map/sum_stage/pallas_call | solution.py:341
  156.5 1.8 collective-permute-start.12
  158.2 1.5 collective-permute-start.13
  159.8 3.1 %sum_stage.10 = (bf16[2,128,512]{2,1,0:T(8,128)(2,1)S(1)}, bf16[2,128,512]{2,1,0:T(8,128)(2,1)S(1)}, f32[2,128,512]{2,1,0:T(8,128)S(1)}, f32[2,128,512]{2,1,0:T(8,128)S(1)}) custom-call(bf16[128,5120]{1,0:T(8,128)(2,1)S(1)} %bitcast.16, f32[2,5120]{1,0:T(2,128)S(1)} %pad_maximum_fusion.refs_1_, bf16[512,384]{1,0:T(8,128)(2,1)S(1)} %attend.3.refs_2_, ...), custom_call_target="tpu_custom_call" | custom-call | flops 1 | bytes 1 | tf_op jit(solution)/shard_map/sum_stage/pallas_call | solution.py:341
  162.9 0.6 collective-permute-start.16
  163.6 0.3 collective-permute-start.17
  163.8 1.3 collective-permute-done.12.refs_6_
  165.1 2.2 collective-permute-done.13.refs_7_
  167.3 3.4 %sum_stage.11 = (bf16[3,128,512]{2,1,0:T(8,128)(2,1)S(1)}, bf16[3,128,512]{2,1,0:T(8,128)(2,1)S(1)}, f32[2,128,512]{2,1,0:T(8,128)S(1)}, f32[2,128,512]{2,1,0:T(...) custom-call(bf16[128,5120]{1,0:T(8,128)(2,1)S(1)} %bitcast.17, f32[2,5120]{1,0:T(2,128)S(1)} %pad_maximum_fusion.refs_1_, ...), custom_call_target="tpu_custom_call" | custom-call | flops 1 | bytes 1 | tf_op jit(solution)/shard_map/sum_stage/pallas_call | solution.py:341
  170.8 2.1 collective-permute-start.15
  173.0 3.4 %sum_stage.12 = (bf16[3,128,512]{2,1,0:T(8,128)(2,1)S(1)}, bf16[3,128,512]{2,1,0:T(8,128)(2,1)S(1)}, f32[2,128,512]{2,1,0:T(8,128)S(1)}, f32[2,128,512]{2,1,0:T(...) custom-call(bf16[128,5120]{1,0:T(8,128)(2,1)S(1)} %bitcast.18, f32[2,5120]{1,0:T(2,128)S(1)} %pad_maximum_fusion.refs_1_, ...), custom_call_target="tpu_custom_call" | custom-call | flops 1 | bytes 1 | tf_op jit(solution)/shard_map/sum_stage/pallas_call | solution.py:341
  176.4 1.5 collective-permute-start.19
  177.9 0.4 collective-permute-start.20
  178.3 4.5 %collective-permute-done.14.refs_6_ = bf16[3,128,512]{2,1,0:T(8,128)(2,1)S(1)} collective-permute-done((bf16[3,128,512]{2,1,0:T(8,128)(2,1)S(1)}, bf16[3,128,512]{2,1,0:T(8,128)(2,1)S(1)}, u32[]{:S(2)}, u32[]{:S(2)}) %collective-permute-start.14) | collective-permute-done | bytes 393248 | tf_op jit(solution)/shard_map/ppermute | solution.py:26
  183.0 3.5 %sum_stage.13 = (bf16[3,128,512]{2,1,0:T(8,128)(2,1)S(1)}, bf16[3,128,512]{2,1,0:T(8,128)(2,1)S(1)}, f32[2,128,512]{2,1,0:T(8,128)S(1)}, f32[2,128,512]{2,1,0:T(...) custom-call(bf16[128,5120]{1,0:T(8,128)(2,1)S(1)} %bitcast.19, ...), custom_call_target="tpu_custom_call" | custom-call | flops 1 | bytes 1 | tf_op jit(solution)/shard_map/sum_stage/pallas_call | solution.py:341
  186.5 1.7 collective-permute-start.22
  188.2 1.6 collective-permute-start.23
  189.8 1.6 collective-permute-start.18
  191.6 1.6 collective-permute-start.21
  193.3 1.7 collective-permute-start.25
  194.9 3.0 %collective-permute-done.18.refs_9_ = bf16[128,1024]{1,0:T(8,128)(2,1)S(1)} collective-permute-done((bf16[128,1024]{1,0:T(8,128)(2,1)S(1)}, bf16[128,1024]{1,0:T(8,128)(2,1)S(1)}, u32[]{:S(2)}, u32[]{:S(2)}) %collective-permute-start.18) | collective-permute-done | bytes 262176 | tf_op jit(solution)/shard_map/ppermute | solution.py:21
  198.0 0.4 collective-permute-start.26
  198.5 0.3 collective-permute-done.23.refs_3_
  199.1 1.6 collective-permute-start.24
  200.7 1.4 collective-permute-start.28
  202.1 1.5 collective-permute-start.29
  203.7 1.6 collective-permute-start.27
  205.3 0.3 collective-permute-done.28.refs_2_
  205.7 1.4 collective-permute-done.29.refs_3_
  207.1 1.6 collective-permute-start.30
  208.8 1.6 collective-permute-done.24
  210.4 4.4 %collective-permute-done.27 = bf16[128,1024]{1,0:T(8,128)(2,1)S(1)} collective-permute-done((bf16[128,1024]{1,0:T(8,128)(2,1)S(1)}, bf16[128,1024]{1,0:T(8,128)(2,1)S(1)}, u32[]{:S(2)}, u32[]{:S(2)}) %collective-permute-start.27) | collective-permute-done | bytes 262176 | tf_op jit(solution)/shard_map/ppermute | solution.py:21
  214.8 2.8 %collective-permute-done.30 = bf16[128,1024]{1,0:T(8,128)(2,1)S(1)} collective-permute-done((bf16[128,1024]{1,0:T(8,128)(2,1)S(1)}, bf16[128,1024]{1,0:T(8,128)(2,1)S(1)}, u32[]{:S(2)}, u32[]{:S(2)}) %collective-permute-start.30) | collective-permute-done | bytes 262176 | tf_op jit(solution)/shard_map/ppermute | solution.py:21
  217.7 1.0 copy-done.13
  (58 shorter events, 1.6 us)
Async XLA Ops:
  0.9 1.3 copy-start
  5.7 32.0 %collective-permute-start.2 = (bf16[128,5120]{1,0:T(8,128)(2,1)}, bf16[128,5120]{1,0:T(8,128)(2,1)S(1)}, u32[]{:S(2)}, u32[]{:S(2)}) collective-permute-start(bf16[128,5120]{1,0:T(8,128)(2,1)} %modulated_norm.1.refs_0_), channel_id=1, source_target_pairs={{0,4},{2,6},{4,0},{6,2},{1,5},{3,7},{5,1},{7,3},{8,12},{10,14},{12... | collective-permute-start | bytes 3932168 | tf_op jit(solution)/shard_map/ppermute | solution.py:26
  8.7 112.5 %collective-permute-start.10 = (bf16[384,5120]{1,0:T(8,128)(2,1)}, bf16[384,5120]{1,0:T(8,128)(2,1)}, u32[]{:S(2)}, u32[]{:S(2)}) collective-permute-start(bf16[384,5120]{1,0:T(8,128)(2,1)} %bitcast.24), channel_id=1, source_target_pairs={{0,2},{2,0},{4,6},{6,4},{1,3},{3,1},{5,7},{7,5},{8,10},{10,8},{12,... | collective-permute-start | bytes 11796488 | tf_op jit(solution)/shard_map/ppermute | solution.py:26
  9.4 23.5 %collective-permute-start = (f32[1,5120]{1,0:T(1,128)S(1)}, f32[1,5120]{1,0:T(1,128)S(1)}, u32[]{:S(2)}, u32[]{:S(2)}) collective-permute-start(f32[1,5120]{1,0:T(1,128)S(1)} %slice_bitcast_fusion), channel_id=1, source_target_pairs={{0,1},{1,0},{2,3},{3,2},{4,5},{5,4},{6,7},{7,6},{8,9},{9,8},{10,11... | collective-permute-start | bytes 61448 | tf_op jit(solution)/shard_map/ppermute | solution.py:26
  32.9 4.7 %copy-start.11 = (f32[1,5120]{1,0:T(1,128)}, f32[1,5120]{1,0:T(1,128)S(1)}, u32[]{:S(2)}) copy-start(f32[1,5120]{1,0:T(1,128)S(1)} %collective-permute-done.refs_1_) | copy-start | bytes 61444
  37.6 1.1 copy-start.5
  38.7 5.6 %collective-permute-start.7 = (bf16[128,5120]{1,0:T(8,128)(2,1)}, bf16[128,5120]{1,0:T(8,128)(2,1)S(1)}, u32[]{:S(2)}, u32[]{:S(2)}) collective-permute-start(bf16[128,5120]{1,0:T(8,128)(2,1)} %after.4.rows_ref.refs_2_), channel_id=1, source_target_pairs={{0,2},{2,0},{4,6},{6,4},{1,3},{3,1},{5,7},{7,5},{8,10},{10,8},{12,... | collective-permute-start | bytes 3932168 | tf_op jit(solution)/shard_map/ppermute | solution.py:26
  38.7 31.9 %collective-permute-start.1 = (bf16[128,5120]{1,0:T(8,128)(2,1)}, bf16[128,5120]{1,0:T(8,128)(2,1)}, u32[]{:S(2)}, u32[]{:S(2)}) collective-permute-start(bf16[128,5120]{1,0:T(8,128)(2,1)} %modulated_norm.1.refs_0_), channel_id=1, source_target_pairs={{0,1},{1,0},{2,3},{3,2},{4,5},{5,4},{6,7},{7,6},{8,9},{9,8},{10,11... | collective-permute-start | bytes 3932168 | tf_op jit(solution)/shard_map/ppermute | solution.py:26
  44.3 1.0 copy-start.8
  45.3 98.1 %all-to-all-start = ((bf16[8,256,768]{2,1,0:T(8,128)(2,1)}), bf16[8,256,768]{2,1,0:T(8,128)(2,1)S(1)}, u32[]{:S(2)}, u32[]{:S(2)}) async-start(bf16[8,256,768]{2,1,0:T(8,128)(2,1)} %after.5), calls=%async_computation | async-start | bytes 6291456 | tf_op jit(solution)/shard_map/all_to_all | solution.py:390
  49.2 1.3 copy-start.6
  51.3 66.7 %collective-permute-start.4 = (bf16[128,2560]{1,0:T(8,128)(2,1)}, bf16[128,2560]{1,0:T(8,128)(2,1)}, u32[]{:S(2)}, u32[]{:S(2)}) collective-permute-start(bf16[128,2560]{1,0:T(8,128)(2,1)} %half_of.3), channel_id=1, source_target_pairs={{0,1},{1,0},{2,3},{3,2},{4,5},{5,4},{6,7},{7,6},{8,9},{9,8},{10,11... | collective-permute-start | bytes 1966088 | tf_op jit(solution)/shard_map/ppermute | solution.py:26
  70.6 50.6 %copy-start.7 = (bf16[128,5120]{1,0:T(8,128)(2,1)S(1)}, bf16[128,5120]{1,0:T(8,128)(2,1)}, u32[]{:S(2)}) copy-start(bf16[128,5120]{1,0:T(8,128)(2,1)} %after.4.rows_ref.refs_2_) | copy-start | bytes 3932164
  70.6 47.9 %collective-permute-start.5 = (bf16[128,5120]{1,0:T(8,128)(2,1)}, bf16[128,5120]{1,0:T(8,128)(2,1)S(1)}, u32[]{:S(2)}, u32[]{:S(2)}) collective-permute-start(bf16[128,5120]{1,0:T(8,128)(2,1)} %modulated_norm.1.refs_0_), channel_id=1, source_target_pairs={{0,2},{2,0},{4,6},{6,4},{1,3},{3,1},{5,7},{7,5},{8,10},{10,8},{12,... | collective-permute-start | bytes 3932168 | tf_op jit(solution)/shard_map/ppermute | solution.py:26
  72.1 45.9 %collective-permute-start.3 = (bf16[128,2560]{1,0:T(8,128)(2,1)S(1)}, bf16[128,2560]{1,0:T(8,128)(2,1)S(1)}, u32[]{:S(2)}, u32[]{:S(2)}) collective-permute-start(bf16[128,2560]{1,0:T(8,128)(2,1)S(1)} %half_of.2), channel_id=1, source_target_pairs={{0,4},{2,6},{4,0},{6,2},{1,5},{3,7},{5,1},{7,3},{8,12},{10,14},{12... | collective-permute-start | bytes 1966088 | tf_op jit(solution)/shard_map/ppermute | solution.py:26
  73.9 47.3 %collective-permute-start.6 = (bf16[128,5120]{1,0:T(8,128)(2,1)}, bf16[128,5120]{1,0:T(8,128)(2,1)S(1)}, u32[]{:S(2)}, u32[]{:S(2)}) collective-permute-start(bf16[128,5120]{1,0:T(8,128)(2,1)} %after.3.rows_ref.refs_1_), channel_id=1, source_target_pairs={{0,2},{2,0},{4,6},{6,4},{1,3},{3,1},{5,7},{7,5},{8,10},{10,8},{12,... | collective-permute-start | bytes 3932168 | tf_op jit(solution)/shard_map/ppermute | solution.py:26
  118.0 3.2 %collective-permute-start.9 = (bf16[128,2560]{1,0:T(8,128)(2,1)}, bf16[128,2560]{1,0:T(8,128)(2,1)S(1)}, u32[]{:S(2)}, u32[]{:S(2)}) collective-permute-start(bf16[128,2560]{1,0:T(8,128)(2,1)} %collective-permute-done.4.refs_4_), channel_id=1, source_target_pairs={{0,2},{2,0},{4,6},{6,4},{1,3},{3,1},{5,7},{7,5},{8,10},{10,8},{12,... | collective-permute-start | bytes 1966088 | tf_op jit(solution)/shard_map/ppermute | solution.py:26
  118.0 3.2 %collective-permute-start.8 = (bf16[128,2560]{1,0:T(8,128)(2,1)S(1)}, bf16[128,2560]{1,0:T(8,128)(2,1)S(1)}, u32[]{:S(2)}, u32[]{:S(2)}) collective-permute-start(bf16[128,2560]{1,0:T(8,128)(2,1)S(1)} %collective-permute-done.3.refs_3_), channel_id=1, source_target_pairs={{0,2},{2,0},{4,6},{6,4},{1,3},{3,1},{5,7},{7,5},{8,10},{10,8},{12,... | collective-permute-start | bytes 1966088 | tf_op jit(solution)/shard_map/ppermute | solution.py:26
  121.2 1.3 copy-start.9
  122.5 20.9 %copy-start.10 = (s32[1,4,6]{2,1,0:T(4,128)S(1)}, s32[1,4,6]{2,1,0:T(4,128)}, u32[]{:S(2)}) copy-start(s32[1,4,6]{2,1,0:T(4,128)} %param.11) | copy-start | bytes 292
  142.0 1.4 copy-start.3
  143.4 1.7 copy-start.4
  145.1 4.2 %copy-start.12 = (f32[1,5120]{1,0:T(1,128)S(1)}, f32[1,5120]{1,0:T(1,128)}, u32[]{:S(2)}) copy-start(f32[1,5120]{1,0:T(1,128)} %copy-done.11) | copy-start | bytes 61444
  149.1 4.3 %collective-permute-start.11 = (bf16[512,384]{1,0:T(8,128)(2,1)S(1)}, bf16[512,384]{1,0:T(8,128)(2,1)S(1)}, u32[]{:S(2)}, u32[]{:S(2)}) collective-permute-start(bf16[512,384]{1,0:T(8,128)(2,1)S(1)} %attend.2.refs_0_), channel_id=1, source_target_pairs={{0,2},{2,0},{4,6},{6,4},{1,3},{3,1},{5,7},{7,5},{8,10},{10,8},{12,... | collective-permute-start | bytes 1179656 | tf_op jit(solution)/shard_map/ppermute | solution.py:26
  149.3 4.0 %copy-start.1 = (bf16[1,1,128,5120]{3,2,1,0:T(8,128)(2,1)S(1)}, bf16[1,1,128,5120]{3,2,1,0:T(8,128)(2,1)}, u32[]{:S(2)}) copy-start(bf16[1,1,128,5120]{3,2,1,0:T(8,128)(2,1)} %param.6) | copy-start | bytes 3932164
  149.3 4.0 %copy-start.2 = (bf16[1,384,5120]{2,1,0:T(8,128)(2,1)S(1)}, bf16[1,384,5120]{2,1,0:T(8,128)(2,1)}, u32[]{:S(2)}) copy-start(bf16[1,384,5120]{2,1,0:T(8,128)(2,1)} %param.9) | copy-start | bytes 11796484
  156.5 8.7 %collective-permute-start.12 = (bf16[2,128,512]{2,1,0:T(8,128)(2,1)S(1)}, bf16[2,128,512]{2,1,0:T(8,128)(2,1)S(1)}, u32[]{:S(2)}, u32[]{:S(2)}) collective-permute-start(bf16[2,128,512]{2,1,0:T(8,128)(2,1)S(1)} %get-tuple-element.42), channel_id=1, source_target_pairs={{0,1},{1,0},{2,3},{3,2},{4,5},{5,4},{6,7},{7,6},{8,9},{9,8},{10,11... | collective-permute-start | bytes 786440 | tf_op jit(solution)/shard_map/ppermute | solution.py:26
  158.2 9.1 %collective-permute-start.13 = (bf16[2,128,512]{2,1,0:T(8,128)(2,1)S(1)}, bf16[2,128,512]{2,1,0:T(8,128)(2,1)S(1)}, u32[]{:S(2)}, u32[]{:S(2)}) collective-permute-start(bf16[2,128,512]{2,1,0:T(8,128)(2,1)S(1)} %get-tuple-element.43), channel_id=1, source_target_pairs={{0,4},{2,6},{4,0},{6,2},{1,5},{3,7},{5,1},{7,3},{8,12},{10,14},{12... | collective-permute-start | bytes 786440 | tf_op jit(solution)/shard_map/ppermute | solution.py:26
  162.9 10.1 %collective-permute-start.16 = (bf16[2,128,512]{2,1,0:T(8,128)(2,1)S(1)}, bf16[2,128,512]{2,1,0:T(8,128)(2,1)S(1)}, u32[]{:S(2)}, u32[]{:S(2)}) collective-permute-start(bf16[2,128,512]{2,1,0:T(8,128)(2,1)S(1)} %get-tuple-element.53), channel_id=1, source_target_pairs={{0,1},{1,0},{2,3},{3,2},{4,5},{5,4},{6,7},{7,6},{8,9},{9,8},{10,11... | collective-permute-start | bytes 786440 | tf_op jit(solution)/shard_map/ppermute | solution.py:26
  163.6 9.4 %collective-permute-start.17 = (bf16[2,128,512]{2,1,0:T(8,128)(2,1)S(1)}, bf16[2,128,512]{2,1,0:T(8,128)(2,1)S(1)}, u32[]{:S(2)}, u32[]{:S(2)}) collective-permute-start(bf16[2,128,512]{2,1,0:T(8,128)(2,1)S(1)} %get-tuple-element.54), channel_id=1, source_target_pairs={{0,4},{2,6},{4,0},{6,2},{1,5},{3,7},{5,1},{7,3},{8,12},{10,14},{12... | collective-permute-start | bytes 786440 | tf_op jit(solution)/shard_map/ppermute | solution.py:26
  170.7 12.1 %collective-permute-start.14 = (bf16[3,128,512]{2,1,0:T(8,128)(2,1)S(1)}, bf16[3,128,512]{2,1,0:T(8,128)(2,1)S(1)}, u32[]{:S(2)}, u32[]{:S(2)}) collective-permute-start(bf16[3,128,512]{2,1,0:T(8,128)(2,1)S(1)} %get-tuple-element.47), channel_id=1, source_target_pairs={{0,1},{1,0},{2,3},{3,2},{4,5},{5,4},{6,7},{7,6},{8,9},{9,8},{10,11... | collective-permute-start | bytes 1179656 | tf_op jit(solution)/shard_map/ppermute | solution.py:26
  170.8 12.2 %collective-permute-start.15 = (bf16[3,128,512]{2,1,0:T(8,128)(2,1)S(1)}, bf16[3,128,512]{2,1,0:T(8,128)(2,1)S(1)}, u32[]{:S(2)}, u32[]{:S(2)}) collective-permute-start(bf16[3,128,512]{2,1,0:T(8,128)(2,1)S(1)} %get-tuple-element.48), channel_id=1, source_target_pairs={{0,4},{2,6},{4,0},{6,2},{1,5},{3,7},{5,1},{7,3},{8,12},{10,14},{12... | collective-permute-start | bytes 1179656 | tf_op jit(solution)/shard_map/ppermute | solution.py:26
  176.4 15.0 %collective-permute-start.19 = (bf16[3,128,512]{2,1,0:T(8,128)(2,1)S(1)}, bf16[3,128,512]{2,1,0:T(8,128)(2,1)S(1)}, u32[]{:S(2)}, u32[]{:S(2)}) collective-permute-start(bf16[3,128,512]{2,1,0:T(8,128)(2,1)S(1)} %get-tuple-element.58), channel_id=1, source_target_pairs={{0,1},{1,0},{2,3},{3,2},{4,5},{5,4},{6,7},{7,6},{8,9},{9,8},{10,11... | collective-permute-start | bytes 1179656 | tf_op jit(solution)/shard_map/ppermute | solution.py:26
  177.9 13.5 %collective-permute-start.20 = (bf16[3,128,512]{2,1,0:T(8,128)(2,1)S(1)}, bf16[3,128,512]{2,1,0:T(8,128)(2,1)S(1)}, u32[]{:S(2)}, u32[]{:S(2)}) collective-permute-start(bf16[3,128,512]{2,1,0:T(8,128)(2,1)S(1)} %get-tuple-element.59), channel_id=1, source_target_pairs={{0,4},{2,6},{4,0},{6,2},{1,5},{3,7},{5,1},{7,3},{8,12},{10,14},{12... | collective-permute-start | bytes 1179656 | tf_op jit(solution)/shard_map/ppermute | solution.py:26
  186.5 12.0 %collective-permute-start.22 = (bf16[3,128,512]{2,1,0:T(8,128)(2,1)S(1)}, bf16[3,128,512]{2,1,0:T(8,128)(2,1)S(1)}, u32[]{:S(2)}, u32[]{:S(2)}) collective-permute-start(bf16[3,128,512]{2,1,0:T(8,128)(2,1)S(1)} %get-tuple-element.64), channel_id=1, source_target_pairs={{0,1},{1,0},{2,3},{3,2},{4,5},{5,4},{6,7},{7,6},{8,9},{9,8},{10,11... | collective-permute-start | bytes 1179656 | tf_op jit(solution)/shard_map/ppermute | solution.py:26
  188.2 10.7 %collective-permute-start.23 = (bf16[3,128,512]{2,1,0:T(8,128)(2,1)S(1)}, bf16[3,128,512]{2,1,0:T(8,128)(2,1)S(1)}, u32[]{:S(2)}, u32[]{:S(2)}) collective-permute-start(bf16[3,128,512]{2,1,0:T(8,128)(2,1)S(1)} %get-tuple-element.65), channel_id=1, source_target_pairs={{0,4},{2,6},{4,0},{6,2},{1,5},{3,7},{5,1},{7,3},{8,12},{10,14},{12... | collective-permute-start | bytes 1179656 | tf_op jit(solution)/shard_map/ppermute | solution.py:26
  189.8 8.2 %collective-permute-start.18 = (bf16[128,1024]{1,0:T(8,128)(2,1)S(1)}, bf16[128,1024]{1,0:T(8,128)(2,1)S(1)}, u32[]{:S(2)}, u32[]{:S(2)}) collective-permute-start(bf16[128,1024]{1,0:T(8,128)(2,1)S(1)} %get-tuple-element.57.refs_8_), channel_id=1, source_target_pairs={{0,8},{8,16},{16,24},{24,0},{1,9},{9,17},{17,25},{25,1},{2,10},{10... | collective-permute-start | bytes 786440 | tf_op jit(solution)/shard_map/ppermute | solution.py:21
  191.6 12.0 %collective-permute-start.21 = (bf16[128,1024]{1,0:T(8,128)(2,1)S(1)}, bf16[128,1024]{1,0:T(8,128)(2,1)S(1)}, u32[]{:S(2)}, u32[]{:S(2)}) collective-permute-start(bf16[128,1024]{1,0:T(8,128)(2,1)S(1)} %get-tuple-element.63.refs_8_), channel_id=1, source_target_pairs={{0,8},{8,16},{16,24},{24,0},{1,9},{9,17},{17,25},{25,1},{2,10},{10... | collective-permute-start | bytes 786440 | tf_op jit(solution)/shard_map/ppermute | solution.py:21
  193.3 8.8 %collective-permute-start.25 = (bf16[1,128,512]{2,1,0:T(8,128)(2,1)S(1)}, bf16[1,128,512]{2,1,0:T(8,128)(2,1)S(1)}, u32[]{:S(2)}, u32[]{:S(2)}) collective-permute-start(bf16[1,128,512]{2,1,0:T(8,128)(2,1)S(1)} %get-tuple-element.71), channel_id=1, source_target_pairs={{0,1},{1,0},{2,3},{3,2},{4,5},{5,4},{6,7},{7,6},{8,9},{9,8},{10,11... | collective-permute-start | bytes 393224 | tf_op jit(solution)/shard_map/ppermute | solution.py:26
  198.0 5.7 %collective-permute-start.26 = (bf16[1,128,512]{2,1,0:T(8,128)(2,1)S(1)}, bf16[1,128,512]{2,1,0:T(8,128)(2,1)S(1)}, u32[]{:S(2)}, u32[]{:S(2)}) collective-permute-start(bf16[1,128,512]{2,1,0:T(8,128)(2,1)S(1)} %get-tuple-element.72), channel_id=1, source_target_pairs={{0,4},{2,6},{4,0},{6,2},{1,5},{3,7},{5,1},{7,3},{8,12},{10,14},{12... | collective-permute-start | bytes 393224 | tf_op jit(solution)/shard_map/ppermute | solution.py:26
  199.1 11.3 %collective-permute-start.24 = (bf16[128,1024]{1,0:T(8,128)(2,1)S(1)}, bf16[128,1024]{1,0:T(8,128)(2,1)S(1)}, u32[]{:S(2)}, u32[]{:S(2)}) collective-permute-start(bf16[128,1024]{1,0:T(8,128)(2,1)S(1)} %get-tuple-element.70.refs_6_), channel_id=1, source_target_pairs={{0,8},{8,16},{16,24},{24,0},{1,9},{9,17},{17,25},{25,1},{2,10},{10... | collective-permute-start | bytes 786440 | tf_op jit(solution)/shard_map/ppermute | solution.py:21
  200.7 5.0 %collective-permute-start.28 = (bf16[1,128,512]{2,1,0:T(8,128)(2,1)S(1)}, bf16[1,128,512]{2,1,0:T(8,128)(2,1)S(1)}, u32[]{:S(2)}, u32[]{:S(2)}) collective-permute-start(bf16[1,128,512]{2,1,0:T(8,128)(2,1)S(1)} %get-tuple-element.75), channel_id=1, source_target_pairs={{0,1},{1,0},{2,3},{3,2},{4,5},{5,4},{6,7},{7,6},{8,9},{9,8},{10,11... | collective-permute-start | bytes 393224 | tf_op jit(solution)/shard_map/ppermute | solution.py:26
  202.1 5.0 %collective-permute-start.29 = (bf16[1,128,512]{2,1,0:T(8,128)(2,1)S(1)}, bf16[1,128,512]{2,1,0:T(8,128)(2,1)S(1)}, u32[]{:S(2)}, u32[]{:S(2)}) collective-permute-start(bf16[1,128,512]{2,1,0:T(8,128)(2,1)S(1)} %get-tuple-element.76), channel_id=1, source_target_pairs={{0,4},{2,6},{4,0},{6,2},{1,5},{3,7},{5,1},{7,3},{8,12},{10,14},{12... | collective-permute-start | bytes 393224 | tf_op jit(solution)/shard_map/ppermute | solution.py:26
  203.7 11.1 %collective-permute-start.27 = (bf16[128,1024]{1,0:T(8,128)(2,1)S(1)}, bf16[128,1024]{1,0:T(8,128)(2,1)S(1)}, u32[]{:S(2)}, u32[]{:S(2)}) collective-permute-start(bf16[128,1024]{1,0:T(8,128)(2,1)S(1)} %sum_stage.16.refs_6_), channel_id=1, source_target_pairs={{0,8},{8,16},{16,24},{24,0},{1,9},{9,17},{17,25},{25,1},{2,10},{10... | collective-permute-start | bytes 786440 | tf_op jit(solution)/shard_map/ppermute | solution.py:21
  207.1 10.5 %collective-permute-start.30 = (bf16[128,1024]{1,0:T(8,128)(2,1)S(1)}, bf16[128,1024]{1,0:T(8,128)(2,1)S(1)}, u32[]{:S(2)}, u32[]{:S(2)}) collective-permute-start(bf16[128,1024]{1,0:T(8,128)(2,1)S(1)} %sum_stage.17), channel_id=1, source_target_pairs={{0,8},{8,16},{16,24},{24,0},{1,9},{9,17},{17,25},{25,1},{2,10},{10... | collective-permute-start | bytes 786440 | tf_op jit(solution)/shard_map/ppermute | solution.py:21
  217.6 1.1 copy-start.13

commit v6 on v5

--- a/solution.py
+++ b/solution.py
@@ -75,13 +75,16 @@
     weights_ref, out_ref, total_ref = refs[sum(halves)], refs[-2], refs[-1]
     step, steps = pl.program_id(0), pl.num_programs(0)
     weights = jnp.concatenate([weights_ref[0], weights_ref[1], weights_ref[2]], axis=1)
-    early = step < steps // 2
+    early, block = step < steps // 2, weights.shape[0]
+    columns = pl.ds(pl.multiple_of(step * block, block), block)
+    half_columns = pl.ds(pl.multiple_of(step % (steps // 2) * block, block), block)
     blocks, place = [], 0
     for count in halves:
         if count == 1:
-            blocks.append(refs[place][...])
+            blocks.append(refs[place][:, columns])
         else:
-            blocks.append(jnp.where(early, refs[place][...], refs[place + 1][...]))
+            parts = refs[place][:, half_columns], refs[place + 1][:, half_columns]
+            blocks.append(jnp.where(early, *parts))
         place += count
     rows = jnp.concatenate(blocks, axis=0)
     product = jnp.dot(rows, weights, preferred_element_type=jnp.float32)
@@ -111,14 +114,10 @@
     steps = 4
     block = depth // steps
     count = len(blocks) * rows
-    whole = pl.BlockSpec((rows, block), lambda k: (0, k))
-    first = pl.BlockSpec((rows, block), lambda k: (0, jnp.minimum(k, steps // 2 - 1)))
-    second = pl.BlockSpec((rows, block), lambda k: (0, jnp.maximum(k - steps // 2, 0)))
-    specs = [spec for parts in blocks for spec in ([whole] if len(parts) == 1 else [first, second])]
     return pl.pallas_call(
         functools.partial(project_kernel, halves=[len(parts) for parts in blocks]),
         grid=(steps,),
-        in_specs=specs
+        in_specs=[pl.BlockSpec(memory_space=pltpu.VMEM)] * sum(len(parts) for parts in blocks)
         + [pl.BlockSpec((3, block, width), lambda k: (0, k, 0))]
         + [pl.BlockSpec(memory_space=pl.ANY)] * len(earlier),
         out_specs=pl.BlockSpec((count, 3 * width), lambda k: (0, 0)),
@@ -130,7 +129,7 @@
             bytes_accessed=2 * (count * depth + weights.size),
             transcendentals=0,
         ),
-        compiler_params=pltpu.CompilerParams(vmem_limit_bytes=30 * MIB),
+        compiler_params=pltpu.CompilerParams(vmem_limit_bytes=26 * MIB),
     )(*[part for parts in blocks for part in parts], weights, *earlier)
 
 
@@ -213,7 +212,7 @@
             bytes_accessed=2 * (heads.size + context.size),
             transcendentals=count * visible.shape[1] * TILE * width // HD,
         ),
-        compiler_params=pltpu.CompilerParams(vmem_limit_bytes=32 * MIB),
+        compiler_params=pltpu.CompilerParams(vmem_limit_bytes=16 * MIB),
     )(visible, heads, context, *earlier)
 
 
@@ -250,11 +249,14 @@
 def begin(start, refs, across_out, along_out, first_kept, second_kept):
     attended_ref, core_attended_ref, weights_ref, core_weights_ref, rows_ref, gates_ref = refs
     tokens, half = rows_ref.shape[0], first_kept.shape[2]
-    attended = jnp.concatenate([attended_ref[...], core_attended_ref[...]], axis=1)
 
     def product_of(columns):
-        weights = jnp.concatenate([weights_ref[:, columns], core_weights_ref[:, columns]], axis=0)
-        return jnp.dot(attended, weights, preferred_element_type=jnp.float32)
+        near = jnp.dot(
+            attended_ref[...], weights_ref[:, columns], preferred_element_type=jnp.float32
+        )
+        return near + jnp.dot(
+            core_attended_ref[...], core_weights_ref[:, columns], preferred_element_type=jnp.float32
+        )
 
     columns = slice(start, start + half)
     product = product_of(columns)
@@ -353,7 +355,7 @@
         out_shape=list(outs.values()),
         name="sum_stage",
         cost_estimate=SHORT,
-        compiler_params=pltpu.CompilerParams(vmem_limit_bytes=24 * MIB),
+        compiler_params=pltpu.CompilerParams(vmem_limit_bytes=16 * MIB),
     )(*operands.values(), *earlier)
     return dict(zip(outs, results))
 
@@ -376,9 +378,9 @@
     middle = features // 2
     gate = modulate[2:3]
     other_gate = from_partner(gate, "cfg", 1)
-    across, along = after(across, (packed,)), after(along, (packed, other_gate))
-    first = from_partner(half_of(across, 0, ()), "sp", 2)
-    second = from_partner(half_of(along, middle, ()), "cfg", 1)
+    halves = half_of(across, 0, (packed,)), half_of(along, middle, (packed,))
+    first = from_partner(halves[0], "sp", 2)
+    second = from_partner(halves[1], "cfg", 1)
     gates = jnp.concatenate([gate, other_gate], axis=0)
     core_weights = from_partner(project_out[0], "sp", 1)
     near = [(own,), (across,), (along,), (first, second)]
@@ -386,7 +388,7 @@
         tuple(from_partner(part, "sp", 1) for part in parts) for parts in near[1:]
     ]
 
-    packed = after(packed, far[2])
+    packed = after(packed, (first, second, other_gate))
     context = lax.all_to_all(packed, ("sp", "cfg"), split_axis=0, concat_axis=0, tiled=True)
     context = context.reshape(devices * context_rows, 2 * width)
 

time: 220 us -> 177 us (0.80)
  waiting for transfers between devices: 91.2 us -> 55.6 us
  local copies, waits for them, and re-layouts: 37.8 us -> 31.9 us
  starting transfers between devices: 39.2 us -> 34.8 us
  Pallas kernels: 50.3 us -> 53.1 us
    ppermute x26, waiting for transfers between devices: 79.3 us -> 42.4 us  [from_partner(): return lax.ppermute(value, axis, pairs)]
    ppermute x26, starting transfers between devices: 27.3 us -> 23.3 us  [from_partner(): return lax.ppermute(value, axis, pairs)]
    another operation x2, local copies, waits for them, and re-layouts: 14 us -> 11 us  [per_device(): packed = stale_cache[0, 0].reshape(context_rows, 2, devices, width)]
    all_to_all x1, waiting for transfers between devices: 0.01 us -> 2.37 us  [per_device(): lax.all_to_all(packed, ('sp', 'cfg'), split_axis=0, concat_axis=0, tiled=...]
    unnamed x34 -> x33, local copies, waits for them, and re-layouts: 15 us -> 13.3 us
  transfers between devices with their start and end apart: 32 -> 32, of which waited for: 17 -> 20; matrix products, arithmetic and copies ran while one was open for 12% -> 11% of each run, Pallas kernels for 18% -> 24%
where the time goes in v6:
time: 177 us; the launch traced here: 176 us
  waiting for transfers between devices  55.6 us (31%)
  Pallas kernels  53.1 us (30%)
  starting transfers between devices  34.8 us (20%)
  local copies, waits for them, and re-layouts  31.9 us (18%)
    ppermute x26, waiting for transfers between devices, from_partner(): return lax.ppermute(value, axis, pairs)  42.4 us
    ppermute x26, starting transfers between devices, from_partner(): return lax.ppermute(value, axis, pairs)  23.3 us
    pallas_call x1, Pallas kernels, project(): pl.pallas_call(functools.partial(project_kernel, halves=[len(parts) for p...  20.6 us
    pallas_call x9, Pallas kernels, stage(): pl.pallas_call(functools.partial(stage_kernel, parts=parts, start=start,...  18.3 us
    unnamed x33, local copies, waits for them, and re-layouts  13.3 us
    another operation x2, local copies, waits for them, and re-layouts, per_device(): packed = stale_cache[0, 0].reshape(context_rows, 2, devices, width)  11 us
    ppermute x5, waiting for transfers between devices, from_behind(): return lax.ppermute(x, axis, [(i, (i + by) % count) for i in range(count)])  10.8 us
    pallas_call x2, Pallas kernels, attend(): pl.pallas_call(functools.partial(attend_kernel, first_block=first_block),...  8.11 us
  transfers between devices with their start and end apart: 32, of which 20 were waited for; matrix products, arithmetic and copies ran while one was open for 11% of the time, Pallas kernels for 24%

profile of v6, /device:TPU:0, one launch (start us, length us, event | category | flops | bytes accessed | tf_op | source)
XLA Modules:
  0.0 175.8 jit_solution(14450245123458742057)
XLA Ops:
  0.0 0.8 copy.13
  0.9 1.3 copy-done
  2.2 3.5 %modulated_norm.1.refs_0_ = bf16[128,5120]{1,0:T(8,128)(2,1)} custom-call(bf16[128,5120]{1,0:T(8,128)(2,1)S(1)} %bitcast.14, f32[3,5120]{1,0:T(4,128)S(1)} %bitcast.32), custom_call_target="tpu_custom_call" | custom-call | flops 6553600 | bytes 2621440 | tf_op jit(solution)/shard_map/modulated_norm/pallas_call | solution.py:47
  5.7 2.9 %collective-permute-start.1 = (bf16[128,5120]{1,0:T(8,128)(2,1)}, bf16[128,5120]{1,0:T(8,128)(2,1)}, u32[]{:S(2)}, u32[]{:S(2)}) collective-permute-start(bf16[128,5120]{1,0:T(8,128)(2,1)} %modulated_norm.1.refs_0_), channel_id=1, source_target_pairs={{0,1},{1,0},{2,3},{3,2},{4,5},{5,4},{6,7},{7,6},{8,9},{9,8},{10,11... | collective-permute-start | bytes 3932168 | tf_op jit(solution)/shard_map/ppermute | solution.py:26
  8.6 1.5 collective-permute-start.2
  10.7 6.9 %reshape_squeeze.3 = bf16[256,2,8,384]{3,2,1,0:T(8,128)(2,1)S(1)} reshape(bf16[1,1,256,2,3072]{4,3,2,1,0:T(2,128)(2,1)} %param.10) | data formatting | bytes 6291456 | tf_op jit(solution)/shard_map/reshape;squeeze | solution.py:371
  17.6 4.1 %copy.12 = bf16[256,2,8,384]{3,1,0,2:T(2,128)(2,1)} copy(bf16[256,2,8,384]{3,2,1,0:T(8,128)(2,1)S(1)} %reshape_squeeze.3) | data formatting | bytes 6291456 | tf_op jit(solution)/shard_map/reshape;squeeze | solution.py:371
  21.6 6.8 %reshape.7.refs_0_.value_ref = bf16[8,256,768]{2,1,0:T(8,128)(2,1)S(1)} reshape(bf16[8,256,2,384]{3,2,1,0:T(2,128)(2,1)} %bitcast.36) | data formatting | bytes 6291456 | tf_op jit(solution)/shard_map/reshape | solution.py:372
  28.5 9.2 %collective-permute-done.1.rows_ref.refs_1_ = bf16[128,5120]{1,0:T(8,128)(2,1)} collective-permute-done((bf16[128,5120]{1,0:T(8,128)(2,1)}, bf16[128,5120]{1,0:T(8,128)(2,1)}, u32[]{:S(2)}, u32[]{:S(2)}) %collective-permute-start.1) | collective-permute-done | bytes 1310752 | tf_op jit(solution)/shard_map/ppermute | solution.py:26
  37.7 1.4 half_of.2
  39.1 1.8 %collective-permute-start.3 = (bf16[128,2560]{1,0:T(8,128)(2,1)S(1)}, bf16[128,2560]{1,0:T(8,128)(2,1)}, u32[]{:S(2)}, u32[]{:S(2)}) collective-permute-start(bf16[128,2560]{1,0:T(8,128)(2,1)S(1)} %half_of.2), channel_id=1, source_target_pairs={{0,4},{2,6},{4,0},{6,2},{1,5},{3,7},{5,1},{7,3},{8,12},{10,14},{12... | collective-permute-start | bytes 1966088 | tf_op jit(solution)/shard_map/ppermute | solution.py:26
  40.9 1.4 half_of.3
  42.3 1.6 collective-permute-start.4
  43.8 0.7 slice_bitcast_fusion
  45.1 13.0 %collective-permute-done.refs_2_ = f32[1,5120]{1,0:T(1,128)S(1)} collective-permute-done((f32[1,5120]{1,0:T(1,128)S(1)}, f32[1,5120]{1,0:T(1,128)S(1)}, u32[]{:S(2)}, u32[]{:S(2)}) %collective-permute-start) | collective-permute-done | bytes 20512 | tf_op jit(solution)/shard_map/ppermute | solution.py:26
  58.1 0.6 copy-done.11
  58.7 0.9 copy-done.7
  59.6 3.8 %all-to-all-start = ((bf16[8,256,768]{2,1,0:T(8,128)(2,1)}), bf16[8,256,768]{2,1,0:T(8,128)(2,1)S(1)}, u32[]{:S(2)}, u32[]{:S(2)}) async-start(bf16[8,256,768]{2,1,0:T(8,128)(2,1)} %after.1), calls=%async_computation | async-start | bytes 6291456 | tf_op jit(solution)/shard_map/all_to_all | solution.py:392
  64.5 5.2 %collective-permute-done.8.refs_8_ = bf16[128,2560]{1,0:T(8,128)(2,1)S(1)} collective-permute-done((bf16[128,2560]{1,0:T(8,128)(2,1)}, bf16[128,2560]{1,0:T(8,128)(2,1)S(1)}, u32[]{:S(2)}, u32[]{:S(2)}) %collective-permute-start.8) | collective-permute-done | bytes 655392 | tf_op jit(solution)/shard_map/ppermute | solution.py:26
  69.8 0.9 collective-permute-done.9.refs_9_
  70.7 1.1 copy-done.8
  71.8 4.3 %copy-done.10 = bf16[1,3,5120,384]{3,2,1,0:T(8,128)(2,1)S(1)} copy-done((bf16[1,3,5120,384]{3,2,1,0:T(8,128)(2,1)S(1)}, bf16[1,3,5120,384]{3,2,1,0:T(8,128)(2,1)}, u32[]{:S(2)}) %copy-start.10) | copy-done | bytes 11796504
  76.1 20.6 %project_heads.1.heads_ref = bf16[1024,1152]{1,0:T(8,128)(2,1)S(1)} custom-call(bf16[128,5120]{1,0:T(8,128)(2,1)} %modulated_norm.1.refs_0_, bf16[128,5120]{1,0:T(8,128)(2,1)} %collective-permute-done.1.rows_ref.refs_1_, bf16[128,5120]{1,0:T(8,128)(2,1)} %collective-permute-done.2.rows_ref.refs_2_, bf16[128,2560]{1,0:T(8,128)(2,1)} %collective-permute-done.3.refs_3_.refs_0_, ...), custom_call_target="tpu_custom_call" | custom-call | flops 12079595520 | bytes 22282240 | tf_op jit(solution)/shard_map/project_heads/pallas_call | solution.py:117
  96.7 1.5 copy-done.4
  98.2 2.4 %all-to-all-done = bf16[8,256,768]{2,1,0:T(8,128)(2,1)S(1)} async-done(((bf16[8,256,768]{2,1,0:T(8,128)(2,1)}), bf16[8,256,768]{2,1,0:T(8,128)(2,1)S(1)}, u32[]{:S(2)}, u32[]{:S(2)}) %all-to-all-start) | async-done | bytes 3145760 | tf_op jit(solution)/shard_map/all_to_all | solution.py:392
  100.6 1.7 copy-done.5
  102.2 3.9 %attend.2.refs_0_ = bf16[512,384]{1,0:T(8,128)(2,1)S(1)} custom-call(s32[4,6]{1,0:T(4,128)S(1)} %bitcast.33, bf16[1024,1152]{1,0:T(8,128)(2,1)S(1)} %copy-done.5, bf16[2048,768]{1,0:T(8,128)(2,1)S(1)} %bitcast.30), custom_call_target="tpu_custom_call" | custom-call | flops 603979776 | bytes 5505024 | tf_op jit(solution)/shard_map/attend/pallas_call | solution.py:200
  106.3 4.2 %attend.3.refs_2_ = bf16[512,384]{1,0:T(8,128)(2,1)S(1)} custom-call(s32[4,6]{1,0:T(4,128)S(1)} %bitcast.34, bf16[1024,1152]{1,0:T(8,128)(2,1)S(1)} %copy-done.6, bf16[2048,768]{1,0:T(8,128)(2,1)S(1)} %bitcast.31, bf16[512,384]{1,0:T(8,128)(2,1)S(1)} %attend.2.refs_0_), custom_call_target="tpu_custom_call" | custom-call | flops 603979776 | bytes 5505024 | tf_op jit(solution)/shard_map/attend/pallas_call | solution.py:200
  110.6 3.4 %sum_stage.9 = (bf16[2,128,512]{2,1,0:T(8,128)(2,1)S(1)}, bf16[2,128,512]{2,1,0:T(8,128)(2,1)S(1)}, f32[2,128,512]{2,1,0:T(8,128)S(1)}, f32[2,128,512]{2,1,0:T(8,128)S(1)}) custom-call(bf16[128,5120]{1,0:T(8,128)(2,1)S(1)} %bitcast.15, f32[2,5120]{1,0:T(2,128)S(1)} %pad_maximum_fusion.refs_1_, bf16[512,384]{1,0:T(8,128)(2,1)S(1)} %attend.3.refs_2_, ...), custom_call_target="tpu_custom_call" | custom-call | flops 1 | bytes 1 | tf_op jit(solution)/shard_map/sum_stage/pallas_call | solution.py:343
  114.0 1.1 collective-permute-start.12
  115.0 0.6 collective-permute-start.13
  115.6 3.4 %sum_stage.10 = (bf16[2,128,512]{2,1,0:T(8,128)(2,1)S(1)}, bf16[2,128,512]{2,1,0:T(8,128)(2,1)S(1)}, f32[2,128,512]{2,1,0:T(8,128)S(1)}, f32[2,128,512]{2,1,0:T(8,128)S(1)}) custom-call(bf16[128,5120]{1,0:T(8,128)(2,1)S(1)} %bitcast.16, f32[2,5120]{1,0:T(2,128)S(1)} %pad_maximum_fusion.refs_1_, bf16[512,384]{1,0:T(8,128)(2,1)S(1)} %attend.3.refs_2_, ...), custom_call_target="tpu_custom_call" | custom-call | flops 1 | bytes 1 | tf_op jit(solution)/shard_map/sum_stage/pallas_call | solution.py:343
  119.0 1.4 collective-permute-start.16
  120.3 1.2 collective-permute-start.17
  121.5 1.6 collective-permute-done.12.refs_6_
  123.1 1.0 collective-permute-done.13.refs_7_
  124.2 3.6 %sum_stage.11 = (bf16[3,128,512]{2,1,0:T(8,128)(2,1)S(1)}, bf16[3,128,512]{2,1,0:T(8,128)(2,1)S(1)}, f32[2,128,512]{2,1,0:T(8,128)S(1)}, f32[2,128,512]{2,1,0:T(...) custom-call(bf16[128,5120]{1,0:T(8,128)(2,1)S(1)} %bitcast.17, f32[2,5120]{1,0:T(2,128)S(1)} %pad_maximum_fusion.refs_1_, ...), custom_call_target="tpu_custom_call" | custom-call | flops 1 | bytes 1 | tf_op jit(solution)/shard_map/sum_stage/pallas_call | solution.py:343
  127.8 1.1 collective-permute-start.14
  129.1 3.6 %sum_stage.12 = (bf16[3,128,512]{2,1,0:T(8,128)(2,1)S(1)}, bf16[3,128,512]{2,1,0:T(8,128)(2,1)S(1)}, f32[2,128,512]{2,1,0:T(8,128)S(1)}, f32[2,128,512]{2,1,0:T(...) custom-call(bf16[128,5120]{1,0:T(8,128)(2,1)S(1)} %bitcast.18, f32[2,5120]{1,0:T(2,128)S(1)} %pad_maximum_fusion.refs_1_, ...), custom_call_target="tpu_custom_call" | custom-call | flops 1 | bytes 1 | tf_op jit(solution)/shard_map/sum_stage/pallas_call | solution.py:343
  132.7 1.1 collective-permute-start.19
  133.8 1.9 %collective-permute-start.20 = (bf16[3,128,512]{2,1,0:T(8,128)(2,1)S(1)}, bf16[3,128,512]{2,1,0:T(8,128)(2,1)S(1)}, u32[]{:S(2)}, u32[]{:S(2)}) collective-permute-start(bf16[3,128,512]{2,1,0:T(8,128)(2,1)S(1)} %get-tuple-element.59), channel_id=1, source_target_pairs={{0,4},{2,6},{4,0},{6,2},{1,5},{3,7},{5,1},{7,3},{8,12},{10,14},{12... | collective-permute-start | bytes 1179656 | tf_op jit(solution)/shard_map/ppermute | solution.py:26
  135.6 4.3 %collective-permute-done.14.refs_6_ = bf16[3,128,512]{2,1,0:T(8,128)(2,1)S(1)} collective-permute-done((bf16[3,128,512]{2,1,0:T(8,128)(2,1)S(1)}, bf16[3,128,512]{2,1,0:T(8,128)(2,1)S(1)}, u32[]{:S(2)}, u32[]{:S(2)}) %collective-permute-start.14) | collective-permute-done | bytes 393248 | tf_op jit(solution)/shard_map/ppermute | solution.py:26
  139.9 1.0 collective-permute-done.15.refs_7_
  141.0 3.7 %sum_stage.13 = (bf16[3,128,512]{2,1,0:T(8,128)(2,1)S(1)}, bf16[3,128,512]{2,1,0:T(8,128)(2,1)S(1)}, f32[2,128,512]{2,1,0:T(8,128)S(1)}, f32[2,128,512]{2,1,0:T(...) custom-call(bf16[128,5120]{1,0:T(8,128)(2,1)S(1)} %bitcast.19, ...), custom_call_target="tpu_custom_call" | custom-call | flops 1 | bytes 1 | tf_op jit(solution)/shard_map/sum_stage/pallas_call | solution.py:343
  144.7 1.1 collective-permute-start.22
  145.7 1.6 collective-permute-start.18
  147.3 1.1 collective-permute-done.19.refs_2_
  148.4 1.0 collective-permute-done.20.refs_3_
  149.6 1.6 collective-permute-start.21
  151.2 1.0 collective-permute-start.25
  152.2 2.3 %collective-permute-done.18.refs_9_ = bf16[128,1024]{1,0:T(8,128)(2,1)S(1)} collective-permute-done((bf16[128,1024]{1,0:T(8,128)(2,1)S(1)}, bf16[128,1024]{1,0:T(8,128)(2,1)S(1)}, u32[]{:S(2)}, u32[]{:S(2)}) %collective-permute-start.18) | collective-permute-done | bytes 262176 | tf_op jit(solution)/shard_map/ppermute | solution.py:21
  154.5 1.4 collective-permute-start.26
  155.9 0.6 collective-permute-done.23.refs_3_
  156.8 1.6 collective-permute-start.24
  158.4 1.0 collective-permute-start.28
  159.4 0.6 collective-permute-start.29
  160.4 1.2 collective-permute-start.27
  161.7 1.7 collective-permute-done.28.refs_2_
  163.4 1.0 collective-permute-done.29.refs_3_
  164.4 1.6 collective-permute-start.30
  166.1 1.8 %collective-permute-done.24 = bf16[128,1024]{1,0:T(8,128)(2,1)S(1)} collective-permute-done((bf16[128,1024]{1,0:T(8,128)(2,1)S(1)}, bf16[128,1024]{1,0:T(8,128)(2,1)S(1)}, u32[]{:S(2)}, u32[]{:S(2)}) %collective-permute-start.24) | collective-permute-done | bytes 262176 | tf_op jit(solution)/shard_map/ppermute | solution.py:21
  167.9 4.0 %collective-permute-done.27 = bf16[128,1024]{1,0:T(8,128)(2,1)S(1)} collective-permute-done((bf16[128,1024]{1,0:T(8,128)(2,1)S(1)}, bf16[128,1024]{1,0:T(8,128)(2,1)S(1)}, u32[]{:S(2)}, u32[]{:S(2)}) %collective-permute-start.27) | collective-permute-done | bytes 262176 | tf_op jit(solution)/shard_map/ppermute | solution.py:21
  171.9 2.8 %collective-permute-done.30 = bf16[128,1024]{1,0:T(8,128)(2,1)S(1)} collective-permute-done((bf16[128,1024]{1,0:T(8,128)(2,1)S(1)}, bf16[128,1024]{1,0:T(8,128)(2,1)S(1)}, u32[]{:S(2)}, u32[]{:S(2)}) %collective-permute-start.30) | collective-permute-done | bytes 262176 | tf_op jit(solution)/shard_map/ppermute | solution.py:21
  174.7 1.0 copy-done.13
  (55 shorter events, 3.5 us)
Async XLA Ops:
  0.9 1.3 copy-start
  5.7 32.0 %collective-permute-start.1 = (bf16[128,5120]{1,0:T(8,128)(2,1)}, bf16[128,5120]{1,0:T(8,128)(2,1)}, u32[]{:S(2)}, u32[]{:S(2)}) collective-permute-start(bf16[128,5120]{1,0:T(8,128)(2,1)} %modulated_norm.1.refs_0_), channel_id=1, source_target_pairs={{0,1},{1,0},{2,3},{3,2},{4,5},{5,4},{6,7},{7,6},{8,9},{9,8},{10,11... | collective-permute-start | bytes 3932168 | tf_op jit(solution)/shard_map/ppermute | solution.py:26
  8.6 32.3 %collective-permute-start.2 = (bf16[128,5120]{1,0:T(8,128)(2,1)}, bf16[128,5120]{1,0:T(8,128)(2,1)}, u32[]{:S(2)}, u32[]{:S(2)}) collective-permute-start(bf16[128,5120]{1,0:T(8,128)(2,1)} %modulated_norm.1.refs_0_), channel_id=1, source_target_pairs={{0,4},{2,6},{4,0},{6,2},{1,5},{3,7},{5,1},{7,3},{8,12},{10,14},{12... | collective-permute-start | bytes 3932168 | tf_op jit(solution)/shard_map/ppermute | solution.py:26
  10.1 60.6 %collective-permute-start.10 = (bf16[384,5120]{1,0:T(8,128)(2,1)}, bf16[384,5120]{1,0:T(8,128)(2,1)}, u32[]{:S(2)}, u32[]{:S(2)}) collective-permute-start(bf16[384,5120]{1,0:T(8,128)(2,1)} %bitcast.24), channel_id=1, source_target_pairs={{0,2},{2,0},{4,6},{6,4},{1,3},{3,1},{5,7},{7,5},{8,10},{10,8},{12,... | collective-permute-start | bytes 11796488 | tf_op jit(solution)/shard_map/ppermute | solution.py:26
  10.1 54.0 %collective-permute-start.5 = (bf16[128,5120]{1,0:T(8,128)(2,1)}, bf16[128,5120]{1,0:T(8,128)(2,1)}, u32[]{:S(2)}, u32[]{:S(2)}) collective-permute-start(bf16[128,5120]{1,0:T(8,128)(2,1)} %modulated_norm.1.refs_0_), channel_id=1, source_target_pairs={{0,2},{2,0},{4,6},{6,4},{1,3},{3,1},{5,7},{7,5},{8,10},{10,8},{12,... | collective-permute-start | bytes 3932168 | tf_op jit(solution)/shard_map/ppermute | solution.py:26
  28.5 12.5 %copy-start.3 = (bf16[8,256,768]{2,1,0:T(8,128)(2,1)}, bf16[8,256,768]{2,1,0:T(8,128)(2,1)S(1)}, u32[]{:S(2)}) copy-start(bf16[8,256,768]{2,1,0:T(8,128)(2,1)S(1)} %reshape.7.refs_0_.value_ref) | copy-start | bytes 9437188
  39.1 19.0 %collective-permute-start.3 = (bf16[128,2560]{1,0:T(8,128)(2,1)S(1)}, bf16[128,2560]{1,0:T(8,128)(2,1)}, u32[]{:S(2)}, u32[]{:S(2)}) collective-permute-start(bf16[128,2560]{1,0:T(8,128)(2,1)S(1)} %half_of.2), channel_id=1, source_target_pairs={{0,4},{2,6},{4,0},{6,2},{1,5},{3,7},{5,1},{7,3},{8,12},{10,14},{12... | collective-permute-start | bytes 1966088 | tf_op jit(solution)/shard_map/ppermute | solution.py:26
  42.3 15.8 %collective-permute-start.4 = (bf16[128,2560]{1,0:T(8,128)(2,1)S(1)}, bf16[128,2560]{1,0:T(8,128)(2,1)S(1)}, u32[]{:S(2)}, u32[]{:S(2)}) collective-permute-start(bf16[128,2560]{1,0:T(8,128)(2,1)S(1)} %half_of.3), channel_id=1, source_target_pairs={{0,1},{1,0},{2,3},{3,2},{4,5},{5,4},{6,7},{7,6},{8,9},{9,8},{10,11... | collective-permute-start | bytes 1966088 | tf_op jit(solution)/shard_map/ppermute | solution.py:26
  44.6 13.5 %collective-permute-start = (f32[1,5120]{1,0:T(1,128)S(1)}, f32[1,5120]{1,0:T(1,128)S(1)}, u32[]{:S(2)}, u32[]{:S(2)}) collective-permute-start(f32[1,5120]{1,0:T(1,128)S(1)} %slice_bitcast_fusion), channel_id=1, source_target_pairs={{0,1},{1,0},{2,3},{3,2},{4,5},{5,4},{6,7},{7,6},{8,9},{9,8},{10,11... | collective-permute-start | bytes 61448 | tf_op jit(solution)/shard_map/ppermute | solution.py:26
  58.1 0.6 copy-start.11
  58.7 0.9 copy-start.7
  59.6 41.0 %all-to-all-start = ((bf16[8,256,768]{2,1,0:T(8,128)(2,1)}), bf16[8,256,768]{2,1,0:T(8,128)(2,1)S(1)}, u32[]{:S(2)}, u32[]{:S(2)}) async-start(bf16[8,256,768]{2,1,0:T(8,128)(2,1)} %after.1), calls=%async_computation | async-start | bytes 6291456 | tf_op jit(solution)/shard_map/all_to_all | solution.py:392
  63.4 7.3 %collective-permute-start.6 = (bf16[128,5120]{1,0:T(8,128)(2,1)}, bf16[128,5120]{1,0:T(8,128)(2,1)S(1)}, u32[]{:S(2)}, u32[]{:S(2)}) collective-permute-start(bf16[128,5120]{1,0:T(8,128)(2,1)} %collective-permute-done.1.rows_ref.refs_1_), channel_id=1, source_target_pairs={{0,2},{2,0},{4,6},{6,4},{1,3},{3,1},{5,7},{7,5},{8,10},{10,8},{12,... | collective-permute-start | bytes 3932168 | tf_op jit(solution)/shard_map/ppermute | solution.py:26
  63.6 7.1 %collective-permute-start.7 = (bf16[128,5120]{1,0:T(8,128)(2,1)}, bf16[128,5120]{1,0:T(8,128)(2,1)S(1)}, u32[]{:S(2)}, u32[]{:S(2)}) collective-permute-start(bf16[128,5120]{1,0:T(8,128)(2,1)} %collective-permute-done.2.rows_ref.refs_2_), channel_id=1, source_target_pairs={{0,2},{2,0},{4,6},{6,4},{1,3},{3,1},{5,7},{7,5},{8,10},{10,8},{12,... | collective-permute-start | bytes 3932168 | tf_op jit(solution)/shard_map/ppermute | solution.py:26
  64.0 5.8 %collective-permute-start.8 = (bf16[128,2560]{1,0:T(8,128)(2,1)}, bf16[128,2560]{1,0:T(8,128)(2,1)S(1)}, u32[]{:S(2)}, u32[]{:S(2)}) collective-permute-start(bf16[128,2560]{1,0:T(8,128)(2,1)} %collective-permute-done.3.refs_3_.refs_0_), channel_id=1, source_target_pairs={{0,2},{2,0},{4,6},{6,4},{1,3},{3,1},{5,7},{7,5},{8,10},{10,8},{12,... | collective-permute-start | bytes 1966088 | tf_op jit(solution)/shard_map/ppermute | solution.py:26
  64.2 6.5 %collective-permute-start.9 = (bf16[128,2560]{1,0:T(8,128)(2,1)}, bf16[128,2560]{1,0:T(8,128)(2,1)S(1)}, u32[]{:S(2)}, u32[]{:S(2)}) collective-permute-start(bf16[128,2560]{1,0:T(8,128)(2,1)} %copy-done.7), channel_id=1, source_target_pairs={{0,2},{2,0},{4,6},{6,4},{1,3},{3,1},{5,7},{7,5},{8,10},{10,8},{12,... | collective-permute-start | bytes 1966088 | tf_op jit(solution)/shard_map/ppermute | solution.py:26
  70.7 1.1 copy-start.8
  71.8 4.4 %copy-start.10 = (bf16[1,3,5120,384]{3,2,1,0:T(8,128)(2,1)S(1)}, bf16[1,3,5120,384]{3,2,1,0:T(8,128)(2,1)}, u32[]{:S(2)}) copy-start(bf16[1,3,5120,384]{3,2,1,0:T(8,128)(2,1)} %param.8) | copy-start | bytes 35389444
  76.1 24.4 %copy-start.9 = (s32[1,4,6]{2,1,0:T(4,128)S(1)}, s32[1,4,6]{2,1,0:T(4,128)}, u32[]{:S(2)}) copy-start(s32[1,4,6]{2,1,0:T(4,128)} %param.11) | copy-start | bytes 292
  96.7 1.5 copy-start.4
  100.6 1.7 copy-start.5
  102.2 4.0 %copy-start.12 = (f32[1,5120]{1,0:T(1,128)S(1)}, f32[1,5120]{1,0:T(1,128)}, u32[]{:S(2)}) copy-start(f32[1,5120]{1,0:T(1,128)} %copy-done.11) | copy-start | bytes 61444
  102.2 4.1 %copy-start.6 = (bf16[1024,1152]{1,0:T(8,128)(2,1)S(1)}, bf16[1024,1152]{1,0:T(8,128)(2,1)}, u32[]{:S(2)}) copy-start(bf16[1024,1152]{1,0:T(8,128)(2,1)} %copy-done.4) | copy-start | bytes 7077892
  106.2 4.4 %collective-permute-start.11 = (bf16[512,384]{1,0:T(8,128)(2,1)S(1)}, bf16[512,384]{1,0:T(8,128)(2,1)S(1)}, u32[]{:S(2)}, u32[]{:S(2)}) collective-permute-start(bf16[512,384]{1,0:T(8,128)(2,1)S(1)} %attend.2.refs_0_), channel_id=1, source_target_pairs={{0,2},{2,0},{4,6},{6,4},{1,3},{3,1},{5,7},{7,5},{8,10},{10,8},{12,... | collective-permute-start | bytes 1179656 | tf_op jit(solution)/shard_map/ppermute | solution.py:26
  106.3 4.2 %copy-start.1 = (bf16[1,1,128,5120]{3,2,1,0:T(8,128)(2,1)S(1)}, bf16[1,1,128,5120]{3,2,1,0:T(8,128)(2,1)}, u32[]{:S(2)}) copy-start(bf16[1,1,128,5120]{3,2,1,0:T(8,128)(2,1)} %param.6) | copy-start | bytes 3932164
  106.3 4.2 %copy-start.2 = (bf16[1,384,5120]{2,1,0:T(8,128)(2,1)S(1)}, bf16[1,384,5120]{2,1,0:T(8,128)(2,1)}, u32[]{:S(2)}) copy-start(bf16[1,384,5120]{2,1,0:T(8,128)(2,1)} %param.9) | copy-start | bytes 11796484
  114.0 9.2 %collective-permute-start.12 = (bf16[2,128,512]{2,1,0:T(8,128)(2,1)S(1)}, bf16[2,128,512]{2,1,0:T(8,128)(2,1)S(1)}, u32[]{:S(2)}, u32[]{:S(2)}) collective-permute-start(bf16[2,128,512]{2,1,0:T(8,128)(2,1)S(1)} %get-tuple-element.42), channel_id=1, source_target_pairs={{0,1},{1,0},{2,3},{3,2},{4,5},{5,4},{6,7},{7,6},{8,9},{9,8},{10,11... | collective-permute-start | bytes 786440 | tf_op jit(solution)/shard_map/ppermute | solution.py:26
  115.0 9.1 %collective-permute-start.13 = (bf16[2,128,512]{2,1,0:T(8,128)(2,1)S(1)}, bf16[2,128,512]{2,1,0:T(8,128)(2,1)S(1)}, u32[]{:S(2)}, u32[]{:S(2)}) collective-permute-start(bf16[2,128,512]{2,1,0:T(8,128)(2,1)S(1)} %get-tuple-element.43), channel_id=1, source_target_pairs={{0,4},{2,6},{4,0},{6,2},{1,5},{3,7},{5,1},{7,3},{8,12},{10,14},{12... | collective-permute-start | bytes 786440 | tf_op jit(solution)/shard_map/ppermute | solution.py:26
  119.0 9.9 %collective-permute-start.16 = (bf16[2,128,512]{2,1,0:T(8,128)(2,1)S(1)}, bf16[2,128,512]{2,1,0:T(8,128)(2,1)S(1)}, u32[]{:S(2)}, u32[]{:S(2)}) collective-permute-start(bf16[2,128,512]{2,1,0:T(8,128)(2,1)S(1)} %get-tuple-element.53), channel_id=1, source_target_pairs={{0,1},{1,0},{2,3},{3,2},{4,5},{5,4},{6,7},{7,6},{8,9},{9,8},{10,11... | collective-permute-start | bytes 786440 | tf_op jit(solution)/shard_map/ppermute | solution.py:26
  120.3 8.7 %collective-permute-start.17 = (bf16[2,128,512]{2,1,0:T(8,128)(2,1)S(1)}, bf16[2,128,512]{2,1,0:T(8,128)(2,1)S(1)}, u32[]{:S(2)}, u32[]{:S(2)}) collective-permute-start(bf16[2,128,512]{2,1,0:T(8,128)(2,1)S(1)} %get-tuple-element.54), channel_id=1, source_target_pairs={{0,4},{2,6},{4,0},{6,2},{1,5},{3,7},{5,1},{7,3},{8,12},{10,14},{12... | collective-permute-start | bytes 786440 | tf_op jit(solution)/shard_map/ppermute | solution.py:26
  127.8 12.1 %collective-permute-start.14 = (bf16[3,128,512]{2,1,0:T(8,128)(2,1)S(1)}, bf16[3,128,512]{2,1,0:T(8,128)(2,1)S(1)}, u32[]{:S(2)}, u32[]{:S(2)}) collective-permute-start(bf16[3,128,512]{2,1,0:T(8,128)(2,1)S(1)} %get-tuple-element.47), channel_id=1, source_target_pairs={{0,1},{1,0},{2,3},{3,2},{4,5},{5,4},{6,7},{7,6},{8,9},{9,8},{10,11... | collective-permute-start | bytes 1179656 | tf_op jit(solution)/shard_map/ppermute | solution.py:26
  128.9 12.1 %collective-permute-start.15 = (bf16[3,128,512]{2,1,0:T(8,128)(2,1)S(1)}, bf16[3,128,512]{2,1,0:T(8,128)(2,1)S(1)}, u32[]{:S(2)}, u32[]{:S(2)}) collective-permute-start(bf16[3,128,512]{2,1,0:T(8,128)(2,1)S(1)} %get-tuple-element.48), channel_id=1, source_target_pairs={{0,4},{2,6},{4,0},{6,2},{1,5},{3,7},{5,1},{7,3},{8,12},{10,14},{12... | collective-permute-start | bytes 1179656 | tf_op jit(solution)/shard_map/ppermute | solution.py:26
  132.7 15.7 %collective-permute-start.19 = (bf16[3,128,512]{2,1,0:T(8,128)(2,1)S(1)}, bf16[3,128,512]{2,1,0:T(8,128)(2,1)S(1)}, u32[]{:S(2)}, u32[]{:S(2)}) collective-permute-start(bf16[3,128,512]{2,1,0:T(8,128)(2,1)S(1)} %get-tuple-element.58), channel_id=1, source_target_pairs={{0,1},{1,0},{2,3},{3,2},{4,5},{5,4},{6,7},{7,6},{8,9},{9,8},{10,11... | collective-permute-start | bytes 1179656 | tf_op jit(solution)/shard_map/ppermute | solution.py:26
  133.8 15.6 %collective-permute-start.20 = (bf16[3,128,512]{2,1,0:T(8,128)(2,1)S(1)}, bf16[3,128,512]{2,1,0:T(8,128)(2,1)S(1)}, u32[]{:S(2)}, u32[]{:S(2)}) collective-permute-start(bf16[3,128,512]{2,1,0:T(8,128)(2,1)S(1)} %get-tuple-element.59), channel_id=1, source_target_pairs={{0,4},{2,6},{4,0},{6,2},{1,5},{3,7},{5,1},{7,3},{8,12},{10,14},{12... | collective-permute-start | bytes 1179656 | tf_op jit(solution)/shard_map/ppermute | solution.py:26
  144.7 11.3 %collective-permute-start.22 = (bf16[3,128,512]{2,1,0:T(8,128)(2,1)S(1)}, bf16[3,128,512]{2,1,0:T(8,128)(2,1)S(1)}, u32[]{:S(2)}, u32[]{:S(2)}) collective-permute-start(bf16[3,128,512]{2,1,0:T(8,128)(2,1)S(1)} %get-tuple-element.64), channel_id=1, source_target_pairs={{0,1},{1,0},{2,3},{3,2},{4,5},{5,4},{6,7},{7,6},{8,9},{9,8},{10,11... | collective-permute-start | bytes 1179656 | tf_op jit(solution)/shard_map/ppermute | solution.py:26
  145.7 10.8 %collective-permute-start.23 = (bf16[3,128,512]{2,1,0:T(8,128)(2,1)S(1)}, bf16[3,128,512]{2,1,0:T(8,128)(2,1)S(1)}, u32[]{:S(2)}, u32[]{:S(2)}) collective-permute-start(bf16[3,128,512]{2,1,0:T(8,128)(2,1)S(1)} %get-tuple-element.65), channel_id=1, source_target_pairs={{0,4},{2,6},{4,0},{6,2},{1,5},{3,7},{5,1},{7,3},{8,12},{10,14},{12... | collective-permute-start | bytes 1179656 | tf_op jit(solution)/shard_map/ppermute | solution.py:26
  145.7 8.8 %collective-permute-start.18 = (bf16[128,1024]{1,0:T(8,128)(2,1)S(1)}, bf16[128,1024]{1,0:T(8,128)(2,1)S(1)}, u32[]{:S(2)}, u32[]{:S(2)}) collective-permute-start(bf16[128,1024]{1,0:T(8,128)(2,1)S(1)} %get-tuple-element.57.refs_8_), channel_id=1, source_target_pairs={{0,8},{8,16},{16,24},{24,0},{1,9},{9,17},{17,25},{25,1},{2,10},{10... | collective-permute-start | bytes 786440 | tf_op jit(solution)/shard_map/ppermute | solution.py:21
  149.6 10.8 %collective-permute-start.21 = (bf16[128,1024]{1,0:T(8,128)(2,1)S(1)}, bf16[128,1024]{1,0:T(8,128)(2,1)S(1)}, u32[]{:S(2)}, u32[]{:S(2)}) collective-permute-start(bf16[128,1024]{1,0:T(8,128)(2,1)S(1)} %get-tuple-element.63.refs_8_), channel_id=1, source_target_pairs={{0,8},{8,16},{16,24},{24,0},{1,9},{9,17},{17,25},{25,1},{2,10},{10... | collective-permute-start | bytes 786440 | tf_op jit(solution)/shard_map/ppermute | solution.py:21
  151.2 8.2 %collective-permute-start.25 = (bf16[1,128,512]{2,1,0:T(8,128)(2,1)S(1)}, bf16[1,128,512]{2,1,0:T(8,128)(2,1)S(1)}, u32[]{:S(2)}, u32[]{:S(2)}) collective-permute-start(bf16[1,128,512]{2,1,0:T(8,128)(2,1)S(1)} %get-tuple-element.71), channel_id=1, source_target_pairs={{0,1},{1,0},{2,3},{3,2},{4,5},{5,4},{6,7},{7,6},{8,9},{9,8},{10,11... | collective-permute-start | bytes 393224 | tf_op jit(solution)/shard_map/ppermute | solution.py:26
  154.5 5.8 %collective-permute-start.26 = (bf16[1,128,512]{2,1,0:T(8,128)(2,1)S(1)}, bf16[1,128,512]{2,1,0:T(8,128)(2,1)S(1)}, u32[]{:S(2)}, u32[]{:S(2)}) collective-permute-start(bf16[1,128,512]{2,1,0:T(8,128)(2,1)S(1)} %get-tuple-element.72), channel_id=1, source_target_pairs={{0,4},{2,6},{4,0},{6,2},{1,5},{3,7},{5,1},{7,3},{8,12},{10,14},{12... | collective-permute-start | bytes 393224 | tf_op jit(solution)/shard_map/ppermute | solution.py:26
  156.8 11.1 %collective-permute-start.24 = (bf16[128,1024]{1,0:T(8,128)(2,1)S(1)}, bf16[128,1024]{1,0:T(8,128)(2,1)S(1)}, u32[]{:S(2)}, u32[]{:S(2)}) collective-permute-start(bf16[128,1024]{1,0:T(8,128)(2,1)S(1)} %get-tuple-element.70.refs_6_), channel_id=1, source_target_pairs={{0,8},{8,16},{16,24},{24,0},{1,9},{9,17},{17,25},{25,1},{2,10},{10... | collective-permute-start | bytes 786440 | tf_op jit(solution)/shard_map/ppermute | solution.py:21
  158.4 5.0 %collective-permute-start.28 = (bf16[1,128,512]{2,1,0:T(8,128)(2,1)S(1)}, bf16[1,128,512]{2,1,0:T(8,128)(2,1)S(1)}, u32[]{:S(2)}, u32[]{:S(2)}) collective-permute-start(bf16[1,128,512]{2,1,0:T(8,128)(2,1)S(1)} %get-tuple-element.75), channel_id=1, source_target_pairs={{0,1},{1,0},{2,3},{3,2},{4,5},{5,4},{6,7},{7,6},{8,9},{9,8},{10,11... | collective-permute-start | bytes 393224 | tf_op jit(solution)/shard_map/ppermute | solution.py:26
  159.4 5.0 %collective-permute-start.29 = (bf16[1,128,512]{2,1,0:T(8,128)(2,1)S(1)}, bf16[1,128,512]{2,1,0:T(8,128)(2,1)S(1)}, u32[]{:S(2)}, u32[]{:S(2)}) collective-permute-start(bf16[1,128,512]{2,1,0:T(8,128)(2,1)S(1)} %get-tuple-element.76), channel_id=1, source_target_pairs={{0,4},{2,6},{4,0},{6,2},{1,5},{3,7},{5,1},{7,3},{8,12},{10,14},{12... | collective-permute-start | bytes 393224 | tf_op jit(solution)/shard_map/ppermute | solution.py:26
  160.4 11.5 %collective-permute-start.27 = (bf16[128,1024]{1,0:T(8,128)(2,1)S(1)}, bf16[128,1024]{1,0:T(8,128)(2,1)S(1)}, u32[]{:S(2)}, u32[]{:S(2)}) collective-permute-start(bf16[128,1024]{1,0:T(8,128)(2,1)S(1)} %sum_stage.16.refs_6_), channel_id=1, source_target_pairs={{0,8},{8,16},{16,24},{24,0},{1,9},{9,17},{17,25},{25,1},{2,10},{10... | collective-permute-start | bytes 786440 | tf_op jit(solution)/shard_map/ppermute | solution.py:21
  164.4 10.3 %collective-permute-start.30 = (bf16[128,1024]{1,0:T(8,128)(2,1)S(1)}, bf16[128,1024]{1,0:T(8,128)(2,1)S(1)}, u32[]{:S(2)}, u32[]{:S(2)}) collective-permute-start(bf16[128,1024]{1,0:T(8,128)(2,1)S(1)} %sum_stage.17), channel_id=1, source_target_pairs={{0,8},{8,16},{16,24},{24,0},{1,9},{9,17},{17,25},{25,1},{2,10},{10... | collective-permute-start | bytes 786440 | tf_op jit(solution)/shard_map/ppermute | solution.py:21
  174.7 1.1 copy-start.13

commit v7 on v6

--- a/solution.py
+++ b/solution.py
@@ -68,10 +68,11 @@
         input_output_aliases={0: 0},
         name="after",
         cost_estimate=SHORT,
+        compiler_params=pltpu.CompilerParams(vmem_limit_bytes=MIB),
     )(value, *earlier)
 
 
-def project_kernel(*refs, halves):
+def project_kernel(*refs, halves, carried):
     weights_ref, out_ref, total_ref = refs[sum(halves)], refs[-2], refs[-1]
     step, steps = pl.program_id(0), pl.num_programs(0)
     weights = jnp.concatenate([weights_ref[0], weights_ref[1], weights_ref[2]], axis=1)
@@ -100,28 +101,34 @@
     @pl.when(step == steps - 1)
     def _():
         width = weights_ref.shape[2]
+        if carried:
+            out_ref[:carried, :] = refs[sum(halves) + 1][...]
         for head in range(2 * width // HD):
             columns = slice(head * HD, (head + 1) * HD)
             values = total_ref[:, columns]
             scale = lax.rsqrt(jnp.mean(values * values, axis=-1, keepdims=True) + 1e-06)
-            out_ref[:, columns] = (values * scale).astype(jnp.bfloat16)
-        out_ref[:, 2 * width :] = total_ref[:, 2 * width :].astype(jnp.bfloat16)
-
-
-def project(blocks, weights, earlier):
+            out_ref[carried:, columns] = (values * scale).astype(jnp.bfloat16)
+        out_ref[carried:, 2 * width :] = total_ref[:, 2 * width :].astype(jnp.bfloat16)
+
+
+def project(blocks, weights, held, earlier):
     _, depth, width = weights.shape
     rows = blocks[0][0].shape[0]
     steps = 4
     block = depth // steps
     count = len(blocks) * rows
+    carried = sum(array.shape[0] for array in held)
     return pl.pallas_call(
-        functools.partial(project_kernel, halves=[len(parts) for parts in blocks]),
+        functools.partial(
+            project_kernel, halves=[len(parts) for parts in blocks], carried=carried
+        ),
         grid=(steps,),
         in_specs=[pl.BlockSpec(memory_space=pltpu.VMEM)] * sum(len(parts) for parts in blocks)
         + [pl.BlockSpec((3, block, width), lambda k: (0, k, 0))]
+        + [pl.BlockSpec(memory_space=pltpu.VMEM)] * len(held)
         + [pl.BlockSpec(memory_space=pl.ANY)] * len(earlier),
-        out_specs=pl.BlockSpec((count, 3 * width), lambda k: (0, 0)),
-        out_shape=jax.ShapeDtypeStruct((count, 3 * width), jnp.bfloat16),
+        out_specs=pl.BlockSpec((carried + count, 3 * width), lambda k: (0, 0)),
+        out_shape=jax.ShapeDtypeStruct((carried + count, 3 * width), jnp.bfloat16),
         scratch_shapes=[pltpu.VMEM((count, 3 * width), jnp.float32)],
         name="project_heads",
         cost_estimate=pl.CostEstimate(
@@ -129,13 +136,17 @@
             bytes_accessed=2 * (count * depth + weights.size),
             transcendentals=0,
         ),
-        compiler_params=pltpu.CompilerParams(vmem_limit_bytes=26 * MIB),
-    )(*[part for parts in blocks for part in parts], weights, *earlier)
-
-
-def attend_kernel(visible_ref, heads_ref, context_ref, *refs, first_block):
-    out_ref = refs[-1]
-    width = out_ref.shape[1]
+        compiler_params=pltpu.CompilerParams(vmem_limit_bytes=44 * MIB),
+    )(*[part for parts in blocks for part in parts], weights, *held, *earlier)
+
+
+def place_of(core, across):
+    return jnp.where(across == 3, 6 + core, 3 * core + across)
+
+
+def attend_blocks(visible_ref, heads_ref, context_ref, out_ref, first_block, first_head):
+    width = heads_ref.shape[1] // 3
+    held = context_ref.shape[1] // 2
     tiles_seen = visible_ref.shape[1]
     tiles_fresh = visible_ref.shape[0]
     mine_high, mine_low = lax.axis_index("sp") // 2, lax.axis_index("sp") % 2
@@ -145,14 +156,15 @@
         index = first_block + step
         high, low = mine_high ^ ((index // 2) % 2), mine_low ^ (index // 4)
         tile, branch = high * 2 + low, mine_branch ^ (index % 2)
-        rows = pl.ds(pl.multiple_of(index * TILE, TILE), TILE)
+        place = place_of(index // 4, index % 4)
+        rows = pl.ds(pl.multiple_of(place * TILE, TILE), TILE)
         out_rows = pl.ds(pl.multiple_of(step * TILE, TILE), TILE)
         places = []
         for seen in range(tiles_seen):
             number = visible_ref[tile, seen]
             older = jnp.maximum(number - tiles_fresh, 0)
-            fresh = (mine_low ^ (number % 2)) * 4 + (mine_high ^ ((number // 2) % 2)) * 2
-            fresh = (fresh + index % 2) * TILE
+            across = (mine_high ^ ((number // 2) % 2)) * 2 + index % 2
+            fresh = place_of(mine_low ^ (number % 2), across) * TILE
             stale = ((older // 2) * 2 + branch) * 2 * TILE + (older % 2) * TILE
             places.append(
                 (
@@ -163,20 +175,22 @@
             )
 
         def tiles(kind, head):
-            fresh_columns = slice(kind * width + head * HD, kind * width + (head + 1) * HD)
-            start = (kind - 1) * width + head * HD
+            start = kind * width + (first_head + head) * HD
+            held_start = (kind - 1) * held + head * HD
             return jnp.concatenate(
                 [
                     jnp.where(
-                        is_fresh, heads_ref[fresh, fresh_columns], context_ref[stale, start : start + HD]
+                        is_fresh,
+                        heads_ref[fresh, start : start + HD],
+                        context_ref[stale, held_start : held_start + HD],
                     )
                     for is_fresh, fresh, stale in places
                 ],
                 axis=0,
             )
 
-        for head in range(width // HD):
-            columns = slice(head * HD, (head + 1) * HD)
+        for head in range(held // HD):
+            columns = slice((first_head + head) * HD, (first_head + head + 1) * HD)
             scores = lax.dot_general(
                 heads_ref[rows, columns],
                 tiles(1, head),
@@ -188,45 +202,74 @@
             mixed = jnp.dot(
                 exponent.astype(jnp.bfloat16), tiles(2, head), preferred_element_type=jnp.float32
             )
-            out_ref[out_rows, columns] = (mixed / total).astype(jnp.bfloat16)
+            out_ref[out_rows, head * HD : (head + 1) * HD] = (mixed / total).astype(jnp.bfloat16)
         return carry
 
     lax.fori_loop(0, out_ref.shape[0] // TILE, body, 0)
 
 
-def attend(heads, context, visible, first_block, earlier):
-    count = heads.shape[0] // 2
-    width = heads.shape[1] // 3
+def attend_cost(heads, context, visible, count):
+    keys = visible.shape[1] * TILE
+    return pl.CostEstimate(
+        flops=2 * count * keys * context.shape[1],
+        bytes_accessed=2 * (heads.size + context.size),
+        transcendentals=count * keys * context.shape[1] // (2 * HD),
+    )
+
+
+def attend_first_kernel(visible_ref, heads_ref, context_ref, kept_ref, sent_ref):
+    attend_blocks(visible_ref, heads_ref, context_ref, sent_ref, kept_ref.shape[0] // TILE, 0)
+    attend_blocks(visible_ref, heads_ref, context_ref, kept_ref, 0, 0)
+
+
+def attend_first(heads, context, visible):
+    count, width = heads.shape[0], context.shape[1] // 2
     return pl.pallas_call(
-        functools.partial(attend_kernel, first_block=first_block),
-        in_specs=[
-            pl.BlockSpec(memory_space=pltpu.SMEM),
-            pl.BlockSpec(memory_space=pltpu.VMEM),
-            pl.BlockSpec(memory_space=pltpu.VMEM),
-        ]
+        attend_first_kernel,
+        in_specs=[pl.BlockSpec(memory_space=pltpu.SMEM)]
+        + [pl.BlockSpec(memory_space=pltpu.VMEM)] * 2,
+        out_shape=[jax.ShapeDtypeStruct((count // 2, width), jnp.bfloat16)] * 2,
+        name="attend_first",
+        cost_estimate=attend_cost(heads, context, visible, count),
+        compiler_params=pltpu.CompilerParams(vmem_limit_bytes=12 * MIB),
+    )(visible, heads, context)
+
+
+def attend_last_kernel(visible_ref, heads_ref, context_ref, *refs, first_block, first_head):
+    attend_blocks(visible_ref, heads_ref, context_ref, refs[-1], first_block, first_head)
+
+
+def attend_last(heads, context, visible, first_block, first_head, earlier):
+    count, width = heads.shape[0], context.shape[1] // 2
+    return pl.pallas_call(
+        functools.partial(
+            attend_last_kernel, first_block=first_block, first_head=first_head
+        ),
+        in_specs=[pl.BlockSpec(memory_space=pltpu.SMEM)]
+        + [pl.BlockSpec(memory_space=pltpu.VMEM)] * 2
         + [pl.BlockSpec(memory_space=pl.ANY)] * len(earlier),
-        out_shape=jax.ShapeDtypeStruct((count, width), jnp.bfloat16),
-        name="attend",
-        cost_estimate=pl.CostEstimate(
-            flops=4 * count * visible.shape[1] * TILE * width,
-            bytes_accessed=2 * (heads.size + context.size),
-            transcendentals=count * visible.shape[1] * TILE * width // HD,
-        ),
-        compiler_params=pltpu.CompilerParams(vmem_limit_bytes=16 * MIB),
+        out_shape=jax.ShapeDtypeStruct((count // 2, width), jnp.bfloat16),
+        name="attend_last",
+        cost_estimate=attend_cost(heads, context, visible, count // 2),
+        compiler_params=pltpu.CompilerParams(vmem_limit_bytes=12 * MIB),
     )(visible, heads, context, *earlier)
 
 
 def half_kernel(rows_ref, *refs, start):
-    out_ref = refs[-1]
-    out_ref[...] = rows_ref[:, start : start + out_ref.shape[1]]
+    half_ref, whole_ref = refs[-2:]
+    half_ref[...] = rows_ref[:, start : start + half_ref.shape[1]]
+    whole_ref[...] = rows_ref[...]
 
 
 def half_of(rows, start, earlier):
+    count, columns = rows.shape
     return pl.pallas_call(
         functools.partial(half_kernel, start=start),
         in_specs=[pl.BlockSpec(memory_space=pltpu.VMEM)]
         + [pl.BlockSpec(memory_space=pl.ANY)] * len(earlier),
-        out_shape=jax.ShapeDtypeStruct((rows.shape[0], rows.shape[1] // 2), rows.dtype),
+        out_shape=[
+            jax.ShapeDtypeStruct((count, width), rows.dtype) for width in (columns // 2, columns)
+        ],
         name="half_of",
         cost_estimate=SHORT,
         compiler_params=pltpu.CompilerParams(vmem_limit_bytes=8 * MIB),
@@ -247,19 +290,16 @@
 
 
 def begin(start, refs, across_out, along_out, first_kept, second_kept):
-    attended_ref, core_attended_ref, weights_ref, core_weights_ref, rows_ref, gates_ref = refs
+    *attended_refs, weights_ref, core_weights_ref, rows_ref, gates_ref = refs
     tokens, half = rows_ref.shape[0], first_kept.shape[2]
+    attended = jnp.concatenate([ref[...] for ref in attended_refs], axis=1)
 
     def product_of(columns):
-        near = jnp.dot(
-            attended_ref[...], weights_ref[:, columns], preferred_element_type=jnp.float32
-        )
-        return near + jnp.dot(
-            core_attended_ref[...], core_weights_ref[:, columns], preferred_element_type=jnp.float32
-        )
+        weights = jnp.concatenate([weights_ref[:, columns], core_weights_ref[:, columns]], axis=0)
+        return jnp.dot(attended, weights, preferred_element_type=jnp.float32)
 
     columns = slice(start, start + half)
-    product = product_of(columns)
+    product = product_of(slice(0, half))
     for tile in range(2):
         own = product[2 * tile * tokens : (2 * tile + 1) * tokens]
         other = product[(2 * tile + 1) * tokens : (2 * tile + 2) * tokens]
@@ -267,8 +307,7 @@
         sent, kept = combined(own, other, mine, gates_ref, columns)
         across_out[tile] = sent.astype(jnp.bfloat16)
         first_kept[tile] = kept
-    columns = slice(start + half, start + 2 * half)
-    product = product_of(columns)
+    product = product_of(slice(half, 2 * half))
     for branch in range(2):
         second_kept[branch] = product[branch * tokens : (branch + 1) * tokens]
         along_out[branch] = product[(branch + 2) * tokens : (branch + 3) * tokens].astype(
@@ -284,7 +323,14 @@
             [
                 named[name]
                 for name in (
-                    "attended", "core_attended", "weights", "core_weights", "rows", "gates"
+                    "near_first",
+                    "near_last",
+                    "far_first",
+                    "far_last",
+                    "weights",
+                    "core_weights",
+                    "rows",
+                    "gates",
                 )
             ],
             named["across_out"],
@@ -350,8 +396,15 @@
             middle=middle,
             final=final,
         ),
-        in_specs=[pl.BlockSpec(memory_space=pltpu.VMEM)] * len(operands)
+        grid=(1,),
+        in_specs=[
+            pl.BlockSpec((array.shape[0], chunk), lambda step: (0, next_start // chunk))
+            if name in ("weights", "core_weights")
+            else pl.BlockSpec(memory_space=pltpu.VMEM)
+            for name, array in operands.items()
+        ]
         + [pl.BlockSpec(memory_space=pl.ANY)] * len(earlier),
+        out_specs=[pl.BlockSpec(memory_space=pltpu.VMEM)] * len(outs),
         out_shape=list(outs.values()),
         name="sum_stage",
         cost_estimate=SHORT,
@@ -368,36 +421,48 @@
 
     context_rows = stale_cache.shape[2]
     width = project_in.shape[3]
-    packed = stale_cache[0, 0].reshape(context_rows, 2, devices, width)
-    packed = packed.transpose(2, 0, 1, 3).reshape(devices, context_rows, 2 * width)
+    split = (width // HD - 1) * HD
+    by_device = stale_cache[0, 0].reshape(context_rows, 2, devices, width).transpose(2, 0, 1, 3)
+    packed, packed_last = [
+        part.reshape(devices, context_rows, -1)
+        for part in (by_device[..., :split], by_device[..., split:])
+    ]
 
     own = modulated_norm(current, modulate)
     across = from_partner(own, "cfg", 1)
     along = from_partner(own, "sp", 2)
     own_core = from_partner(own, "sp", 1)
     middle = features // 2
-    gate = modulate[2:3]
-    other_gate = from_partner(gate, "cfg", 1)
-    halves = half_of(across, 0, (packed,)), half_of(along, middle, (packed,))
-    first = from_partner(halves[0], "sp", 2)
-    second = from_partner(halves[1], "cfg", 1)
-    gates = jnp.concatenate([gate, other_gate], axis=0)
+    first_half, across = half_of(across, 0, (packed,))
+    second_half, along = half_of(along, middle, (packed,))
+    first = from_partner(first_half, "sp", 2)
+    second = from_partner(second_half, "cfg", 1)
     core_weights = from_partner(project_out[0], "sp", 1)
     near = [(own,), (across,), (along,), (first, second)]
     far = [(own_core,)] + [
         tuple(from_partner(part, "sp", 1) for part in parts) for parts in near[1:]
     ]
 
-    packed = after(packed, (first, second, other_gate))
-    context = lax.all_to_all(packed, ("sp", "cfg"), split_axis=0, concat_axis=0, tiled=True)
-    context = context.reshape(devices * context_rows, 2 * width)
-
-    heads = project(near + far, project_in[0], (core_weights,))
-    for_core = attend(heads, context, visible[0], 4, ())
-    core_attended = from_partner(for_core, "sp", 1)
-    attended = attend(heads, context, visible[0], 0, (for_core,))
-
-    weights = project_out[0]
+    def exchange(part):
+        context = lax.all_to_all(part, ("sp", "cfg"), split_axis=0, concat_axis=0, tiled=True)
+        return context.reshape(devices * context_rows, -1)
+
+    context = exchange(packed)
+    heads = project(near[:3] + far[:3], project_in[0], (), ())
+    packed_last = after(packed_last, (context, heads))
+    context_last = exchange(packed_last)
+    heads = project([near[3], far[3]], project_in[0], (heads,), (packed_last,))
+    near_first, for_core = attend_first(heads, context, visible[0])
+    far_first = from_partner(for_core, "sp", 1)
+    gate = modulate[2:3]
+    gates = jnp.concatenate([gate, from_partner(after(gate, (for_core,)), "cfg", 1)], axis=0)
+    for_core = attend_last(heads, context_last, visible[0], 4, split // HD, (near_first,))
+    far_last = from_partner(for_core, "sp", 1)
+    near_last = attend_last(heads, context_last, visible[0], 0, split // HD, (for_core,))
+    attended = dict(
+        near_first=near_first, near_last=near_last, far_first=far_first, far_last=far_last
+    )
+
     count = COLUMN_CHUNKS
     chunk = features // count
     kept, left, flights, arrivals, earlier = {}, {}, {}, [], []
@@ -405,8 +470,7 @@
         fresh, middle, final = index + 2 < count, 0 <= index < count, index >= 2
         operands = {"rows": current, "gates": gates}
         if fresh:
-            operands["attended"], operands["core_attended"] = attended, core_attended
-            operands["weights"], operands["core_weights"] = weights, core_weights
+            operands.update(attended, weights=project_out[0], core_weights=core_weights)
         if index >= 0:
             operands["across"], operands["along"] = flights.pop(index)
         if middle:

time: 177 us -> 201 us (1.14)
  starting transfers between devices: 34.8 us -> 46.4 us
  local copies, waits for them, and re-layouts: 31.9 us -> 38.9 us
  Pallas kernels: 53.1 us -> 56.4 us
  waiting for transfers between devices: 55.6 us -> 57.7 us
    slice x0 -> x2, local copies, waits for them, and re-layouts: none -> 7.31 us  [the longest x1 4.38 us: per_device(): by_device[..., :split]]
    ppermute x26 -> x27, starting transfers between devices: 23.3 us -> 29.9 us  [from_partner(): return lax.ppermute(value, axis, pairs)]
    pallas_call x9, Pallas kernels: 18.3 us -> 13.3 us  [stage(): pl.pallas_call(functools.partial(stage_kernel, parts=parts, start=start,...]
    pallas_call x1 -> x2, Pallas kernels: 20.6 us -> 25.2 us  [project(): pl.pallas_call(functools.partial(project_kernel, halves=[len(parts) for p...]
    all_to_all x1 -> x2, starting transfers between devices: 3.83 us -> 8.49 us  [exchange(): lax.all_to_all(part, ('sp', 'cfg'), split_axis=0, concat_axis=0, tiled=True)]
    pallas_call x2 -> x3, Pallas kernels: 8.11 us -> 11.7 us  [the longest x2 6.19 us: attend_last(): pl.pallas_call(functools.partial(attend_last_kernel, first_block=first_bl...]
    ppermute x26 -> x27, waiting for transfers between devices: 42.4 us -> 45.8 us  [from_partner(): return lax.ppermute(value, axis, pairs)]
    unnamed x33 -> x28, local copies, waits for them, and re-layouts: 13.3 us -> 9.92 us
  transfers between devices with their start and end apart: 32 -> 34, of which waited for: 20 -> 15; matrix products, arithmetic and copies ran while one was open for 11% -> 15% of each run, Pallas kernels for 24% -> 26%
where the time goes in v7:
time: 201 us; the launch traced here: 200 us
  waiting for transfers between devices  57.7 us (29%)
  Pallas kernels  56.4 us (28%)
  starting transfers between devices  46.4 us (23%)
  local copies, waits for them, and re-layouts  38.9 us (19%)
    ppermute x27, waiting for transfers between devices, from_partner(): return lax.ppermute(value, axis, pairs)  45.8 us
    ppermute x27, starting transfers between devices, from_partner(): return lax.ppermute(value, axis, pairs)  29.9 us
    pallas_call x2, Pallas kernels, project(): pl.pallas_call(functools.partial(project_kernel, halves=[len(parts) for p...  25.2 us
    another operation x2, local copies, waits for them, and re-layouts, per_device(): stale_cache[0, 0].reshape(context_rows, 2, devices, width)  14 us
    pallas_call x9, Pallas kernels, stage(): pl.pallas_call(functools.partial(stage_kernel, parts=parts, start=start,...  13.3 us
    ppermute x5, waiting for transfers between devices, from_behind(): return lax.ppermute(x, axis, [(i, (i + by) % count) for i in range(count)])  11.9 us
    unnamed x28, local copies, waits for them, and re-layouts  9.92 us
    all_to_all x2, starting transfers between devices, exchange(): lax.all_to_all(part, ('sp', 'cfg'), split_axis=0, concat_axis=0, tiled=True)  8.49 us
  transfers between devices with their start and end apart: 34, of which 15 were waited for; matrix products, arithmetic and copies ran while one was open for 15% of the time, Pallas kernels for 26%

profile of v7, /device:TPU:0, one launch (start us, length us, event | category | flops | bytes accessed | tf_op | source)
XLA Modules:
  0.0 199.7 jit_solution(10839583671938706672)
XLA Ops:
  0.0 0.8 copy.14
  0.9 1.3 copy-done
  2.2 2.5 %modulated_norm.1.refs_0_ = bf16[128,5120]{1,0:T(8,128)(2,1)S(1)} custom-call(bf16[128,5120]{1,0:T(8,128)(2,1)S(1)} %bitcast.15, f32[3,5120]{1,0:T(4,128)S(1)} %bitcast.27), custom_call_target="tpu_custom_call" | custom-call | flops 6553600 | bytes 2621440 | tf_op jit(solution)/shard_map/modulated_norm/pallas_call | solution.py:47
  4.6 3.0 %collective-permute-start.2 = (bf16[128,5120]{1,0:T(8,128)(2,1)S(1)}, bf16[128,5120]{1,0:T(8,128)(2,1)}, u32[]{:S(2)}, u32[]{:S(2)}) collective-permute-start(bf16[128,5120]{1,0:T(8,128)(2,1)S(1)} %modulated_norm.1.refs_0_), channel_id=1, source_target_pairs={{0,4},{2,6},{4,0},{6,2},{1,5},{3,7},{5,1},{7,3},{8,12},{10,14},{12... | collective-permute-start | bytes 3932168 | tf_op jit(solution)/shard_map/ppermute | solution.py:26
  7.7 1.5 collective-permute-start
  9.2 8.0 %reshape_squeeze.3 = bf16[256,2,8,384]{3,2,1,0:T(8,128)(2,1)} reshape(bf16[1,1,256,2,3072]{4,3,2,1,0:T(2,128)(2,1)} %param.10) | data formatting | bytes 6291456 | tf_op jit(solution)/shard_map/reshape;squeeze | solution.py:425
  17.2 6.0 %copy.13 = bf16[256,2,8,384]{3,1,0,2:T(2,128)(2,1)} copy(bf16[256,2,8,384]{3,2,1,0:T(8,128)(2,1)} %reshape_squeeze.3) | data formatting | bytes 6291456 | tf_op jit(solution)/shard_map/reshape;squeeze | solution.py:425
  23.1 4.4 %slice.16 = bf16[8,256,2,256]{3,2,1,0:T(2,128)(2,1)} slice(bf16[8,256,2,384]{3,2,1,0:T(2,128)(2,1)} %bitcast.13), slice={[0:8], [0:256], [0:2], [0:256]} | slice | bytes 4194304 | tf_op jit(solution)/shard_map/slice | solution.py:428
  27.5 4.4 %reshape.13.refs_0_ = bf16[8,256,512]{2,1,0:T(8,128)(2,1)} reshape(bf16[8,256,2,256]{3,2,1,0:T(2,128)(2,1)} %slice.16) | data formatting | bytes 4194304 | tf_op jit(solution)/shard_map/reshape | solution.py:427
  31.9 4.6 %collective-permute-done.2.rows_ref = bf16[128,5120]{1,0:T(8,128)(2,1)} collective-permute-done((bf16[128,5120]{1,0:T(8,128)(2,1)S(1)}, bf16[128,5120]{1,0:T(8,128)(2,1)}, u32[]{:S(2)}, u32[]{:S(2)}) %collective-permute-start.2) | collective-permute-done | bytes 1310752 | tf_op jit(solution)/shard_map/ppermute | solution.py:26
  36.5 2.5 %half_of.3 = (bf16[128,2560]{1,0:T(8,128)(2,1)S(1)}, bf16[128,5120]{1,0:T(8,128)(2,1)}) custom-call(bf16[128,5120]{1,0:T(8,128)(2,1)} %collective-permute-done.2.rows_ref, bf16[8,256,512]{2,1,0:T(8,128)(2,1)} %reshape.13.refs_0_), custom_call_target="tpu_custom_call" | custom-call | flops 1 | bytes 1 | tf_op jit(solution)/shard_map/half_of/pallas_call | solution.py:266
  39.1 0.9 copy-done.8
  39.9 1.2 half_of.2
  41.1 0.9 copy-done.9
  42.5 4.1 %all-to-all-start = ((bf16[8,256,512]{2,1,0:T(8,128)(2,1)}), bf16[8,256,512]{2,1,0:T(8,128)(2,1)S(1)}, u32[]{:S(2)}, u32[]{:S(2)}) async-start(bf16[8,256,512]{2,1,0:T(8,128)(2,1)} %reshape.13.refs_0_), calls=%async_computation | async-start | bytes 4194304 | tf_op jit(solution)/shard_map/all_to_all | solution.py:447
  46.5 2.0 %collective-permute-start.3 = (bf16[128,2560]{1,0:T(8,128)(2,1)}, bf16[128,2560]{1,0:T(8,128)(2,1)}, u32[]{:S(2)}, u32[]{:S(2)}) collective-permute-start(bf16[128,2560]{1,0:T(8,128)(2,1)} %copy-done.8), channel_id=1, source_target_pairs={{0,1},{1,0},{2,3},{3,2},{4,5},{5,4},{6,7},{7,6},{8,9},{9,8},{10,11... | collective-permute-start | bytes 1966088 | tf_op jit(solution)/shard_map/ppermute | solution.py:26
  48.5 1.5 collective-permute-start.1
  50.0 2.9 %slice.17 = bf16[8,256,2,128]{3,2,1,0:T(2,128)(2,1)} slice(bf16[8,256,2,384]{3,2,1,0:T(2,128)(2,1)} %bitcast.13), slice={[0:8], [0:256], [0:2], [256:384]} | slice | bytes 2097152 | tf_op jit(solution)/shard_map/slice | solution.py:428
  52.9 2.5 %reshape.14.value_ref = bf16[8,256,256]{2,1,0:T(8,128)(2,1)} reshape(bf16[8,256,2,128]{3,2,1,0:T(2,128)(2,1)} %slice.17) | data formatting | bytes 2097152 | tf_op jit(solution)/shard_map/reshape | solution.py:427
  55.4 31.0 %collective-permute-done.3.refs_1_ = bf16[128,2560]{1,0:T(8,128)(2,1)} collective-permute-done((bf16[128,2560]{1,0:T(8,128)(2,1)}, bf16[128,2560]{1,0:T(8,128)(2,1)}, u32[]{:S(2)}, u32[]{:S(2)}) %collective-permute-start.3) | collective-permute-done | bytes 655392 | tf_op jit(solution)/shard_map/ppermute | solution.py:26
  86.9 16.7 %project_heads.2.refs_1_.refs_5_ = bf16[768,1152]{1,0:T(8,128)(2,1)S(1)} custom-call(bf16[128,5120]{1,0:T(8,128)(2,1)S(1)} %modulated_norm.1.refs_0_, bf16[128,5120]{1,0:T(8,128)(2,1)} %get-tuple-element.50.refs_1_, bf16[128,5120]{1,0:T(8,128)(2,1)} %get-tuple-element.51.refs_2_, bf16[128,5120]{1,0:T(8,128)(2,1)} %collective-permute-done.6.refs_3_, ...), custom_call_target="tpu_custom_call" | custom-call | flops 9059696640 | bytes 19660800 | tf_op jit(solution)/shard_map/project_heads/pallas_call | solution.py:121
  103.6 1.2 copy-done.4
  104.8 2.2 %copy-done.5 = bf16[768,1152]{1,0:T(8,128)(2,1)S(1)} copy-done((bf16[768,1152]{1,0:T(8,128)(2,1)S(1)}, bf16[768,1152]{1,0:T(8,128)(2,1)}, u32[]{:S(2)}) %copy-start.5) | copy-done | bytes 1769496
  107.1 4.4 %all-to-all-start.1 = ((bf16[8,256,256]{2,1,0:T(8,128)(2,1)}), bf16[8,256,256]{2,1,0:T(8,128)(2,1)}, u32[]{:S(2)}, u32[]{:S(2)}) async-start(bf16[8,256,256]{2,1,0:T(8,128)(2,1)} %after.2.refs_6_), calls=%async_computation.1 | async-start | bytes 2097152 | tf_op jit(solution)/shard_map/all_to_all | solution.py:447
  111.5 0.7 slice_bitcast_fusion
  112.3 1.5 copy-done.6
  113.8 8.5 %project_heads.3.heads_ref = bf16[1024,1152]{1,0:T(8,128)(2,1)S(1)} custom-call(bf16[128,2560]{1,0:T(8,128)(2,1)} %collective-permute-done.1.refs_0_, bf16[128,2560]{1,0:T(8,128)(2,1)} %collective-permute-done.3.refs_1_, bf16[128,2560]{1,0:T(8,128)(2,1)} %collective-permute-done.4.refs_2_, bf16[128,2560]{1,0:T(8,128)(2,1)} %collective-permute-done.5.refs_3_, ...), custom_call_target="tpu_custom_call" | custom-call | flops 3019898880 | bytes 14417920 | tf_op jit(solution)/shard_map/project_heads/pallas_call | solution.py:121
  122.3 5.5 %attend_first.1 = (bf16[512,256]{1,0:T(8,128)(2,1)S(1)}, bf16[512,256]{1,0:T(8,128)(2,1)S(1)}) custom-call(s32[4,6]{1,0:T(4,128)S(1)} %bitcast.28, bf16[1024,1152]{1,0:T(8,128)(2,1)S(1)} %project_heads.3.heads_ref, bf16[2048,512]{1,0:T(8,128)(2,1)S(1)} %bitcast.26), custom_call_target="tpu_custom_call" | custom-call | flops 805306368 | bytes 4456448 | tf_op jit(solution)/shard_map/attend_first/pallas_call | solution.py:227
  127.9 1.8 collective-permute-start.9
  129.6 3.0 %attend_last.2.refs_0_ = bf16[512,128]{1,0:T(8,128)(2,1)S(1)} custom-call(s32[4,6]{1,0:T(4,128)S(1)} %bitcast.29, bf16[1024,1152]{1,0:T(8,128)(2,1)S(1)} %project_heads.3.heads_ref, bf16[2048,256]{1,0:T(8,128)(2,1)} %bitcast.6.context_ref, bf16[512,256]{1,0:T(8,128)(2,1)S(1)} %get-tuple-element.53.refs_0_.refs_2_), custom_call_target="tpu_custom_call" | custom-call | flops 201326592 | bytes 3407872 | tf_op jit(solution)/shard_map/attend_last/pallas_call | solution.py:244
  132.7 0.6 collective-permute-start.11
  133.3 3.1 %attend_last.3.refs_3_ = bf16[512,128]{1,0:T(8,128)(2,1)S(1)} custom-call(s32[4,6]{1,0:T(4,128)S(1)} %bitcast.30, bf16[1024,1152]{1,0:T(8,128)(2,1)S(1)} %project_heads.3.heads_ref, bf16[2048,256]{1,0:T(8,128)(2,1)} %bitcast.6.context_ref, bf16[512,128]{1,0:T(8,128)(2,1)S(1)} %attend_last.2.refs_0_), custom_call_target="tpu_custom_call" | custom-call | flops 201326592 | bytes 3407872 | tf_op jit(solution)/shard_map/attend_last/pallas_call | solution.py:244
  136.5 2.4 %sum_stage.9 = (bf16[2,128,512]{2,1,0:T(8,128)(2,1)S(1)}, bf16[2,128,512]{2,1,0:T(8,128)(2,1)S(1)}, f32[2,128,512]{2,1,0:T(8,128)S(1)}, f32[2,128,512]{2,1,0:T(8,128)S(1)}) custom-call(bf16[128,5120]{1,0:T(8,128)(2,1)S(1)} %bitcast.16, f32[2,5120]{1,0:T(2,128)S(1)} %pad_maximum_fusion.refs_1_, bf16[512,256]{1,0:T(8,128)(2,1)S(1)} %get-tuple-element.53.refs_0_.refs_2_, ...), custom_call_target="tpu_custom_call" | custom-call | flops 1 | bytes 1 | tf_op jit(solution)/shard_map/sum_stage/pallas_call | solution.py:389
  139.3 1.7 collective-permute-start.14
  141.1 2.4 %sum_stage.10 = (bf16[2,128,512]{2,1,0:T(8,128)(2,1)S(1)}, bf16[2,128,512]{2,1,0:T(8,128)(2,1)S(1)}, f32[2,128,512]{2,1,0:T(8,128)S(1)}, f32[2,128,512]{2,1,0:T(8,128)S(1)}) custom-call(bf16[128,5120]{1,0:T(8,128)(2,1)S(1)} %bitcast.17, f32[2,5120]{1,0:T(2,128)S(1)} %pad_maximum_fusion.refs_1_, bf16[512,256]{1,0:T(8,128)(2,1)S(1)} %get-tuple-element.53.refs_0_.refs_2_, ...), custom_call_target="tpu_custom_call" | custom-call | flops 1 | bytes 1 | tf_op jit(solution)/shard_map/sum_stage/pallas_call | solution.py:389
  143.5 1.5 collective-permute-start.17
  145.5 2.6 %collective-permute-done.13.refs_8_ = bf16[2,128,512]{2,1,0:T(8,128)(2,1)S(1)} collective-permute-done((bf16[2,128,512]{2,1,0:T(8,128)(2,1)S(1)}, bf16[2,128,512]{2,1,0:T(8,128)(2,1)S(1)}, u32[]{:S(2)}, u32[]{:S(2)}) %collective-permute-start.13) | collective-permute-done | bytes 262176 | tf_op jit(solution)/shard_map/ppermute | solution.py:26
  148.2 2.6 %sum_stage.11 = (bf16[3,128,512]{2,1,0:T(8,128)(2,1)S(1)}, bf16[3,128,512]{2,1,0:T(8,128)(2,1)S(1)}, f32[2,128,512]{2,1,0:T(8,128)S(1)}, f32[2,128,512]{2,1,0:T(...) custom-call(bf16[128,5120]{1,0:T(8,128)(2,1)S(1)} %bitcast.18, f32[2,5120]{1,0:T(2,128)S(1)} %pad_maximum_fusion.refs_1_, ...), custom_call_target="tpu_custom_call" | custom-call | flops 1 | bytes 1 | tf_op jit(solution)/shard_map/sum_stage/pallas_call | solution.py:389
  150.8 2.1 %collective-permute-start.15 = (bf16[3,128,512]{2,1,0:T(8,128)(2,1)S(1)}, bf16[3,128,512]{2,1,0:T(8,128)(2,1)S(1)}, u32[]{:S(2)}, u32[]{:S(2)}) collective-permute-start(bf16[3,128,512]{2,1,0:T(8,128)(2,1)S(1)} %get-tuple-element.59), channel_id=1, source_target_pairs={{0,1},{1,0},{2,3},{3,2},{4,5},{5,4},{6,7},{7,6},{8,9},{9,8},{10,11... | collective-permute-start | bytes 1179656 | tf_op jit(solution)/shard_map/ppermute | solution.py:26
  153.0 1.5 collective-permute-start.16
  154.4 2.6 %sum_stage.12 = (bf16[3,128,512]{2,1,0:T(8,128)(2,1)S(1)}, bf16[3,128,512]{2,1,0:T(8,128)(2,1)S(1)}, f32[2,128,512]{2,1,0:T(8,128)S(1)}, f32[2,128,512]{2,1,0:T(...) custom-call(bf16[128,5120]{1,0:T(8,128)(2,1)S(1)} %bitcast.19, f32[2,5120]{1,0:T(2,128)S(1)} %pad_maximum_fusion.refs_1_, ...), custom_call_target="tpu_custom_call" | custom-call | flops 1 | bytes 1 | tf_op jit(solution)/shard_map/sum_stage/pallas_call | solution.py:389
  157.1 1.3 collective-permute-start.20
  158.4 1.5 collective-permute-start.21
  159.9 3.1 %collective-permute-done.15.refs_8_ = bf16[3,128,512]{2,1,0:T(8,128)(2,1)S(1)} collective-permute-done((bf16[3,128,512]{2,1,0:T(8,128)(2,1)S(1)}, bf16[3,128,512]{2,1,0:T(8,128)(2,1)S(1)}, u32[]{:S(2)}, u32[]{:S(2)}) %collective-permute-start.15) | collective-permute-done | bytes 393248 | tf_op jit(solution)/shard_map/ppermute | solution.py:26
  163.0 1.2 collective-permute-done.16.refs_9_
  164.2 2.7 %sum_stage.13 = (bf16[3,128,512]{2,1,0:T(8,128)(2,1)S(1)}, bf16[3,128,512]{2,1,0:T(8,128)(2,1)S(1)}, f32[2,128,512]{2,1,0:T(8,128)S(1)}, f32[2,128,512]{2,1,0:T(...) custom-call(bf16[128,5120]{1,0:T(8,128)(2,1)S(1)} %bitcast.20, ...), custom_call_target="tpu_custom_call" | custom-call | flops 1 | bytes 1 | tf_op jit(solution)/shard_map/sum_stage/pallas_call | solution.py:389
  166.9 1.0 collective-permute-start.23
  167.9 2.0 collective-permute-start.24
  169.8 1.6 collective-permute-start.19
  171.4 1.2 collective-permute-done.21.refs_3_
  172.8 1.6 collective-permute-start.22
  174.4 0.9 collective-permute-start.26
  175.4 3.1 %collective-permute-done.19.refs_9_ = bf16[128,1024]{1,0:T(8,128)(2,1)S(1)} collective-permute-done((bf16[128,1024]{1,0:T(8,128)(2,1)S(1)}, bf16[128,1024]{1,0:T(8,128)(2,1)S(1)}, u32[]{:S(2)}, u32[]{:S(2)}) %collective-permute-start.19) | collective-permute-done | bytes 262176 | tf_op jit(solution)/shard_map/ppermute | solution.py:21
  178.5 0.9 collective-permute-start.27
  179.8 1.6 collective-permute-start.25
  181.5 1.7 collective-permute-start.29
  183.1 1.5 collective-permute-start.30
  184.8 1.5 collective-permute-start.28
  186.4 1.7 collective-permute-done.30.refs_3_
  188.2 1.6 collective-permute-start.31
  189.8 1.0 collective-permute-done.25
  190.8 5.0 %collective-permute-done.28 = bf16[128,1024]{1,0:T(8,128)(2,1)S(1)} collective-permute-done((bf16[128,1024]{1,0:T(8,128)(2,1)S(1)}, bf16[128,1024]{1,0:T(8,128)(2,1)S(1)}, u32[]{:S(2)}, u32[]{:S(2)}) %collective-permute-start.28) | collective-permute-done | bytes 262176 | tf_op jit(solution)/shard_map/ppermute | solution.py:21
  195.8 2.8 %collective-permute-done.31 = bf16[128,1024]{1,0:T(8,128)(2,1)S(1)} collective-permute-done((bf16[128,1024]{1,0:T(8,128)(2,1)S(1)}, bf16[128,1024]{1,0:T(8,128)(2,1)S(1)}, u32[]{:S(2)}, u32[]{:S(2)}) %collective-permute-start.31) | collective-permute-done | bytes 262176 | tf_op jit(solution)/shard_map/ppermute | solution.py:21
  198.7 1.0 copy-done.10
  (60 shorter events, 3.1 us)
Async XLA Ops:
  0.9 1.3 copy-start
  4.6 31.9 %collective-permute-start.2 = (bf16[128,5120]{1,0:T(8,128)(2,1)S(1)}, bf16[128,5120]{1,0:T(8,128)(2,1)}, u32[]{:S(2)}, u32[]{:S(2)}) collective-permute-start(bf16[128,5120]{1,0:T(8,128)(2,1)S(1)} %modulated_norm.1.refs_0_), channel_id=1, source_target_pairs={{0,4},{2,6},{4,0},{6,2},{1,5},{3,7},{5,1},{7,3},{8,12},{10,14},{12... | collective-permute-start | bytes 3932168 | tf_op jit(solution)/shard_map/ppermute | solution.py:26
  7.7 32.2 %collective-permute-start = (bf16[128,5120]{1,0:T(8,128)(2,1)S(1)}, bf16[128,5120]{1,0:T(8,128)(2,1)S(1)}, u32[]{:S(2)}, u32[]{:S(2)}) collective-permute-start(bf16[128,5120]{1,0:T(8,128)(2,1)S(1)} %modulated_norm.1.refs_0_), channel_id=1, source_target_pairs={{0,1},{1,0},{2,3},{3,2},{4,5},{5,4},{6,7},{7,6},{8,9},{9,8},{10,11... | collective-permute-start | bytes 3932168 | tf_op jit(solution)/shard_map/ppermute | solution.py:26
  9.2 39.4 %collective-permute-start.6 = (bf16[128,5120]{1,0:T(8,128)(2,1)S(1)}, bf16[128,5120]{1,0:T(8,128)(2,1)}, u32[]{:S(2)}, u32[]{:S(2)}) collective-permute-start(bf16[128,5120]{1,0:T(8,128)(2,1)S(1)} %modulated_norm.1.refs_0_), channel_id=1, source_target_pairs={{0,2},{2,0},{4,6},{6,4},{1,3},{3,1},{5,7},{7,5},{8,10},{10,8},{12,... | collective-permute-start | bytes 3932168 | tf_op jit(solution)/shard_map/ppermute | solution.py:26
  39.1 0.9 copy-start.8
  39.9 47.0 %collective-permute-start.8 = (bf16[128,5120]{1,0:T(8,128)(2,1)}, bf16[128,5120]{1,0:T(8,128)(2,1)}, u32[]{:S(2)}, u32[]{:S(2)}) collective-permute-start(bf16[128,5120]{1,0:T(8,128)(2,1)} %get-tuple-element.51.refs_2_), channel_id=1, source_target_pairs={{0,2},{2,0},{4,6},{6,4},{1,3},{3,1},{5,7},{7,5},{8,10},{10,8},{12,... | collective-permute-start | bytes 3932168 | tf_op jit(solution)/shard_map/ppermute | solution.py:26
  41.1 0.9 copy-start.9
  42.0 45.0 %collective-permute-start.7 = (bf16[128,5120]{1,0:T(8,128)(2,1)}, bf16[128,5120]{1,0:T(8,128)(2,1)}, u32[]{:S(2)}, u32[]{:S(2)}) collective-permute-start(bf16[128,5120]{1,0:T(8,128)(2,1)} %get-tuple-element.50.refs_1_), channel_id=1, source_target_pairs={{0,2},{2,0},{4,6},{6,4},{1,3},{3,1},{5,7},{7,5},{8,10},{10,8},{12,... | collective-permute-start | bytes 3932168 | tf_op jit(solution)/shard_map/ppermute | solution.py:26
  42.5 94.0 %collective-permute-start.12 = (bf16[384,5120]{1,0:T(8,128)(2,1)}, bf16[384,5120]{1,0:T(8,128)(2,1)}, u32[]{:S(2)}, u32[]{:S(2)}) collective-permute-start(bf16[384,5120]{1,0:T(8,128)(2,1)} %bitcast.7.refs_6_), channel_id=1, source_target_pairs={{0,2},{2,0},{4,6},{6,4},{1,3},{3,1},{5,7},{7,5},{8,10},{10,8},{12,... | collective-permute-start | bytes 11796488 | tf_op jit(solution)/shard_map/ppermute | solution.py:26
  42.5 62.4 %all-to-all-start = ((bf16[8,256,512]{2,1,0:T(8,128)(2,1)}), bf16[8,256,512]{2,1,0:T(8,128)(2,1)S(1)}, u32[]{:S(2)}, u32[]{:S(2)}) async-start(bf16[8,256,512]{2,1,0:T(8,128)(2,1)} %reshape.13.refs_0_), calls=%async_computation | async-start | bytes 4194304 | tf_op jit(solution)/shard_map/all_to_all | solution.py:447
  46.5 39.9 %collective-permute-start.3 = (bf16[128,2560]{1,0:T(8,128)(2,1)}, bf16[128,2560]{1,0:T(8,128)(2,1)}, u32[]{:S(2)}, u32[]{:S(2)}) collective-permute-start(bf16[128,2560]{1,0:T(8,128)(2,1)} %copy-done.8), channel_id=1, source_target_pairs={{0,1},{1,0},{2,3},{3,2},{4,5},{5,4},{6,7},{7,6},{8,9},{9,8},{10,11... | collective-permute-start | bytes 1966088 | tf_op jit(solution)/shard_map/ppermute | solution.py:26
  48.5 37.9 %collective-permute-start.1 = (bf16[128,2560]{1,0:T(8,128)(2,1)}, bf16[128,2560]{1,0:T(8,128)(2,1)}, u32[]{:S(2)}, u32[]{:S(2)}) collective-permute-start(bf16[128,2560]{1,0:T(8,128)(2,1)} %copy-done.9), channel_id=1, source_target_pairs={{0,4},{2,6},{4,0},{6,2},{1,5},{3,7},{5,1},{7,3},{8,12},{10,14},{12... | collective-permute-start | bytes 1966088 | tf_op jit(solution)/shard_map/ppermute | solution.py:26
  86.4 25.8 %collective-permute-start.5 = (bf16[128,2560]{1,0:T(8,128)(2,1)}, bf16[128,2560]{1,0:T(8,128)(2,1)}, u32[]{:S(2)}, u32[]{:S(2)}) collective-permute-start(bf16[128,2560]{1,0:T(8,128)(2,1)} %collective-permute-done.3.refs_1_), channel_id=1, source_target_pairs={{0,2},{2,0},{4,6},{6,4},{1,3},{3,1},{5,7},{7,5},{8,10},{10,8},{12,... | collective-permute-start | bytes 1966088 | tf_op jit(solution)/shard_map/ppermute | solution.py:26
  86.4 25.8 %collective-permute-start.4 = (bf16[128,2560]{1,0:T(8,128)(2,1)}, bf16[128,2560]{1,0:T(8,128)(2,1)}, u32[]{:S(2)}, u32[]{:S(2)}) collective-permute-start(bf16[128,2560]{1,0:T(8,128)(2,1)} %collective-permute-done.1.refs_0_), channel_id=1, source_target_pairs={{0,2},{2,0},{4,6},{6,4},{1,3},{3,1},{5,7},{7,5},{8,10},{10,8},{12,... | collective-permute-start | bytes 1966088 | tf_op jit(solution)/shard_map/ppermute | solution.py:26
  103.6 1.2 copy-start.4
  104.8 2.2 %copy-start.2 = (bf16[8,256,512]{2,1,0:T(8,128)(2,1)}, bf16[8,256,512]{2,1,0:T(8,128)(2,1)S(1)}, u32[]{:S(2)}) copy-start(bf16[8,256,512]{2,1,0:T(8,128)(2,1)S(1)} %all-to-all-done) | copy-start | bytes 6291460
  104.8 2.2 %copy-start.5 = (bf16[768,1152]{1,0:T(8,128)(2,1)S(1)}, bf16[768,1152]{1,0:T(8,128)(2,1)}, u32[]{:S(2)}) copy-start(bf16[768,1152]{1,0:T(8,128)(2,1)} %copy-done.4) | copy-start | bytes 5308420
  107.1 22.6 %all-to-all-start.1 = ((bf16[8,256,256]{2,1,0:T(8,128)(2,1)}), bf16[8,256,256]{2,1,0:T(8,128)(2,1)}, u32[]{:S(2)}, u32[]{:S(2)}) async-start(bf16[8,256,256]{2,1,0:T(8,128)(2,1)} %after.2.refs_6_), calls=%async_computation.1 | async-start | bytes 2097152 | tf_op jit(solution)/shard_map/all_to_all | solution.py:447
  112.3 10.1 %copy-start.7 = (s32[1,4,6]{2,1,0:T(4,128)S(1)}, s32[1,4,6]{2,1,0:T(4,128)}, u32[]{:S(2)}) copy-start(s32[1,4,6]{2,1,0:T(4,128)} %param.11) | copy-start | bytes 292
  112.3 1.5 copy-start.6
  113.8 8.6 %copy-start.3 = (bf16[8,256,512]{2,1,0:T(8,128)(2,1)S(1)}, bf16[8,256,512]{2,1,0:T(8,128)(2,1)}, u32[]{:S(2)}) copy-start(bf16[8,256,512]{2,1,0:T(8,128)(2,1)} %copy-done.2) | copy-start | bytes 6291460
  127.9 5.4 %collective-permute-start.9 = (f32[1,5120]{1,0:T(1,128)S(1)}, f32[1,5120]{1,0:T(1,128)S(1)}, u32[]{:S(2)}, u32[]{:S(2)}) collective-permute-start(f32[1,5120]{1,0:T(1,128)S(1)} %after.3), channel_id=1, source_target_pairs={{0,1},{1,0},{2,3},{3,2},{4,5},{5,4},{6,7},{7,6},{8,9},{9,8},{10,11... | collective-permute-start | bytes 61448 | tf_op jit(solution)/shard_map/ppermute | solution.py:26
  129.6 6.8 %collective-permute-start.10 = (bf16[512,256]{1,0:T(8,128)(2,1)S(1)}, bf16[512,256]{1,0:T(8,128)(2,1)S(1)}, u32[]{:S(2)}, u32[]{:S(2)}) collective-permute-start(bf16[512,256]{1,0:T(8,128)(2,1)S(1)} %get-tuple-element.52.refs_0_), channel_id=1, source_target_pairs={{0,2},{2,0},{4,6},{6,4},{1,3},{3,1},{5,7},{7,5},{8,10},{10,8},{12,... | collective-permute-start | bytes 786440 | tf_op jit(solution)/shard_map/ppermute | solution.py:26
  132.7 3.8 %collective-permute-start.11 = (bf16[512,128]{1,0:T(8,128)(2,1)S(1)}, bf16[512,128]{1,0:T(8,128)(2,1)S(1)}, u32[]{:S(2)}, u32[]{:S(2)}) collective-permute-start(bf16[512,128]{1,0:T(8,128)(2,1)S(1)} %attend_last.2.refs_0_), channel_id=1, source_target_pairs={{0,2},{2,0},{4,6},{6,4},{1,3},{3,1},{5,7},{7,5},{8,10},{10,8},{12,... | collective-permute-start | bytes 393224 | tf_op jit(solution)/shard_map/ppermute | solution.py:26
  133.3 3.2 %copy-start.1 = (bf16[1,1,128,5120]{3,2,1,0:T(8,128)(2,1)S(1)}, bf16[1,1,128,5120]{3,2,1,0:T(8,128)(2,1)}, u32[]{:S(2)}) copy-start(bf16[1,1,128,5120]{3,2,1,0:T(8,128)(2,1)} %param.6) | copy-start | bytes 3932164
  138.9 9.2 %collective-permute-start.13 = (bf16[2,128,512]{2,1,0:T(8,128)(2,1)S(1)}, bf16[2,128,512]{2,1,0:T(8,128)(2,1)S(1)}, u32[]{:S(2)}, u32[]{:S(2)}) collective-permute-start(bf16[2,128,512]{2,1,0:T(8,128)(2,1)S(1)} %get-tuple-element.54), channel_id=1, source_target_pairs={{0,1},{1,0},{2,3},{3,2},{4,5},{5,4},{6,7},{7,6},{8,9},{9,8},{10,11... | collective-permute-start | bytes 786440 | tf_op jit(solution)/shard_map/ppermute | solution.py:26
  139.3 8.9 %collective-permute-start.14 = (bf16[2,128,512]{2,1,0:T(8,128)(2,1)S(1)}, bf16[2,128,512]{2,1,0:T(8,128)(2,1)S(1)}, u32[]{:S(2)}, u32[]{:S(2)}) collective-permute-start(bf16[2,128,512]{2,1,0:T(8,128)(2,1)S(1)} %get-tuple-element.55), channel_id=1, source_target_pairs={{0,4},{2,6},{4,0},{6,2},{1,5},{3,7},{5,1},{7,3},{8,12},{10,14},{12... | collective-permute-start | bytes 786440 | tf_op jit(solution)/shard_map/ppermute | solution.py:26
  143.5 11.0 %collective-permute-start.17 = (bf16[2,128,512]{2,1,0:T(8,128)(2,1)S(1)}, bf16[2,128,512]{2,1,0:T(8,128)(2,1)S(1)}, u32[]{:S(2)}, u32[]{:S(2)}) collective-permute-start(bf16[2,128,512]{2,1,0:T(8,128)(2,1)S(1)} %get-tuple-element.65), channel_id=1, source_target_pairs={{0,1},{1,0},{2,3},{3,2},{4,5},{5,4},{6,7},{7,6},{8,9},{9,8},{10,11... | collective-permute-start | bytes 786440 | tf_op jit(solution)/shard_map/ppermute | solution.py:26
  145.0 9.5 %collective-permute-start.18 = (bf16[2,128,512]{2,1,0:T(8,128)(2,1)S(1)}, bf16[2,128,512]{2,1,0:T(8,128)(2,1)S(1)}, u32[]{:S(2)}, u32[]{:S(2)}) collective-permute-start(bf16[2,128,512]{2,1,0:T(8,128)(2,1)S(1)} %get-tuple-element.66), channel_id=1, source_target_pairs={{0,4},{2,6},{4,0},{6,2},{1,5},{3,7},{5,1},{7,3},{8,12},{10,14},{12... | collective-permute-start | bytes 786440 | tf_op jit(solution)/shard_map/ppermute | solution.py:26
  150.8 12.2 %collective-permute-start.15 = (bf16[3,128,512]{2,1,0:T(8,128)(2,1)S(1)}, bf16[3,128,512]{2,1,0:T(8,128)(2,1)S(1)}, u32[]{:S(2)}, u32[]{:S(2)}) collective-permute-start(bf16[3,128,512]{2,1,0:T(8,128)(2,1)S(1)} %get-tuple-element.59), channel_id=1, source_target_pairs={{0,1},{1,0},{2,3},{3,2},{4,5},{5,4},{6,7},{7,6},{8,9},{9,8},{10,11... | collective-permute-start | bytes 1179656 | tf_op jit(solution)/shard_map/ppermute | solution.py:26
  153.0 11.2 %collective-permute-start.16 = (bf16[3,128,512]{2,1,0:T(8,128)(2,1)S(1)}, bf16[3,128,512]{2,1,0:T(8,128)(2,1)S(1)}, u32[]{:S(2)}, u32[]{:S(2)}) collective-permute-start(bf16[3,128,512]{2,1,0:T(8,128)(2,1)S(1)} %get-tuple-element.60), channel_id=1, source_target_pairs={{0,4},{2,6},{4,0},{6,2},{1,5},{3,7},{5,1},{7,3},{8,12},{10,14},{12... | collective-permute-start | bytes 1179656 | tf_op jit(solution)/shard_map/ppermute | solution.py:26
  157.1 14.3 %collective-permute-start.20 = (bf16[3,128,512]{2,1,0:T(8,128)(2,1)S(1)}, bf16[3,128,512]{2,1,0:T(8,128)(2,1)S(1)}, u32[]{:S(2)}, u32[]{:S(2)}) collective-permute-start(bf16[3,128,512]{2,1,0:T(8,128)(2,1)S(1)} %get-tuple-element.70), channel_id=1, source_target_pairs={{0,1},{1,0},{2,3},{3,2},{4,5},{5,4},{6,7},{7,6},{8,9},{9,8},{10,11... | collective-permute-start | bytes 1179656 | tf_op jit(solution)/shard_map/ppermute | solution.py:26
  158.4 14.2 %collective-permute-start.21 = (bf16[3,128,512]{2,1,0:T(8,128)(2,1)S(1)}, bf16[3,128,512]{2,1,0:T(8,128)(2,1)S(1)}, u32[]{:S(2)}, u32[]{:S(2)}) collective-permute-start(bf16[3,128,512]{2,1,0:T(8,128)(2,1)S(1)} %get-tuple-element.71), channel_id=1, source_target_pairs={{0,4},{2,6},{4,0},{6,2},{1,5},{3,7},{5,1},{7,3},{8,12},{10,14},{12... | collective-permute-start | bytes 1179656 | tf_op jit(solution)/shard_map/ppermute | solution.py:26
  166.9 12.7 %collective-permute-start.23 = (bf16[3,128,512]{2,1,0:T(8,128)(2,1)S(1)}, bf16[3,128,512]{2,1,0:T(8,128)(2,1)S(1)}, u32[]{:S(2)}, u32[]{:S(2)}) collective-permute-start(bf16[3,128,512]{2,1,0:T(8,128)(2,1)S(1)} %get-tuple-element.76), channel_id=1, source_target_pairs={{0,1},{1,0},{2,3},{3,2},{4,5},{5,4},{6,7},{7,6},{8,9},{9,8},{10,11... | collective-permute-start | bytes 1179656 | tf_op jit(solution)/shard_map/ppermute | solution.py:26
  167.9 11.8 %collective-permute-start.24 = (bf16[3,128,512]{2,1,0:T(8,128)(2,1)S(1)}, bf16[3,128,512]{2,1,0:T(8,128)(2,1)S(1)}, u32[]{:S(2)}, u32[]{:S(2)}) collective-permute-start(bf16[3,128,512]{2,1,0:T(8,128)(2,1)S(1)} %get-tuple-element.77), channel_id=1, source_target_pairs={{0,4},{2,6},{4,0},{6,2},{1,5},{3,7},{5,1},{7,3},{8,12},{10,14},{12... | collective-permute-start | bytes 1179656 | tf_op jit(solution)/shard_map/ppermute | solution.py:26
  169.8 8.6 %collective-permute-start.19 = (bf16[128,1024]{1,0:T(8,128)(2,1)S(1)}, bf16[128,1024]{1,0:T(8,128)(2,1)S(1)}, u32[]{:S(2)}, u32[]{:S(2)}) collective-permute-start(bf16[128,1024]{1,0:T(8,128)(2,1)S(1)} %get-tuple-element.69.refs_8_), channel_id=1, source_target_pairs={{0,8},{8,16},{16,24},{24,0},{1,9},{9,17},{17,25},{25,1},{2,10},{10... | collective-permute-start | bytes 786440 | tf_op jit(solution)/shard_map/ppermute | solution.py:21
  172.8 11.9 %collective-permute-start.22 = (bf16[128,1024]{1,0:T(8,128)(2,1)S(1)}, bf16[128,1024]{1,0:T(8,128)(2,1)S(1)}, u32[]{:S(2)}, u32[]{:S(2)}) collective-permute-start(bf16[128,1024]{1,0:T(8,128)(2,1)S(1)} %get-tuple-element.75.refs_8_), channel_id=1, source_target_pairs={{0,8},{8,16},{16,24},{24,0},{1,9},{9,17},{17,25},{25,1},{2,10},{10... | collective-permute-start | bytes 786440 | tf_op jit(solution)/shard_map/ppermute | solution.py:21
  174.4 8.7 %collective-permute-start.26 = (bf16[1,128,512]{2,1,0:T(8,128)(2,1)S(1)}, bf16[1,128,512]{2,1,0:T(8,128)(2,1)S(1)}, u32[]{:S(2)}, u32[]{:S(2)}) collective-permute-start(bf16[1,128,512]{2,1,0:T(8,128)(2,1)S(1)} %get-tuple-element.83), channel_id=1, source_target_pairs={{0,1},{1,0},{2,3},{3,2},{4,5},{5,4},{6,7},{7,6},{8,9},{9,8},{10,11... | collective-permute-start | bytes 393224 | tf_op jit(solution)/shard_map/ppermute | solution.py:26
  178.5 6.3 %collective-permute-start.27 = (bf16[1,128,512]{2,1,0:T(8,128)(2,1)S(1)}, bf16[1,128,512]{2,1,0:T(8,128)(2,1)S(1)}, u32[]{:S(2)}, u32[]{:S(2)}) collective-permute-start(bf16[1,128,512]{2,1,0:T(8,128)(2,1)S(1)} %get-tuple-element.84), channel_id=1, source_target_pairs={{0,4},{2,6},{4,0},{6,2},{1,5},{3,7},{5,1},{7,3},{8,12},{10,14},{12... | collective-permute-start | bytes 393224 | tf_op jit(solution)/shard_map/ppermute | solution.py:26
  179.8 11.0 %collective-permute-start.25 = (bf16[128,1024]{1,0:T(8,128)(2,1)S(1)}, bf16[128,1024]{1,0:T(8,128)(2,1)S(1)}, u32[]{:S(2)}, u32[]{:S(2)}) collective-permute-start(bf16[128,1024]{1,0:T(8,128)(2,1)S(1)} %get-tuple-element.82.refs_6_), channel_id=1, source_target_pairs={{0,8},{8,16},{16,24},{24,0},{1,9},{9,17},{17,25},{25,1},{2,10},{10... | collective-permute-start | bytes 786440 | tf_op jit(solution)/shard_map/ppermute | solution.py:21
  181.5 5.0 %collective-permute-start.29 = (bf16[1,128,512]{2,1,0:T(8,128)(2,1)S(1)}, bf16[1,128,512]{2,1,0:T(8,128)(2,1)S(1)}, u32[]{:S(2)}, u32[]{:S(2)}) collective-permute-start(bf16[1,128,512]{2,1,0:T(8,128)(2,1)S(1)} %get-tuple-element.87), channel_id=1, source_target_pairs={{0,1},{1,0},{2,3},{3,2},{4,5},{5,4},{6,7},{7,6},{8,9},{9,8},{10,11... | collective-permute-start | bytes 393224 | tf_op jit(solution)/shard_map/ppermute | solution.py:26
  183.1 5.0 %collective-permute-start.30 = (bf16[1,128,512]{2,1,0:T(8,128)(2,1)S(1)}, bf16[1,128,512]{2,1,0:T(8,128)(2,1)S(1)}, u32[]{:S(2)}, u32[]{:S(2)}) collective-permute-start(bf16[1,128,512]{2,1,0:T(8,128)(2,1)S(1)} %get-tuple-element.88), channel_id=1, source_target_pairs={{0,4},{2,6},{4,0},{6,2},{1,5},{3,7},{5,1},{7,3},{8,12},{10,14},{12... | collective-permute-start | bytes 393224 | tf_op jit(solution)/shard_map/ppermute | solution.py:26
  184.8 11.0 %collective-permute-start.28 = (bf16[128,1024]{1,0:T(8,128)(2,1)S(1)}, bf16[128,1024]{1,0:T(8,128)(2,1)S(1)}, u32[]{:S(2)}, u32[]{:S(2)}) collective-permute-start(bf16[128,1024]{1,0:T(8,128)(2,1)S(1)} %sum_stage.16.refs_6_), channel_id=1, source_target_pairs={{0,8},{8,16},{16,24},{24,0},{1,9},{9,17},{17,25},{25,1},{2,10},{10... | collective-permute-start | bytes 786440 | tf_op jit(solution)/shard_map/ppermute | solution.py:21
  188.2 10.5 %collective-permute-start.31 = (bf16[128,1024]{1,0:T(8,128)(2,1)S(1)}, bf16[128,1024]{1,0:T(8,128)(2,1)S(1)}, u32[]{:S(2)}, u32[]{:S(2)}) collective-permute-start(bf16[128,1024]{1,0:T(8,128)(2,1)S(1)} %sum_stage.17), channel_id=1, source_target_pairs={{0,8},{8,16},{16,24},{24,0},{1,9},{9,17},{17,25},{25,1},{2,10},{10... | collective-permute-start | bytes 786440 | tf_op jit(solution)/shard_map/ppermute | solution.py:21
  198.7 1.1 copy-start.10

commit v8 on v5

--- a/solution.py
+++ b/solution.py
@@ -26,12 +26,14 @@
     return lax.ppermute(value, axis, pairs)
 
 
-def norm_kernel(rows_ref, modulation_ref, out_ref):
+def norm_kernel(*refs):
+    *parts, modulation_ref, out_ref = refs
     step = 16
 
     def body(index, carry):
         rows = pl.ds(pl.multiple_of(index * step, step), step)
-        values = rows_ref[rows, :].astype(jnp.float32)
+        values = [part[rows, :].astype(jnp.float32) for part in parts]
+        values = jnp.concatenate(values, axis=1) if len(values) > 1 else values[0]
         centre = values - jnp.mean(values, axis=-1, keepdims=True)
         spread = jnp.mean(centre * centre, axis=-1, keepdims=True)
         normed = centre * lax.rsqrt(spread + 1e-06)
@@ -40,19 +42,19 @@
         ).astype(jnp.bfloat16)
         return carry
 
-    lax.fori_loop(0, rows_ref.shape[0] // step, body, 0)
-
-
-def modulated_norm(rows, modulation):
+    lax.fori_loop(0, out_ref.shape[0] // step, body, 0)
+
+
+def modulated_norm(parts, modulation):
+    rows, features = parts[0].shape[0], modulation.shape[1]
     return pl.pallas_call(
         norm_kernel,
-        out_shape=jax.ShapeDtypeStruct(rows.shape, jnp.bfloat16),
+        in_specs=[pl.BlockSpec(memory_space=pltpu.VMEM)] * (len(parts) + 1),
+        out_shape=jax.ShapeDtypeStruct((rows, features), jnp.bfloat16),
         name="modulated_norm",
-        cost_estimate=pl.CostEstimate(
-            flops=10 * rows.size, bytes_accessed=4 * rows.size, transcendentals=0
-        ),
-        compiler_params=pltpu.CompilerParams(vmem_limit_bytes=16 * MIB),
-    )(rows, modulation)
+        cost_estimate=SHORT,
+        compiler_params=pltpu.CompilerParams(vmem_limit_bytes=8 * MIB),
+    )(*parts, modulation)
 
 
 def gate_kernel(value_ref, *refs):
@@ -68,22 +70,17 @@
         input_output_aliases={0: 0},
         name="after",
         cost_estimate=SHORT,
+        compiler_params=pltpu.CompilerParams(vmem_limit_bytes=MIB),
     )(value, *earlier)
 
 
-def project_kernel(*refs, halves):
-    weights_ref, out_ref, total_ref = refs[sum(halves)], refs[-2], refs[-1]
+def project_kernel(*refs):
+    *block_refs, weights_ref, out_ref, total_ref = refs
     step, steps = pl.program_id(0), pl.num_programs(0)
     weights = jnp.concatenate([weights_ref[0], weights_ref[1], weights_ref[2]], axis=1)
-    early = step < steps // 2
-    blocks, place = [], 0
-    for count in halves:
-        if count == 1:
-            blocks.append(refs[place][...])
-        else:
-            blocks.append(jnp.where(early, refs[place][...], refs[place + 1][...]))
-        place += count
-    rows = jnp.concatenate(blocks, axis=0)
+    block = weights.shape[0]
+    columns = pl.ds(pl.multiple_of(step * block, block), block)
+    rows = jnp.concatenate([ref[:, columns] for ref in block_refs], axis=0)
     product = jnp.dot(rows, weights, preferred_element_type=jnp.float32)
 
     @pl.when(step == 0)
@@ -105,22 +102,16 @@
         out_ref[:, 2 * width :] = total_ref[:, 2 * width :].astype(jnp.bfloat16)
 
 
-def project(blocks, weights, earlier):
+def project(blocks, weights):
     _, depth, width = weights.shape
-    rows = blocks[0][0].shape[0]
     steps = 4
     block = depth // steps
-    count = len(blocks) * rows
-    whole = pl.BlockSpec((rows, block), lambda k: (0, k))
-    first = pl.BlockSpec((rows, block), lambda k: (0, jnp.minimum(k, steps // 2 - 1)))
-    second = pl.BlockSpec((rows, block), lambda k: (0, jnp.maximum(k - steps // 2, 0)))
-    specs = [spec for parts in blocks for spec in ([whole] if len(parts) == 1 else [first, second])]
+    count = sum(rows.shape[0] for rows in blocks)
     return pl.pallas_call(
-        functools.partial(project_kernel, halves=[len(parts) for parts in blocks]),
+        project_kernel,
         grid=(steps,),
-        in_specs=specs
-        + [pl.BlockSpec((3, block, width), lambda k: (0, k, 0))]
-        + [pl.BlockSpec(memory_space=pl.ANY)] * len(earlier),
+        in_specs=[pl.BlockSpec(memory_space=pltpu.VMEM)] * len(blocks)
+        + [pl.BlockSpec((3, block, width), lambda k: (0, k, 0))],
         out_specs=pl.BlockSpec((count, 3 * width), lambda k: (0, 0)),
         out_shape=jax.ShapeDtypeStruct((count, 3 * width), jnp.bfloat16),
         scratch_shapes=[pltpu.VMEM((count, 3 * width), jnp.float32)],
@@ -130,13 +121,13 @@
             bytes_accessed=2 * (count * depth + weights.size),
             transcendentals=0,
         ),
-        compiler_params=pltpu.CompilerParams(vmem_limit_bytes=30 * MIB),
-    )(*[part for parts in blocks for part in parts], weights, *earlier)
+        compiler_params=pltpu.CompilerParams(vmem_limit_bytes=40 * MIB),
+    )(*blocks, weights)
 
 
 def attend_kernel(visible_ref, heads_ref, context_ref, *refs, first_block):
     out_ref = refs[-1]
-    width = out_ref.shape[1]
+    width = heads_ref.shape[1] // 3
     tiles_seen = visible_ref.shape[1]
     tiles_fresh = visible_ref.shape[0]
     mine_high, mine_low = lax.axis_index("sp") // 2, lax.axis_index("sp") % 2
@@ -164,12 +155,14 @@
             )
 
         def tiles(kind, head):
-            fresh_columns = slice(kind * width + head * HD, kind * width + (head + 1) * HD)
-            start = (kind - 1) * width + head * HD
+            start = kind * width + head * HD
+            held_start = start - width
             return jnp.concatenate(
                 [
                     jnp.where(
-                        is_fresh, heads_ref[fresh, fresh_columns], context_ref[stale, start : start + HD]
+                        is_fresh,
+                        heads_ref[fresh, start : start + HD],
+                        context_ref[stale, held_start : held_start + HD],
                     )
                     for is_fresh, fresh, stale in places
                 ],
@@ -192,42 +185,35 @@
             out_ref[out_rows, columns] = (mixed / total).astype(jnp.bfloat16)
         return carry
 
-    lax.fori_loop(0, out_ref.shape[0] // TILE, body, 0)
+    lax.fori_loop(0, out_ref.shape[0] // TILE, body, 0, unroll=2)
 
 
 def attend(heads, context, visible, first_block, earlier):
-    count = heads.shape[0] // 2
-    width = heads.shape[1] // 3
+    count, width = heads.shape[0] // 2, heads.shape[1] // 3
     return pl.pallas_call(
         functools.partial(attend_kernel, first_block=first_block),
-        in_specs=[
-            pl.BlockSpec(memory_space=pltpu.SMEM),
-            pl.BlockSpec(memory_space=pltpu.VMEM),
-            pl.BlockSpec(memory_space=pltpu.VMEM),
-        ]
+        in_specs=[pl.BlockSpec(memory_space=pltpu.SMEM)]
+        + [pl.BlockSpec(memory_space=pltpu.VMEM)] * 2
         + [pl.BlockSpec(memory_space=pl.ANY)] * len(earlier),
         out_shape=jax.ShapeDtypeStruct((count, width), jnp.bfloat16),
         name="attend",
-        cost_estimate=pl.CostEstimate(
-            flops=4 * count * visible.shape[1] * TILE * width,
-            bytes_accessed=2 * (heads.size + context.size),
-            transcendentals=count * visible.shape[1] * TILE * width // HD,
-        ),
-        compiler_params=pltpu.CompilerParams(vmem_limit_bytes=32 * MIB),
+        cost_estimate=SHORT,
+        compiler_params=pltpu.CompilerParams(vmem_limit_bytes=12 * MIB),
     )(visible, heads, context, *earlier)
 
 
 def half_kernel(rows_ref, *refs, start):
-    out_ref = refs[-1]
-    out_ref[...] = rows_ref[:, start : start + out_ref.shape[1]]
+    half_ref = refs[-1]
+    half_ref[...] = rows_ref[:, start : start + half_ref.shape[1]]
 
 
 def half_of(rows, start, earlier):
+    count, columns = rows.shape
     return pl.pallas_call(
         functools.partial(half_kernel, start=start),
         in_specs=[pl.BlockSpec(memory_space=pltpu.VMEM)]
         + [pl.BlockSpec(memory_space=pl.ANY)] * len(earlier),
-        out_shape=jax.ShapeDtypeStruct((rows.shape[0], rows.shape[1] // 2), rows.dtype),
+        out_shape=jax.ShapeDtypeStruct((count, columns // 2), rows.dtype),
         name="half_of",
         cost_estimate=SHORT,
         compiler_params=pltpu.CompilerParams(vmem_limit_bytes=8 * MIB),
@@ -248,16 +234,16 @@
 
 
 def begin(start, refs, across_out, along_out, first_kept, second_kept):
-    attended_ref, core_attended_ref, weights_ref, core_weights_ref, rows_ref, gates_ref = refs
+    *attended_refs, weights_ref, core_weights_ref, rows_ref, gates_ref = refs
     tokens, half = rows_ref.shape[0], first_kept.shape[2]
-    attended = jnp.concatenate([attended_ref[...], core_attended_ref[...]], axis=1)
+    attended = jnp.concatenate([ref[...] for ref in attended_refs], axis=1)
 
     def product_of(columns):
         weights = jnp.concatenate([weights_ref[:, columns], core_weights_ref[:, columns]], axis=0)
         return jnp.dot(attended, weights, preferred_element_type=jnp.float32)
 
     columns = slice(start, start + half)
-    product = product_of(columns)
+    product = product_of(slice(0, half))
     for tile in range(2):
         own = product[2 * tile * tokens : (2 * tile + 1) * tokens]
         other = product[(2 * tile + 1) * tokens : (2 * tile + 2) * tokens]
@@ -265,8 +251,7 @@
         sent, kept = combined(own, other, mine, gates_ref, columns)
         across_out[tile] = sent.astype(jnp.bfloat16)
         first_kept[tile] = kept
-    columns = slice(start + half, start + 2 * half)
-    product = product_of(columns)
+    product = product_of(slice(half, 2 * half))
     for branch in range(2):
         second_kept[branch] = product[branch * tokens : (branch + 1) * tokens]
         along_out[branch] = product[(branch + 2) * tokens : (branch + 3) * tokens].astype(
@@ -348,12 +333,19 @@
             middle=middle,
             final=final,
         ),
-        in_specs=[pl.BlockSpec(memory_space=pltpu.VMEM)] * len(operands)
+        grid=(1,),
+        in_specs=[
+            pl.BlockSpec((array.shape[0], chunk), lambda step: (0, next_start // chunk))
+            if name in ("weights", "core_weights")
+            else pl.BlockSpec(memory_space=pltpu.VMEM)
+            for name, array in operands.items()
+        ]
         + [pl.BlockSpec(memory_space=pl.ANY)] * len(earlier),
+        out_specs=[pl.BlockSpec(memory_space=pltpu.VMEM)] * len(outs),
         out_shape=list(outs.values()),
         name="sum_stage",
         cost_estimate=SHORT,
-        compiler_params=pltpu.CompilerParams(vmem_limit_bytes=24 * MIB),
+        compiler_params=pltpu.CompilerParams(vmem_limit_bytes=16 * MIB),
     )(*operands.values(), *earlier)
     return dict(zip(outs, results))
 
@@ -369,33 +361,32 @@
     packed = stale_cache[0, 0].reshape(context_rows, 2, devices, width)
     packed = packed.transpose(2, 0, 1, 3).reshape(devices, context_rows, 2 * width)
 
-    own = modulated_norm(current, modulate)
-    across = from_partner(own, "cfg", 1)
-    along = from_partner(own, "sp", 2)
-    own_core = from_partner(own, "sp", 1)
+    across = from_partner(current, "cfg", 1)
+    along = from_partner(current, "sp", 2)
+    other_modulate = from_partner(modulate, "cfg", 1)
+    own = modulated_norm([current], modulate)
     middle = features // 2
-    gate = modulate[2:3]
-    other_gate = from_partner(gate, "cfg", 1)
-    across, along = after(across, (packed,)), after(along, (packed, other_gate))
-    first = from_partner(half_of(across, 0, ()), "sp", 2)
-    second = from_partner(half_of(along, middle, ()), "cfg", 1)
-    gates = jnp.concatenate([gate, other_gate], axis=0)
+    first = from_partner(half_of(across, 0, (packed, other_modulate)), "sp", 2)
+    second = from_partner(half_of(along, middle, (packed, other_modulate)), "cfg", 1)
     core_weights = from_partner(project_out[0], "sp", 1)
-    near = [(own,), (across,), (along,), (first, second)]
-    far = [(own_core,)] + [
-        tuple(from_partner(part, "sp", 1) for part in parts) for parts in near[1:]
+    near = [
+        own,
+        modulated_norm([across], other_modulate),
+        modulated_norm([along], modulate),
+        modulated_norm([first, second], other_modulate),
     ]
-
-    packed = after(packed, far[2])
+    far = [from_partner(rows, "sp", 1) for rows in near]
+
+    packed = after(packed, (first, second, near[0]))
     context = lax.all_to_all(packed, ("sp", "cfg"), split_axis=0, concat_axis=0, tiled=True)
     context = context.reshape(devices * context_rows, 2 * width)
 
-    heads = project(near + far, project_in[0], (core_weights,))
+    heads = project(near + far, project_in[0])
+    gates = jnp.concatenate([modulate[2:3], other_modulate[2:3]], axis=0)
     for_core = attend(heads, context, visible[0], 4, ())
     core_attended = from_partner(for_core, "sp", 1)
-    attended = attend(heads, context, visible[0], 0, (for_core,))
-
-    weights = project_out[0]
+    attended = attend(heads, context, visible[0], 0, (for_core, gates))
+
     count = COLUMN_CHUNKS
     chunk = features // count
     kept, left, flights, arrivals, earlier = {}, {}, {}, [], []
@@ -403,8 +394,12 @@
         fresh, middle, final = index + 2 < count, 0 <= index < count, index >= 2
         operands = {"rows": current, "gates": gates}
         if fresh:
-            operands["attended"], operands["core_attended"] = attended, core_attended
-            operands["weights"], operands["core_weights"] = weights, core_weights
+            operands.update(
+                attended=attended,
+                core_attended=core_attended,
+                weights=project_out[0],
+                core_weights=core_weights,
+            )
         if index >= 0:
             operands["across"], operands["along"] = flights.pop(index)
         if middle:

time: 220 us -> 176 us (0.80)
  waiting for transfers between devices: 91.2 us -> 52.1 us
  starting transfers between devices: 39.2 us -> 34.3 us
  Pallas kernels: 50.3 us -> 54.7 us
  local copies, waits for them, and re-layouts: 37.8 us -> 33.4 us
    ppermute x26 -> x25, waiting for transfers between devices: 79.3 us -> 36.9 us  [from_partner(): return lax.ppermute(value, axis, pairs)]
    pallas_call x2 -> x5, Pallas kernels: 22.9 us -> 30 us  [the longest x1 18.7 us: project(): pl.pallas_call(project_kernel, grid=(steps,), in_specs=[pl.BlockSpec(memo...]
    ppermute x26 -> x25, starting transfers between devices: 27.3 us -> 22.2 us  [from_partner(): return lax.ppermute(value, axis, pairs)]
    unnamed x34 -> x29, local copies, waits for them, and re-layouts: 15 us -> 10.7 us
    all_to_all x1, waiting for transfers between devices: 0.01 us -> 4.24 us  [per_device(): lax.all_to_all(packed, ('sp', 'cfg'), split_axis=0, concat_axis=0, tiled=...]
    pallas_call x9, Pallas kernels: 17 us -> 13.4 us  [stage(): pl.pallas_call(functools.partial(stage_kernel, parts=parts, start=start,...]
  transfers between devices with their start and end apart: 32 -> 31, of which waited for: 17 -> 21; matrix products, arithmetic and copies ran while one was open for 12% -> 14% of each run, Pallas kernels for 18% -> 30%
where the time goes in v8:
time: 176 us; the launch traced here: 175 us
  Pallas kernels  54.7 us (31%)
  waiting for transfers between devices  52.1 us (30%)
  starting transfers between devices  34.3 us (19%)
  local copies, waits for them, and re-layouts  33.4 us (19%)
    ppermute x25, waiting for transfers between devices, from_partner(): return lax.ppermute(value, axis, pairs)  36.9 us
    ppermute x25, starting transfers between devices, from_partner(): return lax.ppermute(value, axis, pairs)  22.2 us
    pallas_call x1, Pallas kernels, project(): pl.pallas_call(project_kernel, grid=(steps,), in_specs=[pl.BlockSpec(memo...  18.7 us
    another operation x2, local copies, waits for them, and re-layouts, per_device(): packed = stale_cache[0, 0].reshape(context_rows, 2, devices, width)  13.9 us
    pallas_call x9, Pallas kernels, stage(): pl.pallas_call(functools.partial(stage_kernel, parts=parts, start=start,...  13.4 us
    pallas_call x4, Pallas kernels, modulated_norm(): pl.pallas_call(norm_kernel, in_specs=[pl.BlockSpec(memory_space=pltpu.VME...  11.2 us
    ppermute x5, waiting for transfers between devices, from_behind(): return lax.ppermute(x, axis, [(i, (i + by) % count) for i in range(count)])  11 us
    unnamed x29, local copies, waits for them, and re-layouts  10.7 us
  transfers between devices with their start and end apart: 31, of which 21 were waited for; matrix products, arithmetic and copies ran while one was open for 14% of the time, Pallas kernels for 30%

profile of v8, /device:TPU:0, one launch (start us, length us, event | category | flops | bytes accessed | tf_op | source)
XLA Modules:
  0.0 174.9 jit_solution(10932496211790545121)
XLA Ops:
  0.0 2.9 %collective-permute-start.1 = (bf16[128,5120]{1,0:T(8,128)(2,1)}, bf16[128,5120]{1,0:T(8,128)(2,1)S(1)}, u32[]{:S(2)}, u32[]{:S(2)}) collective-permute-start(bf16[128,5120]{1,0:T(8,128)(2,1)} %bitcast.14), channel_id=1, source_target_pairs={{0,1},{1,0},{2,3},{3,2},{4,5},{5,4},{6,7},{7,6},{8,9},{9,8},{10,11... | collective-permute-start | bytes 3932168 | tf_op jit(solution)/shard_map/ppermute | solution.py:26
  2.9 1.5 collective-permute-start.2
  4.5 0.8 copy.13
  5.9 8.0 %reshape_squeeze.3 = bf16[256,2,8,384]{3,2,1,0:T(8,128)(2,1)} reshape(bf16[1,1,256,2,3072]{4,3,2,1,0:T(2,128)(2,1)} %param.10) | data formatting | bytes 6291456 | tf_op jit(solution)/shard_map/reshape;squeeze | solution.py:361
  13.9 5.9 %copy.12 = bf16[256,2,8,384]{3,1,0,2:T(2,128)(2,1)} copy(bf16[256,2,8,384]{3,2,1,0:T(8,128)(2,1)} %reshape_squeeze.3) | data formatting | bytes 6291456 | tf_op jit(solution)/shard_map/reshape;squeeze | solution.py:361
  19.9 8.0 %reshape.7.refs_0_.value_ref = bf16[8,256,768]{2,1,0:T(8,128)(2,1)} reshape(bf16[8,256,2,384]{3,2,1,0:T(2,128)(2,1)} %bitcast.31) | data formatting | bytes 6291456 | tf_op jit(solution)/shard_map/reshape | solution.py:362
  27.9 5.8 %collective-permute-done.refs_1_.refs_2_ = f32[3,5120]{1,0:T(4,128)S(1)} collective-permute-done((f32[3,5120]{1,0:T(4,128)S(1)}, f32[3,5120]{1,0:T(4,128)S(1)}, u32[]{:S(2)}, u32[]{:S(2)}) %collective-permute-start) | collective-permute-done | bytes 61472 | tf_op jit(solution)/shard_map/ppermute | solution.py:26
  33.7 1.9 %copy-done.1 = bf16[8,256,768]{2,1,0:T(8,128)(2,1)S(1)} copy-done((bf16[8,256,768]{2,1,0:T(8,128)(2,1)S(1)}, bf16[8,256,768]{2,1,0:T(8,128)(2,1)}, u32[]{:S(2)}) %copy-start.1) | copy-done | bytes 3145752
  35.6 1.8 %collective-permute-start.3 = (bf16[128,2560]{1,0:T(8,128)(2,1)S(1)}, bf16[128,2560]{1,0:T(8,128)(2,1)S(1)}, u32[]{:S(2)}, u32[]{:S(2)}) collective-permute-start(bf16[128,2560]{1,0:T(8,128)(2,1)S(1)} %half_of.2), channel_id=1, source_target_pairs={{0,4},{2,6},{4,0},{6,2},{1,5},{3,7},{5,1},{7,3},{8,12},{10,14},{12... | collective-permute-start | bytes 1966088 | tf_op jit(solution)/shard_map/ppermute | solution.py:26
  37.5 1.5 half_of.3
  39.0 1.6 collective-permute-start.4
  40.5 2.5 %modulated_norm.4.refs_0_.refs_2_ = bf16[128,5120]{1,0:T(8,128)(2,1)S(1)} custom-call(bf16[128,5120]{1,0:T(8,128)(2,1)S(1)} %bitcast.16, f32[3,5120]{1,0:T(4,128)S(1)} %bitcast.27), custom_call_target="tpu_custom_call" | custom-call | flops 1 | bytes 1 | tf_op jit(solution)/shard_map/modulated_norm/pallas_call | solution.py:50
  43.0 8.7 %collective-permute-done.3.refs_0_ = bf16[128,2560]{1,0:T(8,128)(2,1)S(1)} collective-permute-done((bf16[128,2560]{1,0:T(8,128)(2,1)S(1)}, bf16[128,2560]{1,0:T(8,128)(2,1)S(1)}, u32[]{:S(2)}, u32[]{:S(2)}) %collective-permute-start.3) | collective-permute-done | bytes 655392 | tf_op jit(solution)/shard_map/ppermute | solution.py:26
  51.7 2.8 %collective-permute-done.4.refs_1_ = bf16[128,2560]{1,0:T(8,128)(2,1)S(1)} collective-permute-done((bf16[128,2560]{1,0:T(8,128)(2,1)S(1)}, bf16[128,2560]{1,0:T(8,128)(2,1)S(1)}, u32[]{:S(2)}, u32[]{:S(2)}) %collective-permute-start.4) | collective-permute-done | bytes 655392 | tf_op jit(solution)/shard_map/ppermute | solution.py:26
  54.5 1.7 %copy-done.3 = bf16[8,256,768]{2,1,0:T(8,128)(2,1)} copy-done((bf16[8,256,768]{2,1,0:T(8,128)(2,1)}, bf16[8,256,768]{2,1,0:T(8,128)(2,1)S(1)}, u32[]{:S(2)}) %copy-start.3) | copy-done | bytes 3145752
  56.2 1.1 copy-done.6
  57.3 0.8 copy-done.8
  58.1 4.6 %all-to-all-start = ((bf16[8,256,768]{2,1,0:T(8,128)(2,1)}), bf16[8,256,768]{2,1,0:T(8,128)(2,1)}, u32[]{:S(2)}, u32[]{:S(2)}) async-start(bf16[8,256,768]{2,1,0:T(8,128)(2,1)} %copy-done.3), calls=%async_computation | async-start | bytes 6291456 | tf_op jit(solution)/shard_map/all_to_all | solution.py:381
  63.0 3.8 %modulated_norm.6.refs_2_ = bf16[128,5120]{1,0:T(8,128)(2,1)S(1)} custom-call(bf16[128,5120]{1,0:T(8,128)(2,1)} %collective-permute-done.2.refs_0_.rows_ref, f32[3,5120]{1,0:T(4,128)S(1)} %bitcast.28), custom_call_target="tpu_custom_call" | custom-call | flops 1 | bytes 1 | tf_op jit(solution)/shard_map/modulated_norm/pallas_call | solution.py:50
  67.2 2.5 %modulated_norm.5.refs_1_ = bf16[128,5120]{1,0:T(8,128)(2,1)S(1)} custom-call(bf16[128,5120]{1,0:T(8,128)(2,1)S(1)} %collective-permute-done.1.refs_0_.rows_ref, f32[3,5120]{1,0:T(4,128)S(1)} %collective-permute-done.refs_1_.refs_2_), custom_call_target="tpu_custom_call" | custom-call | flops 1 | bytes 1 | tf_op jit(solution)/shard_map/modulated_norm/pallas_call | solution.py:50
  69.9 2.5 %modulated_norm.7.refs_3_ = bf16[128,5120]{1,0:T(8,128)(2,1)S(1)} custom-call(bf16[128,2560]{1,0:T(8,128)(2,1)S(1)} %collective-permute-done.3.refs_0_, bf16[128,2560]{1,0:T(8,128)(2,1)S(1)} %copy-done.9, f32[3,5120]{1,0:T(4,128)S(1)} %collective-permute-done.refs_1_.refs_2_), custom_call_target="tpu_custom_call" | custom-call | flops 1 | bytes 1 | tf_op jit(solution)/shard_map/modulated_norm/pallas_call | solution.py:50
  72.9 0.7 slice_bitcast_fusion
  73.6 1.9 %collective-permute-done.8.refs_7_ = bf16[128,5120]{1,0:T(8,128)(2,1)S(1)} collective-permute-done((bf16[128,5120]{1,0:T(8,128)(2,1)S(1)}, bf16[128,5120]{1,0:T(8,128)(2,1)S(1)}, u32[]{:S(2)}, u32[]{:S(2)}) %collective-permute-start.8) | collective-permute-done | bytes 1310752 | tf_op jit(solution)/shard_map/ppermute | solution.py:26
  75.5 18.7 %project_heads.1.heads_ref = bf16[1024,1152]{1,0:T(8,128)(2,1)S(1)} custom-call(bf16[128,5120]{1,0:T(8,128)(2,1)S(1)} %copy-done.7, bf16[128,5120]{1,0:T(8,128)(2,1)S(1)} %modulated_norm.5.refs_1_, bf16[128,5120]{1,0:T(8,128)(2,1)S(1)} %modulated_norm.6.refs_2_, bf16[128,5120]{1,0:T(8,128)(2,1)S(1)} %modulated_norm.7.refs_3_, ...), custom_call_target="tpu_custom_call" | custom-call | flops 12079595520 | bytes 22282240 | tf_op jit(solution)/shard_map/project_heads/pallas_call | solution.py:110
  94.3 1.5 copy-done.4
  95.8 4.2 %all-to-all-done = bf16[8,256,768]{2,1,0:T(8,128)(2,1)} async-done(((bf16[8,256,768]{2,1,0:T(8,128)(2,1)}), bf16[8,256,768]{2,1,0:T(8,128)(2,1)}, u32[]{:S(2)}, u32[]{:S(2)}) %all-to-all-start) | async-done | bytes 3145760 | tf_op jit(solution)/shard_map/all_to_all | solution.py:381
  100.0 1.7 copy-done.5
  101.7 4.8 %attend.2.refs_0_ = bf16[512,384]{1,0:T(8,128)(2,1)S(1)} custom-call(s32[4,6]{1,0:T(4,128)S(1)} %bitcast.29, bf16[1024,1152]{1,0:T(8,128)(2,1)S(1)} %copy-done.5, bf16[2048,768]{1,0:T(8,128)(2,1)} %bitcast.5.context_ref), custom_call_target="tpu_custom_call" | custom-call | flops 1 | bytes 1 | tf_op jit(solution)/shard_map/attend/pallas_call | solution.py:193
  106.6 5.0 %attend.3.refs_2_ = bf16[512,384]{1,0:T(8,128)(2,1)S(1)} custom-call(s32[4,6]{1,0:T(4,128)S(1)} %bitcast.30, bf16[1024,1152]{1,0:T(8,128)(2,1)S(1)} %copy-done.5, bf16[2048,768]{1,0:T(8,128)(2,1)} %bitcast.5.context_ref, bf16[512,384]{1,0:T(8,128)(2,1)S(1)} %attend.2.refs_0_, f32[2,5120]{1,0:T(2,128)S(1)} %pad_maximum_fusion.refs_1_), custom_call_target="tpu_custom_call" | custom-call | flops 1 | bytes 1 | tf_op jit(solution)/shard_map/attend/pallas_call | solution.py:193
  111.7 2.4 %sum_stage.9 = (bf16[2,128,512]{2,1,0:T(8,128)(2,1)S(1)}, bf16[2,128,512]{2,1,0:T(8,128)(2,1)S(1)}, f32[2,128,512]{2,1,0:T(8,128)S(1)}, f32[2,128,512]{2,1,0:T(8,128)S(1)}) custom-call(bf16[128,5120]{1,0:T(8,128)(2,1)S(1)} %bitcast.17, f32[2,5120]{1,0:T(2,128)S(1)} %pad_maximum_fusion.refs_1_, bf16[512,384]{1,0:T(8,128)(2,1)S(1)} %attend.3.refs_2_, ...), custom_call_target="tpu_custom_call" | custom-call | flops 1 | bytes 1 | tf_op jit(solution)/shard_map/sum_stage/pallas_call | solution.py:326
  114.1 1.1 collective-permute-start.11
  115.7 2.4 %sum_stage.10 = (bf16[2,128,512]{2,1,0:T(8,128)(2,1)S(1)}, bf16[2,128,512]{2,1,0:T(8,128)(2,1)S(1)}, f32[2,128,512]{2,1,0:T(8,128)S(1)}, f32[2,128,512]{2,1,0:T(8,128)S(1)}) custom-call(bf16[128,5120]{1,0:T(8,128)(2,1)S(1)} %bitcast.18, f32[2,5120]{1,0:T(2,128)S(1)} %pad_maximum_fusion.refs_1_, bf16[512,384]{1,0:T(8,128)(2,1)S(1)} %attend.3.refs_2_, ...), custom_call_target="tpu_custom_call" | custom-call | flops 1 | bytes 1 | tf_op jit(solution)/shard_map/sum_stage/pallas_call | solution.py:326
  118.1 1.4 collective-permute-start.15
  119.5 1.2 collective-permute-start.16
  120.7 2.6 %collective-permute-done.11.refs_6_ = bf16[2,128,512]{2,1,0:T(8,128)(2,1)S(1)} collective-permute-done((bf16[2,128,512]{2,1,0:T(8,128)(2,1)S(1)}, bf16[2,128,512]{2,1,0:T(8,128)(2,1)S(1)}, u32[]{:S(2)}, u32[]{:S(2)}) %collective-permute-start.11) | collective-permute-done | bytes 262176 | tf_op jit(solution)/shard_map/ppermute | solution.py:26
  123.2 1.0 collective-permute-done.12.refs_7_
  124.3 2.6 %sum_stage.11 = (bf16[3,128,512]{2,1,0:T(8,128)(2,1)S(1)}, bf16[3,128,512]{2,1,0:T(8,128)(2,1)S(1)}, f32[2,128,512]{2,1,0:T(8,128)S(1)}, f32[2,128,512]{2,1,0:T(...) custom-call(bf16[128,5120]{1,0:T(8,128)(2,1)S(1)} %bitcast.19, f32[2,5120]{1,0:T(2,128)S(1)} %pad_maximum_fusion.refs_1_, ...), custom_call_target="tpu_custom_call" | custom-call | flops 1 | bytes 1 | tf_op jit(solution)/shard_map/sum_stage/pallas_call | solution.py:326
  126.9 1.1 collective-permute-start.13
  128.0 0.9 collective-permute-start.14
  129.3 2.7 %sum_stage.12 = (bf16[3,128,512]{2,1,0:T(8,128)(2,1)S(1)}, bf16[3,128,512]{2,1,0:T(8,128)(2,1)S(1)}, f32[2,128,512]{2,1,0:T(8,128)S(1)}, f32[2,128,512]{2,1,0:T(...) custom-call(bf16[128,5120]{1,0:T(8,128)(2,1)S(1)} %bitcast.20, f32[2,5120]{1,0:T(2,128)S(1)} %pad_maximum_fusion.refs_1_, ...), custom_call_target="tpu_custom_call" | custom-call | flops 1 | bytes 1 | tf_op jit(solution)/shard_map/sum_stage/pallas_call | solution.py:326
  131.9 1.1 collective-permute-start.18
  133.1 0.7 collective-permute-start.19
  133.8 5.3 %collective-permute-done.13.refs_6_ = bf16[3,128,512]{2,1,0:T(8,128)(2,1)S(1)} collective-permute-done((bf16[3,128,512]{2,1,0:T(8,128)(2,1)S(1)}, bf16[3,128,512]{2,1,0:T(8,128)(2,1)S(1)}, u32[]{:S(2)}, u32[]{:S(2)}) %collective-permute-start.13) | collective-permute-done | bytes 393248 | tf_op jit(solution)/shard_map/ppermute | solution.py:26
  139.1 1.0 collective-permute-done.14.refs_7_
  140.1 2.7 %sum_stage.13 = (bf16[3,128,512]{2,1,0:T(8,128)(2,1)S(1)}, bf16[3,128,512]{2,1,0:T(8,128)(2,1)S(1)}, f32[2,128,512]{2,1,0:T(8,128)S(1)}, f32[2,128,512]{2,1,0:T(...) custom-call(bf16[128,5120]{1,0:T(8,128)(2,1)S(1)} %bitcast.21, ...), custom_call_target="tpu_custom_call" | custom-call | flops 1 | bytes 1 | tf_op jit(solution)/shard_map/sum_stage/pallas_call | solution.py:326
  142.8 1.1 collective-permute-start.21
  144.4 1.6 collective-permute-start.17
  146.0 1.5 collective-permute-done.18.refs_2_
  147.5 1.0 collective-permute-done.19.refs_3_
  148.7 1.6 collective-permute-start.20
  150.4 1.0 collective-permute-start.24
  151.4 2.6 %collective-permute-done.17.refs_9_ = bf16[128,1024]{1,0:T(8,128)(2,1)S(1)} collective-permute-done((bf16[128,1024]{1,0:T(8,128)(2,1)S(1)}, bf16[128,1024]{1,0:T(8,128)(2,1)S(1)}, u32[]{:S(2)}, u32[]{:S(2)}) %collective-permute-start.17) | collective-permute-done | bytes 262176 | tf_op jit(solution)/shard_map/ppermute | solution.py:21
  154.2 0.9 collective-permute-done.21.refs_2_
  155.1 0.7 collective-permute-done.22.refs_3_
  156.1 1.6 collective-permute-start.23
  157.7 1.0 collective-permute-start.27
  159.9 1.0 collective-permute-start.26
  161.0 1.7 collective-permute-done.27.refs_2_
  162.7 1.0 collective-permute-done.28.refs_3_
  163.8 1.6 collective-permute-start.29
  165.4 1.2 collective-permute-done.23
  166.6 4.4 %collective-permute-done.26 = bf16[128,1024]{1,0:T(8,128)(2,1)S(1)} collective-permute-done((bf16[128,1024]{1,0:T(8,128)(2,1)S(1)}, bf16[128,1024]{1,0:T(8,128)(2,1)S(1)}, u32[]{:S(2)}, u32[]{:S(2)}) %collective-permute-start.26) | collective-permute-done | bytes 262176 | tf_op jit(solution)/shard_map/ppermute | solution.py:21
  171.0 2.8 %collective-permute-done.29 = bf16[128,1024]{1,0:T(8,128)(2,1)S(1)} collective-permute-done((bf16[128,1024]{1,0:T(8,128)(2,1)S(1)}, bf16[128,1024]{1,0:T(8,128)(2,1)S(1)}, u32[]{:S(2)}, u32[]{:S(2)}) %collective-permute-start.29) | collective-permute-done | bytes 262176 | tf_op jit(solution)/shard_map/ppermute | solution.py:21
  173.8 1.0 copy-done.11
  (53 shorter events, 5.6 us)
Async XLA Ops:
  0.0 33.7 %collective-permute-start.1 = (bf16[128,5120]{1,0:T(8,128)(2,1)}, bf16[128,5120]{1,0:T(8,128)(2,1)S(1)}, u32[]{:S(2)}, u32[]{:S(2)}) collective-permute-start(bf16[128,5120]{1,0:T(8,128)(2,1)} %bitcast.14), channel_id=1, source_target_pairs={{0,1},{1,0},{2,3},{3,2},{4,5},{5,4},{6,7},{7,6},{8,9},{9,8},{10,11... | collective-permute-start | bytes 3932168 | tf_op jit(solution)/shard_map/ppermute | solution.py:26
  2.9 34.5 %collective-permute-start.2 = (bf16[128,5120]{1,0:T(8,128)(2,1)}, bf16[128,5120]{1,0:T(8,128)(2,1)}, u32[]{:S(2)}, u32[]{:S(2)}) collective-permute-start(bf16[128,5120]{1,0:T(8,128)(2,1)} %bitcast.15), channel_id=1, source_target_pairs={{0,4},{2,6},{4,0},{6,2},{1,5},{3,7},{5,1},{7,3},{8,12},{10,14},{12... | collective-permute-start | bytes 3932168 | tf_op jit(solution)/shard_map/ppermute | solution.py:26
  5.3 28.4 %collective-permute-start = (f32[3,5120]{1,0:T(4,128)S(1)}, f32[3,5120]{1,0:T(4,128)S(1)}, u32[]{:S(2)}, u32[]{:S(2)}) collective-permute-start(f32[3,5120]{1,0:T(4,128)S(1)} %bitcast.26), channel_id=1, source_target_pairs={{0,1},{1,0},{2,3},{3,2},{4,5},{5,4},{6,7},{7,6},{8,9},{9,8},{10,11... | collective-permute-start | bytes 184328 | tf_op jit(solution)/shard_map/ppermute | solution.py:26
  33.7 1.9 %copy-start.1 = (bf16[8,256,768]{2,1,0:T(8,128)(2,1)S(1)}, bf16[8,256,768]{2,1,0:T(8,128)(2,1)}, u32[]{:S(2)}) copy-start(bf16[8,256,768]{2,1,0:T(8,128)(2,1)} %reshape.7.refs_0_.value_ref) | copy-start | bytes 9437188
  35.6 4.9 %copy-start = (bf16[1,1,128,5120]{3,2,1,0:T(8,128)(2,1)S(1)}, bf16[1,1,128,5120]{3,2,1,0:T(8,128)(2,1)}, u32[]{:S(2)}) copy-start(bf16[1,1,128,5120]{3,2,1,0:T(8,128)(2,1)} %param.6) | copy-start | bytes 3932164
  35.6 16.1 %collective-permute-start.3 = (bf16[128,2560]{1,0:T(8,128)(2,1)S(1)}, bf16[128,2560]{1,0:T(8,128)(2,1)S(1)}, u32[]{:S(2)}, u32[]{:S(2)}) collective-permute-start(bf16[128,2560]{1,0:T(8,128)(2,1)S(1)} %half_of.2), channel_id=1, source_target_pairs={{0,4},{2,6},{4,0},{6,2},{1,5},{3,7},{5,1},{7,3},{8,12},{10,14},{12... | collective-permute-start | bytes 1966088 | tf_op jit(solution)/shard_map/ppermute | solution.py:26
  37.5 17.0 %copy-start.2 = (bf16[8,256,768]{2,1,0:T(8,128)(2,1)S(1)}, bf16[8,256,768]{2,1,0:T(8,128)(2,1)}, u32[]{:S(2)}) copy-start(bf16[8,256,768]{2,1,0:T(8,128)(2,1)} %reshape.7.refs_0_.value_ref) | copy-start | bytes 9437188
  39.0 15.5 %collective-permute-start.4 = (bf16[128,2560]{1,0:T(8,128)(2,1)S(1)}, bf16[128,2560]{1,0:T(8,128)(2,1)S(1)}, u32[]{:S(2)}, u32[]{:S(2)}) collective-permute-start(bf16[128,2560]{1,0:T(8,128)(2,1)S(1)} %half_of.3), channel_id=1, source_target_pairs={{0,1},{1,0},{2,3},{3,2},{4,5},{5,4},{6,7},{7,6},{8,9},{9,8},{10,11... | collective-permute-start | bytes 1966088 | tf_op jit(solution)/shard_map/ppermute | solution.py:26
  40.5 71.1 %collective-permute-start.10 = (bf16[384,5120]{1,0:T(8,128)(2,1)}, bf16[384,5120]{1,0:T(8,128)(2,1)}, u32[]{:S(2)}, u32[]{:S(2)}) collective-permute-start(bf16[384,5120]{1,0:T(8,128)(2,1)} %bitcast.6.refs_4_), channel_id=1, source_target_pairs={{0,2},{2,0},{4,6},{6,4},{1,3},{3,1},{5,7},{7,5},{8,10},{10,8},{12,... | collective-permute-start | bytes 11796488 | tf_op jit(solution)/shard_map/ppermute | solution.py:26
  54.5 1.8 %copy-start.3 = (bf16[8,256,768]{2,1,0:T(8,128)(2,1)}, bf16[8,256,768]{2,1,0:T(8,128)(2,1)S(1)}, u32[]{:S(2)}) copy-start(bf16[8,256,768]{2,1,0:T(8,128)(2,1)S(1)} %after.1) | copy-start | bytes 9437188
  56.2 1.1 copy-start.6
  57.3 0.8 copy-start.8
  58.1 41.9 %all-to-all-start = ((bf16[8,256,768]{2,1,0:T(8,128)(2,1)}), bf16[8,256,768]{2,1,0:T(8,128)(2,1)}, u32[]{:S(2)}, u32[]{:S(2)}) async-start(bf16[8,256,768]{2,1,0:T(8,128)(2,1)} %copy-done.3), calls=%async_computation | async-start | bytes 6291456 | tf_op jit(solution)/shard_map/all_to_all | solution.py:381
  62.8 10.8 %collective-permute-start.5 = (bf16[128,5120]{1,0:T(8,128)(2,1)}, bf16[128,5120]{1,0:T(8,128)(2,1)S(1)}, u32[]{:S(2)}, u32[]{:S(2)}) collective-permute-start(bf16[128,5120]{1,0:T(8,128)(2,1)} %copy-done.6), channel_id=1, source_target_pairs={{0,2},{2,0},{4,6},{6,4},{1,3},{3,1},{5,7},{7,5},{8,10},{10,8},{12,... | collective-permute-start | bytes 3932168 | tf_op jit(solution)/shard_map/ppermute | solution.py:26
  66.8 3.1 %copy-start.9 = (bf16[128,2560]{1,0:T(8,128)(2,1)S(1)}, bf16[128,2560]{1,0:T(8,128)(2,1)}, u32[]{:S(2)}) copy-start(bf16[128,2560]{1,0:T(8,128)(2,1)} %copy-done.8) | copy-start | bytes 1966084
  66.8 6.8 %collective-permute-start.7 = (bf16[128,5120]{1,0:T(8,128)(2,1)S(1)}, bf16[128,5120]{1,0:T(8,128)(2,1)S(1)}, u32[]{:S(2)}, u32[]{:S(2)}) collective-permute-start(bf16[128,5120]{1,0:T(8,128)(2,1)S(1)} %modulated_norm.6.refs_2_), channel_id=1, source_target_pairs={{0,2},{2,0},{4,6},{6,4},{1,3},{3,1},{5,7},{7,5},{8,10},{10,8},{12,... | collective-permute-start | bytes 3932168 | tf_op jit(solution)/shard_map/ppermute | solution.py:26
  69.7 5.8 %copy-start.7 = (bf16[128,5120]{1,0:T(8,128)(2,1)S(1)}, bf16[128,5120]{1,0:T(8,128)(2,1)}, u32[]{:S(2)}) copy-start(bf16[128,5120]{1,0:T(8,128)(2,1)} %copy-done.6) | copy-start | bytes 3932164
  69.7 3.9 %collective-permute-start.6 = (bf16[128,5120]{1,0:T(8,128)(2,1)S(1)}, bf16[128,5120]{1,0:T(8,128)(2,1)S(1)}, u32[]{:S(2)}, u32[]{:S(2)}) collective-permute-start(bf16[128,5120]{1,0:T(8,128)(2,1)S(1)} %modulated_norm.5.refs_1_), channel_id=1, source_target_pairs={{0,2},{2,0},{4,6},{6,4},{1,3},{3,1},{5,7},{7,5},{8,10},{10,8},{12,... | collective-permute-start | bytes 3932168 | tf_op jit(solution)/shard_map/ppermute | solution.py:26
  72.4 3.1 %collective-permute-start.8 = (bf16[128,5120]{1,0:T(8,128)(2,1)S(1)}, bf16[128,5120]{1,0:T(8,128)(2,1)S(1)}, u32[]{:S(2)}, u32[]{:S(2)}) collective-permute-start(bf16[128,5120]{1,0:T(8,128)(2,1)S(1)} %modulated_norm.7.refs_3_), channel_id=1, source_target_pairs={{0,2},{2,0},{4,6},{6,4},{1,3},{3,1},{5,7},{7,5},{8,10},{10,8},{12,... | collective-permute-start | bytes 3932168 | tf_op jit(solution)/shard_map/ppermute | solution.py:26
  75.5 24.5 %copy-start.10 = (s32[1,4,6]{2,1,0:T(4,128)S(1)}, s32[1,4,6]{2,1,0:T(4,128)}, u32[]{:S(2)}) copy-start(s32[1,4,6]{2,1,0:T(4,128)} %param.11) | copy-start | bytes 292
  94.3 1.5 copy-start.4
  100.0 1.7 copy-start.5
  106.5 5.2 %collective-permute-start.9 = (bf16[512,384]{1,0:T(8,128)(2,1)S(1)}, bf16[512,384]{1,0:T(8,128)(2,1)S(1)}, u32[]{:S(2)}, u32[]{:S(2)}) collective-permute-start(bf16[512,384]{1,0:T(8,128)(2,1)S(1)} %attend.2.refs_0_), channel_id=1, source_target_pairs={{0,2},{2,0},{4,6},{6,4},{1,3},{3,1},{5,7},{7,5},{8,10},{10,8},{12,... | collective-permute-start | bytes 1179656 | tf_op jit(solution)/shard_map/ppermute | solution.py:26
  114.1 9.2 %collective-permute-start.11 = (bf16[2,128,512]{2,1,0:T(8,128)(2,1)S(1)}, bf16[2,128,512]{2,1,0:T(8,128)(2,1)S(1)}, u32[]{:S(2)}, u32[]{:S(2)}) collective-permute-start(bf16[2,128,512]{2,1,0:T(8,128)(2,1)S(1)} %get-tuple-element.42), channel_id=1, source_target_pairs={{0,1},{1,0},{2,3},{3,2},{4,5},{5,4},{6,7},{7,6},{8,9},{9,8},{10,11... | collective-permute-start | bytes 786440 | tf_op jit(solution)/shard_map/ppermute | solution.py:26
  115.1 9.1 %collective-permute-start.12 = (bf16[2,128,512]{2,1,0:T(8,128)(2,1)S(1)}, bf16[2,128,512]{2,1,0:T(8,128)(2,1)S(1)}, u32[]{:S(2)}, u32[]{:S(2)}) collective-permute-start(bf16[2,128,512]{2,1,0:T(8,128)(2,1)S(1)} %get-tuple-element.43), channel_id=1, source_target_pairs={{0,4},{2,6},{4,0},{6,2},{1,5},{3,7},{5,1},{7,3},{8,12},{10,14},{12... | collective-permute-start | bytes 786440 | tf_op jit(solution)/shard_map/ppermute | solution.py:26
  118.1 10.8 %collective-permute-start.15 = (bf16[2,128,512]{2,1,0:T(8,128)(2,1)S(1)}, bf16[2,128,512]{2,1,0:T(8,128)(2,1)S(1)}, u32[]{:S(2)}, u32[]{:S(2)}) collective-permute-start(bf16[2,128,512]{2,1,0:T(8,128)(2,1)S(1)} %get-tuple-element.53), channel_id=1, source_target_pairs={{0,1},{1,0},{2,3},{3,2},{4,5},{5,4},{6,7},{7,6},{8,9},{9,8},{10,11... | collective-permute-start | bytes 786440 | tf_op jit(solution)/shard_map/ppermute | solution.py:26
  119.5 9.8 %collective-permute-start.16 = (bf16[2,128,512]{2,1,0:T(8,128)(2,1)S(1)}, bf16[2,128,512]{2,1,0:T(8,128)(2,1)S(1)}, u32[]{:S(2)}, u32[]{:S(2)}) collective-permute-start(bf16[2,128,512]{2,1,0:T(8,128)(2,1)S(1)} %get-tuple-element.54), channel_id=1, source_target_pairs={{0,4},{2,6},{4,0},{6,2},{1,5},{3,7},{5,1},{7,3},{8,12},{10,14},{12... | collective-permute-start | bytes 786440 | tf_op jit(solution)/shard_map/ppermute | solution.py:26
  126.9 12.1 %collective-permute-start.13 = (bf16[3,128,512]{2,1,0:T(8,128)(2,1)S(1)}, bf16[3,128,512]{2,1,0:T(8,128)(2,1)S(1)}, u32[]{:S(2)}, u32[]{:S(2)}) collective-permute-start(bf16[3,128,512]{2,1,0:T(8,128)(2,1)S(1)} %get-tuple-element.47), channel_id=1, source_target_pairs={{0,1},{1,0},{2,3},{3,2},{4,5},{5,4},{6,7},{7,6},{8,9},{9,8},{10,11... | collective-permute-start | bytes 1179656 | tf_op jit(solution)/shard_map/ppermute | solution.py:26
  128.0 12.1 %collective-permute-start.14 = (bf16[3,128,512]{2,1,0:T(8,128)(2,1)S(1)}, bf16[3,128,512]{2,1,0:T(8,128)(2,1)S(1)}, u32[]{:S(2)}, u32[]{:S(2)}) collective-permute-start(bf16[3,128,512]{2,1,0:T(8,128)(2,1)S(1)} %get-tuple-element.48), channel_id=1, source_target_pairs={{0,4},{2,6},{4,0},{6,2},{1,5},{3,7},{5,1},{7,3},{8,12},{10,14},{12... | collective-permute-start | bytes 1179656 | tf_op jit(solution)/shard_map/ppermute | solution.py:26
  131.9 15.6 %collective-permute-start.18 = (bf16[3,128,512]{2,1,0:T(8,128)(2,1)S(1)}, bf16[3,128,512]{2,1,0:T(8,128)(2,1)S(1)}, u32[]{:S(2)}, u32[]{:S(2)}) collective-permute-start(bf16[3,128,512]{2,1,0:T(8,128)(2,1)S(1)} %get-tuple-element.58), channel_id=1, source_target_pairs={{0,1},{1,0},{2,3},{3,2},{4,5},{5,4},{6,7},{7,6},{8,9},{9,8},{10,11... | collective-permute-start | bytes 1179656 | tf_op jit(solution)/shard_map/ppermute | solution.py:26
  133.1 15.5 %collective-permute-start.19 = (bf16[3,128,512]{2,1,0:T(8,128)(2,1)S(1)}, bf16[3,128,512]{2,1,0:T(8,128)(2,1)S(1)}, u32[]{:S(2)}, u32[]{:S(2)}) collective-permute-start(bf16[3,128,512]{2,1,0:T(8,128)(2,1)S(1)} %get-tuple-element.59), channel_id=1, source_target_pairs={{0,4},{2,6},{4,0},{6,2},{1,5},{3,7},{5,1},{7,3},{8,12},{10,14},{12... | collective-permute-start | bytes 1179656 | tf_op jit(solution)/shard_map/ppermute | solution.py:26
  142.8 12.3 %collective-permute-start.21 = (bf16[3,128,512]{2,1,0:T(8,128)(2,1)S(1)}, bf16[3,128,512]{2,1,0:T(8,128)(2,1)S(1)}, u32[]{:S(2)}, u32[]{:S(2)}) collective-permute-start(bf16[3,128,512]{2,1,0:T(8,128)(2,1)S(1)} %get-tuple-element.64), channel_id=1, source_target_pairs={{0,1},{1,0},{2,3},{3,2},{4,5},{5,4},{6,7},{7,6},{8,9},{9,8},{10,11... | collective-permute-start | bytes 1179656 | tf_op jit(solution)/shard_map/ppermute | solution.py:26
  143.9 12.0 %collective-permute-start.22 = (bf16[3,128,512]{2,1,0:T(8,128)(2,1)S(1)}, bf16[3,128,512]{2,1,0:T(8,128)(2,1)S(1)}, u32[]{:S(2)}, u32[]{:S(2)}) collective-permute-start(bf16[3,128,512]{2,1,0:T(8,128)(2,1)S(1)} %get-tuple-element.65), channel_id=1, source_target_pairs={{0,4},{2,6},{4,0},{6,2},{1,5},{3,7},{5,1},{7,3},{8,12},{10,14},{12... | collective-permute-start | bytes 1179656 | tf_op jit(solution)/shard_map/ppermute | solution.py:26
  144.4 9.6 %collective-permute-start.17 = (bf16[128,1024]{1,0:T(8,128)(2,1)S(1)}, bf16[128,1024]{1,0:T(8,128)(2,1)S(1)}, u32[]{:S(2)}, u32[]{:S(2)}) collective-permute-start(bf16[128,1024]{1,0:T(8,128)(2,1)S(1)} %get-tuple-element.57.refs_8_), channel_id=1, source_target_pairs={{0,8},{8,16},{16,24},{24,0},{1,9},{9,17},{17,25},{25,1},{2,10},{10... | collective-permute-start | bytes 786440 | tf_op jit(solution)/shard_map/ppermute | solution.py:21
  148.7 11.2 %collective-permute-start.20 = (bf16[128,1024]{1,0:T(8,128)(2,1)S(1)}, bf16[128,1024]{1,0:T(8,128)(2,1)S(1)}, u32[]{:S(2)}, u32[]{:S(2)}) collective-permute-start(bf16[128,1024]{1,0:T(8,128)(2,1)S(1)} %get-tuple-element.63.refs_8_), channel_id=1, source_target_pairs={{0,8},{8,16},{16,24},{24,0},{1,9},{9,17},{17,25},{25,1},{2,10},{10... | collective-permute-start | bytes 786440 | tf_op jit(solution)/shard_map/ppermute | solution.py:21
  150.4 8.4 %collective-permute-start.24 = (bf16[1,128,512]{2,1,0:T(8,128)(2,1)S(1)}, bf16[1,128,512]{2,1,0:T(8,128)(2,1)S(1)}, u32[]{:S(2)}, u32[]{:S(2)}) collective-permute-start(bf16[1,128,512]{2,1,0:T(8,128)(2,1)S(1)} %get-tuple-element.71), channel_id=1, source_target_pairs={{0,1},{1,0},{2,3},{3,2},{4,5},{5,4},{6,7},{7,6},{8,9},{9,8},{10,11... | collective-permute-start | bytes 393224 | tf_op jit(solution)/shard_map/ppermute | solution.py:26
  154.0 5.9 %collective-permute-start.25 = (bf16[1,128,512]{2,1,0:T(8,128)(2,1)S(1)}, bf16[1,128,512]{2,1,0:T(8,128)(2,1)S(1)}, u32[]{:S(2)}, u32[]{:S(2)}) collective-permute-start(bf16[1,128,512]{2,1,0:T(8,128)(2,1)S(1)} %get-tuple-element.72), channel_id=1, source_target_pairs={{0,4},{2,6},{4,0},{6,2},{1,5},{3,7},{5,1},{7,3},{8,12},{10,14},{12... | collective-permute-start | bytes 393224 | tf_op jit(solution)/shard_map/ppermute | solution.py:26
  156.1 10.5 %collective-permute-start.23 = (bf16[128,1024]{1,0:T(8,128)(2,1)S(1)}, bf16[128,1024]{1,0:T(8,128)(2,1)S(1)}, u32[]{:S(2)}, u32[]{:S(2)}) collective-permute-start(bf16[128,1024]{1,0:T(8,128)(2,1)S(1)} %get-tuple-element.70.refs_6_), channel_id=1, source_target_pairs={{0,8},{8,16},{16,24},{24,0},{1,9},{9,17},{17,25},{25,1},{2,10},{10... | collective-permute-start | bytes 786440 | tf_op jit(solution)/shard_map/ppermute | solution.py:21
  157.7 5.0 %collective-permute-start.27 = (bf16[1,128,512]{2,1,0:T(8,128)(2,1)S(1)}, bf16[1,128,512]{2,1,0:T(8,128)(2,1)S(1)}, u32[]{:S(2)}, u32[]{:S(2)}) collective-permute-start(bf16[1,128,512]{2,1,0:T(8,128)(2,1)S(1)} %get-tuple-element.75), channel_id=1, source_target_pairs={{0,1},{1,0},{2,3},{3,2},{4,5},{5,4},{6,7},{7,6},{8,9},{9,8},{10,11... | collective-permute-start | bytes 393224 | tf_op jit(solution)/shard_map/ppermute | solution.py:26
  158.7 5.0 %collective-permute-start.28 = (bf16[1,128,512]{2,1,0:T(8,128)(2,1)S(1)}, bf16[1,128,512]{2,1,0:T(8,128)(2,1)S(1)}, u32[]{:S(2)}, u32[]{:S(2)}) collective-permute-start(bf16[1,128,512]{2,1,0:T(8,128)(2,1)S(1)} %get-tuple-element.76), channel_id=1, source_target_pairs={{0,4},{2,6},{4,0},{6,2},{1,5},{3,7},{5,1},{7,3},{8,12},{10,14},{12... | collective-permute-start | bytes 393224 | tf_op jit(solution)/shard_map/ppermute | solution.py:26
  159.9 11.0 %collective-permute-start.26 = (bf16[128,1024]{1,0:T(8,128)(2,1)S(1)}, bf16[128,1024]{1,0:T(8,128)(2,1)S(1)}, u32[]{:S(2)}, u32[]{:S(2)}) collective-permute-start(bf16[128,1024]{1,0:T(8,128)(2,1)S(1)} %sum_stage.16.refs_6_), channel_id=1, source_target_pairs={{0,8},{8,16},{16,24},{24,0},{1,9},{9,17},{17,25},{25,1},{2,10},{10... | collective-permute-start | bytes 786440 | tf_op jit(solution)/shard_map/ppermute | solution.py:21
  163.8 10.0 %collective-permute-start.29 = (bf16[128,1024]{1,0:T(8,128)(2,1)S(1)}, bf16[128,1024]{1,0:T(8,128)(2,1)S(1)}, u32[]{:S(2)}, u32[]{:S(2)}) collective-permute-start(bf16[128,1024]{1,0:T(8,128)(2,1)S(1)} %sum_stage.17), channel_id=1, source_target_pairs={{0,8},{8,16},{16,24},{24,0},{1,9},{9,17},{17,25},{25,1},{2,10},{10... | collective-permute-start | bytes 786440 | tf_op jit(solution)/shard_map/ppermute | solution.py:21
  173.8 1.1 copy-start.11

commit v9 on v8

--- a/solution.py
+++ b/solution.py
@@ -10,7 +10,7 @@
 HD = 128
 TILE = 128
 MIB = 2**20
-COLUMN_CHUNKS = 5
+CHUNK_SHARES = (4, 4, 4, 4, 2, 2)
 
 guidance_scale = 5.0
 SHORT = pl.CostEstimate(flops=1, bytes_accessed=1, transcendentals=0)
@@ -29,24 +29,27 @@
 def norm_kernel(*refs):
     *parts, modulation_ref, out_ref = refs
     step = 16
-
-    def body(index, carry):
-        rows = pl.ds(pl.multiple_of(index * step, step), step)
-        values = [part[rows, :].astype(jnp.float32) for part in parts]
-        values = jnp.concatenate(values, axis=1) if len(values) > 1 else values[0]
-        centre = values - jnp.mean(values, axis=-1, keepdims=True)
-        spread = jnp.mean(centre * centre, axis=-1, keepdims=True)
-        normed = centre * lax.rsqrt(spread + 1e-06)
-        out_ref[rows, :] = (
-            normed * (1.0 + modulation_ref[1:2, :]) + modulation_ref[0:1, :]
-        ).astype(jnp.bfloat16)
-        return carry
-
-    lax.fori_loop(0, out_ref.shape[0] // step, body, 0)
+    start = 0
+    for part in parts:
+
+        def body(index, carry, part=part, start=start):
+            rows = pl.ds(pl.multiple_of(index * step, step), step)
+            out_rows = pl.ds(pl.multiple_of(start + index * step, step), step)
+            values = part[rows, :].astype(jnp.float32)
+            centre = values - jnp.mean(values, axis=-1, keepdims=True)
+            spread = jnp.mean(centre * centre, axis=-1, keepdims=True)
+            normed = centre * lax.rsqrt(spread + 1e-06)
+            out_ref[out_rows, :] = (
+                normed * (1.0 + modulation_ref[1:2, :]) + modulation_ref[0:1, :]
+            ).astype(jnp.bfloat16)
+            return carry
+
+        lax.fori_loop(0, part.shape[0] // step, body, 0)
+        start += part.shape[0]
 
 
 def modulated_norm(parts, modulation):
-    rows, features = parts[0].shape[0], modulation.shape[1]
+    rows, features = sum(part.shape[0] for part in parts), modulation.shape[1]
     return pl.pallas_call(
         norm_kernel,
         in_specs=[pl.BlockSpec(memory_space=pltpu.VMEM)] * (len(parts) + 1),
@@ -185,7 +188,7 @@
             out_ref[out_rows, columns] = (mixed / total).astype(jnp.bfloat16)
         return carry
 
-    lax.fori_loop(0, out_ref.shape[0] // TILE, body, 0, unroll=2)
+    lax.fori_loop(0, out_ref.shape[0] // TILE, body, 0)
 
 
 def attend(heads, context, visible, first_block, earlier):
@@ -202,24 +205,6 @@
     )(visible, heads, context, *earlier)
 
 
-def half_kernel(rows_ref, *refs, start):
-    half_ref = refs[-1]
-    half_ref[...] = rows_ref[:, start : start + half_ref.shape[1]]
-
-
-def half_of(rows, start, earlier):
-    count, columns = rows.shape
-    return pl.pallas_call(
-        functools.partial(half_kernel, start=start),
-        in_specs=[pl.BlockSpec(memory_space=pltpu.VMEM)]
-        + [pl.BlockSpec(memory_space=pl.ANY)] * len(earlier),
-        out_shape=jax.ShapeDtypeStruct((count, columns // 2), rows.dtype),
-        name="half_of",
-        cost_estimate=SHORT,
-        compiler_params=pltpu.CompilerParams(vmem_limit_bytes=8 * MIB),
-    )(rows, *earlier)
-
-
 def combined(own, other, mine, gates_ref, columns):
     conditional = lax.axis_index("cfg") == 1
     last = lax.axis_index("pipe") == lax.axis_size("pipe") - 1
@@ -245,16 +230,18 @@
     columns = slice(start, start + half)
     product = product_of(slice(0, half))
     for tile in range(2):
+        sent_columns = slice(tile * half, (tile + 1) * half)
         own = product[2 * tile * tokens : (2 * tile + 1) * tokens]
         other = product[(2 * tile + 1) * tokens : (2 * tile + 2) * tokens]
         mine = rows_ref[:, columns].astype(jnp.float32) if tile == 0 else None
         sent, kept = combined(own, other, mine, gates_ref, columns)
-        across_out[tile] = sent.astype(jnp.bfloat16)
+        across_out[:, sent_columns] = sent.astype(jnp.bfloat16)
         first_kept[tile] = kept
     product = product_of(slice(half, 2 * half))
     for branch in range(2):
+        sent_columns = slice(branch * half, (branch + 1) * half)
         second_kept[branch] = product[branch * tokens : (branch + 1) * tokens]
-        along_out[branch] = product[(branch + 2) * tokens : (branch + 3) * tokens].astype(
+        along_out[:, sent_columns] = product[(branch + 2) * tokens : (branch + 3) * tokens].astype(
             jnp.bfloat16
         )
 
@@ -279,49 +266,51 @@
         across, along = named["across"], named["along"]
         first_kept, second_kept = named["first_kept"], named["second_kept"]
         half = first_kept.shape[2]
-        place = 2 if fresh else 0
-        named["along_out"][place] = (first_kept[1] + across[1].astype(jnp.float32)).astype(
-            jnp.bfloat16
-        )
-        named["first_left_out"][...] = first_kept[0] + across[0].astype(jnp.float32)
+        sent_columns = slice(named["across_out"].shape[1] - half, named["across_out"].shape[1])
+        named["along_out"][:, sent_columns] = (
+            first_kept[1] + across[:, half : 2 * half].astype(jnp.float32)
+        ).astype(jnp.bfloat16)
+        named["first_left_out"][...] = first_kept[0] + across[:, :half].astype(jnp.float32)
         columns = slice(start + half, start + 2 * half)
         sent, kept = combined(
-            second_kept[0] + along[0].astype(jnp.float32),
-            second_kept[1] + along[1].astype(jnp.float32),
+            second_kept[0] + along[:, :half].astype(jnp.float32),
+            second_kept[1] + along[:, half : 2 * half].astype(jnp.float32),
             named["rows"][:, columns].astype(jnp.float32),
             named["gates"],
             columns,
         )
-        named["across_out"][place] = sent.astype(jnp.bfloat16)
+        named["across_out"][:, sent_columns] = sent.astype(jnp.bfloat16)
         named["second_left_out"][...] = kept
     if final:
         across, along = named["across"], named["along"]
         first_left, second_left = named["first_left"], named["second_left"]
         half = first_left.shape[1]
-        place = 2 if middle else 0
+        columns = slice(across.shape[1] - half, across.shape[1])
         named["done_out"][:, :half] = (
-            first_left[...] + along[place].astype(jnp.float32)
+            first_left[...] + along[:, columns].astype(jnp.float32)
         ).astype(jnp.bfloat16)
         named["done_out"][:, half:] = (
-            second_left[...] + across[place].astype(jnp.float32)
+            second_left[...] + across[:, columns].astype(jnp.float32)
         ).astype(jnp.bfloat16)
 
 
-def stage(operands, earlier, chunk, start, next_start, fresh, middle, final):
-    tokens, half = operands["rows"].shape[0], chunk // 2
+def stage(operands, earlier, chunks, index, fresh, middle, final):
+    tokens = operands["rows"].shape[0]
+    next_start, next_chunk = chunks[index + 2] if fresh else (0, 0)
+    start, chunk = chunks[index] if middle else (0, 0)
     outs = {}
     if fresh or middle:
-        pieces = 2 * fresh + middle
-        outs["across_out"] = jax.ShapeDtypeStruct((pieces, tokens, half), jnp.bfloat16)
+        columns = next_chunk + chunk // 2
+        outs["across_out"] = jax.ShapeDtypeStruct((tokens, columns), jnp.bfloat16)
         outs["along_out"] = outs["across_out"]
     if fresh:
-        outs["first_kept_out"] = jax.ShapeDtypeStruct((2, tokens, half), jnp.float32)
+        outs["first_kept_out"] = jax.ShapeDtypeStruct((2, tokens, next_chunk // 2), jnp.float32)
         outs["second_kept_out"] = outs["first_kept_out"]
     if middle:
-        outs["first_left_out"] = jax.ShapeDtypeStruct((tokens, half), jnp.float32)
+        outs["first_left_out"] = jax.ShapeDtypeStruct((tokens, chunk // 2), jnp.float32)
         outs["second_left_out"] = outs["first_left_out"]
     if final:
-        outs["done_out"] = jax.ShapeDtypeStruct((tokens, chunk), jnp.bfloat16)
+        outs["done_out"] = jax.ShapeDtypeStruct((tokens, chunks[index - 2][1]), jnp.bfloat16)
     parts = list(operands) + ["earlier"] * len(earlier) + list(outs)
     results = pl.pallas_call(
         functools.partial(
@@ -335,7 +324,7 @@
         ),
         grid=(1,),
         in_specs=[
-            pl.BlockSpec((array.shape[0], chunk), lambda step: (0, next_start // chunk))
+            pl.BlockSpec((array.shape[0], next_chunk), lambda step: (0, next_start // next_chunk))
             if name in ("weights", "core_weights")
             else pl.BlockSpec(memory_space=pltpu.VMEM)
             for name, array in operands.items()
@@ -361,23 +350,21 @@
     packed = stale_cache[0, 0].reshape(context_rows, 2, devices, width)
     packed = packed.transpose(2, 0, 1, 3).reshape(devices, context_rows, 2 * width)
 
-    across = from_partner(current, "cfg", 1)
-    along = from_partner(current, "sp", 2)
+    upper, lower = current[: token_rows // 2], current[token_rows // 2 :]
+    across_upper, along_lower = from_partner(upper, "cfg", 1), from_partner(lower, "sp", 2)
+    across_lower, along_upper = from_partner(lower, "cfg", 1), from_partner(upper, "sp", 2)
     other_modulate = from_partner(modulate, "cfg", 1)
-    own = modulated_norm([current], modulate)
-    middle = features // 2
-    first = from_partner(half_of(across, 0, (packed, other_modulate)), "sp", 2)
-    second = from_partner(half_of(along, middle, (packed, other_modulate)), "cfg", 1)
+    first, second = from_partner(across_upper, "sp", 2), from_partner(along_lower, "cfg", 1)
     core_weights = from_partner(project_out[0], "sp", 1)
     near = [
-        own,
-        modulated_norm([across], other_modulate),
-        modulated_norm([along], modulate),
+        modulated_norm([current], modulate),
+        modulated_norm([across_upper, across_lower], other_modulate),
+        modulated_norm([along_upper, along_lower], modulate),
         modulated_norm([first, second], other_modulate),
     ]
     far = [from_partner(rows, "sp", 1) for rows in near]
 
-    packed = after(packed, (first, second, near[0]))
+    packed = after(packed, (across_lower, along_upper, other_modulate))
     context = lax.all_to_all(packed, ("sp", "cfg"), split_axis=0, concat_axis=0, tiled=True)
     context = context.reshape(devices * context_rows, 2 * width)
 
@@ -387,8 +374,11 @@
     core_attended = from_partner(for_core, "sp", 1)
     attended = attend(heads, context, visible[0], 0, (for_core, gates))
 
-    count = COLUMN_CHUNKS
-    chunk = features // count
+    count = len(CHUNK_SHARES)
+    unit = features // sum(CHUNK_SHARES)
+    chunks = [
+        (sum(CHUNK_SHARES[:index]) * unit, share * unit) for index, share in enumerate(CHUNK_SHARES)
+    ]
     kept, left, flights, arrivals, earlier = {}, {}, {}, [], []
     for index in range(-2, count + 2):
         fresh, middle, final = index + 2 < count, 0 <= index < count, index >= 2
@@ -409,9 +399,8 @@
         outs = stage(
             operands,
             earlier,
-            chunk,
-            max(index, 0) * chunk,
-            (index + 2) * chunk,
+            chunks,
+            index,
             fresh,
             middle,
             final,

time: 176 us -> 170 us (0.966)
  waiting for transfers between devices: 52.1 us -> 40.6 us
  starting transfers between devices: 34.3 us -> 41.5 us
  local copies, waits for them, and re-layouts: 33.4 us -> 31.5 us
    ppermute x25 -> x29, starting transfers between devices: 22.2 us -> 30.2 us  [from_partner(): return lax.ppermute(value, axis, pairs)]
    ppermute x25 -> x29, waiting for transfers between devices: 36.9 us -> 29.7 us  [from_partner(): return lax.ppermute(value, axis, pairs)]
    all_to_all x1, waiting for transfers between devices: 4.24 us -> 0.74 us  [per_device(): lax.all_to_all(packed, ('sp', 'cfg'), split_axis=0, concat_axis=0, tiled=...]
    unnamed x29 -> x26, local copies, waits for them, and re-layouts: 10.7 us -> 7.99 us
    ppermute x5 -> x6, starting transfers between devices: 7.49 us -> 6.47 us  [from_behind(): return lax.ppermute(x, axis, [(i, (i + by) % count) for i in range(count)])]
    ppermute x5 -> x6, waiting for transfers between devices: 11 us -> 10.1 us  [from_behind(): return lax.ppermute(x, axis, [(i, (i + by) % count) for i in range(count)])]
    pallas_call x9 -> x10, Pallas kernels: 13.4 us -> 13.2 us  [stage(): pl.pallas_call(functools.partial(stage_kernel, parts=parts, start=start,...]
  transfers between devices with their start and end apart: 31 -> 36, of which waited for: 21 -> 18; matrix products, arithmetic and copies ran while one was open for 14% -> 13% of each run, Pallas kernels for 30% -> 31%
where the time goes in v9:
time: 170 us; the launch traced here: 169 us
  Pallas kernels  54.9 us (32%)
  starting transfers between devices  41.5 us (24%)
  waiting for transfers between devices  40.6 us (24%)
  local copies, waits for them, and re-layouts  31.5 us (19%)
    ppermute x29, starting transfers between devices, from_partner(): return lax.ppermute(value, axis, pairs)  30.2 us
    ppermute x29, waiting for transfers between devices, from_partner(): return lax.ppermute(value, axis, pairs)  29.7 us
    pallas_call x1, Pallas kernels, project(): pl.pallas_call(project_kernel, grid=(steps,), in_specs=[pl.BlockSpec(memo...  18.7 us
    another operation x2, local copies, waits for them, and re-layouts, per_device(): packed = stale_cache[0, 0].reshape(context_rows, 2, devices, width)  14 us
    pallas_call x10, Pallas kernels, stage(): pl.pallas_call(functools.partial(stage_kernel, parts=parts, start=start,...  13.2 us
    pallas_call x4, Pallas kernels, modulated_norm(): pl.pallas_call(norm_kernel, in_specs=[pl.BlockSpec(memory_space=pltpu.VME...  12.2 us
    pallas_call x2, Pallas kernels, attend(): pl.pallas_call(functools.partial(attend_kernel, first_block=first_block),...  10.8 us
    ppermute x6, waiting for transfers between devices, from_behind(): return lax.ppermute(x, axis, [(i, (i + by) % count) for i in range(count)])  10.1 us
  transfers between devices with their start and end apart: 36, of which 18 were waited for; matrix products, arithmetic and copies ran while one was open for 13% of the time, Pallas kernels for 31%

profile of v9, /device:TPU:0, one launch (start us, length us, event | category | flops | bytes accessed | tf_op | source)
XLA Modules:
  0.0 168.8 jit_solution(6607227754887864201)
XLA Ops:
  0.0 1.4 slice_bitcast_fusion
  1.4 3.0 %collective-permute-start.1 = (bf16[64,5120]{1,0:T(8,128)(2,1)S(1)}, bf16[64,5120]{1,0:T(8,128)(2,1)}, u32[]{:S(2)}, u32[]{:S(2)}) collective-permute-start(bf16[64,5120]{1,0:T(8,128)(2,1)S(1)} %get-tuple-element.94), channel_id=1, source_target_pairs={{0,1},{1,0},{2,3},{3,2},{4,5},{5,4},{6,7},{7,6},{8,9},{9,8},{10,11... | collective-permute-start | bytes 1966088 | tf_op jit(solution)/shard_map/ppermute | solution.py:26
  4.4 1.5 collective-permute-start.4
  5.9 0.6 collective-permute-start
  6.5 1.5 collective-permute-start.2
  8.5 13.2 %collective-permute-done.refs_2_ = f32[3,5120]{1,0:T(4,128)S(1)} collective-permute-done((f32[3,5120]{1,0:T(4,128)S(1)}, f32[3,5120]{1,0:T(4,128)S(1)}, u32[]{:S(2)}, u32[]{:S(2)}) %collective-permute-start) | collective-permute-done | bytes 61472 | tf_op jit(solution)/shard_map/ppermute | solution.py:26
  21.7 2.1 %collective-permute-start.5 = (bf16[64,5120]{1,0:T(8,128)(2,1)}, bf16[64,5120]{1,0:T(8,128)(2,1)}, u32[]{:S(2)}, u32[]{:S(2)}) collective-permute-start(bf16[64,5120]{1,0:T(8,128)(2,1)} %collective-permute-done.1.refs_0_), channel_id=1, source_target_pairs={{0,4},{2,6},{4,0},{6,2},{1,5},{3,7},{5,1},{7,3},{8,12},{10,14},{12... | collective-permute-start | bytes 1966088 | tf_op jit(solution)/shard_map/ppermute | solution.py:26
  23.8 1.5 collective-permute-start.6
  25.3 8.0 %reshape_squeeze.3 = bf16[256,2,8,384]{3,2,1,0:T(8,128)(2,1)} reshape(bf16[1,1,256,2,3072]{4,3,2,1,0:T(2,128)(2,1)} %param.10) | data formatting | bytes 6291456 | tf_op jit(solution)/shard_map/reshape;squeeze | solution.py:350
  33.3 6.0 %copy.12 = bf16[256,2,8,384]{3,1,0,2:T(2,128)(2,1)} copy(bf16[256,2,8,384]{3,2,1,0:T(8,128)(2,1)} %reshape_squeeze.3) | data formatting | bytes 6291456 | tf_op jit(solution)/shard_map/reshape;squeeze | solution.py:350
  39.3 8.1 %reshape.9.value_ref = bf16[8,256,768]{2,1,0:T(8,128)(2,1)} reshape(bf16[8,256,2,384]{3,2,1,0:T(2,128)(2,1)} %bitcast.41) | data formatting | bytes 6291456 | tf_op jit(solution)/shard_map/reshape | solution.py:351
  47.4 1.9 %copy-done.2 = bf16[8,256,768]{2,1,0:T(8,128)(2,1)S(1)} copy-done((bf16[8,256,768]{2,1,0:T(8,128)(2,1)S(1)}, bf16[8,256,768]{2,1,0:T(8,128)(2,1)}, u32[]{:S(2)}) %copy-start.2) | copy-done | bytes 3145752
  49.2 1.8 %copy-done.3 = bf16[8,256,768]{2,1,0:T(8,128)(2,1)} copy-done((bf16[8,256,768]{2,1,0:T(8,128)(2,1)}, bf16[8,256,768]{2,1,0:T(8,128)(2,1)S(1)}, u32[]{:S(2)}) %copy-start.3) | copy-done | bytes 3145752
  51.0 4.8 %all-to-all-start = ((bf16[8,256,768]{2,1,0:T(8,128)(2,1)}), bf16[8,256,768]{2,1,0:T(8,128)(2,1)}, u32[]{:S(2)}, u32[]{:S(2)}) async-start(bf16[8,256,768]{2,1,0:T(8,128)(2,1)} %copy-done.3), calls=%async_computation | async-start | bytes 6291456 | tf_op jit(solution)/shard_map/all_to_all | solution.py:368
  55.8 2.5 %modulated_norm.4.refs_0_ = bf16[128,5120]{1,0:T(8,128)(2,1)S(1)} custom-call(bf16[128,5120]{1,0:T(8,128)(2,1)S(1)} %bitcast.18, f32[3,5120]{1,0:T(4,128)S(1)} %bitcast.37), custom_call_target="tpu_custom_call" | custom-call | flops 1 | bytes 1 | tf_op jit(solution)/shard_map/modulated_norm/pallas_call | solution.py:53
  58.5 3.5 %modulated_norm.5.refs_1_ = bf16[128,5120]{1,0:T(8,128)(2,1)S(1)} custom-call(bf16[64,5120]{1,0:T(8,128)(2,1)} %collective-permute-done.1.refs_0_, bf16[64,5120]{1,0:T(8,128)(2,1)S(1)} %collective-permute-done.2.refs_1_.refs_0_, f32[3,5120]{1,0:T(4,128)S(1)} %collective-permute-done.refs_2_), custom_call_target="tpu_custom_call" | custom-call | flops 1 | bytes 1 | tf_op jit(solution)/shard_map/modulated_norm/pallas_call | solution.py:53
  62.5 2.4 %modulated_norm.6.refs_2_ = bf16[128,5120]{1,0:T(8,128)(2,1)S(1)} custom-call(bf16[64,5120]{1,0:T(8,128)(2,1)S(1)} %collective-permute-done.3.refs_0_.refs_1_, bf16[64,5120]{1,0:T(8,128)(2,1)S(1)} %collective-permute-done.4.refs_1_, f32[3,5120]{1,0:T(4,128)S(1)} %bitcast.38), custom_call_target="tpu_custom_call" | custom-call | flops 1 | bytes 1 | tf_op jit(solution)/shard_map/modulated_norm/pallas_call | solution.py:53
  65.2 3.7 %modulated_norm.7.refs_3_ = bf16[128,5120]{1,0:T(8,128)(2,1)S(1)} custom-call(bf16[64,5120]{1,0:T(8,128)(2,1)} %collective-permute-done.5.refs_0_, bf16[64,5120]{1,0:T(8,128)(2,1)} %collective-permute-done.6.refs_1_, f32[3,5120]{1,0:T(4,128)S(1)} %collective-permute-done.refs_2_), custom_call_target="tpu_custom_call" | custom-call | flops 1 | bytes 1 | tf_op jit(solution)/shard_map/modulated_norm/pallas_call | solution.py:53
  69.4 2.7 %collective-permute-done.10.refs_7_ = bf16[128,5120]{1,0:T(8,128)(2,1)S(1)} collective-permute-done((bf16[128,5120]{1,0:T(8,128)(2,1)S(1)}, bf16[128,5120]{1,0:T(8,128)(2,1)S(1)}, u32[]{:S(2)}, u32[]{:S(2)}) %collective-permute-start.10) | collective-permute-done | bytes 1310752 | tf_op jit(solution)/shard_map/ppermute | solution.py:26
  72.0 18.7 %project_heads.1.heads_ref = bf16[1024,1152]{1,0:T(8,128)(2,1)S(1)} custom-call(bf16[128,5120]{1,0:T(8,128)(2,1)S(1)} %modulated_norm.4.refs_0_, bf16[128,5120]{1,0:T(8,128)(2,1)S(1)} %modulated_norm.5.refs_1_, bf16[128,5120]{1,0:T(8,128)(2,1)S(1)} %modulated_norm.6.refs_2_, bf16[128,5120]{1,0:T(8,128)(2,1)S(1)} %modulated_norm.7.refs_3_, ...), custom_call_target="tpu_custom_call" | custom-call | flops 12079595520 | bytes 22282240 | tf_op jit(solution)/shard_map/project_heads/pallas_call | solution.py:113
  90.8 1.5 copy-done.4
  92.3 0.7 all-to-all-done
  93.0 1.7 copy-done.5
  94.7 5.4 %attend.2.refs_0_ = bf16[512,384]{1,0:T(8,128)(2,1)S(1)} custom-call(s32[4,6]{1,0:T(4,128)S(1)} %bitcast.39, bf16[1024,1152]{1,0:T(8,128)(2,1)S(1)} %copy-done.5, bf16[2048,768]{1,0:T(8,128)(2,1)} %bitcast.7.context_ref), custom_call_target="tpu_custom_call" | custom-call | flops 1 | bytes 1 | tf_op jit(solution)/shard_map/attend/pallas_call | solution.py:196
  100.2 5.4 %attend.3.refs_2_ = bf16[512,384]{1,0:T(8,128)(2,1)S(1)} custom-call(s32[4,6]{1,0:T(4,128)S(1)} %bitcast.40, bf16[1024,1152]{1,0:T(8,128)(2,1)S(1)} %copy-done.6, bf16[2048,768]{1,0:T(8,128)(2,1)} %bitcast.7.context_ref, bf16[512,384]{1,0:T(8,128)(2,1)S(1)} %attend.2.refs_0_, f32[2,5120]{1,0:T(2,128)S(1)} %pad_maximum_fusion.refs_1_), custom_call_target="tpu_custom_call" | custom-call | flops 1 | bytes 1 | tf_op jit(solution)/shard_map/attend/pallas_call | solution.py:196
  105.7 2.2 %sum_stage.10 = (bf16[128,1024]{1,0:T(8,128)(2,1)S(1)}, bf16[128,1024]{1,0:T(8,128)(2,1)S(1)}, f32[2,128,512]{2,1,0:T(8,128)S(1)}, f32[2,128,512]{2,1,0:T(8,128)S(1)}) custom-call(bf16[128,5120]{1,0:T(8,128)(2,1)S(1)} %bitcast.19, f32[2,5120]{1,0:T(2,128)S(1)} %pad_maximum_fusion.refs_1_, bf16[512,384]{1,0:T(8,128)(2,1)S(1)} %attend.3.refs_2_, ...), custom_call_target="tpu_custom_call" | custom-call | flops 1 | bytes 1 | tf_op jit(solution)/shard_map/sum_stage/pallas_call | solution.py:315
  107.9 1.3 collective-permute-start.13
  109.2 1.5 collective-permute-start.14
  110.7 2.2 %sum_stage.11 = (bf16[128,1024]{1,0:T(8,128)(2,1)S(1)}, bf16[128,1024]{1,0:T(8,128)(2,1)S(1)}, f32[2,128,512]{2,1,0:T(8,128)S(1)}, f32[2,128,512]{2,1,0:T(8,128)S(1)}) custom-call(bf16[128,5120]{1,0:T(8,128)(2,1)S(1)} %bitcast.20, f32[2,5120]{1,0:T(2,128)S(1)} %pad_maximum_fusion.refs_1_, bf16[512,384]{1,0:T(8,128)(2,1)S(1)} %attend.3.refs_2_, ...), custom_call_target="tpu_custom_call" | custom-call | flops 1 | bytes 1 | tf_op jit(solution)/shard_map/sum_stage/pallas_call | solution.py:315
  112.9 0.6 collective-permute-start.17
  113.6 0.7 collective-permute-start.18
  114.3 2.8 %collective-permute-done.13.refs_6_ = bf16[128,1024]{1,0:T(8,128)(2,1)S(1)} collective-permute-done((bf16[128,1024]{1,0:T(8,128)(2,1)S(1)}, bf16[128,1024]{1,0:T(8,128)(2,1)S(1)}, u32[]{:S(2)}, u32[]{:S(2)}) %collective-permute-start.13) | collective-permute-done | bytes 262176 | tf_op jit(solution)/shard_map/ppermute | solution.py:26
  117.1 1.4 collective-permute-done.14.refs_7_
  118.4 2.4 %sum_stage.12 = (bf16[128,1536]{1,0:T(8,128)(2,1)S(1)}, bf16[128,1536]{1,0:T(8,128)(2,1)S(1)}, f32[2,128,512]{2,1,0:T(8,128)S(1)}, f32[2,128,512]{2,1,0:T(8,128)...) custom-call(bf16[128,5120]{1,0:T(8,128)(2,1)S(1)} %bitcast.21, f32[2,5120]{1,0:T(2,128)S(1)} %pad_maximum_fusion.refs_1_, ...), custom_call_target="tpu_custom_call" | custom-call | flops 1 | bytes 1 | tf_op jit(solution)/shard_map/sum_stage/pallas_call | solution.py:315
  120.8 0.8 collective-permute-start.15
  121.6 1.3 collective-permute-start.16
  123.3 2.4 %sum_stage.13 = (bf16[128,1536]{1,0:T(8,128)(2,1)S(1)}, bf16[128,1536]{1,0:T(8,128)(2,1)S(1)}, f32[2,128,512]{2,1,0:T(8,128)S(1)}, f32[2,128,512]{2,1,0:T(8,128)...) custom-call(bf16[128,5120]{1,0:T(8,128)(2,1)S(1)} %bitcast.22, f32[2,5120]{1,0:T(2,128)S(1)} %pad_maximum_fusion.refs_1_, ...), custom_call_target="tpu_custom_call" | custom-call | flops 1 | bytes 1 | tf_op jit(solution)/shard_map/sum_stage/pallas_call | solution.py:315
  125.7 1.5 collective-permute-start.20
  127.2 0.9 collective-permute-start.21
  128.1 4.9 %collective-permute-done.15.refs_6_ = bf16[128,1536]{1,0:T(8,128)(2,1)S(1)} collective-permute-done((bf16[128,1536]{1,0:T(8,128)(2,1)S(1)}, bf16[128,1536]{1,0:T(8,128)(2,1)S(1)}, u32[]{:S(2)}, u32[]{:S(2)}) %collective-permute-start.15) | collective-permute-done | bytes 393248 | tf_op jit(solution)/shard_map/ppermute | solution.py:26
  132.9 0.7 collective-permute-done.16.refs_7_
  133.7 1.9 %sum_stage.14 = (bf16[128,1024]{1,0:T(8,128)(2,1)S(1)}, bf16[128,1024]{1,0:T(8,128)(2,1)S(1)}, f32[2,128,256]{2,1,0:T(8,128)S(1)}, f32[2,128,256]{2,1,0:T(8,128)...) custom-call(bf16[128,5120]{1,0:T(8,128)(2,1)S(1)} %bitcast.23, ...), custom_call_target="tpu_custom_call" | custom-call | flops 1 | bytes 1 | tf_op jit(solution)/shard_map/sum_stage/pallas_call | solution.py:315
  135.5 1.6 collective-permute-start.19
  137.1 1.3 collective-permute-start.23
  138.4 1.5 collective-permute-start.24
  139.9 1.4 collective-permute-done.20.refs_6_
  141.4 0.7 collective-permute-done.21.refs_7_
  142.1 1.9 %sum_stage.15 = (bf16[128,1024]{1,0:T(8,128)(2,1)S(1)}, bf16[128,1024]{1,0:T(8,128)(2,1)S(1)}, f32[2,128,256]{2,1,0:T(8,128)S(1)}, f32[2,128,256]{2,1,0:T(8,128)...) custom-call(bf16[128,5120]{1,0:T(8,128)(2,1)S(1)} %bitcast.24, ...), custom_call_target="tpu_custom_call" | custom-call | flops 1 | bytes 1 | tf_op jit(solution)/shard_map/sum_stage/pallas_call | solution.py:315
  143.9 1.6 collective-permute-start.22
  145.6 1.3 collective-permute-start.26
  146.9 1.2 collective-permute-start.27
  148.3 1.6 collective-permute-start.25
  149.9 0.8 collective-permute-start.29
  150.7 2.9 %collective-permute-done.22.refs_9_ = bf16[128,1024]{1,0:T(8,128)(2,1)S(1)} collective-permute-done((bf16[128,1024]{1,0:T(8,128)(2,1)S(1)}, bf16[128,1024]{1,0:T(8,128)(2,1)S(1)}, u32[]{:S(2)}, u32[]{:S(2)}) %collective-permute-start.22) | collective-permute-done | bytes 262176 | tf_op jit(solution)/shard_map/ppermute | solution.py:21
  153.6 1.8 %collective-permute-start.30 = (bf16[128,256]{1,0:T(8,128)(2,1)S(1)}, bf16[128,256]{1,0:T(8,128)(2,1)S(1)}, u32[]{:S(2)}, u32[]{:S(2)}) collective-permute-start(bf16[128,256]{1,0:T(8,128)(2,1)S(1)} %get-tuple-element.86), channel_id=1, source_target_pairs={{0,4},{2,6},{4,0},{6,2},{1,5},{3,7},{5,1},{7,3},{8,12},{10,14},{12... | collective-permute-start | bytes 196616 | tf_op jit(solution)/shard_map/ppermute | solution.py:26
  155.9 1.3 collective-permute-start.33
  157.2 0.7 collective-permute-done.30.refs_3_
  157.9 1.3 collective-permute-done.25.refs_7_
  159.3 0.6 collective-permute-done.32.refs_2_
  160.3 1.5 collective-permute-start.34
  161.8 3.1 %collective-permute-done.28 = bf16[128,1024]{1,0:T(8,128)(2,1)S(1)} collective-permute-done((bf16[128,1024]{1,0:T(8,128)(2,1)S(1)}, bf16[128,1024]{1,0:T(8,128)(2,1)S(1)}, u32[]{:S(2)}, u32[]{:S(2)}) %collective-permute-start.28) | collective-permute-done | bytes 262176 | tf_op jit(solution)/shard_map/ppermute | solution.py:21
  164.9 1.4 collective-permute-done.31
  166.3 1.4 collective-permute-done.34
  167.7 1.0 copy-done.9
  (60 shorter events, 3.6 us)
Async XLA Ops:
  0.0 5.9 %copy-start.8 = (f32[1,1,3,5120]{3,1,2,0:T(1,128)S(1)}, f32[1,1,3,5120]{3,1,2,0:T(1,128)}, u32[]{:S(2)}) copy-start(f32[1,1,3,5120]{3,1,2,0:T(1,128)} %param.7) | copy-start | bytes 184324
  1.4 20.3 %collective-permute-start.1 = (bf16[64,5120]{1,0:T(8,128)(2,1)S(1)}, bf16[64,5120]{1,0:T(8,128)(2,1)}, u32[]{:S(2)}, u32[]{:S(2)}) collective-permute-start(bf16[64,5120]{1,0:T(8,128)(2,1)S(1)} %get-tuple-element.94), channel_id=1, source_target_pairs={{0,1},{1,0},{2,3},{3,2},{4,5},{5,4},{6,7},{7,6},{8,9},{9,8},{10,11... | collective-permute-start | bytes 1966088 | tf_op jit(solution)/shard_map/ppermute | solution.py:26
  4.4 19.4 %collective-permute-start.4 = (bf16[64,5120]{1,0:T(8,128)(2,1)S(1)}, bf16[64,5120]{1,0:T(8,128)(2,1)S(1)}, u32[]{:S(2)}, u32[]{:S(2)}) collective-permute-start(bf16[64,5120]{1,0:T(8,128)(2,1)S(1)} %get-tuple-element.93), channel_id=1, source_target_pairs={{0,4},{2,6},{4,0},{6,2},{1,5},{3,7},{5,1},{7,3},{8,12},{10,14},{12... | collective-permute-start | bytes 1966088 | tf_op jit(solution)/shard_map/ppermute | solution.py:26
  5.9 15.8 %collective-permute-start = (f32[3,5120]{1,0:T(4,128)S(1)}, f32[3,5120]{1,0:T(4,128)S(1)}, u32[]{:S(2)}, u32[]{:S(2)}) collective-permute-start(f32[3,5120]{1,0:T(4,128)S(1)} %bitcast.36), channel_id=1, source_target_pairs={{0,1},{1,0},{2,3},{3,2},{4,5},{5,4},{6,7},{7,6},{8,9},{9,8},{10,11... | collective-permute-start | bytes 184328 | tf_op jit(solution)/shard_map/ppermute | solution.py:26
  6.5 40.8 %collective-permute-start.2 = (bf16[64,5120]{1,0:T(8,128)(2,1)S(1)}, bf16[64,5120]{1,0:T(8,128)(2,1)S(1)}, u32[]{:S(2)}, u32[]{:S(2)}) collective-permute-start(bf16[64,5120]{1,0:T(8,128)(2,1)S(1)} %get-tuple-element.93), channel_id=1, source_target_pairs={{0,1},{1,0},{2,3},{3,2},{4,5},{5,4},{6,7},{7,6},{8,9},{9,8},{10,11... | collective-permute-start | bytes 1966088 | tf_op jit(solution)/shard_map/ppermute | solution.py:26
  8.0 39.3 %collective-permute-start.3 = (bf16[64,5120]{1,0:T(8,128)(2,1)S(1)}, bf16[64,5120]{1,0:T(8,128)(2,1)S(1)}, u32[]{:S(2)}, u32[]{:S(2)}) collective-permute-start(bf16[64,5120]{1,0:T(8,128)(2,1)S(1)} %get-tuple-element.94), channel_id=1, source_target_pairs={{0,4},{2,6},{4,0},{6,2},{1,5},{3,7},{5,1},{7,3},{8,12},{10,14},{12... | collective-permute-start | bytes 1966088 | tf_op jit(solution)/shard_map/ppermute | solution.py:26
  21.7 84.0 %collective-permute-start.12 = (bf16[384,5120]{1,0:T(8,128)(2,1)}, bf16[384,5120]{1,0:T(8,128)(2,1)}, u32[]{:S(2)}, u32[]{:S(2)}) collective-permute-start(bf16[384,5120]{1,0:T(8,128)(2,1)} %bitcast.29), channel_id=1, source_target_pairs={{0,2},{2,0},{4,6},{6,4},{1,3},{3,1},{5,7},{7,5},{8,10},{10,8},{12,... | collective-permute-start | bytes 11796488 | tf_op jit(solution)/shard_map/ppermute | solution.py:26
  21.7 43.2 %collective-permute-start.5 = (bf16[64,5120]{1,0:T(8,128)(2,1)}, bf16[64,5120]{1,0:T(8,128)(2,1)}, u32[]{:S(2)}, u32[]{:S(2)}) collective-permute-start(bf16[64,5120]{1,0:T(8,128)(2,1)} %collective-permute-done.1.refs_0_), channel_id=1, source_target_pairs={{0,4},{2,6},{4,0},{6,2},{1,5},{3,7},{5,1},{7,3},{8,12},{10,14},{12... | collective-permute-start | bytes 1966088 | tf_op jit(solution)/shard_map/ppermute | solution.py:26
  23.8 41.4 %collective-permute-start.6 = (bf16[64,5120]{1,0:T(8,128)(2,1)S(1)}, bf16[64,5120]{1,0:T(8,128)(2,1)}, u32[]{:S(2)}, u32[]{:S(2)}) collective-permute-start(bf16[64,5120]{1,0:T(8,128)(2,1)S(1)} %collective-permute-done.4.refs_1_), channel_id=1, source_target_pairs={{0,1},{1,0},{2,3},{3,2},{4,5},{5,4},{6,7},{7,6},{8,9},{9,8},{10,11... | collective-permute-start | bytes 1966088 | tf_op jit(solution)/shard_map/ppermute | solution.py:26
  47.3 1.9 %copy-start.2 = (bf16[8,256,768]{2,1,0:T(8,128)(2,1)S(1)}, bf16[8,256,768]{2,1,0:T(8,128)(2,1)}, u32[]{:S(2)}) copy-start(bf16[8,256,768]{2,1,0:T(8,128)(2,1)} %reshape.9.value_ref) | copy-start | bytes 9437188
  49.2 1.8 %copy-start.3 = (bf16[8,256,768]{2,1,0:T(8,128)(2,1)}, bf16[8,256,768]{2,1,0:T(8,128)(2,1)S(1)}, u32[]{:S(2)}) copy-start(bf16[8,256,768]{2,1,0:T(8,128)(2,1)S(1)} %after.1) | copy-start | bytes 9437188
  51.0 4.8 %copy-start = (bf16[1,1,128,5120]{3,2,1,0:T(8,128)(2,1)S(1)}, bf16[1,1,128,5120]{3,2,1,0:T(8,128)(2,1)}, u32[]{:S(2)}) copy-start(bf16[1,1,128,5120]{3,2,1,0:T(8,128)(2,1)} %param.6) | copy-start | bytes 3932164
  51.0 42.0 %all-to-all-start = ((bf16[8,256,768]{2,1,0:T(8,128)(2,1)}), bf16[8,256,768]{2,1,0:T(8,128)(2,1)}, u32[]{:S(2)}, u32[]{:S(2)}) async-start(bf16[8,256,768]{2,1,0:T(8,128)(2,1)} %copy-done.3), calls=%async_computation | async-start | bytes 6291456 | tf_op jit(solution)/shard_map/all_to_all | solution.py:368
  58.3 11.1 %collective-permute-start.7 = (bf16[128,5120]{1,0:T(8,128)(2,1)S(1)}, bf16[128,5120]{1,0:T(8,128)(2,1)S(1)}, u32[]{:S(2)}, u32[]{:S(2)}) collective-permute-start(bf16[128,5120]{1,0:T(8,128)(2,1)S(1)} %modulated_norm.4.refs_0_), channel_id=1, source_target_pairs={{0,2},{2,0},{4,6},{6,4},{1,3},{3,1},{5,7},{7,5},{8,10},{10,8},{12,... | collective-permute-start | bytes 3932168 | tf_op jit(solution)/shard_map/ppermute | solution.py:26
  62.1 7.3 %collective-permute-start.8 = (bf16[128,5120]{1,0:T(8,128)(2,1)S(1)}, bf16[128,5120]{1,0:T(8,128)(2,1)S(1)}, u32[]{:S(2)}, u32[]{:S(2)}) collective-permute-start(bf16[128,5120]{1,0:T(8,128)(2,1)S(1)} %modulated_norm.5.refs_1_), channel_id=1, source_target_pairs={{0,2},{2,0},{4,6},{6,4},{1,3},{3,1},{5,7},{7,5},{8,10},{10,8},{12,... | collective-permute-start | bytes 3932168 | tf_op jit(solution)/shard_map/ppermute | solution.py:26
  64.9 4.4 %collective-permute-start.9 = (bf16[128,5120]{1,0:T(8,128)(2,1)S(1)}, bf16[128,5120]{1,0:T(8,128)(2,1)S(1)}, u32[]{:S(2)}, u32[]{:S(2)}) collective-permute-start(bf16[128,5120]{1,0:T(8,128)(2,1)S(1)} %modulated_norm.6.refs_2_), channel_id=1, source_target_pairs={{0,2},{2,0},{4,6},{6,4},{1,3},{3,1},{5,7},{7,5},{8,10},{10,8},{12,... | collective-permute-start | bytes 3932168 | tf_op jit(solution)/shard_map/ppermute | solution.py:26
  68.9 3.1 %collective-permute-start.10 = (bf16[128,5120]{1,0:T(8,128)(2,1)S(1)}, bf16[128,5120]{1,0:T(8,128)(2,1)S(1)}, u32[]{:S(2)}, u32[]{:S(2)}) collective-permute-start(bf16[128,5120]{1,0:T(8,128)(2,1)S(1)} %modulated_norm.7.refs_3_), channel_id=1, source_target_pairs={{0,2},{2,0},{4,6},{6,4},{1,3},{3,1},{5,7},{7,5},{8,10},{10,8},{12,... | collective-permute-start | bytes 3932168 | tf_op jit(solution)/shard_map/ppermute | solution.py:26
  72.0 21.0 %copy-start.7 = (s32[1,4,6]{2,1,0:T(4,128)S(1)}, s32[1,4,6]{2,1,0:T(4,128)}, u32[]{:S(2)}) copy-start(s32[1,4,6]{2,1,0:T(4,128)} %param.11) | copy-start | bytes 292
  90.8 1.5 copy-start.4
  93.0 1.7 copy-start.5
  94.7 5.5 %copy-start.6 = (bf16[1024,1152]{1,0:T(8,128)(2,1)S(1)}, bf16[1024,1152]{1,0:T(8,128)(2,1)}, u32[]{:S(2)}) copy-start(bf16[1024,1152]{1,0:T(8,128)(2,1)} %copy-done.4) | copy-start | bytes 7077892
  100.1 5.5 %collective-permute-start.11 = (bf16[512,384]{1,0:T(8,128)(2,1)S(1)}, bf16[512,384]{1,0:T(8,128)(2,1)S(1)}, u32[]{:S(2)}, u32[]{:S(2)}) collective-permute-start(bf16[512,384]{1,0:T(8,128)(2,1)S(1)} %attend.2.refs_0_), channel_id=1, source_target_pairs={{0,2},{2,0},{4,6},{6,4},{1,3},{3,1},{5,7},{7,5},{8,10},{10,8},{12,... | collective-permute-start | bytes 1179656 | tf_op jit(solution)/shard_map/ppermute | solution.py:26
  100.2 5.4 %copy-start.1 = (bf16[1,384,5120]{2,1,0:T(8,128)(2,1)S(1)}, bf16[1,384,5120]{2,1,0:T(8,128)(2,1)}, u32[]{:S(2)}) copy-start(bf16[1,384,5120]{2,1,0:T(8,128)(2,1)} %param.9) | copy-start | bytes 11796484
  107.9 9.2 %collective-permute-start.13 = (bf16[128,1024]{1,0:T(8,128)(2,1)S(1)}, bf16[128,1024]{1,0:T(8,128)(2,1)S(1)}, u32[]{:S(2)}, u32[]{:S(2)}) collective-permute-start(bf16[128,1024]{1,0:T(8,128)(2,1)S(1)} %get-tuple-element.49), channel_id=1, source_target_pairs={{0,1},{1,0},{2,3},{3,2},{4,5},{5,4},{6,7},{7,6},{8,9},{9,8},{10,11... | collective-permute-start | bytes 786440 | tf_op jit(solution)/shard_map/ppermute | solution.py:26
  109.2 9.2 %collective-permute-start.14 = (bf16[128,1024]{1,0:T(8,128)(2,1)S(1)}, bf16[128,1024]{1,0:T(8,128)(2,1)S(1)}, u32[]{:S(2)}, u32[]{:S(2)}) collective-permute-start(bf16[128,1024]{1,0:T(8,128)(2,1)S(1)} %get-tuple-element.50), channel_id=1, source_target_pairs={{0,4},{2,6},{4,0},{6,2},{1,5},{3,7},{5,1},{7,3},{8,12},{10,14},{12... | collective-permute-start | bytes 786440 | tf_op jit(solution)/shard_map/ppermute | solution.py:26
  112.9 10.0 %collective-permute-start.17 = (bf16[128,1024]{1,0:T(8,128)(2,1)S(1)}, bf16[128,1024]{1,0:T(8,128)(2,1)S(1)}, u32[]{:S(2)}, u32[]{:S(2)}) collective-permute-start(bf16[128,1024]{1,0:T(8,128)(2,1)S(1)} %get-tuple-element.60), channel_id=1, source_target_pairs={{0,1},{1,0},{2,3},{3,2},{4,5},{5,4},{6,7},{7,6},{8,9},{9,8},{10,11... | collective-permute-start | bytes 786440 | tf_op jit(solution)/shard_map/ppermute | solution.py:26
  113.6 9.8 %collective-permute-start.18 = (bf16[128,1024]{1,0:T(8,128)(2,1)S(1)}, bf16[128,1024]{1,0:T(8,128)(2,1)S(1)}, u32[]{:S(2)}, u32[]{:S(2)}) collective-permute-start(bf16[128,1024]{1,0:T(8,128)(2,1)S(1)} %get-tuple-element.61), channel_id=1, source_target_pairs={{0,4},{2,6},{4,0},{6,2},{1,5},{3,7},{5,1},{7,3},{8,12},{10,14},{12... | collective-permute-start | bytes 786440 | tf_op jit(solution)/shard_map/ppermute | solution.py:26
  120.8 12.1 %collective-permute-start.15 = (bf16[128,1536]{1,0:T(8,128)(2,1)S(1)}, bf16[128,1536]{1,0:T(8,128)(2,1)S(1)}, u32[]{:S(2)}, u32[]{:S(2)}) collective-permute-start(bf16[128,1536]{1,0:T(8,128)(2,1)S(1)} %get-tuple-element.54), channel_id=1, source_target_pairs={{0,1},{1,0},{2,3},{3,2},{4,5},{5,4},{6,7},{7,6},{8,9},{9,8},{10,11... | collective-permute-start | bytes 1179656 | tf_op jit(solution)/shard_map/ppermute | solution.py:26
  121.6 12.1 %collective-permute-start.16 = (bf16[128,1536]{1,0:T(8,128)(2,1)S(1)}, bf16[128,1536]{1,0:T(8,128)(2,1)S(1)}, u32[]{:S(2)}, u32[]{:S(2)}) collective-permute-start(bf16[128,1536]{1,0:T(8,128)(2,1)S(1)} %get-tuple-element.55), channel_id=1, source_target_pairs={{0,4},{2,6},{4,0},{6,2},{1,5},{3,7},{5,1},{7,3},{8,12},{10,14},{12... | collective-permute-start | bytes 1179656 | tf_op jit(solution)/shard_map/ppermute | solution.py:26
  125.7 15.6 %collective-permute-start.20 = (bf16[128,1536]{1,0:T(8,128)(2,1)S(1)}, bf16[128,1536]{1,0:T(8,128)(2,1)S(1)}, u32[]{:S(2)}, u32[]{:S(2)}) collective-permute-start(bf16[128,1536]{1,0:T(8,128)(2,1)S(1)} %get-tuple-element.65), channel_id=1, source_target_pairs={{0,1},{1,0},{2,3},{3,2},{4,5},{5,4},{6,7},{7,6},{8,9},{9,8},{10,11... | collective-permute-start | bytes 1179656 | tf_op jit(solution)/shard_map/ppermute | solution.py:26
  127.2 14.9 %collective-permute-start.21 = (bf16[128,1536]{1,0:T(8,128)(2,1)S(1)}, bf16[128,1536]{1,0:T(8,128)(2,1)S(1)}, u32[]{:S(2)}, u32[]{:S(2)}) collective-permute-start(bf16[128,1536]{1,0:T(8,128)(2,1)S(1)} %get-tuple-element.66), channel_id=1, source_target_pairs={{0,4},{2,6},{4,0},{6,2},{1,5},{3,7},{5,1},{7,3},{8,12},{10,14},{12... | collective-permute-start | bytes 1179656 | tf_op jit(solution)/shard_map/ppermute | solution.py:26
  135.5 11.4 %collective-permute-start.19 = (bf16[128,1024]{1,0:T(8,128)(2,1)S(1)}, bf16[128,1024]{1,0:T(8,128)(2,1)S(1)}, u32[]{:S(2)}, u32[]{:S(2)}) collective-permute-start(bf16[128,1024]{1,0:T(8,128)(2,1)S(1)} %get-tuple-element.64.refs_12_), channel_id=1, source_target_pairs={{0,8},{8,16},{16,24},{24,0},{1,9},{9,17},{17,25},{25,1},{2,10},{10... | collective-permute-start | bytes 786440 | tf_op jit(solution)/shard_map/ppermute | solution.py:21
  137.1 11.0 %collective-permute-start.23 = (bf16[128,1024]{1,0:T(8,128)(2,1)S(1)}, bf16[128,1024]{1,0:T(8,128)(2,1)S(1)}, u32[]{:S(2)}, u32[]{:S(2)}) collective-permute-start(bf16[128,1024]{1,0:T(8,128)(2,1)S(1)} %get-tuple-element.71), channel_id=1, source_target_pairs={{0,1},{1,0},{2,3},{3,2},{4,5},{5,4},{6,7},{7,6},{8,9},{9,8},{10,11... | collective-permute-start | bytes 786440 | tf_op jit(solution)/shard_map/ppermute | solution.py:26
  138.4 9.7 %collective-permute-start.24 = (bf16[128,1024]{1,0:T(8,128)(2,1)S(1)}, bf16[128,1024]{1,0:T(8,128)(2,1)S(1)}, u32[]{:S(2)}, u32[]{:S(2)}) collective-permute-start(bf16[128,1024]{1,0:T(8,128)(2,1)S(1)} %get-tuple-element.72), channel_id=1, source_target_pairs={{0,4},{2,6},{4,0},{6,2},{1,5},{3,7},{5,1},{7,3},{8,12},{10,14},{12... | collective-permute-start | bytes 786440 | tf_op jit(solution)/shard_map/ppermute | solution.py:26
  143.9 9.7 %collective-permute-start.22 = (bf16[128,1024]{1,0:T(8,128)(2,1)S(1)}, bf16[128,1024]{1,0:T(8,128)(2,1)S(1)}, u32[]{:S(2)}, u32[]{:S(2)}) collective-permute-start(bf16[128,1024]{1,0:T(8,128)(2,1)S(1)} %get-tuple-element.70.refs_8_), channel_id=1, source_target_pairs={{0,8},{8,16},{16,24},{24,0},{1,9},{9,17},{17,25},{25,1},{2,10},{10... | collective-permute-start | bytes 786440 | tf_op jit(solution)/shard_map/ppermute | solution.py:21
  145.6 9.8 %collective-permute-start.26 = (bf16[128,1024]{1,0:T(8,128)(2,1)S(1)}, bf16[128,1024]{1,0:T(8,128)(2,1)S(1)}, u32[]{:S(2)}, u32[]{:S(2)}) collective-permute-start(bf16[128,1024]{1,0:T(8,128)(2,1)S(1)} %get-tuple-element.78), channel_id=1, source_target_pairs={{0,1},{1,0},{2,3},{3,2},{4,5},{5,4},{6,7},{7,6},{8,9},{9,8},{10,11... | collective-permute-start | bytes 786440 | tf_op jit(solution)/shard_map/ppermute | solution.py:26
  146.9 8.5 %collective-permute-start.27 = (bf16[128,1024]{1,0:T(8,128)(2,1)S(1)}, bf16[128,1024]{1,0:T(8,128)(2,1)S(1)}, u32[]{:S(2)}, u32[]{:S(2)}) collective-permute-start(bf16[128,1024]{1,0:T(8,128)(2,1)S(1)} %get-tuple-element.79), channel_id=1, source_target_pairs={{0,4},{2,6},{4,0},{6,2},{1,5},{3,7},{5,1},{7,3},{8,12},{10,14},{12... | collective-permute-start | bytes 786440 | tf_op jit(solution)/shard_map/ppermute | solution.py:26
  148.3 10.9 %collective-permute-start.25 = (bf16[128,1024]{1,0:T(8,128)(2,1)S(1)}, bf16[128,1024]{1,0:T(8,128)(2,1)S(1)}, u32[]{:S(2)}, u32[]{:S(2)}) collective-permute-start(bf16[128,1024]{1,0:T(8,128)(2,1)S(1)} %get-tuple-element.77.refs_8_), channel_id=1, source_target_pairs={{0,8},{8,16},{16,24},{24,0},{1,9},{9,17},{17,25},{25,1},{2,10},{10... | collective-permute-start | bytes 786440 | tf_op jit(solution)/shard_map/ppermute | solution.py:21
  149.9 6.0 %collective-permute-start.29 = (bf16[128,256]{1,0:T(8,128)(2,1)S(1)}, bf16[128,256]{1,0:T(8,128)(2,1)S(1)}, u32[]{:S(2)}, u32[]{:S(2)}) collective-permute-start(bf16[128,256]{1,0:T(8,128)(2,1)S(1)} %get-tuple-element.85), channel_id=1, source_target_pairs={{0,1},{1,0},{2,3},{3,2},{4,5},{5,4},{6,7},{7,6},{8,9},{9,8},{10,11... | collective-permute-start | bytes 196616 | tf_op jit(solution)/shard_map/ppermute | solution.py:26
  153.6 4.3 %collective-permute-start.30 = (bf16[128,256]{1,0:T(8,128)(2,1)S(1)}, bf16[128,256]{1,0:T(8,128)(2,1)S(1)}, u32[]{:S(2)}, u32[]{:S(2)}) collective-permute-start(bf16[128,256]{1,0:T(8,128)(2,1)S(1)} %get-tuple-element.86), channel_id=1, source_target_pairs={{0,4},{2,6},{4,0},{6,2},{1,5},{3,7},{5,1},{7,3},{8,12},{10,14},{12... | collective-permute-start | bytes 196616 | tf_op jit(solution)/shard_map/ppermute | solution.py:26
  155.5 4.3 %collective-permute-start.32 = (bf16[128,256]{1,0:T(8,128)(2,1)S(1)}, bf16[128,256]{1,0:T(8,128)(2,1)S(1)}, u32[]{:S(2)}, u32[]{:S(2)}) collective-permute-start(bf16[128,256]{1,0:T(8,128)(2,1)S(1)} %get-tuple-element.89), channel_id=1, source_target_pairs={{0,1},{1,0},{2,3},{3,2},{4,5},{5,4},{6,7},{7,6},{8,9},{9,8},{10,11... | collective-permute-start | bytes 196616 | tf_op jit(solution)/shard_map/ppermute | solution.py:26
  155.9 9.0 %collective-permute-start.28 = (bf16[128,1024]{1,0:T(8,128)(2,1)S(1)}, bf16[128,1024]{1,0:T(8,128)(2,1)S(1)}, u32[]{:S(2)}, u32[]{:S(2)}) collective-permute-start(bf16[128,1024]{1,0:T(8,128)(2,1)S(1)} %get-tuple-element.84.refs_6_), channel_id=1, source_target_pairs={{0,8},{8,16},{16,24},{24,0},{1,9},{9,17},{17,25},{25,1},{2,10},{10... | collective-permute-start | bytes 786440 | tf_op jit(solution)/shard_map/ppermute | solution.py:21
  155.9 4.3 %collective-permute-start.33 = (bf16[128,256]{1,0:T(8,128)(2,1)S(1)}, bf16[128,256]{1,0:T(8,128)(2,1)S(1)}, u32[]{:S(2)}, u32[]{:S(2)}) collective-permute-start(bf16[128,256]{1,0:T(8,128)(2,1)S(1)} %get-tuple-element.90), channel_id=1, source_target_pairs={{0,4},{2,6},{4,0},{6,2},{1,5},{3,7},{5,1},{7,3},{8,12},{10,14},{12... | collective-permute-start | bytes 196616 | tf_op jit(solution)/shard_map/ppermute | solution.py:26
  159.2 7.1 %collective-permute-start.31 = (bf16[128,512]{1,0:T(8,128)(2,1)S(1)}, bf16[128,512]{1,0:T(8,128)(2,1)S(1)}, u32[]{:S(2)}, u32[]{:S(2)}) collective-permute-start(bf16[128,512]{1,0:T(8,128)(2,1)S(1)} %sum_stage.18.refs_6_), channel_id=1, source_target_pairs={{0,8},{8,16},{16,24},{24,0},{1,9},{9,17},{17,25},{25,1},{2,10},{10... | collective-permute-start | bytes 393224 | tf_op jit(solution)/shard_map/ppermute | solution.py:21
  160.3 7.5 %collective-permute-start.34 = (bf16[128,512]{1,0:T(8,128)(2,1)S(1)}, bf16[128,512]{1,0:T(8,128)(2,1)S(1)}, u32[]{:S(2)}, u32[]{:S(2)}) collective-permute-start(bf16[128,512]{1,0:T(8,128)(2,1)S(1)} %sum_stage.19), channel_id=1, source_target_pairs={{0,8},{8,16},{16,24},{24,0},{1,9},{9,17},{17,25},{25,1},{2,10},{10... | collective-permute-start | bytes 393224 | tf_op jit(solution)/shard_map/ppermute | solution.py:21
  167.7 1.1 copy-start.9

commit v10 on v9

--- a/solution.py
+++ b/solution.py
@@ -77,8 +77,8 @@
     )(value, *earlier)
 
 
-def project_kernel(*refs):
-    *block_refs, weights_ref, out_ref, total_ref = refs
+def project_kernel(*refs, blocks):
+    block_refs, (weights_ref, out_ref, total_ref, heads_ref, sems) = refs[:blocks], refs[blocks:]
     step, steps = pl.program_id(0), pl.num_programs(0)
     weights = jnp.concatenate([weights_ref[0], weights_ref[1], weights_ref[2]], axis=1)
     block = weights.shape[0]
@@ -96,13 +96,20 @@
 
     @pl.when(step == steps - 1)
     def _():
-        width = weights_ref.shape[2]
-        for head in range(2 * width // HD):
-            columns = slice(head * HD, (head + 1) * HD)
-            values = total_ref[:, columns]
-            scale = lax.rsqrt(jnp.mean(values * values, axis=-1, keepdims=True) + 1e-06)
-            out_ref[:, columns] = (values * scale).astype(jnp.bfloat16)
-        out_ref[:, 2 * width :] = total_ref[:, 2 * width :].astype(jnp.bfloat16)
+        heads = heads_ref.shape[0]
+        copies = []
+        for head in range(heads):
+            values = total_ref[:, head * HD : (head + 1) * HD]
+            if head < 2 * heads // 3:
+                square = jnp.mean(values * values, axis=-1, keepdims=True)
+                values = values * lax.rsqrt(square + 1e-06)
+            heads_ref[head] = values.astype(jnp.bfloat16)
+            copies.append(
+                pltpu.make_async_copy(heads_ref.at[head], out_ref.at[head], sems.at[head])
+            )
+            copies[-1].start()
+        for copy in copies:
+            copy.wait()
 
 
 def project(blocks, weights):
@@ -110,27 +117,31 @@
     steps = 4
     block = depth // steps
     count = sum(rows.shape[0] for rows in blocks)
+    heads = 3 * width // HD
     return pl.pallas_call(
-        project_kernel,
+        functools.partial(project_kernel, blocks=len(blocks)),
         grid=(steps,),
         in_specs=[pl.BlockSpec(memory_space=pltpu.VMEM)] * len(blocks)
         + [pl.BlockSpec((3, block, width), lambda k: (0, k, 0))],
-        out_specs=pl.BlockSpec((count, 3 * width), lambda k: (0, 0)),
-        out_shape=jax.ShapeDtypeStruct((count, 3 * width), jnp.bfloat16),
-        scratch_shapes=[pltpu.VMEM((count, 3 * width), jnp.float32)],
+        out_specs=pl.BlockSpec(memory_space=pltpu.HBM),
+        out_shape=jax.ShapeDtypeStruct((heads, count, HD), jnp.bfloat16),
+        scratch_shapes=[
+            pltpu.VMEM((count, 3 * width), jnp.float32),
+            pltpu.VMEM((heads, count, HD), jnp.bfloat16),
+            pltpu.SemaphoreType.DMA((heads,)),
+        ],
         name="project_heads",
         cost_estimate=pl.CostEstimate(
             flops=2 * count * depth * 3 * width,
             bytes_accessed=2 * (count * depth + weights.size),
             transcendentals=0,
         ),
-        compiler_params=pltpu.CompilerParams(vmem_limit_bytes=40 * MIB),
+        compiler_params=pltpu.CompilerParams(vmem_limit_bytes=42 * MIB),
     )(*blocks, weights)
 
 
-def attend_kernel(visible_ref, heads_ref, context_ref, *refs, first_block):
-    out_ref = refs[-1]
-    width = heads_ref.shape[1] // 3
+def attend_head(visible_ref, heads_ref, context_ref, out_ref, first_block, head):
+    heads = heads_ref.shape[0] // 3
     tiles_seen = visible_ref.shape[1]
     tiles_fresh = visible_ref.shape[0]
     mine_high, mine_low = lax.axis_index("sp") // 2, lax.axis_index("sp") % 2
@@ -157,51 +168,84 @@
                 )
             )
 
-        def tiles(kind, head):
-            start = kind * width + head * HD
-            held_start = start - width
+        def tiles(kind):
+            start = ((kind - 1) * heads + head) * HD
             return jnp.concatenate(
                 [
                     jnp.where(
                         is_fresh,
-                        heads_ref[fresh, start : start + HD],
-                        context_ref[stale, held_start : held_start + HD],
+                        heads_ref[kind * heads + head, fresh, :],
+                        context_ref[stale, start : start + HD],
                     )
                     for is_fresh, fresh, stale in places
                 ],
                 axis=0,
             )
 
-        for head in range(width // HD):
-            columns = slice(head * HD, (head + 1) * HD)
-            scores = lax.dot_general(
-                heads_ref[rows, columns],
-                tiles(1, head),
-                (((1,), (1,)), ((), ())),
-                preferred_element_type=jnp.float32,
-            )
-            exponent = jnp.exp(scores * HD ** (-0.5))
-            total = jnp.sum(exponent, axis=-1, keepdims=True)
-            mixed = jnp.dot(
-                exponent.astype(jnp.bfloat16), tiles(2, head), preferred_element_type=jnp.float32
-            )
-            out_ref[out_rows, columns] = (mixed / total).astype(jnp.bfloat16)
+        scores = lax.dot_general(
+            heads_ref[head, rows, :],
+            tiles(1),
+            (((1,), (1,)), ((), ())),
+            preferred_element_type=jnp.float32,
+        )
+        exponent = jnp.exp(scores * HD ** (-0.5))
+        total = jnp.sum(exponent, axis=-1, keepdims=True)
+        mixed = jnp.dot(
+            exponent.astype(jnp.bfloat16), tiles(2), preferred_element_type=jnp.float32
+        )
+        out_ref[out_rows, head * HD : (head + 1) * HD] = (mixed / total).astype(jnp.bfloat16)
         return carry
 
-    lax.fori_loop(0, out_ref.shape[0] // TILE, body, 0)
+    lax.fori_loop(0, out_ref.shape[0] // TILE, body, 0, unroll=2)
+
+
+def attend_kernel(visible_ref, heads_in, context_in, *refs, first_block):
+    out_ref, heads_ref, context_ref, sems = refs[-4:]
+    heads = heads_ref.shape[0] // 3
+    copies = []
+    for head in range(heads):
+        of_head = []
+        for kind in range(3):
+            place = kind * heads + head
+            of_head.append(
+                pltpu.make_async_copy(heads_in.at[place], heads_ref.at[place], sems.at[head, kind])
+            )
+        for kind in range(2):
+            columns = pl.ds((kind * heads + head) * HD, HD)
+            of_head.append(
+                pltpu.make_async_copy(
+                    context_in.at[:, columns], context_ref.at[:, columns], sems.at[head, 3 + kind]
+                )
+            )
+        for copy in of_head:
+            copy.start()
+        copies.append(of_head)
+    for head in range(heads):
+        for copy in copies[head]:
+            copy.wait()
+        attend_head(visible_ref, heads_ref, context_ref, out_ref, first_block, head)
 
 
 def attend(heads, context, visible, first_block, earlier):
-    count, width = heads.shape[0] // 2, heads.shape[1] // 3
+    count = heads.shape[1] // 2
     return pl.pallas_call(
         functools.partial(attend_kernel, first_block=first_block),
-        in_specs=[pl.BlockSpec(memory_space=pltpu.SMEM)]
-        + [pl.BlockSpec(memory_space=pltpu.VMEM)] * 2
+        in_specs=[
+            pl.BlockSpec(memory_space=pltpu.SMEM),
+            pl.BlockSpec(memory_space=pltpu.HBM),
+            pl.BlockSpec(memory_space=pl.ANY),
+        ]
         + [pl.BlockSpec(memory_space=pl.ANY)] * len(earlier),
-        out_shape=jax.ShapeDtypeStruct((count, width), jnp.bfloat16),
+        out_specs=pl.BlockSpec(memory_space=pltpu.VMEM),
+        out_shape=jax.ShapeDtypeStruct((count, heads.shape[0] // 3 * HD), jnp.bfloat16),
+        scratch_shapes=[
+            pltpu.VMEM(heads.shape, heads.dtype),
+            pltpu.VMEM(context.shape, context.dtype),
+            pltpu.SemaphoreType.DMA((heads.shape[0] // 3, 5)),
+        ],
         name="attend",
         cost_estimate=SHORT,
-        compiler_params=pltpu.CompilerParams(vmem_limit_bytes=12 * MIB),
+        compiler_params=pltpu.CompilerParams(vmem_limit_bytes=53 * MIB),
     )(visible, heads, context, *earlier)
 
 
@@ -219,12 +263,12 @@
 
 
 def begin(start, refs, across_out, along_out, first_kept, second_kept):
-    *attended_refs, weights_ref, core_weights_ref, rows_ref, gates_ref = refs
+    attended_ref, core_attended_ref, *weights_refs, rows_ref, gates_ref = refs
     tokens, half = rows_ref.shape[0], first_kept.shape[2]
-    attended = jnp.concatenate([ref[...] for ref in attended_refs], axis=1)
+    attended = jnp.concatenate([attended_ref[...], core_attended_ref[...]], axis=1)
 
     def product_of(columns):
-        weights = jnp.concatenate([weights_ref[:, columns], core_weights_ref[:, columns]], axis=0)
+        weights = jnp.concatenate([ref[:, columns] for ref in weights_refs], axis=0)
         return jnp.dot(attended, weights, preferred_element_type=jnp.float32)
 
     columns = slice(start, start + half)
@@ -370,15 +414,15 @@
 
     heads = project(near + far, project_in[0])
     gates = jnp.concatenate([modulate[2:3], other_modulate[2:3]], axis=0)
-    for_core = attend(heads, context, visible[0], 4, ())
-    core_attended = from_partner(for_core, "sp", 1)
-    attended = attend(heads, context, visible[0], 0, (for_core, gates))
-
     count = len(CHUNK_SHARES)
     unit = features // sum(CHUNK_SHARES)
     chunks = [
         (sum(CHUNK_SHARES[:index]) * unit, share * unit) for index, share in enumerate(CHUNK_SHARES)
     ]
+    for_core = attend(heads, context, visible[0], heads.shape[1] // TILE // 2, ())
+    core_attended = from_partner(for_core, "sp", 1)
+    attended = attend(heads, context, visible[0], 0, (for_core, gates))
+
     kept, left, flights, arrivals, earlier = {}, {}, {}, [], []
     for index in range(-2, count + 2):
         fresh, middle, final = index + 2 < count, 0 <= index < count, index >= 2

time: 170 us -> 169 us (level)
  local copies, waits for them, and re-layouts: 31.5 us -> 28.2 us
  Pallas kernels: 54.9 us -> 57.5 us
  waiting for transfers between devices: 40.6 us -> 42.5 us
    unnamed x26 -> x20, local copies, waits for them, and re-layouts: 7.99 us -> 4.82 us
    ppermute x29, starting transfers between devices: 30.2 us -> 28.3 us  [from_partner(): return lax.ppermute(value, axis, pairs)]
  transfers between devices with their start and end apart: 36 -> 36, of which waited for: 18 -> 19; matrix products, arithmetic and copies ran while one was open for 13% -> 13% of each run, Pallas kernels for 31% -> 33%
where the time goes in v10:
time: 169 us
  Pallas kernels  57.5 us (34%)
  waiting for transfers between devices  42.5 us (25%)
  starting transfers between devices  40 us (24%)
  local copies, waits for them, and re-layouts  28.2 us (17%)
    ppermute x29, waiting for transfers between devices, from_partner(): return lax.ppermute(value, axis, pairs)  31 us
    ppermute x29, starting transfers between devices, from_partner(): return lax.ppermute(value, axis, pairs)  28.3 us
    pallas_call x1, Pallas kernels, project(): pl.pallas_call(functools.partial(project_kernel, blocks=len(blocks)), gri...  19.8 us
    another operation x2, local copies, waits for them, and re-layouts, per_device(): packed = stale_cache[0, 0].reshape(context_rows, 2, devices, width)  14 us
    pallas_call x10, Pallas kernels, stage(): pl.pallas_call(functools.partial(stage_kernel, parts=parts, start=start,...  13.2 us
    pallas_call x2, Pallas kernels, attend(): pl.pallas_call(functools.partial(attend_kernel, first_block=first_block),...  12.3 us
    pallas_call x4, Pallas kernels, modulated_norm(): pl.pallas_call(norm_kernel, in_specs=[pl.BlockSpec(memory_space=pltpu.VME...  12.2 us
    ppermute x6, waiting for transfers between devices, from_behind(): return lax.ppermute(x, axis, [(i, (i + by) % count) for i in range(count)])  10.3 us
  transfers between devices with their start and end apart: 36, of which 19 were waited for; matrix products, arithmetic and copies ran while one was open for 13% of the time, Pallas kernels for 33%

profile of v10, /device:TPU:0, one launch (start us, length us, event | category | flops | bytes accessed | tf_op | source)
XLA Modules:
  0.0 168.6 jit_solution(11258194643286561688)
XLA Ops:
  0.0 1.4 slice_bitcast_fusion
  1.4 3.0 %collective-permute-start.1 = (bf16[64,5120]{1,0:T(8,128)(2,1)S(1)}, bf16[64,5120]{1,0:T(8,128)(2,1)}, u32[]{:S(2)}, u32[]{:S(2)}) collective-permute-start(bf16[64,5120]{1,0:T(8,128)(2,1)S(1)} %get-tuple-element.94), channel_id=1, source_target_pairs={{0,1},{1,0},{2,3},{3,2},{4,5},{5,4},{6,7},{7,6},{8,9},{9,8},{10,11... | collective-permute-start | bytes 1966088 | tf_op jit(solution)/shard_map/ppermute | solution.py:26
  4.4 1.5 collective-permute-start.4
  5.9 0.6 collective-permute-start
  6.5 1.5 collective-permute-start.2
  8.0 0.5 collective-permute-start.3
  8.5 13.2 %collective-permute-done.refs_2_ = f32[3,5120]{1,0:T(4,128)S(1)} collective-permute-done((f32[3,5120]{1,0:T(4,128)S(1)}, f32[3,5120]{1,0:T(4,128)S(1)}, u32[]{:S(2)}, u32[]{:S(2)}) %collective-permute-start) | collective-permute-done | bytes 61472 | tf_op jit(solution)/shard_map/ppermute | solution.py:26
  21.7 2.1 %collective-permute-start.5 = (bf16[64,5120]{1,0:T(8,128)(2,1)}, bf16[64,5120]{1,0:T(8,128)(2,1)}, u32[]{:S(2)}, u32[]{:S(2)}) collective-permute-start(bf16[64,5120]{1,0:T(8,128)(2,1)} %collective-permute-done.1.refs_0_), channel_id=1, source_target_pairs={{0,4},{2,6},{4,0},{6,2},{1,5},{3,7},{5,1},{7,3},{8,12},{10,14},{12... | collective-permute-start | bytes 1966088 | tf_op jit(solution)/shard_map/ppermute | solution.py:26
  23.8 1.5 collective-permute-start.6
  25.3 8.0 %reshape_squeeze.3 = bf16[256,2,8,384]{3,2,1,0:T(8,128)(2,1)} reshape(bf16[1,1,256,2,3072]{4,3,2,1,0:T(2,128)(2,1)} %param.10) | data formatting | bytes 6291456 | tf_op jit(solution)/shard_map/reshape;squeeze | solution.py:394
  33.3 6.0 %copy.12 = bf16[256,2,8,384]{3,1,0,2:T(2,128)(2,1)} copy(bf16[256,2,8,384]{3,2,1,0:T(8,128)(2,1)} %reshape_squeeze.3) | data formatting | bytes 6291456 | tf_op jit(solution)/shard_map/reshape;squeeze | solution.py:394
  39.3 8.0 %reshape.9.value_ref = bf16[8,256,768]{2,1,0:T(8,128)(2,1)} reshape(bf16[8,256,2,384]{3,2,1,0:T(2,128)(2,1)} %bitcast.41) | data formatting | bytes 6291456 | tf_op jit(solution)/shard_map/reshape | solution.py:395
  47.3 1.9 %copy-done.2 = bf16[8,256,768]{2,1,0:T(8,128)(2,1)S(1)} copy-done((bf16[8,256,768]{2,1,0:T(8,128)(2,1)S(1)}, bf16[8,256,768]{2,1,0:T(8,128)(2,1)}, u32[]{:S(2)}) %copy-start.2) | copy-done | bytes 3145752
  49.2 1.8 %copy-done.3 = bf16[8,256,768]{2,1,0:T(8,128)(2,1)} copy-done((bf16[8,256,768]{2,1,0:T(8,128)(2,1)}, bf16[8,256,768]{2,1,0:T(8,128)(2,1)S(1)}, u32[]{:S(2)}) %copy-start.3) | copy-done | bytes 3145752
  51.0 4.8 %all-to-all-start = ((bf16[8,256,768]{2,1,0:T(8,128)(2,1)}), bf16[8,256,768]{2,1,0:T(8,128)(2,1)}, u32[]{:S(2)}, u32[]{:S(2)}) async-start(bf16[8,256,768]{2,1,0:T(8,128)(2,1)} %copy-done.3), calls=%async_computation | async-start | bytes 6291456 | tf_op jit(solution)/shard_map/all_to_all | solution.py:412
  55.8 2.5 %modulated_norm.4.refs_0_ = bf16[128,5120]{1,0:T(8,128)(2,1)S(1)} custom-call(bf16[128,5120]{1,0:T(8,128)(2,1)S(1)} %bitcast.18, f32[3,5120]{1,0:T(4,128)S(1)} %bitcast.37), custom_call_target="tpu_custom_call" | custom-call | flops 1 | bytes 1 | tf_op jit(solution)/shard_map/modulated_norm/pallas_call | solution.py:53
  58.5 3.5 %modulated_norm.5.refs_1_ = bf16[128,5120]{1,0:T(8,128)(2,1)S(1)} custom-call(bf16[64,5120]{1,0:T(8,128)(2,1)} %collective-permute-done.1.refs_0_, bf16[64,5120]{1,0:T(8,128)(2,1)S(1)} %collective-permute-done.2.refs_1_.refs_0_, f32[3,5120]{1,0:T(4,128)S(1)} %collective-permute-done.refs_2_), custom_call_target="tpu_custom_call" | custom-call | flops 1 | bytes 1 | tf_op jit(solution)/shard_map/modulated_norm/pallas_call | solution.py:53
  62.4 2.4 %modulated_norm.6.refs_2_ = bf16[128,5120]{1,0:T(8,128)(2,1)S(1)} custom-call(bf16[64,5120]{1,0:T(8,128)(2,1)S(1)} %collective-permute-done.3.refs_0_.refs_1_, bf16[64,5120]{1,0:T(8,128)(2,1)S(1)} %collective-permute-done.4.refs_1_, f32[3,5120]{1,0:T(4,128)S(1)} %bitcast.38), custom_call_target="tpu_custom_call" | custom-call | flops 1 | bytes 1 | tf_op jit(solution)/shard_map/modulated_norm/pallas_call | solution.py:53
  65.2 3.7 %modulated_norm.7.refs_3_ = bf16[128,5120]{1,0:T(8,128)(2,1)S(1)} custom-call(bf16[64,5120]{1,0:T(8,128)(2,1)} %collective-permute-done.5.refs_0_, bf16[64,5120]{1,0:T(8,128)(2,1)} %collective-permute-done.6.refs_1_, f32[3,5120]{1,0:T(4,128)S(1)} %collective-permute-done.refs_2_), custom_call_target="tpu_custom_call" | custom-call | flops 1 | bytes 1 | tf_op jit(solution)/shard_map/modulated_norm/pallas_call | solution.py:53
  69.3 2.7 %collective-permute-done.10.refs_7_ = bf16[128,5120]{1,0:T(8,128)(2,1)S(1)} collective-permute-done((bf16[128,5120]{1,0:T(8,128)(2,1)S(1)}, bf16[128,5120]{1,0:T(8,128)(2,1)S(1)}, u32[]{:S(2)}, u32[]{:S(2)}) %collective-permute-start.10) | collective-permute-done | bytes 1310752 | tf_op jit(solution)/shard_map/ppermute | solution.py:26
  72.0 19.8 %project_heads.1.heads_in = bf16[9,1024,128]{2,1,0:T(8,128)(2,1)} custom-call(bf16[128,5120]{1,0:T(8,128)(2,1)S(1)} %modulated_norm.4.refs_0_, bf16[128,5120]{1,0:T(8,128)(2,1)S(1)} %modulated_norm.5.refs_1_, bf16[128,5120]{1,0:T(8,128)(2,1)S(1)} %modulated_norm.6.refs_2_, bf16[128,5120]{1,0:T(8,128)(2,1)S(1)} %modulated_norm.7.refs_3_, ...), custom_call_target="tpu_custom_call" | custom-call | flops 12079595520 | bytes 22282240 | tf_op jit(solution)/shard_map/project_heads/pallas_call | solution.py:121
  91.8 1.2 all-to-all-done
  93.0 5.9 %attend.2.refs_0_ = bf16[512,384]{1,0:T(8,128)(2,1)S(1)} custom-call(s32[4,6]{1,0:T(4,128)S(1)} %bitcast.39, bf16[9,1024,128]{2,1,0:T(8,128)(2,1)} %project_heads.1.heads_in, bf16[2048,768]{1,0:T(8,128)(2,1)} %bitcast.7.context_in), custom_call_target="tpu_custom_call" | custom-call | flops 1 | bytes 1 | tf_op jit(solution)/shard_map/attend/pallas_call | solution.py:231
  99.1 6.4 %attend.3.refs_2_ = bf16[512,384]{1,0:T(8,128)(2,1)S(1)} custom-call(s32[4,6]{1,0:T(4,128)S(1)} %bitcast.40, bf16[9,1024,128]{2,1,0:T(8,128)(2,1)} %project_heads.1.heads_in, bf16[2048,768]{1,0:T(8,128)(2,1)} %bitcast.7.context_in, bf16[512,384]{1,0:T(8,128)(2,1)S(1)} %attend.2.refs_0_, f32[2,5120]{1,0:T(2,128)S(1)} %pad_maximum_fusion.refs_1_), custom_call_target="tpu_custom_call" | custom-call | flops 1 | bytes 1 | tf_op jit(solution)/shard_map/attend/pallas_call | solution.py:231
  105.5 2.2 %sum_stage.10 = (bf16[128,1024]{1,0:T(8,128)(2,1)S(1)}, bf16[128,1024]{1,0:T(8,128)(2,1)S(1)}, f32[2,128,512]{2,1,0:T(8,128)S(1)}, f32[2,128,512]{2,1,0:T(8,128)S(1)}) custom-call(bf16[128,5120]{1,0:T(8,128)(2,1)S(1)} %bitcast.19, f32[2,5120]{1,0:T(2,128)S(1)} %pad_maximum_fusion.refs_1_, bf16[512,384]{1,0:T(8,128)(2,1)S(1)} %attend.3.refs_2_, ...), custom_call_target="tpu_custom_call" | custom-call | flops 1 | bytes 1 | tf_op jit(solution)/shard_map/sum_stage/pallas_call | solution.py:359
  107.7 1.1 collective-permute-start.13
  108.8 1.3 collective-permute-start.14
  110.1 2.2 %sum_stage.11 = (bf16[128,1024]{1,0:T(8,128)(2,1)S(1)}, bf16[128,1024]{1,0:T(8,128)(2,1)S(1)}, f32[2,128,512]{2,1,0:T(8,128)S(1)}, f32[2,128,512]{2,1,0:T(8,128)S(1)}) custom-call(bf16[128,5120]{1,0:T(8,128)(2,1)S(1)} %bitcast.20, f32[2,5120]{1,0:T(2,128)S(1)} %pad_maximum_fusion.refs_1_, bf16[512,384]{1,0:T(8,128)(2,1)S(1)} %attend.3.refs_2_, ...), custom_call_target="tpu_custom_call" | custom-call | flops 1 | bytes 1 | tf_op jit(solution)/shard_map/sum_stage/pallas_call | solution.py:359
  112.3 0.6 collective-permute-start.17
  113.0 1.2 collective-permute-start.18
  114.1 2.8 %collective-permute-done.13.refs_6_ = bf16[128,1024]{1,0:T(8,128)(2,1)S(1)} collective-permute-done((bf16[128,1024]{1,0:T(8,128)(2,1)S(1)}, bf16[128,1024]{1,0:T(8,128)(2,1)S(1)}, u32[]{:S(2)}, u32[]{:S(2)}) %collective-permute-start.13) | collective-permute-done | bytes 262176 | tf_op jit(solution)/shard_map/ppermute | solution.py:26
  116.9 1.0 collective-permute-done.14.refs_7_
  117.9 2.4 %sum_stage.12 = (bf16[128,1536]{1,0:T(8,128)(2,1)S(1)}, bf16[128,1536]{1,0:T(8,128)(2,1)S(1)}, f32[2,128,512]{2,1,0:T(8,128)S(1)}, f32[2,128,512]{2,1,0:T(8,128)...) custom-call(bf16[128,5120]{1,0:T(8,128)(2,1)S(1)} %bitcast.21, f32[2,5120]{1,0:T(2,128)S(1)} %pad_maximum_fusion.refs_1_, ...), custom_call_target="tpu_custom_call" | custom-call | flops 1 | bytes 1 | tf_op jit(solution)/shard_map/sum_stage/pallas_call | solution.py:359
  120.4 1.1 collective-permute-start.15
  121.4 0.9 collective-permute-start.16
  122.5 0.7 collective-permute-done.18.refs_7_
  123.2 2.4 %sum_stage.13 = (bf16[128,1536]{1,0:T(8,128)(2,1)S(1)}, bf16[128,1536]{1,0:T(8,128)(2,1)S(1)}, f32[2,128,512]{2,1,0:T(8,128)S(1)}, f32[2,128,512]{2,1,0:T(8,128)...) custom-call(bf16[128,5120]{1,0:T(8,128)(2,1)S(1)} %bitcast.22, f32[2,5120]{1,0:T(2,128)S(1)} %pad_maximum_fusion.refs_1_, ...), custom_call_target="tpu_custom_call" | custom-call | flops 1 | bytes 1 | tf_op jit(solution)/shard_map/sum_stage/pallas_call | solution.py:359
  125.6 1.1 collective-permute-start.20
  126.7 0.8 collective-permute-start.21
  127.5 5.0 %collective-permute-done.15.refs_6_ = bf16[128,1536]{1,0:T(8,128)(2,1)S(1)} collective-permute-done((bf16[128,1536]{1,0:T(8,128)(2,1)S(1)}, bf16[128,1536]{1,0:T(8,128)(2,1)S(1)}, u32[]{:S(2)}, u32[]{:S(2)}) %collective-permute-start.15) | collective-permute-done | bytes 393248 | tf_op jit(solution)/shard_map/ppermute | solution.py:26
  132.5 1.0 collective-permute-done.16.refs_7_
  133.5 1.8 %sum_stage.14 = (bf16[128,1024]{1,0:T(8,128)(2,1)S(1)}, bf16[128,1024]{1,0:T(8,128)(2,1)S(1)}, f32[2,128,256]{2,1,0:T(8,128)S(1)}, f32[2,128,256]{2,1,0:T(8,128)...) custom-call(bf16[128,5120]{1,0:T(8,128)(2,1)S(1)} %bitcast.23, ...), custom_call_target="tpu_custom_call" | custom-call | flops 1 | bytes 1 | tf_op jit(solution)/shard_map/sum_stage/pallas_call | solution.py:359
  135.4 1.6 collective-permute-start.19
  137.0 1.0 collective-permute-start.23
  138.0 1.4 collective-permute-start.24
  139.4 1.5 collective-permute-done.20.refs_6_
  140.9 1.0 collective-permute-done.21.refs_7_
  141.9 1.8 %sum_stage.15 = (bf16[128,1024]{1,0:T(8,128)(2,1)S(1)}, bf16[128,1024]{1,0:T(8,128)(2,1)S(1)}, f32[2,128,256]{2,1,0:T(8,128)S(1)}, f32[2,128,256]{2,1,0:T(8,128)...) custom-call(bf16[128,5120]{1,0:T(8,128)(2,1)S(1)} %bitcast.24, ...), custom_call_target="tpu_custom_call" | custom-call | flops 1 | bytes 1 | tf_op jit(solution)/shard_map/sum_stage/pallas_call | solution.py:359
  143.8 1.6 collective-permute-start.22
  145.4 1.0 collective-permute-start.26
  146.4 1.2 collective-permute-start.27
  147.7 1.6 collective-permute-start.25
  149.3 0.8 collective-permute-start.29
  150.1 3.3 %collective-permute-done.22.refs_9_ = bf16[128,1024]{1,0:T(8,128)(2,1)S(1)} collective-permute-done((bf16[128,1024]{1,0:T(8,128)(2,1)S(1)}, bf16[128,1024]{1,0:T(8,128)(2,1)S(1)}, u32[]{:S(2)}, u32[]{:S(2)}) %collective-permute-start.22) | collective-permute-done | bytes 262176 | tf_op jit(solution)/shard_map/ppermute | solution.py:21
  153.5 1.4 collective-permute-start.30
  155.6 1.2 collective-permute-start.33
  156.9 0.9 collective-permute-done.30.refs_3_
  157.7 1.1 collective-permute-done.25.refs_7_
  159.3 0.7 collective-permute-done.33.refs_3_
  160.0 1.6 collective-permute-start.34
  161.6 3.1 %collective-permute-done.28 = bf16[128,1024]{1,0:T(8,128)(2,1)S(1)} collective-permute-done((bf16[128,1024]{1,0:T(8,128)(2,1)S(1)}, bf16[128,1024]{1,0:T(8,128)(2,1)S(1)}, u32[]{:S(2)}, u32[]{:S(2)}) %collective-permute-start.28) | collective-permute-done | bytes 262176 | tf_op jit(solution)/shard_map/ppermute | solution.py:21
  164.7 1.4 collective-permute-done.31
  166.1 1.4 collective-permute-done.34
  167.5 1.0 copy-done.6
  (54 shorter events, 3.1 us)
Async XLA Ops:
  0.0 5.9 %copy-start.5 = (f32[1,1,3,5120]{3,1,2,0:T(1,128)S(1)}, f32[1,1,3,5120]{3,1,2,0:T(1,128)}, u32[]{:S(2)}) copy-start(f32[1,1,3,5120]{3,1,2,0:T(1,128)} %param.7) | copy-start | bytes 184324
  1.4 20.3 %collective-permute-start.1 = (bf16[64,5120]{1,0:T(8,128)(2,1)S(1)}, bf16[64,5120]{1,0:T(8,128)(2,1)}, u32[]{:S(2)}, u32[]{:S(2)}) collective-permute-start(bf16[64,5120]{1,0:T(8,128)(2,1)S(1)} %get-tuple-element.94), channel_id=1, source_target_pairs={{0,1},{1,0},{2,3},{3,2},{4,5},{5,4},{6,7},{7,6},{8,9},{9,8},{10,11... | collective-permute-start | bytes 1966088 | tf_op jit(solution)/shard_map/ppermute | solution.py:26
  4.4 19.4 %collective-permute-start.4 = (bf16[64,5120]{1,0:T(8,128)(2,1)S(1)}, bf16[64,5120]{1,0:T(8,128)(2,1)S(1)}, u32[]{:S(2)}, u32[]{:S(2)}) collective-permute-start(bf16[64,5120]{1,0:T(8,128)(2,1)S(1)} %get-tuple-element.93), channel_id=1, source_target_pairs={{0,4},{2,6},{4,0},{6,2},{1,5},{3,7},{5,1},{7,3},{8,12},{10,14},{12... | collective-permute-start | bytes 1966088 | tf_op jit(solution)/shard_map/ppermute | solution.py:26
  5.9 15.8 %collective-permute-start = (f32[3,5120]{1,0:T(4,128)S(1)}, f32[3,5120]{1,0:T(4,128)S(1)}, u32[]{:S(2)}, u32[]{:S(2)}) collective-permute-start(f32[3,5120]{1,0:T(4,128)S(1)} %bitcast.36), channel_id=1, source_target_pairs={{0,1},{1,0},{2,3},{3,2},{4,5},{5,4},{6,7},{7,6},{8,9},{9,8},{10,11... | collective-permute-start | bytes 184328 | tf_op jit(solution)/shard_map/ppermute | solution.py:26
  6.5 40.8 %collective-permute-start.2 = (bf16[64,5120]{1,0:T(8,128)(2,1)S(1)}, bf16[64,5120]{1,0:T(8,128)(2,1)S(1)}, u32[]{:S(2)}, u32[]{:S(2)}) collective-permute-start(bf16[64,5120]{1,0:T(8,128)(2,1)S(1)} %get-tuple-element.93), channel_id=1, source_target_pairs={{0,1},{1,0},{2,3},{3,2},{4,5},{5,4},{6,7},{7,6},{8,9},{9,8},{10,11... | collective-permute-start | bytes 1966088 | tf_op jit(solution)/shard_map/ppermute | solution.py:26
  8.0 39.3 %collective-permute-start.3 = (bf16[64,5120]{1,0:T(8,128)(2,1)S(1)}, bf16[64,5120]{1,0:T(8,128)(2,1)S(1)}, u32[]{:S(2)}, u32[]{:S(2)}) collective-permute-start(bf16[64,5120]{1,0:T(8,128)(2,1)S(1)} %get-tuple-element.94), channel_id=1, source_target_pairs={{0,4},{2,6},{4,0},{6,2},{1,5},{3,7},{5,1},{7,3},{8,12},{10,14},{12... | collective-permute-start | bytes 1966088 | tf_op jit(solution)/shard_map/ppermute | solution.py:26
  21.7 83.8 %collective-permute-start.12 = (bf16[384,5120]{1,0:T(8,128)(2,1)}, bf16[384,5120]{1,0:T(8,128)(2,1)}, u32[]{:S(2)}, u32[]{:S(2)}) collective-permute-start(bf16[384,5120]{1,0:T(8,128)(2,1)} %bitcast.29), channel_id=1, source_target_pairs={{0,2},{2,0},{4,6},{6,4},{1,3},{3,1},{5,7},{7,5},{8,10},{10,8},{12,... | collective-permute-start | bytes 11796488 | tf_op jit(solution)/shard_map/ppermute | solution.py:26
  21.7 43.2 %collective-permute-start.5 = (bf16[64,5120]{1,0:T(8,128)(2,1)}, bf16[64,5120]{1,0:T(8,128)(2,1)}, u32[]{:S(2)}, u32[]{:S(2)}) collective-permute-start(bf16[64,5120]{1,0:T(8,128)(2,1)} %collective-permute-done.1.refs_0_), channel_id=1, source_target_pairs={{0,4},{2,6},{4,0},{6,2},{1,5},{3,7},{5,1},{7,3},{8,12},{10,14},{12... | collective-permute-start | bytes 1966088 | tf_op jit(solution)/shard_map/ppermute | solution.py:26
  23.8 41.4 %collective-permute-start.6 = (bf16[64,5120]{1,0:T(8,128)(2,1)S(1)}, bf16[64,5120]{1,0:T(8,128)(2,1)}, u32[]{:S(2)}, u32[]{:S(2)}) collective-permute-start(bf16[64,5120]{1,0:T(8,128)(2,1)S(1)} %collective-permute-done.4.refs_1_), channel_id=1, source_target_pairs={{0,1},{1,0},{2,3},{3,2},{4,5},{5,4},{6,7},{7,6},{8,9},{9,8},{10,11... | collective-permute-start | bytes 1966088 | tf_op jit(solution)/shard_map/ppermute | solution.py:26
  47.3 1.9 %copy-start.2 = (bf16[8,256,768]{2,1,0:T(8,128)(2,1)S(1)}, bf16[8,256,768]{2,1,0:T(8,128)(2,1)}, u32[]{:S(2)}) copy-start(bf16[8,256,768]{2,1,0:T(8,128)(2,1)} %reshape.9.value_ref) | copy-start | bytes 9437188
  49.2 1.8 %copy-start.3 = (bf16[8,256,768]{2,1,0:T(8,128)(2,1)}, bf16[8,256,768]{2,1,0:T(8,128)(2,1)S(1)}, u32[]{:S(2)}) copy-start(bf16[8,256,768]{2,1,0:T(8,128)(2,1)S(1)} %after.1) | copy-start | bytes 9437188
  51.0 4.8 %copy-start = (bf16[1,1,128,5120]{3,2,1,0:T(8,128)(2,1)S(1)}, bf16[1,1,128,5120]{3,2,1,0:T(8,128)(2,1)}, u32[]{:S(2)}) copy-start(bf16[1,1,128,5120]{3,2,1,0:T(8,128)(2,1)} %param.6) | copy-start | bytes 3932164
  51.0 42.0 %all-to-all-start = ((bf16[8,256,768]{2,1,0:T(8,128)(2,1)}), bf16[8,256,768]{2,1,0:T(8,128)(2,1)}, u32[]{:S(2)}, u32[]{:S(2)}) async-start(bf16[8,256,768]{2,1,0:T(8,128)(2,1)} %copy-done.3), calls=%async_computation | async-start | bytes 6291456 | tf_op jit(solution)/shard_map/all_to_all | solution.py:412
  58.2 11.1 %collective-permute-start.7 = (bf16[128,5120]{1,0:T(8,128)(2,1)S(1)}, bf16[128,5120]{1,0:T(8,128)(2,1)S(1)}, u32[]{:S(2)}, u32[]{:S(2)}) collective-permute-start(bf16[128,5120]{1,0:T(8,128)(2,1)S(1)} %modulated_norm.4.refs_0_), channel_id=1, source_target_pairs={{0,2},{2,0},{4,6},{6,4},{1,3},{3,1},{5,7},{7,5},{8,10},{10,8},{12,... | collective-permute-start | bytes 3932168 | tf_op jit(solution)/shard_map/ppermute | solution.py:26
  62.0 7.3 %collective-permute-start.8 = (bf16[128,5120]{1,0:T(8,128)(2,1)S(1)}, bf16[128,5120]{1,0:T(8,128)(2,1)S(1)}, u32[]{:S(2)}, u32[]{:S(2)}) collective-permute-start(bf16[128,5120]{1,0:T(8,128)(2,1)S(1)} %modulated_norm.5.refs_1_), channel_id=1, source_target_pairs={{0,2},{2,0},{4,6},{6,4},{1,3},{3,1},{5,7},{7,5},{8,10},{10,8},{12,... | collective-permute-start | bytes 3932168 | tf_op jit(solution)/shard_map/ppermute | solution.py:26
  64.9 4.4 %collective-permute-start.9 = (bf16[128,5120]{1,0:T(8,128)(2,1)S(1)}, bf16[128,5120]{1,0:T(8,128)(2,1)S(1)}, u32[]{:S(2)}, u32[]{:S(2)}) collective-permute-start(bf16[128,5120]{1,0:T(8,128)(2,1)S(1)} %modulated_norm.6.refs_2_), channel_id=1, source_target_pairs={{0,2},{2,0},{4,6},{6,4},{1,3},{3,1},{5,7},{7,5},{8,10},{10,8},{12,... | collective-permute-start | bytes 3932168 | tf_op jit(solution)/shard_map/ppermute | solution.py:26
  68.9 3.1 %collective-permute-start.10 = (bf16[128,5120]{1,0:T(8,128)(2,1)S(1)}, bf16[128,5120]{1,0:T(8,128)(2,1)S(1)}, u32[]{:S(2)}, u32[]{:S(2)}) collective-permute-start(bf16[128,5120]{1,0:T(8,128)(2,1)S(1)} %modulated_norm.7.refs_3_), channel_id=1, source_target_pairs={{0,2},{2,0},{4,6},{6,4},{1,3},{3,1},{5,7},{7,5},{8,10},{10,8},{12,... | collective-permute-start | bytes 3932168 | tf_op jit(solution)/shard_map/ppermute | solution.py:26
  72.0 21.0 %copy-start.4 = (s32[1,4,6]{2,1,0:T(4,128)S(1)}, s32[1,4,6]{2,1,0:T(4,128)}, u32[]{:S(2)}) copy-start(s32[1,4,6]{2,1,0:T(4,128)} %param.11) | copy-start | bytes 292
  98.9 6.6 %collective-permute-start.11 = (bf16[512,384]{1,0:T(8,128)(2,1)S(1)}, bf16[512,384]{1,0:T(8,128)(2,1)S(1)}, u32[]{:S(2)}, u32[]{:S(2)}) collective-permute-start(bf16[512,384]{1,0:T(8,128)(2,1)S(1)} %attend.2.refs_0_), channel_id=1, source_target_pairs={{0,2},{2,0},{4,6},{6,4},{1,3},{3,1},{5,7},{7,5},{8,10},{10,8},{12,... | collective-permute-start | bytes 1179656 | tf_op jit(solution)/shard_map/ppermute | solution.py:26
  99.0 6.5 %copy-start.1 = (bf16[1,384,5120]{2,1,0:T(8,128)(2,1)S(1)}, bf16[1,384,5120]{2,1,0:T(8,128)(2,1)}, u32[]{:S(2)}) copy-start(bf16[1,384,5120]{2,1,0:T(8,128)(2,1)} %param.9) | copy-start | bytes 11796484
  107.7 9.2 %collective-permute-start.13 = (bf16[128,1024]{1,0:T(8,128)(2,1)S(1)}, bf16[128,1024]{1,0:T(8,128)(2,1)S(1)}, u32[]{:S(2)}, u32[]{:S(2)}) collective-permute-start(bf16[128,1024]{1,0:T(8,128)(2,1)S(1)} %get-tuple-element.49), channel_id=1, source_target_pairs={{0,1},{1,0},{2,3},{3,2},{4,5},{5,4},{6,7},{7,6},{8,9},{9,8},{10,11... | collective-permute-start | bytes 786440 | tf_op jit(solution)/shard_map/ppermute | solution.py:26
  108.8 9.1 %collective-permute-start.14 = (bf16[128,1024]{1,0:T(8,128)(2,1)S(1)}, bf16[128,1024]{1,0:T(8,128)(2,1)S(1)}, u32[]{:S(2)}, u32[]{:S(2)}) collective-permute-start(bf16[128,1024]{1,0:T(8,128)(2,1)S(1)} %get-tuple-element.50), channel_id=1, source_target_pairs={{0,4},{2,6},{4,0},{6,2},{1,5},{3,7},{5,1},{7,3},{8,12},{10,14},{12... | collective-permute-start | bytes 786440 | tf_op jit(solution)/shard_map/ppermute | solution.py:26
  112.3 10.2 %collective-permute-start.17 = (bf16[128,1024]{1,0:T(8,128)(2,1)S(1)}, bf16[128,1024]{1,0:T(8,128)(2,1)S(1)}, u32[]{:S(2)}, u32[]{:S(2)}) collective-permute-start(bf16[128,1024]{1,0:T(8,128)(2,1)S(1)} %get-tuple-element.60), channel_id=1, source_target_pairs={{0,1},{1,0},{2,3},{3,2},{4,5},{5,4},{6,7},{7,6},{8,9},{9,8},{10,11... | collective-permute-start | bytes 786440 | tf_op jit(solution)/shard_map/ppermute | solution.py:26
  113.0 10.2 %collective-permute-start.18 = (bf16[128,1024]{1,0:T(8,128)(2,1)S(1)}, bf16[128,1024]{1,0:T(8,128)(2,1)S(1)}, u32[]{:S(2)}, u32[]{:S(2)}) collective-permute-start(bf16[128,1024]{1,0:T(8,128)(2,1)S(1)} %get-tuple-element.61), channel_id=1, source_target_pairs={{0,4},{2,6},{4,0},{6,2},{1,5},{3,7},{5,1},{7,3},{8,12},{10,14},{12... | collective-permute-start | bytes 786440 | tf_op jit(solution)/shard_map/ppermute | solution.py:26
  120.4 12.1 %collective-permute-start.15 = (bf16[128,1536]{1,0:T(8,128)(2,1)S(1)}, bf16[128,1536]{1,0:T(8,128)(2,1)S(1)}, u32[]{:S(2)}, u32[]{:S(2)}) collective-permute-start(bf16[128,1536]{1,0:T(8,128)(2,1)S(1)} %get-tuple-element.54), channel_id=1, source_target_pairs={{0,1},{1,0},{2,3},{3,2},{4,5},{5,4},{6,7},{7,6},{8,9},{9,8},{10,11... | collective-permute-start | bytes 1179656 | tf_op jit(solution)/shard_map/ppermute | solution.py:26
  121.4 12.1 %collective-permute-start.16 = (bf16[128,1536]{1,0:T(8,128)(2,1)S(1)}, bf16[128,1536]{1,0:T(8,128)(2,1)S(1)}, u32[]{:S(2)}, u32[]{:S(2)}) collective-permute-start(bf16[128,1536]{1,0:T(8,128)(2,1)S(1)} %get-tuple-element.55), channel_id=1, source_target_pairs={{0,4},{2,6},{4,0},{6,2},{1,5},{3,7},{5,1},{7,3},{8,12},{10,14},{12... | collective-permute-start | bytes 1179656 | tf_op jit(solution)/shard_map/ppermute | solution.py:26
  125.6 15.3 %collective-permute-start.20 = (bf16[128,1536]{1,0:T(8,128)(2,1)S(1)}, bf16[128,1536]{1,0:T(8,128)(2,1)S(1)}, u32[]{:S(2)}, u32[]{:S(2)}) collective-permute-start(bf16[128,1536]{1,0:T(8,128)(2,1)S(1)} %get-tuple-element.65), channel_id=1, source_target_pairs={{0,1},{1,0},{2,3},{3,2},{4,5},{5,4},{6,7},{7,6},{8,9},{9,8},{10,11... | collective-permute-start | bytes 1179656 | tf_op jit(solution)/shard_map/ppermute | solution.py:26
  126.7 15.2 %collective-permute-start.21 = (bf16[128,1536]{1,0:T(8,128)(2,1)S(1)}, bf16[128,1536]{1,0:T(8,128)(2,1)S(1)}, u32[]{:S(2)}, u32[]{:S(2)}) collective-permute-start(bf16[128,1536]{1,0:T(8,128)(2,1)S(1)} %get-tuple-element.66), channel_id=1, source_target_pairs={{0,4},{2,6},{4,0},{6,2},{1,5},{3,7},{5,1},{7,3},{8,12},{10,14},{12... | collective-permute-start | bytes 1179656 | tf_op jit(solution)/shard_map/ppermute | solution.py:26
  135.4 11.1 %collective-permute-start.19 = (bf16[128,1024]{1,0:T(8,128)(2,1)S(1)}, bf16[128,1024]{1,0:T(8,128)(2,1)S(1)}, u32[]{:S(2)}, u32[]{:S(2)}) collective-permute-start(bf16[128,1024]{1,0:T(8,128)(2,1)S(1)} %get-tuple-element.64.refs_12_), channel_id=1, source_target_pairs={{0,8},{8,16},{16,24},{24,0},{1,9},{9,17},{17,25},{25,1},{2,10},{10... | collective-permute-start | bytes 786440 | tf_op jit(solution)/shard_map/ppermute | solution.py:21
  137.0 10.6 %collective-permute-start.23 = (bf16[128,1024]{1,0:T(8,128)(2,1)S(1)}, bf16[128,1024]{1,0:T(8,128)(2,1)S(1)}, u32[]{:S(2)}, u32[]{:S(2)}) collective-permute-start(bf16[128,1024]{1,0:T(8,128)(2,1)S(1)} %get-tuple-element.71), channel_id=1, source_target_pairs={{0,1},{1,0},{2,3},{3,2},{4,5},{5,4},{6,7},{7,6},{8,9},{9,8},{10,11... | collective-permute-start | bytes 786440 | tf_op jit(solution)/shard_map/ppermute | solution.py:26
  138.0 9.6 %collective-permute-start.24 = (bf16[128,1024]{1,0:T(8,128)(2,1)S(1)}, bf16[128,1024]{1,0:T(8,128)(2,1)S(1)}, u32[]{:S(2)}, u32[]{:S(2)}) collective-permute-start(bf16[128,1024]{1,0:T(8,128)(2,1)S(1)} %get-tuple-element.72), channel_id=1, source_target_pairs={{0,4},{2,6},{4,0},{6,2},{1,5},{3,7},{5,1},{7,3},{8,12},{10,14},{12... | collective-permute-start | bytes 786440 | tf_op jit(solution)/shard_map/ppermute | solution.py:26
  143.8 9.7 %collective-permute-start.22 = (bf16[128,1024]{1,0:T(8,128)(2,1)S(1)}, bf16[128,1024]{1,0:T(8,128)(2,1)S(1)}, u32[]{:S(2)}, u32[]{:S(2)}) collective-permute-start(bf16[128,1024]{1,0:T(8,128)(2,1)S(1)} %get-tuple-element.70.refs_8_), channel_id=1, source_target_pairs={{0,8},{8,16},{16,24},{24,0},{1,9},{9,17},{17,25},{25,1},{2,10},{10... | collective-permute-start | bytes 786440 | tf_op jit(solution)/shard_map/ppermute | solution.py:21
  145.4 9.4 %collective-permute-start.26 = (bf16[128,1024]{1,0:T(8,128)(2,1)S(1)}, bf16[128,1024]{1,0:T(8,128)(2,1)S(1)}, u32[]{:S(2)}, u32[]{:S(2)}) collective-permute-start(bf16[128,1024]{1,0:T(8,128)(2,1)S(1)} %get-tuple-element.78), channel_id=1, source_target_pairs={{0,1},{1,0},{2,3},{3,2},{4,5},{5,4},{6,7},{7,6},{8,9},{9,8},{10,11... | collective-permute-start | bytes 786440 | tf_op jit(solution)/shard_map/ppermute | solution.py:26
  146.4 8.4 %collective-permute-start.27 = (bf16[128,1024]{1,0:T(8,128)(2,1)S(1)}, bf16[128,1024]{1,0:T(8,128)(2,1)S(1)}, u32[]{:S(2)}, u32[]{:S(2)}) collective-permute-start(bf16[128,1024]{1,0:T(8,128)(2,1)S(1)} %get-tuple-element.79), channel_id=1, source_target_pairs={{0,4},{2,6},{4,0},{6,2},{1,5},{3,7},{5,1},{7,3},{8,12},{10,14},{12... | collective-permute-start | bytes 786440 | tf_op jit(solution)/shard_map/ppermute | solution.py:26
  147.7 11.1 %collective-permute-start.25 = (bf16[128,1024]{1,0:T(8,128)(2,1)S(1)}, bf16[128,1024]{1,0:T(8,128)(2,1)S(1)}, u32[]{:S(2)}, u32[]{:S(2)}) collective-permute-start(bf16[128,1024]{1,0:T(8,128)(2,1)S(1)} %get-tuple-element.77.refs_8_), channel_id=1, source_target_pairs={{0,8},{8,16},{16,24},{24,0},{1,9},{9,17},{17,25},{25,1},{2,10},{10... | collective-permute-start | bytes 786440 | tf_op jit(solution)/shard_map/ppermute | solution.py:21
  149.3 6.3 %collective-permute-start.29 = (bf16[128,256]{1,0:T(8,128)(2,1)S(1)}, bf16[128,256]{1,0:T(8,128)(2,1)S(1)}, u32[]{:S(2)}, u32[]{:S(2)}) collective-permute-start(bf16[128,256]{1,0:T(8,128)(2,1)S(1)} %get-tuple-element.85), channel_id=1, source_target_pairs={{0,1},{1,0},{2,3},{3,2},{4,5},{5,4},{6,7},{7,6},{8,9},{9,8},{10,11... | collective-permute-start | bytes 196616 | tf_op jit(solution)/shard_map/ppermute | solution.py:26
  153.5 4.3 %collective-permute-start.30 = (bf16[128,256]{1,0:T(8,128)(2,1)S(1)}, bf16[128,256]{1,0:T(8,128)(2,1)S(1)}, u32[]{:S(2)}, u32[]{:S(2)}) collective-permute-start(bf16[128,256]{1,0:T(8,128)(2,1)S(1)} %get-tuple-element.86), channel_id=1, source_target_pairs={{0,4},{2,6},{4,0},{6,2},{1,5},{3,7},{5,1},{7,3},{8,12},{10,14},{12... | collective-permute-start | bytes 196616 | tf_op jit(solution)/shard_map/ppermute | solution.py:26
  154.9 4.3 %collective-permute-start.32 = (bf16[128,256]{1,0:T(8,128)(2,1)S(1)}, bf16[128,256]{1,0:T(8,128)(2,1)S(1)}, u32[]{:S(2)}, u32[]{:S(2)}) collective-permute-start(bf16[128,256]{1,0:T(8,128)(2,1)S(1)} %get-tuple-element.89), channel_id=1, source_target_pairs={{0,1},{1,0},{2,3},{3,2},{4,5},{5,4},{6,7},{7,6},{8,9},{9,8},{10,11... | collective-permute-start | bytes 196616 | tf_op jit(solution)/shard_map/ppermute | solution.py:26
  155.3 9.4 %collective-permute-start.28 = (bf16[128,1024]{1,0:T(8,128)(2,1)S(1)}, bf16[128,1024]{1,0:T(8,128)(2,1)S(1)}, u32[]{:S(2)}, u32[]{:S(2)}) collective-permute-start(bf16[128,1024]{1,0:T(8,128)(2,1)S(1)} %get-tuple-element.84.refs_6_), channel_id=1, source_target_pairs={{0,8},{8,16},{16,24},{24,0},{1,9},{9,17},{17,25},{25,1},{2,10},{10... | collective-permute-start | bytes 786440 | tf_op jit(solution)/shard_map/ppermute | solution.py:21
  155.6 4.3 %collective-permute-start.33 = (bf16[128,256]{1,0:T(8,128)(2,1)S(1)}, bf16[128,256]{1,0:T(8,128)(2,1)S(1)}, u32[]{:S(2)}, u32[]{:S(2)}) collective-permute-start(bf16[128,256]{1,0:T(8,128)(2,1)S(1)} %get-tuple-element.90), channel_id=1, source_target_pairs={{0,4},{2,6},{4,0},{6,2},{1,5},{3,7},{5,1},{7,3},{8,12},{10,14},{12... | collective-permute-start | bytes 196616 | tf_op jit(solution)/shard_map/ppermute | solution.py:26
  158.9 7.2 %collective-permute-start.31 = (bf16[128,512]{1,0:T(8,128)(2,1)S(1)}, bf16[128,512]{1,0:T(8,128)(2,1)S(1)}, u32[]{:S(2)}, u32[]{:S(2)}) collective-permute-start(bf16[128,512]{1,0:T(8,128)(2,1)S(1)} %sum_stage.18.refs_6_), channel_id=1, source_target_pairs={{0,8},{8,16},{16,24},{24,0},{1,9},{9,17},{17,25},{25,1},{2,10},{10... | collective-permute-start | bytes 393224 | tf_op jit(solution)/shard_map/ppermute | solution.py:21
  160.0 7.5 %collective-permute-start.34 = (bf16[128,512]{1,0:T(8,128)(2,1)S(1)}, bf16[128,512]{1,0:T(8,128)(2,1)S(1)}, u32[]{:S(2)}, u32[]{:S(2)}) collective-permute-start(bf16[128,512]{1,0:T(8,128)(2,1)S(1)} %sum_stage.19), channel_id=1, source_target_pairs={{0,8},{8,16},{16,24},{24,0},{1,9},{9,17},{17,25},{25,1},{2,10},{10... | collective-permute-start | bytes 393224 | tf_op jit(solution)/shard_map/ppermute | solution.py:21
  167.5 1.1 copy-start.6

commit v11 on v10

--- a/solution.py
+++ b/solution.py
@@ -10,6 +10,7 @@
 HD = 128
 TILE = 128
 MIB = 2**20
+SPARE = 39
 CHUNK_SHARES = (4, 4, 4, 4, 2, 2)
 
 guidance_scale = 5.0
@@ -44,7 +45,7 @@
             ).astype(jnp.bfloat16)
             return carry
 
-        lax.fori_loop(0, part.shape[0] // step, body, 0)
+        lax.fori_loop(0, part.shape[0] // step, body, 0, unroll=2)
         start += part.shape[0]
 
 
@@ -90,7 +91,7 @@
     def _():
         total_ref[...] = product
 
-    @pl.when(step > 0)
+    @pl.when((step > 0) & (step < steps - 1))
     def _():
         total_ref[...] += product
 
@@ -99,7 +100,8 @@
         heads = heads_ref.shape[0]
         copies = []
         for head in range(heads):
-            values = total_ref[:, head * HD : (head + 1) * HD]
+            columns = slice(head * HD, (head + 1) * HD)
+            values = total_ref[:, columns] + product[:, columns]
             if head < 2 * heads // 3:
                 square = jnp.mean(values * values, axis=-1, keepdims=True)
                 values = values * lax.rsqrt(square + 1e-06)
@@ -114,7 +116,7 @@
 
 def project(blocks, weights):
     _, depth, width = weights.shape
-    steps = 4
+    steps = 2
     block = depth // steps
     count = sum(rows.shape[0] for rows in blocks)
     heads = 3 * width // HD
@@ -124,7 +126,7 @@
         in_specs=[pl.BlockSpec(memory_space=pltpu.VMEM)] * len(blocks)
         + [pl.BlockSpec((3, block, width), lambda k: (0, k, 0))],
         out_specs=pl.BlockSpec(memory_space=pltpu.HBM),
-        out_shape=jax.ShapeDtypeStruct((heads, count, HD), jnp.bfloat16),
+        out_shape=jax.ShapeDtypeStruct((heads + SPARE, count, HD), jnp.bfloat16),
         scratch_shapes=[
             pltpu.VMEM((count, 3 * width), jnp.float32),
             pltpu.VMEM((heads, count, HD), jnp.bfloat16),
@@ -140,7 +142,7 @@
     )(*blocks, weights)
 
 
-def attend_head(visible_ref, heads_ref, context_ref, out_ref, first_block, head):
+def attend_blocks(visible_ref, heads_ref, context_ref, out_ref, first_block):
     heads = heads_ref.shape[0] // 3
     tiles_seen = visible_ref.shape[1]
     tiles_fresh = visible_ref.shape[0]
@@ -168,7 +170,7 @@
                 )
             )
 
-        def tiles(kind):
+        def tiles(kind, head):
             start = ((kind - 1) * heads + head) * HD
             return jnp.concatenate(
                 [
@@ -182,70 +184,78 @@
                 axis=0,
             )
 
-        scores = lax.dot_general(
-            heads_ref[head, rows, :],
-            tiles(1),
-            (((1,), (1,)), ((), ())),
-            preferred_element_type=jnp.float32,
-        )
-        exponent = jnp.exp(scores * HD ** (-0.5))
-        total = jnp.sum(exponent, axis=-1, keepdims=True)
-        mixed = jnp.dot(
-            exponent.astype(jnp.bfloat16), tiles(2), preferred_element_type=jnp.float32
-        )
-        out_ref[out_rows, head * HD : (head + 1) * HD] = (mixed / total).astype(jnp.bfloat16)
+        for head in range(heads):
+            scores = lax.dot_general(
+                heads_ref[head, rows, :],
+                tiles(1, head),
+                (((1,), (1,)), ((), ())),
+                preferred_element_type=jnp.float32,
+            )
+            exponent = jnp.exp(scores * HD ** (-0.5))
+            total = jnp.sum(exponent, axis=-1, keepdims=True)
+            mixed = jnp.dot(
+                exponent.astype(jnp.bfloat16), tiles(2, head), preferred_element_type=jnp.float32
+            )
+            out_ref[out_rows, head * HD : (head + 1) * HD] = (mixed / total).astype(jnp.bfloat16)
         return carry
 
     lax.fori_loop(0, out_ref.shape[0] // TILE, body, 0, unroll=2)
 
 
-def attend_kernel(visible_ref, heads_in, context_in, *refs, first_block):
-    out_ref, heads_ref, context_ref, sems = refs[-4:]
-    heads = heads_ref.shape[0] // 3
-    copies = []
-    for head in range(heads):
-        of_head = []
-        for kind in range(3):
-            place = kind * heads + head
-            of_head.append(
-                pltpu.make_async_copy(heads_in.at[place], heads_ref.at[place], sems.at[head, kind])
-            )
-        for kind in range(2):
-            columns = pl.ds((kind * heads + head) * HD, HD)
-            of_head.append(
-                pltpu.make_async_copy(
-                    context_in.at[:, columns], context_ref.at[:, columns], sems.at[head, 3 + kind]
-                )
-            )
-        for copy in of_head:
-            copy.start()
-        copies.append(of_head)
-    for head in range(heads):
-        for copy in copies[head]:
-            copy.wait()
-        attend_head(visible_ref, heads_ref, context_ref, out_ref, first_block, head)
-
-
-def attend(heads, context, visible, first_block, earlier):
-    count = heads.shape[1] // 2
+def attend_first_kernel(
+    visible_ref, heads_in, context_in, out_ref, heads_ref, context_ref, heads_sem, context_sem
+):
+    copies = (
+        pltpu.make_async_copy(
+            heads_in.at[pl.ds(0, heads_ref.shape[0])], heads_ref, heads_sem
+        ),
+        pltpu.make_async_copy(context_in, context_ref, context_sem),
+    )
+    for copy in copies:
+        copy.start()
+    for copy in copies:
+        copy.wait()
+    attend_blocks(visible_ref, heads_ref, context_ref, out_ref, out_ref.shape[0] // TILE)
+
+
+def attend_first(heads, context, visible):
+    number, count = heads.shape[0] - SPARE, heads.shape[1] // 2
     return pl.pallas_call(
-        functools.partial(attend_kernel, first_block=first_block),
+        attend_first_kernel,
         in_specs=[
             pl.BlockSpec(memory_space=pltpu.SMEM),
             pl.BlockSpec(memory_space=pltpu.HBM),
             pl.BlockSpec(memory_space=pl.ANY),
-        ]
+        ],
+        out_specs=[pl.BlockSpec(memory_space=pltpu.VMEM)] * 3,
+        out_shape=[
+            jax.ShapeDtypeStruct((count, number // 3 * HD), jnp.bfloat16),
+            jax.ShapeDtypeStruct((number,) + heads.shape[1:], heads.dtype),
+            jax.ShapeDtypeStruct(context.shape, context.dtype),
+        ],
+        scratch_shapes=[pltpu.SemaphoreType.DMA, pltpu.SemaphoreType.DMA],
+        name="attend_first",
+        cost_estimate=SHORT,
+        compiler_params=pltpu.CompilerParams(vmem_limit_bytes=44 * MIB),
+    )(visible, heads, context)
+
+
+def attend_second_kernel(visible_ref, heads_ref, context_ref, *refs):
+    attend_blocks(visible_ref, heads_ref, context_ref, refs[-1], 0)
+
+
+def attend_second(heads, context, visible, earlier):
+    count = heads.shape[1] // 2
+    return pl.pallas_call(
+        attend_second_kernel,
+        in_specs=[pl.BlockSpec(memory_space=pltpu.SMEM)]
+        + [pl.BlockSpec(memory_space=pltpu.VMEM)] * 2
         + [pl.BlockSpec(memory_space=pl.ANY)] * len(earlier),
         out_specs=pl.BlockSpec(memory_space=pltpu.VMEM),
         out_shape=jax.ShapeDtypeStruct((count, heads.shape[0] // 3 * HD), jnp.bfloat16),
-        scratch_shapes=[
-            pltpu.VMEM(heads.shape, heads.dtype),
-            pltpu.VMEM(context.shape, context.dtype),
-            pltpu.SemaphoreType.DMA((heads.shape[0] // 3, 5)),
-        ],
-        name="attend",
+        name="attend_second",
         cost_estimate=SHORT,
-        compiler_params=pltpu.CompilerParams(vmem_limit_bytes=53 * MIB),
+        compiler_params=pltpu.CompilerParams(vmem_limit_bytes=12 * MIB),
     )(visible, heads, context, *earlier)
 
 
@@ -419,9 +429,9 @@
     chunks = [
         (sum(CHUNK_SHARES[:index]) * unit, share * unit) for index, share in enumerate(CHUNK_SHARES)
     ]
-    for_core = attend(heads, context, visible[0], heads.shape[1] // TILE // 2, ())
+    for_core, heads, context = attend_first(heads, context, visible[0])
     core_attended = from_partner(for_core, "sp", 1)
-    attended = attend(heads, context, visible[0], 0, (for_core, gates))
+    attended = attend_second(heads, context, visible[0], (for_core, gates))
 
     kept, left, flights, arrivals, earlier = {}, {}, {}, [], []
     for index in range(-2, count + 2):

time: 169 us -> 167 us (0.988)
  Pallas kernels: 57.5 us -> 50.1 us
  waiting for transfers between devices: 42.5 us -> 48.2 us
    all_to_all x1, waiting for transfers between devices: 1.19 us -> 5.88 us  [per_device(): lax.all_to_all(packed, ('sp', 'cfg'), split_axis=0, concat_axis=0, tiled=...]
    pallas_call x4, Pallas kernels: 12.2 us -> 8.47 us  [modulated_norm(): pl.pallas_call(norm_kernel, in_specs=[pl.BlockSpec(memory_space=pltpu.VME...]
    pallas_call x2, Pallas kernels: 12.3 us -> 9.66 us  [the longest x1 6 us: attend_first(): pl.pallas_call(attend_first_kernel, in_specs=[pl.BlockSpec(memory_space=p...]
  transfers between devices with their start and end apart: 36 -> 36, of which waited for: 19 -> 18; matrix products, arithmetic and copies ran while one was open for 13% -> 13% of each run, Pallas kernels for 33% -> 29%
where the time goes in v11:
time: 167 us; the launch traced here: 166 us
  Pallas kernels  50.1 us (30%)
  waiting for transfers between devices  48.2 us (29%)
  starting transfers between devices  38.9 us (23%)
  local copies, waits for them, and re-layouts  28.1 us (17%)
    ppermute x29, waiting for transfers between devices, from_partner(): return lax.ppermute(value, axis, pairs)  32 us
    ppermute x29, starting transfers between devices, from_partner(): return lax.ppermute(value, axis, pairs)  27.2 us
    pallas_call x1, Pallas kernels, project(): pl.pallas_call(functools.partial(project_kernel, blocks=len(blocks)), gri...  18.8 us
    another operation x2, local copies, waits for them, and re-layouts, per_device(): packed = stale_cache[0, 0].reshape(context_rows, 2, devices, width)  13.9 us
    pallas_call x10, Pallas kernels, stage(): pl.pallas_call(functools.partial(stage_kernel, parts=parts, start=start,...  13.2 us
    ppermute x6, waiting for transfers between devices, from_behind(): return lax.ppermute(x, axis, [(i, (i + by) % count) for i in range(count)])  10.3 us
    pallas_call x4, Pallas kernels, modulated_norm(): pl.pallas_call(norm_kernel, in_specs=[pl.BlockSpec(memory_space=pltpu.VME...  8.47 us
    reshape x1, local copies, waits for them, and re-layouts, per_device(): packed.transpose(2, 0, 1, 3).reshape(devices, context_rows, 2 * width)  8.02 us
  transfers between devices with their start and end apart: 36, of which 18 were waited for; matrix products, arithmetic and copies ran while one was open for 13% of the time, Pallas kernels for 29%

profile of v11, /device:TPU:0, one launch (start us, length us, event | category | flops | bytes accessed | tf_op | source)
XLA Modules:
  0.0 165.7 jit_solution(14054519424865643517)
XLA Ops:
  0.0 1.4 slice_bitcast_fusion
  1.4 3.0 %collective-permute-start.1 = (bf16[64,5120]{1,0:T(8,128)(2,1)S(1)}, bf16[64,5120]{1,0:T(8,128)(2,1)}, u32[]{:S(2)}, u32[]{:S(2)}) collective-permute-start(bf16[64,5120]{1,0:T(8,128)(2,1)S(1)} %get-tuple-element.100), channel_id=1, source_target_pairs={{0,1},{1,0},{2,3},{3,2},{4,5},{5,4},{6,7},{7,6},{8,9},{9,8},{10,11... | collective-permute-start | bytes 1966088 | tf_op jit(solution)/shard_map/ppermute | solution.py:27
  4.4 1.5 collective-permute-start.4
  5.9 0.6 collective-permute-start
  6.5 1.5 collective-permute-start.2
  8.0 0.5 collective-permute-start.3
  8.5 13.2 %collective-permute-done.refs_2_ = f32[3,5120]{1,0:T(4,128)S(1)} collective-permute-done((f32[3,5120]{1,0:T(4,128)S(1)}, f32[3,5120]{1,0:T(4,128)S(1)}, u32[]{:S(2)}, u32[]{:S(2)}) %collective-permute-start) | collective-permute-done | bytes 61472 | tf_op jit(solution)/shard_map/ppermute | solution.py:27
  21.7 2.1 %collective-permute-start.5 = (bf16[64,5120]{1,0:T(8,128)(2,1)}, bf16[64,5120]{1,0:T(8,128)(2,1)}, u32[]{:S(2)}, u32[]{:S(2)}) collective-permute-start(bf16[64,5120]{1,0:T(8,128)(2,1)} %collective-permute-done.1.refs_0_), channel_id=1, source_target_pairs={{0,4},{2,6},{4,0},{6,2},{1,5},{3,7},{5,1},{7,3},{8,12},{10,14},{12... | collective-permute-start | bytes 1966088 | tf_op jit(solution)/shard_map/ppermute | solution.py:27
  23.8 1.5 collective-permute-start.6
  25.3 8.0 %reshape_squeeze.3 = bf16[256,2,8,384]{3,2,1,0:T(8,128)(2,1)} reshape(bf16[1,1,256,2,3072]{4,3,2,1,0:T(2,128)(2,1)} %param.10) | data formatting | bytes 6291456 | tf_op jit(solution)/shard_map/reshape;squeeze | solution.py:404
  33.3 5.9 %copy.12 = bf16[256,2,8,384]{3,1,0,2:T(2,128)(2,1)} copy(bf16[256,2,8,384]{3,2,1,0:T(8,128)(2,1)} %reshape_squeeze.3) | data formatting | bytes 6291456 | tf_op jit(solution)/shard_map/reshape;squeeze | solution.py:404
  39.2 8.0 %reshape.9.value_ref = bf16[8,256,768]{2,1,0:T(8,128)(2,1)} reshape(bf16[8,256,2,384]{3,2,1,0:T(2,128)(2,1)} %bitcast.41) | data formatting | bytes 6291456 | tf_op jit(solution)/shard_map/reshape | solution.py:405
  47.3 1.9 %copy-done.2 = bf16[8,256,768]{2,1,0:T(8,128)(2,1)S(1)} copy-done((bf16[8,256,768]{2,1,0:T(8,128)(2,1)S(1)}, bf16[8,256,768]{2,1,0:T(8,128)(2,1)}, u32[]{:S(2)}) %copy-start.2) | copy-done | bytes 3145752
  49.1 1.7 %copy-done.3 = bf16[8,256,768]{2,1,0:T(8,128)(2,1)} copy-done((bf16[8,256,768]{2,1,0:T(8,128)(2,1)}, bf16[8,256,768]{2,1,0:T(8,128)(2,1)S(1)}, u32[]{:S(2)}) %copy-start.3) | copy-done | bytes 3145752
  50.8 4.8 %all-to-all-start = ((bf16[8,256,768]{2,1,0:T(8,128)(2,1)}), bf16[8,256,768]{2,1,0:T(8,128)(2,1)}, u32[]{:S(2)}, u32[]{:S(2)}) async-start(bf16[8,256,768]{2,1,0:T(8,128)(2,1)} %copy-done.3), calls=%async_computation | async-start | bytes 6291456 | tf_op jit(solution)/shard_map/all_to_all | solution.py:422
  55.6 1.5 modulated_norm.4.refs_0_
  57.4 2.6 %modulated_norm.5.refs_1_ = bf16[128,5120]{1,0:T(8,128)(2,1)S(1)} custom-call(bf16[64,5120]{1,0:T(8,128)(2,1)} %collective-permute-done.1.refs_0_, bf16[64,5120]{1,0:T(8,128)(2,1)S(1)} %collective-permute-done.2.refs_1_.refs_0_, f32[3,5120]{1,0:T(4,128)S(1)} %collective-permute-done.refs_2_), custom_call_target="tpu_custom_call" | custom-call | flops 1 | bytes 1 | tf_op jit(solution)/shard_map/modulated_norm/pallas_call | solution.py:54
  60.4 1.5 modulated_norm.6.refs_2_
  62.2 2.8 %modulated_norm.7.refs_3_ = bf16[128,5120]{1,0:T(8,128)(2,1)S(1)} custom-call(bf16[64,5120]{1,0:T(8,128)(2,1)} %collective-permute-done.5.refs_0_, bf16[64,5120]{1,0:T(8,128)(2,1)} %collective-permute-done.6.refs_1_, f32[3,5120]{1,0:T(4,128)S(1)} %collective-permute-done.refs_2_), custom_call_target="tpu_custom_call" | custom-call | flops 1 | bytes 1 | tf_op jit(solution)/shard_map/modulated_norm/pallas_call | solution.py:54
  65.5 2.7 %collective-permute-done.10.refs_7_ = bf16[128,5120]{1,0:T(8,128)(2,1)S(1)} collective-permute-done((bf16[128,5120]{1,0:T(8,128)(2,1)S(1)}, bf16[128,5120]{1,0:T(8,128)(2,1)S(1)}, u32[]{:S(2)}, u32[]{:S(2)}) %collective-permute-start.10) | collective-permute-done | bytes 1310752 | tf_op jit(solution)/shard_map/ppermute | solution.py:27
  68.1 18.8 %project_heads.1.heads_in = bf16[48,1024,128]{2,1,0:T(8,128)(2,1)} custom-call(bf16[128,5120]{1,0:T(8,128)(2,1)S(1)} %modulated_norm.4.refs_0_, bf16[128,5120]{1,0:T(8,128)(2,1)S(1)} %modulated_norm.5.refs_1_, bf16[128,5120]{1,0:T(8,128)(2,1)S(1)} %modulated_norm.6.refs_2_, bf16[128,5120]{1,0:T(8,128)(2,1)S(1)} %modulated_norm.7.refs_3_, ...), custom_call_target="tpu_custom_call" | custom-call | flops 12079595520 | bytes 22282240 | tf_op jit(solution)/shard_map/project_heads/pallas_call | solution.py:123
  86.9 5.9 %all-to-all-done = bf16[8,256,768]{2,1,0:T(8,128)(2,1)} async-done(((bf16[8,256,768]{2,1,0:T(8,128)(2,1)}), bf16[8,256,768]{2,1,0:T(8,128)(2,1)}, u32[]{:S(2)}, u32[]{:S(2)}) %all-to-all-start) | async-done | bytes 3145760 | tf_op jit(solution)/shard_map/all_to_all | solution.py:422
  92.8 6.0 %attend_first.1 = (bf16[512,384]{1,0:T(8,128)(2,1)S(1)}, bf16[9,1024,128]{2,1,0:T(8,128)(2,1)S(1)}, bf16[2048,768]{1,0:T(8,128)(2,1)S(1)}) custom-call(s32[4,6]{1,0:T(4,128)S(1)} %bitcast.39, bf16[48,1024,128]{2,1,0:T(8,128)(2,1)} %project_heads.1.heads_in, bf16[2048,768]{1,0:T(8,128)(2,1)} %bitcast.7.context_in), custom_call_target="tpu_custom_call" | custom-call | flops 1 | bytes 1 | tf_op jit(solution)/shard_map/attend_first/pallas_call | solution.py:223
  99.0 3.7 %attend_second.1.refs_2_ = bf16[512,384]{1,0:T(8,128)(2,1)S(1)} custom-call(s32[4,6]{1,0:T(4,128)S(1)} %bitcast.40, bf16[9,1024,128]{2,1,0:T(8,128)(2,1)S(1)} %get-tuple-element.52.heads_ref, bf16[2048,768]{1,0:T(8,128)(2,1)S(1)} %get-tuple-element.53.context_ref, bf16[512,384]{1,0:T(8,128)(2,1)S(1)} %get-tuple-element.54.refs_0_, ...), custom_call_target="tpu_custom_call" | custom-call | flops 1 | bytes 1 | tf_op jit(solution)/shard_map/attend_second/pallas_call | solution.py:249
  102.7 2.2 %sum_stage.10 = (bf16[128,1024]{1,0:T(8,128)(2,1)S(1)}, bf16[128,1024]{1,0:T(8,128)(2,1)S(1)}, f32[2,128,512]{2,1,0:T(8,128)S(1)}, f32[2,128,512]{2,1,0:T(8,128)S(1)}) custom-call(bf16[128,5120]{1,0:T(8,128)(2,1)S(1)} %bitcast.19, f32[2,5120]{1,0:T(2,128)S(1)} %pad_maximum_fusion.refs_1_, bf16[512,384]{1,0:T(8,128)(2,1)S(1)} %attend_second.1.refs_2_, ...), custom_call_target="tpu_custom_call" | custom-call | flops 1 | bytes 1 | tf_op jit(solution)/shard_map/sum_stage/pallas_call | solution.py:369
  104.9 1.1 collective-permute-start.13
  106.0 0.6 collective-permute-start.14
  106.5 2.2 %sum_stage.11 = (bf16[128,1024]{1,0:T(8,128)(2,1)S(1)}, bf16[128,1024]{1,0:T(8,128)(2,1)S(1)}, f32[2,128,512]{2,1,0:T(8,128)S(1)}, f32[2,128,512]{2,1,0:T(8,128)S(1)}) custom-call(bf16[128,5120]{1,0:T(8,128)(2,1)S(1)} %bitcast.20, f32[2,5120]{1,0:T(2,128)S(1)} %pad_maximum_fusion.refs_1_, bf16[512,384]{1,0:T(8,128)(2,1)S(1)} %attend_second.1.refs_2_, ...), custom_call_target="tpu_custom_call" | custom-call | flops 1 | bytes 1 | tf_op jit(solution)/shard_map/sum_stage/pallas_call | solution.py:369
  108.7 1.4 collective-permute-start.17
  110.1 1.2 collective-permute-start.18
  111.3 2.8 %collective-permute-done.13.refs_6_ = bf16[128,1024]{1,0:T(8,128)(2,1)S(1)} collective-permute-done((bf16[128,1024]{1,0:T(8,128)(2,1)S(1)}, bf16[128,1024]{1,0:T(8,128)(2,1)S(1)}, u32[]{:S(2)}, u32[]{:S(2)}) %collective-permute-start.13) | collective-permute-done | bytes 262176 | tf_op jit(solution)/shard_map/ppermute | solution.py:27
  114.1 1.0 collective-permute-done.14.refs_7_
  115.1 2.4 %sum_stage.12 = (bf16[128,1536]{1,0:T(8,128)(2,1)S(1)}, bf16[128,1536]{1,0:T(8,128)(2,1)S(1)}, f32[2,128,512]{2,1,0:T(8,128)S(1)}, f32[2,128,512]{2,1,0:T(8,128)...) custom-call(bf16[128,5120]{1,0:T(8,128)(2,1)S(1)} %bitcast.21, f32[2,5120]{1,0:T(2,128)S(1)} %pad_maximum_fusion.refs_1_, ...), custom_call_target="tpu_custom_call" | custom-call | flops 1 | bytes 1 | tf_op jit(solution)/shard_map/sum_stage/pallas_call | solution.py:369
  117.5 1.1 collective-permute-start.15
  118.6 0.9 collective-permute-start.16
  119.7 0.7 collective-permute-done.18.refs_7_
  120.3 2.4 %sum_stage.13 = (bf16[128,1536]{1,0:T(8,128)(2,1)S(1)}, bf16[128,1536]{1,0:T(8,128)(2,1)S(1)}, f32[2,128,512]{2,1,0:T(8,128)S(1)}, f32[2,128,512]{2,1,0:T(8,128)...) custom-call(bf16[128,5120]{1,0:T(8,128)(2,1)S(1)} %bitcast.22, f32[2,5120]{1,0:T(2,128)S(1)} %pad_maximum_fusion.refs_1_, ...), custom_call_target="tpu_custom_call" | custom-call | flops 1 | bytes 1 | tf_op jit(solution)/shard_map/sum_stage/pallas_call | solution.py:369
  122.7 1.1 collective-permute-start.20
  123.9 0.5 collective-permute-start.21
  124.4 5.2 %collective-permute-done.15.refs_6_ = bf16[128,1536]{1,0:T(8,128)(2,1)S(1)} collective-permute-done((bf16[128,1536]{1,0:T(8,128)(2,1)S(1)}, bf16[128,1536]{1,0:T(8,128)(2,1)S(1)}, u32[]{:S(2)}, u32[]{:S(2)}) %collective-permute-start.15) | collective-permute-done | bytes 393248 | tf_op jit(solution)/shard_map/ppermute | solution.py:27
  129.6 1.0 collective-permute-done.16.refs_7_
  130.6 1.9 %sum_stage.14 = (bf16[128,1024]{1,0:T(8,128)(2,1)S(1)}, bf16[128,1024]{1,0:T(8,128)(2,1)S(1)}, f32[2,128,256]{2,1,0:T(8,128)S(1)}, f32[2,128,256]{2,1,0:T(8,128)...) custom-call(bf16[128,5120]{1,0:T(8,128)(2,1)S(1)} %bitcast.23, ...), custom_call_target="tpu_custom_call" | custom-call | flops 1 | bytes 1 | tf_op jit(solution)/shard_map/sum_stage/pallas_call | solution.py:369
  132.5 1.6 collective-permute-start.19
  134.1 1.0 collective-permute-start.23
  135.1 0.6 collective-permute-start.24
  135.7 2.4 %collective-permute-done.20.refs_6_ = bf16[128,1536]{1,0:T(8,128)(2,1)S(1)} collective-permute-done((bf16[128,1536]{1,0:T(8,128)(2,1)S(1)}, bf16[128,1536]{1,0:T(8,128)(2,1)S(1)}, u32[]{:S(2)}, u32[]{:S(2)}) %collective-permute-start.20) | collective-permute-done | bytes 393248 | tf_op jit(solution)/shard_map/ppermute | solution.py:27
  138.0 1.0 collective-permute-done.21.refs_7_
  139.1 1.9 %sum_stage.15 = (bf16[128,1024]{1,0:T(8,128)(2,1)S(1)}, bf16[128,1024]{1,0:T(8,128)(2,1)S(1)}, f32[2,128,256]{2,1,0:T(8,128)S(1)}, f32[2,128,256]{2,1,0:T(8,128)...) custom-call(bf16[128,5120]{1,0:T(8,128)(2,1)S(1)} %bitcast.24, ...), custom_call_target="tpu_custom_call" | custom-call | flops 1 | bytes 1 | tf_op jit(solution)/shard_map/sum_stage/pallas_call | solution.py:369
  140.9 1.6 collective-permute-start.22
  142.6 1.0 collective-permute-start.26
  143.6 0.6 collective-permute-start.27
  144.3 1.6 collective-permute-start.25
  145.9 1.4 collective-permute-start.29
  147.2 3.4 %collective-permute-done.22.refs_9_ = bf16[128,1024]{1,0:T(8,128)(2,1)S(1)} collective-permute-done((bf16[128,1024]{1,0:T(8,128)(2,1)S(1)}, bf16[128,1024]{1,0:T(8,128)(2,1)S(1)}, u32[]{:S(2)}, u32[]{:S(2)}) %collective-permute-start.22) | collective-permute-done | bytes 262176 | tf_op jit(solution)/shard_map/ppermute | solution.py:22
  151.0 1.4 collective-permute-start.32
  152.8 1.3 collective-permute-start.33
  154.0 0.8 collective-permute-done.30.refs_3_
  154.9 1.1 collective-permute-done.25.refs_7_
  156.1 1.0 collective-permute-done.33.refs_3_
  157.1 1.6 collective-permute-start.34
  158.8 3.1 %collective-permute-done.28 = bf16[128,1024]{1,0:T(8,128)(2,1)S(1)} collective-permute-done((bf16[128,1024]{1,0:T(8,128)(2,1)S(1)}, bf16[128,1024]{1,0:T(8,128)(2,1)S(1)}, u32[]{:S(2)}, u32[]{:S(2)}) %collective-permute-start.28) | collective-permute-done | bytes 262176 | tf_op jit(solution)/shard_map/ppermute | solution.py:22
  161.9 1.4 collective-permute-done.31
  163.3 1.4 collective-permute-done.34
  164.7 1.0 copy-done.6
  (54 shorter events, 2.7 us)
Async XLA Ops:
  0.0 5.9 %copy-start.5 = (f32[1,1,3,5120]{3,1,2,0:T(1,128)S(1)}, f32[1,1,3,5120]{3,1,2,0:T(1,128)}, u32[]{:S(2)}) copy-start(f32[1,1,3,5120]{3,1,2,0:T(1,128)} %param.7) | copy-start | bytes 184324
  1.4 20.3 %collective-permute-start.1 = (bf16[64,5120]{1,0:T(8,128)(2,1)S(1)}, bf16[64,5120]{1,0:T(8,128)(2,1)}, u32[]{:S(2)}, u32[]{:S(2)}) collective-permute-start(bf16[64,5120]{1,0:T(8,128)(2,1)S(1)} %get-tuple-element.100), channel_id=1, source_target_pairs={{0,1},{1,0},{2,3},{3,2},{4,5},{5,4},{6,7},{7,6},{8,9},{9,8},{10,11... | collective-permute-start | bytes 1966088 | tf_op jit(solution)/shard_map/ppermute | solution.py:27
  4.4 19.4 %collective-permute-start.4 = (bf16[64,5120]{1,0:T(8,128)(2,1)S(1)}, bf16[64,5120]{1,0:T(8,128)(2,1)S(1)}, u32[]{:S(2)}, u32[]{:S(2)}) collective-permute-start(bf16[64,5120]{1,0:T(8,128)(2,1)S(1)} %get-tuple-element.99), channel_id=1, source_target_pairs={{0,4},{2,6},{4,0},{6,2},{1,5},{3,7},{5,1},{7,3},{8,12},{10,14},{12... | collective-permute-start | bytes 1966088 | tf_op jit(solution)/shard_map/ppermute | solution.py:27
  5.9 15.8 %collective-permute-start = (f32[3,5120]{1,0:T(4,128)S(1)}, f32[3,5120]{1,0:T(4,128)S(1)}, u32[]{:S(2)}, u32[]{:S(2)}) collective-permute-start(f32[3,5120]{1,0:T(4,128)S(1)} %bitcast.36), channel_id=1, source_target_pairs={{0,1},{1,0},{2,3},{3,2},{4,5},{5,4},{6,7},{7,6},{8,9},{9,8},{10,11... | collective-permute-start | bytes 184328 | tf_op jit(solution)/shard_map/ppermute | solution.py:27
  6.5 40.7 %collective-permute-start.2 = (bf16[64,5120]{1,0:T(8,128)(2,1)S(1)}, bf16[64,5120]{1,0:T(8,128)(2,1)S(1)}, u32[]{:S(2)}, u32[]{:S(2)}) collective-permute-start(bf16[64,5120]{1,0:T(8,128)(2,1)S(1)} %get-tuple-element.99), channel_id=1, source_target_pairs={{0,1},{1,0},{2,3},{3,2},{4,5},{5,4},{6,7},{7,6},{8,9},{9,8},{10,11... | collective-permute-start | bytes 1966088 | tf_op jit(solution)/shard_map/ppermute | solution.py:27
  8.0 39.2 %collective-permute-start.3 = (bf16[64,5120]{1,0:T(8,128)(2,1)S(1)}, bf16[64,5120]{1,0:T(8,128)(2,1)S(1)}, u32[]{:S(2)}, u32[]{:S(2)}) collective-permute-start(bf16[64,5120]{1,0:T(8,128)(2,1)S(1)} %get-tuple-element.100), channel_id=1, source_target_pairs={{0,4},{2,6},{4,0},{6,2},{1,5},{3,7},{5,1},{7,3},{8,12},{10,14},{12... | collective-permute-start | bytes 1966088 | tf_op jit(solution)/shard_map/ppermute | solution.py:27
  21.7 81.0 %collective-permute-start.12 = (bf16[384,5120]{1,0:T(8,128)(2,1)}, bf16[384,5120]{1,0:T(8,128)(2,1)}, u32[]{:S(2)}, u32[]{:S(2)}) collective-permute-start(bf16[384,5120]{1,0:T(8,128)(2,1)} %bitcast.29), channel_id=1, source_target_pairs={{0,2},{2,0},{4,6},{6,4},{1,3},{3,1},{5,7},{7,5},{8,10},{10,8},{12,... | collective-permute-start | bytes 11796488 | tf_op jit(solution)/shard_map/ppermute | solution.py:27
  21.7 40.2 %collective-permute-start.5 = (bf16[64,5120]{1,0:T(8,128)(2,1)}, bf16[64,5120]{1,0:T(8,128)(2,1)}, u32[]{:S(2)}, u32[]{:S(2)}) collective-permute-start(bf16[64,5120]{1,0:T(8,128)(2,1)} %collective-permute-done.1.refs_0_), channel_id=1, source_target_pairs={{0,4},{2,6},{4,0},{6,2},{1,5},{3,7},{5,1},{7,3},{8,12},{10,14},{12... | collective-permute-start | bytes 1966088 | tf_op jit(solution)/shard_map/ppermute | solution.py:27
  23.8 38.4 %collective-permute-start.6 = (bf16[64,5120]{1,0:T(8,128)(2,1)S(1)}, bf16[64,5120]{1,0:T(8,128)(2,1)}, u32[]{:S(2)}, u32[]{:S(2)}) collective-permute-start(bf16[64,5120]{1,0:T(8,128)(2,1)S(1)} %collective-permute-done.4.refs_1_), channel_id=1, source_target_pairs={{0,1},{1,0},{2,3},{3,2},{4,5},{5,4},{6,7},{7,6},{8,9},{9,8},{10,11... | collective-permute-start | bytes 1966088 | tf_op jit(solution)/shard_map/ppermute | solution.py:27
  47.3 1.9 %copy-start.2 = (bf16[8,256,768]{2,1,0:T(8,128)(2,1)S(1)}, bf16[8,256,768]{2,1,0:T(8,128)(2,1)}, u32[]{:S(2)}) copy-start(bf16[8,256,768]{2,1,0:T(8,128)(2,1)} %reshape.9.value_ref) | copy-start | bytes 9437188
  49.1 1.7 %copy-start.3 = (bf16[8,256,768]{2,1,0:T(8,128)(2,1)}, bf16[8,256,768]{2,1,0:T(8,128)(2,1)S(1)}, u32[]{:S(2)}) copy-start(bf16[8,256,768]{2,1,0:T(8,128)(2,1)S(1)} %after.1) | copy-start | bytes 9437188
  50.8 4.8 %copy-start = (bf16[1,1,128,5120]{3,2,1,0:T(8,128)(2,1)S(1)}, bf16[1,1,128,5120]{3,2,1,0:T(8,128)(2,1)}, u32[]{:S(2)}) copy-start(bf16[1,1,128,5120]{3,2,1,0:T(8,128)(2,1)} %param.6) | copy-start | bytes 3932164
  50.8 42.0 %all-to-all-start = ((bf16[8,256,768]{2,1,0:T(8,128)(2,1)}), bf16[8,256,768]{2,1,0:T(8,128)(2,1)}, u32[]{:S(2)}, u32[]{:S(2)}) async-start(bf16[8,256,768]{2,1,0:T(8,128)(2,1)} %copy-done.3), calls=%async_computation | async-start | bytes 6291456 | tf_op jit(solution)/shard_map/all_to_all | solution.py:422
  57.2 8.3 %collective-permute-start.7 = (bf16[128,5120]{1,0:T(8,128)(2,1)S(1)}, bf16[128,5120]{1,0:T(8,128)(2,1)S(1)}, u32[]{:S(2)}, u32[]{:S(2)}) collective-permute-start(bf16[128,5120]{1,0:T(8,128)(2,1)S(1)} %modulated_norm.4.refs_0_), channel_id=1, source_target_pairs={{0,2},{2,0},{4,6},{6,4},{1,3},{3,1},{5,7},{7,5},{8,10},{10,8},{12,... | collective-permute-start | bytes 3932168 | tf_op jit(solution)/shard_map/ppermute | solution.py:27
  60.0 5.4 %collective-permute-start.8 = (bf16[128,5120]{1,0:T(8,128)(2,1)S(1)}, bf16[128,5120]{1,0:T(8,128)(2,1)S(1)}, u32[]{:S(2)}, u32[]{:S(2)}) collective-permute-start(bf16[128,5120]{1,0:T(8,128)(2,1)S(1)} %modulated_norm.5.refs_1_), channel_id=1, source_target_pairs={{0,2},{2,0},{4,6},{6,4},{1,3},{3,1},{5,7},{7,5},{8,10},{10,8},{12,... | collective-permute-start | bytes 3932168 | tf_op jit(solution)/shard_map/ppermute | solution.py:27
  61.9 3.5 %collective-permute-start.9 = (bf16[128,5120]{1,0:T(8,128)(2,1)S(1)}, bf16[128,5120]{1,0:T(8,128)(2,1)S(1)}, u32[]{:S(2)}, u32[]{:S(2)}) collective-permute-start(bf16[128,5120]{1,0:T(8,128)(2,1)S(1)} %modulated_norm.6.refs_2_), channel_id=1, source_target_pairs={{0,2},{2,0},{4,6},{6,4},{1,3},{3,1},{5,7},{7,5},{8,10},{10,8},{12,... | collective-permute-start | bytes 3932168 | tf_op jit(solution)/shard_map/ppermute | solution.py:27
  65.0 3.1 %collective-permute-start.10 = (bf16[128,5120]{1,0:T(8,128)(2,1)S(1)}, bf16[128,5120]{1,0:T(8,128)(2,1)S(1)}, u32[]{:S(2)}, u32[]{:S(2)}) collective-permute-start(bf16[128,5120]{1,0:T(8,128)(2,1)S(1)} %modulated_norm.7.refs_3_), channel_id=1, source_target_pairs={{0,2},{2,0},{4,6},{6,4},{1,3},{3,1},{5,7},{7,5},{8,10},{10,8},{12,... | collective-permute-start | bytes 3932168 | tf_op jit(solution)/shard_map/ppermute | solution.py:27
  68.1 24.7 %copy-start.4 = (s32[1,4,6]{2,1,0:T(4,128)S(1)}, s32[1,4,6]{2,1,0:T(4,128)}, u32[]{:S(2)}) copy-start(s32[1,4,6]{2,1,0:T(4,128)} %param.11) | copy-start | bytes 292
  98.8 3.8 %collective-permute-start.11 = (bf16[512,384]{1,0:T(8,128)(2,1)S(1)}, bf16[512,384]{1,0:T(8,128)(2,1)S(1)}, u32[]{:S(2)}, u32[]{:S(2)}) collective-permute-start(bf16[512,384]{1,0:T(8,128)(2,1)S(1)} %get-tuple-element.54.refs_0_), channel_id=1, source_target_pairs={{0,2},{2,0},{4,6},{6,4},{1,3},{3,1},{5,7},{7,5},{8,10},{10,8},{12,... | collective-permute-start | bytes 1179656 | tf_op jit(solution)/shard_map/ppermute | solution.py:27
  99.0 3.7 %copy-start.1 = (bf16[1,384,5120]{2,1,0:T(8,128)(2,1)S(1)}, bf16[1,384,5120]{2,1,0:T(8,128)(2,1)}, u32[]{:S(2)}) copy-start(bf16[1,384,5120]{2,1,0:T(8,128)(2,1)} %param.9) | copy-start | bytes 11796484
  104.9 9.2 %collective-permute-start.13 = (bf16[128,1024]{1,0:T(8,128)(2,1)S(1)}, bf16[128,1024]{1,0:T(8,128)(2,1)S(1)}, u32[]{:S(2)}, u32[]{:S(2)}) collective-permute-start(bf16[128,1024]{1,0:T(8,128)(2,1)S(1)} %get-tuple-element.55), channel_id=1, source_target_pairs={{0,1},{1,0},{2,3},{3,2},{4,5},{5,4},{6,7},{7,6},{8,9},{9,8},{10,11... | collective-permute-start | bytes 786440 | tf_op jit(solution)/shard_map/ppermute | solution.py:27
  106.0 9.1 %collective-permute-start.14 = (bf16[128,1024]{1,0:T(8,128)(2,1)S(1)}, bf16[128,1024]{1,0:T(8,128)(2,1)S(1)}, u32[]{:S(2)}, u32[]{:S(2)}) collective-permute-start(bf16[128,1024]{1,0:T(8,128)(2,1)S(1)} %get-tuple-element.56), channel_id=1, source_target_pairs={{0,4},{2,6},{4,0},{6,2},{1,5},{3,7},{5,1},{7,3},{8,12},{10,14},{12... | collective-permute-start | bytes 786440 | tf_op jit(solution)/shard_map/ppermute | solution.py:27
  108.7 10.9 %collective-permute-start.17 = (bf16[128,1024]{1,0:T(8,128)(2,1)S(1)}, bf16[128,1024]{1,0:T(8,128)(2,1)S(1)}, u32[]{:S(2)}, u32[]{:S(2)}) collective-permute-start(bf16[128,1024]{1,0:T(8,128)(2,1)S(1)} %get-tuple-element.66), channel_id=1, source_target_pairs={{0,1},{1,0},{2,3},{3,2},{4,5},{5,4},{6,7},{7,6},{8,9},{9,8},{10,11... | collective-permute-start | bytes 786440 | tf_op jit(solution)/shard_map/ppermute | solution.py:27
  110.1 10.2 %collective-permute-start.18 = (bf16[128,1024]{1,0:T(8,128)(2,1)S(1)}, bf16[128,1024]{1,0:T(8,128)(2,1)S(1)}, u32[]{:S(2)}, u32[]{:S(2)}) collective-permute-start(bf16[128,1024]{1,0:T(8,128)(2,1)S(1)} %get-tuple-element.67), channel_id=1, source_target_pairs={{0,4},{2,6},{4,0},{6,2},{1,5},{3,7},{5,1},{7,3},{8,12},{10,14},{12... | collective-permute-start | bytes 786440 | tf_op jit(solution)/shard_map/ppermute | solution.py:27
  117.5 12.1 %collective-permute-start.15 = (bf16[128,1536]{1,0:T(8,128)(2,1)S(1)}, bf16[128,1536]{1,0:T(8,128)(2,1)S(1)}, u32[]{:S(2)}, u32[]{:S(2)}) collective-permute-start(bf16[128,1536]{1,0:T(8,128)(2,1)S(1)} %get-tuple-element.60), channel_id=1, source_target_pairs={{0,1},{1,0},{2,3},{3,2},{4,5},{5,4},{6,7},{7,6},{8,9},{9,8},{10,11... | collective-permute-start | bytes 1179656 | tf_op jit(solution)/shard_map/ppermute | solution.py:27
  118.6 12.1 %collective-permute-start.16 = (bf16[128,1536]{1,0:T(8,128)(2,1)S(1)}, bf16[128,1536]{1,0:T(8,128)(2,1)S(1)}, u32[]{:S(2)}, u32[]{:S(2)}) collective-permute-start(bf16[128,1536]{1,0:T(8,128)(2,1)S(1)} %get-tuple-element.61), channel_id=1, source_target_pairs={{0,4},{2,6},{4,0},{6,2},{1,5},{3,7},{5,1},{7,3},{8,12},{10,14},{12... | collective-permute-start | bytes 1179656 | tf_op jit(solution)/shard_map/ppermute | solution.py:27
  122.7 15.3 %collective-permute-start.20 = (bf16[128,1536]{1,0:T(8,128)(2,1)S(1)}, bf16[128,1536]{1,0:T(8,128)(2,1)S(1)}, u32[]{:S(2)}, u32[]{:S(2)}) collective-permute-start(bf16[128,1536]{1,0:T(8,128)(2,1)S(1)} %get-tuple-element.71), channel_id=1, source_target_pairs={{0,1},{1,0},{2,3},{3,2},{4,5},{5,4},{6,7},{7,6},{8,9},{9,8},{10,11... | collective-permute-start | bytes 1179656 | tf_op jit(solution)/shard_map/ppermute | solution.py:27
  123.9 15.2 %collective-permute-start.21 = (bf16[128,1536]{1,0:T(8,128)(2,1)S(1)}, bf16[128,1536]{1,0:T(8,128)(2,1)S(1)}, u32[]{:S(2)}, u32[]{:S(2)}) collective-permute-start(bf16[128,1536]{1,0:T(8,128)(2,1)S(1)} %get-tuple-element.72), channel_id=1, source_target_pairs={{0,4},{2,6},{4,0},{6,2},{1,5},{3,7},{5,1},{7,3},{8,12},{10,14},{12... | collective-permute-start | bytes 1179656 | tf_op jit(solution)/shard_map/ppermute | solution.py:27
  132.5 11.1 %collective-permute-start.19 = (bf16[128,1024]{1,0:T(8,128)(2,1)S(1)}, bf16[128,1024]{1,0:T(8,128)(2,1)S(1)}, u32[]{:S(2)}, u32[]{:S(2)}) collective-permute-start(bf16[128,1024]{1,0:T(8,128)(2,1)S(1)} %get-tuple-element.70.refs_12_), channel_id=1, source_target_pairs={{0,8},{8,16},{16,24},{24,0},{1,9},{9,17},{17,25},{25,1},{2,10},{10... | collective-permute-start | bytes 786440 | tf_op jit(solution)/shard_map/ppermute | solution.py:22
  134.1 10.0 %collective-permute-start.23 = (bf16[128,1024]{1,0:T(8,128)(2,1)S(1)}, bf16[128,1024]{1,0:T(8,128)(2,1)S(1)}, u32[]{:S(2)}, u32[]{:S(2)}) collective-permute-start(bf16[128,1024]{1,0:T(8,128)(2,1)S(1)} %get-tuple-element.77), channel_id=1, source_target_pairs={{0,1},{1,0},{2,3},{3,2},{4,5},{5,4},{6,7},{7,6},{8,9},{9,8},{10,11... | collective-permute-start | bytes 786440 | tf_op jit(solution)/shard_map/ppermute | solution.py:27
  135.1 9.0 %collective-permute-start.24 = (bf16[128,1024]{1,0:T(8,128)(2,1)S(1)}, bf16[128,1024]{1,0:T(8,128)(2,1)S(1)}, u32[]{:S(2)}, u32[]{:S(2)}) collective-permute-start(bf16[128,1024]{1,0:T(8,128)(2,1)S(1)} %get-tuple-element.78), channel_id=1, source_target_pairs={{0,4},{2,6},{4,0},{6,2},{1,5},{3,7},{5,1},{7,3},{8,12},{10,14},{12... | collective-permute-start | bytes 786440 | tf_op jit(solution)/shard_map/ppermute | solution.py:27
  140.9 9.7 %collective-permute-start.22 = (bf16[128,1024]{1,0:T(8,128)(2,1)S(1)}, bf16[128,1024]{1,0:T(8,128)(2,1)S(1)}, u32[]{:S(2)}, u32[]{:S(2)}) collective-permute-start(bf16[128,1024]{1,0:T(8,128)(2,1)S(1)} %get-tuple-element.76.refs_8_), channel_id=1, source_target_pairs={{0,8},{8,16},{16,24},{24,0},{1,9},{9,17},{17,25},{25,1},{2,10},{10... | collective-permute-start | bytes 786440 | tf_op jit(solution)/shard_map/ppermute | solution.py:22
  142.6 8.3 %collective-permute-start.26 = (bf16[128,1024]{1,0:T(8,128)(2,1)S(1)}, bf16[128,1024]{1,0:T(8,128)(2,1)S(1)}, u32[]{:S(2)}, u32[]{:S(2)}) collective-permute-start(bf16[128,1024]{1,0:T(8,128)(2,1)S(1)} %get-tuple-element.84), channel_id=1, source_target_pairs={{0,1},{1,0},{2,3},{3,2},{4,5},{5,4},{6,7},{7,6},{8,9},{9,8},{10,11... | collective-permute-start | bytes 786440 | tf_op jit(solution)/shard_map/ppermute | solution.py:27
  143.6 7.3 %collective-permute-start.27 = (bf16[128,1024]{1,0:T(8,128)(2,1)S(1)}, bf16[128,1024]{1,0:T(8,128)(2,1)S(1)}, u32[]{:S(2)}, u32[]{:S(2)}) collective-permute-start(bf16[128,1024]{1,0:T(8,128)(2,1)S(1)} %get-tuple-element.85), channel_id=1, source_target_pairs={{0,4},{2,6},{4,0},{6,2},{1,5},{3,7},{5,1},{7,3},{8,12},{10,14},{12... | collective-permute-start | bytes 786440 | tf_op jit(solution)/shard_map/ppermute | solution.py:27
  144.3 11.7 %collective-permute-start.25 = (bf16[128,1024]{1,0:T(8,128)(2,1)S(1)}, bf16[128,1024]{1,0:T(8,128)(2,1)S(1)}, u32[]{:S(2)}, u32[]{:S(2)}) collective-permute-start(bf16[128,1024]{1,0:T(8,128)(2,1)S(1)} %get-tuple-element.83.refs_8_), channel_id=1, source_target_pairs={{0,8},{8,16},{16,24},{24,0},{1,9},{9,17},{17,25},{25,1},{2,10},{10... | collective-permute-start | bytes 786440 | tf_op jit(solution)/shard_map/ppermute | solution.py:22
  145.9 6.9 %collective-permute-start.29 = (bf16[128,256]{1,0:T(8,128)(2,1)S(1)}, bf16[128,256]{1,0:T(8,128)(2,1)S(1)}, u32[]{:S(2)}, u32[]{:S(2)}) collective-permute-start(bf16[128,256]{1,0:T(8,128)(2,1)S(1)} %get-tuple-element.91), channel_id=1, source_target_pairs={{0,1},{1,0},{2,3},{3,2},{4,5},{5,4},{6,7},{7,6},{8,9},{9,8},{10,11... | collective-permute-start | bytes 196616 | tf_op jit(solution)/shard_map/ppermute | solution.py:27
  150.6 4.3 %collective-permute-start.30 = (bf16[128,256]{1,0:T(8,128)(2,1)S(1)}, bf16[128,256]{1,0:T(8,128)(2,1)S(1)}, u32[]{:S(2)}, u32[]{:S(2)}) collective-permute-start(bf16[128,256]{1,0:T(8,128)(2,1)S(1)} %get-tuple-element.92), channel_id=1, source_target_pairs={{0,4},{2,6},{4,0},{6,2},{1,5},{3,7},{5,1},{7,3},{8,12},{10,14},{12... | collective-permute-start | bytes 196616 | tf_op jit(solution)/shard_map/ppermute | solution.py:27
  151.0 5.1 %collective-permute-start.32 = (bf16[128,256]{1,0:T(8,128)(2,1)S(1)}, bf16[128,256]{1,0:T(8,128)(2,1)S(1)}, u32[]{:S(2)}, u32[]{:S(2)}) collective-permute-start(bf16[128,256]{1,0:T(8,128)(2,1)S(1)} %get-tuple-element.95), channel_id=1, source_target_pairs={{0,1},{1,0},{2,3},{3,2},{4,5},{5,4},{6,7},{7,6},{8,9},{9,8},{10,11... | collective-permute-start | bytes 196616 | tf_op jit(solution)/shard_map/ppermute | solution.py:27
  152.4 9.4 %collective-permute-start.28 = (bf16[128,1024]{1,0:T(8,128)(2,1)S(1)}, bf16[128,1024]{1,0:T(8,128)(2,1)S(1)}, u32[]{:S(2)}, u32[]{:S(2)}) collective-permute-start(bf16[128,1024]{1,0:T(8,128)(2,1)S(1)} %get-tuple-element.90.refs_6_), channel_id=1, source_target_pairs={{0,8},{8,16},{16,24},{24,0},{1,9},{9,17},{17,25},{25,1},{2,10},{10... | collective-permute-start | bytes 786440 | tf_op jit(solution)/shard_map/ppermute | solution.py:22
  152.8 4.3 %collective-permute-start.33 = (bf16[128,256]{1,0:T(8,128)(2,1)S(1)}, bf16[128,256]{1,0:T(8,128)(2,1)S(1)}, u32[]{:S(2)}, u32[]{:S(2)}) collective-permute-start(bf16[128,256]{1,0:T(8,128)(2,1)S(1)} %get-tuple-element.96), channel_id=1, source_target_pairs={{0,4},{2,6},{4,0},{6,2},{1,5},{3,7},{5,1},{7,3},{8,12},{10,14},{12... | collective-permute-start | bytes 196616 | tf_op jit(solution)/shard_map/ppermute | solution.py:27
  156.0 7.2 %collective-permute-start.31 = (bf16[128,512]{1,0:T(8,128)(2,1)S(1)}, bf16[128,512]{1,0:T(8,128)(2,1)S(1)}, u32[]{:S(2)}, u32[]{:S(2)}) collective-permute-start(bf16[128,512]{1,0:T(8,128)(2,1)S(1)} %sum_stage.18.refs_6_), channel_id=1, source_target_pairs={{0,8},{8,16},{16,24},{24,0},{1,9},{9,17},{17,25},{25,1},{2,10},{10... | collective-permute-start | bytes 393224 | tf_op jit(solution)/shard_map/ppermute | solution.py:22
  157.1 7.5 %collective-permute-start.34 = (bf16[128,512]{1,0:T(8,128)(2,1)S(1)}, bf16[128,512]{1,0:T(8,128)(2,1)S(1)}, u32[]{:S(2)}, u32[]{:S(2)}) collective-permute-start(bf16[128,512]{1,0:T(8,128)(2,1)S(1)} %sum_stage.19), channel_id=1, source_target_pairs={{0,8},{8,16},{16,24},{24,0},{1,9},{9,17},{17,25},{25,1},{2,10},{10... | collective-permute-start | bytes 393224 | tf_op jit(solution)/shard_map/ppermute | solution.py:22
  164.7 1.1 copy-start.6

commit v12 on v10

--- a/solution.py
+++ b/solution.py
@@ -10,6 +10,7 @@
 HD = 128
 TILE = 128
 MIB = 2**20
+SPARE = 39
 CHUNK_SHARES = (4, 4, 4, 4, 2, 2)
 
 guidance_scale = 5.0
@@ -44,7 +45,7 @@
             ).astype(jnp.bfloat16)
             return carry
 
-        lax.fori_loop(0, part.shape[0] // step, body, 0)
+        lax.fori_loop(0, part.shape[0] // step, body, 0, unroll=2)
         start += part.shape[0]
 
 
@@ -90,7 +91,7 @@
     def _():
         total_ref[...] = product
 
-    @pl.when(step > 0)
+    @pl.when((step > 0) & (step < steps - 1))
     def _():
         total_ref[...] += product
 
@@ -99,7 +100,8 @@
         heads = heads_ref.shape[0]
         copies = []
         for head in range(heads):
-            values = total_ref[:, head * HD : (head + 1) * HD]
+            columns = slice(head * HD, (head + 1) * HD)
+            values = total_ref[:, columns] + product[:, columns]
             if head < 2 * heads // 3:
                 square = jnp.mean(values * values, axis=-1, keepdims=True)
                 values = values * lax.rsqrt(square + 1e-06)
@@ -114,7 +116,7 @@
 
 def project(blocks, weights):
     _, depth, width = weights.shape
-    steps = 4
+    steps = 2
     block = depth // steps
     count = sum(rows.shape[0] for rows in blocks)
     heads = 3 * width // HD
@@ -124,7 +126,7 @@
         in_specs=[pl.BlockSpec(memory_space=pltpu.VMEM)] * len(blocks)
         + [pl.BlockSpec((3, block, width), lambda k: (0, k, 0))],
         out_specs=pl.BlockSpec(memory_space=pltpu.HBM),
-        out_shape=jax.ShapeDtypeStruct((heads, count, HD), jnp.bfloat16),
+        out_shape=jax.ShapeDtypeStruct((heads + SPARE, count, HD), jnp.bfloat16),
         scratch_shapes=[
             pltpu.VMEM((count, 3 * width), jnp.float32),
             pltpu.VMEM((heads, count, HD), jnp.bfloat16),
@@ -196,11 +198,12 @@
         out_ref[out_rows, head * HD : (head + 1) * HD] = (mixed / total).astype(jnp.bfloat16)
         return carry
 
-    lax.fori_loop(0, out_ref.shape[0] // TILE, body, 0, unroll=2)
-
-
-def attend_kernel(visible_ref, heads_in, context_in, *refs, first_block):
-    out_ref, heads_ref, context_ref, sems = refs[-4:]
+    lax.fori_loop(0, out_ref.shape[0] // TILE, body, 0, unroll=True)
+
+
+def attend_first_kernel(
+    visible_ref, heads_in, context_in, out_ref, heads_ref, context_ref, sems
+):
     heads = heads_ref.shape[0] // 3
     copies = []
     for head in range(heads):
@@ -223,30 +226,67 @@
     for head in range(heads):
         for copy in copies[head]:
             copy.wait()
+        first_block = out_ref.shape[0] // TILE
         attend_head(visible_ref, heads_ref, context_ref, out_ref, first_block, head)
 
 
-def attend(heads, context, visible, first_block, earlier):
-    count = heads.shape[1] // 2
+def attend_first(heads, context, visible):
+    number, count = heads.shape[0] - SPARE, heads.shape[1] // 2
     return pl.pallas_call(
-        functools.partial(attend_kernel, first_block=first_block),
+        attend_first_kernel,
         in_specs=[
             pl.BlockSpec(memory_space=pltpu.SMEM),
             pl.BlockSpec(memory_space=pltpu.HBM),
             pl.BlockSpec(memory_space=pl.ANY),
-        ]
-        + [pl.BlockSpec(memory_space=pl.ANY)] * len(earlier),
-        out_specs=pl.BlockSpec(memory_space=pltpu.VMEM),
-        out_shape=jax.ShapeDtypeStruct((count, heads.shape[0] // 3 * HD), jnp.bfloat16),
-        scratch_shapes=[
-            pltpu.VMEM(heads.shape, heads.dtype),
-            pltpu.VMEM(context.shape, context.dtype),
-            pltpu.SemaphoreType.DMA((heads.shape[0] // 3, 5)),
         ],
-        name="attend",
+        out_specs=[pl.BlockSpec(memory_space=pltpu.VMEM)] * 3,
+        out_shape=[
+            jax.ShapeDtypeStruct((count, number // 3 * HD), jnp.bfloat16),
+            jax.ShapeDtypeStruct((number,) + heads.shape[1:], heads.dtype),
+            jax.ShapeDtypeStruct(context.shape, context.dtype),
+        ],
+        scratch_shapes=[pltpu.SemaphoreType.DMA((number // 3, 5))],
+        name="attend_first",
         cost_estimate=SHORT,
-        compiler_params=pltpu.CompilerParams(vmem_limit_bytes=53 * MIB),
-    )(visible, heads, context, *earlier)
+        compiler_params=pltpu.CompilerParams(vmem_limit_bytes=44 * MIB),
+    )(visible, heads, context)
+
+
+def attend_second_kernel(visible_ref, heads_ref, context_ref, *refs):
+    weights_ref, core_weights_ref = refs[:2]
+    out_ref, both_ref, sems = refs[-3:]
+    depth, columns = weights_ref.shape[0], pl.ds(0, both_ref.shape[1])
+    copies = [
+        pltpu.make_async_copy(
+            ref.at[:, columns], both_ref.at[pl.ds(core * depth, depth)], sems.at[core]
+        )
+        for core, ref in enumerate((weights_ref, core_weights_ref))
+    ]
+    for copy in copies:
+        copy.start()
+    for head in range(heads_ref.shape[0] // 3):
+        attend_head(visible_ref, heads_ref, context_ref, out_ref, 0, head)
+    for copy in copies:
+        copy.wait()
+
+
+def attend_second(heads, context, visible, weights, core_weights, columns, earlier):
+    count = heads.shape[1] // 2
+    return pl.pallas_call(
+        attend_second_kernel,
+        in_specs=[pl.BlockSpec(memory_space=pltpu.SMEM)]
+        + [pl.BlockSpec(memory_space=pltpu.VMEM)] * 2
+        + [pl.BlockSpec(memory_space=pl.ANY)] * (2 + len(earlier)),
+        out_specs=[pl.BlockSpec(memory_space=pltpu.VMEM)] * 2,
+        out_shape=[
+            jax.ShapeDtypeStruct((count, heads.shape[0] // 3 * HD), jnp.bfloat16),
+            jax.ShapeDtypeStruct((2 * weights.shape[0], columns), weights.dtype),
+        ],
+        scratch_shapes=[pltpu.SemaphoreType.DMA((2,))],
+        name="attend_second",
+        cost_estimate=SHORT,
+        compiler_params=pltpu.CompilerParams(vmem_limit_bytes=12 * MIB),
+    )(visible, heads, context, weights, core_weights, *earlier)
 
 
 def combined(own, other, mine, gates_ref, columns):
@@ -298,8 +338,9 @@
             [
                 named[name]
                 for name in (
-                    "attended", "core_attended", "weights", "core_weights", "rows", "gates"
+                    "attended", "core_attended", "weights", "core_weights", "both", "rows", "gates"
                 )
+                if name in named
             ],
             named["across_out"],
             named["along_out"],
@@ -391,13 +432,14 @@
 
     context_rows = stale_cache.shape[2]
     width = project_in.shape[3]
-    packed = stale_cache[0, 0].reshape(context_rows, 2, devices, width)
-    packed = packed.transpose(2, 0, 1, 3).reshape(devices, context_rows, 2 * width)
+    unpacked = stale_cache[0, 0].reshape(context_rows, 2, devices, width)
+    packed = unpacked.transpose(2, 0, 1, 3).reshape(devices, context_rows, 2 * width)
 
     upper, lower = current[: token_rows // 2], current[token_rows // 2 :]
     across_upper, along_lower = from_partner(upper, "cfg", 1), from_partner(lower, "sp", 2)
     across_lower, along_upper = from_partner(lower, "cfg", 1), from_partner(upper, "sp", 2)
-    other_modulate = from_partner(modulate, "cfg", 1)
+    other_modulate = from_partner(modulation, "cfg", 1)[0, 0]
+    across_upper, along_lower = after(across_upper, (unpacked,)), after(along_lower, (unpacked,))
     first, second = from_partner(across_upper, "sp", 2), from_partner(along_lower, "cfg", 1)
     core_weights = from_partner(project_out[0], "sp", 1)
     near = [
@@ -408,7 +450,7 @@
     ]
     far = [from_partner(rows, "sp", 1) for rows in near]
 
-    packed = after(packed, (across_lower, along_upper, other_modulate))
+    packed = after(packed, (across_lower, along_upper))
     context = lax.all_to_all(packed, ("sp", "cfg"), split_axis=0, concat_axis=0, tiled=True)
     context = context.reshape(devices * context_rows, 2 * width)
 
@@ -419,21 +461,22 @@
     chunks = [
         (sum(CHUNK_SHARES[:index]) * unit, share * unit) for index, share in enumerate(CHUNK_SHARES)
     ]
-    for_core = attend(heads, context, visible[0], heads.shape[1] // TILE // 2, ())
+    for_core, heads, context = attend_first(heads, context, visible[0])
     core_attended = from_partner(for_core, "sp", 1)
-    attended = attend(heads, context, visible[0], 0, (for_core, gates))
+    attended, first_weights = attend_second(
+        heads, context, visible[0], project_out[0], core_weights, chunks[0][1], (for_core, gates)
+    )
 
     kept, left, flights, arrivals, earlier = {}, {}, {}, [], []
     for index in range(-2, count + 2):
         fresh, middle, final = index + 2 < count, 0 <= index < count, index >= 2
         operands = {"rows": current, "gates": gates}
         if fresh:
-            operands.update(
-                attended=attended,
-                core_attended=core_attended,
-                weights=project_out[0],
-                core_weights=core_weights,
-            )
+            operands.update(attended=attended, core_attended=core_attended)
+            if index == -2:
+                operands["both"] = first_weights
+            else:
+                operands.update(weights=project_out[0], core_weights=core_weights)
         if index >= 0:
             operands["across"], operands["along"] = flights.pop(index)
         if middle:

time: 169 us -> 164 us (0.970)
  Pallas kernels: 57.5 us -> 49.7 us
  local copies, waits for them, and re-layouts: 28.2 us -> 30.3 us
    ppermute x29, waiting for transfers between devices: 31 us -> 23.5 us  [from_partner(): return lax.ppermute(value, axis, pairs)]
    all_to_all x1, waiting for transfers between devices: 1.19 us -> 7.27 us  [per_device(): lax.all_to_all(packed, ('sp', 'cfg'), split_axis=0, concat_axis=0, tiled=...]
    another operation x2 -> x1, local copies, waits for them, and re-layouts: 14 us -> 8 us  [per_device(): unpacked = stale_cache[0, 0].reshape(context_rows, 2, devices, width)]
    transpose x0 -> x1, local copies, waits for them, and re-layouts: none -> 4.09 us  [per_device(): unpacked.transpose(2, 0, 1, 3).reshape(devices, context_rows, 2 * width)]
    pallas_call x4, Pallas kernels: 12.2 us -> 8.42 us  [modulated_norm(): pl.pallas_call(norm_kernel, in_specs=[pl.BlockSpec(memory_space=pltpu.VME...]
    ppermute x29, starting transfers between devices: 28.3 us -> 24.7 us  [from_partner(): return lax.ppermute(value, axis, pairs)]
    unnamed x20 -> x28, local copies, waits for them, and re-layouts: 4.82 us -> 7.69 us
    ppermute x6, waiting for transfers between devices: 10.3 us -> 13 us  [from_behind(): return lax.ppermute(x, axis, [(i, (i + by) % count) for i in range(count)])]
  transfers between devices with their start and end apart: 36 -> 36, of which waited for: 19 -> 16; matrix products, arithmetic and copies ran while one was open for 13% -> 12% of each run, Pallas kernels for 33% -> 30%
where the time goes in v12:
time: 164 us; the launch traced here: 163 us
  Pallas kernels  49.7 us (30%)
  waiting for transfers between devices  43.8 us (27%)
  starting transfers between devices  38.7 us (24%)
  local copies, waits for them, and re-layouts  30.3 us (18%)
    ppermute x29, starting transfers between devices, from_partner(): return lax.ppermute(value, axis, pairs)  24.7 us
    ppermute x29, waiting for transfers between devices, from_partner(): return lax.ppermute(value, axis, pairs)  23.5 us
    pallas_call x1, Pallas kernels, project(): pl.pallas_call(functools.partial(project_kernel, blocks=len(blocks)), gri...  19.2 us
    ppermute x6, waiting for transfers between devices, from_behind(): return lax.ppermute(x, axis, [(i, (i + by) % count) for i in range(count)])  13 us
    pallas_call x10, Pallas kernels, stage(): pl.pallas_call(functools.partial(stage_kernel, parts=parts, start=start,...  12.1 us
    ppermute x6, starting transfers between devices, from_behind(): return lax.ppermute(x, axis, [(i, (i + by) % count) for i in range(count)])  9.33 us
    pallas_call x4, Pallas kernels, modulated_norm(): pl.pallas_call(norm_kernel, in_specs=[pl.BlockSpec(memory_space=pltpu.VME...  8.42 us
    reshape x1, local copies, waits for them, and re-layouts, per_device(): unpacked.transpose(2, 0, 1, 3).reshape(devices, context_rows, 2 * width)  8.04 us
  transfers between devices with their start and end apart: 36, of which 16 were waited for; matrix products, arithmetic and copies ran while one was open for 12% of the time, Pallas kernels for 30%

profile of v12, /device:TPU:0, one launch (start us, length us, event | category | flops | bytes accessed | tf_op | source)
XLA Modules:
  0.0 162.9 jit_solution(6827311367554708634)
XLA Ops:
  0.0 2.5 %slice_bitcast_fusion = (bf16[64,5120]{1,0:T(8,128)(2,1)}, bf16[64,5120]{1,0:T(8,128)(2,1)}) fusion(bf16[1,1,128,5120]{3,2,1,0:T(8,128)(2,1)} %param.6), kind=kLoop, calls=%fused_computation | loop fusion | bytes 2621440 | tf_op jit(solution)/shard_map/slice | solution.py:438
  2.5 2.9 %collective-permute-start.1 = (bf16[64,5120]{1,0:T(8,128)(2,1)}, bf16[64,5120]{1,0:T(8,128)(2,1)S(1)}, u32[]{:S(2)}, u32[]{:S(2)}) collective-permute-start(bf16[64,5120]{1,0:T(8,128)(2,1)} %get-tuple-element.104), channel_id=1, source_target_pairs={{0,1},{1,0},{2,3},{3,2},{4,5},{5,4},{6,7},{7,6},{8,9},{9,8},{10,11... | collective-permute-start | bytes 1966088 | tf_op jit(solution)/shard_map/ppermute | solution.py:27
  5.4 1.5 collective-permute-start.4
  7.5 8.0 %reshape_squeeze.3.refs_0_ = bf16[256,2,8,384]{3,2,1,0:T(8,128)(2,1)} reshape(bf16[1,1,256,2,3072]{4,3,2,1,0:T(2,128)(2,1)} %param.10) | data formatting | bytes 6291456 | tf_op jit(solution)/shard_map/reshape;squeeze | solution.py:435
  15.5 5.7 %collective-permute-done.1.value_ref = bf16[64,5120]{1,0:T(8,128)(2,1)S(1)} collective-permute-done((bf16[64,5120]{1,0:T(8,128)(2,1)}, bf16[64,5120]{1,0:T(8,128)(2,1)S(1)}, u32[]{:S(2)}, u32[]{:S(2)}) %collective-permute-start.1) | collective-permute-done | bytes 655392 | tf_op jit(solution)/shard_map/ppermute | solution.py:27
  21.2 1.9 %copy-done.2 = bf16[256,2,8,384]{3,2,1,0:T(8,128)(2,1)S(1)} copy-done((bf16[256,2,8,384]{3,2,1,0:T(8,128)(2,1)S(1)}, bf16[256,2,8,384]{3,2,1,0:T(8,128)(2,1)}, u32[]{:S(2)}) %copy-start.2) | copy-done | bytes 3145752
  23.1 2.1 %collective-permute-start.5 = (bf16[64,5120]{1,0:T(8,128)(2,1)S(1)}, bf16[64,5120]{1,0:T(8,128)(2,1)}, u32[]{:S(2)}, u32[]{:S(2)}) collective-permute-start(bf16[64,5120]{1,0:T(8,128)(2,1)S(1)} %after.3.refs_0_), channel_id=1, source_target_pairs={{0,4},{2,6},{4,0},{6,2},{1,5},{3,7},{5,1},{7,3},{8,12},{10,14},{12... | collective-permute-start | bytes 1966088 | tf_op jit(solution)/shard_map/ppermute | solution.py:27
  25.2 1.8 %collective-permute-start.6 = (bf16[64,5120]{1,0:T(8,128)(2,1)S(1)}, bf16[64,5120]{1,0:T(8,128)(2,1)}, u32[]{:S(2)}, u32[]{:S(2)}) collective-permute-start(bf16[64,5120]{1,0:T(8,128)(2,1)S(1)} %after.4.refs_1_), channel_id=1, source_target_pairs={{0,1},{1,0},{2,3},{3,2},{4,5},{5,4},{6,7},{7,6},{8,9},{9,8},{10,11... | collective-permute-start | bytes 1966088 | tf_op jit(solution)/shard_map/ppermute | solution.py:27
  27.3 1.5 modulated_norm.4.refs_0_
  28.8 1.0 copy-done.6
  29.9 4.1 %copy.11 = bf16[8,256,2,384]{3,2,1,0:T(2,128)(2,1)} copy(bf16[8,256,2,384]{3,0,2,1:T(8,128)(2,1)S(1)} %bitcast.37) | data formatting | bytes 6291456 | tf_op jit(solution)/shard_map/transpose | solution.py:436
  34.0 8.0 %reshape.10.value_ref = bf16[8,256,768]{2,1,0:T(8,128)(2,1)} reshape(bf16[8,256,2,384]{3,2,1,0:T(2,128)(2,1)} %copy.11) | data formatting | bytes 6291456 | tf_op jit(solution)/shard_map/reshape | solution.py:436
  42.5 1.9 %copy-done.4 = bf16[8,256,768]{2,1,0:T(8,128)(2,1)S(1)} copy-done((bf16[8,256,768]{2,1,0:T(8,128)(2,1)S(1)}, bf16[8,256,768]{2,1,0:T(8,128)(2,1)}, u32[]{:S(2)}) %copy-start.4) | copy-done | bytes 3145752
  44.4 1.7 %copy-done.5 = bf16[8,256,768]{2,1,0:T(8,128)(2,1)} copy-done((bf16[8,256,768]{2,1,0:T(8,128)(2,1)}, bf16[8,256,768]{2,1,0:T(8,128)(2,1)S(1)}, u32[]{:S(2)}) %copy-start.5) | copy-done | bytes 3145752
  46.1 4.6 %all-to-all-start = ((bf16[8,256,768]{2,1,0:T(8,128)(2,1)}), bf16[8,256,768]{2,1,0:T(8,128)(2,1)}, u32[]{:S(2)}, u32[]{:S(2)}) async-start(bf16[8,256,768]{2,1,0:T(8,128)(2,1)} %copy-done.5), calls=%async_computation | async-start | bytes 6291456 | tf_op jit(solution)/shard_map/all_to_all | solution.py:454
  50.7 2.6 %modulated_norm.5.refs_1_ = bf16[128,5120]{1,0:T(8,128)(2,1)S(1)} custom-call(bf16[64,5120]{1,0:T(8,128)(2,1)S(1)} %after.3.refs_0_, bf16[64,5120]{1,0:T(8,128)(2,1)} %collective-permute-done.2.refs_1_.refs_0_, f32[3,5120]{1,0:T(4,128)S(1)} %bitcast.40), custom_call_target="tpu_custom_call" | custom-call | flops 1 | bytes 1 | tf_op jit(solution)/shard_map/modulated_norm/pallas_call | solution.py:54
  53.6 1.5 modulated_norm.6.refs_2_
  55.5 2.8 %modulated_norm.7.refs_3_ = bf16[128,5120]{1,0:T(8,128)(2,1)S(1)} custom-call(bf16[64,5120]{1,0:T(8,128)(2,1)} %collective-permute-done.5.refs_0_, bf16[64,5120]{1,0:T(8,128)(2,1)} %collective-permute-done.6.refs_1_, f32[3,5120]{1,0:T(4,128)S(1)} %bitcast.41), custom_call_target="tpu_custom_call" | custom-call | flops 1 | bytes 1 | tf_op jit(solution)/shard_map/modulated_norm/pallas_call | solution.py:54
  58.8 2.7 %collective-permute-done.10.refs_7_ = bf16[128,5120]{1,0:T(8,128)(2,1)S(1)} collective-permute-done((bf16[128,5120]{1,0:T(8,128)(2,1)S(1)}, bf16[128,5120]{1,0:T(8,128)(2,1)S(1)}, u32[]{:S(2)}, u32[]{:S(2)}) %collective-permute-start.10) | collective-permute-done | bytes 1310752 | tf_op jit(solution)/shard_map/ppermute | solution.py:27
  61.4 19.2 %project_heads.1.heads_in = bf16[48,1024,128]{2,1,0:T(8,128)(2,1)} custom-call(bf16[128,5120]{1,0:T(8,128)(2,1)S(1)} %copy-done.7, bf16[128,5120]{1,0:T(8,128)(2,1)S(1)} %modulated_norm.5.refs_1_, bf16[128,5120]{1,0:T(8,128)(2,1)S(1)} %modulated_norm.6.refs_2_, bf16[128,5120]{1,0:T(8,128)(2,1)S(1)} %modulated_norm.7.refs_3_, ...), custom_call_target="tpu_custom_call" | custom-call | flops 12079595520 | bytes 22282240 | tf_op jit(solution)/shard_map/project_heads/pallas_call | solution.py:123
  80.6 7.3 %all-to-all-done = bf16[8,256,768]{2,1,0:T(8,128)(2,1)} async-done(((bf16[8,256,768]{2,1,0:T(8,128)(2,1)}), bf16[8,256,768]{2,1,0:T(8,128)(2,1)}, u32[]{:S(2)}, u32[]{:S(2)}) %all-to-all-start) | async-done | bytes 3145760 | tf_op jit(solution)/shard_map/all_to_all | solution.py:454
  87.9 5.5 %attend_first.1 = (bf16[512,384]{1,0:T(8,128)(2,1)S(1)}, bf16[9,1024,128]{2,1,0:T(8,128)(2,1)S(1)}, bf16[2048,768]{1,0:T(8,128)(2,1)S(1)}) custom-call(s32[4,6]{1,0:T(4,128)S(1)} %bitcast.42, bf16[48,1024,128]{2,1,0:T(8,128)(2,1)} %project_heads.1.heads_in, bf16[2048,768]{1,0:T(8,128)(2,1)} %bitcast.9.context_in), custom_call_target="tpu_custom_call" | custom-call | flops 1 | bytes 1 | tf_op jit(solution)/shard_map/attend_first/pallas_call | solution.py:235
  93.6 4.5 %attend_second.1 = (bf16[512,384]{1,0:T(8,128)(2,1)S(1)}, bf16[768,1024]{1,0:T(8,128)(2,1)S(1)}) custom-call(s32[4,6]{1,0:T(4,128)S(1)} %bitcast.43, bf16[9,1024,128]{2,1,0:T(8,128)(2,1)S(1)} %get-tuple-element.54.heads_ref, bf16[2048,768]{1,0:T(8,128)(2,1)S(1)} %get-tuple-element.55.context_ref, bf16[384,5120]{1,0:T(8,128)(2,1)S(1)} %bitcast.31, ...), custom_call_target="tpu_custom_call" | custom-call | flops 1 | bytes 1 | tf_op jit(solution)/shard_map/attend_second/pallas_call | solution.py:275
  98.1 1.0 sum_stage.10
  99.2 1.1 collective-permute-start.13
  100.3 0.5 collective-permute-start.14
  100.8 2.2 %sum_stage.11 = (bf16[128,1024]{1,0:T(8,128)(2,1)S(1)}, bf16[128,1024]{1,0:T(8,128)(2,1)S(1)}, f32[2,128,512]{2,1,0:T(8,128)S(1)}, f32[2,128,512]{2,1,0:T(8,128)S(1)}) custom-call(bf16[128,5120]{1,0:T(8,128)(2,1)S(1)} %bitcast.21, f32[2,5120]{1,0:T(2,128)S(1)} %pad_maximum_fusion.refs_3_.refs_1_, bf16[512,384]{1,0:T(8,128)(2,1)S(1)} %get-tuple-element.57.refs_2_, ...), custom_call_target="tpu_custom_call" | custom-call | flops 1 | bytes 1 | tf_op jit(solution)/shard_map/sum_stage/pallas_call | solution.py:400
  103.0 1.4 collective-permute-start.17
  104.4 1.1 collective-permute-start.18
  105.6 2.8 %collective-permute-done.13.refs_6_ = bf16[128,1024]{1,0:T(8,128)(2,1)S(1)} collective-permute-done((bf16[128,1024]{1,0:T(8,128)(2,1)S(1)}, bf16[128,1024]{1,0:T(8,128)(2,1)S(1)}, u32[]{:S(2)}, u32[]{:S(2)}) %collective-permute-start.13) | collective-permute-done | bytes 262176 | tf_op jit(solution)/shard_map/ppermute | solution.py:27
  108.3 1.1 collective-permute-done.14.refs_7_
  109.4 2.4 %sum_stage.12 = (bf16[128,1536]{1,0:T(8,128)(2,1)S(1)}, bf16[128,1536]{1,0:T(8,128)(2,1)S(1)}, f32[2,128,512]{2,1,0:T(8,128)S(1)}, f32[2,128,512]{2,1,0:T(8,128)...) custom-call(bf16[128,5120]{1,0:T(8,128)(2,1)S(1)} %bitcast.22, f32[2,5120]{1,0:T(2,128)S(1)} %pad_maximum_fusion.refs_3_.refs_1_, ...), custom_call_target="tpu_custom_call" | custom-call | flops 1 | bytes 1 | tf_op jit(solution)/shard_map/sum_stage/pallas_call | solution.py:400
  111.8 1.0 collective-permute-start.15
  112.9 0.9 collective-permute-start.16
  113.8 0.9 collective-permute-done.18.refs_7_
  114.7 2.4 %sum_stage.13 = (bf16[128,1536]{1,0:T(8,128)(2,1)S(1)}, bf16[128,1536]{1,0:T(8,128)(2,1)S(1)}, f32[2,128,512]{2,1,0:T(8,128)S(1)}, f32[2,128,512]{2,1,0:T(8,128)...) custom-call(bf16[128,5120]{1,0:T(8,128)(2,1)S(1)} %bitcast.23, f32[2,5120]{1,0:T(2,128)S(1)} %pad_maximum_fusion.refs_3_.refs_1_, ...), custom_call_target="tpu_custom_call" | custom-call | flops 1 | bytes 1 | tf_op jit(solution)/shard_map/sum_stage/pallas_call | solution.py:400
  117.1 0.9 collective-permute-start.20
  118.1 0.6 collective-permute-start.21
  118.6 5.3 %collective-permute-done.15.refs_6_ = bf16[128,1536]{1,0:T(8,128)(2,1)S(1)} collective-permute-done((bf16[128,1536]{1,0:T(8,128)(2,1)S(1)}, bf16[128,1536]{1,0:T(8,128)(2,1)S(1)}, u32[]{:S(2)}, u32[]{:S(2)}) %collective-permute-start.15) | collective-permute-done | bytes 393248 | tf_op jit(solution)/shard_map/ppermute | solution.py:27
  124.0 1.0 collective-permute-done.16.refs_7_
  124.9 1.9 %sum_stage.14 = (bf16[128,1024]{1,0:T(8,128)(2,1)S(1)}, bf16[128,1024]{1,0:T(8,128)(2,1)S(1)}, f32[2,128,256]{2,1,0:T(8,128)S(1)}, f32[2,128,256]{2,1,0:T(8,128)...) custom-call(bf16[128,5120]{1,0:T(8,128)(2,1)S(1)} %bitcast.24, ...), custom_call_target="tpu_custom_call" | custom-call | flops 1 | bytes 1 | tf_op jit(solution)/shard_map/sum_stage/pallas_call | solution.py:400
  126.8 1.1 collective-permute-start.23
  127.9 0.5 collective-permute-start.24
  128.4 1.9 %collective-permute-start.19 = (bf16[128,1024]{1,0:T(8,128)(2,1)S(1)}, bf16[128,1024]{1,0:T(8,128)(2,1)S(1)}, u32[]{:S(2)}, u32[]{:S(2)}) collective-permute-start(bf16[128,1024]{1,0:T(8,128)(2,1)S(1)} %get-tuple-element.74.refs_12_), channel_id=1, source_target_pairs={{0,8},{8,16},{16,24},{24,0},{1,9},{9,17},{17,25},{25,1},{2,10},{10... | collective-permute-start | bytes 786440 | tf_op jit(solution)/shard_map/ppermute | solution.py:22
  130.4 2.0 %collective-permute-done.20.refs_6_ = bf16[128,1536]{1,0:T(8,128)(2,1)S(1)} collective-permute-done((bf16[128,1536]{1,0:T(8,128)(2,1)S(1)}, bf16[128,1536]{1,0:T(8,128)(2,1)S(1)}, u32[]{:S(2)}, u32[]{:S(2)}) %collective-permute-start.20) | collective-permute-done | bytes 393248 | tf_op jit(solution)/shard_map/ppermute | solution.py:27
  132.4 1.0 collective-permute-done.21.refs_7_
  133.3 1.9 %sum_stage.15 = (bf16[128,1024]{1,0:T(8,128)(2,1)S(1)}, bf16[128,1024]{1,0:T(8,128)(2,1)S(1)}, f32[2,128,256]{2,1,0:T(8,128)S(1)}, f32[2,128,256]{2,1,0:T(8,128)...) custom-call(bf16[128,5120]{1,0:T(8,128)(2,1)S(1)} %bitcast.25, ...), custom_call_target="tpu_custom_call" | custom-call | flops 1 | bytes 1 | tf_op jit(solution)/shard_map/sum_stage/pallas_call | solution.py:400
  135.2 1.1 collective-permute-start.26
  136.3 0.5 collective-permute-start.27
  136.9 1.1 collective-permute-done.23.refs_2_
  138.0 1.9 %collective-permute-start.22 = (bf16[128,1024]{1,0:T(8,128)(2,1)S(1)}, bf16[128,1024]{1,0:T(8,128)(2,1)S(1)}, u32[]{:S(2)}, u32[]{:S(2)}) collective-permute-start(bf16[128,1024]{1,0:T(8,128)(2,1)S(1)} %get-tuple-element.80.refs_8_), channel_id=1, source_target_pairs={{0,8},{8,16},{16,24},{24,0},{1,9},{9,17},{17,25},{25,1},{2,10},{10... | collective-permute-start | bytes 786440 | tf_op jit(solution)/shard_map/ppermute | solution.py:22
  140.1 1.6 %collective-permute-start.25 = (bf16[128,1024]{1,0:T(8,128)(2,1)S(1)}, bf16[128,1024]{1,0:T(8,128)(2,1)S(1)}, u32[]{:S(2)}, u32[]{:S(2)}) collective-permute-start(bf16[128,1024]{1,0:T(8,128)(2,1)S(1)} %get-tuple-element.87.refs_8_), channel_id=1, source_target_pairs={{0,8},{8,16},{16,24},{24,0},{1,9},{9,17},{17,25},{25,1},{2,10},{10... | collective-permute-start | bytes 786440 | tf_op jit(solution)/shard_map/ppermute | solution.py:22
  141.7 1.0 collective-permute-start.29
  142.7 0.9 collective-permute-start.30
  143.6 4.3 %collective-permute-done.22.refs_9_ = bf16[128,1024]{1,0:T(8,128)(2,1)S(1)} collective-permute-done((bf16[128,1024]{1,0:T(8,128)(2,1)S(1)}, bf16[128,1024]{1,0:T(8,128)(2,1)S(1)}, u32[]{:S(2)}, u32[]{:S(2)}) %collective-permute-start.22) | collective-permute-done | bytes 262176 | tf_op jit(solution)/shard_map/ppermute | solution.py:22
  148.1 1.0 collective-permute-start.32
  149.0 0.9 collective-permute-start.28
  150.1 3.4 %collective-permute-done.25.refs_7_ = bf16[128,1024]{1,0:T(8,128)(2,1)S(1)} collective-permute-done((bf16[128,1024]{1,0:T(8,128)(2,1)S(1)}, bf16[128,1024]{1,0:T(8,128)(2,1)S(1)}, u32[]{:S(2)}, u32[]{:S(2)}) %collective-permute-start.25) | collective-permute-done | bytes 262176 | tf_op jit(solution)/shard_map/ppermute | solution.py:22
  153.6 1.0 collective-permute-start.31
  154.6 1.9 %collective-permute-start.34 = (bf16[128,512]{1,0:T(8,128)(2,1)S(1)}, bf16[128,512]{1,0:T(8,128)(2,1)S(1)}, u32[]{:S(2)}, u32[]{:S(2)}) collective-permute-start(bf16[128,512]{1,0:T(8,128)(2,1)S(1)} %sum_stage.19), channel_id=1, source_target_pairs={{0,8},{8,16},{16,24},{24,0},{1,9},{9,17},{17,25},{25,1},{2,10},{10... | collective-permute-start | bytes 393224 | tf_op jit(solution)/shard_map/ppermute | solution.py:22
  156.5 2.2 %collective-permute-done.28 = bf16[128,1024]{1,0:T(8,128)(2,1)S(1)} collective-permute-done((bf16[128,1024]{1,0:T(8,128)(2,1)S(1)}, bf16[128,1024]{1,0:T(8,128)(2,1)S(1)}, u32[]{:S(2)}, u32[]{:S(2)}) %collective-permute-start.28) | collective-permute-done | bytes 262176 | tf_op jit(solution)/shard_map/ppermute | solution.py:22
  158.7 1.7 %collective-permute-done.31 = bf16[128,512]{1,0:T(8,128)(2,1)S(1)} collective-permute-done((bf16[128,512]{1,0:T(8,128)(2,1)S(1)}, bf16[128,512]{1,0:T(8,128)(2,1)S(1)}, u32[]{:S(2)}, u32[]{:S(2)}) %collective-permute-start.31) | collective-permute-done | bytes 131104 | tf_op jit(solution)/shard_map/ppermute | solution.py:22
  160.4 1.4 collective-permute-done.34
  161.8 1.0 copy-done.10
  (64 shorter events, 3.1 us)
Async XLA Ops:
  2.5 18.7 %collective-permute-start.1 = (bf16[64,5120]{1,0:T(8,128)(2,1)}, bf16[64,5120]{1,0:T(8,128)(2,1)S(1)}, u32[]{:S(2)}, u32[]{:S(2)}) collective-permute-start(bf16[64,5120]{1,0:T(8,128)(2,1)} %get-tuple-element.104), channel_id=1, source_target_pairs={{0,1},{1,0},{2,3},{3,2},{4,5},{5,4},{6,7},{7,6},{8,9},{9,8},{10,11... | collective-permute-start | bytes 1966088 | tf_op jit(solution)/shard_map/ppermute | solution.py:27
  5.4 19.8 %collective-permute-start.4 = (bf16[64,5120]{1,0:T(8,128)(2,1)}, bf16[64,5120]{1,0:T(8,128)(2,1)S(1)}, u32[]{:S(2)}, u32[]{:S(2)}) collective-permute-start(bf16[64,5120]{1,0:T(8,128)(2,1)} %get-tuple-element.103), channel_id=1, source_target_pairs={{0,4},{2,6},{4,0},{6,2},{1,5},{3,7},{5,1},{7,3},{8,12},{10,14},{12... | collective-permute-start | bytes 1966088 | tf_op jit(solution)/shard_map/ppermute | solution.py:27
  6.9 35.1 %collective-permute-start.2 = (bf16[64,5120]{1,0:T(8,128)(2,1)}, bf16[64,5120]{1,0:T(8,128)(2,1)}, u32[]{:S(2)}, u32[]{:S(2)}) collective-permute-start(bf16[64,5120]{1,0:T(8,128)(2,1)} %get-tuple-element.103), channel_id=1, source_target_pairs={{0,1},{1,0},{2,3},{3,2},{4,5},{5,4},{6,7},{7,6},{8,9},{9,8},{10,11... | collective-permute-start | bytes 1966088 | tf_op jit(solution)/shard_map/ppermute | solution.py:27
  7.5 34.6 %collective-permute-start.3 = (bf16[64,5120]{1,0:T(8,128)(2,1)}, bf16[64,5120]{1,0:T(8,128)(2,1)S(1)}, u32[]{:S(2)}, u32[]{:S(2)}) collective-permute-start(bf16[64,5120]{1,0:T(8,128)(2,1)} %get-tuple-element.104), channel_id=1, source_target_pairs={{0,4},{2,6},{4,0},{6,2},{1,5},{3,7},{5,1},{7,3},{8,12},{10,14},{12... | collective-permute-start | bytes 1966088 | tf_op jit(solution)/shard_map/ppermute | solution.py:27
  21.2 1.9 %copy-start.2 = (bf16[256,2,8,384]{3,2,1,0:T(8,128)(2,1)S(1)}, bf16[256,2,8,384]{3,2,1,0:T(8,128)(2,1)}, u32[]{:S(2)}) copy-start(bf16[256,2,8,384]{3,2,1,0:T(8,128)(2,1)} %reshape_squeeze.3.refs_0_) | copy-start | bytes 9437188
  23.1 2.1 %copy-start.3 = (bf16[256,2,8,384]{3,2,1,0:T(8,128)(2,1)S(1)}, bf16[256,2,8,384]{3,2,1,0:T(8,128)(2,1)}, u32[]{:S(2)}) copy-start(bf16[256,2,8,384]{3,2,1,0:T(8,128)(2,1)} %reshape_squeeze.3.refs_0_) | copy-start | bytes 9437188
  23.1 4.0 %copy-start.9 = (f32[1,1,3,5120]{3,1,2,0:T(1,128)S(1)}, f32[1,1,3,5120]{3,1,2,0:T(1,128)}, u32[]{:S(2)}) copy-start(f32[1,1,3,5120]{3,1,2,0:T(1,128)} %param.7) | copy-start | bytes 184324
  23.1 4.2 %copy-start = (bf16[1,1,128,5120]{3,2,1,0:T(8,128)(2,1)S(1)}, bf16[1,1,128,5120]{3,2,1,0:T(8,128)(2,1)}, u32[]{:S(2)}) copy-start(bf16[1,1,128,5120]{3,2,1,0:T(8,128)(2,1)} %param.6) | copy-start | bytes 3932164
  23.1 32.1 %collective-permute-start.5 = (bf16[64,5120]{1,0:T(8,128)(2,1)S(1)}, bf16[64,5120]{1,0:T(8,128)(2,1)}, u32[]{:S(2)}, u32[]{:S(2)}) collective-permute-start(bf16[64,5120]{1,0:T(8,128)(2,1)S(1)} %after.3.refs_0_), channel_id=1, source_target_pairs={{0,4},{2,6},{4,0},{6,2},{1,5},{3,7},{5,1},{7,3},{8,12},{10,14},{12... | collective-permute-start | bytes 1966088 | tf_op jit(solution)/shard_map/ppermute | solution.py:27
  25.2 30.4 %collective-permute-start.6 = (bf16[64,5120]{1,0:T(8,128)(2,1)S(1)}, bf16[64,5120]{1,0:T(8,128)(2,1)}, u32[]{:S(2)}, u32[]{:S(2)}) collective-permute-start(bf16[64,5120]{1,0:T(8,128)(2,1)S(1)} %after.4.refs_1_), channel_id=1, source_target_pairs={{0,1},{1,0},{2,3},{3,2},{4,5},{5,4},{6,7},{7,6},{8,9},{9,8},{10,11... | collective-permute-start | bytes 1966088 | tf_op jit(solution)/shard_map/ppermute | solution.py:27
  27.0 23.7 %collective-permute-start = (f32[1,1,3,5120]{3,2,1,0:T(4,128)S(1)}, f32[1,1,3,5120]{3,2,1,0:T(4,128)S(1)}, u32[]{:S(2)}, u32[]{:S(2)}) collective-permute-start(f32[1,1,3,5120]{3,2,1,0:T(4,128)S(1)} %copy.15), channel_id=1, source_target_pairs={{0,1},{1,0},{2,3},{3,2},{4,5},{5,4},{6,7},{7,6},{8,9},{9,8},{10,11... | collective-permute-start | bytes 184328 | tf_op jit(solution)/shard_map/ppermute | solution.py:27
  28.8 1.1 copy-start.6
  42.0 16.7 %collective-permute-start.7 = (bf16[128,5120]{1,0:T(8,128)(2,1)}, bf16[128,5120]{1,0:T(8,128)(2,1)}, u32[]{:S(2)}, u32[]{:S(2)}) collective-permute-start(bf16[128,5120]{1,0:T(8,128)(2,1)} %copy-done.6), channel_id=1, source_target_pairs={{0,2},{2,0},{4,6},{6,4},{1,3},{3,1},{5,7},{7,5},{8,10},{10,8},{12,... | collective-permute-start | bytes 3932168 | tf_op jit(solution)/shard_map/ppermute | solution.py:27
  42.0 51.6 %collective-permute-start.11 = (bf16[384,5120]{1,0:T(8,128)(2,1)}, bf16[384,5120]{1,0:T(8,128)(2,1)}, u32[]{:S(2)}, u32[]{:S(2)}) collective-permute-start(bf16[384,5120]{1,0:T(8,128)(2,1)} %bitcast.30), channel_id=1, source_target_pairs={{0,2},{2,0},{4,6},{6,4},{1,3},{3,1},{5,7},{7,5},{8,10},{10,8},{12,... | collective-permute-start | bytes 11796488 | tf_op jit(solution)/shard_map/ppermute | solution.py:27
  42.5 1.9 %copy-start.4 = (bf16[8,256,768]{2,1,0:T(8,128)(2,1)S(1)}, bf16[8,256,768]{2,1,0:T(8,128)(2,1)}, u32[]{:S(2)}) copy-start(bf16[8,256,768]{2,1,0:T(8,128)(2,1)} %reshape.10.value_ref) | copy-start | bytes 9437188
  44.4 1.7 %copy-start.5 = (bf16[8,256,768]{2,1,0:T(8,128)(2,1)}, bf16[8,256,768]{2,1,0:T(8,128)(2,1)S(1)}, u32[]{:S(2)}) copy-start(bf16[8,256,768]{2,1,0:T(8,128)(2,1)S(1)} %after.5) | copy-start | bytes 9437188
  46.1 41.8 %all-to-all-start = ((bf16[8,256,768]{2,1,0:T(8,128)(2,1)}), bf16[8,256,768]{2,1,0:T(8,128)(2,1)}, u32[]{:S(2)}, u32[]{:S(2)}) async-start(bf16[8,256,768]{2,1,0:T(8,128)(2,1)} %copy-done.5), calls=%async_computation | async-start | bytes 6291456 | tf_op jit(solution)/shard_map/all_to_all | solution.py:454
  53.3 5.4 %collective-permute-start.8 = (bf16[128,5120]{1,0:T(8,128)(2,1)S(1)}, bf16[128,5120]{1,0:T(8,128)(2,1)S(1)}, u32[]{:S(2)}, u32[]{:S(2)}) collective-permute-start(bf16[128,5120]{1,0:T(8,128)(2,1)S(1)} %modulated_norm.5.refs_1_), channel_id=1, source_target_pairs={{0,2},{2,0},{4,6},{6,4},{1,3},{3,1},{5,7},{7,5},{8,10},{10,8},{12,... | collective-permute-start | bytes 3932168 | tf_op jit(solution)/shard_map/ppermute | solution.py:27
  55.1 6.3 %copy-start.7 = (bf16[128,5120]{1,0:T(8,128)(2,1)S(1)}, bf16[128,5120]{1,0:T(8,128)(2,1)}, u32[]{:S(2)}) copy-start(bf16[128,5120]{1,0:T(8,128)(2,1)} %copy-done.6) | copy-start | bytes 3932164
  55.1 3.6 %collective-permute-start.9 = (bf16[128,5120]{1,0:T(8,128)(2,1)S(1)}, bf16[128,5120]{1,0:T(8,128)(2,1)S(1)}, u32[]{:S(2)}, u32[]{:S(2)}) collective-permute-start(bf16[128,5120]{1,0:T(8,128)(2,1)S(1)} %modulated_norm.6.refs_2_), channel_id=1, source_target_pairs={{0,2},{2,0},{4,6},{6,4},{1,3},{3,1},{5,7},{7,5},{8,10},{10,8},{12,... | collective-permute-start | bytes 3932168 | tf_op jit(solution)/shard_map/ppermute | solution.py:27
  58.3 3.1 %collective-permute-start.10 = (bf16[128,5120]{1,0:T(8,128)(2,1)S(1)}, bf16[128,5120]{1,0:T(8,128)(2,1)S(1)}, u32[]{:S(2)}, u32[]{:S(2)}) collective-permute-start(bf16[128,5120]{1,0:T(8,128)(2,1)S(1)} %modulated_norm.7.refs_3_), channel_id=1, source_target_pairs={{0,2},{2,0},{4,6},{6,4},{1,3},{3,1},{5,7},{7,5},{8,10},{10,8},{12,... | collective-permute-start | bytes 3932168 | tf_op jit(solution)/shard_map/ppermute | solution.py:27
  61.4 26.5 %copy-start.8 = (s32[1,4,6]{2,1,0:T(4,128)S(1)}, s32[1,4,6]{2,1,0:T(4,128)}, u32[]{:S(2)}) copy-start(s32[1,4,6]{2,1,0:T(4,128)} %param.11) | copy-start | bytes 292
  87.9 5.7 %copy-start.1 = (bf16[1,384,5120]{2,1,0:T(8,128)(2,1)S(1)}, bf16[1,384,5120]{2,1,0:T(8,128)(2,1)}, u32[]{:S(2)}) copy-start(bf16[1,384,5120]{2,1,0:T(8,128)(2,1)} %param.9) | copy-start | bytes 11796484
  93.4 4.7 %collective-permute-start.12 = (bf16[512,384]{1,0:T(8,128)(2,1)S(1)}, bf16[512,384]{1,0:T(8,128)(2,1)S(1)}, u32[]{:S(2)}, u32[]{:S(2)}) collective-permute-start(bf16[512,384]{1,0:T(8,128)(2,1)S(1)} %get-tuple-element.56.refs_2_), channel_id=1, source_target_pairs={{0,2},{2,0},{4,6},{6,4},{1,3},{3,1},{5,7},{7,5},{8,10},{10,8},{12,... | collective-permute-start | bytes 1179656 | tf_op jit(solution)/shard_map/ppermute | solution.py:27
  99.2 9.2 %collective-permute-start.13 = (bf16[128,1024]{1,0:T(8,128)(2,1)S(1)}, bf16[128,1024]{1,0:T(8,128)(2,1)S(1)}, u32[]{:S(2)}, u32[]{:S(2)}) collective-permute-start(bf16[128,1024]{1,0:T(8,128)(2,1)S(1)} %get-tuple-element.59), channel_id=1, source_target_pairs={{0,1},{1,0},{2,3},{3,2},{4,5},{5,4},{6,7},{7,6},{8,9},{9,8},{10,11... | collective-permute-start | bytes 786440 | tf_op jit(solution)/shard_map/ppermute | solution.py:27
  100.3 9.1 %collective-permute-start.14 = (bf16[128,1024]{1,0:T(8,128)(2,1)S(1)}, bf16[128,1024]{1,0:T(8,128)(2,1)S(1)}, u32[]{:S(2)}, u32[]{:S(2)}) collective-permute-start(bf16[128,1024]{1,0:T(8,128)(2,1)S(1)} %get-tuple-element.60), channel_id=1, source_target_pairs={{0,4},{2,6},{4,0},{6,2},{1,5},{3,7},{5,1},{7,3},{8,12},{10,14},{12... | collective-permute-start | bytes 786440 | tf_op jit(solution)/shard_map/ppermute | solution.py:27
  103.0 10.8 %collective-permute-start.17 = (bf16[128,1024]{1,0:T(8,128)(2,1)S(1)}, bf16[128,1024]{1,0:T(8,128)(2,1)S(1)}, u32[]{:S(2)}, u32[]{:S(2)}) collective-permute-start(bf16[128,1024]{1,0:T(8,128)(2,1)S(1)} %get-tuple-element.70), channel_id=1, source_target_pairs={{0,1},{1,0},{2,3},{3,2},{4,5},{5,4},{6,7},{7,6},{8,9},{9,8},{10,11... | collective-permute-start | bytes 786440 | tf_op jit(solution)/shard_map/ppermute | solution.py:27
  104.4 10.3 %collective-permute-start.18 = (bf16[128,1024]{1,0:T(8,128)(2,1)S(1)}, bf16[128,1024]{1,0:T(8,128)(2,1)S(1)}, u32[]{:S(2)}, u32[]{:S(2)}) collective-permute-start(bf16[128,1024]{1,0:T(8,128)(2,1)S(1)} %get-tuple-element.71), channel_id=1, source_target_pairs={{0,4},{2,6},{4,0},{6,2},{1,5},{3,7},{5,1},{7,3},{8,12},{10,14},{12... | collective-permute-start | bytes 786440 | tf_op jit(solution)/shard_map/ppermute | solution.py:27
  111.8 12.1 %collective-permute-start.15 = (bf16[128,1536]{1,0:T(8,128)(2,1)S(1)}, bf16[128,1536]{1,0:T(8,128)(2,1)S(1)}, u32[]{:S(2)}, u32[]{:S(2)}) collective-permute-start(bf16[128,1536]{1,0:T(8,128)(2,1)S(1)} %get-tuple-element.64), channel_id=1, source_target_pairs={{0,1},{1,0},{2,3},{3,2},{4,5},{5,4},{6,7},{7,6},{8,9},{9,8},{10,11... | collective-permute-start | bytes 1179656 | tf_op jit(solution)/shard_map/ppermute | solution.py:27
  112.9 12.1 %collective-permute-start.16 = (bf16[128,1536]{1,0:T(8,128)(2,1)S(1)}, bf16[128,1536]{1,0:T(8,128)(2,1)S(1)}, u32[]{:S(2)}, u32[]{:S(2)}) collective-permute-start(bf16[128,1536]{1,0:T(8,128)(2,1)S(1)} %get-tuple-element.65), channel_id=1, source_target_pairs={{0,4},{2,6},{4,0},{6,2},{1,5},{3,7},{5,1},{7,3},{8,12},{10,14},{12... | collective-permute-start | bytes 1179656 | tf_op jit(solution)/shard_map/ppermute | solution.py:27
  117.1 15.2 %collective-permute-start.20 = (bf16[128,1536]{1,0:T(8,128)(2,1)S(1)}, bf16[128,1536]{1,0:T(8,128)(2,1)S(1)}, u32[]{:S(2)}, u32[]{:S(2)}) collective-permute-start(bf16[128,1536]{1,0:T(8,128)(2,1)S(1)} %get-tuple-element.75), channel_id=1, source_target_pairs={{0,1},{1,0},{2,3},{3,2},{4,5},{5,4},{6,7},{7,6},{8,9},{9,8},{10,11... | collective-permute-start | bytes 1179656 | tf_op jit(solution)/shard_map/ppermute | solution.py:27
  118.1 15.3 %collective-permute-start.21 = (bf16[128,1536]{1,0:T(8,128)(2,1)S(1)}, bf16[128,1536]{1,0:T(8,128)(2,1)S(1)}, u32[]{:S(2)}, u32[]{:S(2)}) collective-permute-start(bf16[128,1536]{1,0:T(8,128)(2,1)S(1)} %get-tuple-element.76), channel_id=1, source_target_pairs={{0,4},{2,6},{4,0},{6,2},{1,5},{3,7},{5,1},{7,3},{8,12},{10,14},{12... | collective-permute-start | bytes 1179656 | tf_op jit(solution)/shard_map/ppermute | solution.py:27
  126.8 11.2 %collective-permute-start.23 = (bf16[128,1024]{1,0:T(8,128)(2,1)S(1)}, bf16[128,1024]{1,0:T(8,128)(2,1)S(1)}, u32[]{:S(2)}, u32[]{:S(2)}) collective-permute-start(bf16[128,1024]{1,0:T(8,128)(2,1)S(1)} %get-tuple-element.81), channel_id=1, source_target_pairs={{0,1},{1,0},{2,3},{3,2},{4,5},{5,4},{6,7},{7,6},{8,9},{9,8},{10,11... | collective-permute-start | bytes 786440 | tf_op jit(solution)/shard_map/ppermute | solution.py:27
  127.9 12.0 %collective-permute-start.24 = (bf16[128,1024]{1,0:T(8,128)(2,1)S(1)}, bf16[128,1024]{1,0:T(8,128)(2,1)S(1)}, u32[]{:S(2)}, u32[]{:S(2)}) collective-permute-start(bf16[128,1024]{1,0:T(8,128)(2,1)S(1)} %get-tuple-element.82), channel_id=1, source_target_pairs={{0,4},{2,6},{4,0},{6,2},{1,5},{3,7},{5,1},{7,3},{8,12},{10,14},{12... | collective-permute-start | bytes 786440 | tf_op jit(solution)/shard_map/ppermute | solution.py:27
  128.4 11.5 %collective-permute-start.19 = (bf16[128,1024]{1,0:T(8,128)(2,1)S(1)}, bf16[128,1024]{1,0:T(8,128)(2,1)S(1)}, u32[]{:S(2)}, u32[]{:S(2)}) collective-permute-start(bf16[128,1024]{1,0:T(8,128)(2,1)S(1)} %get-tuple-element.74.refs_12_), channel_id=1, source_target_pairs={{0,8},{8,16},{16,24},{24,0},{1,9},{9,17},{17,25},{25,1},{2,10},{10... | collective-permute-start | bytes 786440 | tf_op jit(solution)/shard_map/ppermute | solution.py:22
  135.2 7.5 %collective-permute-start.26 = (bf16[128,1024]{1,0:T(8,128)(2,1)S(1)}, bf16[128,1024]{1,0:T(8,128)(2,1)S(1)}, u32[]{:S(2)}, u32[]{:S(2)}) collective-permute-start(bf16[128,1024]{1,0:T(8,128)(2,1)S(1)} %get-tuple-element.88), channel_id=1, source_target_pairs={{0,1},{1,0},{2,3},{3,2},{4,5},{5,4},{6,7},{7,6},{8,9},{9,8},{10,11... | collective-permute-start | bytes 786440 | tf_op jit(solution)/shard_map/ppermute | solution.py:27
  136.3 7.3 %collective-permute-start.27 = (bf16[128,1024]{1,0:T(8,128)(2,1)S(1)}, bf16[128,1024]{1,0:T(8,128)(2,1)S(1)}, u32[]{:S(2)}, u32[]{:S(2)}) collective-permute-start(bf16[128,1024]{1,0:T(8,128)(2,1)S(1)} %get-tuple-element.89), channel_id=1, source_target_pairs={{0,4},{2,6},{4,0},{6,2},{1,5},{3,7},{5,1},{7,3},{8,12},{10,14},{12... | collective-permute-start | bytes 786440 | tf_op jit(solution)/shard_map/ppermute | solution.py:27
  138.0 9.9 %collective-permute-start.22 = (bf16[128,1024]{1,0:T(8,128)(2,1)S(1)}, bf16[128,1024]{1,0:T(8,128)(2,1)S(1)}, u32[]{:S(2)}, u32[]{:S(2)}) collective-permute-start(bf16[128,1024]{1,0:T(8,128)(2,1)S(1)} %get-tuple-element.80.refs_8_), channel_id=1, source_target_pairs={{0,8},{8,16},{16,24},{24,0},{1,9},{9,17},{17,25},{25,1},{2,10},{10... | collective-permute-start | bytes 786440 | tf_op jit(solution)/shard_map/ppermute | solution.py:22
  140.1 13.5 %collective-permute-start.25 = (bf16[128,1024]{1,0:T(8,128)(2,1)S(1)}, bf16[128,1024]{1,0:T(8,128)(2,1)S(1)}, u32[]{:S(2)}, u32[]{:S(2)}) collective-permute-start(bf16[128,1024]{1,0:T(8,128)(2,1)S(1)} %get-tuple-element.87.refs_8_), channel_id=1, source_target_pairs={{0,8},{8,16},{16,24},{24,0},{1,9},{9,17},{17,25},{25,1},{2,10},{10... | collective-permute-start | bytes 786440 | tf_op jit(solution)/shard_map/ppermute | solution.py:22
  141.7 8.3 %collective-permute-start.29 = (bf16[128,256]{1,0:T(8,128)(2,1)S(1)}, bf16[128,256]{1,0:T(8,128)(2,1)S(1)}, u32[]{:S(2)}, u32[]{:S(2)}) collective-permute-start(bf16[128,256]{1,0:T(8,128)(2,1)S(1)} %get-tuple-element.95), channel_id=1, source_target_pairs={{0,1},{1,0},{2,3},{3,2},{4,5},{5,4},{6,7},{7,6},{8,9},{9,8},{10,11... | collective-permute-start | bytes 196616 | tf_op jit(solution)/shard_map/ppermute | solution.py:27
  142.7 7.4 %collective-permute-start.30 = (bf16[128,256]{1,0:T(8,128)(2,1)S(1)}, bf16[128,256]{1,0:T(8,128)(2,1)S(1)}, u32[]{:S(2)}, u32[]{:S(2)}) collective-permute-start(bf16[128,256]{1,0:T(8,128)(2,1)S(1)} %get-tuple-element.96), channel_id=1, source_target_pairs={{0,4},{2,6},{4,0},{6,2},{1,5},{3,7},{5,1},{7,3},{8,12},{10,14},{12... | collective-permute-start | bytes 196616 | tf_op jit(solution)/shard_map/ppermute | solution.py:27
  148.1 6.5 %collective-permute-start.32 = (bf16[128,256]{1,0:T(8,128)(2,1)S(1)}, bf16[128,256]{1,0:T(8,128)(2,1)S(1)}, u32[]{:S(2)}, u32[]{:S(2)}) collective-permute-start(bf16[128,256]{1,0:T(8,128)(2,1)S(1)} %get-tuple-element.99), channel_id=1, source_target_pairs={{0,1},{1,0},{2,3},{3,2},{4,5},{5,4},{6,7},{7,6},{8,9},{9,8},{10,11... | collective-permute-start | bytes 196616 | tf_op jit(solution)/shard_map/ppermute | solution.py:27
  149.0 9.7 %collective-permute-start.28 = (bf16[128,1024]{1,0:T(8,128)(2,1)S(1)}, bf16[128,1024]{1,0:T(8,128)(2,1)S(1)}, u32[]{:S(2)}, u32[]{:S(2)}) collective-permute-start(bf16[128,1024]{1,0:T(8,128)(2,1)S(1)} %get-tuple-element.94.refs_6_), channel_id=1, source_target_pairs={{0,8},{8,16},{16,24},{24,0},{1,9},{9,17},{17,25},{25,1},{2,10},{10... | collective-permute-start | bytes 786440 | tf_op jit(solution)/shard_map/ppermute | solution.py:22
  150.0 4.6 %collective-permute-start.33 = (bf16[128,256]{1,0:T(8,128)(2,1)S(1)}, bf16[128,256]{1,0:T(8,128)(2,1)S(1)}, u32[]{:S(2)}, u32[]{:S(2)}) collective-permute-start(bf16[128,256]{1,0:T(8,128)(2,1)S(1)} %get-tuple-element.100), channel_id=1, source_target_pairs={{0,4},{2,6},{4,0},{6,2},{1,5},{3,7},{5,1},{7,3},{8,12},{10,14},{12... | collective-permute-start | bytes 196616 | tf_op jit(solution)/shard_map/ppermute | solution.py:27
  153.6 6.8 %collective-permute-start.31 = (bf16[128,512]{1,0:T(8,128)(2,1)S(1)}, bf16[128,512]{1,0:T(8,128)(2,1)S(1)}, u32[]{:S(2)}, u32[]{:S(2)}) collective-permute-start(bf16[128,512]{1,0:T(8,128)(2,1)S(1)} %sum_stage.18.refs_6_), channel_id=1, source_target_pairs={{0,8},{8,16},{16,24},{24,0},{1,9},{9,17},{17,25},{25,1},{2,10},{10... | collective-permute-start | bytes 393224 | tf_op jit(solution)/shard_map/ppermute | solution.py:22
  154.6 7.2 %collective-permute-start.34 = (bf16[128,512]{1,0:T(8,128)(2,1)S(1)}, bf16[128,512]{1,0:T(8,128)(2,1)S(1)}, u32[]{:S(2)}, u32[]{:S(2)}) collective-permute-start(bf16[128,512]{1,0:T(8,128)(2,1)S(1)} %sum_stage.19), channel_id=1, source_target_pairs={{0,8},{8,16},{16,24},{24,0},{1,9},{9,17},{17,25},{25,1},{2,10},{10... | collective-permute-start | bytes 393224 | tf_op jit(solution)/shard_map/ppermute | solution.py:22
  161.8 1.1 copy-start.10

commit v13 on v12

--- a/solution.py
+++ b/solution.py
@@ -11,6 +11,7 @@
 TILE = 128
 MIB = 2**20
 SPARE = 39
+LOG2E = 1.4426950408889634
 CHUNK_SHARES = (4, 4, 4, 4, 2, 2)
 
 guidance_scale = 5.0
@@ -142,12 +143,13 @@
     )(*blocks, weights)
 
 
-def attend_head(visible_ref, heads_ref, context_ref, out_ref, first_block, head):
-    heads = heads_ref.shape[0] // 3
+def attend_head(visible_ref, queries_ref, pool_ref, out_ref, first_block, head):
+    heads, fresh_rows, _ = queries_ref.shape
     tiles_seen = visible_ref.shape[1]
     tiles_fresh = visible_ref.shape[0]
     mine_high, mine_low = lax.axis_index("sp") // 2, lax.axis_index("sp") % 2
     mine_branch = lax.axis_index("cfg")
+    ones = jnp.ones((tiles_seen * TILE, HD), jnp.bfloat16)
 
     def body(step, carry):
         index = first_block + step
@@ -158,68 +160,50 @@
         places = []
         for seen in range(tiles_seen):
             number = visible_ref[tile, seen]
-            older = jnp.maximum(number - tiles_fresh, 0)
+            older = number - tiles_fresh
             fresh = (mine_low ^ (number % 2)) * 4 + (mine_high ^ ((number // 2) % 2)) * 2
             fresh = (fresh + index % 2) * TILE
-            stale = ((older // 2) * 2 + branch) * 2 * TILE + (older % 2) * TILE
-            places.append(
-                (
-                    number < tiles_fresh,
-                    pl.ds(pl.multiple_of(fresh, TILE), TILE),
-                    pl.ds(pl.multiple_of(stale, TILE), TILE),
-                )
-            )
-
-        def tiles(kind):
-            start = ((kind - 1) * heads + head) * HD
-            return jnp.concatenate(
-                [
-                    jnp.where(
-                        is_fresh,
-                        heads_ref[kind * heads + head, fresh, :],
-                        context_ref[stale, start : start + HD],
-                    )
-                    for is_fresh, fresh, stale in places
-                ],
-                axis=0,
-            )
-
+            stale = fresh_rows + ((older // 2) * 2 + branch) * 2 * TILE + (older % 2) * TILE
+            start = jnp.where(number < tiles_fresh, fresh, stale)
+            places.append(pl.ds(pl.multiple_of(start, TILE), TILE))
+
+        keys = jnp.concatenate([pool_ref[head, place, :] for place in places], axis=0)
+        values = jnp.concatenate([pool_ref[heads + head, place, :] for place in places], axis=0)
         scores = lax.dot_general(
-            heads_ref[head, rows, :],
-            tiles(1),
+            queries_ref[head, rows, :],
+            keys,
             (((1,), (1,)), ((), ())),
             preferred_element_type=jnp.float32,
         )
-        exponent = jnp.exp(scores * HD ** (-0.5))
-        total = jnp.sum(exponent, axis=-1, keepdims=True)
+        exponent = jnp.exp2(scores * (HD ** (-0.5) * LOG2E)).astype(jnp.bfloat16)
         mixed = jnp.dot(
-            exponent.astype(jnp.bfloat16), tiles(2), preferred_element_type=jnp.float32
-        )
-        out_ref[out_rows, head * HD : (head + 1) * HD] = (mixed / total).astype(jnp.bfloat16)
+            exponent, jnp.concatenate([values, ones], axis=1), preferred_element_type=jnp.float32
+        )
+        out_ref[out_rows, head * HD : (head + 1) * HD] = (mixed[:, :HD] / mixed[:, HD:]).astype(
+            jnp.bfloat16
+        )
         return carry
 
     lax.fori_loop(0, out_ref.shape[0] // TILE, body, 0, unroll=True)
 
 
 def attend_first_kernel(
-    visible_ref, heads_in, context_in, out_ref, heads_ref, context_ref, sems
+    visible_ref, heads_in, context_in, out_ref, queries_ref, pool_ref, sems
 ):
-    heads = heads_ref.shape[0] // 3
+    heads, fresh_rows, _ = queries_ref.shape
+    fresh, stale = pl.ds(0, fresh_rows), pl.ds(fresh_rows, context_in.shape[0])
     copies = []
     for head in range(heads):
-        of_head = []
-        for kind in range(3):
+        pairs = [(heads_in.at[head], queries_ref.at[head])]
+        for kind in range(2):
             place = kind * heads + head
-            of_head.append(
-                pltpu.make_async_copy(heads_in.at[place], heads_ref.at[place], sems.at[head, kind])
-            )
-        for kind in range(2):
-            columns = pl.ds((kind * heads + head) * HD, HD)
-            of_head.append(
-                pltpu.make_async_copy(
-                    context_in.at[:, columns], context_ref.at[:, columns], sems.at[head, 3 + kind]
-                )
-            )
+            columns = pl.ds(place * HD, HD)
+            pairs.append((heads_in.at[heads + place], pool_ref.at[place, fresh]))
+            pairs.append((context_in.at[:, columns], pool_ref.at[place, stale]))
+        of_head = [
+            pltpu.make_async_copy(source, target, sems.at[head, number])
+            for number, (source, target) in enumerate(pairs)
+        ]
         for copy in of_head:
             copy.start()
         copies.append(of_head)
@@ -227,11 +211,11 @@
         for copy in copies[head]:
             copy.wait()
         first_block = out_ref.shape[0] // TILE
-        attend_head(visible_ref, heads_ref, context_ref, out_ref, first_block, head)
+        attend_head(visible_ref, queries_ref, pool_ref, out_ref, first_block, head)
 
 
 def attend_first(heads, context, visible):
-    number, count = heads.shape[0] - SPARE, heads.shape[1] // 2
+    number, rows = (heads.shape[0] - SPARE) // 3, heads.shape[1]
     return pl.pallas_call(
         attend_first_kernel,
         in_specs=[
@@ -241,18 +225,18 @@
         ],
         out_specs=[pl.BlockSpec(memory_space=pltpu.VMEM)] * 3,
         out_shape=[
-            jax.ShapeDtypeStruct((count, number // 3 * HD), jnp.bfloat16),
-            jax.ShapeDtypeStruct((number,) + heads.shape[1:], heads.dtype),
-            jax.ShapeDtypeStruct(context.shape, context.dtype),
+            jax.ShapeDtypeStruct((rows // 2, number * HD), jnp.bfloat16),
+            jax.ShapeDtypeStruct((number, rows, HD), heads.dtype),
+            jax.ShapeDtypeStruct((2 * number, rows + context.shape[0], HD), heads.dtype),
         ],
-        scratch_shapes=[pltpu.SemaphoreType.DMA((number // 3, 5))],
+        scratch_shapes=[pltpu.SemaphoreType.DMA((number, 5))],
         name="attend_first",
         cost_estimate=SHORT,
         compiler_params=pltpu.CompilerParams(vmem_limit_bytes=44 * MIB),
     )(visible, heads, context)
 
 
-def attend_second_kernel(visible_ref, heads_ref, context_ref, *refs):
+def attend_second_kernel(visible_ref, queries_ref, pool_ref, *refs):
     weights_ref, core_weights_ref = refs[:2]
     out_ref, both_ref, sems = refs[-3:]
     depth, columns = weights_ref.shape[0], pl.ds(0, both_ref.shape[1])
@@ -264,14 +248,14 @@
     ]
     for copy in copies:
         copy.start()
-    for head in range(heads_ref.shape[0] // 3):
-        attend_head(visible_ref, heads_ref, context_ref, out_ref, 0, head)
+    for head in range(queries_ref.shape[0]):
+        attend_head(visible_ref, queries_ref, pool_ref, out_ref, 0, head)
     for copy in copies:
         copy.wait()
 
 
-def attend_second(heads, context, visible, weights, core_weights, columns, earlier):
-    count = heads.shape[1] // 2
+def attend_second(queries, pool, visible, weights, core_weights, columns, earlier):
+    number, rows, _ = queries.shape
     return pl.pallas_call(
         attend_second_kernel,
         in_specs=[pl.BlockSpec(memory_space=pltpu.SMEM)]
@@ -279,14 +263,14 @@
         + [pl.BlockSpec(memory_space=pl.ANY)] * (2 + len(earlier)),
         out_specs=[pl.BlockSpec(memory_space=pltpu.VMEM)] * 2,
         out_shape=[
-            jax.ShapeDtypeStruct((count, heads.shape[0] // 3 * HD), jnp.bfloat16),
+            jax.ShapeDtypeStruct((rows // 2, number * HD), jnp.bfloat16),
             jax.ShapeDtypeStruct((2 * weights.shape[0], columns), weights.dtype),
         ],
         scratch_shapes=[pltpu.SemaphoreType.DMA((2,))],
         name="attend_second",
         cost_estimate=SHORT,
         compiler_params=pltpu.CompilerParams(vmem_limit_bytes=12 * MIB),
-    )(visible, heads, context, weights, core_weights, *earlier)
+    )(visible, queries, pool, weights, core_weights, *earlier)
 
 
 def combined(own, other, mine, gates_ref, columns):
@@ -461,10 +445,10 @@
     chunks = [
         (sum(CHUNK_SHARES[:index]) * unit, share * unit) for index, share in enumerate(CHUNK_SHARES)
     ]
-    for_core, heads, context = attend_first(heads, context, visible[0])
+    for_core, queries, pool = attend_first(heads, context, visible[0])
     core_attended = from_partner(for_core, "sp", 1)
     attended, first_weights = attend_second(
-        heads, context, visible[0], project_out[0], core_weights, chunks[0][1], (for_core, gates)
+        queries, pool, visible[0], project_out[0], core_weights, chunks[0][1], (for_core, gates)
     )
 
     kept, left, flights, arrivals, earlier = {}, {}, {}, [], []

time: 164 us -> 162 us (0.988)
  transfers between devices with their start and end apart: 36 -> 36, of which waited for: 16 -> 16; matrix products, arithmetic and copies ran while one was open for 12% -> 13% of each run, Pallas kernels for 30% -> 29%
where the time goes in v13:
time: 162 us; the launch traced here: 161 us
  Pallas kernels  48.2 us (30%)
  waiting for transfers between devices  43.8 us (27%)
  starting transfers between devices  38.7 us (24%)
  local copies, waits for them, and re-layouts  30.3 us (19%)
    ppermute x29, starting transfers between devices, from_partner(): return lax.ppermute(value, axis, pairs)  24.8 us
    ppermute x29, waiting for transfers between devices, from_partner(): return lax.ppermute(value, axis, pairs)  23.6 us
    pallas_call x1, Pallas kernels, project(): pl.pallas_call(functools.partial(project_kernel, blocks=len(blocks)), gri...  19.2 us
    ppermute x6, waiting for transfers between devices, from_behind(): return lax.ppermute(x, axis, [(i, (i + by) % count) for i in range(count)])  12.9 us
    pallas_call x10, Pallas kernels, stage(): pl.pallas_call(functools.partial(stage_kernel, parts=parts, start=start,...  12.1 us
    ppermute x6, starting transfers between devices, from_behind(): return lax.ppermute(x, axis, [(i, (i + by) % count) for i in range(count)])  9.3 us
    pallas_call x4, Pallas kernels, modulated_norm(): pl.pallas_call(norm_kernel, in_specs=[pl.BlockSpec(memory_space=pltpu.VME...  8.42 us
    reshape x1, local copies, waits for them, and re-layouts, per_device(): unpacked.transpose(2, 0, 1, 3).reshape(devices, context_rows, 2 * width)  8.04 us
  transfers between devices with their start and end apart: 36, of which 16 were waited for; matrix products, arithmetic and copies ran while one was open for 13% of the time, Pallas kernels for 29%

profile of v13, /device:TPU:0, one launch (start us, length us, event | category | flops | bytes accessed | tf_op | source)
XLA Modules:
  0.0 161.4 jit_solution(16036170295845497124)
XLA Ops:
  0.0 2.5 %slice_bitcast_fusion = (bf16[64,5120]{1,0:T(8,128)(2,1)}, bf16[64,5120]{1,0:T(8,128)(2,1)}) fusion(bf16[1,1,128,5120]{3,2,1,0:T(8,128)(2,1)} %param.6), kind=kLoop, calls=%fused_computation | loop fusion | bytes 2621440 | tf_op jit(solution)/shard_map/slice | solution.py:422
  2.5 2.9 %collective-permute-start.1 = (bf16[64,5120]{1,0:T(8,128)(2,1)}, bf16[64,5120]{1,0:T(8,128)(2,1)S(1)}, u32[]{:S(2)}, u32[]{:S(2)}) collective-permute-start(bf16[64,5120]{1,0:T(8,128)(2,1)} %get-tuple-element.104), channel_id=1, source_target_pairs={{0,1},{1,0},{2,3},{3,2},{4,5},{5,4},{6,7},{7,6},{8,9},{9,8},{10,11... | collective-permute-start | bytes 1966088 | tf_op jit(solution)/shard_map/ppermute | solution.py:28
  5.4 1.5 collective-permute-start.4
  7.5 8.0 %reshape_squeeze.3.refs_0_ = bf16[256,2,8,384]{3,2,1,0:T(8,128)(2,1)} reshape(bf16[1,1,256,2,3072]{4,3,2,1,0:T(2,128)(2,1)} %param.10) | data formatting | bytes 6291456 | tf_op jit(solution)/shard_map/reshape;squeeze | solution.py:419
  15.5 5.7 %collective-permute-done.1.value_ref = bf16[64,5120]{1,0:T(8,128)(2,1)S(1)} collective-permute-done((bf16[64,5120]{1,0:T(8,128)(2,1)}, bf16[64,5120]{1,0:T(8,128)(2,1)S(1)}, u32[]{:S(2)}, u32[]{:S(2)}) %collective-permute-start.1) | collective-permute-done | bytes 655392 | tf_op jit(solution)/shard_map/ppermute | solution.py:28
  21.2 1.9 %copy-done.2 = bf16[256,2,8,384]{3,2,1,0:T(8,128)(2,1)S(1)} copy-done((bf16[256,2,8,384]{3,2,1,0:T(8,128)(2,1)S(1)}, bf16[256,2,8,384]{3,2,1,0:T(8,128)(2,1)}, u32[]{:S(2)}) %copy-start.2) | copy-done | bytes 3145752
  23.1 2.1 %collective-permute-start.5 = (bf16[64,5120]{1,0:T(8,128)(2,1)S(1)}, bf16[64,5120]{1,0:T(8,128)(2,1)}, u32[]{:S(2)}, u32[]{:S(2)}) collective-permute-start(bf16[64,5120]{1,0:T(8,128)(2,1)S(1)} %after.3.refs_0_), channel_id=1, source_target_pairs={{0,4},{2,6},{4,0},{6,2},{1,5},{3,7},{5,1},{7,3},{8,12},{10,14},{12... | collective-permute-start | bytes 1966088 | tf_op jit(solution)/shard_map/ppermute | solution.py:28
  25.2 1.8 %collective-permute-start.6 = (bf16[64,5120]{1,0:T(8,128)(2,1)S(1)}, bf16[64,5120]{1,0:T(8,128)(2,1)}, u32[]{:S(2)}, u32[]{:S(2)}) collective-permute-start(bf16[64,5120]{1,0:T(8,128)(2,1)S(1)} %after.4.refs_1_), channel_id=1, source_target_pairs={{0,1},{1,0},{2,3},{3,2},{4,5},{5,4},{6,7},{7,6},{8,9},{9,8},{10,11... | collective-permute-start | bytes 1966088 | tf_op jit(solution)/shard_map/ppermute | solution.py:28
  27.3 1.5 modulated_norm.4.refs_0_
  28.8 1.0 copy-done.6
  29.9 4.1 %copy.11 = bf16[8,256,2,384]{3,2,1,0:T(2,128)(2,1)} copy(bf16[8,256,2,384]{3,0,2,1:T(8,128)(2,1)S(1)} %bitcast.37) | data formatting | bytes 6291456 | tf_op jit(solution)/shard_map/transpose | solution.py:420
  34.0 8.0 %reshape.10.value_ref = bf16[8,256,768]{2,1,0:T(8,128)(2,1)} reshape(bf16[8,256,2,384]{3,2,1,0:T(2,128)(2,1)} %copy.11) | data formatting | bytes 6291456 | tf_op jit(solution)/shard_map/reshape | solution.py:420
  42.5 1.9 %copy-done.4 = bf16[8,256,768]{2,1,0:T(8,128)(2,1)S(1)} copy-done((bf16[8,256,768]{2,1,0:T(8,128)(2,1)S(1)}, bf16[8,256,768]{2,1,0:T(8,128)(2,1)}, u32[]{:S(2)}) %copy-start.4) | copy-done | bytes 3145752
  44.4 1.7 %copy-done.5 = bf16[8,256,768]{2,1,0:T(8,128)(2,1)} copy-done((bf16[8,256,768]{2,1,0:T(8,128)(2,1)}, bf16[8,256,768]{2,1,0:T(8,128)(2,1)S(1)}, u32[]{:S(2)}) %copy-start.5) | copy-done | bytes 3145752
  46.1 4.6 %all-to-all-start = ((bf16[8,256,768]{2,1,0:T(8,128)(2,1)}), bf16[8,256,768]{2,1,0:T(8,128)(2,1)}, u32[]{:S(2)}, u32[]{:S(2)}) async-start(bf16[8,256,768]{2,1,0:T(8,128)(2,1)} %copy-done.5), calls=%async_computation | async-start | bytes 6291456 | tf_op jit(solution)/shard_map/all_to_all | solution.py:438
  50.7 2.6 %modulated_norm.5.refs_1_ = bf16[128,5120]{1,0:T(8,128)(2,1)S(1)} custom-call(bf16[64,5120]{1,0:T(8,128)(2,1)S(1)} %after.3.refs_0_, bf16[64,5120]{1,0:T(8,128)(2,1)} %collective-permute-done.2.refs_1_.refs_0_, f32[3,5120]{1,0:T(4,128)S(1)} %bitcast.40), custom_call_target="tpu_custom_call" | custom-call | flops 1 | bytes 1 | tf_op jit(solution)/shard_map/modulated_norm/pallas_call | solution.py:55
  53.6 1.5 modulated_norm.6.refs_2_
  55.5 2.8 %modulated_norm.7.refs_3_ = bf16[128,5120]{1,0:T(8,128)(2,1)S(1)} custom-call(bf16[64,5120]{1,0:T(8,128)(2,1)} %collective-permute-done.5.refs_0_, bf16[64,5120]{1,0:T(8,128)(2,1)} %collective-permute-done.6.refs_1_, f32[3,5120]{1,0:T(4,128)S(1)} %bitcast.41), custom_call_target="tpu_custom_call" | custom-call | flops 1 | bytes 1 | tf_op jit(solution)/shard_map/modulated_norm/pallas_call | solution.py:55
  58.8 2.7 %collective-permute-done.10.refs_7_ = bf16[128,5120]{1,0:T(8,128)(2,1)S(1)} collective-permute-done((bf16[128,5120]{1,0:T(8,128)(2,1)S(1)}, bf16[128,5120]{1,0:T(8,128)(2,1)S(1)}, u32[]{:S(2)}, u32[]{:S(2)}) %collective-permute-start.10) | collective-permute-done | bytes 1310752 | tf_op jit(solution)/shard_map/ppermute | solution.py:28
  61.4 19.2 %project_heads.1.heads_in = bf16[48,1024,128]{2,1,0:T(8,128)(2,1)} custom-call(bf16[128,5120]{1,0:T(8,128)(2,1)S(1)} %copy-done.7, bf16[128,5120]{1,0:T(8,128)(2,1)S(1)} %modulated_norm.5.refs_1_, bf16[128,5120]{1,0:T(8,128)(2,1)S(1)} %modulated_norm.6.refs_2_, bf16[128,5120]{1,0:T(8,128)(2,1)S(1)} %modulated_norm.7.refs_3_, ...), custom_call_target="tpu_custom_call" | custom-call | flops 12079595520 | bytes 22282240 | tf_op jit(solution)/shard_map/project_heads/pallas_call | solution.py:124
  80.6 7.3 %all-to-all-done = bf16[8,256,768]{2,1,0:T(8,128)(2,1)} async-done(((bf16[8,256,768]{2,1,0:T(8,128)(2,1)}), bf16[8,256,768]{2,1,0:T(8,128)(2,1)}, u32[]{:S(2)}, u32[]{:S(2)}) %all-to-all-start) | async-done | bytes 3145760 | tf_op jit(solution)/shard_map/all_to_all | solution.py:438
  87.9 4.8 %attend_first.1 = (bf16[512,384]{1,0:T(8,128)(2,1)S(1)}, bf16[3,1024,128]{2,1,0:T(8,128)(2,1)S(1)}, bf16[6,3072,128]{2,1,0:T(8,128)(2,1)S(1)}) custom-call(s32[4,6]{1,0:T(4,128)S(1)} %bitcast.42, bf16[48,1024,128]{2,1,0:T(8,128)(2,1)} %project_heads.1.heads_in, bf16[2048,768]{1,0:T(8,128)(2,1)} %bitcast.9.context_in), custom_call_target="tpu_custom_call" | custom-call | flops 1 | bytes 1 | tf_op jit(solution)/shard_map/attend_first/pallas_call | solution.py:219
  92.9 3.7 %attend_second.1 = (bf16[512,384]{1,0:T(8,128)(2,1)S(1)}, bf16[768,1024]{1,0:T(8,128)(2,1)S(1)}) custom-call(s32[4,6]{1,0:T(4,128)S(1)} %bitcast.43, bf16[3,1024,128]{2,1,0:T(8,128)(2,1)S(1)} %get-tuple-element.54.queries_ref, bf16[6,3072,128]{2,1,0:T(8,128)(2,1)S(1)} %get-tuple-element.55.pool_ref, bf16[384,5120]{1,0:T(8,128)(2,1)S(1)} %bitcast.31, ...), custom_call_target="tpu_custom_call" | custom-call | flops 1 | bytes 1 | tf_op jit(solution)/shard_map/attend_second/pallas_call | solution.py:259
  96.6 1.0 sum_stage.10
  97.7 1.1 collective-permute-start.13
  98.8 0.5 collective-permute-start.14
  99.4 2.2 %sum_stage.11 = (bf16[128,1024]{1,0:T(8,128)(2,1)S(1)}, bf16[128,1024]{1,0:T(8,128)(2,1)S(1)}, f32[2,128,512]{2,1,0:T(8,128)S(1)}, f32[2,128,512]{2,1,0:T(8,128)S(1)}) custom-call(bf16[128,5120]{1,0:T(8,128)(2,1)S(1)} %bitcast.21, f32[2,5120]{1,0:T(2,128)S(1)} %pad_maximum_fusion.refs_3_.refs_1_, bf16[512,384]{1,0:T(8,128)(2,1)S(1)} %get-tuple-element.57.refs_2_, ...), custom_call_target="tpu_custom_call" | custom-call | flops 1 | bytes 1 | tf_op jit(solution)/shard_map/sum_stage/pallas_call | solution.py:384
  101.6 1.4 collective-permute-start.17
  102.9 1.1 collective-permute-start.18
  104.1 2.8 %collective-permute-done.13.refs_6_ = bf16[128,1024]{1,0:T(8,128)(2,1)S(1)} collective-permute-done((bf16[128,1024]{1,0:T(8,128)(2,1)S(1)}, bf16[128,1024]{1,0:T(8,128)(2,1)S(1)}, u32[]{:S(2)}, u32[]{:S(2)}) %collective-permute-start.13) | collective-permute-done | bytes 262176 | tf_op jit(solution)/shard_map/ppermute | solution.py:28
  106.8 1.1 collective-permute-done.14.refs_7_
  108.0 2.4 %sum_stage.12 = (bf16[128,1536]{1,0:T(8,128)(2,1)S(1)}, bf16[128,1536]{1,0:T(8,128)(2,1)S(1)}, f32[2,128,512]{2,1,0:T(8,128)S(1)}, f32[2,128,512]{2,1,0:T(8,128)...) custom-call(bf16[128,5120]{1,0:T(8,128)(2,1)S(1)} %bitcast.22, f32[2,5120]{1,0:T(2,128)S(1)} %pad_maximum_fusion.refs_3_.refs_1_, ...), custom_call_target="tpu_custom_call" | custom-call | flops 1 | bytes 1 | tf_op jit(solution)/shard_map/sum_stage/pallas_call | solution.py:384
  110.4 1.0 collective-permute-start.15
  111.4 0.9 collective-permute-start.16
  112.4 0.9 collective-permute-done.18.refs_7_
  113.3 2.4 %sum_stage.13 = (bf16[128,1536]{1,0:T(8,128)(2,1)S(1)}, bf16[128,1536]{1,0:T(8,128)(2,1)S(1)}, f32[2,128,512]{2,1,0:T(8,128)S(1)}, f32[2,128,512]{2,1,0:T(8,128)...) custom-call(bf16[128,5120]{1,0:T(8,128)(2,1)S(1)} %bitcast.23, f32[2,5120]{1,0:T(2,128)S(1)} %pad_maximum_fusion.refs_3_.refs_1_, ...), custom_call_target="tpu_custom_call" | custom-call | flops 1 | bytes 1 | tf_op jit(solution)/shard_map/sum_stage/pallas_call | solution.py:384
  115.7 0.9 collective-permute-start.20
  116.6 0.6 collective-permute-start.21
  117.2 5.3 %collective-permute-done.15.refs_6_ = bf16[128,1536]{1,0:T(8,128)(2,1)S(1)} collective-permute-done((bf16[128,1536]{1,0:T(8,128)(2,1)S(1)}, bf16[128,1536]{1,0:T(8,128)(2,1)S(1)}, u32[]{:S(2)}, u32[]{:S(2)}) %collective-permute-start.15) | collective-permute-done | bytes 393248 | tf_op jit(solution)/shard_map/ppermute | solution.py:28
  122.5 1.0 collective-permute-done.16.refs_7_
  123.4 1.9 %sum_stage.14 = (bf16[128,1024]{1,0:T(8,128)(2,1)S(1)}, bf16[128,1024]{1,0:T(8,128)(2,1)S(1)}, f32[2,128,256]{2,1,0:T(8,128)S(1)}, f32[2,128,256]{2,1,0:T(8,128)...) custom-call(bf16[128,5120]{1,0:T(8,128)(2,1)S(1)} %bitcast.24, ...), custom_call_target="tpu_custom_call" | custom-call | flops 1 | bytes 1 | tf_op jit(solution)/shard_map/sum_stage/pallas_call | solution.py:384
  125.3 1.1 collective-permute-start.23
  126.4 0.5 collective-permute-start.24
  127.0 1.9 %collective-permute-start.19 = (bf16[128,1024]{1,0:T(8,128)(2,1)S(1)}, bf16[128,1024]{1,0:T(8,128)(2,1)S(1)}, u32[]{:S(2)}, u32[]{:S(2)}) collective-permute-start(bf16[128,1024]{1,0:T(8,128)(2,1)S(1)} %get-tuple-element.74.refs_12_), channel_id=1, source_target_pairs={{0,8},{8,16},{16,24},{24,0},{1,9},{9,17},{17,25},{25,1},{2,10},{10... | collective-permute-start | bytes 786440 | tf_op jit(solution)/shard_map/ppermute | solution.py:23
  128.9 2.0 %collective-permute-done.20.refs_6_ = bf16[128,1536]{1,0:T(8,128)(2,1)S(1)} collective-permute-done((bf16[128,1536]{1,0:T(8,128)(2,1)S(1)}, bf16[128,1536]{1,0:T(8,128)(2,1)S(1)}, u32[]{:S(2)}, u32[]{:S(2)}) %collective-permute-start.20) | collective-permute-done | bytes 393248 | tf_op jit(solution)/shard_map/ppermute | solution.py:28
  130.9 1.0 collective-permute-done.21.refs_7_
  131.9 1.9 %sum_stage.15 = (bf16[128,1024]{1,0:T(8,128)(2,1)S(1)}, bf16[128,1024]{1,0:T(8,128)(2,1)S(1)}, f32[2,128,256]{2,1,0:T(8,128)S(1)}, f32[2,128,256]{2,1,0:T(8,128)...) custom-call(bf16[128,5120]{1,0:T(8,128)(2,1)S(1)} %bitcast.25, ...), custom_call_target="tpu_custom_call" | custom-call | flops 1 | bytes 1 | tf_op jit(solution)/shard_map/sum_stage/pallas_call | solution.py:384
  133.7 1.1 collective-permute-start.26
  134.9 0.5 collective-permute-start.27
  135.4 1.1 collective-permute-done.23.refs_2_
  136.5 1.9 %collective-permute-start.22 = (bf16[128,1024]{1,0:T(8,128)(2,1)S(1)}, bf16[128,1024]{1,0:T(8,128)(2,1)S(1)}, u32[]{:S(2)}, u32[]{:S(2)}) collective-permute-start(bf16[128,1024]{1,0:T(8,128)(2,1)S(1)} %get-tuple-element.80.refs_8_), channel_id=1, source_target_pairs={{0,8},{8,16},{16,24},{24,0},{1,9},{9,17},{17,25},{25,1},{2,10},{10... | collective-permute-start | bytes 786440 | tf_op jit(solution)/shard_map/ppermute | solution.py:23
  138.6 1.6 %collective-permute-start.25 = (bf16[128,1024]{1,0:T(8,128)(2,1)S(1)}, bf16[128,1024]{1,0:T(8,128)(2,1)S(1)}, u32[]{:S(2)}, u32[]{:S(2)}) collective-permute-start(bf16[128,1024]{1,0:T(8,128)(2,1)S(1)} %get-tuple-element.87.refs_8_), channel_id=1, source_target_pairs={{0,8},{8,16},{16,24},{24,0},{1,9},{9,17},{17,25},{25,1},{2,10},{10... | collective-permute-start | bytes 786440 | tf_op jit(solution)/shard_map/ppermute | solution.py:23
  140.2 1.0 collective-permute-start.29
  141.2 0.9 collective-permute-start.30
  142.1 4.3 %collective-permute-done.22.refs_9_ = bf16[128,1024]{1,0:T(8,128)(2,1)S(1)} collective-permute-done((bf16[128,1024]{1,0:T(8,128)(2,1)S(1)}, bf16[128,1024]{1,0:T(8,128)(2,1)S(1)}, u32[]{:S(2)}, u32[]{:S(2)}) %collective-permute-start.22) | collective-permute-done | bytes 262176 | tf_op jit(solution)/shard_map/ppermute | solution.py:23
  146.6 1.0 collective-permute-start.32
  147.6 0.9 collective-permute-start.28
  148.6 3.4 %collective-permute-done.25.refs_7_ = bf16[128,1024]{1,0:T(8,128)(2,1)S(1)} collective-permute-done((bf16[128,1024]{1,0:T(8,128)(2,1)S(1)}, bf16[128,1024]{1,0:T(8,128)(2,1)S(1)}, u32[]{:S(2)}, u32[]{:S(2)}) %collective-permute-start.25) | collective-permute-done | bytes 262176 | tf_op jit(solution)/shard_map/ppermute | solution.py:23
  152.1 1.0 collective-permute-start.31
  153.1 1.9 %collective-permute-start.34 = (bf16[128,512]{1,0:T(8,128)(2,1)S(1)}, bf16[128,512]{1,0:T(8,128)(2,1)S(1)}, u32[]{:S(2)}, u32[]{:S(2)}) collective-permute-start(bf16[128,512]{1,0:T(8,128)(2,1)S(1)} %sum_stage.19), channel_id=1, source_target_pairs={{0,8},{8,16},{16,24},{24,0},{1,9},{9,17},{17,25},{25,1},{2,10},{10... | collective-permute-start | bytes 393224 | tf_op jit(solution)/shard_map/ppermute | solution.py:23
  155.1 2.2 %collective-permute-done.28 = bf16[128,1024]{1,0:T(8,128)(2,1)S(1)} collective-permute-done((bf16[128,1024]{1,0:T(8,128)(2,1)S(1)}, bf16[128,1024]{1,0:T(8,128)(2,1)S(1)}, u32[]{:S(2)}, u32[]{:S(2)}) %collective-permute-start.28) | collective-permute-done | bytes 262176 | tf_op jit(solution)/shard_map/ppermute | solution.py:23
  157.3 1.6 %collective-permute-done.31 = bf16[128,512]{1,0:T(8,128)(2,1)S(1)} collective-permute-done((bf16[128,512]{1,0:T(8,128)(2,1)S(1)}, bf16[128,512]{1,0:T(8,128)(2,1)S(1)}, u32[]{:S(2)}, u32[]{:S(2)}) %collective-permute-start.31) | collective-permute-done | bytes 131104 | tf_op jit(solution)/shard_map/ppermute | solution.py:23
  158.9 1.4 collective-permute-done.34
  160.3 1.0 copy-done.10
  (64 shorter events, 3.1 us)
Async XLA Ops:
  2.5 18.7 %collective-permute-start.1 = (bf16[64,5120]{1,0:T(8,128)(2,1)}, bf16[64,5120]{1,0:T(8,128)(2,1)S(1)}, u32[]{:S(2)}, u32[]{:S(2)}) collective-permute-start(bf16[64,5120]{1,0:T(8,128)(2,1)} %get-tuple-element.104), channel_id=1, source_target_pairs={{0,1},{1,0},{2,3},{3,2},{4,5},{5,4},{6,7},{7,6},{8,9},{9,8},{10,11... | collective-permute-start | bytes 1966088 | tf_op jit(solution)/shard_map/ppermute | solution.py:28
  5.4 19.8 %collective-permute-start.4 = (bf16[64,5120]{1,0:T(8,128)(2,1)}, bf16[64,5120]{1,0:T(8,128)(2,1)S(1)}, u32[]{:S(2)}, u32[]{:S(2)}) collective-permute-start(bf16[64,5120]{1,0:T(8,128)(2,1)} %get-tuple-element.103), channel_id=1, source_target_pairs={{0,4},{2,6},{4,0},{6,2},{1,5},{3,7},{5,1},{7,3},{8,12},{10,14},{12... | collective-permute-start | bytes 1966088 | tf_op jit(solution)/shard_map/ppermute | solution.py:28
  6.9 35.1 %collective-permute-start.2 = (bf16[64,5120]{1,0:T(8,128)(2,1)}, bf16[64,5120]{1,0:T(8,128)(2,1)}, u32[]{:S(2)}, u32[]{:S(2)}) collective-permute-start(bf16[64,5120]{1,0:T(8,128)(2,1)} %get-tuple-element.103), channel_id=1, source_target_pairs={{0,1},{1,0},{2,3},{3,2},{4,5},{5,4},{6,7},{7,6},{8,9},{9,8},{10,11... | collective-permute-start | bytes 1966088 | tf_op jit(solution)/shard_map/ppermute | solution.py:28
  7.5 34.6 %collective-permute-start.3 = (bf16[64,5120]{1,0:T(8,128)(2,1)}, bf16[64,5120]{1,0:T(8,128)(2,1)S(1)}, u32[]{:S(2)}, u32[]{:S(2)}) collective-permute-start(bf16[64,5120]{1,0:T(8,128)(2,1)} %get-tuple-element.104), channel_id=1, source_target_pairs={{0,4},{2,6},{4,0},{6,2},{1,5},{3,7},{5,1},{7,3},{8,12},{10,14},{12... | collective-permute-start | bytes 1966088 | tf_op jit(solution)/shard_map/ppermute | solution.py:28
  21.2 1.9 %copy-start.2 = (bf16[256,2,8,384]{3,2,1,0:T(8,128)(2,1)S(1)}, bf16[256,2,8,384]{3,2,1,0:T(8,128)(2,1)}, u32[]{:S(2)}) copy-start(bf16[256,2,8,384]{3,2,1,0:T(8,128)(2,1)} %reshape_squeeze.3.refs_0_) | copy-start | bytes 9437188
  23.1 2.1 %copy-start.3 = (bf16[256,2,8,384]{3,2,1,0:T(8,128)(2,1)S(1)}, bf16[256,2,8,384]{3,2,1,0:T(8,128)(2,1)}, u32[]{:S(2)}) copy-start(bf16[256,2,8,384]{3,2,1,0:T(8,128)(2,1)} %reshape_squeeze.3.refs_0_) | copy-start | bytes 9437188
  23.1 4.0 %copy-start.9 = (f32[1,1,3,5120]{3,1,2,0:T(1,128)S(1)}, f32[1,1,3,5120]{3,1,2,0:T(1,128)}, u32[]{:S(2)}) copy-start(f32[1,1,3,5120]{3,1,2,0:T(1,128)} %param.7) | copy-start | bytes 184324
  23.1 4.2 %copy-start = (bf16[1,1,128,5120]{3,2,1,0:T(8,128)(2,1)S(1)}, bf16[1,1,128,5120]{3,2,1,0:T(8,128)(2,1)}, u32[]{:S(2)}) copy-start(bf16[1,1,128,5120]{3,2,1,0:T(8,128)(2,1)} %param.6) | copy-start | bytes 3932164
  23.1 32.1 %collective-permute-start.5 = (bf16[64,5120]{1,0:T(8,128)(2,1)S(1)}, bf16[64,5120]{1,0:T(8,128)(2,1)}, u32[]{:S(2)}, u32[]{:S(2)}) collective-permute-start(bf16[64,5120]{1,0:T(8,128)(2,1)S(1)} %after.3.refs_0_), channel_id=1, source_target_pairs={{0,4},{2,6},{4,0},{6,2},{1,5},{3,7},{5,1},{7,3},{8,12},{10,14},{12... | collective-permute-start | bytes 1966088 | tf_op jit(solution)/shard_map/ppermute | solution.py:28
  25.2 30.4 %collective-permute-start.6 = (bf16[64,5120]{1,0:T(8,128)(2,1)S(1)}, bf16[64,5120]{1,0:T(8,128)(2,1)}, u32[]{:S(2)}, u32[]{:S(2)}) collective-permute-start(bf16[64,5120]{1,0:T(8,128)(2,1)S(1)} %after.4.refs_1_), channel_id=1, source_target_pairs={{0,1},{1,0},{2,3},{3,2},{4,5},{5,4},{6,7},{7,6},{8,9},{9,8},{10,11... | collective-permute-start | bytes 1966088 | tf_op jit(solution)/shard_map/ppermute | solution.py:28
  27.0 23.7 %collective-permute-start = (f32[1,1,3,5120]{3,2,1,0:T(4,128)S(1)}, f32[1,1,3,5120]{3,2,1,0:T(4,128)S(1)}, u32[]{:S(2)}, u32[]{:S(2)}) collective-permute-start(f32[1,1,3,5120]{3,2,1,0:T(4,128)S(1)} %copy.15), channel_id=1, source_target_pairs={{0,1},{1,0},{2,3},{3,2},{4,5},{5,4},{6,7},{7,6},{8,9},{9,8},{10,11... | collective-permute-start | bytes 184328 | tf_op jit(solution)/shard_map/ppermute | solution.py:28
  28.8 1.1 copy-start.6
  42.0 16.7 %collective-permute-start.7 = (bf16[128,5120]{1,0:T(8,128)(2,1)}, bf16[128,5120]{1,0:T(8,128)(2,1)}, u32[]{:S(2)}, u32[]{:S(2)}) collective-permute-start(bf16[128,5120]{1,0:T(8,128)(2,1)} %copy-done.6), channel_id=1, source_target_pairs={{0,2},{2,0},{4,6},{6,4},{1,3},{3,1},{5,7},{7,5},{8,10},{10,8},{12,... | collective-permute-start | bytes 3932168 | tf_op jit(solution)/shard_map/ppermute | solution.py:28
  42.0 50.9 %collective-permute-start.11 = (bf16[384,5120]{1,0:T(8,128)(2,1)}, bf16[384,5120]{1,0:T(8,128)(2,1)}, u32[]{:S(2)}, u32[]{:S(2)}) collective-permute-start(bf16[384,5120]{1,0:T(8,128)(2,1)} %bitcast.30), channel_id=1, source_target_pairs={{0,2},{2,0},{4,6},{6,4},{1,3},{3,1},{5,7},{7,5},{8,10},{10,8},{12,... | collective-permute-start | bytes 11796488 | tf_op jit(solution)/shard_map/ppermute | solution.py:28
  42.5 1.9 %copy-start.4 = (bf16[8,256,768]{2,1,0:T(8,128)(2,1)S(1)}, bf16[8,256,768]{2,1,0:T(8,128)(2,1)}, u32[]{:S(2)}) copy-start(bf16[8,256,768]{2,1,0:T(8,128)(2,1)} %reshape.10.value_ref) | copy-start | bytes 9437188
  44.4 1.7 %copy-start.5 = (bf16[8,256,768]{2,1,0:T(8,128)(2,1)}, bf16[8,256,768]{2,1,0:T(8,128)(2,1)S(1)}, u32[]{:S(2)}) copy-start(bf16[8,256,768]{2,1,0:T(8,128)(2,1)S(1)} %after.5) | copy-start | bytes 9437188
  46.1 41.8 %all-to-all-start = ((bf16[8,256,768]{2,1,0:T(8,128)(2,1)}), bf16[8,256,768]{2,1,0:T(8,128)(2,1)}, u32[]{:S(2)}, u32[]{:S(2)}) async-start(bf16[8,256,768]{2,1,0:T(8,128)(2,1)} %copy-done.5), calls=%async_computation | async-start | bytes 6291456 | tf_op jit(solution)/shard_map/all_to_all | solution.py:438
  53.3 5.4 %collective-permute-start.8 = (bf16[128,5120]{1,0:T(8,128)(2,1)S(1)}, bf16[128,5120]{1,0:T(8,128)(2,1)S(1)}, u32[]{:S(2)}, u32[]{:S(2)}) collective-permute-start(bf16[128,5120]{1,0:T(8,128)(2,1)S(1)} %modulated_norm.5.refs_1_), channel_id=1, source_target_pairs={{0,2},{2,0},{4,6},{6,4},{1,3},{3,1},{5,7},{7,5},{8,10},{10,8},{12,... | collective-permute-start | bytes 3932168 | tf_op jit(solution)/shard_map/ppermute | solution.py:28
  55.1 6.3 %copy-start.7 = (bf16[128,5120]{1,0:T(8,128)(2,1)S(1)}, bf16[128,5120]{1,0:T(8,128)(2,1)}, u32[]{:S(2)}) copy-start(bf16[128,5120]{1,0:T(8,128)(2,1)} %copy-done.6) | copy-start | bytes 3932164
  55.1 3.6 %collective-permute-start.9 = (bf16[128,5120]{1,0:T(8,128)(2,1)S(1)}, bf16[128,5120]{1,0:T(8,128)(2,1)S(1)}, u32[]{:S(2)}, u32[]{:S(2)}) collective-permute-start(bf16[128,5120]{1,0:T(8,128)(2,1)S(1)} %modulated_norm.6.refs_2_), channel_id=1, source_target_pairs={{0,2},{2,0},{4,6},{6,4},{1,3},{3,1},{5,7},{7,5},{8,10},{10,8},{12,... | collective-permute-start | bytes 3932168 | tf_op jit(solution)/shard_map/ppermute | solution.py:28
  58.3 3.1 %collective-permute-start.10 = (bf16[128,5120]{1,0:T(8,128)(2,1)S(1)}, bf16[128,5120]{1,0:T(8,128)(2,1)S(1)}, u32[]{:S(2)}, u32[]{:S(2)}) collective-permute-start(bf16[128,5120]{1,0:T(8,128)(2,1)S(1)} %modulated_norm.7.refs_3_), channel_id=1, source_target_pairs={{0,2},{2,0},{4,6},{6,4},{1,3},{3,1},{5,7},{7,5},{8,10},{10,8},{12,... | collective-permute-start | bytes 3932168 | tf_op jit(solution)/shard_map/ppermute | solution.py:28
  61.4 26.5 %copy-start.8 = (s32[1,4,6]{2,1,0:T(4,128)S(1)}, s32[1,4,6]{2,1,0:T(4,128)}, u32[]{:S(2)}) copy-start(s32[1,4,6]{2,1,0:T(4,128)} %param.11) | copy-start | bytes 292
  87.9 5.0 %copy-start.1 = (bf16[1,384,5120]{2,1,0:T(8,128)(2,1)S(1)}, bf16[1,384,5120]{2,1,0:T(8,128)(2,1)}, u32[]{:S(2)}) copy-start(bf16[1,384,5120]{2,1,0:T(8,128)(2,1)} %param.9) | copy-start | bytes 11796484
  92.8 3.9 %collective-permute-start.12 = (bf16[512,384]{1,0:T(8,128)(2,1)S(1)}, bf16[512,384]{1,0:T(8,128)(2,1)S(1)}, u32[]{:S(2)}, u32[]{:S(2)}) collective-permute-start(bf16[512,384]{1,0:T(8,128)(2,1)S(1)} %get-tuple-element.56.refs_2_), channel_id=1, source_target_pairs={{0,2},{2,0},{4,6},{6,4},{1,3},{3,1},{5,7},{7,5},{8,10},{10,8},{12,... | collective-permute-start | bytes 1179656 | tf_op jit(solution)/shard_map/ppermute | solution.py:28
  97.7 9.2 %collective-permute-start.13 = (bf16[128,1024]{1,0:T(8,128)(2,1)S(1)}, bf16[128,1024]{1,0:T(8,128)(2,1)S(1)}, u32[]{:S(2)}, u32[]{:S(2)}) collective-permute-start(bf16[128,1024]{1,0:T(8,128)(2,1)S(1)} %get-tuple-element.59), channel_id=1, source_target_pairs={{0,1},{1,0},{2,3},{3,2},{4,5},{5,4},{6,7},{7,6},{8,9},{9,8},{10,11... | collective-permute-start | bytes 786440 | tf_op jit(solution)/shard_map/ppermute | solution.py:28
  98.8 9.1 %collective-permute-start.14 = (bf16[128,1024]{1,0:T(8,128)(2,1)S(1)}, bf16[128,1024]{1,0:T(8,128)(2,1)S(1)}, u32[]{:S(2)}, u32[]{:S(2)}) collective-permute-start(bf16[128,1024]{1,0:T(8,128)(2,1)S(1)} %get-tuple-element.60), channel_id=1, source_target_pairs={{0,4},{2,6},{4,0},{6,2},{1,5},{3,7},{5,1},{7,3},{8,12},{10,14},{12... | collective-permute-start | bytes 786440 | tf_op jit(solution)/shard_map/ppermute | solution.py:28
  101.6 10.8 %collective-permute-start.17 = (bf16[128,1024]{1,0:T(8,128)(2,1)S(1)}, bf16[128,1024]{1,0:T(8,128)(2,1)S(1)}, u32[]{:S(2)}, u32[]{:S(2)}) collective-permute-start(bf16[128,1024]{1,0:T(8,128)(2,1)S(1)} %get-tuple-element.70), channel_id=1, source_target_pairs={{0,1},{1,0},{2,3},{3,2},{4,5},{5,4},{6,7},{7,6},{8,9},{9,8},{10,11... | collective-permute-start | bytes 786440 | tf_op jit(solution)/shard_map/ppermute | solution.py:28
  102.9 10.3 %collective-permute-start.18 = (bf16[128,1024]{1,0:T(8,128)(2,1)S(1)}, bf16[128,1024]{1,0:T(8,128)(2,1)S(1)}, u32[]{:S(2)}, u32[]{:S(2)}) collective-permute-start(bf16[128,1024]{1,0:T(8,128)(2,1)S(1)} %get-tuple-element.71), channel_id=1, source_target_pairs={{0,4},{2,6},{4,0},{6,2},{1,5},{3,7},{5,1},{7,3},{8,12},{10,14},{12... | collective-permute-start | bytes 786440 | tf_op jit(solution)/shard_map/ppermute | solution.py:28
  110.4 12.1 %collective-permute-start.15 = (bf16[128,1536]{1,0:T(8,128)(2,1)S(1)}, bf16[128,1536]{1,0:T(8,128)(2,1)S(1)}, u32[]{:S(2)}, u32[]{:S(2)}) collective-permute-start(bf16[128,1536]{1,0:T(8,128)(2,1)S(1)} %get-tuple-element.64), channel_id=1, source_target_pairs={{0,1},{1,0},{2,3},{3,2},{4,5},{5,4},{6,7},{7,6},{8,9},{9,8},{10,11... | collective-permute-start | bytes 1179656 | tf_op jit(solution)/shard_map/ppermute | solution.py:28
  111.4 12.1 %collective-permute-start.16 = (bf16[128,1536]{1,0:T(8,128)(2,1)S(1)}, bf16[128,1536]{1,0:T(8,128)(2,1)S(1)}, u32[]{:S(2)}, u32[]{:S(2)}) collective-permute-start(bf16[128,1536]{1,0:T(8,128)(2,1)S(1)} %get-tuple-element.65), channel_id=1, source_target_pairs={{0,4},{2,6},{4,0},{6,2},{1,5},{3,7},{5,1},{7,3},{8,12},{10,14},{12... | collective-permute-start | bytes 1179656 | tf_op jit(solution)/shard_map/ppermute | solution.py:28
  115.7 15.2 %collective-permute-start.20 = (bf16[128,1536]{1,0:T(8,128)(2,1)S(1)}, bf16[128,1536]{1,0:T(8,128)(2,1)S(1)}, u32[]{:S(2)}, u32[]{:S(2)}) collective-permute-start(bf16[128,1536]{1,0:T(8,128)(2,1)S(1)} %get-tuple-element.75), channel_id=1, source_target_pairs={{0,1},{1,0},{2,3},{3,2},{4,5},{5,4},{6,7},{7,6},{8,9},{9,8},{10,11... | collective-permute-start | bytes 1179656 | tf_op jit(solution)/shard_map/ppermute | solution.py:28
  116.6 15.3 %collective-permute-start.21 = (bf16[128,1536]{1,0:T(8,128)(2,1)S(1)}, bf16[128,1536]{1,0:T(8,128)(2,1)S(1)}, u32[]{:S(2)}, u32[]{:S(2)}) collective-permute-start(bf16[128,1536]{1,0:T(8,128)(2,1)S(1)} %get-tuple-element.76), channel_id=1, source_target_pairs={{0,4},{2,6},{4,0},{6,2},{1,5},{3,7},{5,1},{7,3},{8,12},{10,14},{12... | collective-permute-start | bytes 1179656 | tf_op jit(solution)/shard_map/ppermute | solution.py:28
  125.3 11.2 %collective-permute-start.23 = (bf16[128,1024]{1,0:T(8,128)(2,1)S(1)}, bf16[128,1024]{1,0:T(8,128)(2,1)S(1)}, u32[]{:S(2)}, u32[]{:S(2)}) collective-permute-start(bf16[128,1024]{1,0:T(8,128)(2,1)S(1)} %get-tuple-element.81), channel_id=1, source_target_pairs={{0,1},{1,0},{2,3},{3,2},{4,5},{5,4},{6,7},{7,6},{8,9},{9,8},{10,11... | collective-permute-start | bytes 786440 | tf_op jit(solution)/shard_map/ppermute | solution.py:28
  126.4 12.0 %collective-permute-start.24 = (bf16[128,1024]{1,0:T(8,128)(2,1)S(1)}, bf16[128,1024]{1,0:T(8,128)(2,1)S(1)}, u32[]{:S(2)}, u32[]{:S(2)}) collective-permute-start(bf16[128,1024]{1,0:T(8,128)(2,1)S(1)} %get-tuple-element.82), channel_id=1, source_target_pairs={{0,4},{2,6},{4,0},{6,2},{1,5},{3,7},{5,1},{7,3},{8,12},{10,14},{12... | collective-permute-start | bytes 786440 | tf_op jit(solution)/shard_map/ppermute | solution.py:28
  127.0 11.5 %collective-permute-start.19 = (bf16[128,1024]{1,0:T(8,128)(2,1)S(1)}, bf16[128,1024]{1,0:T(8,128)(2,1)S(1)}, u32[]{:S(2)}, u32[]{:S(2)}) collective-permute-start(bf16[128,1024]{1,0:T(8,128)(2,1)S(1)} %get-tuple-element.74.refs_12_), channel_id=1, source_target_pairs={{0,8},{8,16},{16,24},{24,0},{1,9},{9,17},{17,25},{25,1},{2,10},{10... | collective-permute-start | bytes 786440 | tf_op jit(solution)/shard_map/ppermute | solution.py:23
  133.7 7.5 %collective-permute-start.26 = (bf16[128,1024]{1,0:T(8,128)(2,1)S(1)}, bf16[128,1024]{1,0:T(8,128)(2,1)S(1)}, u32[]{:S(2)}, u32[]{:S(2)}) collective-permute-start(bf16[128,1024]{1,0:T(8,128)(2,1)S(1)} %get-tuple-element.88), channel_id=1, source_target_pairs={{0,1},{1,0},{2,3},{3,2},{4,5},{5,4},{6,7},{7,6},{8,9},{9,8},{10,11... | collective-permute-start | bytes 786440 | tf_op jit(solution)/shard_map/ppermute | solution.py:28
  134.9 7.3 %collective-permute-start.27 = (bf16[128,1024]{1,0:T(8,128)(2,1)S(1)}, bf16[128,1024]{1,0:T(8,128)(2,1)S(1)}, u32[]{:S(2)}, u32[]{:S(2)}) collective-permute-start(bf16[128,1024]{1,0:T(8,128)(2,1)S(1)} %get-tuple-element.89), channel_id=1, source_target_pairs={{0,4},{2,6},{4,0},{6,2},{1,5},{3,7},{5,1},{7,3},{8,12},{10,14},{12... | collective-permute-start | bytes 786440 | tf_op jit(solution)/shard_map/ppermute | solution.py:28
  136.5 9.9 %collective-permute-start.22 = (bf16[128,1024]{1,0:T(8,128)(2,1)S(1)}, bf16[128,1024]{1,0:T(8,128)(2,1)S(1)}, u32[]{:S(2)}, u32[]{:S(2)}) collective-permute-start(bf16[128,1024]{1,0:T(8,128)(2,1)S(1)} %get-tuple-element.80.refs_8_), channel_id=1, source_target_pairs={{0,8},{8,16},{16,24},{24,0},{1,9},{9,17},{17,25},{25,1},{2,10},{10... | collective-permute-start | bytes 786440 | tf_op jit(solution)/shard_map/ppermute | solution.py:23
  138.6 13.5 %collective-permute-start.25 = (bf16[128,1024]{1,0:T(8,128)(2,1)S(1)}, bf16[128,1024]{1,0:T(8,128)(2,1)S(1)}, u32[]{:S(2)}, u32[]{:S(2)}) collective-permute-start(bf16[128,1024]{1,0:T(8,128)(2,1)S(1)} %get-tuple-element.87.refs_8_), channel_id=1, source_target_pairs={{0,8},{8,16},{16,24},{24,0},{1,9},{9,17},{17,25},{25,1},{2,10},{10... | collective-permute-start | bytes 786440 | tf_op jit(solution)/shard_map/ppermute | solution.py:23
  140.2 8.3 %collective-permute-start.29 = (bf16[128,256]{1,0:T(8,128)(2,1)S(1)}, bf16[128,256]{1,0:T(8,128)(2,1)S(1)}, u32[]{:S(2)}, u32[]{:S(2)}) collective-permute-start(bf16[128,256]{1,0:T(8,128)(2,1)S(1)} %get-tuple-element.95), channel_id=1, source_target_pairs={{0,1},{1,0},{2,3},{3,2},{4,5},{5,4},{6,7},{7,6},{8,9},{9,8},{10,11... | collective-permute-start | bytes 196616 | tf_op jit(solution)/shard_map/ppermute | solution.py:28
  141.2 7.4 %collective-permute-start.30 = (bf16[128,256]{1,0:T(8,128)(2,1)S(1)}, bf16[128,256]{1,0:T(8,128)(2,1)S(1)}, u32[]{:S(2)}, u32[]{:S(2)}) collective-permute-start(bf16[128,256]{1,0:T(8,128)(2,1)S(1)} %get-tuple-element.96), channel_id=1, source_target_pairs={{0,4},{2,6},{4,0},{6,2},{1,5},{3,7},{5,1},{7,3},{8,12},{10,14},{12... | collective-permute-start | bytes 196616 | tf_op jit(solution)/shard_map/ppermute | solution.py:28
  146.6 6.5 %collective-permute-start.32 = (bf16[128,256]{1,0:T(8,128)(2,1)S(1)}, bf16[128,256]{1,0:T(8,128)(2,1)S(1)}, u32[]{:S(2)}, u32[]{:S(2)}) collective-permute-start(bf16[128,256]{1,0:T(8,128)(2,1)S(1)} %get-tuple-element.99), channel_id=1, source_target_pairs={{0,1},{1,0},{2,3},{3,2},{4,5},{5,4},{6,7},{7,6},{8,9},{9,8},{10,11... | collective-permute-start | bytes 196616 | tf_op jit(solution)/shard_map/ppermute | solution.py:28
  147.6 9.7 %collective-permute-start.28 = (bf16[128,1024]{1,0:T(8,128)(2,1)S(1)}, bf16[128,1024]{1,0:T(8,128)(2,1)S(1)}, u32[]{:S(2)}, u32[]{:S(2)}) collective-permute-start(bf16[128,1024]{1,0:T(8,128)(2,1)S(1)} %get-tuple-element.94.refs_6_), channel_id=1, source_target_pairs={{0,8},{8,16},{16,24},{24,0},{1,9},{9,17},{17,25},{25,1},{2,10},{10... | collective-permute-start | bytes 786440 | tf_op jit(solution)/shard_map/ppermute | solution.py:23
  148.5 4.6 %collective-permute-start.33 = (bf16[128,256]{1,0:T(8,128)(2,1)S(1)}, bf16[128,256]{1,0:T(8,128)(2,1)S(1)}, u32[]{:S(2)}, u32[]{:S(2)}) collective-permute-start(bf16[128,256]{1,0:T(8,128)(2,1)S(1)} %get-tuple-element.100), channel_id=1, source_target_pairs={{0,4},{2,6},{4,0},{6,2},{1,5},{3,7},{5,1},{7,3},{8,12},{10,14},{12... | collective-permute-start | bytes 196616 | tf_op jit(solution)/shard_map/ppermute | solution.py:28
  152.1 6.8 %collective-permute-start.31 = (bf16[128,512]{1,0:T(8,128)(2,1)S(1)}, bf16[128,512]{1,0:T(8,128)(2,1)S(1)}, u32[]{:S(2)}, u32[]{:S(2)}) collective-permute-start(bf16[128,512]{1,0:T(8,128)(2,1)S(1)} %sum_stage.18.refs_6_), channel_id=1, source_target_pairs={{0,8},{8,16},{16,24},{24,0},{1,9},{9,17},{17,25},{25,1},{2,10},{10... | collective-permute-start | bytes 393224 | tf_op jit(solution)/shard_map/ppermute | solution.py:23
  153.1 7.2 %collective-permute-start.34 = (bf16[128,512]{1,0:T(8,128)(2,1)S(1)}, bf16[128,512]{1,0:T(8,128)(2,1)S(1)}, u32[]{:S(2)}, u32[]{:S(2)}) collective-permute-start(bf16[128,512]{1,0:T(8,128)(2,1)S(1)} %sum_stage.19), channel_id=1, source_target_pairs={{0,8},{8,16},{16,24},{24,0},{1,9},{9,17},{17,25},{25,1},{2,10},{10... | collective-permute-start | bytes 393224 | tf_op jit(solution)/shard_map/ppermute | solution.py:23
  160.3 1.1 copy-start.10

commit v14 on v13

--- a/solution.py
+++ b/solution.py
@@ -12,7 +12,7 @@
 MIB = 2**20
 SPARE = 39
 LOG2E = 1.4426950408889634
-CHUNK_SHARES = (4, 4, 4, 4, 2, 2)
+CHUNK_SHARES = (5, 5, 2, 3, 3, 2)
 
 guidance_scale = 5.0
 SHORT = pl.CostEstimate(flops=1, bytes_accessed=1, transcendentals=0)

time: 162 us -> 160 us (0.988)
  waiting for transfers between devices: 43.8 us -> 38.3 us
  starting transfers between devices: 38.7 us -> 41.1 us
    ppermute x6, waiting for transfers between devices: 12.9 us -> 9.15 us  [from_behind(): return lax.ppermute(x, axis, [(i, (i + by) % count) for i in range(count)])]
    ppermute x29, starting transfers between devices: 24.8 us -> 26.7 us  [from_partner(): return lax.ppermute(value, axis, pairs)]
    ppermute x29, waiting for transfers between devices: 23.6 us -> 21.9 us  [from_partner(): return lax.ppermute(value, axis, pairs)]
  transfers between devices with their start and end apart: 36 -> 36, of which waited for: 16 -> 17; matrix products, arithmetic and copies ran while one was open for 13% -> 13% of each run, Pallas kernels for 29% -> 30%
where the time goes in v14:
time: 160 us; the launch traced here: 159 us
  Pallas kernels  49 us (31%)
  starting transfers between devices  41.1 us (26%)
  waiting for transfers between devices  38.3 us (24%)
  local copies, waits for them, and re-layouts  30.3 us (19%)
    ppermute x29, starting transfers between devices, from_partner(): return lax.ppermute(value, axis, pairs)  26.7 us
    ppermute x29, waiting for transfers between devices, from_partner(): return lax.ppermute(value, axis, pairs)  21.9 us
    pallas_call x1, Pallas kernels, project(): pl.pallas_call(functools.partial(project_kernel, blocks=len(blocks)), gri...  19.2 us
    pallas_call x10, Pallas kernels, stage(): pl.pallas_call(functools.partial(stage_kernel, parts=parts, start=start,...  12.7 us
    ppermute x6, starting transfers between devices, from_behind(): return lax.ppermute(x, axis, [(i, (i + by) % count) for i in range(count)])  9.82 us
    ppermute x6, waiting for transfers between devices, from_behind(): return lax.ppermute(x, axis, [(i, (i + by) % count) for i in range(count)])  9.15 us
    pallas_call x4, Pallas kernels, modulated_norm(): pl.pallas_call(norm_kernel, in_specs=[pl.BlockSpec(memory_space=pltpu.VME...  8.42 us
    reshape x1, local copies, waits for them, and re-layouts, per_device(): unpacked.transpose(2, 0, 1, 3).reshape(devices, context_rows, 2 * width)  8.04 us
  transfers between devices with their start and end apart: 36, of which 17 were waited for; matrix products, arithmetic and copies ran while one was open for 13% of the time, Pallas kernels for 30%

profile of v14, /device:TPU:0, one launch (start us, length us, event | category | flops | bytes accessed | tf_op | source)
XLA Modules:
  0.0 159.1 jit_solution(5076164648455775666)
XLA Ops:
  0.0 2.5 %slice_bitcast_fusion = (bf16[64,5120]{1,0:T(8,128)(2,1)}, bf16[64,5120]{1,0:T(8,128)(2,1)}) fusion(bf16[1,1,128,5120]{3,2,1,0:T(8,128)(2,1)} %param.6), kind=kLoop, calls=%fused_computation | loop fusion | bytes 2621440 | tf_op jit(solution)/shard_map/slice | solution.py:422
  2.5 2.9 %collective-permute-start.1 = (bf16[64,5120]{1,0:T(8,128)(2,1)}, bf16[64,5120]{1,0:T(8,128)(2,1)S(1)}, u32[]{:S(2)}, u32[]{:S(2)}) collective-permute-start(bf16[64,5120]{1,0:T(8,128)(2,1)} %get-tuple-element.104), channel_id=1, source_target_pairs={{0,1},{1,0},{2,3},{3,2},{4,5},{5,4},{6,7},{7,6},{8,9},{9,8},{10,11... | collective-permute-start | bytes 1966088 | tf_op jit(solution)/shard_map/ppermute | solution.py:28
  5.4 1.5 collective-permute-start.4
  6.9 0.5 collective-permute-start.2
  7.5 8.0 %reshape_squeeze.3.refs_0_ = bf16[256,2,8,384]{3,2,1,0:T(8,128)(2,1)} reshape(bf16[1,1,256,2,3072]{4,3,2,1,0:T(2,128)(2,1)} %param.10) | data formatting | bytes 6291456 | tf_op jit(solution)/shard_map/reshape;squeeze | solution.py:419
  15.5 5.7 %collective-permute-done.1.value_ref = bf16[64,5120]{1,0:T(8,128)(2,1)S(1)} collective-permute-done((bf16[64,5120]{1,0:T(8,128)(2,1)}, bf16[64,5120]{1,0:T(8,128)(2,1)S(1)}, u32[]{:S(2)}, u32[]{:S(2)}) %collective-permute-start.1) | collective-permute-done | bytes 655392 | tf_op jit(solution)/shard_map/ppermute | solution.py:28
  21.2 1.9 %copy-done.2 = bf16[256,2,8,384]{3,2,1,0:T(8,128)(2,1)S(1)} copy-done((bf16[256,2,8,384]{3,2,1,0:T(8,128)(2,1)S(1)}, bf16[256,2,8,384]{3,2,1,0:T(8,128)(2,1)}, u32[]{:S(2)}) %copy-start.2) | copy-done | bytes 3145752
  23.1 2.1 %collective-permute-start.5 = (bf16[64,5120]{1,0:T(8,128)(2,1)S(1)}, bf16[64,5120]{1,0:T(8,128)(2,1)}, u32[]{:S(2)}, u32[]{:S(2)}) collective-permute-start(bf16[64,5120]{1,0:T(8,128)(2,1)S(1)} %after.3.refs_0_), channel_id=1, source_target_pairs={{0,4},{2,6},{4,0},{6,2},{1,5},{3,7},{5,1},{7,3},{8,12},{10,14},{12... | collective-permute-start | bytes 1966088 | tf_op jit(solution)/shard_map/ppermute | solution.py:28
  25.2 1.8 %collective-permute-start.6 = (bf16[64,5120]{1,0:T(8,128)(2,1)S(1)}, bf16[64,5120]{1,0:T(8,128)(2,1)}, u32[]{:S(2)}, u32[]{:S(2)}) collective-permute-start(bf16[64,5120]{1,0:T(8,128)(2,1)S(1)} %after.4.refs_1_), channel_id=1, source_target_pairs={{0,1},{1,0},{2,3},{3,2},{4,5},{5,4},{6,7},{7,6},{8,9},{9,8},{10,11... | collective-permute-start | bytes 1966088 | tf_op jit(solution)/shard_map/ppermute | solution.py:28
  27.3 1.5 modulated_norm.4.refs_0_
  28.8 1.0 copy-done.6
  29.9 4.1 %copy.11 = bf16[8,256,2,384]{3,2,1,0:T(2,128)(2,1)} copy(bf16[8,256,2,384]{3,0,2,1:T(8,128)(2,1)S(1)} %bitcast.37) | data formatting | bytes 6291456 | tf_op jit(solution)/shard_map/transpose | solution.py:420
  34.0 8.0 %reshape.10.value_ref = bf16[8,256,768]{2,1,0:T(8,128)(2,1)} reshape(bf16[8,256,2,384]{3,2,1,0:T(2,128)(2,1)} %copy.11) | data formatting | bytes 6291456 | tf_op jit(solution)/shard_map/reshape | solution.py:420
  42.5 1.9 %copy-done.4 = bf16[8,256,768]{2,1,0:T(8,128)(2,1)S(1)} copy-done((bf16[8,256,768]{2,1,0:T(8,128)(2,1)S(1)}, bf16[8,256,768]{2,1,0:T(8,128)(2,1)}, u32[]{:S(2)}) %copy-start.4) | copy-done | bytes 3145752
  44.4 1.7 %copy-done.5 = bf16[8,256,768]{2,1,0:T(8,128)(2,1)} copy-done((bf16[8,256,768]{2,1,0:T(8,128)(2,1)}, bf16[8,256,768]{2,1,0:T(8,128)(2,1)S(1)}, u32[]{:S(2)}) %copy-start.5) | copy-done | bytes 3145752
  46.1 4.6 %all-to-all-start = ((bf16[8,256,768]{2,1,0:T(8,128)(2,1)}), bf16[8,256,768]{2,1,0:T(8,128)(2,1)}, u32[]{:S(2)}, u32[]{:S(2)}) async-start(bf16[8,256,768]{2,1,0:T(8,128)(2,1)} %copy-done.5), calls=%async_computation | async-start | bytes 6291456 | tf_op jit(solution)/shard_map/all_to_all | solution.py:438
  50.7 2.6 %modulated_norm.5.refs_1_ = bf16[128,5120]{1,0:T(8,128)(2,1)S(1)} custom-call(bf16[64,5120]{1,0:T(8,128)(2,1)S(1)} %after.3.refs_0_, bf16[64,5120]{1,0:T(8,128)(2,1)} %collective-permute-done.2.refs_1_.refs_0_, f32[3,5120]{1,0:T(4,128)S(1)} %bitcast.40), custom_call_target="tpu_custom_call" | custom-call | flops 1 | bytes 1 | tf_op jit(solution)/shard_map/modulated_norm/pallas_call | solution.py:55
  53.6 1.5 modulated_norm.6.refs_2_
  55.5 2.8 %modulated_norm.7.refs_3_ = bf16[128,5120]{1,0:T(8,128)(2,1)S(1)} custom-call(bf16[64,5120]{1,0:T(8,128)(2,1)} %collective-permute-done.5.refs_0_, bf16[64,5120]{1,0:T(8,128)(2,1)} %collective-permute-done.6.refs_1_, f32[3,5120]{1,0:T(4,128)S(1)} %bitcast.41), custom_call_target="tpu_custom_call" | custom-call | flops 1 | bytes 1 | tf_op jit(solution)/shard_map/modulated_norm/pallas_call | solution.py:55
  58.8 2.7 %collective-permute-done.10.refs_7_ = bf16[128,5120]{1,0:T(8,128)(2,1)S(1)} collective-permute-done((bf16[128,5120]{1,0:T(8,128)(2,1)S(1)}, bf16[128,5120]{1,0:T(8,128)(2,1)S(1)}, u32[]{:S(2)}, u32[]{:S(2)}) %collective-permute-start.10) | collective-permute-done | bytes 1310752 | tf_op jit(solution)/shard_map/ppermute | solution.py:28
  61.4 19.2 %project_heads.1.heads_in = bf16[48,1024,128]{2,1,0:T(8,128)(2,1)} custom-call(bf16[128,5120]{1,0:T(8,128)(2,1)S(1)} %copy-done.7, bf16[128,5120]{1,0:T(8,128)(2,1)S(1)} %modulated_norm.5.refs_1_, bf16[128,5120]{1,0:T(8,128)(2,1)S(1)} %modulated_norm.6.refs_2_, bf16[128,5120]{1,0:T(8,128)(2,1)S(1)} %modulated_norm.7.refs_3_, ...), custom_call_target="tpu_custom_call" | custom-call | flops 12079595520 | bytes 22282240 | tf_op jit(solution)/shard_map/project_heads/pallas_call | solution.py:124
  80.6 7.3 %all-to-all-done = bf16[8,256,768]{2,1,0:T(8,128)(2,1)} async-done(((bf16[8,256,768]{2,1,0:T(8,128)(2,1)}), bf16[8,256,768]{2,1,0:T(8,128)(2,1)}, u32[]{:S(2)}, u32[]{:S(2)}) %all-to-all-start) | async-done | bytes 3145760 | tf_op jit(solution)/shard_map/all_to_all | solution.py:438
  87.9 4.8 %attend_first.1 = (bf16[512,384]{1,0:T(8,128)(2,1)S(1)}, bf16[3,1024,128]{2,1,0:T(8,128)(2,1)S(1)}, bf16[6,3072,128]{2,1,0:T(8,128)(2,1)S(1)}) custom-call(s32[4,6]{1,0:T(4,128)S(1)} %bitcast.42, bf16[48,1024,128]{2,1,0:T(8,128)(2,1)} %project_heads.1.heads_in, bf16[2048,768]{1,0:T(8,128)(2,1)} %bitcast.9.context_in), custom_call_target="tpu_custom_call" | custom-call | flops 1 | bytes 1 | tf_op jit(solution)/shard_map/attend_first/pallas_call | solution.py:219
  92.9 3.8 %attend_second.1 = (bf16[512,384]{1,0:T(8,128)(2,1)S(1)}, bf16[768,1280]{1,0:T(8,128)(2,1)S(1)}) custom-call(s32[4,6]{1,0:T(4,128)S(1)} %bitcast.43, bf16[3,1024,128]{2,1,0:T(8,128)(2,1)S(1)} %get-tuple-element.54.queries_ref, bf16[6,3072,128]{2,1,0:T(8,128)(2,1)S(1)} %get-tuple-element.55.pool_ref, bf16[384,5120]{1,0:T(8,128)(2,1)S(1)} %bitcast.31, ...), custom_call_target="tpu_custom_call" | custom-call | flops 1 | bytes 1 | tf_op jit(solution)/shard_map/attend_second/pallas_call | solution.py:259
  96.7 1.4 sum_stage.10
  98.2 1.1 collective-permute-start.13
  99.3 0.5 collective-permute-start.14
  99.8 2.7 %sum_stage.11 = (bf16[128,1280]{1,0:T(8,128)(2,1)S(1)}, bf16[128,1280]{1,0:T(8,128)(2,1)S(1)}, f32[2,128,640]{2,1,0:T(8,128)S(1)}, f32[2,128,640]{2,1,0:T(8,128)S(1)}) custom-call(bf16[128,5120]{1,0:T(8,128)(2,1)S(1)} %bitcast.21, f32[2,5120]{1,0:T(2,128)S(1)} %pad_maximum_fusion.refs_3_.refs_1_, bf16[512,384]{1,0:T(8,128)(2,1)S(1)} %get-tuple-element.57.refs_2_, ...), custom_call_target="tpu_custom_call" | custom-call | flops 1 | bytes 1 | tf_op jit(solution)/shard_map/sum_stage/pallas_call | solution.py:384
  102.5 1.4 collective-permute-start.17
  103.9 1.1 collective-permute-start.18
  105.1 3.7 %collective-permute-done.13.refs_6_ = bf16[128,1280]{1,0:T(8,128)(2,1)S(1)} collective-permute-done((bf16[128,1280]{1,0:T(8,128)(2,1)S(1)}, bf16[128,1280]{1,0:T(8,128)(2,1)S(1)}, u32[]{:S(2)}, u32[]{:S(2)}) %collective-permute-start.13) | collective-permute-done | bytes 327712 | tf_op jit(solution)/shard_map/ppermute | solution.py:28
  108.7 1.1 collective-permute-done.14.refs_7_
  109.8 1.9 %sum_stage.12 = (bf16[128,1152]{1,0:T(8,128)(2,1)S(1)}, bf16[128,1152]{1,0:T(8,128)(2,1)S(1)}, f32[2,128,256]{2,1,0:T(8,128)S(1)}, f32[2,128,256]{2,1,0:T(8,128)...) custom-call(bf16[128,5120]{1,0:T(8,128)(2,1)S(1)} %bitcast.22, f32[2,5120]{1,0:T(2,128)S(1)} %pad_maximum_fusion.refs_3_.refs_1_, ...), custom_call_target="tpu_custom_call" | custom-call | flops 1 | bytes 1 | tf_op jit(solution)/shard_map/sum_stage/pallas_call | solution.py:384
  111.7 1.0 collective-permute-start.15
  112.7 0.9 collective-permute-start.16
  113.7 2.1 %collective-permute-done.17.refs_6_ = bf16[128,1280]{1,0:T(8,128)(2,1)S(1)} collective-permute-done((bf16[128,1280]{1,0:T(8,128)(2,1)S(1)}, bf16[128,1280]{1,0:T(8,128)(2,1)S(1)}, u32[]{:S(2)}, u32[]{:S(2)}) %collective-permute-start.17) | collective-permute-done | bytes 327712 | tf_op jit(solution)/shard_map/ppermute | solution.py:28
  115.8 1.1 collective-permute-done.18.refs_7_
  116.9 2.4 %sum_stage.13 = (bf16[128,1408]{1,0:T(8,128)(2,1)S(1)}, bf16[128,1408]{1,0:T(8,128)(2,1)S(1)}, f32[2,128,384]{2,1,0:T(8,128)S(1)}, f32[2,128,384]{2,1,0:T(8,128)...) custom-call(bf16[128,5120]{1,0:T(8,128)(2,1)S(1)} %bitcast.23, f32[2,5120]{1,0:T(2,128)S(1)} %pad_maximum_fusion.refs_3_.refs_1_, ...), custom_call_target="tpu_custom_call" | custom-call | flops 1 | bytes 1 | tf_op jit(solution)/shard_map/sum_stage/pallas_call | solution.py:384
  119.2 1.0 collective-permute-start.20
  120.3 0.9 collective-permute-start.21
  121.2 0.9 collective-permute-done.15.refs_6_
  122.1 1.1 collective-permute-done.16.refs_7_
  123.2 2.3 %sum_stage.14 = (bf16[128,1024]{1,0:T(8,128)(2,1)S(1)}, bf16[128,1024]{1,0:T(8,128)(2,1)S(1)}, f32[2,128,384]{2,1,0:T(8,128)S(1)}, f32[2,128,384]{2,1,0:T(8,128)...) custom-call(bf16[128,5120]{1,0:T(8,128)(2,1)S(1)} %bitcast.24, ...), custom_call_target="tpu_custom_call" | custom-call | flops 1 | bytes 1 | tf_op jit(solution)/shard_map/sum_stage/pallas_call | solution.py:384
  125.4 2.0 %collective-permute-start.19 = (bf16[128,1280]{1,0:T(8,128)(2,1)S(1)}, bf16[128,1280]{1,0:T(8,128)(2,1)S(1)}, u32[]{:S(2)}, u32[]{:S(2)}) collective-permute-start(bf16[128,1280]{1,0:T(8,128)(2,1)S(1)} %get-tuple-element.74.refs_12_), channel_id=1, source_target_pairs={{0,8},{8,16},{16,24},{24,0},{1,9},{9,17},{17,25},{25,1},{2,10},{10... | collective-permute-start | bytes 983048 | tf_op jit(solution)/shard_map/ppermute | solution.py:23
  127.4 1.0 collective-permute-start.23
  128.5 0.9 collective-permute-start.24
  129.3 1.0 collective-permute-done.20.refs_6_
  130.4 0.8 collective-permute-done.21.refs_7_
  131.2 1.8 %sum_stage.15 = (bf16[128,896]{1,0:T(8,128)(2,1)S(1)}, bf16[128,896]{1,0:T(8,128)(2,1)S(1)}, f32[2,128,256]{2,1,0:T(8,128)S(1)}, f32[2,128,256]{2,1,0:T(8,128)S(...) custom-call(bf16[128,5120]{1,0:T(8,128)(2,1)S(1)} %bitcast.25, ...), custom_call_target="tpu_custom_call" | custom-call | flops 1 | bytes 1 | tf_op jit(solution)/shard_map/sum_stage/pallas_call | solution.py:384
  133.0 2.3 %collective-permute-start.22 = (bf16[128,1280]{1,0:T(8,128)(2,1)S(1)}, bf16[128,1280]{1,0:T(8,128)(2,1)S(1)}, u32[]{:S(2)}, u32[]{:S(2)}) collective-permute-start(bf16[128,1280]{1,0:T(8,128)(2,1)S(1)} %get-tuple-element.80.refs_8_), channel_id=1, source_target_pairs={{0,8},{8,16},{16,24},{24,0},{1,9},{9,17},{17,25},{25,1},{2,10},{10... | collective-permute-start | bytes 983048 | tf_op jit(solution)/shard_map/ppermute | solution.py:23
  135.3 1.0 collective-permute-start.26
  137.0 1.4 collective-permute-start.29
  138.4 1.2 collective-permute-start.30
  139.6 1.7 %collective-permute-done.26.refs_2_ = bf16[128,896]{1,0:T(8,128)(2,1)S(1)} collective-permute-done((bf16[128,896]{1,0:T(8,128)(2,1)S(1)}, bf16[128,896]{1,0:T(8,128)(2,1)S(1)}, u32[]{:S(2)}, u32[]{:S(2)}) %collective-permute-start.26) | collective-permute-done | bytes 229408 | tf_op jit(solution)/shard_map/ppermute | solution.py:28
  141.3 1.7 %collective-permute-start.25 = (bf16[128,512]{1,0:T(8,128)(2,1)S(1)}, bf16[128,512]{1,0:T(8,128)(2,1)S(1)}, u32[]{:S(2)}, u32[]{:S(2)}) collective-permute-start(bf16[128,512]{1,0:T(8,128)(2,1)S(1)} %get-tuple-element.87.refs_8_), channel_id=1, source_target_pairs={{0,8},{8,16},{16,24},{24,0},{1,9},{9,17},{17,25},{25,1},{2,10},{10... | collective-permute-start | bytes 393224 | tf_op jit(solution)/shard_map/ppermute | solution.py:23
  143.4 1.0 collective-permute-start.32
  144.4 0.7 collective-permute-start.33
  145.1 1.6 %collective-permute-start.28 = (bf16[128,768]{1,0:T(8,128)(2,1)S(1)}, bf16[128,768]{1,0:T(8,128)(2,1)S(1)}, u32[]{:S(2)}, u32[]{:S(2)}) collective-permute-start(bf16[128,768]{1,0:T(8,128)(2,1)S(1)} %get-tuple-element.94.refs_6_), channel_id=1, source_target_pairs={{0,8},{8,16},{16,24},{24,0},{1,9},{9,17},{17,25},{25,1},{2,10},{10... | collective-permute-start | bytes 589832 | tf_op jit(solution)/shard_map/ppermute | solution.py:23
  146.8 2.2 %collective-permute-done.25.refs_7_ = bf16[128,512]{1,0:T(8,128)(2,1)S(1)} collective-permute-done((bf16[128,512]{1,0:T(8,128)(2,1)S(1)}, bf16[128,512]{1,0:T(8,128)(2,1)S(1)}, u32[]{:S(2)}, u32[]{:S(2)}) %collective-permute-start.25) | collective-permute-done | bytes 131104 | tf_op jit(solution)/shard_map/ppermute | solution.py:23
  149.3 2.0 %collective-permute-start.34 = (bf16[128,512]{1,0:T(8,128)(2,1)S(1)}, bf16[128,512]{1,0:T(8,128)(2,1)S(1)}, u32[]{:S(2)}, u32[]{:S(2)}) collective-permute-start(bf16[128,512]{1,0:T(8,128)(2,1)S(1)} %sum_stage.19), channel_id=1, source_target_pairs={{0,8},{8,16},{16,24},{24,0},{1,9},{9,17},{17,25},{25,1},{2,10},{10... | collective-permute-start | bytes 393224 | tf_op jit(solution)/shard_map/ppermute | solution.py:23
  151.3 3.2 %collective-permute-done.28 = bf16[128,768]{1,0:T(8,128)(2,1)S(1)} collective-permute-done((bf16[128,768]{1,0:T(8,128)(2,1)S(1)}, bf16[128,768]{1,0:T(8,128)(2,1)S(1)}, u32[]{:S(2)}, u32[]{:S(2)}) %collective-permute-start.28) | collective-permute-done | bytes 196640 | tf_op jit(solution)/shard_map/ppermute | solution.py:23
  154.5 2.1 %collective-permute-done.31 = bf16[128,768]{1,0:T(8,128)(2,1)S(1)} collective-permute-done((bf16[128,768]{1,0:T(8,128)(2,1)S(1)}, bf16[128,768]{1,0:T(8,128)(2,1)S(1)}, u32[]{:S(2)}, u32[]{:S(2)}) %collective-permute-start.31) | collective-permute-done | bytes 196640 | tf_op jit(solution)/shard_map/ppermute | solution.py:23
  156.6 1.4 collective-permute-done.34
  158.0 1.0 copy-done.10
  (64 shorter events, 3.5 us)
Async XLA Ops:
  2.5 18.7 %collective-permute-start.1 = (bf16[64,5120]{1,0:T(8,128)(2,1)}, bf16[64,5120]{1,0:T(8,128)(2,1)S(1)}, u32[]{:S(2)}, u32[]{:S(2)}) collective-permute-start(bf16[64,5120]{1,0:T(8,128)(2,1)} %get-tuple-element.104), channel_id=1, source_target_pairs={{0,1},{1,0},{2,3},{3,2},{4,5},{5,4},{6,7},{7,6},{8,9},{9,8},{10,11... | collective-permute-start | bytes 1966088 | tf_op jit(solution)/shard_map/ppermute | solution.py:28
  5.4 19.8 %collective-permute-start.4 = (bf16[64,5120]{1,0:T(8,128)(2,1)}, bf16[64,5120]{1,0:T(8,128)(2,1)S(1)}, u32[]{:S(2)}, u32[]{:S(2)}) collective-permute-start(bf16[64,5120]{1,0:T(8,128)(2,1)} %get-tuple-element.103), channel_id=1, source_target_pairs={{0,4},{2,6},{4,0},{6,2},{1,5},{3,7},{5,1},{7,3},{8,12},{10,14},{12... | collective-permute-start | bytes 1966088 | tf_op jit(solution)/shard_map/ppermute | solution.py:28
  6.9 35.1 %collective-permute-start.2 = (bf16[64,5120]{1,0:T(8,128)(2,1)}, bf16[64,5120]{1,0:T(8,128)(2,1)}, u32[]{:S(2)}, u32[]{:S(2)}) collective-permute-start(bf16[64,5120]{1,0:T(8,128)(2,1)} %get-tuple-element.103), channel_id=1, source_target_pairs={{0,1},{1,0},{2,3},{3,2},{4,5},{5,4},{6,7},{7,6},{8,9},{9,8},{10,11... | collective-permute-start | bytes 1966088 | tf_op jit(solution)/shard_map/ppermute | solution.py:28
  7.5 34.6 %collective-permute-start.3 = (bf16[64,5120]{1,0:T(8,128)(2,1)}, bf16[64,5120]{1,0:T(8,128)(2,1)S(1)}, u32[]{:S(2)}, u32[]{:S(2)}) collective-permute-start(bf16[64,5120]{1,0:T(8,128)(2,1)} %get-tuple-element.104), channel_id=1, source_target_pairs={{0,4},{2,6},{4,0},{6,2},{1,5},{3,7},{5,1},{7,3},{8,12},{10,14},{12... | collective-permute-start | bytes 1966088 | tf_op jit(solution)/shard_map/ppermute | solution.py:28
  21.2 1.9 %copy-start.2 = (bf16[256,2,8,384]{3,2,1,0:T(8,128)(2,1)S(1)}, bf16[256,2,8,384]{3,2,1,0:T(8,128)(2,1)}, u32[]{:S(2)}) copy-start(bf16[256,2,8,384]{3,2,1,0:T(8,128)(2,1)} %reshape_squeeze.3.refs_0_) | copy-start | bytes 9437188
  23.1 2.1 %copy-start.3 = (bf16[256,2,8,384]{3,2,1,0:T(8,128)(2,1)S(1)}, bf16[256,2,8,384]{3,2,1,0:T(8,128)(2,1)}, u32[]{:S(2)}) copy-start(bf16[256,2,8,384]{3,2,1,0:T(8,128)(2,1)} %reshape_squeeze.3.refs_0_) | copy-start | bytes 9437188
  23.1 4.0 %copy-start.9 = (f32[1,1,3,5120]{3,1,2,0:T(1,128)S(1)}, f32[1,1,3,5120]{3,1,2,0:T(1,128)}, u32[]{:S(2)}) copy-start(f32[1,1,3,5120]{3,1,2,0:T(1,128)} %param.7) | copy-start | bytes 184324
  23.1 4.2 %copy-start = (bf16[1,1,128,5120]{3,2,1,0:T(8,128)(2,1)S(1)}, bf16[1,1,128,5120]{3,2,1,0:T(8,128)(2,1)}, u32[]{:S(2)}) copy-start(bf16[1,1,128,5120]{3,2,1,0:T(8,128)(2,1)} %param.6) | copy-start | bytes 3932164
  23.1 32.1 %collective-permute-start.5 = (bf16[64,5120]{1,0:T(8,128)(2,1)S(1)}, bf16[64,5120]{1,0:T(8,128)(2,1)}, u32[]{:S(2)}, u32[]{:S(2)}) collective-permute-start(bf16[64,5120]{1,0:T(8,128)(2,1)S(1)} %after.3.refs_0_), channel_id=1, source_target_pairs={{0,4},{2,6},{4,0},{6,2},{1,5},{3,7},{5,1},{7,3},{8,12},{10,14},{12... | collective-permute-start | bytes 1966088 | tf_op jit(solution)/shard_map/ppermute | solution.py:28
  25.2 30.4 %collective-permute-start.6 = (bf16[64,5120]{1,0:T(8,128)(2,1)S(1)}, bf16[64,5120]{1,0:T(8,128)(2,1)}, u32[]{:S(2)}, u32[]{:S(2)}) collective-permute-start(bf16[64,5120]{1,0:T(8,128)(2,1)S(1)} %after.4.refs_1_), channel_id=1, source_target_pairs={{0,1},{1,0},{2,3},{3,2},{4,5},{5,4},{6,7},{7,6},{8,9},{9,8},{10,11... | collective-permute-start | bytes 1966088 | tf_op jit(solution)/shard_map/ppermute | solution.py:28
  27.0 23.7 %collective-permute-start = (f32[1,1,3,5120]{3,2,1,0:T(4,128)S(1)}, f32[1,1,3,5120]{3,2,1,0:T(4,128)S(1)}, u32[]{:S(2)}, u32[]{:S(2)}) collective-permute-start(f32[1,1,3,5120]{3,2,1,0:T(4,128)S(1)} %copy.15), channel_id=1, source_target_pairs={{0,1},{1,0},{2,3},{3,2},{4,5},{5,4},{6,7},{7,6},{8,9},{9,8},{10,11... | collective-permute-start | bytes 184328 | tf_op jit(solution)/shard_map/ppermute | solution.py:28
  28.8 1.1 copy-start.6
  42.0 16.7 %collective-permute-start.7 = (bf16[128,5120]{1,0:T(8,128)(2,1)}, bf16[128,5120]{1,0:T(8,128)(2,1)}, u32[]{:S(2)}, u32[]{:S(2)}) collective-permute-start(bf16[128,5120]{1,0:T(8,128)(2,1)} %copy-done.6), channel_id=1, source_target_pairs={{0,2},{2,0},{4,6},{6,4},{1,3},{3,1},{5,7},{7,5},{8,10},{10,8},{12,... | collective-permute-start | bytes 3932168 | tf_op jit(solution)/shard_map/ppermute | solution.py:28
  42.0 50.9 %collective-permute-start.11 = (bf16[384,5120]{1,0:T(8,128)(2,1)}, bf16[384,5120]{1,0:T(8,128)(2,1)}, u32[]{:S(2)}, u32[]{:S(2)}) collective-permute-start(bf16[384,5120]{1,0:T(8,128)(2,1)} %bitcast.30), channel_id=1, source_target_pairs={{0,2},{2,0},{4,6},{6,4},{1,3},{3,1},{5,7},{7,5},{8,10},{10,8},{12,... | collective-permute-start | bytes 11796488 | tf_op jit(solution)/shard_map/ppermute | solution.py:28
  42.5 1.9 %copy-start.4 = (bf16[8,256,768]{2,1,0:T(8,128)(2,1)S(1)}, bf16[8,256,768]{2,1,0:T(8,128)(2,1)}, u32[]{:S(2)}) copy-start(bf16[8,256,768]{2,1,0:T(8,128)(2,1)} %reshape.10.value_ref) | copy-start | bytes 9437188
  44.4 1.7 %copy-start.5 = (bf16[8,256,768]{2,1,0:T(8,128)(2,1)}, bf16[8,256,768]{2,1,0:T(8,128)(2,1)S(1)}, u32[]{:S(2)}) copy-start(bf16[8,256,768]{2,1,0:T(8,128)(2,1)S(1)} %after.5) | copy-start | bytes 9437188
  46.1 41.8 %all-to-all-start = ((bf16[8,256,768]{2,1,0:T(8,128)(2,1)}), bf16[8,256,768]{2,1,0:T(8,128)(2,1)}, u32[]{:S(2)}, u32[]{:S(2)}) async-start(bf16[8,256,768]{2,1,0:T(8,128)(2,1)} %copy-done.5), calls=%async_computation | async-start | bytes 6291456 | tf_op jit(solution)/shard_map/all_to_all | solution.py:438
  53.3 5.4 %collective-permute-start.8 = (bf16[128,5120]{1,0:T(8,128)(2,1)S(1)}, bf16[128,5120]{1,0:T(8,128)(2,1)S(1)}, u32[]{:S(2)}, u32[]{:S(2)}) collective-permute-start(bf16[128,5120]{1,0:T(8,128)(2,1)S(1)} %modulated_norm.5.refs_1_), channel_id=1, source_target_pairs={{0,2},{2,0},{4,6},{6,4},{1,3},{3,1},{5,7},{7,5},{8,10},{10,8},{12,... | collective-permute-start | bytes 3932168 | tf_op jit(solution)/shard_map/ppermute | solution.py:28
  55.1 6.3 %copy-start.7 = (bf16[128,5120]{1,0:T(8,128)(2,1)S(1)}, bf16[128,5120]{1,0:T(8,128)(2,1)}, u32[]{:S(2)}) copy-start(bf16[128,5120]{1,0:T(8,128)(2,1)} %copy-done.6) | copy-start | bytes 3932164
  55.1 3.6 %collective-permute-start.9 = (bf16[128,5120]{1,0:T(8,128)(2,1)S(1)}, bf16[128,5120]{1,0:T(8,128)(2,1)S(1)}, u32[]{:S(2)}, u32[]{:S(2)}) collective-permute-start(bf16[128,5120]{1,0:T(8,128)(2,1)S(1)} %modulated_norm.6.refs_2_), channel_id=1, source_target_pairs={{0,2},{2,0},{4,6},{6,4},{1,3},{3,1},{5,7},{7,5},{8,10},{10,8},{12,... | collective-permute-start | bytes 3932168 | tf_op jit(solution)/shard_map/ppermute | solution.py:28
  58.3 3.1 %collective-permute-start.10 = (bf16[128,5120]{1,0:T(8,128)(2,1)S(1)}, bf16[128,5120]{1,0:T(8,128)(2,1)S(1)}, u32[]{:S(2)}, u32[]{:S(2)}) collective-permute-start(bf16[128,5120]{1,0:T(8,128)(2,1)S(1)} %modulated_norm.7.refs_3_), channel_id=1, source_target_pairs={{0,2},{2,0},{4,6},{6,4},{1,3},{3,1},{5,7},{7,5},{8,10},{10,8},{12,... | collective-permute-start | bytes 3932168 | tf_op jit(solution)/shard_map/ppermute | solution.py:28
  61.4 26.5 %copy-start.8 = (s32[1,4,6]{2,1,0:T(4,128)S(1)}, s32[1,4,6]{2,1,0:T(4,128)}, u32[]{:S(2)}) copy-start(s32[1,4,6]{2,1,0:T(4,128)} %param.11) | copy-start | bytes 292
  87.9 5.0 %copy-start.1 = (bf16[1,384,5120]{2,1,0:T(8,128)(2,1)S(1)}, bf16[1,384,5120]{2,1,0:T(8,128)(2,1)}, u32[]{:S(2)}) copy-start(bf16[1,384,5120]{2,1,0:T(8,128)(2,1)} %param.9) | copy-start | bytes 11796484
  92.8 4.0 %collective-permute-start.12 = (bf16[512,384]{1,0:T(8,128)(2,1)S(1)}, bf16[512,384]{1,0:T(8,128)(2,1)S(1)}, u32[]{:S(2)}, u32[]{:S(2)}) collective-permute-start(bf16[512,384]{1,0:T(8,128)(2,1)S(1)} %get-tuple-element.56.refs_2_), channel_id=1, source_target_pairs={{0,2},{2,0},{4,6},{6,4},{1,3},{3,1},{5,7},{7,5},{8,10},{10,8},{12,... | collective-permute-start | bytes 1179656 | tf_op jit(solution)/shard_map/ppermute | solution.py:28
  98.2 10.6 %collective-permute-start.13 = (bf16[128,1280]{1,0:T(8,128)(2,1)S(1)}, bf16[128,1280]{1,0:T(8,128)(2,1)S(1)}, u32[]{:S(2)}, u32[]{:S(2)}) collective-permute-start(bf16[128,1280]{1,0:T(8,128)(2,1)S(1)} %get-tuple-element.59), channel_id=1, source_target_pairs={{0,1},{1,0},{2,3},{3,2},{4,5},{5,4},{6,7},{7,6},{8,9},{9,8},{10,11... | collective-permute-start | bytes 983048 | tf_op jit(solution)/shard_map/ppermute | solution.py:28
  99.3 10.5 %collective-permute-start.14 = (bf16[128,1280]{1,0:T(8,128)(2,1)S(1)}, bf16[128,1280]{1,0:T(8,128)(2,1)S(1)}, u32[]{:S(2)}, u32[]{:S(2)}) collective-permute-start(bf16[128,1280]{1,0:T(8,128)(2,1)S(1)} %get-tuple-element.60), channel_id=1, source_target_pairs={{0,4},{2,6},{4,0},{6,2},{1,5},{3,7},{5,1},{7,3},{8,12},{10,14},{12... | collective-permute-start | bytes 983048 | tf_op jit(solution)/shard_map/ppermute | solution.py:28
  102.5 13.2 %collective-permute-start.17 = (bf16[128,1280]{1,0:T(8,128)(2,1)S(1)}, bf16[128,1280]{1,0:T(8,128)(2,1)S(1)}, u32[]{:S(2)}, u32[]{:S(2)}) collective-permute-start(bf16[128,1280]{1,0:T(8,128)(2,1)S(1)} %get-tuple-element.70), channel_id=1, source_target_pairs={{0,1},{1,0},{2,3},{3,2},{4,5},{5,4},{6,7},{7,6},{8,9},{9,8},{10,11... | collective-permute-start | bytes 983048 | tf_op jit(solution)/shard_map/ppermute | solution.py:28
  103.9 12.9 %collective-permute-start.18 = (bf16[128,1280]{1,0:T(8,128)(2,1)S(1)}, bf16[128,1280]{1,0:T(8,128)(2,1)S(1)}, u32[]{:S(2)}, u32[]{:S(2)}) collective-permute-start(bf16[128,1280]{1,0:T(8,128)(2,1)S(1)} %get-tuple-element.71), channel_id=1, source_target_pairs={{0,4},{2,6},{4,0},{6,2},{1,5},{3,7},{5,1},{7,3},{8,12},{10,14},{12... | collective-permute-start | bytes 983048 | tf_op jit(solution)/shard_map/ppermute | solution.py:28
  111.7 10.4 %collective-permute-start.15 = (bf16[128,1152]{1,0:T(8,128)(2,1)S(1)}, bf16[128,1152]{1,0:T(8,128)(2,1)S(1)}, u32[]{:S(2)}, u32[]{:S(2)}) collective-permute-start(bf16[128,1152]{1,0:T(8,128)(2,1)S(1)} %get-tuple-element.64), channel_id=1, source_target_pairs={{0,1},{1,0},{2,3},{3,2},{4,5},{5,4},{6,7},{7,6},{8,9},{9,8},{10,11... | collective-permute-start | bytes 884744 | tf_op jit(solution)/shard_map/ppermute | solution.py:28
  112.7 10.4 %collective-permute-start.16 = (bf16[128,1152]{1,0:T(8,128)(2,1)S(1)}, bf16[128,1152]{1,0:T(8,128)(2,1)S(1)}, u32[]{:S(2)}, u32[]{:S(2)}) collective-permute-start(bf16[128,1152]{1,0:T(8,128)(2,1)S(1)} %get-tuple-element.65), channel_id=1, source_target_pairs={{0,4},{2,6},{4,0},{6,2},{1,5},{3,7},{5,1},{7,3},{8,12},{10,14},{12... | collective-permute-start | bytes 884744 | tf_op jit(solution)/shard_map/ppermute | solution.py:28
  119.2 11.1 %collective-permute-start.20 = (bf16[128,1408]{1,0:T(8,128)(2,1)S(1)}, bf16[128,1408]{1,0:T(8,128)(2,1)S(1)}, u32[]{:S(2)}, u32[]{:S(2)}) collective-permute-start(bf16[128,1408]{1,0:T(8,128)(2,1)S(1)} %get-tuple-element.75), channel_id=1, source_target_pairs={{0,1},{1,0},{2,3},{3,2},{4,5},{5,4},{6,7},{7,6},{8,9},{9,8},{10,11... | collective-permute-start | bytes 1081352 | tf_op jit(solution)/shard_map/ppermute | solution.py:28
  120.3 10.9 %collective-permute-start.21 = (bf16[128,1408]{1,0:T(8,128)(2,1)S(1)}, bf16[128,1408]{1,0:T(8,128)(2,1)S(1)}, u32[]{:S(2)}, u32[]{:S(2)}) collective-permute-start(bf16[128,1408]{1,0:T(8,128)(2,1)S(1)} %get-tuple-element.76), channel_id=1, source_target_pairs={{0,4},{2,6},{4,0},{6,2},{1,5},{3,7},{5,1},{7,3},{8,12},{10,14},{12... | collective-permute-start | bytes 1081352 | tf_op jit(solution)/shard_map/ppermute | solution.py:28
  125.4 11.4 %collective-permute-start.19 = (bf16[128,1280]{1,0:T(8,128)(2,1)S(1)}, bf16[128,1280]{1,0:T(8,128)(2,1)S(1)}, u32[]{:S(2)}, u32[]{:S(2)}) collective-permute-start(bf16[128,1280]{1,0:T(8,128)(2,1)S(1)} %get-tuple-element.74.refs_12_), channel_id=1, source_target_pairs={{0,8},{8,16},{16,24},{24,0},{1,9},{9,17},{17,25},{25,1},{2,10},{10... | collective-permute-start | bytes 983048 | tf_op jit(solution)/shard_map/ppermute | solution.py:23
  127.4 8.8 %collective-permute-start.23 = (bf16[128,1024]{1,0:T(8,128)(2,1)S(1)}, bf16[128,1024]{1,0:T(8,128)(2,1)S(1)}, u32[]{:S(2)}, u32[]{:S(2)}) collective-permute-start(bf16[128,1024]{1,0:T(8,128)(2,1)S(1)} %get-tuple-element.81), channel_id=1, source_target_pairs={{0,1},{1,0},{2,3},{3,2},{4,5},{5,4},{6,7},{7,6},{8,9},{9,8},{10,11... | collective-permute-start | bytes 786440 | tf_op jit(solution)/shard_map/ppermute | solution.py:28
  128.5 8.4 %collective-permute-start.24 = (bf16[128,1024]{1,0:T(8,128)(2,1)S(1)}, bf16[128,1024]{1,0:T(8,128)(2,1)S(1)}, u32[]{:S(2)}, u32[]{:S(2)}) collective-permute-start(bf16[128,1024]{1,0:T(8,128)(2,1)S(1)} %get-tuple-element.82), channel_id=1, source_target_pairs={{0,4},{2,6},{4,0},{6,2},{1,5},{3,7},{5,1},{7,3},{8,12},{10,14},{12... | collective-permute-start | bytes 786440 | tf_op jit(solution)/shard_map/ppermute | solution.py:28
  133.0 10.3 %collective-permute-start.22 = (bf16[128,1280]{1,0:T(8,128)(2,1)S(1)}, bf16[128,1280]{1,0:T(8,128)(2,1)S(1)}, u32[]{:S(2)}, u32[]{:S(2)}) collective-permute-start(bf16[128,1280]{1,0:T(8,128)(2,1)S(1)} %get-tuple-element.80.refs_8_), channel_id=1, source_target_pairs={{0,8},{8,16},{16,24},{24,0},{1,9},{9,17},{17,25},{25,1},{2,10},{10... | collective-permute-start | bytes 983048 | tf_op jit(solution)/shard_map/ppermute | solution.py:23
  135.3 6.0 %collective-permute-start.26 = (bf16[128,896]{1,0:T(8,128)(2,1)S(1)}, bf16[128,896]{1,0:T(8,128)(2,1)S(1)}, u32[]{:S(2)}, u32[]{:S(2)}) collective-permute-start(bf16[128,896]{1,0:T(8,128)(2,1)S(1)} %get-tuple-element.88), channel_id=1, source_target_pairs={{0,1},{1,0},{2,3},{3,2},{4,5},{5,4},{6,7},{7,6},{8,9},{9,8},{10,11... | collective-permute-start | bytes 688136 | tf_op jit(solution)/shard_map/ppermute | solution.py:28
  136.3 6.7 %collective-permute-start.27 = (bf16[128,896]{1,0:T(8,128)(2,1)S(1)}, bf16[128,896]{1,0:T(8,128)(2,1)S(1)}, u32[]{:S(2)}, u32[]{:S(2)}) collective-permute-start(bf16[128,896]{1,0:T(8,128)(2,1)S(1)} %get-tuple-element.89), channel_id=1, source_target_pairs={{0,4},{2,6},{4,0},{6,2},{1,5},{3,7},{5,1},{7,3},{8,12},{10,14},{12... | collective-permute-start | bytes 688136 | tf_op jit(solution)/shard_map/ppermute | solution.py:28
  137.0 8.1 %collective-permute-start.29 = (bf16[128,384]{1,0:T(8,128)(2,1)S(1)}, bf16[128,384]{1,0:T(8,128)(2,1)S(1)}, u32[]{:S(2)}, u32[]{:S(2)}) collective-permute-start(bf16[128,384]{1,0:T(8,128)(2,1)S(1)} %get-tuple-element.95), channel_id=1, source_target_pairs={{0,1},{1,0},{2,3},{3,2},{4,5},{5,4},{6,7},{7,6},{8,9},{9,8},{10,11... | collective-permute-start | bytes 294920 | tf_op jit(solution)/shard_map/ppermute | solution.py:28
  138.4 8.4 %collective-permute-start.30 = (bf16[128,384]{1,0:T(8,128)(2,1)S(1)}, bf16[128,384]{1,0:T(8,128)(2,1)S(1)}, u32[]{:S(2)}, u32[]{:S(2)}) collective-permute-start(bf16[128,384]{1,0:T(8,128)(2,1)S(1)} %get-tuple-element.96), channel_id=1, source_target_pairs={{0,4},{2,6},{4,0},{6,2},{1,5},{3,7},{5,1},{7,3},{8,12},{10,14},{12... | collective-permute-start | bytes 294920 | tf_op jit(solution)/shard_map/ppermute | solution.py:28
  141.3 7.7 %collective-permute-start.25 = (bf16[128,512]{1,0:T(8,128)(2,1)S(1)}, bf16[128,512]{1,0:T(8,128)(2,1)S(1)}, u32[]{:S(2)}, u32[]{:S(2)}) collective-permute-start(bf16[128,512]{1,0:T(8,128)(2,1)S(1)} %get-tuple-element.87.refs_8_), channel_id=1, source_target_pairs={{0,8},{8,16},{16,24},{24,0},{1,9},{9,17},{17,25},{25,1},{2,10},{10... | collective-permute-start | bytes 393224 | tf_op jit(solution)/shard_map/ppermute | solution.py:23
  143.4 5.9 %collective-permute-start.32 = (bf16[128,256]{1,0:T(8,128)(2,1)S(1)}, bf16[128,256]{1,0:T(8,128)(2,1)S(1)}, u32[]{:S(2)}, u32[]{:S(2)}) collective-permute-start(bf16[128,256]{1,0:T(8,128)(2,1)S(1)} %get-tuple-element.99), channel_id=1, source_target_pairs={{0,1},{1,0},{2,3},{3,2},{4,5},{5,4},{6,7},{7,6},{8,9},{9,8},{10,11... | collective-permute-start | bytes 196616 | tf_op jit(solution)/shard_map/ppermute | solution.py:28
  144.4 4.9 %collective-permute-start.33 = (bf16[128,256]{1,0:T(8,128)(2,1)S(1)}, bf16[128,256]{1,0:T(8,128)(2,1)S(1)}, u32[]{:S(2)}, u32[]{:S(2)}) collective-permute-start(bf16[128,256]{1,0:T(8,128)(2,1)S(1)} %get-tuple-element.100), channel_id=1, source_target_pairs={{0,4},{2,6},{4,0},{6,2},{1,5},{3,7},{5,1},{7,3},{8,12},{10,14},{12... | collective-permute-start | bytes 196616 | tf_op jit(solution)/shard_map/ppermute | solution.py:28
  145.1 9.4 %collective-permute-start.28 = (bf16[128,768]{1,0:T(8,128)(2,1)S(1)}, bf16[128,768]{1,0:T(8,128)(2,1)S(1)}, u32[]{:S(2)}, u32[]{:S(2)}) collective-permute-start(bf16[128,768]{1,0:T(8,128)(2,1)S(1)} %get-tuple-element.94.refs_6_), channel_id=1, source_target_pairs={{0,8},{8,16},{16,24},{24,0},{1,9},{9,17},{17,25},{25,1},{2,10},{10... | collective-permute-start | bytes 589832 | tf_op jit(solution)/shard_map/ppermute | solution.py:23
  149.0 7.6 %collective-permute-start.31 = (bf16[128,768]{1,0:T(8,128)(2,1)S(1)}, bf16[128,768]{1,0:T(8,128)(2,1)S(1)}, u32[]{:S(2)}, u32[]{:S(2)}) collective-permute-start(bf16[128,768]{1,0:T(8,128)(2,1)S(1)} %sum_stage.18.refs_6_), channel_id=1, source_target_pairs={{0,8},{8,16},{16,24},{24,0},{1,9},{9,17},{17,25},{25,1},{2,10},{10... | collective-permute-start | bytes 589832 | tf_op jit(solution)/shard_map/ppermute | solution.py:23
  149.3 8.7 %collective-permute-start.34 = (bf16[128,512]{1,0:T(8,128)(2,1)S(1)}, bf16[128,512]{1,0:T(8,128)(2,1)S(1)}, u32[]{:S(2)}, u32[]{:S(2)}) collective-permute-start(bf16[128,512]{1,0:T(8,128)(2,1)S(1)} %sum_stage.19), channel_id=1, source_target_pairs={{0,8},{8,16},{16,24},{24,0},{1,9},{9,17},{17,25},{25,1},{2,10},{10... | collective-permute-start | bytes 393224 | tf_op jit(solution)/shard_map/ppermute | solution.py:23
  158.0 1.1 copy-start.10

commit v15 on v14

--- a/solution.py
+++ b/solution.py
@@ -66,7 +66,7 @@
     pass
 
 
-def after(value, earlier):
+def after(value, earlier, limit=1):
     return pl.pallas_call(
         gate_kernel,
         in_specs=[pl.BlockSpec(memory_space=pl.ANY)] * (1 + len(earlier)),
@@ -75,7 +75,7 @@
         input_output_aliases={0: 0},
         name="after",
         cost_estimate=SHORT,
-        compiler_params=pltpu.CompilerParams(vmem_limit_bytes=MIB),
+        compiler_params=pltpu.CompilerParams(vmem_limit_bytes=limit * MIB),
     )(value, *earlier)
 
 
@@ -149,7 +149,6 @@
     tiles_fresh = visible_ref.shape[0]
     mine_high, mine_low = lax.axis_index("sp") // 2, lax.axis_index("sp") % 2
     mine_branch = lax.axis_index("cfg")
-    ones = jnp.ones((tiles_seen * TILE, HD), jnp.bfloat16)
 
     def body(step, carry):
         index = first_block + step
@@ -167,18 +166,24 @@
             start = jnp.where(number < tiles_fresh, fresh, stale)
             places.append(pl.ds(pl.multiple_of(start, TILE), TILE))
 
-        keys = jnp.concatenate([pool_ref[head, place, :] for place in places], axis=0)
-        values = jnp.concatenate([pool_ref[heads + head, place, :] for place in places], axis=0)
-        scores = lax.dot_general(
-            queries_ref[head, rows, :],
-            keys,
-            (((1,), (1,)), ((), ())),
-            preferred_element_type=jnp.float32,
-        )
-        exponent = jnp.exp2(scores * (HD ** (-0.5) * LOG2E)).astype(jnp.bfloat16)
-        mixed = jnp.dot(
-            exponent, jnp.concatenate([values, ones], axis=1), preferred_element_type=jnp.float32
-        )
+        mixed = 0.0
+        for pair in range(0, tiles_seen, 2):
+            pair = places[pair : pair + 2]
+            keys = jnp.concatenate([pool_ref[head, place, :] for place in pair], axis=0)
+            values = jnp.concatenate([pool_ref[heads + head, place, :] for place in pair], axis=0)
+            scores = lax.dot_general(
+                queries_ref[head, rows, :],
+                keys,
+                (((1,), (1,)), ((), ())),
+                preferred_element_type=jnp.float32,
+            )
+            exponent = jnp.exp2(scores * (HD ** (-0.5) * LOG2E)).astype(jnp.bfloat16)
+            ones = jnp.ones(values.shape, jnp.bfloat16)
+            mixed += jnp.dot(
+                exponent,
+                jnp.concatenate([values, ones], axis=1),
+                preferred_element_type=jnp.float32,
+            )
         out_ref[out_rows, head * HD : (head + 1) * HD] = (mixed[:, :HD] / mixed[:, HD:]).astype(
             jnp.bfloat16
         )
@@ -434,7 +439,7 @@
     ]
     far = [from_partner(rows, "sp", 1) for rows in near]
 
-    packed = after(packed, (across_lower, along_upper))
+    packed = after(packed, (across_lower, along_upper), limit=60)
     context = lax.all_to_all(packed, ("sp", "cfg"), split_axis=0, concat_axis=0, tiled=True)
     context = context.reshape(devices * context_rows, 2 * width)
 

time: 160 us -> 158 us (0.988)
  waiting for transfers between devices: 38.3 us -> 41.9 us
  local copies, waits for them, and re-layouts: 30.3 us -> 27.1 us
  starting transfers between devices: 41.1 us -> 38.3 us
    ppermute x29, waiting for transfers between devices: 21.9 us -> 26.9 us  [from_partner(): return lax.ppermute(value, axis, pairs)]
    unnamed x28, local copies, waits for them, and re-layouts: 7.69 us -> 4.47 us
    all_to_all x1, waiting for transfers between devices: 7.27 us -> 5.12 us  [per_device(): lax.all_to_all(packed, ('sp', 'cfg'), split_axis=0, concat_axis=0, tiled=...]
    ppermute x6, starting transfers between devices: 9.82 us -> 7.84 us  [from_behind(): return lax.ppermute(x, axis, [(i, (i + by) % count) for i in range(count)])]
  transfers between devices with their start and end apart: 36 -> 36, of which waited for: 17 -> 19; matrix products, arithmetic and copies ran while one was open for 13% -> 13% of each run, Pallas kernels for 30% -> 30%
where the time goes in v15:
time: 158 us; the launch traced here: 157 us
  Pallas kernels  49.3 us (31%)
  waiting for transfers between devices  41.9 us (27%)
  starting transfers between devices  38.3 us (24%)
  local copies, waits for them, and re-layouts  27.1 us (17%)
    ppermute x29, waiting for transfers between devices, from_partner(): return lax.ppermute(value, axis, pairs)  26.9 us
    ppermute x29, starting transfers between devices, from_partner(): return lax.ppermute(value, axis, pairs)  25.9 us
    pallas_call x1, Pallas kernels, project(): pl.pallas_call(functools.partial(project_kernel, blocks=len(blocks)), gri...  19.2 us
    pallas_call x10, Pallas kernels, stage(): pl.pallas_call(functools.partial(stage_kernel, parts=parts, start=start,...  12.7 us
    ppermute x6, waiting for transfers between devices, from_behind(): return lax.ppermute(x, axis, [(i, (i + by) % count) for i in range(count)])  9.81 us
    pallas_call x4, Pallas kernels, modulated_norm(): pl.pallas_call(norm_kernel, in_specs=[pl.BlockSpec(memory_space=pltpu.VME...  8.49 us
    reshape x1, local copies, waits for them, and re-layouts, per_device(): unpacked.transpose(2, 0, 1, 3).reshape(devices, context_rows, 2 * width)  8.06 us
    another operation x1, local copies, waits for them, and re-layouts, per_device(): unpacked = stale_cache[0, 0].reshape(context_rows, 2, devices, width)  8 us
  transfers between devices with their start and end apart: 36, of which 19 were waited for; matrix products, arithmetic and copies ran while one was open for 13% of the time, Pallas kernels for 30%

profile of v15, /device:TPU:0, one launch (start us, length us, event | category | flops | bytes accessed | tf_op | source)
XLA Modules:
  0.0 157.0 jit_solution(5339642217563251872)
XLA Ops:
  0.0 2.5 %slice_bitcast_fusion = (bf16[64,5120]{1,0:T(8,128)(2,1)}, bf16[64,5120]{1,0:T(8,128)(2,1)}) fusion(bf16[1,1,128,5120]{3,2,1,0:T(8,128)(2,1)} %param.6), kind=kLoop, calls=%fused_computation | loop fusion | bytes 2621440 | tf_op jit(solution)/shard_map/slice | solution.py:427
  2.5 2.9 %collective-permute-start.1 = (bf16[64,5120]{1,0:T(8,128)(2,1)}, bf16[64,5120]{1,0:T(8,128)(2,1)S(1)}, u32[]{:S(2)}, u32[]{:S(2)}) collective-permute-start(bf16[64,5120]{1,0:T(8,128)(2,1)} %get-tuple-element.104), channel_id=1, source_target_pairs={{0,1},{1,0},{2,3},{3,2},{4,5},{5,4},{6,7},{7,6},{8,9},{9,8},{10,11... | collective-permute-start | bytes 1966088 | tf_op jit(solution)/shard_map/ppermute | solution.py:28
  5.4 1.5 collective-permute-start.4
  6.9 0.5 collective-permute-start.2
  7.5 8.0 %reshape_squeeze.3.refs_0_ = bf16[256,2,8,384]{3,2,1,0:T(8,128)(2,1)} reshape(bf16[1,1,256,2,3072]{4,3,2,1,0:T(2,128)(2,1)} %param.10) | data formatting | bytes 6291456 | tf_op jit(solution)/shard_map/reshape;squeeze | solution.py:424
  15.5 5.7 %collective-permute-done.1.value_ref = bf16[64,5120]{1,0:T(8,128)(2,1)S(1)} collective-permute-done((bf16[64,5120]{1,0:T(8,128)(2,1)}, bf16[64,5120]{1,0:T(8,128)(2,1)S(1)}, u32[]{:S(2)}, u32[]{:S(2)}) %collective-permute-start.1) | collective-permute-done | bytes 655392 | tf_op jit(solution)/shard_map/ppermute | solution.py:28
  21.2 1.9 %copy-done.2 = bf16[256,2,8,384]{3,2,1,0:T(8,128)(2,1)S(1)} copy-done((bf16[256,2,8,384]{3,2,1,0:T(8,128)(2,1)S(1)}, bf16[256,2,8,384]{3,2,1,0:T(8,128)(2,1)}, u32[]{:S(2)}) %copy-start.2) | copy-done | bytes 3145752
  23.1 2.1 %collective-permute-start.5 = (bf16[64,5120]{1,0:T(8,128)(2,1)S(1)}, bf16[64,5120]{1,0:T(8,128)(2,1)}, u32[]{:S(2)}, u32[]{:S(2)}) collective-permute-start(bf16[64,5120]{1,0:T(8,128)(2,1)S(1)} %after.3.refs_0_), channel_id=1, source_target_pairs={{0,4},{2,6},{4,0},{6,2},{1,5},{3,7},{5,1},{7,3},{8,12},{10,14},{12... | collective-permute-start | bytes 1966088 | tf_op jit(solution)/shard_map/ppermute | solution.py:28
  25.2 1.8 %collective-permute-start.6 = (bf16[64,5120]{1,0:T(8,128)(2,1)S(1)}, bf16[64,5120]{1,0:T(8,128)(2,1)}, u32[]{:S(2)}, u32[]{:S(2)}) collective-permute-start(bf16[64,5120]{1,0:T(8,128)(2,1)S(1)} %after.4.refs_1_), channel_id=1, source_target_pairs={{0,1},{1,0},{2,3},{3,2},{4,5},{5,4},{6,7},{7,6},{8,9},{9,8},{10,11... | collective-permute-start | bytes 1966088 | tf_op jit(solution)/shard_map/ppermute | solution.py:28
  27.3 1.5 modulated_norm.4.refs_0_
  28.8 1.0 copy-done.6
  29.9 4.1 %copy.11 = bf16[8,256,2,384]{3,2,1,0:T(2,128)(2,1)} copy(bf16[8,256,2,384]{3,0,2,1:T(8,128)(2,1)S(1)} %bitcast.37) | data formatting | bytes 6291456 | tf_op jit(solution)/shard_map/transpose | solution.py:425
  33.9 8.1 %reshape.10.value_ref = bf16[8,256,768]{2,1,0:T(8,128)(2,1)} reshape(bf16[8,256,2,384]{3,2,1,0:T(2,128)(2,1)} %copy.11) | data formatting | bytes 6291456 | tf_op jit(solution)/shard_map/reshape | solution.py:425
  42.0 0.5 collective-permute-start.11
  42.9 4.6 %all-to-all-start = ((bf16[8,256,768]{2,1,0:T(8,128)(2,1)}), bf16[8,256,768]{2,1,0:T(8,128)(2,1)}, u32[]{:S(2)}, u32[]{:S(2)}) async-start(bf16[8,256,768]{2,1,0:T(8,128)(2,1)} %after.5), calls=%async_computation | async-start | bytes 6291456 | tf_op jit(solution)/shard_map/all_to_all | solution.py:443
  47.5 2.9 %collective-permute-done = f32[1,1,3,5120]{3,2,1,0:T(4,128)S(1)} collective-permute-done((f32[1,1,3,5120]{3,2,1,0:T(4,128)S(1)}, f32[1,1,3,5120]{3,2,1,0:T(4,128)S(1)}, u32[]{:S(2)}, u32[]{:S(2)}) %collective-permute-start) | collective-permute-done | bytes 61472 | tf_op jit(solution)/shard_map/ppermute | solution.py:28
  50.4 2.7 %modulated_norm.5.refs_1_ = bf16[128,5120]{1,0:T(8,128)(2,1)S(1)} custom-call(bf16[64,5120]{1,0:T(8,128)(2,1)S(1)} %after.3.refs_0_, bf16[64,5120]{1,0:T(8,128)(2,1)} %collective-permute-done.2.refs_1_.refs_0_, f32[3,5120]{1,0:T(4,128)S(1)} %bitcast.40), custom_call_target="tpu_custom_call" | custom-call | flops 1 | bytes 1 | tf_op jit(solution)/shard_map/modulated_norm/pallas_call | solution.py:55
  53.1 1.5 modulated_norm.6.refs_2_
  54.7 0.6 collective-permute-start.9
  55.2 2.8 %modulated_norm.7.refs_3_ = bf16[128,5120]{1,0:T(8,128)(2,1)S(1)} custom-call(bf16[64,5120]{1,0:T(8,128)(2,1)} %collective-permute-done.5.refs_0_, bf16[64,5120]{1,0:T(8,128)(2,1)} %collective-permute-done.6.refs_1_, f32[3,5120]{1,0:T(4,128)S(1)} %bitcast.41), custom_call_target="tpu_custom_call" | custom-call | flops 1 | bytes 1 | tf_op jit(solution)/shard_map/modulated_norm/pallas_call | solution.py:55
  58.3 2.9 %collective-permute-done.10.refs_7_ = bf16[128,5120]{1,0:T(8,128)(2,1)S(1)} collective-permute-done((bf16[128,5120]{1,0:T(8,128)(2,1)S(1)}, bf16[128,5120]{1,0:T(8,128)(2,1)S(1)}, u32[]{:S(2)}, u32[]{:S(2)}) %collective-permute-start.10) | collective-permute-done | bytes 1310752 | tf_op jit(solution)/shard_map/ppermute | solution.py:28
  61.1 19.2 %project_heads.1.heads_in = bf16[48,1024,128]{2,1,0:T(8,128)(2,1)} custom-call(bf16[128,5120]{1,0:T(8,128)(2,1)S(1)} %copy-done.7, bf16[128,5120]{1,0:T(8,128)(2,1)S(1)} %modulated_norm.5.refs_1_, bf16[128,5120]{1,0:T(8,128)(2,1)S(1)} %modulated_norm.6.refs_2_, bf16[128,5120]{1,0:T(8,128)(2,1)S(1)} %modulated_norm.7.refs_3_, ...), custom_call_target="tpu_custom_call" | custom-call | flops 12079595520 | bytes 22282240 | tf_op jit(solution)/shard_map/project_heads/pallas_call | solution.py:124
  80.3 5.1 %all-to-all-done = bf16[8,256,768]{2,1,0:T(8,128)(2,1)} async-done(((bf16[8,256,768]{2,1,0:T(8,128)(2,1)}), bf16[8,256,768]{2,1,0:T(8,128)(2,1)}, u32[]{:S(2)}, u32[]{:S(2)}) %all-to-all-start) | async-done | bytes 3145760 | tf_op jit(solution)/shard_map/all_to_all | solution.py:443
  85.4 5.0 %attend_first.1 = (bf16[512,384]{1,0:T(8,128)(2,1)S(1)}, bf16[3,1024,128]{2,1,0:T(8,128)(2,1)S(1)}, bf16[6,3072,128]{2,1,0:T(8,128)(2,1)S(1)}) custom-call(s32[4,6]{1,0:T(4,128)S(1)} %bitcast.42, bf16[48,1024,128]{2,1,0:T(8,128)(2,1)} %project_heads.1.heads_in, bf16[2048,768]{1,0:T(8,128)(2,1)} %bitcast.9.context_in), custom_call_target="tpu_custom_call" | custom-call | flops 1 | bytes 1 | tf_op jit(solution)/shard_map/attend_first/pallas_call | solution.py:224
  90.6 3.9 %attend_second.1 = (bf16[512,384]{1,0:T(8,128)(2,1)S(1)}, bf16[768,1280]{1,0:T(8,128)(2,1)S(1)}) custom-call(s32[4,6]{1,0:T(4,128)S(1)} %bitcast.43, bf16[3,1024,128]{2,1,0:T(8,128)(2,1)S(1)} %get-tuple-element.54.queries_ref, bf16[6,3072,128]{2,1,0:T(8,128)(2,1)S(1)} %get-tuple-element.55.pool_ref, bf16[384,5120]{1,0:T(8,128)(2,1)S(1)} %bitcast.31, ...), custom_call_target="tpu_custom_call" | custom-call | flops 1 | bytes 1 | tf_op jit(solution)/shard_map/attend_second/pallas_call | solution.py:264
  94.5 1.4 sum_stage.10
  95.9 0.8 collective-permute-start.13
  96.7 1.2 collective-permute-start.14
  97.9 2.7 %sum_stage.11 = (bf16[128,1280]{1,0:T(8,128)(2,1)S(1)}, bf16[128,1280]{1,0:T(8,128)(2,1)S(1)}, f32[2,128,640]{2,1,0:T(8,128)S(1)}, f32[2,128,640]{2,1,0:T(8,128)S(1)}) custom-call(bf16[128,5120]{1,0:T(8,128)(2,1)S(1)} %bitcast.21, f32[2,5120]{1,0:T(2,128)S(1)} %pad_maximum_fusion.refs_3_.refs_1_, bf16[512,384]{1,0:T(8,128)(2,1)S(1)} %get-tuple-element.57.refs_2_, ...), custom_call_target="tpu_custom_call" | custom-call | flops 1 | bytes 1 | tf_op jit(solution)/shard_map/sum_stage/pallas_call | solution.py:389
  100.6 0.8 collective-permute-start.17
  101.4 1.4 collective-permute-start.18
  102.8 3.7 %collective-permute-done.13.refs_6_ = bf16[128,1280]{1,0:T(8,128)(2,1)S(1)} collective-permute-done((bf16[128,1280]{1,0:T(8,128)(2,1)S(1)}, bf16[128,1280]{1,0:T(8,128)(2,1)S(1)}, u32[]{:S(2)}, u32[]{:S(2)}) %collective-permute-start.13) | collective-permute-done | bytes 327712 | tf_op jit(solution)/shard_map/ppermute | solution.py:28
  106.5 0.8 collective-permute-done.14.refs_7_
  107.3 1.8 %sum_stage.12 = (bf16[128,1152]{1,0:T(8,128)(2,1)S(1)}, bf16[128,1152]{1,0:T(8,128)(2,1)S(1)}, f32[2,128,256]{2,1,0:T(8,128)S(1)}, f32[2,128,256]{2,1,0:T(8,128)...) custom-call(bf16[128,5120]{1,0:T(8,128)(2,1)S(1)} %bitcast.22, f32[2,5120]{1,0:T(2,128)S(1)} %pad_maximum_fusion.refs_3_.refs_1_, ...), custom_call_target="tpu_custom_call" | custom-call | flops 1 | bytes 1 | tf_op jit(solution)/shard_map/sum_stage/pallas_call | solution.py:389
  109.1 1.4 collective-permute-start.15
  110.5 0.6 collective-permute-start.16
  111.1 2.4 %collective-permute-done.17.refs_6_ = bf16[128,1280]{1,0:T(8,128)(2,1)S(1)} collective-permute-done((bf16[128,1280]{1,0:T(8,128)(2,1)S(1)}, bf16[128,1280]{1,0:T(8,128)(2,1)S(1)}, u32[]{:S(2)}, u32[]{:S(2)}) %collective-permute-start.17) | collective-permute-done | bytes 327712 | tf_op jit(solution)/shard_map/ppermute | solution.py:28
  113.5 0.8 collective-permute-done.18.refs_7_
  114.3 2.4 %sum_stage.13 = (bf16[128,1408]{1,0:T(8,128)(2,1)S(1)}, bf16[128,1408]{1,0:T(8,128)(2,1)S(1)}, f32[2,128,384]{2,1,0:T(8,128)S(1)}, f32[2,128,384]{2,1,0:T(8,128)...) custom-call(bf16[128,5120]{1,0:T(8,128)(2,1)S(1)} %bitcast.23, f32[2,5120]{1,0:T(2,128)S(1)} %pad_maximum_fusion.refs_3_.refs_1_, ...), custom_call_target="tpu_custom_call" | custom-call | flops 1 | bytes 1 | tf_op jit(solution)/shard_map/sum_stage/pallas_call | solution.py:389
  116.7 1.4 collective-permute-start.20
  118.0 0.6 collective-permute-start.21
  118.6 1.2 collective-permute-done.15.refs_6_
  119.9 0.8 collective-permute-done.16.refs_7_
  120.6 2.3 %sum_stage.14 = (bf16[128,1024]{1,0:T(8,128)(2,1)S(1)}, bf16[128,1024]{1,0:T(8,128)(2,1)S(1)}, f32[2,128,384]{2,1,0:T(8,128)S(1)}, f32[2,128,384]{2,1,0:T(8,128)...) custom-call(bf16[128,5120]{1,0:T(8,128)(2,1)S(1)} %bitcast.24, ...), custom_call_target="tpu_custom_call" | custom-call | flops 1 | bytes 1 | tf_op jit(solution)/shard_map/sum_stage/pallas_call | solution.py:389
  122.9 1.6 %collective-permute-start.19 = (bf16[128,1280]{1,0:T(8,128)(2,1)S(1)}, bf16[128,1280]{1,0:T(8,128)(2,1)S(1)}, u32[]{:S(2)}, u32[]{:S(2)}) collective-permute-start(bf16[128,1280]{1,0:T(8,128)(2,1)S(1)} %get-tuple-element.74.refs_12_), channel_id=1, source_target_pairs={{0,8},{8,16},{16,24},{24,0},{1,9},{9,17},{17,25},{25,1},{2,10},{10... | collective-permute-start | bytes 983048 | tf_op jit(solution)/shard_map/ppermute | solution.py:23
  124.5 1.1 collective-permute-start.23
  125.8 2.3 %collective-permute-done.20.refs_6_ = bf16[128,1408]{1,0:T(8,128)(2,1)S(1)} collective-permute-done((bf16[128,1408]{1,0:T(8,128)(2,1)S(1)}, bf16[128,1408]{1,0:T(8,128)(2,1)S(1)}, u32[]{:S(2)}, u32[]{:S(2)}) %collective-permute-start.20) | collective-permute-done | bytes 360480 | tf_op jit(solution)/shard_map/ppermute | solution.py:28
  128.1 0.8 collective-permute-done.21.refs_7_
  128.9 1.8 %sum_stage.15 = (bf16[128,896]{1,0:T(8,128)(2,1)S(1)}, bf16[128,896]{1,0:T(8,128)(2,1)S(1)}, f32[2,128,256]{2,1,0:T(8,128)S(1)}, f32[2,128,256]{2,1,0:T(8,128)S(...) custom-call(bf16[128,5120]{1,0:T(8,128)(2,1)S(1)} %bitcast.25, ...), custom_call_target="tpu_custom_call" | custom-call | flops 1 | bytes 1 | tf_op jit(solution)/shard_map/sum_stage/pallas_call | solution.py:389
  130.7 1.6 %collective-permute-start.22 = (bf16[128,1280]{1,0:T(8,128)(2,1)S(1)}, bf16[128,1280]{1,0:T(8,128)(2,1)S(1)}, u32[]{:S(2)}, u32[]{:S(2)}) collective-permute-start(bf16[128,1280]{1,0:T(8,128)(2,1)S(1)} %get-tuple-element.80.refs_8_), channel_id=1, source_target_pairs={{0,8},{8,16},{16,24},{24,0},{1,9},{9,17},{17,25},{25,1},{2,10},{10... | collective-permute-start | bytes 983048 | tf_op jit(solution)/shard_map/ppermute | solution.py:23
  132.3 1.2 collective-permute-start.26
  133.8 1.9 %collective-permute-start.29 = (bf16[128,384]{1,0:T(8,128)(2,1)S(1)}, bf16[128,384]{1,0:T(8,128)(2,1)S(1)}, u32[]{:S(2)}, u32[]{:S(2)}) collective-permute-start(bf16[128,384]{1,0:T(8,128)(2,1)S(1)} %get-tuple-element.95), channel_id=1, source_target_pairs={{0,1},{1,0},{2,3},{3,2},{4,5},{5,4},{6,7},{7,6},{8,9},{9,8},{10,11... | collective-permute-start | bytes 294920 | tf_op jit(solution)/shard_map/ppermute | solution.py:28
  135.6 0.9 collective-permute-start.30
  136.6 2.1 %collective-permute-done.26.refs_2_ = bf16[128,896]{1,0:T(8,128)(2,1)S(1)} collective-permute-done((bf16[128,896]{1,0:T(8,128)(2,1)S(1)}, bf16[128,896]{1,0:T(8,128)(2,1)S(1)}, u32[]{:S(2)}, u32[]{:S(2)}) %collective-permute-start.26) | collective-permute-done | bytes 229408 | tf_op jit(solution)/shard_map/ppermute | solution.py:28
  138.8 1.3 collective-permute-start.25
  140.7 1.4 collective-permute-start.32
  142.1 0.5 collective-permute-start.33
  142.6 2.0 %collective-permute-start.28 = (bf16[128,768]{1,0:T(8,128)(2,1)S(1)}, bf16[128,768]{1,0:T(8,128)(2,1)S(1)}, u32[]{:S(2)}, u32[]{:S(2)}) collective-permute-start(bf16[128,768]{1,0:T(8,128)(2,1)S(1)} %get-tuple-element.94.refs_6_), channel_id=1, source_target_pairs={{0,8},{8,16},{16,24},{24,0},{1,9},{9,17},{17,25},{25,1},{2,10},{10... | collective-permute-start | bytes 589832 | tf_op jit(solution)/shard_map/ppermute | solution.py:23
  144.7 2.2 %collective-permute-done.25.refs_7_ = bf16[128,512]{1,0:T(8,128)(2,1)S(1)} collective-permute-done((bf16[128,512]{1,0:T(8,128)(2,1)S(1)}, bf16[128,512]{1,0:T(8,128)(2,1)S(1)}, u32[]{:S(2)}, u32[]{:S(2)}) %collective-permute-start.25) | collective-permute-done | bytes 131104 | tf_op jit(solution)/shard_map/ppermute | solution.py:23
  147.1 1.2 collective-permute-start.34
  148.3 4.0 %collective-permute-done.28 = bf16[128,768]{1,0:T(8,128)(2,1)S(1)} collective-permute-done((bf16[128,768]{1,0:T(8,128)(2,1)S(1)}, bf16[128,768]{1,0:T(8,128)(2,1)S(1)}, u32[]{:S(2)}, u32[]{:S(2)}) %collective-permute-start.28) | collective-permute-done | bytes 196640 | tf_op jit(solution)/shard_map/ppermute | solution.py:23
  152.2 2.2 %collective-permute-done.31 = bf16[128,768]{1,0:T(8,128)(2,1)S(1)} collective-permute-done((bf16[128,768]{1,0:T(8,128)(2,1)S(1)}, bf16[128,768]{1,0:T(8,128)(2,1)S(1)}, u32[]{:S(2)}, u32[]{:S(2)}) %collective-permute-start.31) | collective-permute-done | bytes 196640 | tf_op jit(solution)/shard_map/ppermute | solution.py:23
  154.5 1.4 collective-permute-done.34
  155.9 1.0 copy-done.10
  (64 shorter events, 2.3 us)
Async XLA Ops:
  2.5 18.7 %collective-permute-start.1 = (bf16[64,5120]{1,0:T(8,128)(2,1)}, bf16[64,5120]{1,0:T(8,128)(2,1)S(1)}, u32[]{:S(2)}, u32[]{:S(2)}) collective-permute-start(bf16[64,5120]{1,0:T(8,128)(2,1)} %get-tuple-element.104), channel_id=1, source_target_pairs={{0,1},{1,0},{2,3},{3,2},{4,5},{5,4},{6,7},{7,6},{8,9},{9,8},{10,11... | collective-permute-start | bytes 1966088 | tf_op jit(solution)/shard_map/ppermute | solution.py:28
  5.4 19.8 %collective-permute-start.4 = (bf16[64,5120]{1,0:T(8,128)(2,1)}, bf16[64,5120]{1,0:T(8,128)(2,1)S(1)}, u32[]{:S(2)}, u32[]{:S(2)}) collective-permute-start(bf16[64,5120]{1,0:T(8,128)(2,1)} %get-tuple-element.103), channel_id=1, source_target_pairs={{0,4},{2,6},{4,0},{6,2},{1,5},{3,7},{5,1},{7,3},{8,12},{10,14},{12... | collective-permute-start | bytes 1966088 | tf_op jit(solution)/shard_map/ppermute | solution.py:28
  6.9 35.1 %collective-permute-start.2 = (bf16[64,5120]{1,0:T(8,128)(2,1)}, bf16[64,5120]{1,0:T(8,128)(2,1)}, u32[]{:S(2)}, u32[]{:S(2)}) collective-permute-start(bf16[64,5120]{1,0:T(8,128)(2,1)} %get-tuple-element.103), channel_id=1, source_target_pairs={{0,1},{1,0},{2,3},{3,2},{4,5},{5,4},{6,7},{7,6},{8,9},{9,8},{10,11... | collective-permute-start | bytes 1966088 | tf_op jit(solution)/shard_map/ppermute | solution.py:28
  7.5 34.5 %collective-permute-start.3 = (bf16[64,5120]{1,0:T(8,128)(2,1)}, bf16[64,5120]{1,0:T(8,128)(2,1)S(1)}, u32[]{:S(2)}, u32[]{:S(2)}) collective-permute-start(bf16[64,5120]{1,0:T(8,128)(2,1)} %get-tuple-element.104), channel_id=1, source_target_pairs={{0,4},{2,6},{4,0},{6,2},{1,5},{3,7},{5,1},{7,3},{8,12},{10,14},{12... | collective-permute-start | bytes 1966088 | tf_op jit(solution)/shard_map/ppermute | solution.py:28
  21.2 1.9 %copy-start.2 = (bf16[256,2,8,384]{3,2,1,0:T(8,128)(2,1)S(1)}, bf16[256,2,8,384]{3,2,1,0:T(8,128)(2,1)}, u32[]{:S(2)}) copy-start(bf16[256,2,8,384]{3,2,1,0:T(8,128)(2,1)} %reshape_squeeze.3.refs_0_) | copy-start | bytes 9437188
  23.1 2.1 %copy-start.3 = (bf16[256,2,8,384]{3,2,1,0:T(8,128)(2,1)S(1)}, bf16[256,2,8,384]{3,2,1,0:T(8,128)(2,1)}, u32[]{:S(2)}) copy-start(bf16[256,2,8,384]{3,2,1,0:T(8,128)(2,1)} %reshape_squeeze.3.refs_0_) | copy-start | bytes 9437188
  23.1 4.0 %copy-start.9 = (f32[1,1,3,5120]{3,1,2,0:T(1,128)S(1)}, f32[1,1,3,5120]{3,1,2,0:T(1,128)}, u32[]{:S(2)}) copy-start(f32[1,1,3,5120]{3,1,2,0:T(1,128)} %param.7) | copy-start | bytes 184324
  23.1 4.2 %copy-start = (bf16[1,1,128,5120]{3,2,1,0:T(8,128)(2,1)S(1)}, bf16[1,1,128,5120]{3,2,1,0:T(8,128)(2,1)}, u32[]{:S(2)}) copy-start(bf16[1,1,128,5120]{3,2,1,0:T(8,128)(2,1)} %param.6) | copy-start | bytes 3932164
  23.1 31.6 %collective-permute-start.5 = (bf16[64,5120]{1,0:T(8,128)(2,1)S(1)}, bf16[64,5120]{1,0:T(8,128)(2,1)}, u32[]{:S(2)}, u32[]{:S(2)}) collective-permute-start(bf16[64,5120]{1,0:T(8,128)(2,1)S(1)} %after.3.refs_0_), channel_id=1, source_target_pairs={{0,4},{2,6},{4,0},{6,2},{1,5},{3,7},{5,1},{7,3},{8,12},{10,14},{12... | collective-permute-start | bytes 1966088 | tf_op jit(solution)/shard_map/ppermute | solution.py:28
  25.2 30.0 %collective-permute-start.6 = (bf16[64,5120]{1,0:T(8,128)(2,1)S(1)}, bf16[64,5120]{1,0:T(8,128)(2,1)}, u32[]{:S(2)}, u32[]{:S(2)}) collective-permute-start(bf16[64,5120]{1,0:T(8,128)(2,1)S(1)} %after.4.refs_1_), channel_id=1, source_target_pairs={{0,1},{1,0},{2,3},{3,2},{4,5},{5,4},{6,7},{7,6},{8,9},{9,8},{10,11... | collective-permute-start | bytes 1966088 | tf_op jit(solution)/shard_map/ppermute | solution.py:28
  27.1 23.3 %collective-permute-start = (f32[1,1,3,5120]{3,2,1,0:T(4,128)S(1)}, f32[1,1,3,5120]{3,2,1,0:T(4,128)S(1)}, u32[]{:S(2)}, u32[]{:S(2)}) collective-permute-start(f32[1,1,3,5120]{3,2,1,0:T(4,128)S(1)} %copy.15), channel_id=1, source_target_pairs={{0,1},{1,0},{2,3},{3,2},{4,5},{5,4},{6,7},{7,6},{8,9},{9,8},{10,11... | collective-permute-start | bytes 184328 | tf_op jit(solution)/shard_map/ppermute | solution.py:28
  28.8 1.1 copy-start.6
  42.0 16.2 %collective-permute-start.7 = (bf16[128,5120]{1,0:T(8,128)(2,1)}, bf16[128,5120]{1,0:T(8,128)(2,1)}, u32[]{:S(2)}, u32[]{:S(2)}) collective-permute-start(bf16[128,5120]{1,0:T(8,128)(2,1)} %copy-done.6), channel_id=1, source_target_pairs={{0,2},{2,0},{4,6},{6,4},{1,3},{3,1},{5,7},{7,5},{8,10},{10,8},{12,... | collective-permute-start | bytes 3932168 | tf_op jit(solution)/shard_map/ppermute | solution.py:28
  42.0 0.9 copy-start.4
  42.0 48.6 %collective-permute-start.11 = (bf16[384,5120]{1,0:T(8,128)(2,1)}, bf16[384,5120]{1,0:T(8,128)(2,1)}, u32[]{:S(2)}, u32[]{:S(2)}) collective-permute-start(bf16[384,5120]{1,0:T(8,128)(2,1)} %bitcast.30), channel_id=1, source_target_pairs={{0,2},{2,0},{4,6},{6,4},{1,3},{3,1},{5,7},{7,5},{8,10},{10,8},{12,... | collective-permute-start | bytes 11796488 | tf_op jit(solution)/shard_map/ppermute | solution.py:28
  42.9 42.6 %all-to-all-start = ((bf16[8,256,768]{2,1,0:T(8,128)(2,1)}), bf16[8,256,768]{2,1,0:T(8,128)(2,1)}, u32[]{:S(2)}, u32[]{:S(2)}) async-start(bf16[8,256,768]{2,1,0:T(8,128)(2,1)} %after.5), calls=%async_computation | async-start | bytes 6291456 | tf_op jit(solution)/shard_map/all_to_all | solution.py:443
  50.4 2.8 %copy-start.5 = (bf16[64,5120]{1,0:T(8,128)(2,1)S(1)}, bf16[64,5120]{1,0:T(8,128)(2,1)}, u32[]{:S(2)}) copy-start(bf16[64,5120]{1,0:T(8,128)(2,1)} %copy-done.4) | copy-start | bytes 1966084
  53.0 5.2 %collective-permute-start.8 = (bf16[128,5120]{1,0:T(8,128)(2,1)S(1)}, bf16[128,5120]{1,0:T(8,128)(2,1)S(1)}, u32[]{:S(2)}, u32[]{:S(2)}) collective-permute-start(bf16[128,5120]{1,0:T(8,128)(2,1)S(1)} %modulated_norm.5.refs_1_), channel_id=1, source_target_pairs={{0,2},{2,0},{4,6},{6,4},{1,3},{3,1},{5,7},{7,5},{8,10},{10,8},{12,... | collective-permute-start | bytes 3932168 | tf_op jit(solution)/shard_map/ppermute | solution.py:28
  54.6 6.5 %copy-start.7 = (bf16[128,5120]{1,0:T(8,128)(2,1)S(1)}, bf16[128,5120]{1,0:T(8,128)(2,1)}, u32[]{:S(2)}) copy-start(bf16[128,5120]{1,0:T(8,128)(2,1)} %copy-done.6) | copy-start | bytes 3932164
  54.7 3.6 %collective-permute-start.9 = (bf16[128,5120]{1,0:T(8,128)(2,1)S(1)}, bf16[128,5120]{1,0:T(8,128)(2,1)S(1)}, u32[]{:S(2)}, u32[]{:S(2)}) collective-permute-start(bf16[128,5120]{1,0:T(8,128)(2,1)S(1)} %modulated_norm.6.refs_2_), channel_id=1, source_target_pairs={{0,2},{2,0},{4,6},{6,4},{1,3},{3,1},{5,7},{7,5},{8,10},{10,8},{12,... | collective-permute-start | bytes 3932168 | tf_op jit(solution)/shard_map/ppermute | solution.py:28
  58.0 3.1 %collective-permute-start.10 = (bf16[128,5120]{1,0:T(8,128)(2,1)S(1)}, bf16[128,5120]{1,0:T(8,128)(2,1)S(1)}, u32[]{:S(2)}, u32[]{:S(2)}) collective-permute-start(bf16[128,5120]{1,0:T(8,128)(2,1)S(1)} %modulated_norm.7.refs_3_), channel_id=1, source_target_pairs={{0,2},{2,0},{4,6},{6,4},{1,3},{3,1},{5,7},{7,5},{8,10},{10,8},{12,... | collective-permute-start | bytes 3932168 | tf_op jit(solution)/shard_map/ppermute | solution.py:28
  61.1 24.3 %copy-start.8 = (s32[1,4,6]{2,1,0:T(4,128)S(1)}, s32[1,4,6]{2,1,0:T(4,128)}, u32[]{:S(2)}) copy-start(s32[1,4,6]{2,1,0:T(4,128)} %param.11) | copy-start | bytes 292
  85.4 5.2 %copy-start.1 = (bf16[1,384,5120]{2,1,0:T(8,128)(2,1)S(1)}, bf16[1,384,5120]{2,1,0:T(8,128)(2,1)}, u32[]{:S(2)}) copy-start(bf16[1,384,5120]{2,1,0:T(8,128)(2,1)} %param.9) | copy-start | bytes 11796484
  90.5 4.0 %collective-permute-start.12 = (bf16[512,384]{1,0:T(8,128)(2,1)S(1)}, bf16[512,384]{1,0:T(8,128)(2,1)S(1)}, u32[]{:S(2)}, u32[]{:S(2)}) collective-permute-start(bf16[512,384]{1,0:T(8,128)(2,1)S(1)} %get-tuple-element.56.refs_2_), channel_id=1, source_target_pairs={{0,2},{2,0},{4,6},{6,4},{1,3},{3,1},{5,7},{7,5},{8,10},{10,8},{12,... | collective-permute-start | bytes 1179656 | tf_op jit(solution)/shard_map/ppermute | solution.py:28
  95.9 10.6 %collective-permute-start.13 = (bf16[128,1280]{1,0:T(8,128)(2,1)S(1)}, bf16[128,1280]{1,0:T(8,128)(2,1)S(1)}, u32[]{:S(2)}, u32[]{:S(2)}) collective-permute-start(bf16[128,1280]{1,0:T(8,128)(2,1)S(1)} %get-tuple-element.59), channel_id=1, source_target_pairs={{0,1},{1,0},{2,3},{3,2},{4,5},{5,4},{6,7},{7,6},{8,9},{9,8},{10,11... | collective-permute-start | bytes 983048 | tf_op jit(solution)/shard_map/ppermute | solution.py:28
  96.7 10.5 %collective-permute-start.14 = (bf16[128,1280]{1,0:T(8,128)(2,1)S(1)}, bf16[128,1280]{1,0:T(8,128)(2,1)S(1)}, u32[]{:S(2)}, u32[]{:S(2)}) collective-permute-start(bf16[128,1280]{1,0:T(8,128)(2,1)S(1)} %get-tuple-element.60), channel_id=1, source_target_pairs={{0,4},{2,6},{4,0},{6,2},{1,5},{3,7},{5,1},{7,3},{8,12},{10,14},{12... | collective-permute-start | bytes 983048 | tf_op jit(solution)/shard_map/ppermute | solution.py:28
  100.6 12.9 %collective-permute-start.17 = (bf16[128,1280]{1,0:T(8,128)(2,1)S(1)}, bf16[128,1280]{1,0:T(8,128)(2,1)S(1)}, u32[]{:S(2)}, u32[]{:S(2)}) collective-permute-start(bf16[128,1280]{1,0:T(8,128)(2,1)S(1)} %get-tuple-element.70), channel_id=1, source_target_pairs={{0,1},{1,0},{2,3},{3,2},{4,5},{5,4},{6,7},{7,6},{8,9},{9,8},{10,11... | collective-permute-start | bytes 983048 | tf_op jit(solution)/shard_map/ppermute | solution.py:28
  101.4 12.9 %collective-permute-start.18 = (bf16[128,1280]{1,0:T(8,128)(2,1)S(1)}, bf16[128,1280]{1,0:T(8,128)(2,1)S(1)}, u32[]{:S(2)}, u32[]{:S(2)}) collective-permute-start(bf16[128,1280]{1,0:T(8,128)(2,1)S(1)} %get-tuple-element.71), channel_id=1, source_target_pairs={{0,4},{2,6},{4,0},{6,2},{1,5},{3,7},{5,1},{7,3},{8,12},{10,14},{12... | collective-permute-start | bytes 983048 | tf_op jit(solution)/shard_map/ppermute | solution.py:28
  109.1 10.7 %collective-permute-start.15 = (bf16[128,1152]{1,0:T(8,128)(2,1)S(1)}, bf16[128,1152]{1,0:T(8,128)(2,1)S(1)}, u32[]{:S(2)}, u32[]{:S(2)}) collective-permute-start(bf16[128,1152]{1,0:T(8,128)(2,1)S(1)} %get-tuple-element.64), channel_id=1, source_target_pairs={{0,1},{1,0},{2,3},{3,2},{4,5},{5,4},{6,7},{7,6},{8,9},{9,8},{10,11... | collective-permute-start | bytes 884744 | tf_op jit(solution)/shard_map/ppermute | solution.py:28
  110.5 10.1 %collective-permute-start.16 = (bf16[128,1152]{1,0:T(8,128)(2,1)S(1)}, bf16[128,1152]{1,0:T(8,128)(2,1)S(1)}, u32[]{:S(2)}, u32[]{:S(2)}) collective-permute-start(bf16[128,1152]{1,0:T(8,128)(2,1)S(1)} %get-tuple-element.65), channel_id=1, source_target_pairs={{0,4},{2,6},{4,0},{6,2},{1,5},{3,7},{5,1},{7,3},{8,12},{10,14},{12... | collective-permute-start | bytes 884744 | tf_op jit(solution)/shard_map/ppermute | solution.py:28
  116.7 11.4 %collective-permute-start.20 = (bf16[128,1408]{1,0:T(8,128)(2,1)S(1)}, bf16[128,1408]{1,0:T(8,128)(2,1)S(1)}, u32[]{:S(2)}, u32[]{:S(2)}) collective-permute-start(bf16[128,1408]{1,0:T(8,128)(2,1)S(1)} %get-tuple-element.75), channel_id=1, source_target_pairs={{0,1},{1,0},{2,3},{3,2},{4,5},{5,4},{6,7},{7,6},{8,9},{9,8},{10,11... | collective-permute-start | bytes 1081352 | tf_op jit(solution)/shard_map/ppermute | solution.py:28
  118.0 10.9 %collective-permute-start.21 = (bf16[128,1408]{1,0:T(8,128)(2,1)S(1)}, bf16[128,1408]{1,0:T(8,128)(2,1)S(1)}, u32[]{:S(2)}, u32[]{:S(2)}) collective-permute-start(bf16[128,1408]{1,0:T(8,128)(2,1)S(1)} %get-tuple-element.76), channel_id=1, source_target_pairs={{0,4},{2,6},{4,0},{6,2},{1,5},{3,7},{5,1},{7,3},{8,12},{10,14},{12... | collective-permute-start | bytes 1081352 | tf_op jit(solution)/shard_map/ppermute | solution.py:28
  122.9 10.7 %collective-permute-start.19 = (bf16[128,1280]{1,0:T(8,128)(2,1)S(1)}, bf16[128,1280]{1,0:T(8,128)(2,1)S(1)}, u32[]{:S(2)}, u32[]{:S(2)}) collective-permute-start(bf16[128,1280]{1,0:T(8,128)(2,1)S(1)} %get-tuple-element.74.refs_12_), channel_id=1, source_target_pairs={{0,8},{8,16},{16,24},{24,0},{1,9},{9,17},{17,25},{25,1},{2,10},{10... | collective-permute-start | bytes 983048 | tf_op jit(solution)/shard_map/ppermute | solution.py:23
  124.5 9.1 %collective-permute-start.23 = (bf16[128,1024]{1,0:T(8,128)(2,1)S(1)}, bf16[128,1024]{1,0:T(8,128)(2,1)S(1)}, u32[]{:S(2)}, u32[]{:S(2)}) collective-permute-start(bf16[128,1024]{1,0:T(8,128)(2,1)S(1)} %get-tuple-element.81), channel_id=1, source_target_pairs={{0,1},{1,0},{2,3},{3,2},{4,5},{5,4},{6,7},{7,6},{8,9},{9,8},{10,11... | collective-permute-start | bytes 786440 | tf_op jit(solution)/shard_map/ppermute | solution.py:28
  125.6 8.0 %collective-permute-start.24 = (bf16[128,1024]{1,0:T(8,128)(2,1)S(1)}, bf16[128,1024]{1,0:T(8,128)(2,1)S(1)}, u32[]{:S(2)}, u32[]{:S(2)}) collective-permute-start(bf16[128,1024]{1,0:T(8,128)(2,1)S(1)} %get-tuple-element.82), channel_id=1, source_target_pairs={{0,4},{2,6},{4,0},{6,2},{1,5},{3,7},{5,1},{7,3},{8,12},{10,14},{12... | collective-permute-start | bytes 786440 | tf_op jit(solution)/shard_map/ppermute | solution.py:28
  130.7 9.9 %collective-permute-start.22 = (bf16[128,1280]{1,0:T(8,128)(2,1)S(1)}, bf16[128,1280]{1,0:T(8,128)(2,1)S(1)}, u32[]{:S(2)}, u32[]{:S(2)}) collective-permute-start(bf16[128,1280]{1,0:T(8,128)(2,1)S(1)} %get-tuple-element.80.refs_8_), channel_id=1, source_target_pairs={{0,8},{8,16},{16,24},{24,0},{1,9},{9,17},{17,25},{25,1},{2,10},{10... | collective-permute-start | bytes 983048 | tf_op jit(solution)/shard_map/ppermute | solution.py:23
  132.3 6.5 %collective-permute-start.26 = (bf16[128,896]{1,0:T(8,128)(2,1)S(1)}, bf16[128,896]{1,0:T(8,128)(2,1)S(1)}, u32[]{:S(2)}, u32[]{:S(2)}) collective-permute-start(bf16[128,896]{1,0:T(8,128)(2,1)S(1)} %get-tuple-element.88), channel_id=1, source_target_pairs={{0,1},{1,0},{2,3},{3,2},{4,5},{5,4},{6,7},{7,6},{8,9},{9,8},{10,11... | collective-permute-start | bytes 688136 | tf_op jit(solution)/shard_map/ppermute | solution.py:28
  133.6 6.9 %collective-permute-start.27 = (bf16[128,896]{1,0:T(8,128)(2,1)S(1)}, bf16[128,896]{1,0:T(8,128)(2,1)S(1)}, u32[]{:S(2)}, u32[]{:S(2)}) collective-permute-start(bf16[128,896]{1,0:T(8,128)(2,1)S(1)} %get-tuple-element.89), channel_id=1, source_target_pairs={{0,4},{2,6},{4,0},{6,2},{1,5},{3,7},{5,1},{7,3},{8,12},{10,14},{12... | collective-permute-start | bytes 688136 | tf_op jit(solution)/shard_map/ppermute | solution.py:28
  133.8 8.9 %collective-permute-start.29 = (bf16[128,384]{1,0:T(8,128)(2,1)S(1)}, bf16[128,384]{1,0:T(8,128)(2,1)S(1)}, u32[]{:S(2)}, u32[]{:S(2)}) collective-permute-start(bf16[128,384]{1,0:T(8,128)(2,1)S(1)} %get-tuple-element.95), channel_id=1, source_target_pairs={{0,1},{1,0},{2,3},{3,2},{4,5},{5,4},{6,7},{7,6},{8,9},{9,8},{10,11... | collective-permute-start | bytes 294920 | tf_op jit(solution)/shard_map/ppermute | solution.py:28
  135.6 9.0 %collective-permute-start.30 = (bf16[128,384]{1,0:T(8,128)(2,1)S(1)}, bf16[128,384]{1,0:T(8,128)(2,1)S(1)}, u32[]{:S(2)}, u32[]{:S(2)}) collective-permute-start(bf16[128,384]{1,0:T(8,128)(2,1)S(1)} %get-tuple-element.96), channel_id=1, source_target_pairs={{0,4},{2,6},{4,0},{6,2},{1,5},{3,7},{5,1},{7,3},{8,12},{10,14},{12... | collective-permute-start | bytes 294920 | tf_op jit(solution)/shard_map/ppermute | solution.py:28
  138.8 8.2 %collective-permute-start.25 = (bf16[128,512]{1,0:T(8,128)(2,1)S(1)}, bf16[128,512]{1,0:T(8,128)(2,1)S(1)}, u32[]{:S(2)}, u32[]{:S(2)}) collective-permute-start(bf16[128,512]{1,0:T(8,128)(2,1)S(1)} %get-tuple-element.87.refs_8_), channel_id=1, source_target_pairs={{0,8},{8,16},{16,24},{24,0},{1,9},{9,17},{17,25},{25,1},{2,10},{10... | collective-permute-start | bytes 393224 | tf_op jit(solution)/shard_map/ppermute | solution.py:23
  140.7 6.4 %collective-permute-start.32 = (bf16[128,256]{1,0:T(8,128)(2,1)S(1)}, bf16[128,256]{1,0:T(8,128)(2,1)S(1)}, u32[]{:S(2)}, u32[]{:S(2)}) collective-permute-start(bf16[128,256]{1,0:T(8,128)(2,1)S(1)} %get-tuple-element.99), channel_id=1, source_target_pairs={{0,1},{1,0},{2,3},{3,2},{4,5},{5,4},{6,7},{7,6},{8,9},{9,8},{10,11... | collective-permute-start | bytes 196616 | tf_op jit(solution)/shard_map/ppermute | solution.py:28
  142.1 5.0 %collective-permute-start.33 = (bf16[128,256]{1,0:T(8,128)(2,1)S(1)}, bf16[128,256]{1,0:T(8,128)(2,1)S(1)}, u32[]{:S(2)}, u32[]{:S(2)}) collective-permute-start(bf16[128,256]{1,0:T(8,128)(2,1)S(1)} %get-tuple-element.100), channel_id=1, source_target_pairs={{0,4},{2,6},{4,0},{6,2},{1,5},{3,7},{5,1},{7,3},{8,12},{10,14},{12... | collective-permute-start | bytes 196616 | tf_op jit(solution)/shard_map/ppermute | solution.py:28
  142.6 9.6 %collective-permute-start.28 = (bf16[128,768]{1,0:T(8,128)(2,1)S(1)}, bf16[128,768]{1,0:T(8,128)(2,1)S(1)}, u32[]{:S(2)}, u32[]{:S(2)}) collective-permute-start(bf16[128,768]{1,0:T(8,128)(2,1)S(1)} %get-tuple-element.94.refs_6_), channel_id=1, source_target_pairs={{0,8},{8,16},{16,24},{24,0},{1,9},{9,17},{17,25},{25,1},{2,10},{10... | collective-permute-start | bytes 589832 | tf_op jit(solution)/shard_map/ppermute | solution.py:23
  147.0 7.5 %collective-permute-start.31 = (bf16[128,768]{1,0:T(8,128)(2,1)S(1)}, bf16[128,768]{1,0:T(8,128)(2,1)S(1)}, u32[]{:S(2)}, u32[]{:S(2)}) collective-permute-start(bf16[128,768]{1,0:T(8,128)(2,1)S(1)} %sum_stage.18.refs_6_), channel_id=1, source_target_pairs={{0,8},{8,16},{16,24},{24,0},{1,9},{9,17},{17,25},{25,1},{2,10},{10... | collective-permute-start | bytes 589832 | tf_op jit(solution)/shard_map/ppermute | solution.py:23
  147.1 8.8 %collective-permute-start.34 = (bf16[128,512]{1,0:T(8,128)(2,1)S(1)}, bf16[128,512]{1,0:T(8,128)(2,1)S(1)}, u32[]{:S(2)}, u32[]{:S(2)}) collective-permute-start(bf16[128,512]{1,0:T(8,128)(2,1)S(1)} %sum_stage.19), channel_id=1, source_target_pairs={{0,8},{8,16},{16,24},{24,0},{1,9},{9,17},{17,25},{25,1},{2,10},{10... | collective-permute-start | bytes 393224 | tf_op jit(solution)/shard_map/ppermute | solution.py:23
  155.9 1.1 copy-start.10

commit v16 on v14

--- a/solution.py
+++ b/solution.py
@@ -66,7 +66,7 @@
     pass
 
 
-def after(value, earlier):
+def after(value, earlier, limit=1):
     return pl.pallas_call(
         gate_kernel,
         in_specs=[pl.BlockSpec(memory_space=pl.ANY)] * (1 + len(earlier)),
@@ -75,7 +75,7 @@
         input_output_aliases={0: 0},
         name="after",
         cost_estimate=SHORT,
-        compiler_params=pltpu.CompilerParams(vmem_limit_bytes=MIB),
+        compiler_params=pltpu.CompilerParams(vmem_limit_bytes=limit * MIB),
     )(value, *earlier)
 
 
@@ -143,48 +143,60 @@
     )(*blocks, weights)
 
 
-def attend_head(visible_ref, queries_ref, pool_ref, out_ref, first_block, head):
+def attend_units(visible_ref, queries_ref, pool_ref, out_ref, first_block, before_head):
     heads, fresh_rows, _ = queries_ref.shape
     tiles_seen = visible_ref.shape[1]
     tiles_fresh = visible_ref.shape[0]
     mine_high, mine_low = lax.axis_index("sp") // 2, lax.axis_index("sp") % 2
     mine_branch = lax.axis_index("cfg")
-    ones = jnp.ones((tiles_seen * TILE, HD), jnp.bfloat16)
-
-    def body(step, carry):
-        index = first_block + step
+    blocks = out_ref.shape[0] // TILE
+    places = []
+    for block in range(blocks):
+        index = first_block + block
         high, low = mine_high ^ ((index // 2) % 2), mine_low ^ (index // 4)
         tile, branch = high * 2 + low, mine_branch ^ (index % 2)
-        rows = pl.ds(pl.multiple_of(index * TILE, TILE), TILE)
-        out_rows = pl.ds(pl.multiple_of(step * TILE, TILE), TILE)
-        places = []
-        for seen in range(tiles_seen):
-            number = visible_ref[tile, seen]
+        seen = []
+        for number in range(tiles_seen):
+            number = visible_ref[tile, number]
             older = number - tiles_fresh
             fresh = (mine_low ^ (number % 2)) * 4 + (mine_high ^ ((number // 2) % 2)) * 2
             fresh = (fresh + index % 2) * TILE
             stale = fresh_rows + ((older // 2) * 2 + branch) * 2 * TILE + (older % 2) * TILE
             start = jnp.where(number < tiles_fresh, fresh, stale)
-            places.append(pl.ds(pl.multiple_of(start, TILE), TILE))
-
-        keys = jnp.concatenate([pool_ref[head, place, :] for place in places], axis=0)
-        values = jnp.concatenate([pool_ref[heads + head, place, :] for place in places], axis=0)
-        scores = lax.dot_general(
+            seen.append(pl.ds(pl.multiple_of(start, TILE), TILE))
+        places.append(seen)
+
+    def scores_of(head, block):
+        rows = pl.ds((first_block + block) * TILE, TILE)
+        keys = jnp.concatenate([pool_ref[head, place, :] for place in places[block]], axis=0)
+        return lax.dot_general(
             queries_ref[head, rows, :],
             keys,
             (((1,), (1,)), ((), ())),
             preferred_element_type=jnp.float32,
         )
+
+    def finish(head, block, scores):
+        values = [pool_ref[heads + head, place, :] for place in places[block]]
+        values = jnp.concatenate(values, axis=0)
         exponent = jnp.exp2(scores * (HD ** (-0.5) * LOG2E)).astype(jnp.bfloat16)
+        ones = jnp.ones(values.shape, jnp.bfloat16)
         mixed = jnp.dot(
             exponent, jnp.concatenate([values, ones], axis=1), preferred_element_type=jnp.float32
         )
-        out_ref[out_rows, head * HD : (head + 1) * HD] = (mixed[:, :HD] / mixed[:, HD:]).astype(
-            jnp.bfloat16
-        )
-        return carry
-
-    lax.fori_loop(0, out_ref.shape[0] // TILE, body, 0, unroll=True)
+        out_ref[block * TILE : (block + 1) * TILE, head * HD : (head + 1) * HD] = (
+            mixed[:, :HD] / mixed[:, HD:]
+        ).astype(jnp.bfloat16)
+
+    waiting = None
+    for head in range(heads):
+        before_head(head)
+        for block in range(blocks):
+            scores = scores_of(head, block)
+            if waiting is not None:
+                finish(*waiting)
+            waiting = head, block, scores
+    finish(*waiting)
 
 
 def attend_first_kernel(
@@ -207,11 +219,13 @@
         for copy in of_head:
             copy.start()
         copies.append(of_head)
-    for head in range(heads):
+
+    def before_head(head):
         for copy in copies[head]:
             copy.wait()
-        first_block = out_ref.shape[0] // TILE
-        attend_head(visible_ref, queries_ref, pool_ref, out_ref, first_block, head)
+
+    first_block = out_ref.shape[0] // TILE
+    attend_units(visible_ref, queries_ref, pool_ref, out_ref, first_block, before_head)
 
 
 def attend_first(heads, context, visible):
@@ -248,8 +262,7 @@
     ]
     for copy in copies:
         copy.start()
-    for head in range(queries_ref.shape[0]):
-        attend_head(visible_ref, queries_ref, pool_ref, out_ref, 0, head)
+    attend_units(visible_ref, queries_ref, pool_ref, out_ref, 0, lambda head: None)
     for copy in copies:
         copy.wait()
 
@@ -434,7 +447,7 @@
     ]
     far = [from_partner(rows, "sp", 1) for rows in near]
 
-    packed = after(packed, (across_lower, along_upper))
+    packed = after(packed, (across_lower, along_upper), limit=60)
     context = lax.all_to_all(packed, ("sp", "cfg"), split_axis=0, concat_axis=0, tiled=True)
     context = context.reshape(devices * context_rows, 2 * width)
 

time: 160 us -> 157 us (0.981)
  waiting for transfers between devices: 38.3 us -> 41.9 us
  local copies, waits for them, and re-layouts: 30.3 us -> 27.1 us
  starting transfers between devices: 41.1 us -> 38.3 us
    ppermute x29, waiting for transfers between devices: 21.9 us -> 26.9 us  [from_partner(): return lax.ppermute(value, axis, pairs)]
    unnamed x28, local copies, waits for them, and re-layouts: 7.69 us -> 4.47 us
    all_to_all x1, waiting for transfers between devices: 7.27 us -> 5.12 us  [per_device(): lax.all_to_all(packed, ('sp', 'cfg'), split_axis=0, concat_axis=0, tiled=...]
    ppermute x6, starting transfers between devices: 9.82 us -> 7.85 us  [from_behind(): return lax.ppermute(x, axis, [(i, (i + by) % count) for i in range(count)])]
  transfers between devices with their start and end apart: 36 -> 36, of which waited for: 17 -> 19; matrix products, arithmetic and copies ran while one was open for 13% -> 13% of each run, Pallas kernels for 30% -> 30%
where the time goes in v16:
time: 157 us; the launch traced here: 156 us
  Pallas kernels  48.2 us (31%)
  waiting for transfers between devices  41.9 us (27%)
  starting transfers between devices  38.3 us (24%)
  local copies, waits for them, and re-layouts  27.1 us (17%)
    ppermute x29, waiting for transfers between devices, from_partner(): return lax.ppermute(value, axis, pairs)  26.9 us
    ppermute x29, starting transfers between devices, from_partner(): return lax.ppermute(value, axis, pairs)  25.8 us
    pallas_call x1, Pallas kernels, project(): pl.pallas_call(functools.partial(project_kernel, blocks=len(blocks)), gri...  19.2 us
    pallas_call x10, Pallas kernels, stage(): pl.pallas_call(functools.partial(stage_kernel, parts=parts, start=start,...  12.7 us
    ppermute x6, waiting for transfers between devices, from_behind(): return lax.ppermute(x, axis, [(i, (i + by) % count) for i in range(count)])  9.82 us
    pallas_call x4, Pallas kernels, modulated_norm(): pl.pallas_call(norm_kernel, in_specs=[pl.BlockSpec(memory_space=pltpu.VME...  8.49 us
    reshape x1, local copies, waits for them, and re-layouts, per_device(): unpacked.transpose(2, 0, 1, 3).reshape(devices, context_rows, 2 * width)  8.06 us
    another operation x1, local copies, waits for them, and re-layouts, per_device(): unpacked = stale_cache[0, 0].reshape(context_rows, 2, devices, width)  8 us
  transfers between devices with their start and end apart: 36, of which 19 were waited for; matrix products, arithmetic and copies ran while one was open for 13% of the time, Pallas kernels for 30%

profile of v16, /device:TPU:0, one launch (start us, length us, event | category | flops | bytes accessed | tf_op | source)
XLA Modules:
  0.0 155.9 jit_solution(14228735012046764803)
XLA Ops:
  0.0 2.5 %slice_bitcast_fusion = (bf16[64,5120]{1,0:T(8,128)(2,1)}, bf16[64,5120]{1,0:T(8,128)(2,1)}) fusion(bf16[1,1,128,5120]{3,2,1,0:T(8,128)(2,1)} %param.6), kind=kLoop, calls=%fused_computation | loop fusion | bytes 2621440 | tf_op jit(solution)/shard_map/slice | solution.py:435
  2.5 2.9 %collective-permute-start.1 = (bf16[64,5120]{1,0:T(8,128)(2,1)}, bf16[64,5120]{1,0:T(8,128)(2,1)S(1)}, u32[]{:S(2)}, u32[]{:S(2)}) collective-permute-start(bf16[64,5120]{1,0:T(8,128)(2,1)} %get-tuple-element.104), channel_id=1, source_target_pairs={{0,1},{1,0},{2,3},{3,2},{4,5},{5,4},{6,7},{7,6},{8,9},{9,8},{10,11... | collective-permute-start | bytes 1966088 | tf_op jit(solution)/shard_map/ppermute | solution.py:28
  5.4 1.5 collective-permute-start.4
  6.9 0.5 collective-permute-start.2
  7.5 8.0 %reshape_squeeze.3.refs_0_ = bf16[256,2,8,384]{3,2,1,0:T(8,128)(2,1)} reshape(bf16[1,1,256,2,3072]{4,3,2,1,0:T(2,128)(2,1)} %param.10) | data formatting | bytes 6291456 | tf_op jit(solution)/shard_map/reshape;squeeze | solution.py:432
  15.5 5.7 %collective-permute-done.1.value_ref = bf16[64,5120]{1,0:T(8,128)(2,1)S(1)} collective-permute-done((bf16[64,5120]{1,0:T(8,128)(2,1)}, bf16[64,5120]{1,0:T(8,128)(2,1)S(1)}, u32[]{:S(2)}, u32[]{:S(2)}) %collective-permute-start.1) | collective-permute-done | bytes 655392 | tf_op jit(solution)/shard_map/ppermute | solution.py:28
  21.2 1.9 %copy-done.2 = bf16[256,2,8,384]{3,2,1,0:T(8,128)(2,1)S(1)} copy-done((bf16[256,2,8,384]{3,2,1,0:T(8,128)(2,1)S(1)}, bf16[256,2,8,384]{3,2,1,0:T(8,128)(2,1)}, u32[]{:S(2)}) %copy-start.2) | copy-done | bytes 3145752
  23.1 2.1 %collective-permute-start.5 = (bf16[64,5120]{1,0:T(8,128)(2,1)S(1)}, bf16[64,5120]{1,0:T(8,128)(2,1)}, u32[]{:S(2)}, u32[]{:S(2)}) collective-permute-start(bf16[64,5120]{1,0:T(8,128)(2,1)S(1)} %after.3.refs_0_), channel_id=1, source_target_pairs={{0,4},{2,6},{4,0},{6,2},{1,5},{3,7},{5,1},{7,3},{8,12},{10,14},{12... | collective-permute-start | bytes 1966088 | tf_op jit(solution)/shard_map/ppermute | solution.py:28
  25.2 1.8 %collective-permute-start.6 = (bf16[64,5120]{1,0:T(8,128)(2,1)S(1)}, bf16[64,5120]{1,0:T(8,128)(2,1)}, u32[]{:S(2)}, u32[]{:S(2)}) collective-permute-start(bf16[64,5120]{1,0:T(8,128)(2,1)S(1)} %after.4.refs_1_), channel_id=1, source_target_pairs={{0,1},{1,0},{2,3},{3,2},{4,5},{5,4},{6,7},{7,6},{8,9},{9,8},{10,11... | collective-permute-start | bytes 1966088 | tf_op jit(solution)/shard_map/ppermute | solution.py:28
  27.3 1.5 modulated_norm.4.refs_0_
  28.8 1.0 copy-done.6
  29.9 4.1 %copy.11 = bf16[8,256,2,384]{3,2,1,0:T(2,128)(2,1)} copy(bf16[8,256,2,384]{3,0,2,1:T(8,128)(2,1)S(1)} %bitcast.37) | data formatting | bytes 6291456 | tf_op jit(solution)/shard_map/transpose | solution.py:433
  33.9 8.1 %reshape.10.value_ref = bf16[8,256,768]{2,1,0:T(8,128)(2,1)} reshape(bf16[8,256,2,384]{3,2,1,0:T(2,128)(2,1)} %copy.11) | data formatting | bytes 6291456 | tf_op jit(solution)/shard_map/reshape | solution.py:433
  42.0 0.5 collective-permute-start.11
  42.9 4.6 %all-to-all-start = ((bf16[8,256,768]{2,1,0:T(8,128)(2,1)}), bf16[8,256,768]{2,1,0:T(8,128)(2,1)}, u32[]{:S(2)}, u32[]{:S(2)}) async-start(bf16[8,256,768]{2,1,0:T(8,128)(2,1)} %after.5), calls=%async_computation | async-start | bytes 6291456 | tf_op jit(solution)/shard_map/all_to_all | solution.py:451
  47.5 2.9 %collective-permute-done = f32[1,1,3,5120]{3,2,1,0:T(4,128)S(1)} collective-permute-done((f32[1,1,3,5120]{3,2,1,0:T(4,128)S(1)}, f32[1,1,3,5120]{3,2,1,0:T(4,128)S(1)}, u32[]{:S(2)}, u32[]{:S(2)}) %collective-permute-start) | collective-permute-done | bytes 61472 | tf_op jit(solution)/shard_map/ppermute | solution.py:28
  50.4 2.7 %modulated_norm.5.refs_1_ = bf16[128,5120]{1,0:T(8,128)(2,1)S(1)} custom-call(bf16[64,5120]{1,0:T(8,128)(2,1)S(1)} %after.3.refs_0_, bf16[64,5120]{1,0:T(8,128)(2,1)} %collective-permute-done.2.refs_1_.refs_0_, f32[3,5120]{1,0:T(4,128)S(1)} %bitcast.40), custom_call_target="tpu_custom_call" | custom-call | flops 1 | bytes 1 | tf_op jit(solution)/shard_map/modulated_norm/pallas_call | solution.py:55
  53.1 1.5 modulated_norm.6.refs_2_
  54.7 0.6 collective-permute-start.9
  55.2 2.8 %modulated_norm.7.refs_3_ = bf16[128,5120]{1,0:T(8,128)(2,1)S(1)} custom-call(bf16[64,5120]{1,0:T(8,128)(2,1)} %collective-permute-done.5.refs_0_, bf16[64,5120]{1,0:T(8,128)(2,1)} %collective-permute-done.6.refs_1_, f32[3,5120]{1,0:T(4,128)S(1)} %bitcast.41), custom_call_target="tpu_custom_call" | custom-call | flops 1 | bytes 1 | tf_op jit(solution)/shard_map/modulated_norm/pallas_call | solution.py:55
  58.3 2.9 %collective-permute-done.10.refs_7_ = bf16[128,5120]{1,0:T(8,128)(2,1)S(1)} collective-permute-done((bf16[128,5120]{1,0:T(8,128)(2,1)S(1)}, bf16[128,5120]{1,0:T(8,128)(2,1)S(1)}, u32[]{:S(2)}, u32[]{:S(2)}) %collective-permute-start.10) | collective-permute-done | bytes 1310752 | tf_op jit(solution)/shard_map/ppermute | solution.py:28
  61.1 19.2 %project_heads.1.heads_in = bf16[48,1024,128]{2,1,0:T(8,128)(2,1)} custom-call(bf16[128,5120]{1,0:T(8,128)(2,1)S(1)} %copy-done.7, bf16[128,5120]{1,0:T(8,128)(2,1)S(1)} %modulated_norm.5.refs_1_, bf16[128,5120]{1,0:T(8,128)(2,1)S(1)} %modulated_norm.6.refs_2_, bf16[128,5120]{1,0:T(8,128)(2,1)S(1)} %modulated_norm.7.refs_3_, ...), custom_call_target="tpu_custom_call" | custom-call | flops 12079595520 | bytes 22282240 | tf_op jit(solution)/shard_map/project_heads/pallas_call | solution.py:124
  80.3 5.1 %all-to-all-done = bf16[8,256,768]{2,1,0:T(8,128)(2,1)} async-done(((bf16[8,256,768]{2,1,0:T(8,128)(2,1)}), bf16[8,256,768]{2,1,0:T(8,128)(2,1)}, u32[]{:S(2)}, u32[]{:S(2)}) %all-to-all-start) | async-done | bytes 3145760 | tf_op jit(solution)/shard_map/all_to_all | solution.py:451
  85.4 4.4 %attend_first.1 = (bf16[512,384]{1,0:T(8,128)(2,1)S(1)}, bf16[3,1024,128]{2,1,0:T(8,128)(2,1)S(1)}, bf16[6,3072,128]{2,1,0:T(8,128)(2,1)S(1)}) custom-call(s32[4,6]{1,0:T(4,128)S(1)} %bitcast.42, bf16[48,1024,128]{2,1,0:T(8,128)(2,1)} %project_heads.1.heads_in, bf16[2048,768]{1,0:T(8,128)(2,1)} %bitcast.9.context_in), custom_call_target="tpu_custom_call" | custom-call | flops 1 | bytes 1 | tf_op jit(solution)/shard_map/attend_first/pallas_call | solution.py:233
  90.0 3.5 %attend_second.1 = (bf16[512,384]{1,0:T(8,128)(2,1)S(1)}, bf16[768,1280]{1,0:T(8,128)(2,1)S(1)}) custom-call(s32[4,6]{1,0:T(4,128)S(1)} %bitcast.43, bf16[3,1024,128]{2,1,0:T(8,128)(2,1)S(1)} %get-tuple-element.54.queries_ref, bf16[6,3072,128]{2,1,0:T(8,128)(2,1)S(1)} %get-tuple-element.55.pool_ref, bf16[384,5120]{1,0:T(8,128)(2,1)S(1)} %bitcast.31, ...), custom_call_target="tpu_custom_call" | custom-call | flops 1 | bytes 1 | tf_op jit(solution)/shard_map/attend_second/pallas_call | solution.py:272
  93.5 1.4 sum_stage.10
  94.9 0.8 collective-permute-start.13
  95.7 1.1 collective-permute-start.14
  96.8 2.7 %sum_stage.11 = (bf16[128,1280]{1,0:T(8,128)(2,1)S(1)}, bf16[128,1280]{1,0:T(8,128)(2,1)S(1)}, f32[2,128,640]{2,1,0:T(8,128)S(1)}, f32[2,128,640]{2,1,0:T(8,128)S(1)}) custom-call(bf16[128,5120]{1,0:T(8,128)(2,1)S(1)} %bitcast.21, f32[2,5120]{1,0:T(2,128)S(1)} %pad_maximum_fusion.refs_3_.refs_1_, bf16[512,384]{1,0:T(8,128)(2,1)S(1)} %get-tuple-element.57.refs_2_, ...), custom_call_target="tpu_custom_call" | custom-call | flops 1 | bytes 1 | tf_op jit(solution)/shard_map/sum_stage/pallas_call | solution.py:397
  99.5 0.8 collective-permute-start.17
  100.4 1.4 collective-permute-start.18
  101.8 3.7 %collective-permute-done.13.refs_6_ = bf16[128,1280]{1,0:T(8,128)(2,1)S(1)} collective-permute-done((bf16[128,1280]{1,0:T(8,128)(2,1)S(1)}, bf16[128,1280]{1,0:T(8,128)(2,1)S(1)}, u32[]{:S(2)}, u32[]{:S(2)}) %collective-permute-start.13) | collective-permute-done | bytes 327712 | tf_op jit(solution)/shard_map/ppermute | solution.py:28
  105.5 0.8 collective-permute-done.14.refs_7_
  106.2 1.8 %sum_stage.12 = (bf16[128,1152]{1,0:T(8,128)(2,1)S(1)}, bf16[128,1152]{1,0:T(8,128)(2,1)S(1)}, f32[2,128,256]{2,1,0:T(8,128)S(1)}, f32[2,128,256]{2,1,0:T(8,128)...) custom-call(bf16[128,5120]{1,0:T(8,128)(2,1)S(1)} %bitcast.22, f32[2,5120]{1,0:T(2,128)S(1)} %pad_maximum_fusion.refs_3_.refs_1_, ...), custom_call_target="tpu_custom_call" | custom-call | flops 1 | bytes 1 | tf_op jit(solution)/shard_map/sum_stage/pallas_call | solution.py:397
  108.1 1.4 collective-permute-start.15
  109.4 0.6 collective-permute-start.16
  110.1 2.4 %collective-permute-done.17.refs_6_ = bf16[128,1280]{1,0:T(8,128)(2,1)S(1)} collective-permute-done((bf16[128,1280]{1,0:T(8,128)(2,1)S(1)}, bf16[128,1280]{1,0:T(8,128)(2,1)S(1)}, u32[]{:S(2)}, u32[]{:S(2)}) %collective-permute-start.17) | collective-permute-done | bytes 327712 | tf_op jit(solution)/shard_map/ppermute | solution.py:28
  112.5 0.8 collective-permute-done.18.refs_7_
  113.3 2.4 %sum_stage.13 = (bf16[128,1408]{1,0:T(8,128)(2,1)S(1)}, bf16[128,1408]{1,0:T(8,128)(2,1)S(1)}, f32[2,128,384]{2,1,0:T(8,128)S(1)}, f32[2,128,384]{2,1,0:T(8,128)...) custom-call(bf16[128,5120]{1,0:T(8,128)(2,1)S(1)} %bitcast.23, f32[2,5120]{1,0:T(2,128)S(1)} %pad_maximum_fusion.refs_3_.refs_1_, ...), custom_call_target="tpu_custom_call" | custom-call | flops 1 | bytes 1 | tf_op jit(solution)/shard_map/sum_stage/pallas_call | solution.py:397
  115.6 1.4 collective-permute-start.20
  117.0 0.6 collective-permute-start.21
  117.6 1.2 collective-permute-done.15.refs_6_
  118.8 0.8 collective-permute-done.16.refs_7_
  119.6 2.3 %sum_stage.14 = (bf16[128,1024]{1,0:T(8,128)(2,1)S(1)}, bf16[128,1024]{1,0:T(8,128)(2,1)S(1)}, f32[2,128,384]{2,1,0:T(8,128)S(1)}, f32[2,128,384]{2,1,0:T(8,128)...) custom-call(bf16[128,5120]{1,0:T(8,128)(2,1)S(1)} %bitcast.24, ...), custom_call_target="tpu_custom_call" | custom-call | flops 1 | bytes 1 | tf_op jit(solution)/shard_map/sum_stage/pallas_call | solution.py:397
  121.8 1.6 %collective-permute-start.19 = (bf16[128,1280]{1,0:T(8,128)(2,1)S(1)}, bf16[128,1280]{1,0:T(8,128)(2,1)S(1)}, u32[]{:S(2)}, u32[]{:S(2)}) collective-permute-start(bf16[128,1280]{1,0:T(8,128)(2,1)S(1)} %get-tuple-element.74.refs_12_), channel_id=1, source_target_pairs={{0,8},{8,16},{16,24},{24,0},{1,9},{9,17},{17,25},{25,1},{2,10},{10... | collective-permute-start | bytes 983048 | tf_op jit(solution)/shard_map/ppermute | solution.py:23
  123.5 1.1 collective-permute-start.23
  124.7 2.4 %collective-permute-done.20.refs_6_ = bf16[128,1408]{1,0:T(8,128)(2,1)S(1)} collective-permute-done((bf16[128,1408]{1,0:T(8,128)(2,1)S(1)}, bf16[128,1408]{1,0:T(8,128)(2,1)S(1)}, u32[]{:S(2)}, u32[]{:S(2)}) %collective-permute-start.20) | collective-permute-done | bytes 360480 | tf_op jit(solution)/shard_map/ppermute | solution.py:28
  127.0 0.8 collective-permute-done.21.refs_7_
  127.8 1.8 %sum_stage.15 = (bf16[128,896]{1,0:T(8,128)(2,1)S(1)}, bf16[128,896]{1,0:T(8,128)(2,1)S(1)}, f32[2,128,256]{2,1,0:T(8,128)S(1)}, f32[2,128,256]{2,1,0:T(8,128)S(...) custom-call(bf16[128,5120]{1,0:T(8,128)(2,1)S(1)} %bitcast.25, ...), custom_call_target="tpu_custom_call" | custom-call | flops 1 | bytes 1 | tf_op jit(solution)/shard_map/sum_stage/pallas_call | solution.py:397
  129.6 1.6 %collective-permute-start.22 = (bf16[128,1280]{1,0:T(8,128)(2,1)S(1)}, bf16[128,1280]{1,0:T(8,128)(2,1)S(1)}, u32[]{:S(2)}, u32[]{:S(2)}) collective-permute-start(bf16[128,1280]{1,0:T(8,128)(2,1)S(1)} %get-tuple-element.80.refs_8_), channel_id=1, source_target_pairs={{0,8},{8,16},{16,24},{24,0},{1,9},{9,17},{17,25},{25,1},{2,10},{10... | collective-permute-start | bytes 983048 | tf_op jit(solution)/shard_map/ppermute | solution.py:23
  131.3 1.2 collective-permute-start.26
  132.7 1.9 %collective-permute-start.29 = (bf16[128,384]{1,0:T(8,128)(2,1)S(1)}, bf16[128,384]{1,0:T(8,128)(2,1)S(1)}, u32[]{:S(2)}, u32[]{:S(2)}) collective-permute-start(bf16[128,384]{1,0:T(8,128)(2,1)S(1)} %get-tuple-element.95), channel_id=1, source_target_pairs={{0,1},{1,0},{2,3},{3,2},{4,5},{5,4},{6,7},{7,6},{8,9},{9,8},{10,11... | collective-permute-start | bytes 294920 | tf_op jit(solution)/shard_map/ppermute | solution.py:28
  134.6 0.9 collective-permute-start.30
  135.6 2.1 %collective-permute-done.26.refs_2_ = bf16[128,896]{1,0:T(8,128)(2,1)S(1)} collective-permute-done((bf16[128,896]{1,0:T(8,128)(2,1)S(1)}, bf16[128,896]{1,0:T(8,128)(2,1)S(1)}, u32[]{:S(2)}, u32[]{:S(2)}) %collective-permute-start.26) | collective-permute-done | bytes 229408 | tf_op jit(solution)/shard_map/ppermute | solution.py:28
  137.7 1.3 collective-permute-start.25
  139.6 1.4 collective-permute-start.32
  141.1 0.5 collective-permute-start.33
  141.6 2.0 %collective-permute-start.28 = (bf16[128,768]{1,0:T(8,128)(2,1)S(1)}, bf16[128,768]{1,0:T(8,128)(2,1)S(1)}, u32[]{:S(2)}, u32[]{:S(2)}) collective-permute-start(bf16[128,768]{1,0:T(8,128)(2,1)S(1)} %get-tuple-element.94.refs_6_), channel_id=1, source_target_pairs={{0,8},{8,16},{16,24},{24,0},{1,9},{9,17},{17,25},{25,1},{2,10},{10... | collective-permute-start | bytes 589832 | tf_op jit(solution)/shard_map/ppermute | solution.py:23
  143.7 2.2 %collective-permute-done.25.refs_7_ = bf16[128,512]{1,0:T(8,128)(2,1)S(1)} collective-permute-done((bf16[128,512]{1,0:T(8,128)(2,1)S(1)}, bf16[128,512]{1,0:T(8,128)(2,1)S(1)}, u32[]{:S(2)}, u32[]{:S(2)}) %collective-permute-start.25) | collective-permute-done | bytes 131104 | tf_op jit(solution)/shard_map/ppermute | solution.py:23
  146.1 1.2 collective-permute-start.34
  147.2 3.9 %collective-permute-done.28 = bf16[128,768]{1,0:T(8,128)(2,1)S(1)} collective-permute-done((bf16[128,768]{1,0:T(8,128)(2,1)S(1)}, bf16[128,768]{1,0:T(8,128)(2,1)S(1)}, u32[]{:S(2)}, u32[]{:S(2)}) %collective-permute-start.28) | collective-permute-done | bytes 196640 | tf_op jit(solution)/shard_map/ppermute | solution.py:23
  151.2 2.2 %collective-permute-done.31 = bf16[128,768]{1,0:T(8,128)(2,1)S(1)} collective-permute-done((bf16[128,768]{1,0:T(8,128)(2,1)S(1)}, bf16[128,768]{1,0:T(8,128)(2,1)S(1)}, u32[]{:S(2)}, u32[]{:S(2)}) %collective-permute-start.31) | collective-permute-done | bytes 196640 | tf_op jit(solution)/shard_map/ppermute | solution.py:23
  153.5 1.4 collective-permute-done.34
  154.9 1.0 copy-done.10
  (64 shorter events, 2.3 us)
Async XLA Ops:
  2.5 18.7 %collective-permute-start.1 = (bf16[64,5120]{1,0:T(8,128)(2,1)}, bf16[64,5120]{1,0:T(8,128)(2,1)S(1)}, u32[]{:S(2)}, u32[]{:S(2)}) collective-permute-start(bf16[64,5120]{1,0:T(8,128)(2,1)} %get-tuple-element.104), channel_id=1, source_target_pairs={{0,1},{1,0},{2,3},{3,2},{4,5},{5,4},{6,7},{7,6},{8,9},{9,8},{10,11... | collective-permute-start | bytes 1966088 | tf_op jit(solution)/shard_map/ppermute | solution.py:28
  5.4 19.8 %collective-permute-start.4 = (bf16[64,5120]{1,0:T(8,128)(2,1)}, bf16[64,5120]{1,0:T(8,128)(2,1)S(1)}, u32[]{:S(2)}, u32[]{:S(2)}) collective-permute-start(bf16[64,5120]{1,0:T(8,128)(2,1)} %get-tuple-element.103), channel_id=1, source_target_pairs={{0,4},{2,6},{4,0},{6,2},{1,5},{3,7},{5,1},{7,3},{8,12},{10,14},{12... | collective-permute-start | bytes 1966088 | tf_op jit(solution)/shard_map/ppermute | solution.py:28
  6.9 35.1 %collective-permute-start.2 = (bf16[64,5120]{1,0:T(8,128)(2,1)}, bf16[64,5120]{1,0:T(8,128)(2,1)}, u32[]{:S(2)}, u32[]{:S(2)}) collective-permute-start(bf16[64,5120]{1,0:T(8,128)(2,1)} %get-tuple-element.103), channel_id=1, source_target_pairs={{0,1},{1,0},{2,3},{3,2},{4,5},{5,4},{6,7},{7,6},{8,9},{9,8},{10,11... | collective-permute-start | bytes 1966088 | tf_op jit(solution)/shard_map/ppermute | solution.py:28
  7.5 34.5 %collective-permute-start.3 = (bf16[64,5120]{1,0:T(8,128)(2,1)}, bf16[64,5120]{1,0:T(8,128)(2,1)S(1)}, u32[]{:S(2)}, u32[]{:S(2)}) collective-permute-start(bf16[64,5120]{1,0:T(8,128)(2,1)} %get-tuple-element.104), channel_id=1, source_target_pairs={{0,4},{2,6},{4,0},{6,2},{1,5},{3,7},{5,1},{7,3},{8,12},{10,14},{12... | collective-permute-start | bytes 1966088 | tf_op jit(solution)/shard_map/ppermute | solution.py:28
  21.2 1.9 %copy-start.2 = (bf16[256,2,8,384]{3,2,1,0:T(8,128)(2,1)S(1)}, bf16[256,2,8,384]{3,2,1,0:T(8,128)(2,1)}, u32[]{:S(2)}) copy-start(bf16[256,2,8,384]{3,2,1,0:T(8,128)(2,1)} %reshape_squeeze.3.refs_0_) | copy-start | bytes 9437188
  23.1 2.1 %copy-start.3 = (bf16[256,2,8,384]{3,2,1,0:T(8,128)(2,1)S(1)}, bf16[256,2,8,384]{3,2,1,0:T(8,128)(2,1)}, u32[]{:S(2)}) copy-start(bf16[256,2,8,384]{3,2,1,0:T(8,128)(2,1)} %reshape_squeeze.3.refs_0_) | copy-start | bytes 9437188
  23.1 4.0 %copy-start.9 = (f32[1,1,3,5120]{3,1,2,0:T(1,128)S(1)}, f32[1,1,3,5120]{3,1,2,0:T(1,128)}, u32[]{:S(2)}) copy-start(f32[1,1,3,5120]{3,1,2,0:T(1,128)} %param.7) | copy-start | bytes 184324
  23.1 4.2 %copy-start = (bf16[1,1,128,5120]{3,2,1,0:T(8,128)(2,1)S(1)}, bf16[1,1,128,5120]{3,2,1,0:T(8,128)(2,1)}, u32[]{:S(2)}) copy-start(bf16[1,1,128,5120]{3,2,1,0:T(8,128)(2,1)} %param.6) | copy-start | bytes 3932164
  23.1 31.6 %collective-permute-start.5 = (bf16[64,5120]{1,0:T(8,128)(2,1)S(1)}, bf16[64,5120]{1,0:T(8,128)(2,1)}, u32[]{:S(2)}, u32[]{:S(2)}) collective-permute-start(bf16[64,5120]{1,0:T(8,128)(2,1)S(1)} %after.3.refs_0_), channel_id=1, source_target_pairs={{0,4},{2,6},{4,0},{6,2},{1,5},{3,7},{5,1},{7,3},{8,12},{10,14},{12... | collective-permute-start | bytes 1966088 | tf_op jit(solution)/shard_map/ppermute | solution.py:28
  25.2 30.0 %collective-permute-start.6 = (bf16[64,5120]{1,0:T(8,128)(2,1)S(1)}, bf16[64,5120]{1,0:T(8,128)(2,1)}, u32[]{:S(2)}, u32[]{:S(2)}) collective-permute-start(bf16[64,5120]{1,0:T(8,128)(2,1)S(1)} %after.4.refs_1_), channel_id=1, source_target_pairs={{0,1},{1,0},{2,3},{3,2},{4,5},{5,4},{6,7},{7,6},{8,9},{9,8},{10,11... | collective-permute-start | bytes 1966088 | tf_op jit(solution)/shard_map/ppermute | solution.py:28
  27.1 23.3 %collective-permute-start = (f32[1,1,3,5120]{3,2,1,0:T(4,128)S(1)}, f32[1,1,3,5120]{3,2,1,0:T(4,128)S(1)}, u32[]{:S(2)}, u32[]{:S(2)}) collective-permute-start(f32[1,1,3,5120]{3,2,1,0:T(4,128)S(1)} %copy.15), channel_id=1, source_target_pairs={{0,1},{1,0},{2,3},{3,2},{4,5},{5,4},{6,7},{7,6},{8,9},{9,8},{10,11... | collective-permute-start | bytes 184328 | tf_op jit(solution)/shard_map/ppermute | solution.py:28
  28.8 1.1 copy-start.6
  42.0 16.2 %collective-permute-start.7 = (bf16[128,5120]{1,0:T(8,128)(2,1)}, bf16[128,5120]{1,0:T(8,128)(2,1)}, u32[]{:S(2)}, u32[]{:S(2)}) collective-permute-start(bf16[128,5120]{1,0:T(8,128)(2,1)} %copy-done.6), channel_id=1, source_target_pairs={{0,2},{2,0},{4,6},{6,4},{1,3},{3,1},{5,7},{7,5},{8,10},{10,8},{12,... | collective-permute-start | bytes 3932168 | tf_op jit(solution)/shard_map/ppermute | solution.py:28
  42.0 0.9 copy-start.4
  42.0 47.9 %collective-permute-start.11 = (bf16[384,5120]{1,0:T(8,128)(2,1)}, bf16[384,5120]{1,0:T(8,128)(2,1)}, u32[]{:S(2)}, u32[]{:S(2)}) collective-permute-start(bf16[384,5120]{1,0:T(8,128)(2,1)} %bitcast.30), channel_id=1, source_target_pairs={{0,2},{2,0},{4,6},{6,4},{1,3},{3,1},{5,7},{7,5},{8,10},{10,8},{12,... | collective-permute-start | bytes 11796488 | tf_op jit(solution)/shard_map/ppermute | solution.py:28
  42.9 42.6 %all-to-all-start = ((bf16[8,256,768]{2,1,0:T(8,128)(2,1)}), bf16[8,256,768]{2,1,0:T(8,128)(2,1)}, u32[]{:S(2)}, u32[]{:S(2)}) async-start(bf16[8,256,768]{2,1,0:T(8,128)(2,1)} %after.5), calls=%async_computation | async-start | bytes 6291456 | tf_op jit(solution)/shard_map/all_to_all | solution.py:451
  50.4 2.8 %copy-start.5 = (bf16[64,5120]{1,0:T(8,128)(2,1)S(1)}, bf16[64,5120]{1,0:T(8,128)(2,1)}, u32[]{:S(2)}) copy-start(bf16[64,5120]{1,0:T(8,128)(2,1)} %copy-done.4) | copy-start | bytes 1966084
  53.0 5.2 %collective-permute-start.8 = (bf16[128,5120]{1,0:T(8,128)(2,1)S(1)}, bf16[128,5120]{1,0:T(8,128)(2,1)S(1)}, u32[]{:S(2)}, u32[]{:S(2)}) collective-permute-start(bf16[128,5120]{1,0:T(8,128)(2,1)S(1)} %modulated_norm.5.refs_1_), channel_id=1, source_target_pairs={{0,2},{2,0},{4,6},{6,4},{1,3},{3,1},{5,7},{7,5},{8,10},{10,8},{12,... | collective-permute-start | bytes 3932168 | tf_op jit(solution)/shard_map/ppermute | solution.py:28
  54.6 6.5 %copy-start.7 = (bf16[128,5120]{1,0:T(8,128)(2,1)S(1)}, bf16[128,5120]{1,0:T(8,128)(2,1)}, u32[]{:S(2)}) copy-start(bf16[128,5120]{1,0:T(8,128)(2,1)} %copy-done.6) | copy-start | bytes 3932164
  54.7 3.6 %collective-permute-start.9 = (bf16[128,5120]{1,0:T(8,128)(2,1)S(1)}, bf16[128,5120]{1,0:T(8,128)(2,1)S(1)}, u32[]{:S(2)}, u32[]{:S(2)}) collective-permute-start(bf16[128,5120]{1,0:T(8,128)(2,1)S(1)} %modulated_norm.6.refs_2_), channel_id=1, source_target_pairs={{0,2},{2,0},{4,6},{6,4},{1,3},{3,1},{5,7},{7,5},{8,10},{10,8},{12,... | collective-permute-start | bytes 3932168 | tf_op jit(solution)/shard_map/ppermute | solution.py:28
  58.0 3.1 %collective-permute-start.10 = (bf16[128,5120]{1,0:T(8,128)(2,1)S(1)}, bf16[128,5120]{1,0:T(8,128)(2,1)S(1)}, u32[]{:S(2)}, u32[]{:S(2)}) collective-permute-start(bf16[128,5120]{1,0:T(8,128)(2,1)S(1)} %modulated_norm.7.refs_3_), channel_id=1, source_target_pairs={{0,2},{2,0},{4,6},{6,4},{1,3},{3,1},{5,7},{7,5},{8,10},{10,8},{12,... | collective-permute-start | bytes 3932168 | tf_op jit(solution)/shard_map/ppermute | solution.py:28
  61.1 24.3 %copy-start.8 = (s32[1,4,6]{2,1,0:T(4,128)S(1)}, s32[1,4,6]{2,1,0:T(4,128)}, u32[]{:S(2)}) copy-start(s32[1,4,6]{2,1,0:T(4,128)} %param.11) | copy-start | bytes 292
  85.4 4.5 %copy-start.1 = (bf16[1,384,5120]{2,1,0:T(8,128)(2,1)S(1)}, bf16[1,384,5120]{2,1,0:T(8,128)(2,1)}, u32[]{:S(2)}) copy-start(bf16[1,384,5120]{2,1,0:T(8,128)(2,1)} %param.9) | copy-start | bytes 11796484
  89.8 3.6 %collective-permute-start.12 = (bf16[512,384]{1,0:T(8,128)(2,1)S(1)}, bf16[512,384]{1,0:T(8,128)(2,1)S(1)}, u32[]{:S(2)}, u32[]{:S(2)}) collective-permute-start(bf16[512,384]{1,0:T(8,128)(2,1)S(1)} %get-tuple-element.56.refs_2_), channel_id=1, source_target_pairs={{0,2},{2,0},{4,6},{6,4},{1,3},{3,1},{5,7},{7,5},{8,10},{10,8},{12,... | collective-permute-start | bytes 1179656 | tf_op jit(solution)/shard_map/ppermute | solution.py:28
  94.9 10.6 %collective-permute-start.13 = (bf16[128,1280]{1,0:T(8,128)(2,1)S(1)}, bf16[128,1280]{1,0:T(8,128)(2,1)S(1)}, u32[]{:S(2)}, u32[]{:S(2)}) collective-permute-start(bf16[128,1280]{1,0:T(8,128)(2,1)S(1)} %get-tuple-element.59), channel_id=1, source_target_pairs={{0,1},{1,0},{2,3},{3,2},{4,5},{5,4},{6,7},{7,6},{8,9},{9,8},{10,11... | collective-permute-start | bytes 983048 | tf_op jit(solution)/shard_map/ppermute | solution.py:28
  95.7 10.5 %collective-permute-start.14 = (bf16[128,1280]{1,0:T(8,128)(2,1)S(1)}, bf16[128,1280]{1,0:T(8,128)(2,1)S(1)}, u32[]{:S(2)}, u32[]{:S(2)}) collective-permute-start(bf16[128,1280]{1,0:T(8,128)(2,1)S(1)} %get-tuple-element.60), channel_id=1, source_target_pairs={{0,4},{2,6},{4,0},{6,2},{1,5},{3,7},{5,1},{7,3},{8,12},{10,14},{12... | collective-permute-start | bytes 983048 | tf_op jit(solution)/shard_map/ppermute | solution.py:28
  99.5 12.9 %collective-permute-start.17 = (bf16[128,1280]{1,0:T(8,128)(2,1)S(1)}, bf16[128,1280]{1,0:T(8,128)(2,1)S(1)}, u32[]{:S(2)}, u32[]{:S(2)}) collective-permute-start(bf16[128,1280]{1,0:T(8,128)(2,1)S(1)} %get-tuple-element.70), channel_id=1, source_target_pairs={{0,1},{1,0},{2,3},{3,2},{4,5},{5,4},{6,7},{7,6},{8,9},{9,8},{10,11... | collective-permute-start | bytes 983048 | tf_op jit(solution)/shard_map/ppermute | solution.py:28
  100.4 12.9 %collective-permute-start.18 = (bf16[128,1280]{1,0:T(8,128)(2,1)S(1)}, bf16[128,1280]{1,0:T(8,128)(2,1)S(1)}, u32[]{:S(2)}, u32[]{:S(2)}) collective-permute-start(bf16[128,1280]{1,0:T(8,128)(2,1)S(1)} %get-tuple-element.71), channel_id=1, source_target_pairs={{0,4},{2,6},{4,0},{6,2},{1,5},{3,7},{5,1},{7,3},{8,12},{10,14},{12... | collective-permute-start | bytes 983048 | tf_op jit(solution)/shard_map/ppermute | solution.py:28
  108.1 10.7 %collective-permute-start.15 = (bf16[128,1152]{1,0:T(8,128)(2,1)S(1)}, bf16[128,1152]{1,0:T(8,128)(2,1)S(1)}, u32[]{:S(2)}, u32[]{:S(2)}) collective-permute-start(bf16[128,1152]{1,0:T(8,128)(2,1)S(1)} %get-tuple-element.64), channel_id=1, source_target_pairs={{0,1},{1,0},{2,3},{3,2},{4,5},{5,4},{6,7},{7,6},{8,9},{9,8},{10,11... | collective-permute-start | bytes 884744 | tf_op jit(solution)/shard_map/ppermute | solution.py:28
  109.4 10.1 %collective-permute-start.16 = (bf16[128,1152]{1,0:T(8,128)(2,1)S(1)}, bf16[128,1152]{1,0:T(8,128)(2,1)S(1)}, u32[]{:S(2)}, u32[]{:S(2)}) collective-permute-start(bf16[128,1152]{1,0:T(8,128)(2,1)S(1)} %get-tuple-element.65), channel_id=1, source_target_pairs={{0,4},{2,6},{4,0},{6,2},{1,5},{3,7},{5,1},{7,3},{8,12},{10,14},{12... | collective-permute-start | bytes 884744 | tf_op jit(solution)/shard_map/ppermute | solution.py:28
  115.6 11.4 %collective-permute-start.20 = (bf16[128,1408]{1,0:T(8,128)(2,1)S(1)}, bf16[128,1408]{1,0:T(8,128)(2,1)S(1)}, u32[]{:S(2)}, u32[]{:S(2)}) collective-permute-start(bf16[128,1408]{1,0:T(8,128)(2,1)S(1)} %get-tuple-element.75), channel_id=1, source_target_pairs={{0,1},{1,0},{2,3},{3,2},{4,5},{5,4},{6,7},{7,6},{8,9},{9,8},{10,11... | collective-permute-start | bytes 1081352 | tf_op jit(solution)/shard_map/ppermute | solution.py:28
  117.0 10.8 %collective-permute-start.21 = (bf16[128,1408]{1,0:T(8,128)(2,1)S(1)}, bf16[128,1408]{1,0:T(8,128)(2,1)S(1)}, u32[]{:S(2)}, u32[]{:S(2)}) collective-permute-start(bf16[128,1408]{1,0:T(8,128)(2,1)S(1)} %get-tuple-element.76), channel_id=1, source_target_pairs={{0,4},{2,6},{4,0},{6,2},{1,5},{3,7},{5,1},{7,3},{8,12},{10,14},{12... | collective-permute-start | bytes 1081352 | tf_op jit(solution)/shard_map/ppermute | solution.py:28
  121.8 10.7 %collective-permute-start.19 = (bf16[128,1280]{1,0:T(8,128)(2,1)S(1)}, bf16[128,1280]{1,0:T(8,128)(2,1)S(1)}, u32[]{:S(2)}, u32[]{:S(2)}) collective-permute-start(bf16[128,1280]{1,0:T(8,128)(2,1)S(1)} %get-tuple-element.74.refs_12_), channel_id=1, source_target_pairs={{0,8},{8,16},{16,24},{24,0},{1,9},{9,17},{17,25},{25,1},{2,10},{10... | collective-permute-start | bytes 983048 | tf_op jit(solution)/shard_map/ppermute | solution.py:23
  123.5 9.1 %collective-permute-start.23 = (bf16[128,1024]{1,0:T(8,128)(2,1)S(1)}, bf16[128,1024]{1,0:T(8,128)(2,1)S(1)}, u32[]{:S(2)}, u32[]{:S(2)}) collective-permute-start(bf16[128,1024]{1,0:T(8,128)(2,1)S(1)} %get-tuple-element.81), channel_id=1, source_target_pairs={{0,1},{1,0},{2,3},{3,2},{4,5},{5,4},{6,7},{7,6},{8,9},{9,8},{10,11... | collective-permute-start | bytes 786440 | tf_op jit(solution)/shard_map/ppermute | solution.py:28
  124.5 8.0 %collective-permute-start.24 = (bf16[128,1024]{1,0:T(8,128)(2,1)S(1)}, bf16[128,1024]{1,0:T(8,128)(2,1)S(1)}, u32[]{:S(2)}, u32[]{:S(2)}) collective-permute-start(bf16[128,1024]{1,0:T(8,128)(2,1)S(1)} %get-tuple-element.82), channel_id=1, source_target_pairs={{0,4},{2,6},{4,0},{6,2},{1,5},{3,7},{5,1},{7,3},{8,12},{10,14},{12... | collective-permute-start | bytes 786440 | tf_op jit(solution)/shard_map/ppermute | solution.py:28
  129.6 9.9 %collective-permute-start.22 = (bf16[128,1280]{1,0:T(8,128)(2,1)S(1)}, bf16[128,1280]{1,0:T(8,128)(2,1)S(1)}, u32[]{:S(2)}, u32[]{:S(2)}) collective-permute-start(bf16[128,1280]{1,0:T(8,128)(2,1)S(1)} %get-tuple-element.80.refs_8_), channel_id=1, source_target_pairs={{0,8},{8,16},{16,24},{24,0},{1,9},{9,17},{17,25},{25,1},{2,10},{10... | collective-permute-start | bytes 983048 | tf_op jit(solution)/shard_map/ppermute | solution.py:23
  131.3 6.5 %collective-permute-start.26 = (bf16[128,896]{1,0:T(8,128)(2,1)S(1)}, bf16[128,896]{1,0:T(8,128)(2,1)S(1)}, u32[]{:S(2)}, u32[]{:S(2)}) collective-permute-start(bf16[128,896]{1,0:T(8,128)(2,1)S(1)} %get-tuple-element.88), channel_id=1, source_target_pairs={{0,1},{1,0},{2,3},{3,2},{4,5},{5,4},{6,7},{7,6},{8,9},{9,8},{10,11... | collective-permute-start | bytes 688136 | tf_op jit(solution)/shard_map/ppermute | solution.py:28
  132.5 7.0 %collective-permute-start.27 = (bf16[128,896]{1,0:T(8,128)(2,1)S(1)}, bf16[128,896]{1,0:T(8,128)(2,1)S(1)}, u32[]{:S(2)}, u32[]{:S(2)}) collective-permute-start(bf16[128,896]{1,0:T(8,128)(2,1)S(1)} %get-tuple-element.89), channel_id=1, source_target_pairs={{0,4},{2,6},{4,0},{6,2},{1,5},{3,7},{5,1},{7,3},{8,12},{10,14},{12... | collective-permute-start | bytes 688136 | tf_op jit(solution)/shard_map/ppermute | solution.py:28
  132.7 8.9 %collective-permute-start.29 = (bf16[128,384]{1,0:T(8,128)(2,1)S(1)}, bf16[128,384]{1,0:T(8,128)(2,1)S(1)}, u32[]{:S(2)}, u32[]{:S(2)}) collective-permute-start(bf16[128,384]{1,0:T(8,128)(2,1)S(1)} %get-tuple-element.95), channel_id=1, source_target_pairs={{0,1},{1,0},{2,3},{3,2},{4,5},{5,4},{6,7},{7,6},{8,9},{9,8},{10,11... | collective-permute-start | bytes 294920 | tf_op jit(solution)/shard_map/ppermute | solution.py:28
  134.6 9.0 %collective-permute-start.30 = (bf16[128,384]{1,0:T(8,128)(2,1)S(1)}, bf16[128,384]{1,0:T(8,128)(2,1)S(1)}, u32[]{:S(2)}, u32[]{:S(2)}) collective-permute-start(bf16[128,384]{1,0:T(8,128)(2,1)S(1)} %get-tuple-element.96), channel_id=1, source_target_pairs={{0,4},{2,6},{4,0},{6,2},{1,5},{3,7},{5,1},{7,3},{8,12},{10,14},{12... | collective-permute-start | bytes 294920 | tf_op jit(solution)/shard_map/ppermute | solution.py:28
  137.7 8.2 %collective-permute-start.25 = (bf16[128,512]{1,0:T(8,128)(2,1)S(1)}, bf16[128,512]{1,0:T(8,128)(2,1)S(1)}, u32[]{:S(2)}, u32[]{:S(2)}) collective-permute-start(bf16[128,512]{1,0:T(8,128)(2,1)S(1)} %get-tuple-element.87.refs_8_), channel_id=1, source_target_pairs={{0,8},{8,16},{16,24},{24,0},{1,9},{9,17},{17,25},{25,1},{2,10},{10... | collective-permute-start | bytes 393224 | tf_op jit(solution)/shard_map/ppermute | solution.py:23
  139.6 6.4 %collective-permute-start.32 = (bf16[128,256]{1,0:T(8,128)(2,1)S(1)}, bf16[128,256]{1,0:T(8,128)(2,1)S(1)}, u32[]{:S(2)}, u32[]{:S(2)}) collective-permute-start(bf16[128,256]{1,0:T(8,128)(2,1)S(1)} %get-tuple-element.99), channel_id=1, source_target_pairs={{0,1},{1,0},{2,3},{3,2},{4,5},{5,4},{6,7},{7,6},{8,9},{9,8},{10,11... | collective-permute-start | bytes 196616 | tf_op jit(solution)/shard_map/ppermute | solution.py:28
  141.1 4.9 %collective-permute-start.33 = (bf16[128,256]{1,0:T(8,128)(2,1)S(1)}, bf16[128,256]{1,0:T(8,128)(2,1)S(1)}, u32[]{:S(2)}, u32[]{:S(2)}) collective-permute-start(bf16[128,256]{1,0:T(8,128)(2,1)S(1)} %get-tuple-element.100), channel_id=1, source_target_pairs={{0,4},{2,6},{4,0},{6,2},{1,5},{3,7},{5,1},{7,3},{8,12},{10,14},{12... | collective-permute-start | bytes 196616 | tf_op jit(solution)/shard_map/ppermute | solution.py:28
  141.6 9.6 %collective-permute-start.28 = (bf16[128,768]{1,0:T(8,128)(2,1)S(1)}, bf16[128,768]{1,0:T(8,128)(2,1)S(1)}, u32[]{:S(2)}, u32[]{:S(2)}) collective-permute-start(bf16[128,768]{1,0:T(8,128)(2,1)S(1)} %get-tuple-element.94.refs_6_), channel_id=1, source_target_pairs={{0,8},{8,16},{16,24},{24,0},{1,9},{9,17},{17,25},{25,1},{2,10},{10... | collective-permute-start | bytes 589832 | tf_op jit(solution)/shard_map/ppermute | solution.py:23
  145.9 7.5 %collective-permute-start.31 = (bf16[128,768]{1,0:T(8,128)(2,1)S(1)}, bf16[128,768]{1,0:T(8,128)(2,1)S(1)}, u32[]{:S(2)}, u32[]{:S(2)}) collective-permute-start(bf16[128,768]{1,0:T(8,128)(2,1)S(1)} %sum_stage.18.refs_6_), channel_id=1, source_target_pairs={{0,8},{8,16},{16,24},{24,0},{1,9},{9,17},{17,25},{25,1},{2,10},{10... | collective-permute-start | bytes 589832 | tf_op jit(solution)/shard_map/ppermute | solution.py:23
  146.1 8.8 %collective-permute-start.34 = (bf16[128,512]{1,0:T(8,128)(2,1)S(1)}, bf16[128,512]{1,0:T(8,128)(2,1)S(1)}, u32[]{:S(2)}, u32[]{:S(2)}) collective-permute-start(bf16[128,512]{1,0:T(8,128)(2,1)S(1)} %sum_stage.19), channel_id=1, source_target_pairs={{0,8},{8,16},{16,24},{24,0},{1,9},{9,17},{17,25},{25,1},{2,10},{10... | collective-permute-start | bytes 393224 | tf_op jit(solution)/shard_map/ppermute | solution.py:23
  154.9 1.1 copy-start.10

commit v17 on v16

--- a/solution.py
+++ b/solution.py
@@ -188,15 +188,15 @@
             mixed[:, :HD] / mixed[:, HD:]
         ).astype(jnp.bfloat16)
 
-    waiting = None
+    waiting = []
     for head in range(heads):
         before_head(head)
         for block in range(blocks):
-            scores = scores_of(head, block)
-            if waiting is not None:
-                finish(*waiting)
-            waiting = head, block, scores
-    finish(*waiting)
+            waiting.append((head, block, scores_of(head, block)))
+            if len(waiting) > 2:
+                finish(*waiting.pop(0))
+    for unit in waiting:
+        finish(*unit)
 
 
 def attend_first_kernel(
@@ -479,16 +479,13 @@
         if middle:
             operands["first_kept"], operands["second_kept"] = kept.pop(index)
         if final:
-            operands["first_left"], operands["second_left"] = left.pop(index - 2)
-        outs = stage(
-            operands,
-            earlier,
-            chunks,
-            index,
-            fresh,
-            middle,
-            final,
-        )
+            last = {name: operands[name] for name in ("rows", "across", "along")}
+            last["first_left"], last["second_left"] = left.pop(index - 2)
+            outs = stage(last, earlier, chunks, index, False, False, True)
+            arrivals.append(from_behind(outs["done_out"], "pipe", 1))
+            earlier = [outs["done_out"]]
+        if fresh or middle:
+            outs = stage(operands, earlier, chunks, index, fresh, middle, False)
         if "across_out" in outs:
             flights[index + 2] = (
                 from_partner(outs["across_out"], "cfg", 1),
@@ -498,8 +495,6 @@
             kept[index + 2] = (outs["first_kept_out"], outs["second_kept_out"])
         if middle:
             left[index] = (outs["first_left_out"], outs["second_left_out"])
-        if final:
-            arrivals.append(from_behind(outs["done_out"], "pipe", 1))
         earlier = [list(outs.values())[-1]] + (arrivals[-2:-1] if 3 <= index < count else [])
     return jnp.concatenate(arrivals, axis=1)[None, None]
 

time: 157 us -> 155 us (0.987)
  waiting for transfers between devices: 41.9 us -> 37.5 us
  starting transfers between devices: 38.3 us -> 41.2 us
    ppermute x6, waiting for transfers between devices: 9.82 us -> 4.84 us  [from_behind(): return lax.ppermute(x, axis, [(i, (i + by) % count) for i in range(count)])]
    ppermute x6, starting transfers between devices: 7.85 us -> 10.1 us  [from_behind(): return lax.ppermute(x, axis, [(i, (i + by) % count) for i in range(count)])]
    pallas_call x10 -> x14, Pallas kernels: 12.7 us -> 12.7 us  [stage(): pl.pallas_call(functools.partial(stage_kernel, parts=parts, start=start,...]
  transfers between devices with their start and end apart: 36 -> 36, of which waited for: 19 -> 20; matrix products, arithmetic and copies ran while one was open for 13% -> 13% of each run, Pallas kernels for 30% -> 30%
where the time goes in v17:
time: 155 us; the launch traced here: 154 us
  Pallas kernels  48.2 us (31%)
  starting transfers between devices  41.2 us (27%)
  waiting for transfers between devices  37.5 us (24%)
  local copies, waits for them, and re-layouts  27.1 us (17%)
    ppermute x29, waiting for transfers between devices, from_partner(): return lax.ppermute(value, axis, pairs)  27.6 us
    ppermute x29, starting transfers between devices, from_partner(): return lax.ppermute(value, axis, pairs)  26.4 us
    pallas_call x1, Pallas kernels, project(): pl.pallas_call(functools.partial(project_kernel, blocks=len(blocks)), gri...  19.2 us
    pallas_call x14, Pallas kernels, stage(): pl.pallas_call(functools.partial(stage_kernel, parts=parts, start=start,...  12.7 us
    ppermute x6, starting transfers between devices, from_behind(): return lax.ppermute(x, axis, [(i, (i + by) % count) for i in range(count)])  10.1 us
    pallas_call x4, Pallas kernels, modulated_norm(): pl.pallas_call(norm_kernel, in_specs=[pl.BlockSpec(memory_space=pltpu.VME...  8.49 us
    reshape x1, local copies, waits for them, and re-layouts, per_device(): unpacked.transpose(2, 0, 1, 3).reshape(devices, context_rows, 2 * width)  8.06 us
    another operation x1, local copies, waits for them, and re-layouts, per_device(): unpacked = stale_cache[0, 0].reshape(context_rows, 2, devices, width)  8 us
  transfers between devices with their start and end apart: 36, of which 20 were waited for; matrix products, arithmetic and copies ran while one was open for 13% of the time, Pallas kernels for 30%

profile of v17, /device:TPU:0, one launch (start us, length us, event | category | flops | bytes accessed | tf_op | source)
XLA Modules:
  0.0 154.4 jit_solution(8117521081674395534)
XLA Ops:
  0.0 2.5 %slice_bitcast_fusion = (bf16[64,5120]{1,0:T(8,128)(2,1)}, bf16[64,5120]{1,0:T(8,128)(2,1)}) fusion(bf16[1,1,128,5120]{3,2,1,0:T(8,128)(2,1)} %param.6), kind=kLoop, calls=%fused_computation | loop fusion | bytes 2621440 | tf_op jit(solution)/shard_map/slice | solution.py:435
  2.5 2.9 %collective-permute-start.1 = (bf16[64,5120]{1,0:T(8,128)(2,1)}, bf16[64,5120]{1,0:T(8,128)(2,1)S(1)}, u32[]{:S(2)}, u32[]{:S(2)}) collective-permute-start(bf16[64,5120]{1,0:T(8,128)(2,1)} %get-tuple-element.96), channel_id=1, source_target_pairs={{0,1},{1,0},{2,3},{3,2},{4,5},{5,4},{6,7},{7,6},{8,9},{9,8},{10,11... | collective-permute-start | bytes 1966088 | tf_op jit(solution)/shard_map/ppermute | solution.py:28
  5.4 1.5 collective-permute-start.4
  6.9 0.5 collective-permute-start.2
  7.5 8.0 %reshape_squeeze.3.refs_0_ = bf16[256,2,8,384]{3,2,1,0:T(8,128)(2,1)} reshape(bf16[1,1,256,2,3072]{4,3,2,1,0:T(2,128)(2,1)} %param.10) | data formatting | bytes 6291456 | tf_op jit(solution)/shard_map/reshape;squeeze | solution.py:432
  15.5 5.7 %collective-permute-done.1.value_ref = bf16[64,5120]{1,0:T(8,128)(2,1)S(1)} collective-permute-done((bf16[64,5120]{1,0:T(8,128)(2,1)}, bf16[64,5120]{1,0:T(8,128)(2,1)S(1)}, u32[]{:S(2)}, u32[]{:S(2)}) %collective-permute-start.1) | collective-permute-done | bytes 655392 | tf_op jit(solution)/shard_map/ppermute | solution.py:28
  21.2 1.9 %copy-done.2 = bf16[256,2,8,384]{3,2,1,0:T(8,128)(2,1)S(1)} copy-done((bf16[256,2,8,384]{3,2,1,0:T(8,128)(2,1)S(1)}, bf16[256,2,8,384]{3,2,1,0:T(8,128)(2,1)}, u32[]{:S(2)}) %copy-start.2) | copy-done | bytes 3145752
  23.1 2.1 %collective-permute-start.5 = (bf16[64,5120]{1,0:T(8,128)(2,1)S(1)}, bf16[64,5120]{1,0:T(8,128)(2,1)}, u32[]{:S(2)}, u32[]{:S(2)}) collective-permute-start(bf16[64,5120]{1,0:T(8,128)(2,1)S(1)} %after.3.refs_0_), channel_id=1, source_target_pairs={{0,4},{2,6},{4,0},{6,2},{1,5},{3,7},{5,1},{7,3},{8,12},{10,14},{12... | collective-permute-start | bytes 1966088 | tf_op jit(solution)/shard_map/ppermute | solution.py:28
  25.2 1.8 %collective-permute-start.6 = (bf16[64,5120]{1,0:T(8,128)(2,1)S(1)}, bf16[64,5120]{1,0:T(8,128)(2,1)}, u32[]{:S(2)}, u32[]{:S(2)}) collective-permute-start(bf16[64,5120]{1,0:T(8,128)(2,1)S(1)} %after.4.refs_1_), channel_id=1, source_target_pairs={{0,1},{1,0},{2,3},{3,2},{4,5},{5,4},{6,7},{7,6},{8,9},{9,8},{10,11... | collective-permute-start | bytes 1966088 | tf_op jit(solution)/shard_map/ppermute | solution.py:28
  27.3 1.5 modulated_norm.4.refs_0_
  28.8 1.0 copy-done.6
  29.9 4.1 %copy.11 = bf16[8,256,2,384]{3,2,1,0:T(2,128)(2,1)} copy(bf16[8,256,2,384]{3,0,2,1:T(8,128)(2,1)S(1)} %bitcast.41) | data formatting | bytes 6291456 | tf_op jit(solution)/shard_map/transpose | solution.py:433
  33.9 8.1 %reshape.10.value_ref = bf16[8,256,768]{2,1,0:T(8,128)(2,1)} reshape(bf16[8,256,2,384]{3,2,1,0:T(2,128)(2,1)} %copy.11) | data formatting | bytes 6291456 | tf_op jit(solution)/shard_map/reshape | solution.py:433
  42.9 4.6 %all-to-all-start = ((bf16[8,256,768]{2,1,0:T(8,128)(2,1)}), bf16[8,256,768]{2,1,0:T(8,128)(2,1)}, u32[]{:S(2)}, u32[]{:S(2)}) async-start(bf16[8,256,768]{2,1,0:T(8,128)(2,1)} %after.5), calls=%async_computation | async-start | bytes 6291456 | tf_op jit(solution)/shard_map/all_to_all | solution.py:451
  47.5 2.9 %collective-permute-done = f32[1,1,3,5120]{3,2,1,0:T(4,128)S(1)} collective-permute-done((f32[1,1,3,5120]{3,2,1,0:T(4,128)S(1)}, f32[1,1,3,5120]{3,2,1,0:T(4,128)S(1)}, u32[]{:S(2)}, u32[]{:S(2)}) %collective-permute-start) | collective-permute-done | bytes 61472 | tf_op jit(solution)/shard_map/ppermute | solution.py:28
  50.4 2.7 %modulated_norm.5.refs_1_ = bf16[128,5120]{1,0:T(8,128)(2,1)S(1)} custom-call(bf16[64,5120]{1,0:T(8,128)(2,1)S(1)} %after.3.refs_0_, bf16[64,5120]{1,0:T(8,128)(2,1)} %collective-permute-done.2.refs_1_.refs_0_, f32[3,5120]{1,0:T(4,128)S(1)} %bitcast.44), custom_call_target="tpu_custom_call" | custom-call | flops 1 | bytes 1 | tf_op jit(solution)/shard_map/modulated_norm/pallas_call | solution.py:55
  53.1 1.5 modulated_norm.6.refs_2_
  54.7 0.6 collective-permute-start.9
  55.2 2.8 %modulated_norm.7.refs_3_ = bf16[128,5120]{1,0:T(8,128)(2,1)S(1)} custom-call(bf16[64,5120]{1,0:T(8,128)(2,1)} %collective-permute-done.5.refs_0_, bf16[64,5120]{1,0:T(8,128)(2,1)} %collective-permute-done.6.refs_1_, f32[3,5120]{1,0:T(4,128)S(1)} %bitcast.45), custom_call_target="tpu_custom_call" | custom-call | flops 1 | bytes 1 | tf_op jit(solution)/shard_map/modulated_norm/pallas_call | solution.py:55
  58.3 2.9 %collective-permute-done.10.refs_7_ = bf16[128,5120]{1,0:T(8,128)(2,1)S(1)} collective-permute-done((bf16[128,5120]{1,0:T(8,128)(2,1)S(1)}, bf16[128,5120]{1,0:T(8,128)(2,1)S(1)}, u32[]{:S(2)}, u32[]{:S(2)}) %collective-permute-start.10) | collective-permute-done | bytes 1310752 | tf_op jit(solution)/shard_map/ppermute | solution.py:28
  61.1 19.2 %project_heads.1.heads_in = bf16[48,1024,128]{2,1,0:T(8,128)(2,1)} custom-call(bf16[128,5120]{1,0:T(8,128)(2,1)S(1)} %copy-done.7, bf16[128,5120]{1,0:T(8,128)(2,1)S(1)} %modulated_norm.5.refs_1_, bf16[128,5120]{1,0:T(8,128)(2,1)S(1)} %modulated_norm.6.refs_2_, bf16[128,5120]{1,0:T(8,128)(2,1)S(1)} %modulated_norm.7.refs_3_, ...), custom_call_target="tpu_custom_call" | custom-call | flops 12079595520 | bytes 22282240 | tf_op jit(solution)/shard_map/project_heads/pallas_call | solution.py:124
  80.3 5.1 %all-to-all-done = bf16[8,256,768]{2,1,0:T(8,128)(2,1)} async-done(((bf16[8,256,768]{2,1,0:T(8,128)(2,1)}), bf16[8,256,768]{2,1,0:T(8,128)(2,1)}, u32[]{:S(2)}, u32[]{:S(2)}) %all-to-all-start) | async-done | bytes 3145760 | tf_op jit(solution)/shard_map/all_to_all | solution.py:451
  85.4 4.3 %attend_first.1 = (bf16[512,384]{1,0:T(8,128)(2,1)S(1)}, bf16[3,1024,128]{2,1,0:T(8,128)(2,1)S(1)}, bf16[6,3072,128]{2,1,0:T(8,128)(2,1)S(1)}) custom-call(s32[4,6]{1,0:T(4,128)S(1)} %bitcast.46, bf16[48,1024,128]{2,1,0:T(8,128)(2,1)} %project_heads.1.heads_in, bf16[2048,768]{1,0:T(8,128)(2,1)} %bitcast.9.context_in), custom_call_target="tpu_custom_call" | custom-call | flops 1 | bytes 1 | tf_op jit(solution)/shard_map/attend_first/pallas_call | solution.py:233
  89.9 3.5 %attend_second.1 = (bf16[512,384]{1,0:T(8,128)(2,1)S(1)}, bf16[768,1280]{1,0:T(8,128)(2,1)S(1)}) custom-call(s32[4,6]{1,0:T(4,128)S(1)} %bitcast.47, bf16[3,1024,128]{2,1,0:T(8,128)(2,1)S(1)} %get-tuple-element.50.queries_ref, bf16[6,3072,128]{2,1,0:T(8,128)(2,1)S(1)} %get-tuple-element.51.pool_ref, bf16[384,5120]{1,0:T(8,128)(2,1)S(1)} %bitcast.35, ...), custom_call_target="tpu_custom_call" | custom-call | flops 1 | bytes 1 | tf_op jit(solution)/shard_map/attend_second/pallas_call | solution.py:272
  93.4 1.4 sum_stage.14
  94.9 0.8 collective-permute-start.13
  95.7 1.1 collective-permute-start.14
  96.8 2.7 %sum_stage.15 = (bf16[128,1280]{1,0:T(8,128)(2,1)S(1)}, bf16[128,1280]{1,0:T(8,128)(2,1)S(1)}, f32[2,128,640]{2,1,0:T(8,128)S(1)}, f32[2,128,640]{2,1,0:T(8,128)S(1)}) custom-call(bf16[128,5120]{1,0:T(8,128)(2,1)S(1)} %bitcast.21, f32[2,5120]{1,0:T(2,128)S(1)} %pad_maximum_fusion.refs_3_.refs_1_, bf16[512,384]{1,0:T(8,128)(2,1)S(1)} %get-tuple-element.53.refs_2_, ...), custom_call_target="tpu_custom_call" | custom-call | flops 1 | bytes 1 | tf_op jit(solution)/shard_map/sum_stage/pallas_call | solution.py:397
  99.5 0.8 collective-permute-start.17
  100.3 1.4 collective-permute-start.18
  101.8 3.7 %collective-permute-done.13.refs_6_ = bf16[128,1280]{1,0:T(8,128)(2,1)S(1)} collective-permute-done((bf16[128,1280]{1,0:T(8,128)(2,1)S(1)}, bf16[128,1280]{1,0:T(8,128)(2,1)S(1)}, u32[]{:S(2)}, u32[]{:S(2)}) %collective-permute-start.13) | collective-permute-done | bytes 327712 | tf_op jit(solution)/shard_map/ppermute | solution.py:28
  105.4 0.8 collective-permute-done.14.refs_7_
  106.2 1.9 %sum_stage.16 = (bf16[128,1152]{1,0:T(8,128)(2,1)S(1)}, bf16[128,1152]{1,0:T(8,128)(2,1)S(1)}, f32[2,128,256]{2,1,0:T(8,128)S(1)}, f32[2,128,256]{2,1,0:T(8,128)...) custom-call(bf16[128,5120]{1,0:T(8,128)(2,1)S(1)} %bitcast.22, f32[2,5120]{1,0:T(2,128)S(1)} %pad_maximum_fusion.refs_3_.refs_1_, ...), custom_call_target="tpu_custom_call" | custom-call | flops 1 | bytes 1 | tf_op jit(solution)/shard_map/sum_stage/pallas_call | solution.py:397
  108.1 1.3 collective-permute-start.15
  109.4 0.6 collective-permute-start.16
  110.0 2.4 %collective-permute-done.17.refs_6_ = bf16[128,1280]{1,0:T(8,128)(2,1)S(1)} collective-permute-done((bf16[128,1280]{1,0:T(8,128)(2,1)S(1)}, bf16[128,1280]{1,0:T(8,128)(2,1)S(1)}, u32[]{:S(2)}, u32[]{:S(2)}) %collective-permute-start.17) | collective-permute-done | bytes 327712 | tf_op jit(solution)/shard_map/ppermute | solution.py:28
  112.5 0.8 collective-permute-done.18.refs_7_
  113.2 2.4 %sum_stage.17 = (bf16[128,1408]{1,0:T(8,128)(2,1)S(1)}, bf16[128,1408]{1,0:T(8,128)(2,1)S(1)}, f32[2,128,384]{2,1,0:T(8,128)S(1)}, f32[2,128,384]{2,1,0:T(8,128)...) custom-call(bf16[128,5120]{1,0:T(8,128)(2,1)S(1)} %bitcast.23, f32[2,5120]{1,0:T(2,128)S(1)} %pad_maximum_fusion.refs_3_.refs_1_, ...), custom_call_target="tpu_custom_call" | custom-call | flops 1 | bytes 1 | tf_op jit(solution)/shard_map/sum_stage/pallas_call | solution.py:397
  115.6 1.3 collective-permute-start.20
  117.0 0.6 collective-permute-start.21
  117.6 1.2 collective-permute-done.15.refs_1_.refs_6_
  118.8 0.8 collective-permute-done.16.refs_2_.refs_7_
  119.6 1.6 %collective-permute-start.19 = (bf16[128,1280]{1,0:T(8,128)(2,1)S(1)}, bf16[128,1280]{1,0:T(8,128)(2,1)S(1)}, u32[]{:S(2)}, u32[]{:S(2)}) collective-permute-start(bf16[128,1280]{1,0:T(8,128)(2,1)S(1)} %sum_stage.18.refs_10_), channel_id=1, source_target_pairs={{0,8},{8,16},{16,24},{24,0},{1,9},{9,17},{17,25},{25,1},{2,10},{10... | collective-permute-start | bytes 983048 | tf_op jit(solution)/shard_map/ppermute | solution.py:23
  121.2 2.2 %sum_stage.19 = (bf16[128,1024]{1,0:T(8,128)(2,1)S(1)}, bf16[128,1024]{1,0:T(8,128)(2,1)S(1)}, f32[2,128,384]{2,1,0:T(8,128)S(1)}, f32[2,128,384]{2,1,0:T(8,128)...) custom-call(bf16[128,5120]{1,0:T(8,128)(2,1)S(1)} %bitcast.25, f32[2,5120]{1,0:T(2,128)S(1)} %pad_maximum_fusion.refs_3_.refs_1_, ...), custom_call_target="tpu_custom_call" | custom-call | flops 1 | bytes 1 | tf_op jit(solution)/shard_map/sum_stage/pallas_call | solution.py:397
  123.4 1.1 collective-permute-start.23
  124.7 2.3 %collective-permute-done.20.refs_1_.refs_6_ = bf16[128,1408]{1,0:T(8,128)(2,1)S(1)} collective-permute-done((bf16[128,1408]{1,0:T(8,128)(2,1)S(1)}, bf16[128,1408]{1,0:T(8,128)(2,1)S(1)}, u32[]{:S(2)}, u32[]{:S(2)}) %collective-permute-start.20) | collective-permute-done | bytes 360480 | tf_op jit(solution)/shard_map/ppermute | solution.py:28
  127.0 0.7 collective-permute-done.21.refs_2_.refs_7_
  127.8 1.6 %collective-permute-start.22 = (bf16[128,1280]{1,0:T(8,128)(2,1)S(1)}, bf16[128,1280]{1,0:T(8,128)(2,1)S(1)}, u32[]{:S(2)}, u32[]{:S(2)}) collective-permute-start(bf16[128,1280]{1,0:T(8,128)(2,1)S(1)} %sum_stage.20.refs_10_), channel_id=1, source_target_pairs={{0,8},{8,16},{16,24},{24,0},{1,9},{9,17},{17,25},{25,1},{2,10},{10... | collective-permute-start | bytes 983048 | tf_op jit(solution)/shard_map/ppermute | solution.py:23
  129.5 1.7 %sum_stage.21 = (bf16[128,896]{1,0:T(8,128)(2,1)S(1)}, bf16[128,896]{1,0:T(8,128)(2,1)S(1)}, f32[2,128,256]{2,1,0:T(8,128)S(1)}, f32[2,128,256]{2,1,0:T(8,128)S(...) custom-call(bf16[128,5120]{1,0:T(8,128)(2,1)S(1)} %bitcast.27, f32[2,5120]{1,0:T(2,128)S(1)} %pad_maximum_fusion.refs_3_.refs_1_, ...), custom_call_target="tpu_custom_call" | custom-call | flops 1 | bytes 1 | tf_op jit(solution)/shard_map/sum_stage/pallas_call | solution.py:397
  131.2 1.2 collective-permute-start.26
  132.5 1.6 %collective-permute-start.25 = (bf16[128,512]{1,0:T(8,128)(2,1)S(1)}, bf16[128,512]{1,0:T(8,128)(2,1)S(1)}, u32[]{:S(2)}, u32[]{:S(2)}) collective-permute-start(bf16[128,512]{1,0:T(8,128)(2,1)S(1)} %sum_stage.22.refs_6_), channel_id=1, source_target_pairs={{0,8},{8,16},{16,24},{24,0},{1,9},{9,17},{17,25},{25,1},{2,10},{10... | collective-permute-start | bytes 393224 | tf_op jit(solution)/shard_map/ppermute | solution.py:23
  134.3 2.0 %collective-permute-start.29 = (bf16[128,384]{1,0:T(8,128)(2,1)S(1)}, bf16[128,384]{1,0:T(8,128)(2,1)S(1)}, u32[]{:S(2)}, u32[]{:S(2)}) collective-permute-start(bf16[128,384]{1,0:T(8,128)(2,1)S(1)} %get-tuple-element.86), channel_id=1, source_target_pairs={{0,1},{1,0},{2,3},{3,2},{4,5},{5,4},{6,7},{7,6},{8,9},{9,8},{10,11... | collective-permute-start | bytes 294920 | tf_op jit(solution)/shard_map/ppermute | solution.py:28
  136.3 2.0 %collective-permute-done.26.refs_1_.refs_2_ = bf16[128,896]{1,0:T(8,128)(2,1)S(1)} collective-permute-done((bf16[128,896]{1,0:T(8,128)(2,1)S(1)}, bf16[128,896]{1,0:T(8,128)(2,1)S(1)}, u32[]{:S(2)}, u32[]{:S(2)}) %collective-permute-start.26) | collective-permute-done | bytes 229408 | tf_op jit(solution)/shard_map/ppermute | solution.py:28
  138.3 1.1 collective-permute-start.30
  139.6 1.6 %collective-permute-start.28 = (bf16[128,768]{1,0:T(8,128)(2,1)S(1)}, bf16[128,768]{1,0:T(8,128)(2,1)S(1)}, u32[]{:S(2)}, u32[]{:S(2)}) collective-permute-start(bf16[128,768]{1,0:T(8,128)(2,1)S(1)} %sum_stage.24.refs_6_), channel_id=1, source_target_pairs={{0,8},{8,16},{16,24},{24,0},{1,9},{9,17},{17,25},{25,1},{2,10},{10... | collective-permute-start | bytes 589832 | tf_op jit(solution)/shard_map/ppermute | solution.py:23
  141.2 0.9 collective-permute-start.32
  142.2 1.2 collective-permute-start.33
  143.4 1.7 %collective-permute-start.31 = (bf16[128,768]{1,0:T(8,128)(2,1)S(1)}, bf16[128,768]{1,0:T(8,128)(2,1)S(1)}, u32[]{:S(2)}, u32[]{:S(2)}) collective-permute-start(bf16[128,768]{1,0:T(8,128)(2,1)S(1)} %sum_stage.26.refs_5_), channel_id=1, source_target_pairs={{0,8},{8,16},{16,24},{24,0},{1,9},{9,17},{17,25},{25,1},{2,10},{10... | collective-permute-start | bytes 589832 | tf_op jit(solution)/shard_map/ppermute | solution.py:23
  145.6 0.9 collective-permute-done.33.refs_2_
  146.5 1.9 %collective-permute-start.34 = (bf16[128,512]{1,0:T(8,128)(2,1)S(1)}, bf16[128,512]{1,0:T(8,128)(2,1)S(1)}, u32[]{:S(2)}, u32[]{:S(2)}) collective-permute-start(bf16[128,512]{1,0:T(8,128)(2,1)S(1)} %sum_stage.27), channel_id=1, source_target_pairs={{0,8},{8,16},{16,24},{24,0},{1,9},{9,17},{17,25},{25,1},{2,10},{10... | collective-permute-start | bytes 393224 | tf_op jit(solution)/shard_map/ppermute | solution.py:23
  148.4 0.9 collective-permute-done.28
  149.4 2.1 %collective-permute-done.31 = bf16[128,768]{1,0:T(8,128)(2,1)S(1)} collective-permute-done((bf16[128,768]{1,0:T(8,128)(2,1)S(1)}, bf16[128,768]{1,0:T(8,128)(2,1)S(1)}, u32[]{:S(2)}, u32[]{:S(2)}) %collective-permute-start.31) | collective-permute-done | bytes 196640 | tf_op jit(solution)/shard_map/ppermute | solution.py:23
  151.5 1.8 %collective-permute-done.34 = bf16[128,512]{1,0:T(8,128)(2,1)S(1)} collective-permute-done((bf16[128,512]{1,0:T(8,128)(2,1)S(1)}, bf16[128,512]{1,0:T(8,128)(2,1)S(1)}, u32[]{:S(2)}, u32[]{:S(2)}) %collective-permute-start.34) | collective-permute-done | bytes 131104 | tf_op jit(solution)/shard_map/ppermute | solution.py:23
  153.3 1.0 copy-done.10
  (68 shorter events, 2.9 us)
Async XLA Ops:
  2.5 18.7 %collective-permute-start.1 = (bf16[64,5120]{1,0:T(8,128)(2,1)}, bf16[64,5120]{1,0:T(8,128)(2,1)S(1)}, u32[]{:S(2)}, u32[]{:S(2)}) collective-permute-start(bf16[64,5120]{1,0:T(8,128)(2,1)} %get-tuple-element.96), channel_id=1, source_target_pairs={{0,1},{1,0},{2,3},{3,2},{4,5},{5,4},{6,7},{7,6},{8,9},{9,8},{10,11... | collective-permute-start | bytes 1966088 | tf_op jit(solution)/shard_map/ppermute | solution.py:28
  5.4 19.8 %collective-permute-start.4 = (bf16[64,5120]{1,0:T(8,128)(2,1)}, bf16[64,5120]{1,0:T(8,128)(2,1)S(1)}, u32[]{:S(2)}, u32[]{:S(2)}) collective-permute-start(bf16[64,5120]{1,0:T(8,128)(2,1)} %get-tuple-element.95), channel_id=1, source_target_pairs={{0,4},{2,6},{4,0},{6,2},{1,5},{3,7},{5,1},{7,3},{8,12},{10,14},{12... | collective-permute-start | bytes 1966088 | tf_op jit(solution)/shard_map/ppermute | solution.py:28
  6.9 35.1 %collective-permute-start.2 = (bf16[64,5120]{1,0:T(8,128)(2,1)}, bf16[64,5120]{1,0:T(8,128)(2,1)}, u32[]{:S(2)}, u32[]{:S(2)}) collective-permute-start(bf16[64,5120]{1,0:T(8,128)(2,1)} %get-tuple-element.95), channel_id=1, source_target_pairs={{0,1},{1,0},{2,3},{3,2},{4,5},{5,4},{6,7},{7,6},{8,9},{9,8},{10,11... | collective-permute-start | bytes 1966088 | tf_op jit(solution)/shard_map/ppermute | solution.py:28
  7.5 34.5 %collective-permute-start.3 = (bf16[64,5120]{1,0:T(8,128)(2,1)}, bf16[64,5120]{1,0:T(8,128)(2,1)S(1)}, u32[]{:S(2)}, u32[]{:S(2)}) collective-permute-start(bf16[64,5120]{1,0:T(8,128)(2,1)} %get-tuple-element.96), channel_id=1, source_target_pairs={{0,4},{2,6},{4,0},{6,2},{1,5},{3,7},{5,1},{7,3},{8,12},{10,14},{12... | collective-permute-start | bytes 1966088 | tf_op jit(solution)/shard_map/ppermute | solution.py:28
  21.2 1.9 %copy-start.2 = (bf16[256,2,8,384]{3,2,1,0:T(8,128)(2,1)S(1)}, bf16[256,2,8,384]{3,2,1,0:T(8,128)(2,1)}, u32[]{:S(2)}) copy-start(bf16[256,2,8,384]{3,2,1,0:T(8,128)(2,1)} %reshape_squeeze.3.refs_0_) | copy-start | bytes 9437188
  23.1 2.1 %copy-start.3 = (bf16[256,2,8,384]{3,2,1,0:T(8,128)(2,1)S(1)}, bf16[256,2,8,384]{3,2,1,0:T(8,128)(2,1)}, u32[]{:S(2)}) copy-start(bf16[256,2,8,384]{3,2,1,0:T(8,128)(2,1)} %reshape_squeeze.3.refs_0_) | copy-start | bytes 9437188
  23.1 4.0 %copy-start.9 = (f32[1,1,3,5120]{3,1,2,0:T(1,128)S(1)}, f32[1,1,3,5120]{3,1,2,0:T(1,128)}, u32[]{:S(2)}) copy-start(f32[1,1,3,5120]{3,1,2,0:T(1,128)} %param.7) | copy-start | bytes 184324
  23.1 4.2 %copy-start = (bf16[1,1,128,5120]{3,2,1,0:T(8,128)(2,1)S(1)}, bf16[1,1,128,5120]{3,2,1,0:T(8,128)(2,1)}, u32[]{:S(2)}) copy-start(bf16[1,1,128,5120]{3,2,1,0:T(8,128)(2,1)} %param.6) | copy-start | bytes 3932164
  23.1 31.6 %collective-permute-start.5 = (bf16[64,5120]{1,0:T(8,128)(2,1)S(1)}, bf16[64,5120]{1,0:T(8,128)(2,1)}, u32[]{:S(2)}, u32[]{:S(2)}) collective-permute-start(bf16[64,5120]{1,0:T(8,128)(2,1)S(1)} %after.3.refs_0_), channel_id=1, source_target_pairs={{0,4},{2,6},{4,0},{6,2},{1,5},{3,7},{5,1},{7,3},{8,12},{10,14},{12... | collective-permute-start | bytes 1966088 | tf_op jit(solution)/shard_map/ppermute | solution.py:28
  25.2 30.0 %collective-permute-start.6 = (bf16[64,5120]{1,0:T(8,128)(2,1)S(1)}, bf16[64,5120]{1,0:T(8,128)(2,1)}, u32[]{:S(2)}, u32[]{:S(2)}) collective-permute-start(bf16[64,5120]{1,0:T(8,128)(2,1)S(1)} %after.4.refs_1_), channel_id=1, source_target_pairs={{0,1},{1,0},{2,3},{3,2},{4,5},{5,4},{6,7},{7,6},{8,9},{9,8},{10,11... | collective-permute-start | bytes 1966088 | tf_op jit(solution)/shard_map/ppermute | solution.py:28
  27.1 23.3 %collective-permute-start = (f32[1,1,3,5120]{3,2,1,0:T(4,128)S(1)}, f32[1,1,3,5120]{3,2,1,0:T(4,128)S(1)}, u32[]{:S(2)}, u32[]{:S(2)}) collective-permute-start(f32[1,1,3,5120]{3,2,1,0:T(4,128)S(1)} %copy.15), channel_id=1, source_target_pairs={{0,1},{1,0},{2,3},{3,2},{4,5},{5,4},{6,7},{7,6},{8,9},{9,8},{10,11... | collective-permute-start | bytes 184328 | tf_op jit(solution)/shard_map/ppermute | solution.py:28
  28.8 1.1 copy-start.6
  42.0 16.2 %collective-permute-start.7 = (bf16[128,5120]{1,0:T(8,128)(2,1)}, bf16[128,5120]{1,0:T(8,128)(2,1)}, u32[]{:S(2)}, u32[]{:S(2)}) collective-permute-start(bf16[128,5120]{1,0:T(8,128)(2,1)} %copy-done.6), channel_id=1, source_target_pairs={{0,2},{2,0},{4,6},{6,4},{1,3},{3,1},{5,7},{7,5},{8,10},{10,8},{12,... | collective-permute-start | bytes 3932168 | tf_op jit(solution)/shard_map/ppermute | solution.py:28
  42.0 0.9 copy-start.4
  42.0 47.9 %collective-permute-start.11 = (bf16[384,5120]{1,0:T(8,128)(2,1)}, bf16[384,5120]{1,0:T(8,128)(2,1)}, u32[]{:S(2)}, u32[]{:S(2)}) collective-permute-start(bf16[384,5120]{1,0:T(8,128)(2,1)} %bitcast.34), channel_id=1, source_target_pairs={{0,2},{2,0},{4,6},{6,4},{1,3},{3,1},{5,7},{7,5},{8,10},{10,8},{12,... | collective-permute-start | bytes 11796488 | tf_op jit(solution)/shard_map/ppermute | solution.py:28
  42.9 42.6 %all-to-all-start = ((bf16[8,256,768]{2,1,0:T(8,128)(2,1)}), bf16[8,256,768]{2,1,0:T(8,128)(2,1)}, u32[]{:S(2)}, u32[]{:S(2)}) async-start(bf16[8,256,768]{2,1,0:T(8,128)(2,1)} %after.5), calls=%async_computation | async-start | bytes 6291456 | tf_op jit(solution)/shard_map/all_to_all | solution.py:451
  50.4 2.8 %copy-start.5 = (bf16[64,5120]{1,0:T(8,128)(2,1)S(1)}, bf16[64,5120]{1,0:T(8,128)(2,1)}, u32[]{:S(2)}) copy-start(bf16[64,5120]{1,0:T(8,128)(2,1)} %copy-done.4) | copy-start | bytes 1966084
  53.0 5.2 %collective-permute-start.8 = (bf16[128,5120]{1,0:T(8,128)(2,1)S(1)}, bf16[128,5120]{1,0:T(8,128)(2,1)S(1)}, u32[]{:S(2)}, u32[]{:S(2)}) collective-permute-start(bf16[128,5120]{1,0:T(8,128)(2,1)S(1)} %modulated_norm.5.refs_1_), channel_id=1, source_target_pairs={{0,2},{2,0},{4,6},{6,4},{1,3},{3,1},{5,7},{7,5},{8,10},{10,8},{12,... | collective-permute-start | bytes 3932168 | tf_op jit(solution)/shard_map/ppermute | solution.py:28
  54.6 6.5 %copy-start.7 = (bf16[128,5120]{1,0:T(8,128)(2,1)S(1)}, bf16[128,5120]{1,0:T(8,128)(2,1)}, u32[]{:S(2)}) copy-start(bf16[128,5120]{1,0:T(8,128)(2,1)} %copy-done.6) | copy-start | bytes 3932164
  54.7 3.6 %collective-permute-start.9 = (bf16[128,5120]{1,0:T(8,128)(2,1)S(1)}, bf16[128,5120]{1,0:T(8,128)(2,1)S(1)}, u32[]{:S(2)}, u32[]{:S(2)}) collective-permute-start(bf16[128,5120]{1,0:T(8,128)(2,1)S(1)} %modulated_norm.6.refs_2_), channel_id=1, source_target_pairs={{0,2},{2,0},{4,6},{6,4},{1,3},{3,1},{5,7},{7,5},{8,10},{10,8},{12,... | collective-permute-start | bytes 3932168 | tf_op jit(solution)/shard_map/ppermute | solution.py:28
  58.0 3.1 %collective-permute-start.10 = (bf16[128,5120]{1,0:T(8,128)(2,1)S(1)}, bf16[128,5120]{1,0:T(8,128)(2,1)S(1)}, u32[]{:S(2)}, u32[]{:S(2)}) collective-permute-start(bf16[128,5120]{1,0:T(8,128)(2,1)S(1)} %modulated_norm.7.refs_3_), channel_id=1, source_target_pairs={{0,2},{2,0},{4,6},{6,4},{1,3},{3,1},{5,7},{7,5},{8,10},{10,8},{12,... | collective-permute-start | bytes 3932168 | tf_op jit(solution)/shard_map/ppermute | solution.py:28
  61.1 24.3 %copy-start.8 = (s32[1,4,6]{2,1,0:T(4,128)S(1)}, s32[1,4,6]{2,1,0:T(4,128)}, u32[]{:S(2)}) copy-start(s32[1,4,6]{2,1,0:T(4,128)} %param.11) | copy-start | bytes 292
  85.4 4.5 %copy-start.1 = (bf16[1,384,5120]{2,1,0:T(8,128)(2,1)S(1)}, bf16[1,384,5120]{2,1,0:T(8,128)(2,1)}, u32[]{:S(2)}) copy-start(bf16[1,384,5120]{2,1,0:T(8,128)(2,1)} %param.9) | copy-start | bytes 11796484
  89.8 3.6 %collective-permute-start.12 = (bf16[512,384]{1,0:T(8,128)(2,1)S(1)}, bf16[512,384]{1,0:T(8,128)(2,1)S(1)}, u32[]{:S(2)}, u32[]{:S(2)}) collective-permute-start(bf16[512,384]{1,0:T(8,128)(2,1)S(1)} %get-tuple-element.52.refs_2_), channel_id=1, source_target_pairs={{0,2},{2,0},{4,6},{6,4},{1,3},{3,1},{5,7},{7,5},{8,10},{10,8},{12,... | collective-permute-start | bytes 1179656 | tf_op jit(solution)/shard_map/ppermute | solution.py:28
  94.9 10.6 %collective-permute-start.13 = (bf16[128,1280]{1,0:T(8,128)(2,1)S(1)}, bf16[128,1280]{1,0:T(8,128)(2,1)S(1)}, u32[]{:S(2)}, u32[]{:S(2)}) collective-permute-start(bf16[128,1280]{1,0:T(8,128)(2,1)S(1)} %get-tuple-element.55), channel_id=1, source_target_pairs={{0,1},{1,0},{2,3},{3,2},{4,5},{5,4},{6,7},{7,6},{8,9},{9,8},{10,11... | collective-permute-start | bytes 983048 | tf_op jit(solution)/shard_map/ppermute | solution.py:28
  95.7 10.6 %collective-permute-start.14 = (bf16[128,1280]{1,0:T(8,128)(2,1)S(1)}, bf16[128,1280]{1,0:T(8,128)(2,1)S(1)}, u32[]{:S(2)}, u32[]{:S(2)}) collective-permute-start(bf16[128,1280]{1,0:T(8,128)(2,1)S(1)} %get-tuple-element.56), channel_id=1, source_target_pairs={{0,4},{2,6},{4,0},{6,2},{1,5},{3,7},{5,1},{7,3},{8,12},{10,14},{12... | collective-permute-start | bytes 983048 | tf_op jit(solution)/shard_map/ppermute | solution.py:28
  99.5 12.9 %collective-permute-start.17 = (bf16[128,1280]{1,0:T(8,128)(2,1)S(1)}, bf16[128,1280]{1,0:T(8,128)(2,1)S(1)}, u32[]{:S(2)}, u32[]{:S(2)}) collective-permute-start(bf16[128,1280]{1,0:T(8,128)(2,1)S(1)} %get-tuple-element.64), channel_id=1, source_target_pairs={{0,1},{1,0},{2,3},{3,2},{4,5},{5,4},{6,7},{7,6},{8,9},{9,8},{10,11... | collective-permute-start | bytes 983048 | tf_op jit(solution)/shard_map/ppermute | solution.py:28
  100.3 12.9 %collective-permute-start.18 = (bf16[128,1280]{1,0:T(8,128)(2,1)S(1)}, bf16[128,1280]{1,0:T(8,128)(2,1)S(1)}, u32[]{:S(2)}, u32[]{:S(2)}) collective-permute-start(bf16[128,1280]{1,0:T(8,128)(2,1)S(1)} %get-tuple-element.65), channel_id=1, source_target_pairs={{0,4},{2,6},{4,0},{6,2},{1,5},{3,7},{5,1},{7,3},{8,12},{10,14},{12... | collective-permute-start | bytes 983048 | tf_op jit(solution)/shard_map/ppermute | solution.py:28
  108.1 10.7 %collective-permute-start.15 = (bf16[128,1152]{1,0:T(8,128)(2,1)S(1)}, bf16[128,1152]{1,0:T(8,128)(2,1)S(1)}, u32[]{:S(2)}, u32[]{:S(2)}) collective-permute-start(bf16[128,1152]{1,0:T(8,128)(2,1)S(1)} %get-tuple-element.60), channel_id=1, source_target_pairs={{0,1},{1,0},{2,3},{3,2},{4,5},{5,4},{6,7},{7,6},{8,9},{9,8},{10,11... | collective-permute-start | bytes 884744 | tf_op jit(solution)/shard_map/ppermute | solution.py:28
  109.4 10.1 %collective-permute-start.16 = (bf16[128,1152]{1,0:T(8,128)(2,1)S(1)}, bf16[128,1152]{1,0:T(8,128)(2,1)S(1)}, u32[]{:S(2)}, u32[]{:S(2)}) collective-permute-start(bf16[128,1152]{1,0:T(8,128)(2,1)S(1)} %get-tuple-element.61), channel_id=1, source_target_pairs={{0,4},{2,6},{4,0},{6,2},{1,5},{3,7},{5,1},{7,3},{8,12},{10,14},{12... | collective-permute-start | bytes 884744 | tf_op jit(solution)/shard_map/ppermute | solution.py:28
  115.6 11.4 %collective-permute-start.20 = (bf16[128,1408]{1,0:T(8,128)(2,1)S(1)}, bf16[128,1408]{1,0:T(8,128)(2,1)S(1)}, u32[]{:S(2)}, u32[]{:S(2)}) collective-permute-start(bf16[128,1408]{1,0:T(8,128)(2,1)S(1)} %get-tuple-element.68), channel_id=1, source_target_pairs={{0,1},{1,0},{2,3},{3,2},{4,5},{5,4},{6,7},{7,6},{8,9},{9,8},{10,11... | collective-permute-start | bytes 1081352 | tf_op jit(solution)/shard_map/ppermute | solution.py:28
  117.0 10.8 %collective-permute-start.21 = (bf16[128,1408]{1,0:T(8,128)(2,1)S(1)}, bf16[128,1408]{1,0:T(8,128)(2,1)S(1)}, u32[]{:S(2)}, u32[]{:S(2)}) collective-permute-start(bf16[128,1408]{1,0:T(8,128)(2,1)S(1)} %get-tuple-element.69), channel_id=1, source_target_pairs={{0,4},{2,6},{4,0},{6,2},{1,5},{3,7},{5,1},{7,3},{8,12},{10,14},{12... | collective-permute-start | bytes 1081352 | tf_op jit(solution)/shard_map/ppermute | solution.py:28
  119.6 12.8 %collective-permute-start.19 = (bf16[128,1280]{1,0:T(8,128)(2,1)S(1)}, bf16[128,1280]{1,0:T(8,128)(2,1)S(1)}, u32[]{:S(2)}, u32[]{:S(2)}) collective-permute-start(bf16[128,1280]{1,0:T(8,128)(2,1)S(1)} %sum_stage.18.refs_10_), channel_id=1, source_target_pairs={{0,8},{8,16},{16,24},{24,0},{1,9},{9,17},{17,25},{25,1},{2,10},{10... | collective-permute-start | bytes 983048 | tf_op jit(solution)/shard_map/ppermute | solution.py:23
  123.4 9.1 %collective-permute-start.23 = (bf16[128,1024]{1,0:T(8,128)(2,1)S(1)}, bf16[128,1024]{1,0:T(8,128)(2,1)S(1)}, u32[]{:S(2)}, u32[]{:S(2)}) collective-permute-start(bf16[128,1024]{1,0:T(8,128)(2,1)S(1)} %get-tuple-element.74), channel_id=1, source_target_pairs={{0,1},{1,0},{2,3},{3,2},{4,5},{5,4},{6,7},{7,6},{8,9},{9,8},{10,11... | collective-permute-start | bytes 786440 | tf_op jit(solution)/shard_map/ppermute | solution.py:28
  124.5 7.9 %collective-permute-start.24 = (bf16[128,1024]{1,0:T(8,128)(2,1)S(1)}, bf16[128,1024]{1,0:T(8,128)(2,1)S(1)}, u32[]{:S(2)}, u32[]{:S(2)}) collective-permute-start(bf16[128,1024]{1,0:T(8,128)(2,1)S(1)} %get-tuple-element.75), channel_id=1, source_target_pairs={{0,4},{2,6},{4,0},{6,2},{1,5},{3,7},{5,1},{7,3},{8,12},{10,14},{12... | collective-permute-start | bytes 786440 | tf_op jit(solution)/shard_map/ppermute | solution.py:28
  127.8 11.7 %collective-permute-start.22 = (bf16[128,1280]{1,0:T(8,128)(2,1)S(1)}, bf16[128,1280]{1,0:T(8,128)(2,1)S(1)}, u32[]{:S(2)}, u32[]{:S(2)}) collective-permute-start(bf16[128,1280]{1,0:T(8,128)(2,1)S(1)} %sum_stage.20.refs_10_), channel_id=1, source_target_pairs={{0,8},{8,16},{16,24},{24,0},{1,9},{9,17},{17,25},{25,1},{2,10},{10... | collective-permute-start | bytes 983048 | tf_op jit(solution)/shard_map/ppermute | solution.py:23
  131.2 7.1 %collective-permute-start.26 = (bf16[128,896]{1,0:T(8,128)(2,1)S(1)}, bf16[128,896]{1,0:T(8,128)(2,1)S(1)}, u32[]{:S(2)}, u32[]{:S(2)}) collective-permute-start(bf16[128,896]{1,0:T(8,128)(2,1)S(1)} %get-tuple-element.80), channel_id=1, source_target_pairs={{0,1},{1,0},{2,3},{3,2},{4,5},{5,4},{6,7},{7,6},{8,9},{9,8},{10,11... | collective-permute-start | bytes 688136 | tf_op jit(solution)/shard_map/ppermute | solution.py:28
  132.5 7.1 %collective-permute-start.27 = (bf16[128,896]{1,0:T(8,128)(2,1)S(1)}, bf16[128,896]{1,0:T(8,128)(2,1)S(1)}, u32[]{:S(2)}, u32[]{:S(2)}) collective-permute-start(bf16[128,896]{1,0:T(8,128)(2,1)S(1)} %get-tuple-element.81), channel_id=1, source_target_pairs={{0,4},{2,6},{4,0},{6,2},{1,5},{3,7},{5,1},{7,3},{8,12},{10,14},{12... | collective-permute-start | bytes 688136 | tf_op jit(solution)/shard_map/ppermute | solution.py:28
  132.5 10.9 %collective-permute-start.25 = (bf16[128,512]{1,0:T(8,128)(2,1)S(1)}, bf16[128,512]{1,0:T(8,128)(2,1)S(1)}, u32[]{:S(2)}, u32[]{:S(2)}) collective-permute-start(bf16[128,512]{1,0:T(8,128)(2,1)S(1)} %sum_stage.22.refs_6_), channel_id=1, source_target_pairs={{0,8},{8,16},{16,24},{24,0},{1,9},{9,17},{17,25},{25,1},{2,10},{10... | collective-permute-start | bytes 393224 | tf_op jit(solution)/shard_map/ppermute | solution.py:23
  134.3 7.9 %collective-permute-start.29 = (bf16[128,384]{1,0:T(8,128)(2,1)S(1)}, bf16[128,384]{1,0:T(8,128)(2,1)S(1)}, u32[]{:S(2)}, u32[]{:S(2)}) collective-permute-start(bf16[128,384]{1,0:T(8,128)(2,1)S(1)} %get-tuple-element.86), channel_id=1, source_target_pairs={{0,1},{1,0},{2,3},{3,2},{4,5},{5,4},{6,7},{7,6},{8,9},{9,8},{10,11... | collective-permute-start | bytes 294920 | tf_op jit(solution)/shard_map/ppermute | solution.py:28
  138.3 5.1 %collective-permute-start.30 = (bf16[128,384]{1,0:T(8,128)(2,1)S(1)}, bf16[128,384]{1,0:T(8,128)(2,1)S(1)}, u32[]{:S(2)}, u32[]{:S(2)}) collective-permute-start(bf16[128,384]{1,0:T(8,128)(2,1)S(1)} %get-tuple-element.87), channel_id=1, source_target_pairs={{0,4},{2,6},{4,0},{6,2},{1,5},{3,7},{5,1},{7,3},{8,12},{10,14},{12... | collective-permute-start | bytes 294920 | tf_op jit(solution)/shard_map/ppermute | solution.py:28
  139.6 9.8 %collective-permute-start.28 = (bf16[128,768]{1,0:T(8,128)(2,1)S(1)}, bf16[128,768]{1,0:T(8,128)(2,1)S(1)}, u32[]{:S(2)}, u32[]{:S(2)}) collective-permute-start(bf16[128,768]{1,0:T(8,128)(2,1)S(1)} %sum_stage.24.refs_6_), channel_id=1, source_target_pairs={{0,8},{8,16},{16,24},{24,0},{1,9},{9,17},{17,25},{25,1},{2,10},{10... | collective-permute-start | bytes 589832 | tf_op jit(solution)/shard_map/ppermute | solution.py:23
  141.2 4.3 %collective-permute-start.32 = (bf16[128,256]{1,0:T(8,128)(2,1)S(1)}, bf16[128,256]{1,0:T(8,128)(2,1)S(1)}, u32[]{:S(2)}, u32[]{:S(2)}) collective-permute-start(bf16[128,256]{1,0:T(8,128)(2,1)S(1)} %get-tuple-element.92), channel_id=1, source_target_pairs={{0,1},{1,0},{2,3},{3,2},{4,5},{5,4},{6,7},{7,6},{8,9},{9,8},{10,11... | collective-permute-start | bytes 196616 | tf_op jit(solution)/shard_map/ppermute | solution.py:28
  142.2 4.3 %collective-permute-start.33 = (bf16[128,256]{1,0:T(8,128)(2,1)S(1)}, bf16[128,256]{1,0:T(8,128)(2,1)S(1)}, u32[]{:S(2)}, u32[]{:S(2)}) collective-permute-start(bf16[128,256]{1,0:T(8,128)(2,1)S(1)} %get-tuple-element.93), channel_id=1, source_target_pairs={{0,4},{2,6},{4,0},{6,2},{1,5},{3,7},{5,1},{7,3},{8,12},{10,14},{12... | collective-permute-start | bytes 196616 | tf_op jit(solution)/shard_map/ppermute | solution.py:28
  143.4 8.0 %collective-permute-start.31 = (bf16[128,768]{1,0:T(8,128)(2,1)S(1)}, bf16[128,768]{1,0:T(8,128)(2,1)S(1)}, u32[]{:S(2)}, u32[]{:S(2)}) collective-permute-start(bf16[128,768]{1,0:T(8,128)(2,1)S(1)} %sum_stage.26.refs_5_), channel_id=1, source_target_pairs={{0,8},{8,16},{16,24},{24,0},{1,9},{9,17},{17,25},{25,1},{2,10},{10... | collective-permute-start | bytes 589832 | tf_op jit(solution)/shard_map/ppermute | solution.py:23
  146.5 6.8 %collective-permute-start.34 = (bf16[128,512]{1,0:T(8,128)(2,1)S(1)}, bf16[128,512]{1,0:T(8,128)(2,1)S(1)}, u32[]{:S(2)}, u32[]{:S(2)}) collective-permute-start(bf16[128,512]{1,0:T(8,128)(2,1)S(1)} %sum_stage.27), channel_id=1, source_target_pairs={{0,8},{8,16},{16,24},{24,0},{1,9},{9,17},{17,25},{25,1},{2,10},{10... | collective-permute-start | bytes 393224 | tf_op jit(solution)/shard_map/ppermute | solution.py:23
  153.3 1.1 copy-start.10

commit v18 on v17

--- a/solution.py
+++ b/solution.py
@@ -60,6 +60,43 @@
         cost_estimate=SHORT,
         compiler_params=pltpu.CompilerParams(vmem_limit_bytes=8 * MIB),
     )(*parts, modulation)
+
+
+def halves_kernel(rows_ref, upper_ref, lower_ref, held, sems):
+    half = upper_ref.shape[0]
+    places = pl.ds(0, half), pl.ds(half, half)
+    copies_in = [
+        pltpu.make_async_copy(rows_ref.at[place], held.at[place], sems.at[0, index])
+        for index, place in enumerate(places)
+    ]
+    copies_out = [
+        pltpu.make_async_copy(held.at[place], ref, sems.at[1, index])
+        for index, (place, ref) in enumerate(zip(places, (upper_ref, lower_ref)))
+    ]
+    for copy in copies_in:
+        copy.start()
+    for copy_in, copy_out in zip(copies_in, copies_out):
+        copy_in.wait()
+        copy_out.start()
+    for copy in copies_out:
+        copy.wait()
+
+
+def halves_of(rows):
+    count, features = rows.shape
+    return pl.pallas_call(
+        halves_kernel,
+        in_specs=[pl.BlockSpec(memory_space=pl.ANY)],
+        out_specs=[pl.BlockSpec(memory_space=pltpu.HBM)] * 2,
+        out_shape=[jax.ShapeDtypeStruct((count // 2, features), rows.dtype)] * 2,
+        scratch_shapes=[
+            pltpu.VMEM((count, features), rows.dtype),
+            pltpu.SemaphoreType.DMA((2, 2)),
+        ],
+        name="halves_of",
+        cost_estimate=SHORT,
+        compiler_params=pltpu.CompilerParams(vmem_limit_bytes=60 * MIB),
+    )(rows)
 
 
 def gate_kernel(value_ref, *refs):
@@ -432,7 +469,7 @@
     unpacked = stale_cache[0, 0].reshape(context_rows, 2, devices, width)
     packed = unpacked.transpose(2, 0, 1, 3).reshape(devices, context_rows, 2 * width)
 
-    upper, lower = current[: token_rows // 2], current[token_rows // 2 :]
+    upper, lower = halves_of(current)
     across_upper, along_lower = from_partner(upper, "cfg", 1), from_partner(lower, "sp", 2)
     across_lower, along_upper = from_partner(lower, "cfg", 1), from_partner(upper, "sp", 2)
     other_modulate = from_partner(modulation, "cfg", 1)[0, 0]

time: 155 us -> 155 us (level)
  local copies, waits for them, and re-layouts: 27.1 us -> 24.6 us
  Pallas kernels: 48.2 us -> 50.4 us
    slice x1 -> x0, local copies, waits for them, and re-layouts: 2.47 us -> none  [per_device(): upper, lower = (current[:token_rows // 2], current[token_rows // 2:])]
    pallas_call x0 -> x1, Pallas kernels: none -> 2.22 us  [halves_of(): pl.pallas_call(halves_kernel, in_specs=[pl.BlockSpec(memory_space=pl.ANY)...]
  transfers between devices with their start and end apart: 36 -> 36, of which waited for: 20 -> 18; matrix products, arithmetic and copies ran while one was open for 13% -> 13% of each run, Pallas kernels for 30% -> 30%
where the time goes in v18:
time: 155 us; the launch traced here: 154 us
  Pallas kernels  50.4 us (33%)
  starting transfers between devices  42.1 us (27%)
  waiting for transfers between devices  36.6 us (24%)
  local copies, waits for them, and re-layouts  24.6 us (16%)
    ppermute x29, waiting for transfers between devices, from_partner(): return lax.ppermute(value, axis, pairs)  27.5 us
    ppermute x29, starting transfers between devices, from_partner(): return lax.ppermute(value, axis, pairs)  26.6 us
    pallas_call x1, Pallas kernels, project(): pl.pallas_call(functools.partial(project_kernel, blocks=len(blocks)), gri...  19.2 us
    pallas_call x14, Pallas kernels, stage(): pl.pallas_call(functools.partial(stage_kernel, parts=parts, start=start,...  12.7 us
    ppermute x6, starting transfers between devices, from_behind(): return lax.ppermute(x, axis, [(i, (i + by) % count) for i in range(count)])  10.9 us
    pallas_call x4, Pallas kernels, modulated_norm(): pl.pallas_call(norm_kernel, in_specs=[pl.BlockSpec(memory_space=pltpu.VME...  8.49 us
    reshape x1, local copies, waits for them, and re-layouts, per_device(): unpacked.transpose(2, 0, 1, 3).reshape(devices, context_rows, 2 * width)  8.06 us
    another operation x1, local copies, waits for them, and re-layouts, per_device(): unpacked = stale_cache[0, 0].reshape(context_rows, 2, devices, width)  8 us
  transfers between devices with their start and end apart: 36, of which 18 were waited for; matrix products, arithmetic and copies ran while one was open for 13% of the time, Pallas kernels for 30%

profile of v18, /device:TPU:0, one launch (start us, length us, event | category | flops | bytes accessed | tf_op | source)
XLA Modules:
  0.0 154.1 jit_solution(2139412533033649822)
XLA Ops:
  0.0 2.2 %halves_of.1 = (bf16[64,5120]{1,0:T(8,128)(2,1)}, bf16[64,5120]{1,0:T(8,128)(2,1)}) custom-call(bf16[128,5120]{1,0:T(8,128)(2,1)} %bitcast.15), custom_call_target="tpu_custom_call" | custom-call | flops 1 | bytes 1 | tf_op jit(solution)/shard_map/halves_of/pallas_call | solution.py:87
  2.2 3.0 %collective-permute-start.1 = (bf16[64,5120]{1,0:T(8,128)(2,1)}, bf16[64,5120]{1,0:T(8,128)(2,1)S(1)}, u32[]{:S(2)}, u32[]{:S(2)}) collective-permute-start(bf16[64,5120]{1,0:T(8,128)(2,1)} %get-tuple-element.52), channel_id=1, source_target_pairs={{0,1},{1,0},{2,3},{3,2},{4,5},{5,4},{6,7},{7,6},{8,9},{9,8},{10,11... | collective-permute-start | bytes 1966088 | tf_op jit(solution)/shard_map/ppermute | solution.py:28
  5.2 1.5 collective-permute-start.4
  6.8 0.5 collective-permute-start.3
  7.3 8.0 %reshape_squeeze.3.refs_0_ = bf16[256,2,8,384]{3,2,1,0:T(8,128)(2,1)} reshape(bf16[1,1,256,2,3072]{4,3,2,1,0:T(2,128)(2,1)} %param.10) | data formatting | bytes 6291456 | tf_op jit(solution)/shard_map/reshape;squeeze | solution.py:469
  15.3 5.7 %collective-permute-done.1.value_ref = bf16[64,5120]{1,0:T(8,128)(2,1)S(1)} collective-permute-done((bf16[64,5120]{1,0:T(8,128)(2,1)}, bf16[64,5120]{1,0:T(8,128)(2,1)S(1)}, u32[]{:S(2)}, u32[]{:S(2)}) %collective-permute-start.1) | collective-permute-done | bytes 655392 | tf_op jit(solution)/shard_map/ppermute | solution.py:28
  21.0 1.9 %copy-done.2 = bf16[256,2,8,384]{3,2,1,0:T(8,128)(2,1)S(1)} copy-done((bf16[256,2,8,384]{3,2,1,0:T(8,128)(2,1)S(1)}, bf16[256,2,8,384]{3,2,1,0:T(8,128)(2,1)}, u32[]{:S(2)}) %copy-start.2) | copy-done | bytes 3145752
  22.9 2.1 %collective-permute-start.5 = (bf16[64,5120]{1,0:T(8,128)(2,1)S(1)}, bf16[64,5120]{1,0:T(8,128)(2,1)}, u32[]{:S(2)}, u32[]{:S(2)}) collective-permute-start(bf16[64,5120]{1,0:T(8,128)(2,1)S(1)} %after.3.refs_0_), channel_id=1, source_target_pairs={{0,4},{2,6},{4,0},{6,2},{1,5},{3,7},{5,1},{7,3},{8,12},{10,14},{12... | collective-permute-start | bytes 1966088 | tf_op jit(solution)/shard_map/ppermute | solution.py:28
  25.0 1.8 %collective-permute-start.6 = (bf16[64,5120]{1,0:T(8,128)(2,1)S(1)}, bf16[64,5120]{1,0:T(8,128)(2,1)}, u32[]{:S(2)}, u32[]{:S(2)}) collective-permute-start(bf16[64,5120]{1,0:T(8,128)(2,1)S(1)} %after.4.refs_1_), channel_id=1, source_target_pairs={{0,1},{1,0},{2,3},{3,2},{4,5},{5,4},{6,7},{7,6},{8,9},{9,8},{10,11... | collective-permute-start | bytes 1966088 | tf_op jit(solution)/shard_map/ppermute | solution.py:28
  27.1 1.5 modulated_norm.4.refs_0_
  28.7 1.0 copy-done.6
  29.7 4.1 %copy.11 = bf16[8,256,2,384]{3,2,1,0:T(2,128)(2,1)} copy(bf16[8,256,2,384]{3,0,2,1:T(8,128)(2,1)S(1)} %bitcast.38) | data formatting | bytes 6291456 | tf_op jit(solution)/shard_map/transpose | solution.py:470
  33.8 8.1 %reshape.8.value_ref = bf16[8,256,768]{2,1,0:T(8,128)(2,1)} reshape(bf16[8,256,2,384]{3,2,1,0:T(2,128)(2,1)} %copy.11) | data formatting | bytes 6291456 | tf_op jit(solution)/shard_map/reshape | solution.py:470
  41.8 0.5 collective-permute-start.11
  42.7 4.6 %all-to-all-start = ((bf16[8,256,768]{2,1,0:T(8,128)(2,1)}), bf16[8,256,768]{2,1,0:T(8,128)(2,1)}, u32[]{:S(2)}, u32[]{:S(2)}) async-start(bf16[8,256,768]{2,1,0:T(8,128)(2,1)} %after.5), calls=%async_computation | async-start | bytes 6291456 | tf_op jit(solution)/shard_map/all_to_all | solution.py:488
  47.3 3.1 %collective-permute-done = f32[1,1,3,5120]{3,2,1,0:T(4,128)S(1)} collective-permute-done((f32[1,1,3,5120]{3,2,1,0:T(4,128)S(1)}, f32[1,1,3,5120]{3,2,1,0:T(4,128)S(1)}, u32[]{:S(2)}, u32[]{:S(2)}) %collective-permute-start) | collective-permute-done | bytes 61472 | tf_op jit(solution)/shard_map/ppermute | solution.py:28
  50.4 2.7 %modulated_norm.5.refs_1_ = bf16[128,5120]{1,0:T(8,128)(2,1)S(1)} custom-call(bf16[64,5120]{1,0:T(8,128)(2,1)S(1)} %after.3.refs_0_, bf16[64,5120]{1,0:T(8,128)(2,1)} %collective-permute-done.2.refs_1_.refs_0_, f32[3,5120]{1,0:T(4,128)S(1)} %bitcast.41), custom_call_target="tpu_custom_call" | custom-call | flops 1 | bytes 1 | tf_op jit(solution)/shard_map/modulated_norm/pallas_call | solution.py:55
  53.2 1.5 modulated_norm.6.refs_2_
  54.7 0.6 collective-permute-start.9
  55.3 2.8 %modulated_norm.7.refs_3_ = bf16[128,5120]{1,0:T(8,128)(2,1)S(1)} custom-call(bf16[64,5120]{1,0:T(8,128)(2,1)} %collective-permute-done.5.refs_0_, bf16[64,5120]{1,0:T(8,128)(2,1)} %collective-permute-done.6.refs_1_, f32[3,5120]{1,0:T(4,128)S(1)} %bitcast.42), custom_call_target="tpu_custom_call" | custom-call | flops 1 | bytes 1 | tf_op jit(solution)/shard_map/modulated_norm/pallas_call | solution.py:55
  58.3 2.9 %collective-permute-done.10.refs_7_ = bf16[128,5120]{1,0:T(8,128)(2,1)S(1)} collective-permute-done((bf16[128,5120]{1,0:T(8,128)(2,1)S(1)}, bf16[128,5120]{1,0:T(8,128)(2,1)S(1)}, u32[]{:S(2)}, u32[]{:S(2)}) %collective-permute-start.10) | collective-permute-done | bytes 1310752 | tf_op jit(solution)/shard_map/ppermute | solution.py:28
  61.2 19.2 %project_heads.1.heads_in = bf16[48,1024,128]{2,1,0:T(8,128)(2,1)} custom-call(bf16[128,5120]{1,0:T(8,128)(2,1)S(1)} %copy-done.7, bf16[128,5120]{1,0:T(8,128)(2,1)S(1)} %modulated_norm.5.refs_1_, bf16[128,5120]{1,0:T(8,128)(2,1)S(1)} %modulated_norm.6.refs_2_, bf16[128,5120]{1,0:T(8,128)(2,1)S(1)} %modulated_norm.7.refs_3_, ...), custom_call_target="tpu_custom_call" | custom-call | flops 12079595520 | bytes 22282240 | tf_op jit(solution)/shard_map/project_heads/pallas_call | solution.py:161
  80.4 4.2 %all-to-all-done = bf16[8,256,768]{2,1,0:T(8,128)(2,1)} async-done(((bf16[8,256,768]{2,1,0:T(8,128)(2,1)}), bf16[8,256,768]{2,1,0:T(8,128)(2,1)}, u32[]{:S(2)}, u32[]{:S(2)}) %all-to-all-start) | async-done | bytes 3145760 | tf_op jit(solution)/shard_map/all_to_all | solution.py:488
  84.6 4.3 %attend_first.1 = (bf16[512,384]{1,0:T(8,128)(2,1)S(1)}, bf16[3,1024,128]{2,1,0:T(8,128)(2,1)S(1)}, bf16[6,3072,128]{2,1,0:T(8,128)(2,1)S(1)}) custom-call(s32[4,6]{1,0:T(4,128)S(1)} %bitcast.43, bf16[48,1024,128]{2,1,0:T(8,128)(2,1)} %project_heads.1.heads_in, bf16[2048,768]{1,0:T(8,128)(2,1)} %bitcast.7.context_in), custom_call_target="tpu_custom_call" | custom-call | flops 1 | bytes 1 | tf_op jit(solution)/shard_map/attend_first/pallas_call | solution.py:270
  89.1 3.5 %attend_second.1 = (bf16[512,384]{1,0:T(8,128)(2,1)S(1)}, bf16[768,1280]{1,0:T(8,128)(2,1)S(1)}) custom-call(s32[4,6]{1,0:T(4,128)S(1)} %bitcast.44, bf16[3,1024,128]{2,1,0:T(8,128)(2,1)S(1)} %get-tuple-element.54.queries_ref, bf16[6,3072,128]{2,1,0:T(8,128)(2,1)S(1)} %get-tuple-element.55.pool_ref, bf16[384,5120]{1,0:T(8,128)(2,1)S(1)} %bitcast.32, ...), custom_call_target="tpu_custom_call" | custom-call | flops 1 | bytes 1 | tf_op jit(solution)/shard_map/attend_second/pallas_call | solution.py:309
  92.6 1.4 sum_stage.14
  94.0 1.1 collective-permute-start.13
  95.1 1.5 collective-permute-start.14
  96.6 2.7 %sum_stage.15 = (bf16[128,1280]{1,0:T(8,128)(2,1)S(1)}, bf16[128,1280]{1,0:T(8,128)(2,1)S(1)}, f32[2,128,640]{2,1,0:T(8,128)S(1)}, f32[2,128,640]{2,1,0:T(8,128)S(1)}) custom-call(bf16[128,5120]{1,0:T(8,128)(2,1)S(1)} %bitcast.18, f32[2,5120]{1,0:T(2,128)S(1)} %pad_maximum_fusion.refs_3_.refs_1_, bf16[512,384]{1,0:T(8,128)(2,1)S(1)} %get-tuple-element.57.refs_2_, ...), custom_call_target="tpu_custom_call" | custom-call | flops 1 | bytes 1 | tf_op jit(solution)/shard_map/sum_stage/pallas_call | solution.py:434
  99.7 1.2 collective-permute-start.18
  100.9 3.7 %collective-permute-done.13.refs_6_ = bf16[128,1280]{1,0:T(8,128)(2,1)S(1)} collective-permute-done((bf16[128,1280]{1,0:T(8,128)(2,1)S(1)}, bf16[128,1280]{1,0:T(8,128)(2,1)S(1)}, u32[]{:S(2)}, u32[]{:S(2)}) %collective-permute-start.13) | collective-permute-done | bytes 327712 | tf_op jit(solution)/shard_map/ppermute | solution.py:28
  104.6 1.0 collective-permute-done.14.refs_7_
  105.7 1.8 %sum_stage.16 = (bf16[128,1152]{1,0:T(8,128)(2,1)S(1)}, bf16[128,1152]{1,0:T(8,128)(2,1)S(1)}, f32[2,128,256]{2,1,0:T(8,128)S(1)}, f32[2,128,256]{2,1,0:T(8,128)...) custom-call(bf16[128,5120]{1,0:T(8,128)(2,1)S(1)} %bitcast.19, f32[2,5120]{1,0:T(2,128)S(1)} %pad_maximum_fusion.refs_3_.refs_1_, ...), custom_call_target="tpu_custom_call" | custom-call | flops 1 | bytes 1 | tf_op jit(solution)/shard_map/sum_stage/pallas_call | solution.py:434
  107.5 1.1 collective-permute-start.15
  108.6 0.8 collective-permute-start.16
  109.4 2.2 %collective-permute-done.17.refs_6_ = bf16[128,1280]{1,0:T(8,128)(2,1)S(1)} collective-permute-done((bf16[128,1280]{1,0:T(8,128)(2,1)S(1)}, bf16[128,1280]{1,0:T(8,128)(2,1)S(1)}, u32[]{:S(2)}, u32[]{:S(2)}) %collective-permute-start.17) | collective-permute-done | bytes 327712 | tf_op jit(solution)/shard_map/ppermute | solution.py:28
  111.6 1.0 collective-permute-done.18.refs_7_
  112.7 2.4 %sum_stage.17 = (bf16[128,1408]{1,0:T(8,128)(2,1)S(1)}, bf16[128,1408]{1,0:T(8,128)(2,1)S(1)}, f32[2,128,384]{2,1,0:T(8,128)S(1)}, f32[2,128,384]{2,1,0:T(8,128)...) custom-call(bf16[128,5120]{1,0:T(8,128)(2,1)S(1)} %bitcast.20, f32[2,5120]{1,0:T(2,128)S(1)} %pad_maximum_fusion.refs_3_.refs_1_, ...), custom_call_target="tpu_custom_call" | custom-call | flops 1 | bytes 1 | tf_op jit(solution)/shard_map/sum_stage/pallas_call | solution.py:434
  115.1 1.1 collective-permute-start.20
  116.1 0.8 collective-permute-start.21
  117.0 1.0 collective-permute-done.15.refs_1_.refs_6_
  118.0 1.0 collective-permute-done.16.refs_2_.refs_7_
  119.1 1.9 %collective-permute-start.19 = (bf16[128,1280]{1,0:T(8,128)(2,1)S(1)}, bf16[128,1280]{1,0:T(8,128)(2,1)S(1)}, u32[]{:S(2)}, u32[]{:S(2)}) collective-permute-start(bf16[128,1280]{1,0:T(8,128)(2,1)S(1)} %sum_stage.18.refs_10_), channel_id=1, source_target_pairs={{0,8},{8,16},{16,24},{24,0},{1,9},{9,17},{17,25},{25,1},{2,10},{10... | collective-permute-start | bytes 983048 | tf_op jit(solution)/shard_map/ppermute | solution.py:23
  121.0 2.2 %sum_stage.19 = (bf16[128,1024]{1,0:T(8,128)(2,1)S(1)}, bf16[128,1024]{1,0:T(8,128)(2,1)S(1)}, f32[2,128,384]{2,1,0:T(8,128)S(1)}, f32[2,128,384]{2,1,0:T(8,128)...) custom-call(bf16[128,5120]{1,0:T(8,128)(2,1)S(1)} %bitcast.22, f32[2,5120]{1,0:T(2,128)S(1)} %pad_maximum_fusion.refs_3_.refs_1_, ...), custom_call_target="tpu_custom_call" | custom-call | flops 1 | bytes 1 | tf_op jit(solution)/shard_map/sum_stage/pallas_call | solution.py:434
  123.1 1.1 collective-permute-start.23
  124.5 1.8 %collective-permute-done.20.refs_1_.refs_6_ = bf16[128,1408]{1,0:T(8,128)(2,1)S(1)} collective-permute-done((bf16[128,1408]{1,0:T(8,128)(2,1)S(1)}, bf16[128,1408]{1,0:T(8,128)(2,1)S(1)}, u32[]{:S(2)}, u32[]{:S(2)}) %collective-permute-start.20) | collective-permute-done | bytes 360480 | tf_op jit(solution)/shard_map/ppermute | solution.py:28
  126.3 0.7 collective-permute-done.21.refs_2_.refs_7_
  127.1 2.2 %collective-permute-start.22 = (bf16[128,1280]{1,0:T(8,128)(2,1)S(1)}, bf16[128,1280]{1,0:T(8,128)(2,1)S(1)}, u32[]{:S(2)}, u32[]{:S(2)}) collective-permute-start(bf16[128,1280]{1,0:T(8,128)(2,1)S(1)} %sum_stage.20.refs_10_), channel_id=1, source_target_pairs={{0,8},{8,16},{16,24},{24,0},{1,9},{9,17},{17,25},{25,1},{2,10},{10... | collective-permute-start | bytes 983048 | tf_op jit(solution)/shard_map/ppermute | solution.py:23
  129.2 1.7 %sum_stage.21 = (bf16[128,896]{1,0:T(8,128)(2,1)S(1)}, bf16[128,896]{1,0:T(8,128)(2,1)S(1)}, f32[2,128,256]{2,1,0:T(8,128)S(1)}, f32[2,128,256]{2,1,0:T(8,128)S(...) custom-call(bf16[128,5120]{1,0:T(8,128)(2,1)S(1)} %bitcast.24, f32[2,5120]{1,0:T(2,128)S(1)} %pad_maximum_fusion.refs_3_.refs_1_, ...), custom_call_target="tpu_custom_call" | custom-call | flops 1 | bytes 1 | tf_op jit(solution)/shard_map/sum_stage/pallas_call | solution.py:434
  130.9 1.1 collective-permute-start.26
  132.2 1.6 %collective-permute-start.25 = (bf16[128,512]{1,0:T(8,128)(2,1)S(1)}, bf16[128,512]{1,0:T(8,128)(2,1)S(1)}, u32[]{:S(2)}, u32[]{:S(2)}) collective-permute-start(bf16[128,512]{1,0:T(8,128)(2,1)S(1)} %sum_stage.22.refs_6_), channel_id=1, source_target_pairs={{0,8},{8,16},{16,24},{24,0},{1,9},{9,17},{17,25},{25,1},{2,10},{10... | collective-permute-start | bytes 393224 | tf_op jit(solution)/shard_map/ppermute | solution.py:23
  134.0 2.0 %collective-permute-start.29 = (bf16[128,384]{1,0:T(8,128)(2,1)S(1)}, bf16[128,384]{1,0:T(8,128)(2,1)S(1)}, u32[]{:S(2)}, u32[]{:S(2)}) collective-permute-start(bf16[128,384]{1,0:T(8,128)(2,1)S(1)} %get-tuple-element.90), channel_id=1, source_target_pairs={{0,1},{1,0},{2,3},{3,2},{4,5},{5,4},{6,7},{7,6},{8,9},{9,8},{10,11... | collective-permute-start | bytes 294920 | tf_op jit(solution)/shard_map/ppermute | solution.py:28
  136.0 2.0 %collective-permute-done.26.refs_1_.refs_2_ = bf16[128,896]{1,0:T(8,128)(2,1)S(1)} collective-permute-done((bf16[128,896]{1,0:T(8,128)(2,1)S(1)}, bf16[128,896]{1,0:T(8,128)(2,1)S(1)}, u32[]{:S(2)}, u32[]{:S(2)}) %collective-permute-start.26) | collective-permute-done | bytes 229408 | tf_op jit(solution)/shard_map/ppermute | solution.py:28
  138.1 1.1 collective-permute-start.30
  139.2 1.6 %collective-permute-start.28 = (bf16[128,768]{1,0:T(8,128)(2,1)S(1)}, bf16[128,768]{1,0:T(8,128)(2,1)S(1)}, u32[]{:S(2)}, u32[]{:S(2)}) collective-permute-start(bf16[128,768]{1,0:T(8,128)(2,1)S(1)} %sum_stage.24.refs_6_), channel_id=1, source_target_pairs={{0,8},{8,16},{16,24},{24,0},{1,9},{9,17},{17,25},{25,1},{2,10},{10... | collective-permute-start | bytes 589832 | tf_op jit(solution)/shard_map/ppermute | solution.py:23
  141.0 1.0 collective-permute-start.32
  141.9 1.2 collective-permute-start.33
  143.2 1.7 %collective-permute-start.31 = (bf16[128,768]{1,0:T(8,128)(2,1)S(1)}, bf16[128,768]{1,0:T(8,128)(2,1)S(1)}, u32[]{:S(2)}, u32[]{:S(2)}) collective-permute-start(bf16[128,768]{1,0:T(8,128)(2,1)S(1)} %sum_stage.26.refs_5_), channel_id=1, source_target_pairs={{0,8},{8,16},{16,24},{24,0},{1,9},{9,17},{17,25},{25,1},{2,10},{10... | collective-permute-start | bytes 589832 | tf_op jit(solution)/shard_map/ppermute | solution.py:23
  145.3 0.9 collective-permute-done.33.refs_2_
  146.2 1.9 %collective-permute-start.34 = (bf16[128,512]{1,0:T(8,128)(2,1)S(1)}, bf16[128,512]{1,0:T(8,128)(2,1)S(1)}, u32[]{:S(2)}, u32[]{:S(2)}) collective-permute-start(bf16[128,512]{1,0:T(8,128)(2,1)S(1)} %sum_stage.27), channel_id=1, source_target_pairs={{0,8},{8,16},{16,24},{24,0},{1,9},{9,17},{17,25},{25,1},{2,10},{10... | collective-permute-start | bytes 393224 | tf_op jit(solution)/shard_map/ppermute | solution.py:23
  148.1 0.9 collective-permute-done.28
  149.1 2.1 %collective-permute-done.31 = bf16[128,768]{1,0:T(8,128)(2,1)S(1)} collective-permute-done((bf16[128,768]{1,0:T(8,128)(2,1)S(1)}, bf16[128,768]{1,0:T(8,128)(2,1)S(1)}, u32[]{:S(2)}, u32[]{:S(2)}) %collective-permute-start.31) | collective-permute-done | bytes 196640 | tf_op jit(solution)/shard_map/ppermute | solution.py:23
  151.2 1.9 %collective-permute-done.34 = bf16[128,512]{1,0:T(8,128)(2,1)S(1)} collective-permute-done((bf16[128,512]{1,0:T(8,128)(2,1)S(1)}, bf16[128,512]{1,0:T(8,128)(2,1)S(1)}, u32[]{:S(2)}, u32[]{:S(2)}) %collective-permute-start.34) | collective-permute-done | bytes 131104 | tf_op jit(solution)/shard_map/ppermute | solution.py:23
  153.1 1.0 copy-done.10
  (68 shorter events, 3.0 us)
Async XLA Ops:
  2.2 18.8 %collective-permute-start.1 = (bf16[64,5120]{1,0:T(8,128)(2,1)}, bf16[64,5120]{1,0:T(8,128)(2,1)S(1)}, u32[]{:S(2)}, u32[]{:S(2)}) collective-permute-start(bf16[64,5120]{1,0:T(8,128)(2,1)} %get-tuple-element.52), channel_id=1, source_target_pairs={{0,1},{1,0},{2,3},{3,2},{4,5},{5,4},{6,7},{7,6},{8,9},{9,8},{10,11... | collective-permute-start | bytes 1966088 | tf_op jit(solution)/shard_map/ppermute | solution.py:28
  5.2 19.8 %collective-permute-start.4 = (bf16[64,5120]{1,0:T(8,128)(2,1)}, bf16[64,5120]{1,0:T(8,128)(2,1)S(1)}, u32[]{:S(2)}, u32[]{:S(2)}) collective-permute-start(bf16[64,5120]{1,0:T(8,128)(2,1)} %get-tuple-element.53), channel_id=1, source_target_pairs={{0,4},{2,6},{4,0},{6,2},{1,5},{3,7},{5,1},{7,3},{8,12},{10,14},{12... | collective-permute-start | bytes 1966088 | tf_op jit(solution)/shard_map/ppermute | solution.py:28
  6.8 35.1 %collective-permute-start.3 = (bf16[64,5120]{1,0:T(8,128)(2,1)}, bf16[64,5120]{1,0:T(8,128)(2,1)S(1)}, u32[]{:S(2)}, u32[]{:S(2)}) collective-permute-start(bf16[64,5120]{1,0:T(8,128)(2,1)} %get-tuple-element.52), channel_id=1, source_target_pairs={{0,4},{2,6},{4,0},{6,2},{1,5},{3,7},{5,1},{7,3},{8,12},{10,14},{12... | collective-permute-start | bytes 1966088 | tf_op jit(solution)/shard_map/ppermute | solution.py:28
  7.3 34.6 %collective-permute-start.2 = (bf16[64,5120]{1,0:T(8,128)(2,1)}, bf16[64,5120]{1,0:T(8,128)(2,1)}, u32[]{:S(2)}, u32[]{:S(2)}) collective-permute-start(bf16[64,5120]{1,0:T(8,128)(2,1)} %get-tuple-element.53), channel_id=1, source_target_pairs={{0,1},{1,0},{2,3},{3,2},{4,5},{5,4},{6,7},{7,6},{8,9},{9,8},{10,11... | collective-permute-start | bytes 1966088 | tf_op jit(solution)/shard_map/ppermute | solution.py:28
  21.0 1.9 %copy-start.2 = (bf16[256,2,8,384]{3,2,1,0:T(8,128)(2,1)S(1)}, bf16[256,2,8,384]{3,2,1,0:T(8,128)(2,1)}, u32[]{:S(2)}) copy-start(bf16[256,2,8,384]{3,2,1,0:T(8,128)(2,1)} %reshape_squeeze.3.refs_0_) | copy-start | bytes 9437188
  22.9 2.1 %copy-start.3 = (bf16[256,2,8,384]{3,2,1,0:T(8,128)(2,1)S(1)}, bf16[256,2,8,384]{3,2,1,0:T(8,128)(2,1)}, u32[]{:S(2)}) copy-start(bf16[256,2,8,384]{3,2,1,0:T(8,128)(2,1)} %reshape_squeeze.3.refs_0_) | copy-start | bytes 9437188
  22.9 3.9 %copy-start.9 = (f32[1,1,3,5120]{3,1,2,0:T(1,128)S(1)}, f32[1,1,3,5120]{3,1,2,0:T(1,128)}, u32[]{:S(2)}) copy-start(f32[1,1,3,5120]{3,1,2,0:T(1,128)} %param.7) | copy-start | bytes 184324
  22.9 4.2 %copy-start = (bf16[1,1,128,5120]{3,2,1,0:T(8,128)(2,1)S(1)}, bf16[1,1,128,5120]{3,2,1,0:T(8,128)(2,1)}, u32[]{:S(2)}) copy-start(bf16[1,1,128,5120]{3,2,1,0:T(8,128)(2,1)} %param.6) | copy-start | bytes 3932164
  22.9 31.8 %collective-permute-start.5 = (bf16[64,5120]{1,0:T(8,128)(2,1)S(1)}, bf16[64,5120]{1,0:T(8,128)(2,1)}, u32[]{:S(2)}, u32[]{:S(2)}) collective-permute-start(bf16[64,5120]{1,0:T(8,128)(2,1)S(1)} %after.3.refs_0_), channel_id=1, source_target_pairs={{0,4},{2,6},{4,0},{6,2},{1,5},{3,7},{5,1},{7,3},{8,12},{10,14},{12... | collective-permute-start | bytes 1966088 | tf_op jit(solution)/shard_map/ppermute | solution.py:28
  25.0 30.3 %collective-permute-start.6 = (bf16[64,5120]{1,0:T(8,128)(2,1)S(1)}, bf16[64,5120]{1,0:T(8,128)(2,1)}, u32[]{:S(2)}, u32[]{:S(2)}) collective-permute-start(bf16[64,5120]{1,0:T(8,128)(2,1)S(1)} %after.4.refs_1_), channel_id=1, source_target_pairs={{0,1},{1,0},{2,3},{3,2},{4,5},{5,4},{6,7},{7,6},{8,9},{9,8},{10,11... | collective-permute-start | bytes 1966088 | tf_op jit(solution)/shard_map/ppermute | solution.py:28
  26.9 23.6 %collective-permute-start = (f32[1,1,3,5120]{3,2,1,0:T(4,128)S(1)}, f32[1,1,3,5120]{3,2,1,0:T(4,128)S(1)}, u32[]{:S(2)}, u32[]{:S(2)}) collective-permute-start(f32[1,1,3,5120]{3,2,1,0:T(4,128)S(1)} %copy.15), channel_id=1, source_target_pairs={{0,1},{1,0},{2,3},{3,2},{4,5},{5,4},{6,7},{7,6},{8,9},{9,8},{10,11... | collective-permute-start | bytes 184328 | tf_op jit(solution)/shard_map/ppermute | solution.py:28
  28.6 1.1 copy-start.6
  41.8 0.9 copy-start.4
  41.8 16.5 %collective-permute-start.7 = (bf16[128,5120]{1,0:T(8,128)(2,1)}, bf16[128,5120]{1,0:T(8,128)(2,1)}, u32[]{:S(2)}, u32[]{:S(2)}) collective-permute-start(bf16[128,5120]{1,0:T(8,128)(2,1)} %copy-done.6), channel_id=1, source_target_pairs={{0,2},{2,0},{4,6},{6,4},{1,3},{3,1},{5,7},{7,5},{8,10},{10,8},{12,... | collective-permute-start | bytes 3932168 | tf_op jit(solution)/shard_map/ppermute | solution.py:28
  41.8 47.2 %collective-permute-start.11 = (bf16[384,5120]{1,0:T(8,128)(2,1)}, bf16[384,5120]{1,0:T(8,128)(2,1)}, u32[]{:S(2)}, u32[]{:S(2)}) collective-permute-start(bf16[384,5120]{1,0:T(8,128)(2,1)} %bitcast.31), channel_id=1, source_target_pairs={{0,2},{2,0},{4,6},{6,4},{1,3},{3,1},{5,7},{7,5},{8,10},{10,8},{12,... | collective-permute-start | bytes 11796488 | tf_op jit(solution)/shard_map/ppermute | solution.py:28
  42.7 41.9 %all-to-all-start = ((bf16[8,256,768]{2,1,0:T(8,128)(2,1)}), bf16[8,256,768]{2,1,0:T(8,128)(2,1)}, u32[]{:S(2)}, u32[]{:S(2)}) async-start(bf16[8,256,768]{2,1,0:T(8,128)(2,1)} %after.5), calls=%async_computation | async-start | bytes 6291456 | tf_op jit(solution)/shard_map/all_to_all | solution.py:488
  50.4 2.8 %copy-start.5 = (bf16[64,5120]{1,0:T(8,128)(2,1)S(1)}, bf16[64,5120]{1,0:T(8,128)(2,1)}, u32[]{:S(2)}) copy-start(bf16[64,5120]{1,0:T(8,128)(2,1)} %copy-done.4) | copy-start | bytes 1966084
  53.1 5.2 %collective-permute-start.8 = (bf16[128,5120]{1,0:T(8,128)(2,1)S(1)}, bf16[128,5120]{1,0:T(8,128)(2,1)S(1)}, u32[]{:S(2)}, u32[]{:S(2)}) collective-permute-start(bf16[128,5120]{1,0:T(8,128)(2,1)S(1)} %modulated_norm.5.refs_1_), channel_id=1, source_target_pairs={{0,2},{2,0},{4,6},{6,4},{1,3},{3,1},{5,7},{7,5},{8,10},{10,8},{12,... | collective-permute-start | bytes 3932168 | tf_op jit(solution)/shard_map/ppermute | solution.py:28
  54.7 6.5 %copy-start.7 = (bf16[128,5120]{1,0:T(8,128)(2,1)S(1)}, bf16[128,5120]{1,0:T(8,128)(2,1)}, u32[]{:S(2)}) copy-start(bf16[128,5120]{1,0:T(8,128)(2,1)} %copy-done.6) | copy-start | bytes 3932164
  54.7 3.6 %collective-permute-start.9 = (bf16[128,5120]{1,0:T(8,128)(2,1)S(1)}, bf16[128,5120]{1,0:T(8,128)(2,1)S(1)}, u32[]{:S(2)}, u32[]{:S(2)}) collective-permute-start(bf16[128,5120]{1,0:T(8,128)(2,1)S(1)} %modulated_norm.6.refs_2_), channel_id=1, source_target_pairs={{0,2},{2,0},{4,6},{6,4},{1,3},{3,1},{5,7},{7,5},{8,10},{10,8},{12,... | collective-permute-start | bytes 3932168 | tf_op jit(solution)/shard_map/ppermute | solution.py:28
  58.1 3.1 %collective-permute-start.10 = (bf16[128,5120]{1,0:T(8,128)(2,1)S(1)}, bf16[128,5120]{1,0:T(8,128)(2,1)S(1)}, u32[]{:S(2)}, u32[]{:S(2)}) collective-permute-start(bf16[128,5120]{1,0:T(8,128)(2,1)S(1)} %modulated_norm.7.refs_3_), channel_id=1, source_target_pairs={{0,2},{2,0},{4,6},{6,4},{1,3},{3,1},{5,7},{7,5},{8,10},{10,8},{12,... | collective-permute-start | bytes 3932168 | tf_op jit(solution)/shard_map/ppermute | solution.py:28
  61.2 23.4 %copy-start.8 = (s32[1,4,6]{2,1,0:T(4,128)S(1)}, s32[1,4,6]{2,1,0:T(4,128)}, u32[]{:S(2)}) copy-start(s32[1,4,6]{2,1,0:T(4,128)} %param.11) | copy-start | bytes 292
  84.6 4.5 %copy-start.1 = (bf16[1,384,5120]{2,1,0:T(8,128)(2,1)S(1)}, bf16[1,384,5120]{2,1,0:T(8,128)(2,1)}, u32[]{:S(2)}) copy-start(bf16[1,384,5120]{2,1,0:T(8,128)(2,1)} %param.9) | copy-start | bytes 11796484
  89.0 3.6 %collective-permute-start.12 = (bf16[512,384]{1,0:T(8,128)(2,1)S(1)}, bf16[512,384]{1,0:T(8,128)(2,1)S(1)}, u32[]{:S(2)}, u32[]{:S(2)}) collective-permute-start(bf16[512,384]{1,0:T(8,128)(2,1)S(1)} %get-tuple-element.56.refs_2_), channel_id=1, source_target_pairs={{0,2},{2,0},{4,6},{6,4},{1,3},{3,1},{5,7},{7,5},{8,10},{10,8},{12,... | collective-permute-start | bytes 1179656 | tf_op jit(solution)/shard_map/ppermute | solution.py:28
  94.0 10.6 %collective-permute-start.13 = (bf16[128,1280]{1,0:T(8,128)(2,1)S(1)}, bf16[128,1280]{1,0:T(8,128)(2,1)S(1)}, u32[]{:S(2)}, u32[]{:S(2)}) collective-permute-start(bf16[128,1280]{1,0:T(8,128)(2,1)S(1)} %get-tuple-element.59), channel_id=1, source_target_pairs={{0,1},{1,0},{2,3},{3,2},{4,5},{5,4},{6,7},{7,6},{8,9},{9,8},{10,11... | collective-permute-start | bytes 983048 | tf_op jit(solution)/shard_map/ppermute | solution.py:28
  95.1 10.5 %collective-permute-start.14 = (bf16[128,1280]{1,0:T(8,128)(2,1)S(1)}, bf16[128,1280]{1,0:T(8,128)(2,1)S(1)}, u32[]{:S(2)}, u32[]{:S(2)}) collective-permute-start(bf16[128,1280]{1,0:T(8,128)(2,1)S(1)} %get-tuple-element.60), channel_id=1, source_target_pairs={{0,4},{2,6},{4,0},{6,2},{1,5},{3,7},{5,1},{7,3},{8,12},{10,14},{12... | collective-permute-start | bytes 983048 | tf_op jit(solution)/shard_map/ppermute | solution.py:28
  99.3 12.3 %collective-permute-start.17 = (bf16[128,1280]{1,0:T(8,128)(2,1)S(1)}, bf16[128,1280]{1,0:T(8,128)(2,1)S(1)}, u32[]{:S(2)}, u32[]{:S(2)}) collective-permute-start(bf16[128,1280]{1,0:T(8,128)(2,1)S(1)} %get-tuple-element.68), channel_id=1, source_target_pairs={{0,1},{1,0},{2,3},{3,2},{4,5},{5,4},{6,7},{7,6},{8,9},{9,8},{10,11... | collective-permute-start | bytes 983048 | tf_op jit(solution)/shard_map/ppermute | solution.py:28
  99.7 12.9 %collective-permute-start.18 = (bf16[128,1280]{1,0:T(8,128)(2,1)S(1)}, bf16[128,1280]{1,0:T(8,128)(2,1)S(1)}, u32[]{:S(2)}, u32[]{:S(2)}) collective-permute-start(bf16[128,1280]{1,0:T(8,128)(2,1)S(1)} %get-tuple-element.69), channel_id=1, source_target_pairs={{0,4},{2,6},{4,0},{6,2},{1,5},{3,7},{5,1},{7,3},{8,12},{10,14},{12... | collective-permute-start | bytes 983048 | tf_op jit(solution)/shard_map/ppermute | solution.py:28
  107.5 10.4 %collective-permute-start.15 = (bf16[128,1152]{1,0:T(8,128)(2,1)S(1)}, bf16[128,1152]{1,0:T(8,128)(2,1)S(1)}, u32[]{:S(2)}, u32[]{:S(2)}) collective-permute-start(bf16[128,1152]{1,0:T(8,128)(2,1)S(1)} %get-tuple-element.64), channel_id=1, source_target_pairs={{0,1},{1,0},{2,3},{3,2},{4,5},{5,4},{6,7},{7,6},{8,9},{9,8},{10,11... | collective-permute-start | bytes 884744 | tf_op jit(solution)/shard_map/ppermute | solution.py:28
  108.6 10.4 %collective-permute-start.16 = (bf16[128,1152]{1,0:T(8,128)(2,1)S(1)}, bf16[128,1152]{1,0:T(8,128)(2,1)S(1)}, u32[]{:S(2)}, u32[]{:S(2)}) collective-permute-start(bf16[128,1152]{1,0:T(8,128)(2,1)S(1)} %get-tuple-element.65), channel_id=1, source_target_pairs={{0,4},{2,6},{4,0},{6,2},{1,5},{3,7},{5,1},{7,3},{8,12},{10,14},{12... | collective-permute-start | bytes 884744 | tf_op jit(solution)/shard_map/ppermute | solution.py:28
  115.1 11.2 %collective-permute-start.20 = (bf16[128,1408]{1,0:T(8,128)(2,1)S(1)}, bf16[128,1408]{1,0:T(8,128)(2,1)S(1)}, u32[]{:S(2)}, u32[]{:S(2)}) collective-permute-start(bf16[128,1408]{1,0:T(8,128)(2,1)S(1)} %get-tuple-element.72), channel_id=1, source_target_pairs={{0,1},{1,0},{2,3},{3,2},{4,5},{5,4},{6,7},{7,6},{8,9},{9,8},{10,11... | collective-permute-start | bytes 1081352 | tf_op jit(solution)/shard_map/ppermute | solution.py:28
  116.1 10.9 %collective-permute-start.21 = (bf16[128,1408]{1,0:T(8,128)(2,1)S(1)}, bf16[128,1408]{1,0:T(8,128)(2,1)S(1)}, u32[]{:S(2)}, u32[]{:S(2)}) collective-permute-start(bf16[128,1408]{1,0:T(8,128)(2,1)S(1)} %get-tuple-element.73), channel_id=1, source_target_pairs={{0,4},{2,6},{4,0},{6,2},{1,5},{3,7},{5,1},{7,3},{8,12},{10,14},{12... | collective-permute-start | bytes 1081352 | tf_op jit(solution)/shard_map/ppermute | solution.py:28
  119.1 13.2 %collective-permute-start.19 = (bf16[128,1280]{1,0:T(8,128)(2,1)S(1)}, bf16[128,1280]{1,0:T(8,128)(2,1)S(1)}, u32[]{:S(2)}, u32[]{:S(2)}) collective-permute-start(bf16[128,1280]{1,0:T(8,128)(2,1)S(1)} %sum_stage.18.refs_10_), channel_id=1, source_target_pairs={{0,8},{8,16},{16,24},{24,0},{1,9},{9,17},{17,25},{25,1},{2,10},{10... | collective-permute-start | bytes 983048 | tf_op jit(solution)/shard_map/ppermute | solution.py:23
  123.1 8.9 %collective-permute-start.23 = (bf16[128,1024]{1,0:T(8,128)(2,1)S(1)}, bf16[128,1024]{1,0:T(8,128)(2,1)S(1)}, u32[]{:S(2)}, u32[]{:S(2)}) collective-permute-start(bf16[128,1024]{1,0:T(8,128)(2,1)S(1)} %get-tuple-element.78), channel_id=1, source_target_pairs={{0,1},{1,0},{2,3},{3,2},{4,5},{5,4},{6,7},{7,6},{8,9},{9,8},{10,11... | collective-permute-start | bytes 786440 | tf_op jit(solution)/shard_map/ppermute | solution.py:28
  124.2 8.0 %collective-permute-start.24 = (bf16[128,1024]{1,0:T(8,128)(2,1)S(1)}, bf16[128,1024]{1,0:T(8,128)(2,1)S(1)}, u32[]{:S(2)}, u32[]{:S(2)}) collective-permute-start(bf16[128,1024]{1,0:T(8,128)(2,1)S(1)} %get-tuple-element.79), channel_id=1, source_target_pairs={{0,4},{2,6},{4,0},{6,2},{1,5},{3,7},{5,1},{7,3},{8,12},{10,14},{12... | collective-permute-start | bytes 786440 | tf_op jit(solution)/shard_map/ppermute | solution.py:28
  127.1 12.1 %collective-permute-start.22 = (bf16[128,1280]{1,0:T(8,128)(2,1)S(1)}, bf16[128,1280]{1,0:T(8,128)(2,1)S(1)}, u32[]{:S(2)}, u32[]{:S(2)}) collective-permute-start(bf16[128,1280]{1,0:T(8,128)(2,1)S(1)} %sum_stage.20.refs_10_), channel_id=1, source_target_pairs={{0,8},{8,16},{16,24},{24,0},{1,9},{9,17},{17,25},{25,1},{2,10},{10... | collective-permute-start | bytes 983048 | tf_op jit(solution)/shard_map/ppermute | solution.py:23
  130.9 7.1 %collective-permute-start.26 = (bf16[128,896]{1,0:T(8,128)(2,1)S(1)}, bf16[128,896]{1,0:T(8,128)(2,1)S(1)}, u32[]{:S(2)}, u32[]{:S(2)}) collective-permute-start(bf16[128,896]{1,0:T(8,128)(2,1)S(1)} %get-tuple-element.84), channel_id=1, source_target_pairs={{0,1},{1,0},{2,3},{3,2},{4,5},{5,4},{6,7},{7,6},{8,9},{9,8},{10,11... | collective-permute-start | bytes 688136 | tf_op jit(solution)/shard_map/ppermute | solution.py:28
  132.1 7.1 %collective-permute-start.27 = (bf16[128,896]{1,0:T(8,128)(2,1)S(1)}, bf16[128,896]{1,0:T(8,128)(2,1)S(1)}, u32[]{:S(2)}, u32[]{:S(2)}) collective-permute-start(bf16[128,896]{1,0:T(8,128)(2,1)S(1)} %get-tuple-element.85), channel_id=1, source_target_pairs={{0,4},{2,6},{4,0},{6,2},{1,5},{3,7},{5,1},{7,3},{8,12},{10,14},{12... | collective-permute-start | bytes 688136 | tf_op jit(solution)/shard_map/ppermute | solution.py:28
  132.2 10.9 %collective-permute-start.25 = (bf16[128,512]{1,0:T(8,128)(2,1)S(1)}, bf16[128,512]{1,0:T(8,128)(2,1)S(1)}, u32[]{:S(2)}, u32[]{:S(2)}) collective-permute-start(bf16[128,512]{1,0:T(8,128)(2,1)S(1)} %sum_stage.22.refs_6_), channel_id=1, source_target_pairs={{0,8},{8,16},{16,24},{24,0},{1,9},{9,17},{17,25},{25,1},{2,10},{10... | collective-permute-start | bytes 393224 | tf_op jit(solution)/shard_map/ppermute | solution.py:23
  134.0 7.9 %collective-permute-start.29 = (bf16[128,384]{1,0:T(8,128)(2,1)S(1)}, bf16[128,384]{1,0:T(8,128)(2,1)S(1)}, u32[]{:S(2)}, u32[]{:S(2)}) collective-permute-start(bf16[128,384]{1,0:T(8,128)(2,1)S(1)} %get-tuple-element.90), channel_id=1, source_target_pairs={{0,1},{1,0},{2,3},{3,2},{4,5},{5,4},{6,7},{7,6},{8,9},{9,8},{10,11... | collective-permute-start | bytes 294920 | tf_op jit(solution)/shard_map/ppermute | solution.py:28
  138.1 5.0 %collective-permute-start.30 = (bf16[128,384]{1,0:T(8,128)(2,1)S(1)}, bf16[128,384]{1,0:T(8,128)(2,1)S(1)}, u32[]{:S(2)}, u32[]{:S(2)}) collective-permute-start(bf16[128,384]{1,0:T(8,128)(2,1)S(1)} %get-tuple-element.91), channel_id=1, source_target_pairs={{0,4},{2,6},{4,0},{6,2},{1,5},{3,7},{5,1},{7,3},{8,12},{10,14},{12... | collective-permute-start | bytes 294920 | tf_op jit(solution)/shard_map/ppermute | solution.py:28
  139.2 9.8 %collective-permute-start.28 = (bf16[128,768]{1,0:T(8,128)(2,1)S(1)}, bf16[128,768]{1,0:T(8,128)(2,1)S(1)}, u32[]{:S(2)}, u32[]{:S(2)}) collective-permute-start(bf16[128,768]{1,0:T(8,128)(2,1)S(1)} %sum_stage.24.refs_6_), channel_id=1, source_target_pairs={{0,8},{8,16},{16,24},{24,0},{1,9},{9,17},{17,25},{25,1},{2,10},{10... | collective-permute-start | bytes 589832 | tf_op jit(solution)/shard_map/ppermute | solution.py:23
  141.0 4.3 %collective-permute-start.32 = (bf16[128,256]{1,0:T(8,128)(2,1)S(1)}, bf16[128,256]{1,0:T(8,128)(2,1)S(1)}, u32[]{:S(2)}, u32[]{:S(2)}) collective-permute-start(bf16[128,256]{1,0:T(8,128)(2,1)S(1)} %get-tuple-element.96), channel_id=1, source_target_pairs={{0,1},{1,0},{2,3},{3,2},{4,5},{5,4},{6,7},{7,6},{8,9},{9,8},{10,11... | collective-permute-start | bytes 196616 | tf_op jit(solution)/shard_map/ppermute | solution.py:28
  141.9 4.3 %collective-permute-start.33 = (bf16[128,256]{1,0:T(8,128)(2,1)S(1)}, bf16[128,256]{1,0:T(8,128)(2,1)S(1)}, u32[]{:S(2)}, u32[]{:S(2)}) collective-permute-start(bf16[128,256]{1,0:T(8,128)(2,1)S(1)} %get-tuple-element.97), channel_id=1, source_target_pairs={{0,4},{2,6},{4,0},{6,2},{1,5},{3,7},{5,1},{7,3},{8,12},{10,14},{12... | collective-permute-start | bytes 196616 | tf_op jit(solution)/shard_map/ppermute | solution.py:28
  143.2 7.9 %collective-permute-start.31 = (bf16[128,768]{1,0:T(8,128)(2,1)S(1)}, bf16[128,768]{1,0:T(8,128)(2,1)S(1)}, u32[]{:S(2)}, u32[]{:S(2)}) collective-permute-start(bf16[128,768]{1,0:T(8,128)(2,1)S(1)} %sum_stage.26.refs_5_), channel_id=1, source_target_pairs={{0,8},{8,16},{16,24},{24,0},{1,9},{9,17},{17,25},{25,1},{2,10},{10... | collective-permute-start | bytes 589832 | tf_op jit(solution)/shard_map/ppermute | solution.py:23
  146.2 6.8 %collective-permute-start.34 = (bf16[128,512]{1,0:T(8,128)(2,1)S(1)}, bf16[128,512]{1,0:T(8,128)(2,1)S(1)}, u32[]{:S(2)}, u32[]{:S(2)}) collective-permute-start(bf16[128,512]{1,0:T(8,128)(2,1)S(1)} %sum_stage.27), channel_id=1, source_target_pairs={{0,8},{8,16},{16,24},{24,0},{1,9},{9,17},{17,25},{25,1},{2,10},{10... | collective-permute-start | bytes 393224 | tf_op jit(solution)/shard_map/ppermute | solution.py:23
  153.1 1.1 copy-start.10

commit v19 on v18

--- a/solution.py
+++ b/solution.py
@@ -12,7 +12,7 @@
 MIB = 2**20
 SPARE = 39
 LOG2E = 1.4426950408889634
-CHUNK_SHARES = (5, 5, 2, 3, 3, 2)
+CHUNKS = ((8, 4), (15, 5), (0, 3), (3, 3), (12, 3), (6, 2))
 
 guidance_scale = 5.0
 SHORT = pl.CostEstimate(flops=1, bytes_accessed=1, transcendentals=0)
@@ -287,10 +287,10 @@
     )(visible, heads, context)
 
 
-def attend_second_kernel(visible_ref, queries_ref, pool_ref, *refs):
+def attend_second_kernel(visible_ref, queries_ref, pool_ref, *refs, start):
     weights_ref, core_weights_ref = refs[:2]
     out_ref, both_ref, sems = refs[-3:]
-    depth, columns = weights_ref.shape[0], pl.ds(0, both_ref.shape[1])
+    depth, columns = weights_ref.shape[0], pl.ds(start, both_ref.shape[1])
     copies = [
         pltpu.make_async_copy(
             ref.at[:, columns], both_ref.at[pl.ds(core * depth, depth)], sems.at[core]
@@ -304,17 +304,17 @@
         copy.wait()
 
 
-def attend_second(queries, pool, visible, weights, core_weights, columns, earlier):
+def attend_second(queries, pool, visible, weights, core_weights, chunk, earlier):
     number, rows, _ = queries.shape
     return pl.pallas_call(
-        attend_second_kernel,
+        functools.partial(attend_second_kernel, start=chunk[0]),
         in_specs=[pl.BlockSpec(memory_space=pltpu.SMEM)]
         + [pl.BlockSpec(memory_space=pltpu.VMEM)] * 2
         + [pl.BlockSpec(memory_space=pl.ANY)] * (2 + len(earlier)),
         out_specs=[pl.BlockSpec(memory_space=pltpu.VMEM)] * 2,
         out_shape=[
             jax.ShapeDtypeStruct((rows // 2, number * HD), jnp.bfloat16),
-            jax.ShapeDtypeStruct((2 * weights.shape[0], columns), weights.dtype),
+            jax.ShapeDtypeStruct((2 * weights.shape[0], chunk[1]), weights.dtype),
         ],
         scratch_shapes=[pltpu.SemaphoreType.DMA((2,))],
         name="attend_second",
@@ -490,15 +490,13 @@
 
     heads = project(near + far, project_in[0])
     gates = jnp.concatenate([modulate[2:3], other_modulate[2:3]], axis=0)
-    count = len(CHUNK_SHARES)
-    unit = features // sum(CHUNK_SHARES)
-    chunks = [
-        (sum(CHUNK_SHARES[:index]) * unit, share * unit) for index, share in enumerate(CHUNK_SHARES)
-    ]
+    count = len(CHUNKS)
+    unit = features // 20
+    chunks = [(start * unit, width * unit) for start, width in CHUNKS]
     for_core, queries, pool = attend_first(heads, context, visible[0])
     core_attended = from_partner(for_core, "sp", 1)
     attended, first_weights = attend_second(
-        queries, pool, visible[0], project_out[0], core_weights, chunks[0][1], (for_core, gates)
+        queries, pool, visible[0], project_out[0], core_weights, chunks[0], (for_core, gates)
     )
 
     kept, left, flights, arrivals, earlier = {}, {}, {}, [], []
@@ -533,7 +531,8 @@
         if middle:
             left[index] = (outs["first_left_out"], outs["second_left_out"])
         earlier = [list(outs.values())[-1]] + (arrivals[-2:-1] if 3 <= index < count else [])
-    return jnp.concatenate(arrivals, axis=1)[None, None]
+    in_order = sorted(range(count), key=lambda index: chunks[index][0])
+    return jnp.concatenate([arrivals[index] for index in in_order], axis=1)[None, None]
 
 
 def solution(mesh):

time: 155 us -> 154 us (level)
  transfers between devices with their start and end apart: 36 -> 36, of which waited for: 18 -> 19; matrix products, arithmetic and copies ran while one was open for 13% -> 13% of each run, Pallas kernels for 30% -> 31%
where the time goes in v19:
time: 154 us; the launch traced here: 153 us
  Pallas kernels  50.4 us (33%)
  starting transfers between devices  41.6 us (27%)
  waiting for transfers between devices  36.2 us (24%)
  local copies, waits for them, and re-layouts  24.6 us (16%)
    ppermute x29, starting transfers between devices, from_partner(): return lax.ppermute(value, axis, pairs)  26.7 us
    ppermute x29, waiting for transfers between devices, from_partner(): return lax.ppermute(value, axis, pairs)  26.5 us
    pallas_call x1, Pallas kernels, project(): pl.pallas_call(functools.partial(project_kernel, blocks=len(blocks)), gri...  19.2 us
    pallas_call x14, Pallas kernels, stage(): pl.pallas_call(functools.partial(stage_kernel, parts=parts, start=start,...  12.8 us
    ppermute x6, starting transfers between devices, from_behind(): return lax.ppermute(x, axis, [(i, (i + by) % count) for i in range(count)])  10.3 us
    pallas_call x4, Pallas kernels, modulated_norm(): pl.pallas_call(norm_kernel, in_specs=[pl.BlockSpec(memory_space=pltpu.VME...  8.49 us
    reshape x1, local copies, waits for them, and re-layouts, per_device(): unpacked.transpose(2, 0, 1, 3).reshape(devices, context_rows, 2 * width)  8.06 us
    another operation x1, local copies, waits for them, and re-layouts, per_device(): unpacked = stale_cache[0, 0].reshape(context_rows, 2, devices, width)  8 us
  transfers between devices with their start and end apart: 36, of which 19 were waited for; matrix products, arithmetic and copies ran while one was open for 13% of the time, Pallas kernels for 31%

profile of v19, /device:TPU:0, one launch (start us, length us, event | category | flops | bytes accessed | tf_op | source)
XLA Modules:
  0.0 153.2 jit_solution(11221625247225987790)
XLA Ops:
  0.0 2.2 %halves_of.1 = (bf16[64,5120]{1,0:T(8,128)(2,1)}, bf16[64,5120]{1,0:T(8,128)(2,1)}) custom-call(bf16[128,5120]{1,0:T(8,128)(2,1)} %bitcast.15), custom_call_target="tpu_custom_call" | custom-call | flops 1 | bytes 1 | tf_op jit(solution)/shard_map/halves_of/pallas_call | solution.py:87
  2.2 3.0 %collective-permute-start.1 = (bf16[64,5120]{1,0:T(8,128)(2,1)}, bf16[64,5120]{1,0:T(8,128)(2,1)S(1)}, u32[]{:S(2)}, u32[]{:S(2)}) collective-permute-start(bf16[64,5120]{1,0:T(8,128)(2,1)} %get-tuple-element.52), channel_id=1, source_target_pairs={{0,1},{1,0},{2,3},{3,2},{4,5},{5,4},{6,7},{7,6},{8,9},{9,8},{10,11... | collective-permute-start | bytes 1966088 | tf_op jit(solution)/shard_map/ppermute | solution.py:28
  5.2 1.5 collective-permute-start.4
  6.8 0.5 collective-permute-start.3
  7.3 8.0 %reshape_squeeze.3.refs_0_ = bf16[256,2,8,384]{3,2,1,0:T(8,128)(2,1)} reshape(bf16[1,1,256,2,3072]{4,3,2,1,0:T(2,128)(2,1)} %param.10) | data formatting | bytes 6291456 | tf_op jit(solution)/shard_map/reshape;squeeze | solution.py:469
  15.3 5.7 %collective-permute-done.1.value_ref = bf16[64,5120]{1,0:T(8,128)(2,1)S(1)} collective-permute-done((bf16[64,5120]{1,0:T(8,128)(2,1)}, bf16[64,5120]{1,0:T(8,128)(2,1)S(1)}, u32[]{:S(2)}, u32[]{:S(2)}) %collective-permute-start.1) | collective-permute-done | bytes 655392 | tf_op jit(solution)/shard_map/ppermute | solution.py:28
  21.0 1.9 %copy-done.2 = bf16[256,2,8,384]{3,2,1,0:T(8,128)(2,1)S(1)} copy-done((bf16[256,2,8,384]{3,2,1,0:T(8,128)(2,1)S(1)}, bf16[256,2,8,384]{3,2,1,0:T(8,128)(2,1)}, u32[]{:S(2)}) %copy-start.2) | copy-done | bytes 3145752
  22.9 2.1 %collective-permute-start.5 = (bf16[64,5120]{1,0:T(8,128)(2,1)S(1)}, bf16[64,5120]{1,0:T(8,128)(2,1)}, u32[]{:S(2)}, u32[]{:S(2)}) collective-permute-start(bf16[64,5120]{1,0:T(8,128)(2,1)S(1)} %after.3.refs_0_), channel_id=1, source_target_pairs={{0,4},{2,6},{4,0},{6,2},{1,5},{3,7},{5,1},{7,3},{8,12},{10,14},{12... | collective-permute-start | bytes 1966088 | tf_op jit(solution)/shard_map/ppermute | solution.py:28
  25.0 1.8 %collective-permute-start.6 = (bf16[64,5120]{1,0:T(8,128)(2,1)S(1)}, bf16[64,5120]{1,0:T(8,128)(2,1)}, u32[]{:S(2)}, u32[]{:S(2)}) collective-permute-start(bf16[64,5120]{1,0:T(8,128)(2,1)S(1)} %after.4.refs_1_), channel_id=1, source_target_pairs={{0,1},{1,0},{2,3},{3,2},{4,5},{5,4},{6,7},{7,6},{8,9},{9,8},{10,11... | collective-permute-start | bytes 1966088 | tf_op jit(solution)/shard_map/ppermute | solution.py:28
  27.1 1.5 modulated_norm.4.refs_0_
  28.7 1.0 copy-done.6
  29.7 4.1 %copy.11 = bf16[8,256,2,384]{3,2,1,0:T(2,128)(2,1)} copy(bf16[8,256,2,384]{3,0,2,1:T(8,128)(2,1)S(1)} %bitcast.38) | data formatting | bytes 6291456 | tf_op jit(solution)/shard_map/transpose | solution.py:470
  33.8 8.1 %reshape.8.value_ref = bf16[8,256,768]{2,1,0:T(8,128)(2,1)} reshape(bf16[8,256,2,384]{3,2,1,0:T(2,128)(2,1)} %copy.11) | data formatting | bytes 6291456 | tf_op jit(solution)/shard_map/reshape | solution.py:470
  41.8 0.5 collective-permute-start.11
  42.7 4.6 %all-to-all-start = ((bf16[8,256,768]{2,1,0:T(8,128)(2,1)}), bf16[8,256,768]{2,1,0:T(8,128)(2,1)}, u32[]{:S(2)}, u32[]{:S(2)}) async-start(bf16[8,256,768]{2,1,0:T(8,128)(2,1)} %after.5), calls=%async_computation | async-start | bytes 6291456 | tf_op jit(solution)/shard_map/all_to_all | solution.py:488
  47.3 3.1 %collective-permute-done = f32[1,1,3,5120]{3,2,1,0:T(4,128)S(1)} collective-permute-done((f32[1,1,3,5120]{3,2,1,0:T(4,128)S(1)}, f32[1,1,3,5120]{3,2,1,0:T(4,128)S(1)}, u32[]{:S(2)}, u32[]{:S(2)}) %collective-permute-start) | collective-permute-done | bytes 61472 | tf_op jit(solution)/shard_map/ppermute | solution.py:28
  50.4 2.7 %modulated_norm.5.refs_1_ = bf16[128,5120]{1,0:T(8,128)(2,1)S(1)} custom-call(bf16[64,5120]{1,0:T(8,128)(2,1)S(1)} %after.3.refs_0_, bf16[64,5120]{1,0:T(8,128)(2,1)} %collective-permute-done.2.refs_1_.refs_0_, f32[3,5120]{1,0:T(4,128)S(1)} %bitcast.41), custom_call_target="tpu_custom_call" | custom-call | flops 1 | bytes 1 | tf_op jit(solution)/shard_map/modulated_norm/pallas_call | solution.py:55
  53.2 1.5 modulated_norm.6.refs_2_
  54.7 0.6 collective-permute-start.9
  55.3 2.8 %modulated_norm.7.refs_3_ = bf16[128,5120]{1,0:T(8,128)(2,1)S(1)} custom-call(bf16[64,5120]{1,0:T(8,128)(2,1)} %collective-permute-done.5.refs_0_, bf16[64,5120]{1,0:T(8,128)(2,1)} %collective-permute-done.6.refs_1_, f32[3,5120]{1,0:T(4,128)S(1)} %bitcast.42), custom_call_target="tpu_custom_call" | custom-call | flops 1 | bytes 1 | tf_op jit(solution)/shard_map/modulated_norm/pallas_call | solution.py:55
  58.3 2.9 %collective-permute-done.10.refs_7_ = bf16[128,5120]{1,0:T(8,128)(2,1)S(1)} collective-permute-done((bf16[128,5120]{1,0:T(8,128)(2,1)S(1)}, bf16[128,5120]{1,0:T(8,128)(2,1)S(1)}, u32[]{:S(2)}, u32[]{:S(2)}) %collective-permute-start.10) | collective-permute-done | bytes 1310752 | tf_op jit(solution)/shard_map/ppermute | solution.py:28
  61.2 19.2 %project_heads.1.heads_in = bf16[48,1024,128]{2,1,0:T(8,128)(2,1)} custom-call(bf16[128,5120]{1,0:T(8,128)(2,1)S(1)} %copy-done.7, bf16[128,5120]{1,0:T(8,128)(2,1)S(1)} %modulated_norm.5.refs_1_, bf16[128,5120]{1,0:T(8,128)(2,1)S(1)} %modulated_norm.6.refs_2_, bf16[128,5120]{1,0:T(8,128)(2,1)S(1)} %modulated_norm.7.refs_3_, ...), custom_call_target="tpu_custom_call" | custom-call | flops 12079595520 | bytes 22282240 | tf_op jit(solution)/shard_map/project_heads/pallas_call | solution.py:161
  80.4 4.2 %all-to-all-done = bf16[8,256,768]{2,1,0:T(8,128)(2,1)} async-done(((bf16[8,256,768]{2,1,0:T(8,128)(2,1)}), bf16[8,256,768]{2,1,0:T(8,128)(2,1)}, u32[]{:S(2)}, u32[]{:S(2)}) %all-to-all-start) | async-done | bytes 3145760 | tf_op jit(solution)/shard_map/all_to_all | solution.py:488
  84.6 4.3 %attend_first.1 = (bf16[512,384]{1,0:T(8,128)(2,1)S(1)}, bf16[3,1024,128]{2,1,0:T(8,128)(2,1)S(1)}, bf16[6,3072,128]{2,1,0:T(8,128)(2,1)S(1)}) custom-call(s32[4,6]{1,0:T(4,128)S(1)} %bitcast.43, bf16[48,1024,128]{2,1,0:T(8,128)(2,1)} %project_heads.1.heads_in, bf16[2048,768]{1,0:T(8,128)(2,1)} %bitcast.7.context_in), custom_call_target="tpu_custom_call" | custom-call | flops 1 | bytes 1 | tf_op jit(solution)/shard_map/attend_first/pallas_call | solution.py:270
  89.1 3.4 %attend_second.1 = (bf16[512,384]{1,0:T(8,128)(2,1)S(1)}, bf16[768,1024]{1,0:T(8,128)(2,1)S(1)}) custom-call(s32[4,6]{1,0:T(4,128)S(1)} %bitcast.44, bf16[3,1024,128]{2,1,0:T(8,128)(2,1)S(1)} %get-tuple-element.54.queries_ref, bf16[6,3072,128]{2,1,0:T(8,128)(2,1)S(1)} %get-tuple-element.55.pool_ref, bf16[384,5120]{1,0:T(8,128)(2,1)S(1)} %bitcast.32, ...), custom_call_target="tpu_custom_call" | custom-call | flops 1 | bytes 1 | tf_op jit(solution)/shard_map/attend_second/pallas_call | solution.py:309
  92.5 1.0 sum_stage.14
  93.5 1.1 collective-permute-start.13
  94.6 1.5 collective-permute-start.14
  96.1 2.7 %sum_stage.15 = (bf16[128,1280]{1,0:T(8,128)(2,1)S(1)}, bf16[128,1280]{1,0:T(8,128)(2,1)S(1)}, f32[2,128,640]{2,1,0:T(8,128)S(1)}, f32[2,128,640]{2,1,0:T(8,128)S(1)}) custom-call(bf16[128,5120]{1,0:T(8,128)(2,1)S(1)} %bitcast.18, f32[2,5120]{1,0:T(2,128)S(1)} %pad_maximum_fusion.refs_3_.refs_1_, bf16[512,384]{1,0:T(8,128)(2,1)S(1)} %get-tuple-element.57.refs_2_, ...), custom_call_target="tpu_custom_call" | custom-call | flops 1 | bytes 1 | tf_op jit(solution)/shard_map/sum_stage/pallas_call | solution.py:434
  99.2 1.2 collective-permute-start.18
  100.4 2.3 %collective-permute-done.13.refs_6_ = bf16[128,1024]{1,0:T(8,128)(2,1)S(1)} collective-permute-done((bf16[128,1024]{1,0:T(8,128)(2,1)S(1)}, bf16[128,1024]{1,0:T(8,128)(2,1)S(1)}, u32[]{:S(2)}, u32[]{:S(2)}) %collective-permute-start.13) | collective-permute-done | bytes 262176 | tf_op jit(solution)/shard_map/ppermute | solution.py:28
  102.7 1.0 collective-permute-done.14.refs_7_
  103.8 2.3 %sum_stage.16 = (bf16[128,1280]{1,0:T(8,128)(2,1)S(1)}, bf16[128,1280]{1,0:T(8,128)(2,1)S(1)}, f32[2,128,384]{2,1,0:T(8,128)S(1)}, f32[2,128,384]{2,1,0:T(8,128)...) custom-call(bf16[128,5120]{1,0:T(8,128)(2,1)S(1)} %bitcast.19, f32[2,5120]{1,0:T(2,128)S(1)} %pad_maximum_fusion.refs_3_.refs_1_, ...), custom_call_target="tpu_custom_call" | custom-call | flops 1 | bytes 1 | tf_op jit(solution)/shard_map/sum_stage/pallas_call | solution.py:434
  106.1 1.1 collective-permute-start.15
  107.2 0.8 collective-permute-start.16
  108.0 1.8 %collective-permute-done.17.refs_6_ = bf16[128,1280]{1,0:T(8,128)(2,1)S(1)} collective-permute-done((bf16[128,1280]{1,0:T(8,128)(2,1)S(1)}, bf16[128,1280]{1,0:T(8,128)(2,1)S(1)}, u32[]{:S(2)}, u32[]{:S(2)}) %collective-permute-start.17) | collective-permute-done | bytes 327712 | tf_op jit(solution)/shard_map/ppermute | solution.py:28
  109.7 1.0 collective-permute-done.18.refs_7_
  110.8 2.4 %sum_stage.17 = (bf16[128,1408]{1,0:T(8,128)(2,1)S(1)}, bf16[128,1408]{1,0:T(8,128)(2,1)S(1)}, f32[2,128,384]{2,1,0:T(8,128)S(1)}, f32[2,128,384]{2,1,0:T(8,128)...) custom-call(bf16[128,5120]{1,0:T(8,128)(2,1)S(1)} %bitcast.20, f32[2,5120]{1,0:T(2,128)S(1)} %pad_maximum_fusion.refs_3_.refs_1_, ...), custom_call_target="tpu_custom_call" | custom-call | flops 1 | bytes 1 | tf_op jit(solution)/shard_map/sum_stage/pallas_call | solution.py:434
  113.2 1.1 collective-permute-start.21
  114.2 0.8 collective-permute-start.22
  115.1 1.7 %collective-permute-done.15.refs_1_.refs_6_ = bf16[128,1280]{1,0:T(8,128)(2,1)S(1)} collective-permute-done((bf16[128,1280]{1,0:T(8,128)(2,1)S(1)}, bf16[128,1280]{1,0:T(8,128)(2,1)S(1)}, u32[]{:S(2)}, u32[]{:S(2)}) %collective-permute-start.15) | collective-permute-done | bytes 327712 | tf_op jit(solution)/shard_map/ppermute | solution.py:28
  116.8 1.0 collective-permute-done.16.refs_2_.refs_7_
  117.9 1.9 %collective-permute-start.23 = (bf16[128,1024]{1,0:T(8,128)(2,1)S(1)}, bf16[128,1024]{1,0:T(8,128)(2,1)S(1)}, u32[]{:S(2)}, u32[]{:S(2)}) collective-permute-start(bf16[128,1024]{1,0:T(8,128)(2,1)S(1)} %sum_stage.18.refs_10_), channel_id=1, source_target_pairs={{0,8},{8,16},{16,24},{24,0},{1,9},{9,17},{17,25},{25,1},{2,10},{10... | collective-permute-start | bytes 786440 | tf_op jit(solution)/shard_map/ppermute | solution.py:23
  119.7 2.2 %sum_stage.19 = (bf16[128,1152]{1,0:T(8,128)(2,1)S(1)}, bf16[128,1152]{1,0:T(8,128)(2,1)S(1)}, f32[2,128,384]{2,1,0:T(8,128)S(1)}, f32[2,128,384]{2,1,0:T(8,128)...) custom-call(bf16[128,5120]{1,0:T(8,128)(2,1)S(1)} %bitcast.22, f32[2,5120]{1,0:T(2,128)S(1)} %pad_maximum_fusion.refs_3_.refs_1_, ...), custom_call_target="tpu_custom_call" | custom-call | flops 1 | bytes 1 | tf_op jit(solution)/shard_map/sum_stage/pallas_call | solution.py:434
  122.0 1.1 collective-permute-start.19
  123.1 1.0 collective-permute-start.20
  124.1 0.5 collective-permute-done.21.refs_1_.refs_6_
  124.6 1.0 collective-permute-done.22.refs_2_.refs_7_
  125.7 1.9 %collective-permute-start.27 = (bf16[128,1280]{1,0:T(8,128)(2,1)S(1)}, bf16[128,1280]{1,0:T(8,128)(2,1)S(1)}, u32[]{:S(2)}, u32[]{:S(2)}) collective-permute-start(bf16[128,1280]{1,0:T(8,128)(2,1)S(1)} %sum_stage.20.refs_10_), channel_id=1, source_target_pairs={{0,8},{8,16},{16,24},{24,0},{1,9},{9,17},{17,25},{25,1},{2,10},{10... | collective-permute-start | bytes 983048 | tf_op jit(solution)/shard_map/ppermute | solution.py:23
  127.6 1.7 %sum_stage.21 = (bf16[128,896]{1,0:T(8,128)(2,1)S(1)}, bf16[128,896]{1,0:T(8,128)(2,1)S(1)}, f32[2,128,256]{2,1,0:T(8,128)S(1)}, f32[2,128,256]{2,1,0:T(8,128)S(...) custom-call(bf16[128,5120]{1,0:T(8,128)(2,1)S(1)} %bitcast.24, f32[2,5120]{1,0:T(2,128)S(1)} %pad_maximum_fusion.refs_3_.refs_1_, ...), custom_call_target="tpu_custom_call" | custom-call | flops 1 | bytes 1 | tf_op jit(solution)/shard_map/sum_stage/pallas_call | solution.py:434
  129.3 1.0 collective-permute-start.25
  131.2 2.2 %collective-permute-start.24 = (bf16[128,768]{1,0:T(8,128)(2,1)S(1)}, bf16[128,768]{1,0:T(8,128)(2,1)S(1)}, u32[]{:S(2)}, u32[]{:S(2)}) collective-permute-start(bf16[128,768]{1,0:T(8,128)(2,1)S(1)} %sum_stage.22.refs_6_), channel_id=1, source_target_pairs={{0,8},{8,16},{16,24},{24,0},{1,9},{9,17},{17,25},{25,1},{2,10},{10... | collective-permute-start | bytes 589832 | tf_op jit(solution)/shard_map/ppermute | solution.py:23
  133.5 1.1 collective-permute-start.31
  134.7 1.7 %collective-permute-done.25.refs_1_.refs_2_ = bf16[128,896]{1,0:T(8,128)(2,1)S(1)} collective-permute-done((bf16[128,896]{1,0:T(8,128)(2,1)S(1)}, bf16[128,896]{1,0:T(8,128)(2,1)S(1)}, u32[]{:S(2)}, u32[]{:S(2)}) %collective-permute-start.25) | collective-permute-done | bytes 229408 | tf_op jit(solution)/shard_map/ppermute | solution.py:28
  136.4 1.0 collective-permute-start.32
  137.5 1.6 %collective-permute-start.28 = (bf16[128,768]{1,0:T(8,128)(2,1)S(1)}, bf16[128,768]{1,0:T(8,128)(2,1)S(1)}, u32[]{:S(2)}, u32[]{:S(2)}) collective-permute-start(bf16[128,768]{1,0:T(8,128)(2,1)S(1)} %sum_stage.24.refs_6_), channel_id=1, source_target_pairs={{0,8},{8,16},{16,24},{24,0},{1,9},{9,17},{17,25},{25,1},{2,10},{10... | collective-permute-start | bytes 589832 | tf_op jit(solution)/shard_map/ppermute | solution.py:23
  139.2 1.6 %collective-permute-start.29 = (bf16[128,256]{1,0:T(8,128)(2,1)S(1)}, bf16[128,256]{1,0:T(8,128)(2,1)S(1)}, u32[]{:S(2)}, u32[]{:S(2)}) collective-permute-start(bf16[128,256]{1,0:T(8,128)(2,1)S(1)} %get-tuple-element.92), channel_id=1, source_target_pairs={{0,1},{1,0},{2,3},{3,2},{4,5},{5,4},{6,7},{7,6},{8,9},{9,8},{10,11... | collective-permute-start | bytes 196616 | tf_op jit(solution)/shard_map/ppermute | solution.py:28
  140.7 0.8 collective-permute-start.30
  141.8 1.2 collective-permute-start.34
  142.9 0.6 collective-permute-done.29.refs_1_
  143.5 1.5 collective-permute-done.30.refs_2_
  145.0 1.5 collective-permute-start.33
  146.8 5.2 %collective-permute-done.33 = bf16[128,512]{1,0:T(8,128)(2,1)S(1)} collective-permute-done((bf16[128,512]{1,0:T(8,128)(2,1)S(1)}, bf16[128,512]{1,0:T(8,128)(2,1)S(1)}, u32[]{:S(2)}, u32[]{:S(2)}) %collective-permute-start.33) | collective-permute-done | bytes 131104 | tf_op jit(solution)/shard_map/ppermute | solution.py:23
  152.2 1.0 copy-done.10
  (68 shorter events, 3.4 us)
Async XLA Ops:
  2.2 18.8 %collective-permute-start.1 = (bf16[64,5120]{1,0:T(8,128)(2,1)}, bf16[64,5120]{1,0:T(8,128)(2,1)S(1)}, u32[]{:S(2)}, u32[]{:S(2)}) collective-permute-start(bf16[64,5120]{1,0:T(8,128)(2,1)} %get-tuple-element.52), channel_id=1, source_target_pairs={{0,1},{1,0},{2,3},{3,2},{4,5},{5,4},{6,7},{7,6},{8,9},{9,8},{10,11... | collective-permute-start | bytes 1966088 | tf_op jit(solution)/shard_map/ppermute | solution.py:28
  5.2 19.8 %collective-permute-start.4 = (bf16[64,5120]{1,0:T(8,128)(2,1)}, bf16[64,5120]{1,0:T(8,128)(2,1)S(1)}, u32[]{:S(2)}, u32[]{:S(2)}) collective-permute-start(bf16[64,5120]{1,0:T(8,128)(2,1)} %get-tuple-element.53), channel_id=1, source_target_pairs={{0,4},{2,6},{4,0},{6,2},{1,5},{3,7},{5,1},{7,3},{8,12},{10,14},{12... | collective-permute-start | bytes 1966088 | tf_op jit(solution)/shard_map/ppermute | solution.py:28
  6.8 35.1 %collective-permute-start.3 = (bf16[64,5120]{1,0:T(8,128)(2,1)}, bf16[64,5120]{1,0:T(8,128)(2,1)S(1)}, u32[]{:S(2)}, u32[]{:S(2)}) collective-permute-start(bf16[64,5120]{1,0:T(8,128)(2,1)} %get-tuple-element.52), channel_id=1, source_target_pairs={{0,4},{2,6},{4,0},{6,2},{1,5},{3,7},{5,1},{7,3},{8,12},{10,14},{12... | collective-permute-start | bytes 1966088 | tf_op jit(solution)/shard_map/ppermute | solution.py:28
  7.3 34.6 %collective-permute-start.2 = (bf16[64,5120]{1,0:T(8,128)(2,1)}, bf16[64,5120]{1,0:T(8,128)(2,1)}, u32[]{:S(2)}, u32[]{:S(2)}) collective-permute-start(bf16[64,5120]{1,0:T(8,128)(2,1)} %get-tuple-element.53), channel_id=1, source_target_pairs={{0,1},{1,0},{2,3},{3,2},{4,5},{5,4},{6,7},{7,6},{8,9},{9,8},{10,11... | collective-permute-start | bytes 1966088 | tf_op jit(solution)/shard_map/ppermute | solution.py:28
  21.0 1.9 %copy-start.2 = (bf16[256,2,8,384]{3,2,1,0:T(8,128)(2,1)S(1)}, bf16[256,2,8,384]{3,2,1,0:T(8,128)(2,1)}, u32[]{:S(2)}) copy-start(bf16[256,2,8,384]{3,2,1,0:T(8,128)(2,1)} %reshape_squeeze.3.refs_0_) | copy-start | bytes 9437188
  22.9 2.1 %copy-start.3 = (bf16[256,2,8,384]{3,2,1,0:T(8,128)(2,1)S(1)}, bf16[256,2,8,384]{3,2,1,0:T(8,128)(2,1)}, u32[]{:S(2)}) copy-start(bf16[256,2,8,384]{3,2,1,0:T(8,128)(2,1)} %reshape_squeeze.3.refs_0_) | copy-start | bytes 9437188
  22.9 3.9 %copy-start.9 = (f32[1,1,3,5120]{3,1,2,0:T(1,128)S(1)}, f32[1,1,3,5120]{3,1,2,0:T(1,128)}, u32[]{:S(2)}) copy-start(f32[1,1,3,5120]{3,1,2,0:T(1,128)} %param.7) | copy-start | bytes 184324
  22.9 4.2 %copy-start = (bf16[1,1,128,5120]{3,2,1,0:T(8,128)(2,1)S(1)}, bf16[1,1,128,5120]{3,2,1,0:T(8,128)(2,1)}, u32[]{:S(2)}) copy-start(bf16[1,1,128,5120]{3,2,1,0:T(8,128)(2,1)} %param.6) | copy-start | bytes 3932164
  22.9 31.8 %collective-permute-start.5 = (bf16[64,5120]{1,0:T(8,128)(2,1)S(1)}, bf16[64,5120]{1,0:T(8,128)(2,1)}, u32[]{:S(2)}, u32[]{:S(2)}) collective-permute-start(bf16[64,5120]{1,0:T(8,128)(2,1)S(1)} %after.3.refs_0_), channel_id=1, source_target_pairs={{0,4},{2,6},{4,0},{6,2},{1,5},{3,7},{5,1},{7,3},{8,12},{10,14},{12... | collective-permute-start | bytes 1966088 | tf_op jit(solution)/shard_map/ppermute | solution.py:28
  25.0 30.3 %collective-permute-start.6 = (bf16[64,5120]{1,0:T(8,128)(2,1)S(1)}, bf16[64,5120]{1,0:T(8,128)(2,1)}, u32[]{:S(2)}, u32[]{:S(2)}) collective-permute-start(bf16[64,5120]{1,0:T(8,128)(2,1)S(1)} %after.4.refs_1_), channel_id=1, source_target_pairs={{0,1},{1,0},{2,3},{3,2},{4,5},{5,4},{6,7},{7,6},{8,9},{9,8},{10,11... | collective-permute-start | bytes 1966088 | tf_op jit(solution)/shard_map/ppermute | solution.py:28
  26.9 23.6 %collective-permute-start = (f32[1,1,3,5120]{3,2,1,0:T(4,128)S(1)}, f32[1,1,3,5120]{3,2,1,0:T(4,128)S(1)}, u32[]{:S(2)}, u32[]{:S(2)}) collective-permute-start(f32[1,1,3,5120]{3,2,1,0:T(4,128)S(1)} %copy.15), channel_id=1, source_target_pairs={{0,1},{1,0},{2,3},{3,2},{4,5},{5,4},{6,7},{7,6},{8,9},{9,8},{10,11... | collective-permute-start | bytes 184328 | tf_op jit(solution)/shard_map/ppermute | solution.py:28
  28.6 1.1 copy-start.6
  41.8 0.9 copy-start.4
  41.8 16.5 %collective-permute-start.7 = (bf16[128,5120]{1,0:T(8,128)(2,1)}, bf16[128,5120]{1,0:T(8,128)(2,1)}, u32[]{:S(2)}, u32[]{:S(2)}) collective-permute-start(bf16[128,5120]{1,0:T(8,128)(2,1)} %copy-done.6), channel_id=1, source_target_pairs={{0,2},{2,0},{4,6},{6,4},{1,3},{3,1},{5,7},{7,5},{8,10},{10,8},{12,... | collective-permute-start | bytes 3932168 | tf_op jit(solution)/shard_map/ppermute | solution.py:28
  41.8 47.2 %collective-permute-start.11 = (bf16[384,5120]{1,0:T(8,128)(2,1)}, bf16[384,5120]{1,0:T(8,128)(2,1)}, u32[]{:S(2)}, u32[]{:S(2)}) collective-permute-start(bf16[384,5120]{1,0:T(8,128)(2,1)} %bitcast.31), channel_id=1, source_target_pairs={{0,2},{2,0},{4,6},{6,4},{1,3},{3,1},{5,7},{7,5},{8,10},{10,8},{12,... | collective-permute-start | bytes 11796488 | tf_op jit(solution)/shard_map/ppermute | solution.py:28
  42.7 41.9 %all-to-all-start = ((bf16[8,256,768]{2,1,0:T(8,128)(2,1)}), bf16[8,256,768]{2,1,0:T(8,128)(2,1)}, u32[]{:S(2)}, u32[]{:S(2)}) async-start(bf16[8,256,768]{2,1,0:T(8,128)(2,1)} %after.5), calls=%async_computation | async-start | bytes 6291456 | tf_op jit(solution)/shard_map/all_to_all | solution.py:488
  50.4 2.8 %copy-start.5 = (bf16[64,5120]{1,0:T(8,128)(2,1)S(1)}, bf16[64,5120]{1,0:T(8,128)(2,1)}, u32[]{:S(2)}) copy-start(bf16[64,5120]{1,0:T(8,128)(2,1)} %copy-done.4) | copy-start | bytes 1966084
  53.1 5.2 %collective-permute-start.8 = (bf16[128,5120]{1,0:T(8,128)(2,1)S(1)}, bf16[128,5120]{1,0:T(8,128)(2,1)S(1)}, u32[]{:S(2)}, u32[]{:S(2)}) collective-permute-start(bf16[128,5120]{1,0:T(8,128)(2,1)S(1)} %modulated_norm.5.refs_1_), channel_id=1, source_target_pairs={{0,2},{2,0},{4,6},{6,4},{1,3},{3,1},{5,7},{7,5},{8,10},{10,8},{12,... | collective-permute-start | bytes 3932168 | tf_op jit(solution)/shard_map/ppermute | solution.py:28
  54.7 6.5 %copy-start.7 = (bf16[128,5120]{1,0:T(8,128)(2,1)S(1)}, bf16[128,5120]{1,0:T(8,128)(2,1)}, u32[]{:S(2)}) copy-start(bf16[128,5120]{1,0:T(8,128)(2,1)} %copy-done.6) | copy-start | bytes 3932164
  54.7 3.6 %collective-permute-start.9 = (bf16[128,5120]{1,0:T(8,128)(2,1)S(1)}, bf16[128,5120]{1,0:T(8,128)(2,1)S(1)}, u32[]{:S(2)}, u32[]{:S(2)}) collective-permute-start(bf16[128,5120]{1,0:T(8,128)(2,1)S(1)} %modulated_norm.6.refs_2_), channel_id=1, source_target_pairs={{0,2},{2,0},{4,6},{6,4},{1,3},{3,1},{5,7},{7,5},{8,10},{10,8},{12,... | collective-permute-start | bytes 3932168 | tf_op jit(solution)/shard_map/ppermute | solution.py:28
  58.1 3.1 %collective-permute-start.10 = (bf16[128,5120]{1,0:T(8,128)(2,1)S(1)}, bf16[128,5120]{1,0:T(8,128)(2,1)S(1)}, u32[]{:S(2)}, u32[]{:S(2)}) collective-permute-start(bf16[128,5120]{1,0:T(8,128)(2,1)S(1)} %modulated_norm.7.refs_3_), channel_id=1, source_target_pairs={{0,2},{2,0},{4,6},{6,4},{1,3},{3,1},{5,7},{7,5},{8,10},{10,8},{12,... | collective-permute-start | bytes 3932168 | tf_op jit(solution)/shard_map/ppermute | solution.py:28
  61.2 23.4 %copy-start.8 = (s32[1,4,6]{2,1,0:T(4,128)S(1)}, s32[1,4,6]{2,1,0:T(4,128)}, u32[]{:S(2)}) copy-start(s32[1,4,6]{2,1,0:T(4,128)} %param.11) | copy-start | bytes 292
  84.6 4.5 %copy-start.1 = (bf16[1,384,5120]{2,1,0:T(8,128)(2,1)S(1)}, bf16[1,384,5120]{2,1,0:T(8,128)(2,1)}, u32[]{:S(2)}) copy-start(bf16[1,384,5120]{2,1,0:T(8,128)(2,1)} %param.9) | copy-start | bytes 11796484
  89.0 3.5 %collective-permute-start.12 = (bf16[512,384]{1,0:T(8,128)(2,1)S(1)}, bf16[512,384]{1,0:T(8,128)(2,1)S(1)}, u32[]{:S(2)}, u32[]{:S(2)}) collective-permute-start(bf16[512,384]{1,0:T(8,128)(2,1)S(1)} %get-tuple-element.56.refs_2_), channel_id=1, source_target_pairs={{0,2},{2,0},{4,6},{6,4},{1,3},{3,1},{5,7},{7,5},{8,10},{10,8},{12,... | collective-permute-start | bytes 1179656 | tf_op jit(solution)/shard_map/ppermute | solution.py:28
  93.5 9.2 %collective-permute-start.13 = (bf16[128,1024]{1,0:T(8,128)(2,1)S(1)}, bf16[128,1024]{1,0:T(8,128)(2,1)S(1)}, u32[]{:S(2)}, u32[]{:S(2)}) collective-permute-start(bf16[128,1024]{1,0:T(8,128)(2,1)S(1)} %get-tuple-element.59), channel_id=1, source_target_pairs={{0,1},{1,0},{2,3},{3,2},{4,5},{5,4},{6,7},{7,6},{8,9},{9,8},{10,11... | collective-permute-start | bytes 786440 | tf_op jit(solution)/shard_map/ppermute | solution.py:28
  94.6 9.1 %collective-permute-start.14 = (bf16[128,1024]{1,0:T(8,128)(2,1)S(1)}, bf16[128,1024]{1,0:T(8,128)(2,1)S(1)}, u32[]{:S(2)}, u32[]{:S(2)}) collective-permute-start(bf16[128,1024]{1,0:T(8,128)(2,1)S(1)} %get-tuple-element.60), channel_id=1, source_target_pairs={{0,4},{2,6},{4,0},{6,2},{1,5},{3,7},{5,1},{7,3},{8,12},{10,14},{12... | collective-permute-start | bytes 786440 | tf_op jit(solution)/shard_map/ppermute | solution.py:28
  98.8 10.9 %collective-permute-start.17 = (bf16[128,1280]{1,0:T(8,128)(2,1)S(1)}, bf16[128,1280]{1,0:T(8,128)(2,1)S(1)}, u32[]{:S(2)}, u32[]{:S(2)}) collective-permute-start(bf16[128,1280]{1,0:T(8,128)(2,1)S(1)} %get-tuple-element.70), channel_id=1, source_target_pairs={{0,1},{1,0},{2,3},{3,2},{4,5},{5,4},{6,7},{7,6},{8,9},{9,8},{10,11... | collective-permute-start | bytes 983048 | tf_op jit(solution)/shard_map/ppermute | solution.py:28
  99.2 11.5 %collective-permute-start.18 = (bf16[128,1280]{1,0:T(8,128)(2,1)S(1)}, bf16[128,1280]{1,0:T(8,128)(2,1)S(1)}, u32[]{:S(2)}, u32[]{:S(2)}) collective-permute-start(bf16[128,1280]{1,0:T(8,128)(2,1)S(1)} %get-tuple-element.71), channel_id=1, source_target_pairs={{0,4},{2,6},{4,0},{6,2},{1,5},{3,7},{5,1},{7,3},{8,12},{10,14},{12... | collective-permute-start | bytes 983048 | tf_op jit(solution)/shard_map/ppermute | solution.py:28
  106.1 10.7 %collective-permute-start.15 = (bf16[128,1280]{1,0:T(8,128)(2,1)S(1)}, bf16[128,1280]{1,0:T(8,128)(2,1)S(1)}, u32[]{:S(2)}, u32[]{:S(2)}) collective-permute-start(bf16[128,1280]{1,0:T(8,128)(2,1)S(1)} %get-tuple-element.64), channel_id=1, source_target_pairs={{0,1},{1,0},{2,3},{3,2},{4,5},{5,4},{6,7},{7,6},{8,9},{9,8},{10,11... | collective-permute-start | bytes 983048 | tf_op jit(solution)/shard_map/ppermute | solution.py:28
  107.2 10.6 %collective-permute-start.16 = (bf16[128,1280]{1,0:T(8,128)(2,1)S(1)}, bf16[128,1280]{1,0:T(8,128)(2,1)S(1)}, u32[]{:S(2)}, u32[]{:S(2)}) collective-permute-start(bf16[128,1280]{1,0:T(8,128)(2,1)S(1)} %get-tuple-element.65), channel_id=1, source_target_pairs={{0,4},{2,6},{4,0},{6,2},{1,5},{3,7},{5,1},{7,3},{8,12},{10,14},{12... | collective-permute-start | bytes 983048 | tf_op jit(solution)/shard_map/ppermute | solution.py:28
  113.2 11.4 %collective-permute-start.21 = (bf16[128,1408]{1,0:T(8,128)(2,1)S(1)}, bf16[128,1408]{1,0:T(8,128)(2,1)S(1)}, u32[]{:S(2)}, u32[]{:S(2)}) collective-permute-start(bf16[128,1408]{1,0:T(8,128)(2,1)S(1)} %get-tuple-element.78), channel_id=1, source_target_pairs={{0,1},{1,0},{2,3},{3,2},{4,5},{5,4},{6,7},{7,6},{8,9},{9,8},{10,11... | collective-permute-start | bytes 1081352 | tf_op jit(solution)/shard_map/ppermute | solution.py:28
  114.2 11.3 %collective-permute-start.22 = (bf16[128,1408]{1,0:T(8,128)(2,1)S(1)}, bf16[128,1408]{1,0:T(8,128)(2,1)S(1)}, u32[]{:S(2)}, u32[]{:S(2)}) collective-permute-start(bf16[128,1408]{1,0:T(8,128)(2,1)S(1)} %get-tuple-element.79), channel_id=1, source_target_pairs={{0,4},{2,6},{4,0},{6,2},{1,5},{3,7},{5,1},{7,3},{8,12},{10,14},{12... | collective-permute-start | bytes 1081352 | tf_op jit(solution)/shard_map/ppermute | solution.py:28
  117.9 12.4 %collective-permute-start.23 = (bf16[128,1024]{1,0:T(8,128)(2,1)S(1)}, bf16[128,1024]{1,0:T(8,128)(2,1)S(1)}, u32[]{:S(2)}, u32[]{:S(2)}) collective-permute-start(bf16[128,1024]{1,0:T(8,128)(2,1)S(1)} %sum_stage.18.refs_10_), channel_id=1, source_target_pairs={{0,8},{8,16},{16,24},{24,0},{1,9},{9,17},{17,25},{25,1},{2,10},{10... | collective-permute-start | bytes 786440 | tf_op jit(solution)/shard_map/ppermute | solution.py:23
  122.0 8.8 %collective-permute-start.19 = (bf16[128,1152]{1,0:T(8,128)(2,1)S(1)}, bf16[128,1152]{1,0:T(8,128)(2,1)S(1)}, u32[]{:S(2)}, u32[]{:S(2)}) collective-permute-start(bf16[128,1152]{1,0:T(8,128)(2,1)S(1)} %get-tuple-element.74), channel_id=1, source_target_pairs={{0,1},{1,0},{2,3},{3,2},{4,5},{5,4},{6,7},{7,6},{8,9},{9,8},{10,11... | collective-permute-start | bytes 884744 | tf_op jit(solution)/shard_map/ppermute | solution.py:28
  123.1 8.1 %collective-permute-start.20 = (bf16[128,1152]{1,0:T(8,128)(2,1)S(1)}, bf16[128,1152]{1,0:T(8,128)(2,1)S(1)}, u32[]{:S(2)}, u32[]{:S(2)}) collective-permute-start(bf16[128,1152]{1,0:T(8,128)(2,1)S(1)} %get-tuple-element.75), channel_id=1, source_target_pairs={{0,4},{2,6},{4,0},{6,2},{1,5},{3,7},{5,1},{7,3},{8,12},{10,14},{12... | collective-permute-start | bytes 884744 | tf_op jit(solution)/shard_map/ppermute | solution.py:28
  125.7 11.8 %collective-permute-start.27 = (bf16[128,1280]{1,0:T(8,128)(2,1)S(1)}, bf16[128,1280]{1,0:T(8,128)(2,1)S(1)}, u32[]{:S(2)}, u32[]{:S(2)}) collective-permute-start(bf16[128,1280]{1,0:T(8,128)(2,1)S(1)} %sum_stage.20.refs_10_), channel_id=1, source_target_pairs={{0,8},{8,16},{16,24},{24,0},{1,9},{9,17},{17,25},{25,1},{2,10},{10... | collective-permute-start | bytes 983048 | tf_op jit(solution)/shard_map/ppermute | solution.py:23
  129.3 7.1 %collective-permute-start.25 = (bf16[128,896]{1,0:T(8,128)(2,1)S(1)}, bf16[128,896]{1,0:T(8,128)(2,1)S(1)}, u32[]{:S(2)}, u32[]{:S(2)}) collective-permute-start(bf16[128,896]{1,0:T(8,128)(2,1)S(1)} %get-tuple-element.84), channel_id=1, source_target_pairs={{0,1},{1,0},{2,3},{3,2},{4,5},{5,4},{6,7},{7,6},{8,9},{9,8},{10,11... | collective-permute-start | bytes 688136 | tf_op jit(solution)/shard_map/ppermute | solution.py:28
  130.3 7.2 %collective-permute-start.26 = (bf16[128,896]{1,0:T(8,128)(2,1)S(1)}, bf16[128,896]{1,0:T(8,128)(2,1)S(1)}, u32[]{:S(2)}, u32[]{:S(2)}) collective-permute-start(bf16[128,896]{1,0:T(8,128)(2,1)S(1)} %get-tuple-element.85), channel_id=1, source_target_pairs={{0,4},{2,6},{4,0},{6,2},{1,5},{3,7},{5,1},{7,3},{8,12},{10,14},{12... | collective-permute-start | bytes 688136 | tf_op jit(solution)/shard_map/ppermute | solution.py:28
  131.2 10.5 %collective-permute-start.24 = (bf16[128,768]{1,0:T(8,128)(2,1)S(1)}, bf16[128,768]{1,0:T(8,128)(2,1)S(1)}, u32[]{:S(2)}, u32[]{:S(2)}) collective-permute-start(bf16[128,768]{1,0:T(8,128)(2,1)S(1)} %sum_stage.22.refs_6_), channel_id=1, source_target_pairs={{0,8},{8,16},{16,24},{24,0},{1,9},{9,17},{17,25},{25,1},{2,10},{10... | collective-permute-start | bytes 589832 | tf_op jit(solution)/shard_map/ppermute | solution.py:23
  133.5 7.2 %collective-permute-start.31 = (bf16[128,384]{1,0:T(8,128)(2,1)S(1)}, bf16[128,384]{1,0:T(8,128)(2,1)S(1)}, u32[]{:S(2)}, u32[]{:S(2)}) collective-permute-start(bf16[128,384]{1,0:T(8,128)(2,1)S(1)} %get-tuple-element.96), channel_id=1, source_target_pairs={{0,1},{1,0},{2,3},{3,2},{4,5},{5,4},{6,7},{7,6},{8,9},{9,8},{10,11... | collective-permute-start | bytes 294920 | tf_op jit(solution)/shard_map/ppermute | solution.py:28
  136.4 5.3 %collective-permute-start.32 = (bf16[128,384]{1,0:T(8,128)(2,1)S(1)}, bf16[128,384]{1,0:T(8,128)(2,1)S(1)}, u32[]{:S(2)}, u32[]{:S(2)}) collective-permute-start(bf16[128,384]{1,0:T(8,128)(2,1)S(1)} %get-tuple-element.97), channel_id=1, source_target_pairs={{0,4},{2,6},{4,0},{6,2},{1,5},{3,7},{5,1},{7,3},{8,12},{10,14},{12... | collective-permute-start | bytes 294920 | tf_op jit(solution)/shard_map/ppermute | solution.py:28
  137.5 9.3 %collective-permute-start.28 = (bf16[128,768]{1,0:T(8,128)(2,1)S(1)}, bf16[128,768]{1,0:T(8,128)(2,1)S(1)}, u32[]{:S(2)}, u32[]{:S(2)}) collective-permute-start(bf16[128,768]{1,0:T(8,128)(2,1)S(1)} %sum_stage.24.refs_6_), channel_id=1, source_target_pairs={{0,8},{8,16},{16,24},{24,0},{1,9},{9,17},{17,25},{25,1},{2,10},{10... | collective-permute-start | bytes 589832 | tf_op jit(solution)/shard_map/ppermute | solution.py:23
  139.2 4.3 %collective-permute-start.29 = (bf16[128,256]{1,0:T(8,128)(2,1)S(1)}, bf16[128,256]{1,0:T(8,128)(2,1)S(1)}, u32[]{:S(2)}, u32[]{:S(2)}) collective-permute-start(bf16[128,256]{1,0:T(8,128)(2,1)S(1)} %get-tuple-element.92), channel_id=1, source_target_pairs={{0,1},{1,0},{2,3},{3,2},{4,5},{5,4},{6,7},{7,6},{8,9},{9,8},{10,11... | collective-permute-start | bytes 196616 | tf_op jit(solution)/shard_map/ppermute | solution.py:28
  140.7 4.3 %collective-permute-start.30 = (bf16[128,256]{1,0:T(8,128)(2,1)S(1)}, bf16[128,256]{1,0:T(8,128)(2,1)S(1)}, u32[]{:S(2)}, u32[]{:S(2)}) collective-permute-start(bf16[128,256]{1,0:T(8,128)(2,1)S(1)} %get-tuple-element.93), channel_id=1, source_target_pairs={{0,4},{2,6},{4,0},{6,2},{1,5},{3,7},{5,1},{7,3},{8,12},{10,14},{12... | collective-permute-start | bytes 196616 | tf_op jit(solution)/shard_map/ppermute | solution.py:28
  141.8 10.3 %collective-permute-start.34 = (bf16[128,768]{1,0:T(8,128)(2,1)S(1)}, bf16[128,768]{1,0:T(8,128)(2,1)S(1)}, u32[]{:S(2)}, u32[]{:S(2)}) collective-permute-start(bf16[128,768]{1,0:T(8,128)(2,1)S(1)} %sum_stage.26.refs_5_), channel_id=1, source_target_pairs={{0,8},{8,16},{16,24},{24,0},{1,9},{9,17},{17,25},{25,1},{2,10},{10... | collective-permute-start | bytes 589832 | tf_op jit(solution)/shard_map/ppermute | solution.py:23
  145.0 7.0 %collective-permute-start.33 = (bf16[128,512]{1,0:T(8,128)(2,1)S(1)}, bf16[128,512]{1,0:T(8,128)(2,1)S(1)}, u32[]{:S(2)}, u32[]{:S(2)}) collective-permute-start(bf16[128,512]{1,0:T(8,128)(2,1)S(1)} %sum_stage.27), channel_id=1, source_target_pairs={{0,8},{8,16},{16,24},{24,0},{1,9},{9,17},{17,25},{25,1},{2,10},{10... | collective-permute-start | bytes 393224 | tf_op jit(solution)/shard_map/ppermute | solution.py:23
  152.1 1.1 copy-start.10

commit v20 on v19

--- a/solution.py
+++ b/solution.py
@@ -180,7 +180,7 @@
     )(*blocks, weights)
 
 
-def attend_units(visible_ref, queries_ref, pool_ref, out_ref, first_block, before_head):
+def attend_units(visible_ref, queries_ref, pool_ref, out_ref, first_block, before):
     heads, fresh_rows, _ = queries_ref.shape
     tiles_seen = visible_ref.shape[1]
     tiles_fresh = visible_ref.shape[0]
@@ -214,6 +214,8 @@
         )
 
     def finish(head, block, scores):
+        if block == 0:
+            before(head, "values")
         values = [pool_ref[heads + head, place, :] for place in places[block]]
         values = jnp.concatenate(values, axis=0)
         exponent = jnp.exp2(scores * (HD ** (-0.5) * LOG2E)).astype(jnp.bfloat16)
@@ -227,7 +229,7 @@
 
     waiting = []
     for head in range(heads):
-        before_head(head)
+        before(head, "scores")
         for block in range(blocks):
             waiting.append((head, block, scores_of(head, block)))
             if len(waiting) > 2:
@@ -257,12 +259,12 @@
             copy.start()
         copies.append(of_head)
 
-    def before_head(head):
-        for copy in copies[head]:
+    def before(head, step):
+        for copy in copies[head][:3] if step == "scores" else copies[head][3:]:
             copy.wait()
 
     first_block = out_ref.shape[0] // TILE
-    attend_units(visible_ref, queries_ref, pool_ref, out_ref, first_block, before_head)
+    attend_units(visible_ref, queries_ref, pool_ref, out_ref, first_block, before)
 
 
 def attend_first(heads, context, visible):
@@ -299,7 +301,7 @@
     ]
     for copy in copies:
         copy.start()
-    attend_units(visible_ref, queries_ref, pool_ref, out_ref, 0, lambda head: None)
+    attend_units(visible_ref, queries_ref, pool_ref, out_ref, 0, lambda head, step: None)
     for copy in copies:
         copy.wait()
 

time: 154 us -> 154 us (level)
  no operation moved by 1% of the time
where the time goes in v20:
time: 154 us
  Pallas kernels  50.8 us (33%)
  starting transfers between devices  41.6 us (27%)
  waiting for transfers between devices  36.2 us (24%)
  local copies, waits for them, and re-layouts  24.6 us (16%)
    ppermute x29, starting transfers between devices, from_partner(): return lax.ppermute(value, axis, pairs)  26.7 us
    ppermute x29, waiting for transfers between devices, from_partner(): return lax.ppermute(value, axis, pairs)  26.5 us
    pallas_call x1, Pallas kernels, project(): pl.pallas_call(functools.partial(project_kernel, blocks=len(blocks)), gri...  19.2 us
    pallas_call x14, Pallas kernels, stage(): pl.pallas_call(functools.partial(stage_kernel, parts=parts, start=start,...  12.8 us
    ppermute x6, starting transfers between devices, from_behind(): return lax.ppermute(x, axis, [(i, (i + by) % count) for i in range(count)])  10.3 us
    pallas_call x4, Pallas kernels, modulated_norm(): pl.pallas_call(norm_kernel, in_specs=[pl.BlockSpec(memory_space=pltpu.VME...  8.49 us
    reshape x1, local copies, waits for them, and re-layouts, per_device(): unpacked.transpose(2, 0, 1, 3).reshape(devices, context_rows, 2 * width)  8.06 us
    another operation x1, local copies, waits for them, and re-layouts, per_device(): unpacked = stale_cache[0, 0].reshape(context_rows, 2, devices, width)  8 us
  transfers between devices with their start and end apart: 36, of which 19 were waited for; matrix products, arithmetic and copies ran while one was open for 13% of the time, Pallas kernels for 31%

profile of v20, /device:TPU:0, one launch (start us, length us, event | category | flops | bytes accessed | tf_op | source)
XLA Modules:
  0.0 153.6 jit_solution(8740728889188255113)
XLA Ops:
  0.0 2.2 %halves_of.1 = (bf16[64,5120]{1,0:T(8,128)(2,1)}, bf16[64,5120]{1,0:T(8,128)(2,1)}) custom-call(bf16[128,5120]{1,0:T(8,128)(2,1)} %bitcast.15), custom_call_target="tpu_custom_call" | custom-call | flops 1 | bytes 1 | tf_op jit(solution)/shard_map/halves_of/pallas_call | solution.py:87
  2.2 3.0 %collective-permute-start.1 = (bf16[64,5120]{1,0:T(8,128)(2,1)}, bf16[64,5120]{1,0:T(8,128)(2,1)S(1)}, u32[]{:S(2)}, u32[]{:S(2)}) collective-permute-start(bf16[64,5120]{1,0:T(8,128)(2,1)} %get-tuple-element.52), channel_id=1, source_target_pairs={{0,1},{1,0},{2,3},{3,2},{4,5},{5,4},{6,7},{7,6},{8,9},{9,8},{10,11... | collective-permute-start | bytes 1966088 | tf_op jit(solution)/shard_map/ppermute | solution.py:28
  5.2 1.5 collective-permute-start.4
  6.8 0.5 collective-permute-start.3
  7.3 8.0 %reshape_squeeze.3.refs_0_ = bf16[256,2,8,384]{3,2,1,0:T(8,128)(2,1)} reshape(bf16[1,1,256,2,3072]{4,3,2,1,0:T(2,128)(2,1)} %param.10) | data formatting | bytes 6291456 | tf_op jit(solution)/shard_map/reshape;squeeze | solution.py:471
  15.3 5.7 %collective-permute-done.1.value_ref = bf16[64,5120]{1,0:T(8,128)(2,1)S(1)} collective-permute-done((bf16[64,5120]{1,0:T(8,128)(2,1)}, bf16[64,5120]{1,0:T(8,128)(2,1)S(1)}, u32[]{:S(2)}, u32[]{:S(2)}) %collective-permute-start.1) | collective-permute-done | bytes 655392 | tf_op jit(solution)/shard_map/ppermute | solution.py:28
  21.0 1.9 %copy-done.2 = bf16[256,2,8,384]{3,2,1,0:T(8,128)(2,1)S(1)} copy-done((bf16[256,2,8,384]{3,2,1,0:T(8,128)(2,1)S(1)}, bf16[256,2,8,384]{3,2,1,0:T(8,128)(2,1)}, u32[]{:S(2)}) %copy-start.2) | copy-done | bytes 3145752
  22.9 2.1 %collective-permute-start.5 = (bf16[64,5120]{1,0:T(8,128)(2,1)S(1)}, bf16[64,5120]{1,0:T(8,128)(2,1)}, u32[]{:S(2)}, u32[]{:S(2)}) collective-permute-start(bf16[64,5120]{1,0:T(8,128)(2,1)S(1)} %after.3.refs_0_), channel_id=1, source_target_pairs={{0,4},{2,6},{4,0},{6,2},{1,5},{3,7},{5,1},{7,3},{8,12},{10,14},{12... | collective-permute-start | bytes 1966088 | tf_op jit(solution)/shard_map/ppermute | solution.py:28
  25.0 1.8 %collective-permute-start.6 = (bf16[64,5120]{1,0:T(8,128)(2,1)S(1)}, bf16[64,5120]{1,0:T(8,128)(2,1)}, u32[]{:S(2)}, u32[]{:S(2)}) collective-permute-start(bf16[64,5120]{1,0:T(8,128)(2,1)S(1)} %after.4.refs_1_), channel_id=1, source_target_pairs={{0,1},{1,0},{2,3},{3,2},{4,5},{5,4},{6,7},{7,6},{8,9},{9,8},{10,11... | collective-permute-start | bytes 1966088 | tf_op jit(solution)/shard_map/ppermute | solution.py:28
  27.1 1.5 modulated_norm.4.refs_0_
  28.7 1.0 copy-done.6
  29.7 4.1 %copy.11 = bf16[8,256,2,384]{3,2,1,0:T(2,128)(2,1)} copy(bf16[8,256,2,384]{3,0,2,1:T(8,128)(2,1)S(1)} %bitcast.38) | data formatting | bytes 6291456 | tf_op jit(solution)/shard_map/transpose | solution.py:472
  33.8 8.1 %reshape.8.value_ref = bf16[8,256,768]{2,1,0:T(8,128)(2,1)} reshape(bf16[8,256,2,384]{3,2,1,0:T(2,128)(2,1)} %copy.11) | data formatting | bytes 6291456 | tf_op jit(solution)/shard_map/reshape | solution.py:472
  41.8 0.5 collective-permute-start.11
  42.7 4.6 %all-to-all-start = ((bf16[8,256,768]{2,1,0:T(8,128)(2,1)}), bf16[8,256,768]{2,1,0:T(8,128)(2,1)}, u32[]{:S(2)}, u32[]{:S(2)}) async-start(bf16[8,256,768]{2,1,0:T(8,128)(2,1)} %after.5), calls=%async_computation | async-start | bytes 6291456 | tf_op jit(solution)/shard_map/all_to_all | solution.py:490
  47.3 3.1 %collective-permute-done = f32[1,1,3,5120]{3,2,1,0:T(4,128)S(1)} collective-permute-done((f32[1,1,3,5120]{3,2,1,0:T(4,128)S(1)}, f32[1,1,3,5120]{3,2,1,0:T(4,128)S(1)}, u32[]{:S(2)}, u32[]{:S(2)}) %collective-permute-start) | collective-permute-done | bytes 61472 | tf_op jit(solution)/shard_map/ppermute | solution.py:28
  50.4 2.7 %modulated_norm.5.refs_1_ = bf16[128,5120]{1,0:T(8,128)(2,1)S(1)} custom-call(bf16[64,5120]{1,0:T(8,128)(2,1)S(1)} %after.3.refs_0_, bf16[64,5120]{1,0:T(8,128)(2,1)} %collective-permute-done.2.refs_1_.refs_0_, f32[3,5120]{1,0:T(4,128)S(1)} %bitcast.41), custom_call_target="tpu_custom_call" | custom-call | flops 1 | bytes 1 | tf_op jit(solution)/shard_map/modulated_norm/pallas_call | solution.py:55
  53.2 1.5 modulated_norm.6.refs_2_
  54.7 0.6 collective-permute-start.9
  55.3 2.8 %modulated_norm.7.refs_3_ = bf16[128,5120]{1,0:T(8,128)(2,1)S(1)} custom-call(bf16[64,5120]{1,0:T(8,128)(2,1)} %collective-permute-done.5.refs_0_, bf16[64,5120]{1,0:T(8,128)(2,1)} %collective-permute-done.6.refs_1_, f32[3,5120]{1,0:T(4,128)S(1)} %bitcast.42), custom_call_target="tpu_custom_call" | custom-call | flops 1 | bytes 1 | tf_op jit(solution)/shard_map/modulated_norm/pallas_call | solution.py:55
  58.3 2.9 %collective-permute-done.10.refs_7_ = bf16[128,5120]{1,0:T(8,128)(2,1)S(1)} collective-permute-done((bf16[128,5120]{1,0:T(8,128)(2,1)S(1)}, bf16[128,5120]{1,0:T(8,128)(2,1)S(1)}, u32[]{:S(2)}, u32[]{:S(2)}) %collective-permute-start.10) | collective-permute-done | bytes 1310752 | tf_op jit(solution)/shard_map/ppermute | solution.py:28
  61.2 19.2 %project_heads.1.heads_in = bf16[48,1024,128]{2,1,0:T(8,128)(2,1)} custom-call(bf16[128,5120]{1,0:T(8,128)(2,1)S(1)} %copy-done.7, bf16[128,5120]{1,0:T(8,128)(2,1)S(1)} %modulated_norm.5.refs_1_, bf16[128,5120]{1,0:T(8,128)(2,1)S(1)} %modulated_norm.6.refs_2_, bf16[128,5120]{1,0:T(8,128)(2,1)S(1)} %modulated_norm.7.refs_3_, ...), custom_call_target="tpu_custom_call" | custom-call | flops 12079595520 | bytes 22282240 | tf_op jit(solution)/shard_map/project_heads/pallas_call | solution.py:161
  80.4 4.2 %all-to-all-done = bf16[8,256,768]{2,1,0:T(8,128)(2,1)} async-done(((bf16[8,256,768]{2,1,0:T(8,128)(2,1)}), bf16[8,256,768]{2,1,0:T(8,128)(2,1)}, u32[]{:S(2)}, u32[]{:S(2)}) %all-to-all-start) | async-done | bytes 3145760 | tf_op jit(solution)/shard_map/all_to_all | solution.py:490
  84.6 4.8 %attend_first.1 = (bf16[512,384]{1,0:T(8,128)(2,1)S(1)}, bf16[3,1024,128]{2,1,0:T(8,128)(2,1)S(1)}, bf16[6,3072,128]{2,1,0:T(8,128)(2,1)S(1)}) custom-call(s32[4,6]{1,0:T(4,128)S(1)} %bitcast.43, bf16[48,1024,128]{2,1,0:T(8,128)(2,1)} %project_heads.1.heads_in, bf16[2048,768]{1,0:T(8,128)(2,1)} %bitcast.7.context_in), custom_call_target="tpu_custom_call" | custom-call | flops 1 | bytes 1 | tf_op jit(solution)/shard_map/attend_first/pallas_call | solution.py:272
  89.5 3.4 %attend_second.1 = (bf16[512,384]{1,0:T(8,128)(2,1)S(1)}, bf16[768,1024]{1,0:T(8,128)(2,1)S(1)}) custom-call(s32[4,6]{1,0:T(4,128)S(1)} %bitcast.44, bf16[3,1024,128]{2,1,0:T(8,128)(2,1)S(1)} %get-tuple-element.54.queries_ref, bf16[6,3072,128]{2,1,0:T(8,128)(2,1)S(1)} %get-tuple-element.55.pool_ref, bf16[384,5120]{1,0:T(8,128)(2,1)S(1)} %bitcast.32, ...), custom_call_target="tpu_custom_call" | custom-call | flops 1 | bytes 1 | tf_op jit(solution)/shard_map/attend_second/pallas_call | solution.py:311
  92.9 1.0 sum_stage.14
  94.0 1.1 collective-permute-start.13
  95.1 1.5 collective-permute-start.14
  96.6 2.7 %sum_stage.15 = (bf16[128,1280]{1,0:T(8,128)(2,1)S(1)}, bf16[128,1280]{1,0:T(8,128)(2,1)S(1)}, f32[2,128,640]{2,1,0:T(8,128)S(1)}, f32[2,128,640]{2,1,0:T(8,128)S(1)}) custom-call(bf16[128,5120]{1,0:T(8,128)(2,1)S(1)} %bitcast.18, f32[2,5120]{1,0:T(2,128)S(1)} %pad_maximum_fusion.refs_3_.refs_1_, bf16[512,384]{1,0:T(8,128)(2,1)S(1)} %get-tuple-element.57.refs_2_, ...), custom_call_target="tpu_custom_call" | custom-call | flops 1 | bytes 1 | tf_op jit(solution)/shard_map/sum_stage/pallas_call | solution.py:436
  99.7 1.2 collective-permute-start.18
  100.9 2.3 %collective-permute-done.13.refs_6_ = bf16[128,1024]{1,0:T(8,128)(2,1)S(1)} collective-permute-done((bf16[128,1024]{1,0:T(8,128)(2,1)S(1)}, bf16[128,1024]{1,0:T(8,128)(2,1)S(1)}, u32[]{:S(2)}, u32[]{:S(2)}) %collective-permute-start.13) | collective-permute-done | bytes 262176 | tf_op jit(solution)/shard_map/ppermute | solution.py:28
  103.2 1.0 collective-permute-done.14.refs_7_
  104.2 2.3 %sum_stage.16 = (bf16[128,1280]{1,0:T(8,128)(2,1)S(1)}, bf16[128,1280]{1,0:T(8,128)(2,1)S(1)}, f32[2,128,384]{2,1,0:T(8,128)S(1)}, f32[2,128,384]{2,1,0:T(8,128)...) custom-call(bf16[128,5120]{1,0:T(8,128)(2,1)S(1)} %bitcast.19, f32[2,5120]{1,0:T(2,128)S(1)} %pad_maximum_fusion.refs_3_.refs_1_, ...), custom_call_target="tpu_custom_call" | custom-call | flops 1 | bytes 1 | tf_op jit(solution)/shard_map/sum_stage/pallas_call | solution.py:436
  106.5 1.1 collective-permute-start.15
  107.6 0.8 collective-permute-start.16
  108.4 1.8 %collective-permute-done.17.refs_6_ = bf16[128,1280]{1,0:T(8,128)(2,1)S(1)} collective-permute-done((bf16[128,1280]{1,0:T(8,128)(2,1)S(1)}, bf16[128,1280]{1,0:T(8,128)(2,1)S(1)}, u32[]{:S(2)}, u32[]{:S(2)}) %collective-permute-start.17) | collective-permute-done | bytes 327712 | tf_op jit(solution)/shard_map/ppermute | solution.py:28
  110.2 1.0 collective-permute-done.18.refs_7_
  111.2 2.4 %sum_stage.17 = (bf16[128,1408]{1,0:T(8,128)(2,1)S(1)}, bf16[128,1408]{1,0:T(8,128)(2,1)S(1)}, f32[2,128,384]{2,1,0:T(8,128)S(1)}, f32[2,128,384]{2,1,0:T(8,128)...) custom-call(bf16[128,5120]{1,0:T(8,128)(2,1)S(1)} %bitcast.20, f32[2,5120]{1,0:T(2,128)S(1)} %pad_maximum_fusion.refs_3_.refs_1_, ...), custom_call_target="tpu_custom_call" | custom-call | flops 1 | bytes 1 | tf_op jit(solution)/shard_map/sum_stage/pallas_call | solution.py:436
  113.6 1.1 collective-permute-start.21
  114.7 0.8 collective-permute-start.22
  115.5 1.7 %collective-permute-done.15.refs_1_.refs_6_ = bf16[128,1280]{1,0:T(8,128)(2,1)S(1)} collective-permute-done((bf16[128,1280]{1,0:T(8,128)(2,1)S(1)}, bf16[128,1280]{1,0:T(8,128)(2,1)S(1)}, u32[]{:S(2)}, u32[]{:S(2)}) %collective-permute-start.15) | collective-permute-done | bytes 327712 | tf_op jit(solution)/shard_map/ppermute | solution.py:28
  117.2 1.0 collective-permute-done.16.refs_2_.refs_7_
  118.3 1.9 %collective-permute-start.23 = (bf16[128,1024]{1,0:T(8,128)(2,1)S(1)}, bf16[128,1024]{1,0:T(8,128)(2,1)S(1)}, u32[]{:S(2)}, u32[]{:S(2)}) collective-permute-start(bf16[128,1024]{1,0:T(8,128)(2,1)S(1)} %sum_stage.18.refs_10_), channel_id=1, source_target_pairs={{0,8},{8,16},{16,24},{24,0},{1,9},{9,17},{17,25},{25,1},{2,10},{10... | collective-permute-start | bytes 786440 | tf_op jit(solution)/shard_map/ppermute | solution.py:23
  120.2 2.2 %sum_stage.19 = (bf16[128,1152]{1,0:T(8,128)(2,1)S(1)}, bf16[128,1152]{1,0:T(8,128)(2,1)S(1)}, f32[2,128,384]{2,1,0:T(8,128)S(1)}, f32[2,128,384]{2,1,0:T(8,128)...) custom-call(bf16[128,5120]{1,0:T(8,128)(2,1)S(1)} %bitcast.22, f32[2,5120]{1,0:T(2,128)S(1)} %pad_maximum_fusion.refs_3_.refs_1_, ...), custom_call_target="tpu_custom_call" | custom-call | flops 1 | bytes 1 | tf_op jit(solution)/shard_map/sum_stage/pallas_call | solution.py:436
  122.4 1.1 collective-permute-start.19
  123.5 1.0 collective-permute-start.20
  124.5 0.5 collective-permute-done.21.refs_1_.refs_6_
  125.0 1.0 collective-permute-done.22.refs_2_.refs_7_
  126.1 1.9 %collective-permute-start.27 = (bf16[128,1280]{1,0:T(8,128)(2,1)S(1)}, bf16[128,1280]{1,0:T(8,128)(2,1)S(1)}, u32[]{:S(2)}, u32[]{:S(2)}) collective-permute-start(bf16[128,1280]{1,0:T(8,128)(2,1)S(1)} %sum_stage.20.refs_10_), channel_id=1, source_target_pairs={{0,8},{8,16},{16,24},{24,0},{1,9},{9,17},{17,25},{25,1},{2,10},{10... | collective-permute-start | bytes 983048 | tf_op jit(solution)/shard_map/ppermute | solution.py:23
  128.0 1.7 %sum_stage.21 = (bf16[128,896]{1,0:T(8,128)(2,1)S(1)}, bf16[128,896]{1,0:T(8,128)(2,1)S(1)}, f32[2,128,256]{2,1,0:T(8,128)S(1)}, f32[2,128,256]{2,1,0:T(8,128)S(...) custom-call(bf16[128,5120]{1,0:T(8,128)(2,1)S(1)} %bitcast.24, f32[2,5120]{1,0:T(2,128)S(1)} %pad_maximum_fusion.refs_3_.refs_1_, ...), custom_call_target="tpu_custom_call" | custom-call | flops 1 | bytes 1 | tf_op jit(solution)/shard_map/sum_stage/pallas_call | solution.py:436
  129.7 1.0 collective-permute-start.25
  131.7 2.1 %collective-permute-start.24 = (bf16[128,768]{1,0:T(8,128)(2,1)S(1)}, bf16[128,768]{1,0:T(8,128)(2,1)S(1)}, u32[]{:S(2)}, u32[]{:S(2)}) collective-permute-start(bf16[128,768]{1,0:T(8,128)(2,1)S(1)} %sum_stage.22.refs_6_), channel_id=1, source_target_pairs={{0,8},{8,16},{16,24},{24,0},{1,9},{9,17},{17,25},{25,1},{2,10},{10... | collective-permute-start | bytes 589832 | tf_op jit(solution)/shard_map/ppermute | solution.py:23
  134.0 1.1 collective-permute-start.31
  135.1 1.8 %collective-permute-done.25.refs_1_.refs_2_ = bf16[128,896]{1,0:T(8,128)(2,1)S(1)} collective-permute-done((bf16[128,896]{1,0:T(8,128)(2,1)S(1)}, bf16[128,896]{1,0:T(8,128)(2,1)S(1)}, u32[]{:S(2)}, u32[]{:S(2)}) %collective-permute-start.25) | collective-permute-done | bytes 229408 | tf_op jit(solution)/shard_map/ppermute | solution.py:28
  136.8 1.0 collective-permute-start.32
  137.9 1.6 %collective-permute-start.28 = (bf16[128,768]{1,0:T(8,128)(2,1)S(1)}, bf16[128,768]{1,0:T(8,128)(2,1)S(1)}, u32[]{:S(2)}, u32[]{:S(2)}) collective-permute-start(bf16[128,768]{1,0:T(8,128)(2,1)S(1)} %sum_stage.24.refs_6_), channel_id=1, source_target_pairs={{0,8},{8,16},{16,24},{24,0},{1,9},{9,17},{17,25},{25,1},{2,10},{10... | collective-permute-start | bytes 589832 | tf_op jit(solution)/shard_map/ppermute | solution.py:23
  139.7 1.5 collective-permute-start.29
  141.2 0.8 collective-permute-start.30
  142.2 1.2 collective-permute-start.34
  143.4 0.6 collective-permute-done.29.refs_1_
  144.0 1.4 collective-permute-done.30.refs_2_
  145.5 1.5 collective-permute-start.33
  147.1 5.4 %collective-permute-done.33 = bf16[128,512]{1,0:T(8,128)(2,1)S(1)} collective-permute-done((bf16[128,512]{1,0:T(8,128)(2,1)S(1)}, bf16[128,512]{1,0:T(8,128)(2,1)S(1)}, u32[]{:S(2)}, u32[]{:S(2)}) %collective-permute-start.33) | collective-permute-done | bytes 131104 | tf_op jit(solution)/shard_map/ppermute | solution.py:23
  152.6 1.0 copy-done.10
  (68 shorter events, 3.3 us)
Async XLA Ops:
  2.2 18.8 %collective-permute-start.1 = (bf16[64,5120]{1,0:T(8,128)(2,1)}, bf16[64,5120]{1,0:T(8,128)(2,1)S(1)}, u32[]{:S(2)}, u32[]{:S(2)}) collective-permute-start(bf16[64,5120]{1,0:T(8,128)(2,1)} %get-tuple-element.52), channel_id=1, source_target_pairs={{0,1},{1,0},{2,3},{3,2},{4,5},{5,4},{6,7},{7,6},{8,9},{9,8},{10,11... | collective-permute-start | bytes 1966088 | tf_op jit(solution)/shard_map/ppermute | solution.py:28
  5.2 19.8 %collective-permute-start.4 = (bf16[64,5120]{1,0:T(8,128)(2,1)}, bf16[64,5120]{1,0:T(8,128)(2,1)S(1)}, u32[]{:S(2)}, u32[]{:S(2)}) collective-permute-start(bf16[64,5120]{1,0:T(8,128)(2,1)} %get-tuple-element.53), channel_id=1, source_target_pairs={{0,4},{2,6},{4,0},{6,2},{1,5},{3,7},{5,1},{7,3},{8,12},{10,14},{12... | collective-permute-start | bytes 1966088 | tf_op jit(solution)/shard_map/ppermute | solution.py:28
  6.8 35.1 %collective-permute-start.3 = (bf16[64,5120]{1,0:T(8,128)(2,1)}, bf16[64,5120]{1,0:T(8,128)(2,1)S(1)}, u32[]{:S(2)}, u32[]{:S(2)}) collective-permute-start(bf16[64,5120]{1,0:T(8,128)(2,1)} %get-tuple-element.52), channel_id=1, source_target_pairs={{0,4},{2,6},{4,0},{6,2},{1,5},{3,7},{5,1},{7,3},{8,12},{10,14},{12... | collective-permute-start | bytes 1966088 | tf_op jit(solution)/shard_map/ppermute | solution.py:28
  7.3 34.6 %collective-permute-start.2 = (bf16[64,5120]{1,0:T(8,128)(2,1)}, bf16[64,5120]{1,0:T(8,128)(2,1)}, u32[]{:S(2)}, u32[]{:S(2)}) collective-permute-start(bf16[64,5120]{1,0:T(8,128)(2,1)} %get-tuple-element.53), channel_id=1, source_target_pairs={{0,1},{1,0},{2,3},{3,2},{4,5},{5,4},{6,7},{7,6},{8,9},{9,8},{10,11... | collective-permute-start | bytes 1966088 | tf_op jit(solution)/shard_map/ppermute | solution.py:28
  21.0 1.9 %copy-start.2 = (bf16[256,2,8,384]{3,2,1,0:T(8,128)(2,1)S(1)}, bf16[256,2,8,384]{3,2,1,0:T(8,128)(2,1)}, u32[]{:S(2)}) copy-start(bf16[256,2,8,384]{3,2,1,0:T(8,128)(2,1)} %reshape_squeeze.3.refs_0_) | copy-start | bytes 9437188
  22.9 2.1 %copy-start.3 = (bf16[256,2,8,384]{3,2,1,0:T(8,128)(2,1)S(1)}, bf16[256,2,8,384]{3,2,1,0:T(8,128)(2,1)}, u32[]{:S(2)}) copy-start(bf16[256,2,8,384]{3,2,1,0:T(8,128)(2,1)} %reshape_squeeze.3.refs_0_) | copy-start | bytes 9437188
  22.9 3.9 %copy-start.9 = (f32[1,1,3,5120]{3,1,2,0:T(1,128)S(1)}, f32[1,1,3,5120]{3,1,2,0:T(1,128)}, u32[]{:S(2)}) copy-start(f32[1,1,3,5120]{3,1,2,0:T(1,128)} %param.7) | copy-start | bytes 184324
  22.9 4.2 %copy-start = (bf16[1,1,128,5120]{3,2,1,0:T(8,128)(2,1)S(1)}, bf16[1,1,128,5120]{3,2,1,0:T(8,128)(2,1)}, u32[]{:S(2)}) copy-start(bf16[1,1,128,5120]{3,2,1,0:T(8,128)(2,1)} %param.6) | copy-start | bytes 3932164
  22.9 31.8 %collective-permute-start.5 = (bf16[64,5120]{1,0:T(8,128)(2,1)S(1)}, bf16[64,5120]{1,0:T(8,128)(2,1)}, u32[]{:S(2)}, u32[]{:S(2)}) collective-permute-start(bf16[64,5120]{1,0:T(8,128)(2,1)S(1)} %after.3.refs_0_), channel_id=1, source_target_pairs={{0,4},{2,6},{4,0},{6,2},{1,5},{3,7},{5,1},{7,3},{8,12},{10,14},{12... | collective-permute-start | bytes 1966088 | tf_op jit(solution)/shard_map/ppermute | solution.py:28
  25.0 30.3 %collective-permute-start.6 = (bf16[64,5120]{1,0:T(8,128)(2,1)S(1)}, bf16[64,5120]{1,0:T(8,128)(2,1)}, u32[]{:S(2)}, u32[]{:S(2)}) collective-permute-start(bf16[64,5120]{1,0:T(8,128)(2,1)S(1)} %after.4.refs_1_), channel_id=1, source_target_pairs={{0,1},{1,0},{2,3},{3,2},{4,5},{5,4},{6,7},{7,6},{8,9},{9,8},{10,11... | collective-permute-start | bytes 1966088 | tf_op jit(solution)/shard_map/ppermute | solution.py:28
  26.9 23.6 %collective-permute-start = (f32[1,1,3,5120]{3,2,1,0:T(4,128)S(1)}, f32[1,1,3,5120]{3,2,1,0:T(4,128)S(1)}, u32[]{:S(2)}, u32[]{:S(2)}) collective-permute-start(f32[1,1,3,5120]{3,2,1,0:T(4,128)S(1)} %copy.15), channel_id=1, source_target_pairs={{0,1},{1,0},{2,3},{3,2},{4,5},{5,4},{6,7},{7,6},{8,9},{9,8},{10,11... | collective-permute-start | bytes 184328 | tf_op jit(solution)/shard_map/ppermute | solution.py:28
  28.6 1.1 copy-start.6
  41.8 0.9 copy-start.4
  41.8 16.5 %collective-permute-start.7 = (bf16[128,5120]{1,0:T(8,128)(2,1)}, bf16[128,5120]{1,0:T(8,128)(2,1)}, u32[]{:S(2)}, u32[]{:S(2)}) collective-permute-start(bf16[128,5120]{1,0:T(8,128)(2,1)} %copy-done.6), channel_id=1, source_target_pairs={{0,2},{2,0},{4,6},{6,4},{1,3},{3,1},{5,7},{7,5},{8,10},{10,8},{12,... | collective-permute-start | bytes 3932168 | tf_op jit(solution)/shard_map/ppermute | solution.py:28
  41.8 47.7 %collective-permute-start.11 = (bf16[384,5120]{1,0:T(8,128)(2,1)}, bf16[384,5120]{1,0:T(8,128)(2,1)}, u32[]{:S(2)}, u32[]{:S(2)}) collective-permute-start(bf16[384,5120]{1,0:T(8,128)(2,1)} %bitcast.31), channel_id=1, source_target_pairs={{0,2},{2,0},{4,6},{6,4},{1,3},{3,1},{5,7},{7,5},{8,10},{10,8},{12,... | collective-permute-start | bytes 11796488 | tf_op jit(solution)/shard_map/ppermute | solution.py:28
  42.7 41.9 %all-to-all-start = ((bf16[8,256,768]{2,1,0:T(8,128)(2,1)}), bf16[8,256,768]{2,1,0:T(8,128)(2,1)}, u32[]{:S(2)}, u32[]{:S(2)}) async-start(bf16[8,256,768]{2,1,0:T(8,128)(2,1)} %after.5), calls=%async_computation | async-start | bytes 6291456 | tf_op jit(solution)/shard_map/all_to_all | solution.py:490
  50.4 2.8 %copy-start.5 = (bf16[64,5120]{1,0:T(8,128)(2,1)S(1)}, bf16[64,5120]{1,0:T(8,128)(2,1)}, u32[]{:S(2)}) copy-start(bf16[64,5120]{1,0:T(8,128)(2,1)} %copy-done.4) | copy-start | bytes 1966084
  53.1 5.2 %collective-permute-start.8 = (bf16[128,5120]{1,0:T(8,128)(2,1)S(1)}, bf16[128,5120]{1,0:T(8,128)(2,1)S(1)}, u32[]{:S(2)}, u32[]{:S(2)}) collective-permute-start(bf16[128,5120]{1,0:T(8,128)(2,1)S(1)} %modulated_norm.5.refs_1_), channel_id=1, source_target_pairs={{0,2},{2,0},{4,6},{6,4},{1,3},{3,1},{5,7},{7,5},{8,10},{10,8},{12,... | collective-permute-start | bytes 3932168 | tf_op jit(solution)/shard_map/ppermute | solution.py:28
  54.7 6.5 %copy-start.7 = (bf16[128,5120]{1,0:T(8,128)(2,1)S(1)}, bf16[128,5120]{1,0:T(8,128)(2,1)}, u32[]{:S(2)}) copy-start(bf16[128,5120]{1,0:T(8,128)(2,1)} %copy-done.6) | copy-start | bytes 3932164
  54.7 3.6 %collective-permute-start.9 = (bf16[128,5120]{1,0:T(8,128)(2,1)S(1)}, bf16[128,5120]{1,0:T(8,128)(2,1)S(1)}, u32[]{:S(2)}, u32[]{:S(2)}) collective-permute-start(bf16[128,5120]{1,0:T(8,128)(2,1)S(1)} %modulated_norm.6.refs_2_), channel_id=1, source_target_pairs={{0,2},{2,0},{4,6},{6,4},{1,3},{3,1},{5,7},{7,5},{8,10},{10,8},{12,... | collective-permute-start | bytes 3932168 | tf_op jit(solution)/shard_map/ppermute | solution.py:28
  58.1 3.1 %collective-permute-start.10 = (bf16[128,5120]{1,0:T(8,128)(2,1)S(1)}, bf16[128,5120]{1,0:T(8,128)(2,1)S(1)}, u32[]{:S(2)}, u32[]{:S(2)}) collective-permute-start(bf16[128,5120]{1,0:T(8,128)(2,1)S(1)} %modulated_norm.7.refs_3_), channel_id=1, source_target_pairs={{0,2},{2,0},{4,6},{6,4},{1,3},{3,1},{5,7},{7,5},{8,10},{10,8},{12,... | collective-permute-start | bytes 3932168 | tf_op jit(solution)/shard_map/ppermute | solution.py:28
  61.2 23.4 %copy-start.8 = (s32[1,4,6]{2,1,0:T(4,128)S(1)}, s32[1,4,6]{2,1,0:T(4,128)}, u32[]{:S(2)}) copy-start(s32[1,4,6]{2,1,0:T(4,128)} %param.11) | copy-start | bytes 292
  84.6 4.9 %copy-start.1 = (bf16[1,384,5120]{2,1,0:T(8,128)(2,1)S(1)}, bf16[1,384,5120]{2,1,0:T(8,128)(2,1)}, u32[]{:S(2)}) copy-start(bf16[1,384,5120]{2,1,0:T(8,128)(2,1)} %param.9) | copy-start | bytes 11796484
  89.4 3.5 %collective-permute-start.12 = (bf16[512,384]{1,0:T(8,128)(2,1)S(1)}, bf16[512,384]{1,0:T(8,128)(2,1)S(1)}, u32[]{:S(2)}, u32[]{:S(2)}) collective-permute-start(bf16[512,384]{1,0:T(8,128)(2,1)S(1)} %get-tuple-element.56.refs_2_), channel_id=1, source_target_pairs={{0,2},{2,0},{4,6},{6,4},{1,3},{3,1},{5,7},{7,5},{8,10},{10,8},{12,... | collective-permute-start | bytes 1179656 | tf_op jit(solution)/shard_map/ppermute | solution.py:28
  94.0 9.2 %collective-permute-start.13 = (bf16[128,1024]{1,0:T(8,128)(2,1)S(1)}, bf16[128,1024]{1,0:T(8,128)(2,1)S(1)}, u32[]{:S(2)}, u32[]{:S(2)}) collective-permute-start(bf16[128,1024]{1,0:T(8,128)(2,1)S(1)} %get-tuple-element.59), channel_id=1, source_target_pairs={{0,1},{1,0},{2,3},{3,2},{4,5},{5,4},{6,7},{7,6},{8,9},{9,8},{10,11... | collective-permute-start | bytes 786440 | tf_op jit(solution)/shard_map/ppermute | solution.py:28
  95.1 9.1 %collective-permute-start.14 = (bf16[128,1024]{1,0:T(8,128)(2,1)S(1)}, bf16[128,1024]{1,0:T(8,128)(2,1)S(1)}, u32[]{:S(2)}, u32[]{:S(2)}) collective-permute-start(bf16[128,1024]{1,0:T(8,128)(2,1)S(1)} %get-tuple-element.60), channel_id=1, source_target_pairs={{0,4},{2,6},{4,0},{6,2},{1,5},{3,7},{5,1},{7,3},{8,12},{10,14},{12... | collective-permute-start | bytes 786440 | tf_op jit(solution)/shard_map/ppermute | solution.py:28
  99.3 10.9 %collective-permute-start.17 = (bf16[128,1280]{1,0:T(8,128)(2,1)S(1)}, bf16[128,1280]{1,0:T(8,128)(2,1)S(1)}, u32[]{:S(2)}, u32[]{:S(2)}) collective-permute-start(bf16[128,1280]{1,0:T(8,128)(2,1)S(1)} %get-tuple-element.70), channel_id=1, source_target_pairs={{0,1},{1,0},{2,3},{3,2},{4,5},{5,4},{6,7},{7,6},{8,9},{9,8},{10,11... | collective-permute-start | bytes 983048 | tf_op jit(solution)/shard_map/ppermute | solution.py:28
  99.7 11.5 %collective-permute-start.18 = (bf16[128,1280]{1,0:T(8,128)(2,1)S(1)}, bf16[128,1280]{1,0:T(8,128)(2,1)S(1)}, u32[]{:S(2)}, u32[]{:S(2)}) collective-permute-start(bf16[128,1280]{1,0:T(8,128)(2,1)S(1)} %get-tuple-element.71), channel_id=1, source_target_pairs={{0,4},{2,6},{4,0},{6,2},{1,5},{3,7},{5,1},{7,3},{8,12},{10,14},{12... | collective-permute-start | bytes 983048 | tf_op jit(solution)/shard_map/ppermute | solution.py:28
  106.5 10.7 %collective-permute-start.15 = (bf16[128,1280]{1,0:T(8,128)(2,1)S(1)}, bf16[128,1280]{1,0:T(8,128)(2,1)S(1)}, u32[]{:S(2)}, u32[]{:S(2)}) collective-permute-start(bf16[128,1280]{1,0:T(8,128)(2,1)S(1)} %get-tuple-element.64), channel_id=1, source_target_pairs={{0,1},{1,0},{2,3},{3,2},{4,5},{5,4},{6,7},{7,6},{8,9},{9,8},{10,11... | collective-permute-start | bytes 983048 | tf_op jit(solution)/shard_map/ppermute | solution.py:28
  107.6 10.7 %collective-permute-start.16 = (bf16[128,1280]{1,0:T(8,128)(2,1)S(1)}, bf16[128,1280]{1,0:T(8,128)(2,1)S(1)}, u32[]{:S(2)}, u32[]{:S(2)}) collective-permute-start(bf16[128,1280]{1,0:T(8,128)(2,1)S(1)} %get-tuple-element.65), channel_id=1, source_target_pairs={{0,4},{2,6},{4,0},{6,2},{1,5},{3,7},{5,1},{7,3},{8,12},{10,14},{12... | collective-permute-start | bytes 983048 | tf_op jit(solution)/shard_map/ppermute | solution.py:28
  113.6 11.4 %collective-permute-start.21 = (bf16[128,1408]{1,0:T(8,128)(2,1)S(1)}, bf16[128,1408]{1,0:T(8,128)(2,1)S(1)}, u32[]{:S(2)}, u32[]{:S(2)}) collective-permute-start(bf16[128,1408]{1,0:T(8,128)(2,1)S(1)} %get-tuple-element.78), channel_id=1, source_target_pairs={{0,1},{1,0},{2,3},{3,2},{4,5},{5,4},{6,7},{7,6},{8,9},{9,8},{10,11... | collective-permute-start | bytes 1081352 | tf_op jit(solution)/shard_map/ppermute | solution.py:28
  114.7 11.3 %collective-permute-start.22 = (bf16[128,1408]{1,0:T(8,128)(2,1)S(1)}, bf16[128,1408]{1,0:T(8,128)(2,1)S(1)}, u32[]{:S(2)}, u32[]{:S(2)}) collective-permute-start(bf16[128,1408]{1,0:T(8,128)(2,1)S(1)} %get-tuple-element.79), channel_id=1, source_target_pairs={{0,4},{2,6},{4,0},{6,2},{1,5},{3,7},{5,1},{7,3},{8,12},{10,14},{12... | collective-permute-start | bytes 1081352 | tf_op jit(solution)/shard_map/ppermute | solution.py:28
  118.3 12.4 %collective-permute-start.23 = (bf16[128,1024]{1,0:T(8,128)(2,1)S(1)}, bf16[128,1024]{1,0:T(8,128)(2,1)S(1)}, u32[]{:S(2)}, u32[]{:S(2)}) collective-permute-start(bf16[128,1024]{1,0:T(8,128)(2,1)S(1)} %sum_stage.18.refs_10_), channel_id=1, source_target_pairs={{0,8},{8,16},{16,24},{24,0},{1,9},{9,17},{17,25},{25,1},{2,10},{10... | collective-permute-start | bytes 786440 | tf_op jit(solution)/shard_map/ppermute | solution.py:23
  122.4 8.8 %collective-permute-start.19 = (bf16[128,1152]{1,0:T(8,128)(2,1)S(1)}, bf16[128,1152]{1,0:T(8,128)(2,1)S(1)}, u32[]{:S(2)}, u32[]{:S(2)}) collective-permute-start(bf16[128,1152]{1,0:T(8,128)(2,1)S(1)} %get-tuple-element.74), channel_id=1, source_target_pairs={{0,1},{1,0},{2,3},{3,2},{4,5},{5,4},{6,7},{7,6},{8,9},{9,8},{10,11... | collective-permute-start | bytes 884744 | tf_op jit(solution)/shard_map/ppermute | solution.py:28
  123.5 8.1 %collective-permute-start.20 = (bf16[128,1152]{1,0:T(8,128)(2,1)S(1)}, bf16[128,1152]{1,0:T(8,128)(2,1)S(1)}, u32[]{:S(2)}, u32[]{:S(2)}) collective-permute-start(bf16[128,1152]{1,0:T(8,128)(2,1)S(1)} %get-tuple-element.75), channel_id=1, source_target_pairs={{0,4},{2,6},{4,0},{6,2},{1,5},{3,7},{5,1},{7,3},{8,12},{10,14},{12... | collective-permute-start | bytes 884744 | tf_op jit(solution)/shard_map/ppermute | solution.py:28
  126.1 11.8 %collective-permute-start.27 = (bf16[128,1280]{1,0:T(8,128)(2,1)S(1)}, bf16[128,1280]{1,0:T(8,128)(2,1)S(1)}, u32[]{:S(2)}, u32[]{:S(2)}) collective-permute-start(bf16[128,1280]{1,0:T(8,128)(2,1)S(1)} %sum_stage.20.refs_10_), channel_id=1, source_target_pairs={{0,8},{8,16},{16,24},{24,0},{1,9},{9,17},{17,25},{25,1},{2,10},{10... | collective-permute-start | bytes 983048 | tf_op jit(solution)/shard_map/ppermute | solution.py:23
  129.7 7.1 %collective-permute-start.25 = (bf16[128,896]{1,0:T(8,128)(2,1)S(1)}, bf16[128,896]{1,0:T(8,128)(2,1)S(1)}, u32[]{:S(2)}, u32[]{:S(2)}) collective-permute-start(bf16[128,896]{1,0:T(8,128)(2,1)S(1)} %get-tuple-element.84), channel_id=1, source_target_pairs={{0,1},{1,0},{2,3},{3,2},{4,5},{5,4},{6,7},{7,6},{8,9},{9,8},{10,11... | collective-permute-start | bytes 688136 | tf_op jit(solution)/shard_map/ppermute | solution.py:28
  130.7 7.2 %collective-permute-start.26 = (bf16[128,896]{1,0:T(8,128)(2,1)S(1)}, bf16[128,896]{1,0:T(8,128)(2,1)S(1)}, u32[]{:S(2)}, u32[]{:S(2)}) collective-permute-start(bf16[128,896]{1,0:T(8,128)(2,1)S(1)} %get-tuple-element.85), channel_id=1, source_target_pairs={{0,4},{2,6},{4,0},{6,2},{1,5},{3,7},{5,1},{7,3},{8,12},{10,14},{12... | collective-permute-start | bytes 688136 | tf_op jit(solution)/shard_map/ppermute | solution.py:28
  131.7 10.5 %collective-permute-start.24 = (bf16[128,768]{1,0:T(8,128)(2,1)S(1)}, bf16[128,768]{1,0:T(8,128)(2,1)S(1)}, u32[]{:S(2)}, u32[]{:S(2)}) collective-permute-start(bf16[128,768]{1,0:T(8,128)(2,1)S(1)} %sum_stage.22.refs_6_), channel_id=1, source_target_pairs={{0,8},{8,16},{16,24},{24,0},{1,9},{9,17},{17,25},{25,1},{2,10},{10... | collective-permute-start | bytes 589832 | tf_op jit(solution)/shard_map/ppermute | solution.py:23
  134.0 7.2 %collective-permute-start.31 = (bf16[128,384]{1,0:T(8,128)(2,1)S(1)}, bf16[128,384]{1,0:T(8,128)(2,1)S(1)}, u32[]{:S(2)}, u32[]{:S(2)}) collective-permute-start(bf16[128,384]{1,0:T(8,128)(2,1)S(1)} %get-tuple-element.96), channel_id=1, source_target_pairs={{0,1},{1,0},{2,3},{3,2},{4,5},{5,4},{6,7},{7,6},{8,9},{9,8},{10,11... | collective-permute-start | bytes 294920 | tf_op jit(solution)/shard_map/ppermute | solution.py:28
  136.8 5.3 %collective-permute-start.32 = (bf16[128,384]{1,0:T(8,128)(2,1)S(1)}, bf16[128,384]{1,0:T(8,128)(2,1)S(1)}, u32[]{:S(2)}, u32[]{:S(2)}) collective-permute-start(bf16[128,384]{1,0:T(8,128)(2,1)S(1)} %get-tuple-element.97), channel_id=1, source_target_pairs={{0,4},{2,6},{4,0},{6,2},{1,5},{3,7},{5,1},{7,3},{8,12},{10,14},{12... | collective-permute-start | bytes 294920 | tf_op jit(solution)/shard_map/ppermute | solution.py:28
  137.9 9.1 %collective-permute-start.28 = (bf16[128,768]{1,0:T(8,128)(2,1)S(1)}, bf16[128,768]{1,0:T(8,128)(2,1)S(1)}, u32[]{:S(2)}, u32[]{:S(2)}) collective-permute-start(bf16[128,768]{1,0:T(8,128)(2,1)S(1)} %sum_stage.24.refs_6_), channel_id=1, source_target_pairs={{0,8},{8,16},{16,24},{24,0},{1,9},{9,17},{17,25},{25,1},{2,10},{10... | collective-permute-start | bytes 589832 | tf_op jit(solution)/shard_map/ppermute | solution.py:23
  139.7 4.3 %collective-permute-start.29 = (bf16[128,256]{1,0:T(8,128)(2,1)S(1)}, bf16[128,256]{1,0:T(8,128)(2,1)S(1)}, u32[]{:S(2)}, u32[]{:S(2)}) collective-permute-start(bf16[128,256]{1,0:T(8,128)(2,1)S(1)} %get-tuple-element.92), channel_id=1, source_target_pairs={{0,1},{1,0},{2,3},{3,2},{4,5},{5,4},{6,7},{7,6},{8,9},{9,8},{10,11... | collective-permute-start | bytes 196616 | tf_op jit(solution)/shard_map/ppermute | solution.py:28
  141.2 4.3 %collective-permute-start.30 = (bf16[128,256]{1,0:T(8,128)(2,1)S(1)}, bf16[128,256]{1,0:T(8,128)(2,1)S(1)}, u32[]{:S(2)}, u32[]{:S(2)}) collective-permute-start(bf16[128,256]{1,0:T(8,128)(2,1)S(1)} %get-tuple-element.93), channel_id=1, source_target_pairs={{0,4},{2,6},{4,0},{6,2},{1,5},{3,7},{5,1},{7,3},{8,12},{10,14},{12... | collective-permute-start | bytes 196616 | tf_op jit(solution)/shard_map/ppermute | solution.py:28
  142.2 10.3 %collective-permute-start.34 = (bf16[128,768]{1,0:T(8,128)(2,1)S(1)}, bf16[128,768]{1,0:T(8,128)(2,1)S(1)}, u32[]{:S(2)}, u32[]{:S(2)}) collective-permute-start(bf16[128,768]{1,0:T(8,128)(2,1)S(1)} %sum_stage.26.refs_5_), channel_id=1, source_target_pairs={{0,8},{8,16},{16,24},{24,0},{1,9},{9,17},{17,25},{25,1},{2,10},{10... | collective-permute-start | bytes 589832 | tf_op jit(solution)/shard_map/ppermute | solution.py:23
  145.5 7.0 %collective-permute-start.33 = (bf16[128,512]{1,0:T(8,128)(2,1)S(1)}, bf16[128,512]{1,0:T(8,128)(2,1)S(1)}, u32[]{:S(2)}, u32[]{:S(2)}) collective-permute-start(bf16[128,512]{1,0:T(8,128)(2,1)S(1)} %sum_stage.27), channel_id=1, source_target_pairs={{0,8},{8,16},{16,24},{24,0},{1,9},{9,17},{17,25},{25,1},{2,10},{10... | collective-permute-start | bytes 393224 | tf_op jit(solution)/shard_map/ppermute | solution.py:23
  152.6 1.1 copy-start.10

commit v21 on v19

--- a/solution.py
+++ b/solution.py
@@ -63,16 +63,17 @@
 
 
 def halves_kernel(rows_ref, upper_ref, lower_ref, held, sems):
-    half = upper_ref.shape[0]
-    places = pl.ds(0, half), pl.ds(half, half)
-    copies_in = [
-        pltpu.make_async_copy(rows_ref.at[place], held.at[place], sems.at[0, index])
-        for index, place in enumerate(places)
-    ]
-    copies_out = [
-        pltpu.make_async_copy(held.at[place], ref, sems.at[1, index])
-        for index, (place, ref) in enumerate(zip(places, (upper_ref, lower_ref)))
-    ]
+    half, pieces = upper_ref.shape[0], sems.shape[1]
+    size = rows_ref.shape[0] // pieces
+    copies_in, copies_out = [], []
+    for piece in range(pieces):
+        start = piece * size
+        place = held.at[pl.ds(start, size)]
+        target = (upper_ref, lower_ref)[start // half].at[pl.ds(start % half, size)]
+        copies_in.append(
+            pltpu.make_async_copy(rows_ref.at[pl.ds(start, size)], place, sems.at[0, piece])
+        )
+        copies_out.append(pltpu.make_async_copy(place, target, sems.at[1, piece]))
     for copy in copies_in:
         copy.start()
     for copy_in, copy_out in zip(copies_in, copies_out):
@@ -91,7 +92,7 @@
         out_shape=[jax.ShapeDtypeStruct((count // 2, features), rows.dtype)] * 2,
         scratch_shapes=[
             pltpu.VMEM((count, features), rows.dtype),
-            pltpu.SemaphoreType.DMA((2, 2)),
+            pltpu.SemaphoreType.DMA((2, 4)),
         ],
         name="halves_of",
         cost_estimate=SHORT,
@@ -230,7 +231,7 @@
         before_head(head)
         for block in range(blocks):
             waiting.append((head, block, scores_of(head, block)))
-            if len(waiting) > 2:
+            if len(waiting) > 3:
                 finish(*waiting.pop(0))
     for unit in waiting:
         finish(*unit)

time: 154 us -> 154 us (level)
  no operation moved by 1% of the time
where the time goes in v21:
time: 154 us; the launch traced here: 153 us
  Pallas kernels  50.3 us (33%)
  starting transfers between devices  41.7 us (27%)
  waiting for transfers between devices  36.1 us (23%)
  local copies, waits for them, and re-layouts  24.6 us (16%)
    ppermute x29, starting transfers between devices, from_partner(): return lax.ppermute(value, axis, pairs)  26.9 us
    ppermute x29, waiting for transfers between devices, from_partner(): return lax.ppermute(value, axis, pairs)  26.3 us
    pallas_call x1, Pallas kernels, project(): pl.pallas_call(functools.partial(project_kernel, blocks=len(blocks)), gri...  19.2 us
    pallas_call x14, Pallas kernels, stage(): pl.pallas_call(functools.partial(stage_kernel, parts=parts, start=start,...  12.8 us
    ppermute x6, starting transfers between devices, from_behind(): return lax.ppermute(x, axis, [(i, (i + by) % count) for i in range(count)])  10.2 us
    pallas_call x4, Pallas kernels, modulated_norm(): pl.pallas_call(norm_kernel, in_specs=[pl.BlockSpec(memory_space=pltpu.VME...  8.49 us
    reshape x1, local copies, waits for them, and re-layouts, per_device(): unpacked.transpose(2, 0, 1, 3).reshape(devices, context_rows, 2 * width)  8.06 us
    another operation x1, local copies, waits for them, and re-layouts, per_device(): unpacked = stale_cache[0, 0].reshape(context_rows, 2, devices, width)  8 us
  transfers between devices with their start and end apart: 36, of which 19 were waited for; matrix products, arithmetic and copies ran while one was open for 13% of the time, Pallas kernels for 31%

profile of v21, /device:TPU:0, one launch (start us, length us, event | category | flops | bytes accessed | tf_op | source)
XLA Modules:
  0.0 153.2 jit_solution(2625738003585100818)
XLA Ops:
  0.0 2.1 %halves_of.1 = (bf16[64,5120]{1,0:T(8,128)(2,1)}, bf16[64,5120]{1,0:T(8,128)(2,1)}) custom-call(bf16[128,5120]{1,0:T(8,128)(2,1)} %bitcast.15), custom_call_target="tpu_custom_call" | custom-call | flops 1 | bytes 1 | tf_op jit(solution)/shard_map/halves_of/pallas_call | solution.py:88
  2.2 3.0 %collective-permute-start.1 = (bf16[64,5120]{1,0:T(8,128)(2,1)}, bf16[64,5120]{1,0:T(8,128)(2,1)S(1)}, u32[]{:S(2)}, u32[]{:S(2)}) collective-permute-start(bf16[64,5120]{1,0:T(8,128)(2,1)} %get-tuple-element.52), channel_id=1, source_target_pairs={{0,1},{1,0},{2,3},{3,2},{4,5},{5,4},{6,7},{7,6},{8,9},{9,8},{10,11... | collective-permute-start | bytes 1966088 | tf_op jit(solution)/shard_map/ppermute | solution.py:28
  5.2 1.5 collective-permute-start.4
  6.7 0.5 collective-permute-start.3
  7.3 8.0 %reshape_squeeze.3.refs_0_ = bf16[256,2,8,384]{3,2,1,0:T(8,128)(2,1)} reshape(bf16[1,1,256,2,3072]{4,3,2,1,0:T(2,128)(2,1)} %param.10) | data formatting | bytes 6291456 | tf_op jit(solution)/shard_map/reshape;squeeze | solution.py:470
  15.3 5.7 %collective-permute-done.1.value_ref = bf16[64,5120]{1,0:T(8,128)(2,1)S(1)} collective-permute-done((bf16[64,5120]{1,0:T(8,128)(2,1)}, bf16[64,5120]{1,0:T(8,128)(2,1)S(1)}, u32[]{:S(2)}, u32[]{:S(2)}) %collective-permute-start.1) | collective-permute-done | bytes 655392 | tf_op jit(solution)/shard_map/ppermute | solution.py:28
  20.9 1.9 %copy-done.2 = bf16[256,2,8,384]{3,2,1,0:T(8,128)(2,1)S(1)} copy-done((bf16[256,2,8,384]{3,2,1,0:T(8,128)(2,1)S(1)}, bf16[256,2,8,384]{3,2,1,0:T(8,128)(2,1)}, u32[]{:S(2)}) %copy-start.2) | copy-done | bytes 3145752
  22.8 2.1 %collective-permute-start.5 = (bf16[64,5120]{1,0:T(8,128)(2,1)S(1)}, bf16[64,5120]{1,0:T(8,128)(2,1)}, u32[]{:S(2)}, u32[]{:S(2)}) collective-permute-start(bf16[64,5120]{1,0:T(8,128)(2,1)S(1)} %after.3.refs_0_), channel_id=1, source_target_pairs={{0,4},{2,6},{4,0},{6,2},{1,5},{3,7},{5,1},{7,3},{8,12},{10,14},{12... | collective-permute-start | bytes 1966088 | tf_op jit(solution)/shard_map/ppermute | solution.py:28
  24.9 1.8 %collective-permute-start.6 = (bf16[64,5120]{1,0:T(8,128)(2,1)S(1)}, bf16[64,5120]{1,0:T(8,128)(2,1)}, u32[]{:S(2)}, u32[]{:S(2)}) collective-permute-start(bf16[64,5120]{1,0:T(8,128)(2,1)S(1)} %after.4.refs_1_), channel_id=1, source_target_pairs={{0,1},{1,0},{2,3},{3,2},{4,5},{5,4},{6,7},{7,6},{8,9},{9,8},{10,11... | collective-permute-start | bytes 1966088 | tf_op jit(solution)/shard_map/ppermute | solution.py:28
  27.0 1.5 modulated_norm.4.refs_0_
  28.6 1.0 copy-done.6
  29.6 4.1 %copy.11 = bf16[8,256,2,384]{3,2,1,0:T(2,128)(2,1)} copy(bf16[8,256,2,384]{3,0,2,1:T(8,128)(2,1)S(1)} %bitcast.38) | data formatting | bytes 6291456 | tf_op jit(solution)/shard_map/transpose | solution.py:471
  33.7 8.1 %reshape.8.value_ref = bf16[8,256,768]{2,1,0:T(8,128)(2,1)} reshape(bf16[8,256,2,384]{3,2,1,0:T(2,128)(2,1)} %copy.11) | data formatting | bytes 6291456 | tf_op jit(solution)/shard_map/reshape | solution.py:471
  41.8 0.5 collective-permute-start.11
  42.6 4.6 %all-to-all-start = ((bf16[8,256,768]{2,1,0:T(8,128)(2,1)}), bf16[8,256,768]{2,1,0:T(8,128)(2,1)}, u32[]{:S(2)}, u32[]{:S(2)}) async-start(bf16[8,256,768]{2,1,0:T(8,128)(2,1)} %after.5), calls=%async_computation | async-start | bytes 6291456 | tf_op jit(solution)/shard_map/all_to_all | solution.py:489
  47.2 3.1 %collective-permute-done = f32[1,1,3,5120]{3,2,1,0:T(4,128)S(1)} collective-permute-done((f32[1,1,3,5120]{3,2,1,0:T(4,128)S(1)}, f32[1,1,3,5120]{3,2,1,0:T(4,128)S(1)}, u32[]{:S(2)}, u32[]{:S(2)}) %collective-permute-start) | collective-permute-done | bytes 61472 | tf_op jit(solution)/shard_map/ppermute | solution.py:28
  50.4 2.7 %modulated_norm.5.refs_1_ = bf16[128,5120]{1,0:T(8,128)(2,1)S(1)} custom-call(bf16[64,5120]{1,0:T(8,128)(2,1)S(1)} %after.3.refs_0_, bf16[64,5120]{1,0:T(8,128)(2,1)} %collective-permute-done.2.refs_1_.refs_0_, f32[3,5120]{1,0:T(4,128)S(1)} %bitcast.41), custom_call_target="tpu_custom_call" | custom-call | flops 1 | bytes 1 | tf_op jit(solution)/shard_map/modulated_norm/pallas_call | solution.py:55
  53.1 1.5 modulated_norm.6.refs_2_
  54.7 0.6 collective-permute-start.9
  55.2 2.8 %modulated_norm.7.refs_3_ = bf16[128,5120]{1,0:T(8,128)(2,1)S(1)} custom-call(bf16[64,5120]{1,0:T(8,128)(2,1)} %collective-permute-done.5.refs_0_, bf16[64,5120]{1,0:T(8,128)(2,1)} %collective-permute-done.6.refs_1_, f32[3,5120]{1,0:T(4,128)S(1)} %bitcast.42), custom_call_target="tpu_custom_call" | custom-call | flops 1 | bytes 1 | tf_op jit(solution)/shard_map/modulated_norm/pallas_call | solution.py:55
  58.3 2.9 %collective-permute-done.10.refs_7_ = bf16[128,5120]{1,0:T(8,128)(2,1)S(1)} collective-permute-done((bf16[128,5120]{1,0:T(8,128)(2,1)S(1)}, bf16[128,5120]{1,0:T(8,128)(2,1)S(1)}, u32[]{:S(2)}, u32[]{:S(2)}) %collective-permute-start.10) | collective-permute-done | bytes 1310752 | tf_op jit(solution)/shard_map/ppermute | solution.py:28
  61.1 19.2 %project_heads.1.heads_in = bf16[48,1024,128]{2,1,0:T(8,128)(2,1)} custom-call(bf16[128,5120]{1,0:T(8,128)(2,1)S(1)} %copy-done.7, bf16[128,5120]{1,0:T(8,128)(2,1)S(1)} %modulated_norm.5.refs_1_, bf16[128,5120]{1,0:T(8,128)(2,1)S(1)} %modulated_norm.6.refs_2_, bf16[128,5120]{1,0:T(8,128)(2,1)S(1)} %modulated_norm.7.refs_3_, ...), custom_call_target="tpu_custom_call" | custom-call | flops 12079595520 | bytes 22282240 | tf_op jit(solution)/shard_map/project_heads/pallas_call | solution.py:162
  80.3 4.2 %all-to-all-done = bf16[8,256,768]{2,1,0:T(8,128)(2,1)} async-done(((bf16[8,256,768]{2,1,0:T(8,128)(2,1)}), bf16[8,256,768]{2,1,0:T(8,128)(2,1)}, u32[]{:S(2)}, u32[]{:S(2)}) %all-to-all-start) | async-done | bytes 3145760 | tf_op jit(solution)/shard_map/all_to_all | solution.py:489
  84.5 4.4 %attend_first.1 = (bf16[512,384]{1,0:T(8,128)(2,1)S(1)}, bf16[3,1024,128]{2,1,0:T(8,128)(2,1)S(1)}, bf16[6,3072,128]{2,1,0:T(8,128)(2,1)S(1)}) custom-call(s32[4,6]{1,0:T(4,128)S(1)} %bitcast.43, bf16[48,1024,128]{2,1,0:T(8,128)(2,1)} %project_heads.1.heads_in, bf16[2048,768]{1,0:T(8,128)(2,1)} %bitcast.7.context_in), custom_call_target="tpu_custom_call" | custom-call | flops 1 | bytes 1 | tf_op jit(solution)/shard_map/attend_first/pallas_call | solution.py:271
  89.1 3.3 %attend_second.1 = (bf16[512,384]{1,0:T(8,128)(2,1)S(1)}, bf16[768,1024]{1,0:T(8,128)(2,1)S(1)}) custom-call(s32[4,6]{1,0:T(4,128)S(1)} %bitcast.44, bf16[3,1024,128]{2,1,0:T(8,128)(2,1)S(1)} %get-tuple-element.54.queries_ref, bf16[6,3072,128]{2,1,0:T(8,128)(2,1)S(1)} %get-tuple-element.55.pool_ref, bf16[384,5120]{1,0:T(8,128)(2,1)S(1)} %bitcast.32, ...), custom_call_target="tpu_custom_call" | custom-call | flops 1 | bytes 1 | tf_op jit(solution)/shard_map/attend_second/pallas_call | solution.py:310
  92.5 1.0 sum_stage.14
  93.5 1.0 collective-permute-start.13
  94.6 1.5 collective-permute-start.14
  96.1 2.7 %sum_stage.15 = (bf16[128,1280]{1,0:T(8,128)(2,1)S(1)}, bf16[128,1280]{1,0:T(8,128)(2,1)S(1)}, f32[2,128,640]{2,1,0:T(8,128)S(1)}, f32[2,128,640]{2,1,0:T(8,128)S(1)}) custom-call(bf16[128,5120]{1,0:T(8,128)(2,1)S(1)} %bitcast.18, f32[2,5120]{1,0:T(2,128)S(1)} %pad_maximum_fusion.refs_3_.refs_1_, bf16[512,384]{1,0:T(8,128)(2,1)S(1)} %get-tuple-element.57.refs_2_, ...), custom_call_target="tpu_custom_call" | custom-call | flops 1 | bytes 1 | tf_op jit(solution)/shard_map/sum_stage/pallas_call | solution.py:435
  99.2 1.2 collective-permute-start.18
  100.4 2.3 %collective-permute-done.13.refs_6_ = bf16[128,1024]{1,0:T(8,128)(2,1)S(1)} collective-permute-done((bf16[128,1024]{1,0:T(8,128)(2,1)S(1)}, bf16[128,1024]{1,0:T(8,128)(2,1)S(1)}, u32[]{:S(2)}, u32[]{:S(2)}) %collective-permute-start.13) | collective-permute-done | bytes 262176 | tf_op jit(solution)/shard_map/ppermute | solution.py:28
  102.7 1.0 collective-permute-done.14.refs_7_
  103.7 2.3 %sum_stage.16 = (bf16[128,1280]{1,0:T(8,128)(2,1)S(1)}, bf16[128,1280]{1,0:T(8,128)(2,1)S(1)}, f32[2,128,384]{2,1,0:T(8,128)S(1)}, f32[2,128,384]{2,1,0:T(8,128)...) custom-call(bf16[128,5120]{1,0:T(8,128)(2,1)S(1)} %bitcast.19, f32[2,5120]{1,0:T(2,128)S(1)} %pad_maximum_fusion.refs_3_.refs_1_, ...), custom_call_target="tpu_custom_call" | custom-call | flops 1 | bytes 1 | tf_op jit(solution)/shard_map/sum_stage/pallas_call | solution.py:435
  106.0 1.1 collective-permute-start.15
  107.1 0.8 collective-permute-start.16
  107.9 1.8 %collective-permute-done.17.refs_6_ = bf16[128,1280]{1,0:T(8,128)(2,1)S(1)} collective-permute-done((bf16[128,1280]{1,0:T(8,128)(2,1)S(1)}, bf16[128,1280]{1,0:T(8,128)(2,1)S(1)}, u32[]{:S(2)}, u32[]{:S(2)}) %collective-permute-start.17) | collective-permute-done | bytes 327712 | tf_op jit(solution)/shard_map/ppermute | solution.py:28
  109.7 1.0 collective-permute-done.18.refs_7_
  110.7 2.4 %sum_stage.17 = (bf16[128,1408]{1,0:T(8,128)(2,1)S(1)}, bf16[128,1408]{1,0:T(8,128)(2,1)S(1)}, f32[2,128,384]{2,1,0:T(8,128)S(1)}, f32[2,128,384]{2,1,0:T(8,128)...) custom-call(bf16[128,5120]{1,0:T(8,128)(2,1)S(1)} %bitcast.20, f32[2,5120]{1,0:T(2,128)S(1)} %pad_maximum_fusion.refs_3_.refs_1_, ...), custom_call_target="tpu_custom_call" | custom-call | flops 1 | bytes 1 | tf_op jit(solution)/shard_map/sum_stage/pallas_call | solution.py:435
  113.1 1.1 collective-permute-start.21
  114.2 0.8 collective-permute-start.22
  115.0 1.7 %collective-permute-done.15.refs_1_.refs_6_ = bf16[128,1280]{1,0:T(8,128)(2,1)S(1)} collective-permute-done((bf16[128,1280]{1,0:T(8,128)(2,1)S(1)}, bf16[128,1280]{1,0:T(8,128)(2,1)S(1)}, u32[]{:S(2)}, u32[]{:S(2)}) %collective-permute-start.15) | collective-permute-done | bytes 327712 | tf_op jit(solution)/shard_map/ppermute | solution.py:28
  116.7 1.0 collective-permute-done.16.refs_2_.refs_7_
  117.8 1.9 %collective-permute-start.23 = (bf16[128,1024]{1,0:T(8,128)(2,1)S(1)}, bf16[128,1024]{1,0:T(8,128)(2,1)S(1)}, u32[]{:S(2)}, u32[]{:S(2)}) collective-permute-start(bf16[128,1024]{1,0:T(8,128)(2,1)S(1)} %sum_stage.18.refs_10_), channel_id=1, source_target_pairs={{0,8},{8,16},{16,24},{24,0},{1,9},{9,17},{17,25},{25,1},{2,10},{10... | collective-permute-start | bytes 786440 | tf_op jit(solution)/shard_map/ppermute | solution.py:23
  119.7 2.2 %sum_stage.19 = (bf16[128,1152]{1,0:T(8,128)(2,1)S(1)}, bf16[128,1152]{1,0:T(8,128)(2,1)S(1)}, f32[2,128,384]{2,1,0:T(8,128)S(1)}, f32[2,128,384]{2,1,0:T(8,128)...) custom-call(bf16[128,5120]{1,0:T(8,128)(2,1)S(1)} %bitcast.22, f32[2,5120]{1,0:T(2,128)S(1)} %pad_maximum_fusion.refs_3_.refs_1_, ...), custom_call_target="tpu_custom_call" | custom-call | flops 1 | bytes 1 | tf_op jit(solution)/shard_map/sum_stage/pallas_call | solution.py:435
  121.9 1.1 collective-permute-start.19
  123.0 1.0 collective-permute-start.20
  124.5 1.1 collective-permute-done.22.refs_2_.refs_7_
  125.6 1.8 %collective-permute-start.27 = (bf16[128,1280]{1,0:T(8,128)(2,1)S(1)}, bf16[128,1280]{1,0:T(8,128)(2,1)S(1)}, u32[]{:S(2)}, u32[]{:S(2)}) collective-permute-start(bf16[128,1280]{1,0:T(8,128)(2,1)S(1)} %sum_stage.20.refs_10_), channel_id=1, source_target_pairs={{0,8},{8,16},{16,24},{24,0},{1,9},{9,17},{17,25},{25,1},{2,10},{10... | collective-permute-start | bytes 983048 | tf_op jit(solution)/shard_map/ppermute | solution.py:23
  127.4 1.7 %sum_stage.21 = (bf16[128,896]{1,0:T(8,128)(2,1)S(1)}, bf16[128,896]{1,0:T(8,128)(2,1)S(1)}, f32[2,128,256]{2,1,0:T(8,128)S(1)}, f32[2,128,256]{2,1,0:T(8,128)S(...) custom-call(bf16[128,5120]{1,0:T(8,128)(2,1)S(1)} %bitcast.24, f32[2,5120]{1,0:T(2,128)S(1)} %pad_maximum_fusion.refs_3_.refs_1_, ...), custom_call_target="tpu_custom_call" | custom-call | flops 1 | bytes 1 | tf_op jit(solution)/shard_map/sum_stage/pallas_call | solution.py:435
  129.1 1.1 collective-permute-start.25
  130.2 0.5 collective-permute-start.26
  131.2 2.2 %collective-permute-start.24 = (bf16[128,768]{1,0:T(8,128)(2,1)S(1)}, bf16[128,768]{1,0:T(8,128)(2,1)S(1)}, u32[]{:S(2)}, u32[]{:S(2)}) collective-permute-start(bf16[128,768]{1,0:T(8,128)(2,1)S(1)} %sum_stage.22.refs_6_), channel_id=1, source_target_pairs={{0,8},{8,16},{16,24},{24,0},{1,9},{9,17},{17,25},{25,1},{2,10},{10... | collective-permute-start | bytes 589832 | tf_op jit(solution)/shard_map/ppermute | solution.py:23
  133.5 1.2 collective-permute-start.31
  134.7 1.7 %collective-permute-done.25.refs_1_.refs_2_ = bf16[128,896]{1,0:T(8,128)(2,1)S(1)} collective-permute-done((bf16[128,896]{1,0:T(8,128)(2,1)S(1)}, bf16[128,896]{1,0:T(8,128)(2,1)S(1)}, u32[]{:S(2)}, u32[]{:S(2)}) %collective-permute-start.25) | collective-permute-done | bytes 229408 | tf_op jit(solution)/shard_map/ppermute | solution.py:28
  136.3 1.1 collective-permute-start.32
  137.5 1.6 %collective-permute-start.28 = (bf16[128,768]{1,0:T(8,128)(2,1)S(1)}, bf16[128,768]{1,0:T(8,128)(2,1)S(1)}, u32[]{:S(2)}, u32[]{:S(2)}) collective-permute-start(bf16[128,768]{1,0:T(8,128)(2,1)S(1)} %sum_stage.24.refs_6_), channel_id=1, source_target_pairs={{0,8},{8,16},{16,24},{24,0},{1,9},{9,17},{17,25},{25,1},{2,10},{10... | collective-permute-start | bytes 589832 | tf_op jit(solution)/shard_map/ppermute | solution.py:23
  139.2 1.5 collective-permute-start.29
  140.7 0.8 collective-permute-start.30
  141.7 1.2 collective-permute-start.34
  142.9 0.6 collective-permute-done.29.refs_1_
  143.5 1.4 collective-permute-done.30.refs_2_
  145.0 1.5 collective-permute-start.33
  146.8 5.2 %collective-permute-done.33 = bf16[128,512]{1,0:T(8,128)(2,1)S(1)} collective-permute-done((bf16[128,512]{1,0:T(8,128)(2,1)S(1)}, bf16[128,512]{1,0:T(8,128)(2,1)S(1)}, u32[]{:S(2)}, u32[]{:S(2)}) %collective-permute-start.33) | collective-permute-done | bytes 131104 | tf_op jit(solution)/shard_map/ppermute | solution.py:23
  152.1 1.0 copy-done.10
  (68 shorter events, 3.5 us)
Async XLA Ops:
  2.2 18.8 %collective-permute-start.1 = (bf16[64,5120]{1,0:T(8,128)(2,1)}, bf16[64,5120]{1,0:T(8,128)(2,1)S(1)}, u32[]{:S(2)}, u32[]{:S(2)}) collective-permute-start(bf16[64,5120]{1,0:T(8,128)(2,1)} %get-tuple-element.52), channel_id=1, source_target_pairs={{0,1},{1,0},{2,3},{3,2},{4,5},{5,4},{6,7},{7,6},{8,9},{9,8},{10,11... | collective-permute-start | bytes 1966088 | tf_op jit(solution)/shard_map/ppermute | solution.py:28
  5.2 19.8 %collective-permute-start.4 = (bf16[64,5120]{1,0:T(8,128)(2,1)}, bf16[64,5120]{1,0:T(8,128)(2,1)S(1)}, u32[]{:S(2)}, u32[]{:S(2)}) collective-permute-start(bf16[64,5120]{1,0:T(8,128)(2,1)} %get-tuple-element.53), channel_id=1, source_target_pairs={{0,4},{2,6},{4,0},{6,2},{1,5},{3,7},{5,1},{7,3},{8,12},{10,14},{12... | collective-permute-start | bytes 1966088 | tf_op jit(solution)/shard_map/ppermute | solution.py:28
  6.7 35.1 %collective-permute-start.3 = (bf16[64,5120]{1,0:T(8,128)(2,1)}, bf16[64,5120]{1,0:T(8,128)(2,1)S(1)}, u32[]{:S(2)}, u32[]{:S(2)}) collective-permute-start(bf16[64,5120]{1,0:T(8,128)(2,1)} %get-tuple-element.52), channel_id=1, source_target_pairs={{0,4},{2,6},{4,0},{6,2},{1,5},{3,7},{5,1},{7,3},{8,12},{10,14},{12... | collective-permute-start | bytes 1966088 | tf_op jit(solution)/shard_map/ppermute | solution.py:28
  7.2 34.6 %collective-permute-start.2 = (bf16[64,5120]{1,0:T(8,128)(2,1)}, bf16[64,5120]{1,0:T(8,128)(2,1)}, u32[]{:S(2)}, u32[]{:S(2)}) collective-permute-start(bf16[64,5120]{1,0:T(8,128)(2,1)} %get-tuple-element.53), channel_id=1, source_target_pairs={{0,1},{1,0},{2,3},{3,2},{4,5},{5,4},{6,7},{7,6},{8,9},{9,8},{10,11... | collective-permute-start | bytes 1966088 | tf_op jit(solution)/shard_map/ppermute | solution.py:28
  20.9 1.9 %copy-start.2 = (bf16[256,2,8,384]{3,2,1,0:T(8,128)(2,1)S(1)}, bf16[256,2,8,384]{3,2,1,0:T(8,128)(2,1)}, u32[]{:S(2)}) copy-start(bf16[256,2,8,384]{3,2,1,0:T(8,128)(2,1)} %reshape_squeeze.3.refs_0_) | copy-start | bytes 9437188
  22.8 2.1 %copy-start.3 = (bf16[256,2,8,384]{3,2,1,0:T(8,128)(2,1)S(1)}, bf16[256,2,8,384]{3,2,1,0:T(8,128)(2,1)}, u32[]{:S(2)}) copy-start(bf16[256,2,8,384]{3,2,1,0:T(8,128)(2,1)} %reshape_squeeze.3.refs_0_) | copy-start | bytes 9437188
  22.8 3.9 %copy-start.9 = (f32[1,1,3,5120]{3,1,2,0:T(1,128)S(1)}, f32[1,1,3,5120]{3,1,2,0:T(1,128)}, u32[]{:S(2)}) copy-start(f32[1,1,3,5120]{3,1,2,0:T(1,128)} %param.7) | copy-start | bytes 184324
  22.8 4.2 %copy-start = (bf16[1,1,128,5120]{3,2,1,0:T(8,128)(2,1)S(1)}, bf16[1,1,128,5120]{3,2,1,0:T(8,128)(2,1)}, u32[]{:S(2)}) copy-start(bf16[1,1,128,5120]{3,2,1,0:T(8,128)(2,1)} %param.6) | copy-start | bytes 3932164
  22.8 31.8 %collective-permute-start.5 = (bf16[64,5120]{1,0:T(8,128)(2,1)S(1)}, bf16[64,5120]{1,0:T(8,128)(2,1)}, u32[]{:S(2)}, u32[]{:S(2)}) collective-permute-start(bf16[64,5120]{1,0:T(8,128)(2,1)S(1)} %after.3.refs_0_), channel_id=1, source_target_pairs={{0,4},{2,6},{4,0},{6,2},{1,5},{3,7},{5,1},{7,3},{8,12},{10,14},{12... | collective-permute-start | bytes 1966088 | tf_op jit(solution)/shard_map/ppermute | solution.py:28
  24.9 30.3 %collective-permute-start.6 = (bf16[64,5120]{1,0:T(8,128)(2,1)S(1)}, bf16[64,5120]{1,0:T(8,128)(2,1)}, u32[]{:S(2)}, u32[]{:S(2)}) collective-permute-start(bf16[64,5120]{1,0:T(8,128)(2,1)S(1)} %after.4.refs_1_), channel_id=1, source_target_pairs={{0,1},{1,0},{2,3},{3,2},{4,5},{5,4},{6,7},{7,6},{8,9},{9,8},{10,11... | collective-permute-start | bytes 1966088 | tf_op jit(solution)/shard_map/ppermute | solution.py:28
  26.8 23.6 %collective-permute-start = (f32[1,1,3,5120]{3,2,1,0:T(4,128)S(1)}, f32[1,1,3,5120]{3,2,1,0:T(4,128)S(1)}, u32[]{:S(2)}, u32[]{:S(2)}) collective-permute-start(f32[1,1,3,5120]{3,2,1,0:T(4,128)S(1)} %copy.15), channel_id=1, source_target_pairs={{0,1},{1,0},{2,3},{3,2},{4,5},{5,4},{6,7},{7,6},{8,9},{9,8},{10,11... | collective-permute-start | bytes 184328 | tf_op jit(solution)/shard_map/ppermute | solution.py:28
  28.6 1.1 copy-start.6
  41.7 0.9 copy-start.4
  41.7 16.5 %collective-permute-start.7 = (bf16[128,5120]{1,0:T(8,128)(2,1)}, bf16[128,5120]{1,0:T(8,128)(2,1)}, u32[]{:S(2)}, u32[]{:S(2)}) collective-permute-start(bf16[128,5120]{1,0:T(8,128)(2,1)} %copy-done.6), channel_id=1, source_target_pairs={{0,2},{2,0},{4,6},{6,4},{1,3},{3,1},{5,7},{7,5},{8,10},{10,8},{12,... | collective-permute-start | bytes 3932168 | tf_op jit(solution)/shard_map/ppermute | solution.py:28
  41.8 47.3 %collective-permute-start.11 = (bf16[384,5120]{1,0:T(8,128)(2,1)}, bf16[384,5120]{1,0:T(8,128)(2,1)}, u32[]{:S(2)}, u32[]{:S(2)}) collective-permute-start(bf16[384,5120]{1,0:T(8,128)(2,1)} %bitcast.31), channel_id=1, source_target_pairs={{0,2},{2,0},{4,6},{6,4},{1,3},{3,1},{5,7},{7,5},{8,10},{10,8},{12,... | collective-permute-start | bytes 11796488 | tf_op jit(solution)/shard_map/ppermute | solution.py:28
  42.6 41.9 %all-to-all-start = ((bf16[8,256,768]{2,1,0:T(8,128)(2,1)}), bf16[8,256,768]{2,1,0:T(8,128)(2,1)}, u32[]{:S(2)}, u32[]{:S(2)}) async-start(bf16[8,256,768]{2,1,0:T(8,128)(2,1)} %after.5), calls=%async_computation | async-start | bytes 6291456 | tf_op jit(solution)/shard_map/all_to_all | solution.py:489
  50.3 2.8 %copy-start.5 = (bf16[64,5120]{1,0:T(8,128)(2,1)S(1)}, bf16[64,5120]{1,0:T(8,128)(2,1)}, u32[]{:S(2)}) copy-start(bf16[64,5120]{1,0:T(8,128)(2,1)} %copy-done.4) | copy-start | bytes 1966084
  53.0 5.2 %collective-permute-start.8 = (bf16[128,5120]{1,0:T(8,128)(2,1)S(1)}, bf16[128,5120]{1,0:T(8,128)(2,1)S(1)}, u32[]{:S(2)}, u32[]{:S(2)}) collective-permute-start(bf16[128,5120]{1,0:T(8,128)(2,1)S(1)} %modulated_norm.5.refs_1_), channel_id=1, source_target_pairs={{0,2},{2,0},{4,6},{6,4},{1,3},{3,1},{5,7},{7,5},{8,10},{10,8},{12,... | collective-permute-start | bytes 3932168 | tf_op jit(solution)/shard_map/ppermute | solution.py:28
  54.6 6.5 %copy-start.7 = (bf16[128,5120]{1,0:T(8,128)(2,1)S(1)}, bf16[128,5120]{1,0:T(8,128)(2,1)}, u32[]{:S(2)}) copy-start(bf16[128,5120]{1,0:T(8,128)(2,1)} %copy-done.6) | copy-start | bytes 3932164
  54.7 3.6 %collective-permute-start.9 = (bf16[128,5120]{1,0:T(8,128)(2,1)S(1)}, bf16[128,5120]{1,0:T(8,128)(2,1)S(1)}, u32[]{:S(2)}, u32[]{:S(2)}) collective-permute-start(bf16[128,5120]{1,0:T(8,128)(2,1)S(1)} %modulated_norm.6.refs_2_), channel_id=1, source_target_pairs={{0,2},{2,0},{4,6},{6,4},{1,3},{3,1},{5,7},{7,5},{8,10},{10,8},{12,... | collective-permute-start | bytes 3932168 | tf_op jit(solution)/shard_map/ppermute | solution.py:28
  58.0 3.1 %collective-permute-start.10 = (bf16[128,5120]{1,0:T(8,128)(2,1)S(1)}, bf16[128,5120]{1,0:T(8,128)(2,1)S(1)}, u32[]{:S(2)}, u32[]{:S(2)}) collective-permute-start(bf16[128,5120]{1,0:T(8,128)(2,1)S(1)} %modulated_norm.7.refs_3_), channel_id=1, source_target_pairs={{0,2},{2,0},{4,6},{6,4},{1,3},{3,1},{5,7},{7,5},{8,10},{10,8},{12,... | collective-permute-start | bytes 3932168 | tf_op jit(solution)/shard_map/ppermute | solution.py:28
  61.1 23.4 %copy-start.8 = (s32[1,4,6]{2,1,0:T(4,128)S(1)}, s32[1,4,6]{2,1,0:T(4,128)}, u32[]{:S(2)}) copy-start(s32[1,4,6]{2,1,0:T(4,128)} %param.11) | copy-start | bytes 292
  84.5 4.6 %copy-start.1 = (bf16[1,384,5120]{2,1,0:T(8,128)(2,1)S(1)}, bf16[1,384,5120]{2,1,0:T(8,128)(2,1)}, u32[]{:S(2)}) copy-start(bf16[1,384,5120]{2,1,0:T(8,128)(2,1)} %param.9) | copy-start | bytes 11796484
  89.0 3.5 %collective-permute-start.12 = (bf16[512,384]{1,0:T(8,128)(2,1)S(1)}, bf16[512,384]{1,0:T(8,128)(2,1)S(1)}, u32[]{:S(2)}, u32[]{:S(2)}) collective-permute-start(bf16[512,384]{1,0:T(8,128)(2,1)S(1)} %get-tuple-element.56.refs_2_), channel_id=1, source_target_pairs={{0,2},{2,0},{4,6},{6,4},{1,3},{3,1},{5,7},{7,5},{8,10},{10,8},{12,... | collective-permute-start | bytes 1179656 | tf_op jit(solution)/shard_map/ppermute | solution.py:28
  93.5 9.2 %collective-permute-start.13 = (bf16[128,1024]{1,0:T(8,128)(2,1)S(1)}, bf16[128,1024]{1,0:T(8,128)(2,1)S(1)}, u32[]{:S(2)}, u32[]{:S(2)}) collective-permute-start(bf16[128,1024]{1,0:T(8,128)(2,1)S(1)} %get-tuple-element.59), channel_id=1, source_target_pairs={{0,1},{1,0},{2,3},{3,2},{4,5},{5,4},{6,7},{7,6},{8,9},{9,8},{10,11... | collective-permute-start | bytes 786440 | tf_op jit(solution)/shard_map/ppermute | solution.py:28
  94.6 9.1 %collective-permute-start.14 = (bf16[128,1024]{1,0:T(8,128)(2,1)S(1)}, bf16[128,1024]{1,0:T(8,128)(2,1)S(1)}, u32[]{:S(2)}, u32[]{:S(2)}) collective-permute-start(bf16[128,1024]{1,0:T(8,128)(2,1)S(1)} %get-tuple-element.60), channel_id=1, source_target_pairs={{0,4},{2,6},{4,0},{6,2},{1,5},{3,7},{5,1},{7,3},{8,12},{10,14},{12... | collective-permute-start | bytes 786440 | tf_op jit(solution)/shard_map/ppermute | solution.py:28
  98.8 10.9 %collective-permute-start.17 = (bf16[128,1280]{1,0:T(8,128)(2,1)S(1)}, bf16[128,1280]{1,0:T(8,128)(2,1)S(1)}, u32[]{:S(2)}, u32[]{:S(2)}) collective-permute-start(bf16[128,1280]{1,0:T(8,128)(2,1)S(1)} %get-tuple-element.70), channel_id=1, source_target_pairs={{0,1},{1,0},{2,3},{3,2},{4,5},{5,4},{6,7},{7,6},{8,9},{9,8},{10,11... | collective-permute-start | bytes 983048 | tf_op jit(solution)/shard_map/ppermute | solution.py:28
  99.2 11.5 %collective-permute-start.18 = (bf16[128,1280]{1,0:T(8,128)(2,1)S(1)}, bf16[128,1280]{1,0:T(8,128)(2,1)S(1)}, u32[]{:S(2)}, u32[]{:S(2)}) collective-permute-start(bf16[128,1280]{1,0:T(8,128)(2,1)S(1)} %get-tuple-element.71), channel_id=1, source_target_pairs={{0,4},{2,6},{4,0},{6,2},{1,5},{3,7},{5,1},{7,3},{8,12},{10,14},{12... | collective-permute-start | bytes 983048 | tf_op jit(solution)/shard_map/ppermute | solution.py:28
  106.0 10.7 %collective-permute-start.15 = (bf16[128,1280]{1,0:T(8,128)(2,1)S(1)}, bf16[128,1280]{1,0:T(8,128)(2,1)S(1)}, u32[]{:S(2)}, u32[]{:S(2)}) collective-permute-start(bf16[128,1280]{1,0:T(8,128)(2,1)S(1)} %get-tuple-element.64), channel_id=1, source_target_pairs={{0,1},{1,0},{2,3},{3,2},{4,5},{5,4},{6,7},{7,6},{8,9},{9,8},{10,11... | collective-permute-start | bytes 983048 | tf_op jit(solution)/shard_map/ppermute | solution.py:28
  107.1 10.6 %collective-permute-start.16 = (bf16[128,1280]{1,0:T(8,128)(2,1)S(1)}, bf16[128,1280]{1,0:T(8,128)(2,1)S(1)}, u32[]{:S(2)}, u32[]{:S(2)}) collective-permute-start(bf16[128,1280]{1,0:T(8,128)(2,1)S(1)} %get-tuple-element.65), channel_id=1, source_target_pairs={{0,4},{2,6},{4,0},{6,2},{1,5},{3,7},{5,1},{7,3},{8,12},{10,14},{12... | collective-permute-start | bytes 983048 | tf_op jit(solution)/shard_map/ppermute | solution.py:28
  113.1 11.4 %collective-permute-start.21 = (bf16[128,1408]{1,0:T(8,128)(2,1)S(1)}, bf16[128,1408]{1,0:T(8,128)(2,1)S(1)}, u32[]{:S(2)}, u32[]{:S(2)}) collective-permute-start(bf16[128,1408]{1,0:T(8,128)(2,1)S(1)} %get-tuple-element.78), channel_id=1, source_target_pairs={{0,1},{1,0},{2,3},{3,2},{4,5},{5,4},{6,7},{7,6},{8,9},{9,8},{10,11... | collective-permute-start | bytes 1081352 | tf_op jit(solution)/shard_map/ppermute | solution.py:28
  114.2 11.4 %collective-permute-start.22 = (bf16[128,1408]{1,0:T(8,128)(2,1)S(1)}, bf16[128,1408]{1,0:T(8,128)(2,1)S(1)}, u32[]{:S(2)}, u32[]{:S(2)}) collective-permute-start(bf16[128,1408]{1,0:T(8,128)(2,1)S(1)} %get-tuple-element.79), channel_id=1, source_target_pairs={{0,4},{2,6},{4,0},{6,2},{1,5},{3,7},{5,1},{7,3},{8,12},{10,14},{12... | collective-permute-start | bytes 1081352 | tf_op jit(solution)/shard_map/ppermute | solution.py:28
  117.8 12.4 %collective-permute-start.23 = (bf16[128,1024]{1,0:T(8,128)(2,1)S(1)}, bf16[128,1024]{1,0:T(8,128)(2,1)S(1)}, u32[]{:S(2)}, u32[]{:S(2)}) collective-permute-start(bf16[128,1024]{1,0:T(8,128)(2,1)S(1)} %sum_stage.18.refs_10_), channel_id=1, source_target_pairs={{0,8},{8,16},{16,24},{24,0},{1,9},{9,17},{17,25},{25,1},{2,10},{10... | collective-permute-start | bytes 786440 | tf_op jit(solution)/shard_map/ppermute | solution.py:23
  121.9 8.8 %collective-permute-start.19 = (bf16[128,1152]{1,0:T(8,128)(2,1)S(1)}, bf16[128,1152]{1,0:T(8,128)(2,1)S(1)}, u32[]{:S(2)}, u32[]{:S(2)}) collective-permute-start(bf16[128,1152]{1,0:T(8,128)(2,1)S(1)} %get-tuple-element.74), channel_id=1, source_target_pairs={{0,1},{1,0},{2,3},{3,2},{4,5},{5,4},{6,7},{7,6},{8,9},{9,8},{10,11... | collective-permute-start | bytes 884744 | tf_op jit(solution)/shard_map/ppermute | solution.py:28
  123.0 8.1 %collective-permute-start.20 = (bf16[128,1152]{1,0:T(8,128)(2,1)S(1)}, bf16[128,1152]{1,0:T(8,128)(2,1)S(1)}, u32[]{:S(2)}, u32[]{:S(2)}) collective-permute-start(bf16[128,1152]{1,0:T(8,128)(2,1)S(1)} %get-tuple-element.75), channel_id=1, source_target_pairs={{0,4},{2,6},{4,0},{6,2},{1,5},{3,7},{5,1},{7,3},{8,12},{10,14},{12... | collective-permute-start | bytes 884744 | tf_op jit(solution)/shard_map/ppermute | solution.py:28
  125.6 11.8 %collective-permute-start.27 = (bf16[128,1280]{1,0:T(8,128)(2,1)S(1)}, bf16[128,1280]{1,0:T(8,128)(2,1)S(1)}, u32[]{:S(2)}, u32[]{:S(2)}) collective-permute-start(bf16[128,1280]{1,0:T(8,128)(2,1)S(1)} %sum_stage.20.refs_10_), channel_id=1, source_target_pairs={{0,8},{8,16},{16,24},{24,0},{1,9},{9,17},{17,25},{25,1},{2,10},{10... | collective-permute-start | bytes 983048 | tf_op jit(solution)/shard_map/ppermute | solution.py:23
  129.1 7.2 %collective-permute-start.25 = (bf16[128,896]{1,0:T(8,128)(2,1)S(1)}, bf16[128,896]{1,0:T(8,128)(2,1)S(1)}, u32[]{:S(2)}, u32[]{:S(2)}) collective-permute-start(bf16[128,896]{1,0:T(8,128)(2,1)S(1)} %get-tuple-element.84), channel_id=1, source_target_pairs={{0,1},{1,0},{2,3},{3,2},{4,5},{5,4},{6,7},{7,6},{8,9},{9,8},{10,11... | collective-permute-start | bytes 688136 | tf_op jit(solution)/shard_map/ppermute | solution.py:28
  130.2 7.2 %collective-permute-start.26 = (bf16[128,896]{1,0:T(8,128)(2,1)S(1)}, bf16[128,896]{1,0:T(8,128)(2,1)S(1)}, u32[]{:S(2)}, u32[]{:S(2)}) collective-permute-start(bf16[128,896]{1,0:T(8,128)(2,1)S(1)} %get-tuple-element.85), channel_id=1, source_target_pairs={{0,4},{2,6},{4,0},{6,2},{1,5},{3,7},{5,1},{7,3},{8,12},{10,14},{12... | collective-permute-start | bytes 688136 | tf_op jit(solution)/shard_map/ppermute | solution.py:28
  131.2 10.5 %collective-permute-start.24 = (bf16[128,768]{1,0:T(8,128)(2,1)S(1)}, bf16[128,768]{1,0:T(8,128)(2,1)S(1)}, u32[]{:S(2)}, u32[]{:S(2)}) collective-permute-start(bf16[128,768]{1,0:T(8,128)(2,1)S(1)} %sum_stage.22.refs_6_), channel_id=1, source_target_pairs={{0,8},{8,16},{16,24},{24,0},{1,9},{9,17},{17,25},{25,1},{2,10},{10... | collective-permute-start | bytes 589832 | tf_op jit(solution)/shard_map/ppermute | solution.py:23
  133.5 7.2 %collective-permute-start.31 = (bf16[128,384]{1,0:T(8,128)(2,1)S(1)}, bf16[128,384]{1,0:T(8,128)(2,1)S(1)}, u32[]{:S(2)}, u32[]{:S(2)}) collective-permute-start(bf16[128,384]{1,0:T(8,128)(2,1)S(1)} %get-tuple-element.96), channel_id=1, source_target_pairs={{0,1},{1,0},{2,3},{3,2},{4,5},{5,4},{6,7},{7,6},{8,9},{9,8},{10,11... | collective-permute-start | bytes 294920 | tf_op jit(solution)/shard_map/ppermute | solution.py:28
  136.3 5.3 %collective-permute-start.32 = (bf16[128,384]{1,0:T(8,128)(2,1)S(1)}, bf16[128,384]{1,0:T(8,128)(2,1)S(1)}, u32[]{:S(2)}, u32[]{:S(2)}) collective-permute-start(bf16[128,384]{1,0:T(8,128)(2,1)S(1)} %get-tuple-element.97), channel_id=1, source_target_pairs={{0,4},{2,6},{4,0},{6,2},{1,5},{3,7},{5,1},{7,3},{8,12},{10,14},{12... | collective-permute-start | bytes 294920 | tf_op jit(solution)/shard_map/ppermute | solution.py:28
  137.5 9.3 %collective-permute-start.28 = (bf16[128,768]{1,0:T(8,128)(2,1)S(1)}, bf16[128,768]{1,0:T(8,128)(2,1)S(1)}, u32[]{:S(2)}, u32[]{:S(2)}) collective-permute-start(bf16[128,768]{1,0:T(8,128)(2,1)S(1)} %sum_stage.24.refs_6_), channel_id=1, source_target_pairs={{0,8},{8,16},{16,24},{24,0},{1,9},{9,17},{17,25},{25,1},{2,10},{10... | collective-permute-start | bytes 589832 | tf_op jit(solution)/shard_map/ppermute | solution.py:23
  139.2 4.3 %collective-permute-start.29 = (bf16[128,256]{1,0:T(8,128)(2,1)S(1)}, bf16[128,256]{1,0:T(8,128)(2,1)S(1)}, u32[]{:S(2)}, u32[]{:S(2)}) collective-permute-start(bf16[128,256]{1,0:T(8,128)(2,1)S(1)} %get-tuple-element.92), channel_id=1, source_target_pairs={{0,1},{1,0},{2,3},{3,2},{4,5},{5,4},{6,7},{7,6},{8,9},{9,8},{10,11... | collective-permute-start | bytes 196616 | tf_op jit(solution)/shard_map/ppermute | solution.py:28
  140.7 4.3 %collective-permute-start.30 = (bf16[128,256]{1,0:T(8,128)(2,1)S(1)}, bf16[128,256]{1,0:T(8,128)(2,1)S(1)}, u32[]{:S(2)}, u32[]{:S(2)}) collective-permute-start(bf16[128,256]{1,0:T(8,128)(2,1)S(1)} %get-tuple-element.93), channel_id=1, source_target_pairs={{0,4},{2,6},{4,0},{6,2},{1,5},{3,7},{5,1},{7,3},{8,12},{10,14},{12... | collective-permute-start | bytes 196616 | tf_op jit(solution)/shard_map/ppermute | solution.py:28
  141.7 10.4 %collective-permute-start.34 = (bf16[128,768]{1,0:T(8,128)(2,1)S(1)}, bf16[128,768]{1,0:T(8,128)(2,1)S(1)}, u32[]{:S(2)}, u32[]{:S(2)}) collective-permute-start(bf16[128,768]{1,0:T(8,128)(2,1)S(1)} %sum_stage.26.refs_5_), channel_id=1, source_target_pairs={{0,8},{8,16},{16,24},{24,0},{1,9},{9,17},{17,25},{25,1},{2,10},{10... | collective-permute-start | bytes 589832 | tf_op jit(solution)/shard_map/ppermute | solution.py:23
  145.0 7.0 %collective-permute-start.33 = (bf16[128,512]{1,0:T(8,128)(2,1)S(1)}, bf16[128,512]{1,0:T(8,128)(2,1)S(1)}, u32[]{:S(2)}, u32[]{:S(2)}) collective-permute-start(bf16[128,512]{1,0:T(8,128)(2,1)S(1)} %sum_stage.27), channel_id=1, source_target_pairs={{0,8},{8,16},{16,24},{24,0},{1,9},{9,17},{17,25},{25,1},{2,10},{10... | collective-permute-start | bytes 393224 | tf_op jit(solution)/shard_map/ppermute | solution.py:23
  152.1 1.1 copy-start.10
